TPU v7x, 32 devices: a whole 2x2x4 slice. The times are simulated.
32 devices in a mesh: blk: 8 (over z, y), grp: 4 (over x, core).
Axes of the slice: x: 2, y: 2, z: 4, core: 2. Of those that a mesh axis runs over, the one named last changes fastest.
Arguments:
- points: bfloat16 [32768, 768], P(('blk', 'grp')), may hold values from -6 to 6, as said below
- counts: int32 [64], P(('blk', 'grp')), may hold values from 256 to 512, as said below
- pair_rows: int32 [512], P('blk'), may hold values from 0 to 7, as said below
- pair_cols: int32 [512], P('blk'), may hold values from 0 to 15, as said below
- pair_live: int32 [8], P('blk'), may hold values from 1 to 64, as said below
- start: float32 [64, 32768], P(None, ('blk', 'grp')), may hold values from -6 to 6
Outputs:
- embed: float32 [64, 32768], P(None, ('blk', 'grp'))
Inputs may be any that keep to these rules, and one draw needn't show every extreme that they name: Padding points are drawn like the others. `counts`: points of a block beyond its count are padding; block 0 is full. `pair_rows`: the live slots of a slab list distinct pairs. `pair_cols`: in a live slot, a value under 8 is above the slot's pair_rows; larger values, naming a block of the next slab, stand in live slots only of slabs below the last. Slots 0 to pair_live - 1 of a slab are live; slab 0 has all 64.
All inputs are finite; a program needn't handle non-finite values.
Results may differ from a plain program's by a relative error of at most 0.0042.
Values may be sent and summed in bfloat16 or wider, within the bound.
No kernel may reach another device: no remote copies, remote signals or barrier semaphores. Data moves between devices by JAX's collectives and lax.ppermute only.
A program may use at most 64 MiB of HBM per device.

v0:
```python
import jax
import jax.numpy as jnp
from jax import lax
from jax.sharding import PartitionSpec as P

PTS = 512
ITERS = 2


def from_behind(value, axis, steps):
    count = lax.axis_size(axis)
    initial, last = (max(0, -steps), min(count, count - steps))
    return lax.ppermute(value, axis, [(source, source + steps) for source in range(initial, last)])


def score(window, wlive, row_blk, col_blk):
    left = lax.dynamic_slice_in_dim(window, row_blk * PTS, PTS, 0)
    right = lax.dynamic_slice_in_dim(window, col_blk * PTS, PTS, 0)
    left_live = lax.dynamic_slice_in_dim(wlive, row_blk * PTS, PTS, 0)
    right_live = lax.dynamic_slice_in_dim(wlive, col_blk * PTS, PTS, 0)
    left_wide = left.astype(jnp.float32)
    right_wide = right.astype(jnp.float32)
    left_norm = jnp.sum(left_wide * left_wide, 1)
    right_norm = jnp.sum(right_wide * right_wide, 1)
    cross = lax.dot_general(
        left, right, (((1,), (1,)), ((), ())), preferred_element_type=jnp.float32
    )
    dist = left_norm[:, None] + right_norm[None, :] - 2.0 * cross
    width = left.shape[1]
    tile = jnp.exp(-3.0 / width * dist) * left_live[:, None] * right_live[None, :]
    return tile.astype(jnp.bfloat16)


def bump(total, start_at, addend):
    old = lax.dynamic_slice_in_dim(total, start_at, addend.shape[-1], total.ndim - 1)
    return lax.dynamic_update_slice_in_dim(total, old + addend, start_at, total.ndim - 1)


def per_device(points, counts, pair_rows, pair_cols, pair_live, start):
    group_size = lax.axis_size("grp")
    member = lax.axis_index("grp")
    blocks_dev = counts.shape[0]
    slab = blocks_dev * group_size
    half = slab * PTS
    slots = pair_rows.shape[0] // group_size
    live_count = pair_live[0]
    live = (jnp.arange(PTS)[None, :] < counts[:, None]).reshape(-1).astype(jnp.float32)
    live_half = live.astype(jnp.bfloat16)
    near = (
        lax.all_gather(points, "grp", axis=0, tiled=True),
        lax.all_gather(live_half, "grp", axis=0, tiled=True),
    )
    far = from_behind((near[0], near[1]), "blk", -1)
    window = jnp.concatenate([near[0], far[0]], 0)
    wlive = jnp.concatenate([near[1], far[1]], 0).astype(jnp.float32)

    def slot_pair(index):
        position = member + group_size * index
        return (position, position < live_count, pair_rows[position], pair_cols[position])

    def tile_of(row_blk, col_blk):
        return score(window, wlive, row_blk, col_blk)

    vecs = start
    columns = start.shape[0]
    for turn in range(ITERS):
        vec_half = vecs.astype(jnp.bfloat16)
        near_vec = lax.all_gather(vec_half, "grp", axis=1, tiled=True)
        far_vec = from_behind(near_vec, "blk", -1)
        vec_window = jnp.concatenate([near_vec, far_vec], 1)

        def turn_body(index, carry):
            position, flag, row_blk, col_blk = slot_pair(index)

            def add(state):
                acc, dacc = state
                tile = tile_of(row_blk, col_blk)
                upper_vec = lax.dynamic_slice_in_dim(vec_window, col_blk * PTS, PTS, 1)
                lower_vec = lax.dynamic_slice_in_dim(vec_window, row_blk * PTS, PTS, 1)
                to_row = lax.dot_general(
                    upper_vec, tile, (((1,), (1,)), ((), ())), preferred_element_type=jnp.float32
                )
                to_col = jnp.dot(lower_vec, tile, preferred_element_type=jnp.float32)
                acc = bump(bump(acc, row_blk * PTS, to_row), col_blk * PTS, to_col)
                tile_wide = tile.astype(jnp.float32)
                dacc = bump(
                    bump(dacc, row_blk * PTS, jnp.sum(tile_wide, 1)),
                    col_blk * PTS,
                    jnp.sum(tile_wide, 0),
                )
                return (acc, dacc)

            return lax.cond(flag, add, lambda state: state, carry)

        init = (jnp.zeros((columns, 2 * half), jnp.float32), jnp.zeros((2 * half,), jnp.float32))
        acc, dacc = lax.fori_loop(0, slots, turn_body, init)
        back = from_behind((acc[:, half:], dacc[half:]), "blk", 1)
        share = (
            lax.psum_scatter(acc[:, :half] + back[0], "grp", scatter_dimension=1, tiled=True),
            lax.psum_scatter(dacc[:half] + back[1], "grp", scatter_dimension=0, tiled=True),
        )
        outcome = live[None, :] * vec_half.astype(jnp.float32) + share[0]
        degree = 1.0 + share[1]
        scaled = outcome / degree[None, :]
        partial_gram = lax.dot_general(
            scaled, scaled, (((1,), (1,)), ((), ())), precision=lax.Precision.HIGHEST
        )
        gram = lax.psum(partial_gram, ("blk", "grp"))
        lower = jnp.linalg.cholesky(gram)
        vecs = lax.linalg.triangular_solve(lower, scaled, left_side=True, lower=True)
    return vecs


def solution(mesh):
    in_specs = (
        P(("blk", "grp"), None),
        P(("blk", "grp")),
        P("blk"),
        P("blk"),
        P("blk"),
        P(None, ("blk", "grp")),
    )
    out_specs = P(None, ("blk", "grp"))
    return jax.shard_map(
        per_device, mesh=mesh, in_specs=in_specs, out_specs=out_specs, check_vma=False
    )
```

profile of v0, /device:TPU:0, one launch (start us, length us, event | category | flops | bytes accessed | tf_op | source)
XLA Modules:
  0.0 728.6 jit_solution(11157249813771259683)
XLA Ops:
  7.3 50.7 %all-gather.2.cloned.1.call-done = bf16[4096,768]{1,0:T(8,128)(2,1)} async-done(((bf16[1024,768]{1,0:T(8,128)(2,1)}), bf16[4096,768]{1,0:T(8,128)(2,1)}) %all-gather.2.cloned.1.call-update) | async-done | bytes 6291472 | tf_op jit(solution)/shard_map/all_gather | solution.py:50
  60.3 7.2 all_gather.12
  68.9 5.2 all_gather.14
  75.3 133.9 %collective-permute-done.2 = bf16[4096]{0:T(1024)(128)(2,1)S(1)} collective-permute-done((bf16[4096]{0:T(1024)(128)(2,1)S(1)}, bf16[4096]{0:T(1024)(128)(2,1)S(1)}, u32[]{:S(2)}, u32[]{:S(2)}) %collective-permute-start.2) | collective-permute-done | bytes 8224 | tf_op jit(solution)/shard_map/ppermute | solution.py:13
  209.3 3.2 constant_dynamic-update-slice_fusion.1
  212.5 3.6 constant_dynamic-update-slice_fusion
  216.3 4.4 copy-done
  220.7 133.8 %while.30 = (s32[]{:T(128)}, f32[64,8192]{1,0:T(8,128)S(1)}, f32[8192]{0:T(1024)S(1)}, s32[]{:T(128)}, s32[]{:T(128)}, /*index=5*/s32[64]{0:T(128)S(1)}, s32[64]...) while((s32[]{:T(128)}, f32[64,8192]{1,0:T(8,128)S(1)}, ...), condition=%wide.region_7.0_spmd, body=%wide.region_0.0_spmd.sunk | while | flops 474807296 | bytes 5411273 | solution.py:96
  221.3 7.7 %conditional.4 = ((f32[64,8192]{1,0:T(8,128)S(1)}, f32[8192]{0:T(1024)S(1)})) conditional(s32[]{:T(128)} %convert_element_type.114, (f32[64,8192]{1,0:T(8,128)S(1)}, f32[8192]{0:T(1024)S(1)}) %tuple.92, (s32[]{:T(128)}, s32[64]{0:T(128)S(1)}, f32[64,8192]{1,0:T(8,128)S(1)}, s32[64]{0:T(128)S(1)}, bf16[64,8192]{1,0:T(8,128)(2,1)S(1)}, ...), branch_computations={%region_1.0_spmd, %region_2.0_spmd} | conditional | flops 474807296 | bytes 5411038 | solution.py:93
  229.7 7.7 %conditional.4 = ((f32[64,8192]{1,0:T(8,128)S(1)}, f32[8192]{0:T(1024)S(1)})) conditional(s32[]{:T(128)} %convert_element_type.114, (f32[64,8192]{1,0:T(8,128)S(1)}, f32[8192]{0:T(1024)S(1)}) %tuple.92, (s32[]{:T(128)}, s32[64]{0:T(128)S(1)}, f32[64,8192]{1,0:T(8,128)S(1)}, s32[64]{0:T(128)S(1)}, bf16[64,8192]{1,0:T(8,128)(2,1)S(1)}, ...), branch_computations={%region_1.0_spmd, %region_2.0_spmd} | conditional | flops 474807296 | bytes 5411038 | solution.py:93
  234.3 2.3 convert_reduce_fusion
  238.1 7.7 %conditional.4 = ((f32[64,8192]{1,0:T(8,128)S(1)}, f32[8192]{0:T(1024)S(1)})) conditional(s32[]{:T(128)} %convert_element_type.114, (f32[64,8192]{1,0:T(8,128)S(1)}, f32[8192]{0:T(1024)S(1)}) %tuple.92, (s32[]{:T(128)}, s32[64]{0:T(128)S(1)}, f32[64,8192]{1,0:T(8,128)S(1)}, s32[64]{0:T(128)S(1)}, bf16[64,8192]{1,0:T(8,128)(2,1)S(1)}, ...), branch_computations={%region_1.0_spmd, %region_2.0_spmd} | conditional | flops 474807296 | bytes 5411038 | solution.py:93
  246.4 7.7 %conditional.4 = ((f32[64,8192]{1,0:T(8,128)S(1)}, f32[8192]{0:T(1024)S(1)})) conditional(s32[]{:T(128)} %convert_element_type.114, (f32[64,8192]{1,0:T(8,128)S(1)}, f32[8192]{0:T(1024)S(1)}) %tuple.92, (s32[]{:T(128)}, s32[64]{0:T(128)S(1)}, f32[64,8192]{1,0:T(8,128)S(1)}, s32[64]{0:T(128)S(1)}, bf16[64,8192]{1,0:T(8,128)(2,1)S(1)}, ...), branch_computations={%region_1.0_spmd, %region_2.0_spmd} | conditional | flops 474807296 | bytes 5411038 | solution.py:93
  254.8 7.7 %conditional.4 = ((f32[64,8192]{1,0:T(8,128)S(1)}, f32[8192]{0:T(1024)S(1)})) conditional(s32[]{:T(128)} %convert_element_type.114, (f32[64,8192]{1,0:T(8,128)S(1)}, f32[8192]{0:T(1024)S(1)}) %tuple.92, (s32[]{:T(128)}, s32[64]{0:T(128)S(1)}, f32[64,8192]{1,0:T(8,128)S(1)}, s32[64]{0:T(128)S(1)}, bf16[64,8192]{1,0:T(8,128)(2,1)S(1)}, ...), branch_computations={%region_1.0_spmd, %region_2.0_spmd} | conditional | flops 474807296 | bytes 5411038 | solution.py:93
  263.2 7.7 %conditional.4 = ((f32[64,8192]{1,0:T(8,128)S(1)}, f32[8192]{0:T(1024)S(1)})) conditional(s32[]{:T(128)} %convert_element_type.114, (f32[64,8192]{1,0:T(8,128)S(1)}, f32[8192]{0:T(1024)S(1)}) %tuple.92, (s32[]{:T(128)}, s32[64]{0:T(128)S(1)}, f32[64,8192]{1,0:T(8,128)S(1)}, s32[64]{0:T(128)S(1)}, bf16[64,8192]{1,0:T(8,128)(2,1)S(1)}, ...), branch_computations={%region_1.0_spmd, %region_2.0_spmd} | conditional | flops 474807296 | bytes 5411038 | solution.py:93
  271.5 7.7 %conditional.4 = ((f32[64,8192]{1,0:T(8,128)S(1)}, f32[8192]{0:T(1024)S(1)})) conditional(s32[]{:T(128)} %convert_element_type.114, (f32[64,8192]{1,0:T(8,128)S(1)}, f32[8192]{0:T(1024)S(1)}) %tuple.92, (s32[]{:T(128)}, s32[64]{0:T(128)S(1)}, f32[64,8192]{1,0:T(8,128)S(1)}, s32[64]{0:T(128)S(1)}, bf16[64,8192]{1,0:T(8,128)(2,1)S(1)}, ...), branch_computations={%region_1.0_spmd, %region_2.0_spmd} | conditional | flops 474807296 | bytes 5411038 | solution.py:93
  279.9 7.7 %conditional.4 = ((f32[64,8192]{1,0:T(8,128)S(1)}, f32[8192]{0:T(1024)S(1)})) conditional(s32[]{:T(128)} %convert_element_type.114, (f32[64,8192]{1,0:T(8,128)S(1)}, f32[8192]{0:T(1024)S(1)}) %tuple.92, (s32[]{:T(128)}, s32[64]{0:T(128)S(1)}, f32[64,8192]{1,0:T(8,128)S(1)}, s32[64]{0:T(128)S(1)}, bf16[64,8192]{1,0:T(8,128)(2,1)S(1)}, ...), branch_computations={%region_1.0_spmd, %region_2.0_spmd} | conditional | flops 474807296 | bytes 5411038 | solution.py:93
  288.3 7.7 %conditional.4 = ((f32[64,8192]{1,0:T(8,128)S(1)}, f32[8192]{0:T(1024)S(1)})) conditional(s32[]{:T(128)} %convert_element_type.114, (f32[64,8192]{1,0:T(8,128)S(1)}, f32[8192]{0:T(1024)S(1)}) %tuple.92, (s32[]{:T(128)}, s32[64]{0:T(128)S(1)}, f32[64,8192]{1,0:T(8,128)S(1)}, s32[64]{0:T(128)S(1)}, bf16[64,8192]{1,0:T(8,128)(2,1)S(1)}, ...), branch_computations={%region_1.0_spmd, %region_2.0_spmd} | conditional | flops 474807296 | bytes 5411038 | solution.py:93
  296.6 7.7 %conditional.4 = ((f32[64,8192]{1,0:T(8,128)S(1)}, f32[8192]{0:T(1024)S(1)})) conditional(s32[]{:T(128)} %convert_element_type.114, (f32[64,8192]{1,0:T(8,128)S(1)}, f32[8192]{0:T(1024)S(1)}) %tuple.92, (s32[]{:T(128)}, s32[64]{0:T(128)S(1)}, f32[64,8192]{1,0:T(8,128)S(1)}, s32[64]{0:T(128)S(1)}, bf16[64,8192]{1,0:T(8,128)(2,1)S(1)}, ...), branch_computations={%region_1.0_spmd, %region_2.0_spmd} | conditional | flops 474807296 | bytes 5411038 | solution.py:93
  305.0 7.7 %conditional.4 = ((f32[64,8192]{1,0:T(8,128)S(1)}, f32[8192]{0:T(1024)S(1)})) conditional(s32[]{:T(128)} %convert_element_type.114, (f32[64,8192]{1,0:T(8,128)S(1)}, f32[8192]{0:T(1024)S(1)}) %tuple.92, (s32[]{:T(128)}, s32[64]{0:T(128)S(1)}, f32[64,8192]{1,0:T(8,128)S(1)}, s32[64]{0:T(128)S(1)}, bf16[64,8192]{1,0:T(8,128)(2,1)S(1)}, ...), branch_computations={%region_1.0_spmd, %region_2.0_spmd} | conditional | flops 474807296 | bytes 5411038 | solution.py:93
  313.3 7.7 %conditional.4 = ((f32[64,8192]{1,0:T(8,128)S(1)}, f32[8192]{0:T(1024)S(1)})) conditional(s32[]{:T(128)} %convert_element_type.114, (f32[64,8192]{1,0:T(8,128)S(1)}, f32[8192]{0:T(1024)S(1)}) %tuple.92, (s32[]{:T(128)}, s32[64]{0:T(128)S(1)}, f32[64,8192]{1,0:T(8,128)S(1)}, s32[64]{0:T(128)S(1)}, bf16[64,8192]{1,0:T(8,128)(2,1)S(1)}, ...), branch_computations={%region_1.0_spmd, %region_2.0_spmd} | conditional | flops 474807296 | bytes 5411038 | solution.py:93
  321.7 7.7 %conditional.4 = ((f32[64,8192]{1,0:T(8,128)S(1)}, f32[8192]{0:T(1024)S(1)})) conditional(s32[]{:T(128)} %convert_element_type.114, (f32[64,8192]{1,0:T(8,128)S(1)}, f32[8192]{0:T(1024)S(1)}) %tuple.92, (s32[]{:T(128)}, s32[64]{0:T(128)S(1)}, f32[64,8192]{1,0:T(8,128)S(1)}, s32[64]{0:T(128)S(1)}, bf16[64,8192]{1,0:T(8,128)(2,1)S(1)}, ...), branch_computations={%region_1.0_spmd, %region_2.0_spmd} | conditional | flops 474807296 | bytes 5411038 | solution.py:93
  330.1 7.7 %conditional.4 = ((f32[64,8192]{1,0:T(8,128)S(1)}, f32[8192]{0:T(1024)S(1)})) conditional(s32[]{:T(128)} %convert_element_type.114, (f32[64,8192]{1,0:T(8,128)S(1)}, f32[8192]{0:T(1024)S(1)}) %tuple.92, (s32[]{:T(128)}, s32[64]{0:T(128)S(1)}, f32[64,8192]{1,0:T(8,128)S(1)}, s32[64]{0:T(128)S(1)}, bf16[64,8192]{1,0:T(8,128)(2,1)S(1)}, ...), branch_computations={%region_1.0_spmd, %region_2.0_spmd} | conditional | flops 474807296 | bytes 5411038 | solution.py:93
  334.6 2.3 convert_reduce_fusion
  338.4 7.7 %conditional.4 = ((f32[64,8192]{1,0:T(8,128)S(1)}, f32[8192]{0:T(1024)S(1)})) conditional(s32[]{:T(128)} %convert_element_type.114, (f32[64,8192]{1,0:T(8,128)S(1)}, f32[8192]{0:T(1024)S(1)}) %tuple.92, (s32[]{:T(128)}, s32[64]{0:T(128)S(1)}, f32[64,8192]{1,0:T(8,128)S(1)}, s32[64]{0:T(128)S(1)}, bf16[64,8192]{1,0:T(8,128)(2,1)S(1)}, ...), branch_computations={%region_1.0_spmd, %region_2.0_spmd} | conditional | flops 474807296 | bytes 5411038 | solution.py:93
  343.0 2.3 convert_reduce_fusion
  346.8 7.7 %conditional.4 = ((f32[64,8192]{1,0:T(8,128)S(1)}, f32[8192]{0:T(1024)S(1)})) conditional(s32[]{:T(128)} %convert_element_type.114, (f32[64,8192]{1,0:T(8,128)S(1)}, f32[8192]{0:T(1024)S(1)}) %tuple.92, (s32[]{:T(128)}, s32[64]{0:T(128)S(1)}, f32[64,8192]{1,0:T(8,128)S(1)}, s32[64]{0:T(128)S(1)}, bf16[64,8192]{1,0:T(8,128)(2,1)S(1)}, ...), branch_computations={%region_1.0_spmd, %region_2.0_spmd} | conditional | flops 474807296 | bytes 5411038 | solution.py:93
  356.0 22.2 %collective-permute-done.3 = f32[64,4096]{1,0:T(8,128)S(1)} collective-permute-done((f32[64,4096]{1,0:T(8,128)S(1)}, f32[64,4096]{1,0:T(8,128)S(1)}, u32[]{:S(2)}, u32[]{:S(2)}) %collective-permute-start.3) | collective-permute-done | bytes 1048608 | tf_op jit(solution)/shard_map/ppermute | solution.py:13
  379.4 5.2 collective-permute-start.4
  386.1 10.2 %all-reduce = f32[4096]{0:T(1024)S(1)} all-reduce(f32[4096]{0:T(1024)S(1)} %slice_add_fusion.3), channel_id=3, replica_groups=mesh['blk'=8,'grp'=4] {'grp'}, use_global_device_ids=true, to_apply=%region_9.0.clone | all-reduce | flops 4096 | bytes 32768
  396.3 9.1 %reduce-scatter.3.cloned.1.call-done = f32[64,1024]{1,0:T(8,128)} async-done(((f32[64,4096]{1,0:T(8,128)}), f32[64,1024]{1,0:T(8,128)}) %reduce-scatter.3.cloned.1.call-update) | async-done | bytes 262160 | tf_op jit(solution)/shard_map/reduce_scatter | solution.py:99
  406.8 39.5 %psum.14 = f32[64,64]{0,1:T(8,128)S(1)} all-reduce(f32[64,64]{0,1:T(8,128)S(1)} %fusion.39), channel_id=1, replica_groups=mesh['blk'=8,'grp'=4] {'blk','grp'}, use_global_device_ids=true, to_apply=%region_10.0 | all-reduce | flops 4096 | bytes 32768 | tf_op jit(solution)/shard_map/psum | solution.py:108
  446.4 5.8 cholesky.44
  453.6 4.9 custom-call.6
  459.9 7.9 %all_gather.15 = bf16[64,4096]{1,0:T(8,128)(2,1)S(1)} all-gather(bf16[64,1024]{1,0:T(8,128)(2,1)S(1)} %convolution_convert_fusion), channel_id=1, replica_groups=mesh['blk'=8,'grp'=4] {'grp'}, dimensions={1}, use_global_device_ids=true | all-gather | bytes 655360 | tf_op jit(solution)/shard_map/all_gather | solution.py:68
  469.1 14.8 %collective-permute-done.5 = bf16[64,4096]{1,0:T(8,128)(2,1)S(1)} collective-permute-done((bf16[64,4096]{1,0:T(8,128)(2,1)S(1)}, bf16[64,4096]{1,0:T(8,128)(2,1)S(1)}, u32[]{:S(2)}, u32[]{:S(2)}) %collective-permute-start.5) | collective-permute-done | bytes 524320 | tf_op jit(solution)/shard_map/ppermute | solution.py:13
  484.1 131.4 %while.31 = (s32[]{:T(128)}, f32[64,8192]{1,0:T(8,128)S(1)}, f32[8192]{0:T(1024)S(1)}, s32[]{:T(128)}, s32[]{:T(128)}, /*index=5*/s32[64]{0:T(128)S(1)}, s32[64]...) while((s32[]{:T(128)}, f32[64,8192]{1,0:T(8,128)S(1)}, ...), condition=%wide.region_20.23_spmd, body=%wide.region_13.22_spmd.sunk | while | flops 474807296 | bytes 5411273 | solution.py:96
  484.8 7.6 %conditional.5 = ((f32[64,8192]{1,0:T(8,128)S(1)}, f32[8192]{0:T(1024)S(1)})) conditional(s32[]{:T(128)} %convert_element_type.115, (f32[64,8192]{1,0:T(8,128)S(1)}, f32[8192]{0:T(1024)S(1)}) %tuple.95, (s32[]{:T(128)}, s32[64]{0:T(128)S(1)}, f32[64,8192]{1,0:T(8,128)S(1)}, s32[64]{0:T(128)S(1)}, bf16[64,8192]{1,0:T(8,128)(2,1)S(1)}, ...), branch_computations={%region_14.16_spmd, %region_15.21_spmd} | conditional | flops 474807296 | bytes 5411038 | solution.py:93
  493.0 7.6 %conditional.5 = ((f32[64,8192]{1,0:T(8,128)S(1)}, f32[8192]{0:T(1024)S(1)})) conditional(s32[]{:T(128)} %convert_element_type.115, (f32[64,8192]{1,0:T(8,128)S(1)}, f32[8192]{0:T(1024)S(1)}) %tuple.95, (s32[]{:T(128)}, s32[64]{0:T(128)S(1)}, f32[64,8192]{1,0:T(8,128)S(1)}, s32[64]{0:T(128)S(1)}, bf16[64,8192]{1,0:T(8,128)(2,1)S(1)}, ...), branch_computations={%region_14.16_spmd, %region_15.21_spmd} | conditional | flops 474807296 | bytes 5411038 | solution.py:93
  497.4 2.3 convert_reduce_fusion.2
  501.2 7.6 %conditional.5 = ((f32[64,8192]{1,0:T(8,128)S(1)}, f32[8192]{0:T(1024)S(1)})) conditional(s32[]{:T(128)} %convert_element_type.115, (f32[64,8192]{1,0:T(8,128)S(1)}, f32[8192]{0:T(1024)S(1)}) %tuple.95, (s32[]{:T(128)}, s32[64]{0:T(128)S(1)}, f32[64,8192]{1,0:T(8,128)S(1)}, s32[64]{0:T(128)S(1)}, bf16[64,8192]{1,0:T(8,128)(2,1)S(1)}, ...), branch_computations={%region_14.16_spmd, %region_15.21_spmd} | conditional | flops 474807296 | bytes 5411038 | solution.py:93
  509.4 7.6 %conditional.5 = ((f32[64,8192]{1,0:T(8,128)S(1)}, f32[8192]{0:T(1024)S(1)})) conditional(s32[]{:T(128)} %convert_element_type.115, (f32[64,8192]{1,0:T(8,128)S(1)}, f32[8192]{0:T(1024)S(1)}) %tuple.95, (s32[]{:T(128)}, s32[64]{0:T(128)S(1)}, f32[64,8192]{1,0:T(8,128)S(1)}, s32[64]{0:T(128)S(1)}, bf16[64,8192]{1,0:T(8,128)(2,1)S(1)}, ...), branch_computations={%region_14.16_spmd, %region_15.21_spmd} | conditional | flops 474807296 | bytes 5411038 | solution.py:93
  517.6 7.6 %conditional.5 = ((f32[64,8192]{1,0:T(8,128)S(1)}, f32[8192]{0:T(1024)S(1)})) conditional(s32[]{:T(128)} %convert_element_type.115, (f32[64,8192]{1,0:T(8,128)S(1)}, f32[8192]{0:T(1024)S(1)}) %tuple.95, (s32[]{:T(128)}, s32[64]{0:T(128)S(1)}, f32[64,8192]{1,0:T(8,128)S(1)}, s32[64]{0:T(128)S(1)}, bf16[64,8192]{1,0:T(8,128)(2,1)S(1)}, ...), branch_computations={%region_14.16_spmd, %region_15.21_spmd} | conditional | flops 474807296 | bytes 5411038 | solution.py:93
  522.1 2.3 convert_reduce_fusion.2
  525.8 7.6 %conditional.5 = ((f32[64,8192]{1,0:T(8,128)S(1)}, f32[8192]{0:T(1024)S(1)})) conditional(s32[]{:T(128)} %convert_element_type.115, (f32[64,8192]{1,0:T(8,128)S(1)}, f32[8192]{0:T(1024)S(1)}) %tuple.95, (s32[]{:T(128)}, s32[64]{0:T(128)S(1)}, f32[64,8192]{1,0:T(8,128)S(1)}, s32[64]{0:T(128)S(1)}, bf16[64,8192]{1,0:T(8,128)(2,1)S(1)}, ...), branch_computations={%region_14.16_spmd, %region_15.21_spmd} | conditional | flops 474807296 | bytes 5411038 | solution.py:93
  534.1 7.6 %conditional.5 = ((f32[64,8192]{1,0:T(8,128)S(1)}, f32[8192]{0:T(1024)S(1)})) conditional(s32[]{:T(128)} %convert_element_type.115, (f32[64,8192]{1,0:T(8,128)S(1)}, f32[8192]{0:T(1024)S(1)}) %tuple.95, (s32[]{:T(128)}, s32[64]{0:T(128)S(1)}, f32[64,8192]{1,0:T(8,128)S(1)}, s32[64]{0:T(128)S(1)}, bf16[64,8192]{1,0:T(8,128)(2,1)S(1)}, ...), branch_computations={%region_14.16_spmd, %region_15.21_spmd} | conditional | flops 474807296 | bytes 5411038 | solution.py:93
  542.3 7.6 %conditional.5 = ((f32[64,8192]{1,0:T(8,128)S(1)}, f32[8192]{0:T(1024)S(1)})) conditional(s32[]{:T(128)} %convert_element_type.115, (f32[64,8192]{1,0:T(8,128)S(1)}, f32[8192]{0:T(1024)S(1)}) %tuple.95, (s32[]{:T(128)}, s32[64]{0:T(128)S(1)}, f32[64,8192]{1,0:T(8,128)S(1)}, s32[64]{0:T(128)S(1)}, bf16[64,8192]{1,0:T(8,128)(2,1)S(1)}, ...), branch_computations={%region_14.16_spmd, %region_15.21_spmd} | conditional | flops 474807296 | bytes 5411038 | solution.py:93
  546.7 2.3 convert_reduce_fusion.2
  550.5 7.6 %conditional.5 = ((f32[64,8192]{1,0:T(8,128)S(1)}, f32[8192]{0:T(1024)S(1)})) conditional(s32[]{:T(128)} %convert_element_type.115, (f32[64,8192]{1,0:T(8,128)S(1)}, f32[8192]{0:T(1024)S(1)}) %tuple.95, (s32[]{:T(128)}, s32[64]{0:T(128)S(1)}, f32[64,8192]{1,0:T(8,128)S(1)}, s32[64]{0:T(128)S(1)}, bf16[64,8192]{1,0:T(8,128)(2,1)S(1)}, ...), branch_computations={%region_14.16_spmd, %region_15.21_spmd} | conditional | flops 474807296 | bytes 5411038 | solution.py:93
  558.7 7.6 %conditional.5 = ((f32[64,8192]{1,0:T(8,128)S(1)}, f32[8192]{0:T(1024)S(1)})) conditional(s32[]{:T(128)} %convert_element_type.115, (f32[64,8192]{1,0:T(8,128)S(1)}, f32[8192]{0:T(1024)S(1)}) %tuple.95, (s32[]{:T(128)}, s32[64]{0:T(128)S(1)}, f32[64,8192]{1,0:T(8,128)S(1)}, s32[64]{0:T(128)S(1)}, bf16[64,8192]{1,0:T(8,128)(2,1)S(1)}, ...), branch_computations={%region_14.16_spmd, %region_15.21_spmd} | conditional | flops 474807296 | bytes 5411038 | solution.py:93
  566.9 7.6 %conditional.5 = ((f32[64,8192]{1,0:T(8,128)S(1)}, f32[8192]{0:T(1024)S(1)})) conditional(s32[]{:T(128)} %convert_element_type.115, (f32[64,8192]{1,0:T(8,128)S(1)}, f32[8192]{0:T(1024)S(1)}) %tuple.95, (s32[]{:T(128)}, s32[64]{0:T(128)S(1)}, f32[64,8192]{1,0:T(8,128)S(1)}, s32[64]{0:T(128)S(1)}, bf16[64,8192]{1,0:T(8,128)(2,1)S(1)}, ...), branch_computations={%region_14.16_spmd, %region_15.21_spmd} | conditional | flops 474807296 | bytes 5411038 | solution.py:93
  575.1 7.6 %conditional.5 = ((f32[64,8192]{1,0:T(8,128)S(1)}, f32[8192]{0:T(1024)S(1)})) conditional(s32[]{:T(128)} %convert_element_type.115, (f32[64,8192]{1,0:T(8,128)S(1)}, f32[8192]{0:T(1024)S(1)}) %tuple.95, (s32[]{:T(128)}, s32[64]{0:T(128)S(1)}, f32[64,8192]{1,0:T(8,128)S(1)}, s32[64]{0:T(128)S(1)}, bf16[64,8192]{1,0:T(8,128)(2,1)S(1)}, ...), branch_computations={%region_14.16_spmd, %region_15.21_spmd} | conditional | flops 474807296 | bytes 5411038 | solution.py:93
  583.3 7.6 %conditional.5 = ((f32[64,8192]{1,0:T(8,128)S(1)}, f32[8192]{0:T(1024)S(1)})) conditional(s32[]{:T(128)} %convert_element_type.115, (f32[64,8192]{1,0:T(8,128)S(1)}, f32[8192]{0:T(1024)S(1)}) %tuple.95, (s32[]{:T(128)}, s32[64]{0:T(128)S(1)}, f32[64,8192]{1,0:T(8,128)S(1)}, s32[64]{0:T(128)S(1)}, bf16[64,8192]{1,0:T(8,128)(2,1)S(1)}, ...), branch_computations={%region_14.16_spmd, %region_15.21_spmd} | conditional | flops 474807296 | bytes 5411038 | solution.py:93
  591.5 7.6 %conditional.5 = ((f32[64,8192]{1,0:T(8,128)S(1)}, f32[8192]{0:T(1024)S(1)})) conditional(s32[]{:T(128)} %convert_element_type.115, (f32[64,8192]{1,0:T(8,128)S(1)}, f32[8192]{0:T(1024)S(1)}) %tuple.95, (s32[]{:T(128)}, s32[64]{0:T(128)S(1)}, f32[64,8192]{1,0:T(8,128)S(1)}, s32[64]{0:T(128)S(1)}, bf16[64,8192]{1,0:T(8,128)(2,1)S(1)}, ...), branch_computations={%region_14.16_spmd, %region_15.21_spmd} | conditional | flops 474807296 | bytes 5411038 | solution.py:93
  599.7 7.6 %conditional.5 = ((f32[64,8192]{1,0:T(8,128)S(1)}, f32[8192]{0:T(1024)S(1)})) conditional(s32[]{:T(128)} %convert_element_type.115, (f32[64,8192]{1,0:T(8,128)S(1)}, f32[8192]{0:T(1024)S(1)}) %tuple.95, (s32[]{:T(128)}, s32[64]{0:T(128)S(1)}, f32[64,8192]{1,0:T(8,128)S(1)}, s32[64]{0:T(128)S(1)}, bf16[64,8192]{1,0:T(8,128)(2,1)S(1)}, ...), branch_computations={%region_14.16_spmd, %region_15.21_spmd} | conditional | flops 474807296 | bytes 5411038 | solution.py:93
  604.2 2.3 convert_reduce_fusion.2
  608.0 7.6 %conditional.5 = ((f32[64,8192]{1,0:T(8,128)S(1)}, f32[8192]{0:T(1024)S(1)})) conditional(s32[]{:T(128)} %convert_element_type.115, (f32[64,8192]{1,0:T(8,128)S(1)}, f32[8192]{0:T(1024)S(1)}) %tuple.95, (s32[]{:T(128)}, s32[64]{0:T(128)S(1)}, f32[64,8192]{1,0:T(8,128)S(1)}, s32[64]{0:T(128)S(1)}, bf16[64,8192]{1,0:T(8,128)(2,1)S(1)}, ...), branch_computations={%region_14.16_spmd, %region_15.21_spmd} | conditional | flops 474807296 | bytes 5411038 | solution.py:93
  616.9 22.3 %collective-permute-done.6 = f32[64,4096]{1,0:T(8,128)S(1)} collective-permute-done((f32[64,4096]{1,0:T(8,128)S(1)}, f32[64,4096]{1,0:T(8,128)S(1)}, u32[]{:S(2)}, u32[]{:S(2)}) %collective-permute-start.6) | collective-permute-done | bytes 1048608 | tf_op jit(solution)/shard_map/ppermute | solution.py:13
  640.4 5.2 collective-permute-start.7
  647.0 10.1 %all-reduce.1 = f32[4096]{0:T(1024)S(1)} all-reduce(f32[4096]{0:T(1024)S(1)} %slice_add_fusion.2), channel_id=5, replica_groups=mesh['blk'=8,'grp'=4] {'grp'}, use_global_device_ids=true, to_apply=%region_22.25.clone | all-reduce | flops 4096 | bytes 32768
  657.1 9.6 %reduce-scatter.5.cloned.1.call-done = f32[64,1024]{1,0:T(8,128)} async-done(((f32[64,4096]{1,0:T(8,128)}), f32[64,1024]{1,0:T(8,128)}) %reduce-scatter.5.cloned.1.call-update) | async-done | bytes 262160 | tf_op jit(solution)/shard_map/reduce_scatter | solution.py:99
  668.1 39.7 %psum.15 = f32[64,64]{0,1:T(8,128)S(1)} all-reduce(f32[64,64]{0,1:T(8,128)S(1)} %fusion.40), channel_id=1, replica_groups=mesh['blk'=8,'grp'=4] {'blk','grp'}, use_global_device_ids=true, to_apply=%region_23.26 | all-reduce | flops 4096 | bytes 32768 | tf_op jit(solution)/shard_map/psum | solution.py:108
  707.9 5.8 cholesky.55
  715.1 4.9 custom-call.7
  (342 shorter events, 208.9 us)
Async XLA Ops:
  6.5 62.2 %copy-start.1 = (s32[2]{0:T(128)S(1)}, s32[2]{0:T(128)}, u32[]{:S(2)}) copy-start(s32[2]{0:T(128)} %param.18) | copy-start | bytes 28
  6.5 51.5 %all-gather.2.cloned.1.call-start = ((), (), s32[]{:S(2)}) async-start(), calls=%async_computation.2 | async-start | bytes 7864320 | tf_op jit(solution)/shard_map/all_gather | solution.py:50
  7.3 398.1 %reduce-scatter.3.cloned.1.call-start = ((), (), s32[]{:S(2)}) async-start(), calls=%async_computation.3 | async-start | bytes 1310720 | tf_op jit(solution)/shard_map/reduce_scatter | solution.py:99
  58.0 154.5 %collective-permute-start.1 = (bf16[4096,768]{1,0:T(8,128)(2,1)}, bf16[4096,768]{1,0:T(8,128)(2,1)}, u32[]{:S(2)}, u32[]{:S(2)}) collective-permute-start(bf16[4096,768]{1,0:T(8,128)(2,1)} %all-gather.2.cloned.1.call-done), channel_id=1, source_target_pairs={{4,0},{8,4},{12,8},{16,12},{20,16},{24,20},{28,24},{5,1},{9,5},{13... | collective-permute-start | bytes 18874376 | tf_op jit(solution)/shard_map/ppermute | solution.py:13
  67.5 141.7 %collective-permute-start = (bf16[64,4096]{1,0:T(8,128)(2,1)S(1)}, bf16[64,4096]{1,0:T(8,128)(2,1)S(1)}, u32[]{:S(2)}, u32[]{:S(2)}) collective-permute-start(bf16[64,4096]{1,0:T(8,128)(2,1)S(1)} %all_gather.12), channel_id=1, source_target_pairs={{4,0},{8,4},{12,8},{16,12},{20,16},{24,20},{28,24},{5,1},{9,5},{13... | collective-permute-start | bytes 1572872 | tf_op jit(solution)/shard_map/ppermute | solution.py:13
  74.0 135.2 %collective-permute-start.2 = (bf16[4096]{0:T(1024)(128)(2,1)S(1)}, bf16[4096]{0:T(1024)(128)(2,1)S(1)}, u32[]{:S(2)}, u32[]{:S(2)}) collective-permute-start(bf16[4096]{0:T(1024)(128)(2,1)S(1)} %all_gather.14), channel_id=1, source_target_pairs={{4,0},{8,4},{12,8},{16,12},{20,16},{24,20},{28,24},{5,1},{9,5},{13... | collective-permute-start | bytes 24584 | tf_op jit(solution)/shard_map/ppermute | solution.py:13
  216.1 4.6 copy-start
  216.1 4.6 copy-start.2
  216.1 4.6 copy-start.3
  354.6 30.1 %copy-start.4 = (u32[32]{0:T(128)S(1)}, u32[32]{0:T(128)}, u32[]{:S(2)}) copy-start(u32[32]{0:T(128)} %constant.158) | copy-start | bytes 388
  354.6 23.6 %collective-permute-start.3 = (f32[64,4096]{1,0:T(8,128)S(1)}, f32[64,4096]{1,0:T(8,128)S(1)}, u32[]{:S(2)}, u32[]{:S(2)}) collective-permute-start(f32[64,4096]{1,0:T(8,128)S(1)} %slice.31), channel_id=1, source_target_pairs={{0,4},{4,8},{8,12},{12,16},{16,20},{20,24},{24,28},{1,5},{5,9},{9,... | collective-permute-start | bytes 3145736 | tf_op jit(solution)/shard_map/ppermute | solution.py:13
  379.4 287.3 %reduce-scatter.5.cloned.1.call-start = ((), (), s32[]{:S(2)}) async-start(), calls=%async_computation.4 | async-start | bytes 1310720 | tf_op jit(solution)/shard_map/reduce_scatter | solution.py:99
  379.4 6.6 collective-permute-start.4
  467.8 16.1 %collective-permute-start.5 = (bf16[64,4096]{1,0:T(8,128)(2,1)S(1)}, bf16[64,4096]{1,0:T(8,128)(2,1)S(1)}, u32[]{:S(2)}, u32[]{:S(2)}) collective-permute-start(bf16[64,4096]{1,0:T(8,128)(2,1)S(1)} %all_gather.15), channel_id=1, source_target_pairs={{4,0},{8,4},{12,8},{16,12},{20,16},{24,20},{28,24},{5,1},{9,5},{13... | collective-permute-start | bytes 1572872 | tf_op jit(solution)/shard_map/ppermute | solution.py:13
  615.6 23.7 %collective-permute-start.6 = (f32[64,4096]{1,0:T(8,128)S(1)}, f32[64,4096]{1,0:T(8,128)S(1)}, u32[]{:S(2)}, u32[]{:S(2)}) collective-permute-start(f32[64,4096]{1,0:T(8,128)S(1)} %slice.35), channel_id=1, source_target_pairs={{0,4},{4,8},{8,12},{12,16},{16,20},{20,24},{24,28},{1,5},{5,9},{9,... | collective-permute-start | bytes 3145736 | tf_op jit(solution)/shard_map/ppermute | solution.py:13
  640.4 6.6 collective-permute-start.7
Sparse Core Ops, SparseCore 0:
  8.9 49.0 all-gather.1
  379.5 25.8 reduce-scatter.2
  640.5 26.0 reduce-scatter.4
where the time goes:
time: 734 us; the launch traced here: 729 us
  waiting for transfers between devices  265 us (36%)
  blocking collectives  120 us (16%)
  other arithmetic  95.2 us (13%)
  matrix products  94.7 us (13%)
  loops' own time  64.5 us (9%)
  local copies, waits for them, and re-layouts  57.1 us (8%)
  starting transfers between devices  18.3 us (2%)
  between operations  14 us (2%)
    ppermute x8, waiting for transfers between devices, from_behind(): lax.ppermute(value, axis, [(source, source + steps) for source in range(i...  195 us
    psum x2, blocking collectives, per_device(): gram = lax.psum(partial_gram, ('blk', 'grp'))  79.2 us
    dot_general x32, matrix products, score(): lax.dot_general(left, right, (((1,), (1,)), ((), ())), preferred_element_...  72.4 us
    reduce_sum x32, other arithmetic, score(): left_norm = jnp.sum(left_wide * left_wide, 1)  56.2 us
    all_gather x1, waiting for transfers between devices, per_device(): lax.all_gather(points, 'grp', axis=0, tiled=True)  50.7 us
    another operation x32, loops' own time, turn_body(): return lax.cond(flag, add, lambda state: state, carry)  43.5 us
    dynamic_slice x32, local copies, waits for them, and re-layouts, slot_pair(): pair_rows[position]  21.1 us
    dynamic_slice x32, local copies, waits for them, and re-layouts, slot_pair(): pair_cols[position]  21 us
  transfers between devices with their start and end apart: 11, of which 9 were waited for; matrix products, arithmetic and copies ran while one was open for 1% of the time, Pallas kernels for 0%

commit v1 on v0

v1 whole, which is shorter than its diff:
```python
import functools

import jax
import jax.numpy as jnp
from jax import lax
from jax.experimental import pallas as pl
from jax.experimental.pallas import tpu as pltpu
from jax.sharding import PartitionSpec as P

PTS = 512
ITERS = 2
LOG2E = 1.4426950408889634
DEAD = 65536.0
EXTRA = 16
VMEM = pltpu.VMEM
SMEM = pltpu.SMEM
HIGHEST = lax.Precision.HIGHEST


def spec(space):
    return pl.BlockSpec(memory_space=space)


def swap(value, axis, bit):
    count = lax.axis_size(axis)
    return lax.ppermute(value, axis, [(source, source ^ bit) for source in range(count)])


def from_behind(value, axis, steps):
    count = lax.axis_size(axis)
    initial, last = (max(0, -steps), min(count, count - steps))
    return lax.ppermute(value, axis, [(source, source + steps) for source in range(initial, last)])


def bits_of(count):
    bits = []
    bit = 1
    while bit < count:
        bits.append(bit)
        bit *= 2
    return bits


def gather_near(value, axis):
    held = {0: value}
    for bit in reversed(bits_of(lax.axis_size(axis))):
        for rel in list(held):
            held[rel ^ bit] = swap(held[rel], axis, bit)
    return [held[rel] for rel in range(len(held))]


def prepare_kernel(group, cap, pts, counts, rows, cols, live, start, aug, out_rows, out_cols, out_n):
    columns, total = start.shape
    width = pts.shape[1]
    blocks_dev = total // PTS
    slab = blocks_dev * group
    slots = rows.shape[0]
    member = lax.axis_index("grp")

    def local_near(block):
        return (lax.div(block, blocks_dev) ^ member) * blocks_dev + lax.rem(block, blocks_dev)

    def count_far(slot, carry):
        col = cols[slot]
        far = jnp.logical_and(slot < live[0], col >= slab)
        owner = lax.div(col - slab, blocks_dev)
        return tuple(
            old + jnp.where(jnp.logical_and(far, owner == device), 1, 0)
            for device, old in enumerate(carry)
        )

    far_counts = lax.fori_loop(0, slots, count_far, (jnp.int32(0),) * group)
    low = jnp.int32(0)
    room = jnp.int32(0)
    for device in range(group):
        low = low + jnp.where(device < member, cap - far_counts[device], 0)
        room = room + jnp.where(device == member, cap - far_counts[device], 0)

    def place(slot, carry):
        near_rank, filled = carry
        row, col = rows[slot], cols[slot]
        used = slot < live[0]
        far = col >= slab
        mine_far = jnp.logical_and(far, lax.div(col - slab, blocks_dev) == member)
        mine_near = jnp.logical_and(
            jnp.logical_not(far), jnp.logical_and(near_rank >= low, near_rank < low + room)
        )
        mine = jnp.logical_and(used, jnp.logical_or(mine_far, mine_near))

        @pl.when(mine)
        def _():
            out_rows[filled] = local_near(row)
            out_cols[filled] = jnp.where(far, slab + lax.rem(col - slab, blocks_dev), local_near(col))

        near_rank = near_rank + jnp.where(jnp.logical_and(used, jnp.logical_not(far)), 1, 0)
        return (near_rank, filled + jnp.where(mine, 1, 0))

    out_n[0] = lax.fori_loop(0, slots, place, (jnp.int32(0), jnp.int32(0)))[1]

    for block in range(blocks_dev):
        lanes = slice(block * PTS, (block + 1) * PTS)
        wide = pts[lanes, :].astype(jnp.float32)
        norm = lax.dot_general(
            jnp.ones((8, width), jnp.float32),
            wide * wide,
            (((1,), (1,)), ((), ())),
            precision=HIGHEST,
            preferred_element_type=jnp.float32,
        )[0:1, :]
        place_in = lax.broadcasted_iota(jnp.int32, (1, PTS), 1)
        level = norm * (3.0 / width * LOG2E) + jnp.where(place_in < counts[block], 0.0, DEAD)
        high = level.astype(jnp.bfloat16).astype(jnp.float32)
        rest = level - high
        middle = rest.astype(jnp.bfloat16).astype(jnp.float32)
        small = rest - middle
        which = lax.broadcasted_iota(jnp.int32, (EXTRA, PTS), 0)
        tail = jnp.where(which == 0, 1.0, 0.0)
        tail = tail + jnp.where(which == 1, high, 0.0)
        tail = tail + jnp.where(which == 2, middle, 0.0)
        tail = tail + jnp.where(which == 3, small, 0.0)
        aug[0:columns, lanes] = start[:, lanes].astype(jnp.bfloat16)
        aug[columns : columns + EXTRA, lanes] = tail.astype(jnp.bfloat16)


def prepare(points, counts, rows, cols, live, start, group, cap):
    columns, total = start.shape
    return pl.pallas_call(
        functools.partial(prepare_kernel, group, cap),
        out_shape=(
            jax.ShapeDtypeStruct((columns + EXTRA, total), jnp.bfloat16),
            jax.ShapeDtypeStruct((cap,), jnp.int32),
            jax.ShapeDtypeStruct((cap,), jnp.int32),
            jax.ShapeDtypeStruct((1,), jnp.int32),
        ),
        in_specs=[spec(VMEM), spec(SMEM), spec(SMEM), spec(SMEM), spec(SMEM), spec(VMEM)],
        out_specs=(spec(VMEM), spec(SMEM), spec(SMEM), spec(SMEM)),
        compiler_params=pltpu.CompilerParams(vmem_limit_bytes=32 * 2**20),
        name="prepare",
    )(points, counts, rows, cols, live, start)


def message_rels(group):
    groups = [[0]]
    for bit in bits_of(group):
        groups.append([rel for rel in range(group) if rel & bit and rel % bit == 0])
    return groups


def product_shapes(group, blocks_dev, height):
    shapes = [
        jax.ShapeDtypeStruct((len(rels) * blocks_dev, height, PTS), jnp.float32)
        for rels in message_rels(group)
    ]
    shapes.append(jax.ShapeDtypeStruct((blocks_dev, height, PTS), jnp.float32))
    return shapes


def write_products(group, blocks_dev, acc, outs):
    for rels, out in zip(message_rels(group), outs[:-1]):
        for index, rel in enumerate(rels):
            for block in range(blocks_dev):
                out[index * blocks_dev + block] = acc[rel * blocks_dev + block]
    for block in range(blocks_dev):
        outs[-1][block] = acc[group * blocks_dev + block]


def add_products(acc, tile, u_row, u_col, row, col):
    height = acc.shape[1]
    to_row = lax.dot_general(
        u_col, tile, (((1,), (1,)), ((), ())), preferred_element_type=jnp.float32
    )
    acc[row] += to_row[:height]
    to_col = jnp.dot(u_row, tile, preferred_element_type=jnp.float32)
    acc[col] += to_col[:height]


def first_kernel(group, refs):
    pieces = group + 1
    n_ref, rows, cols, counts = refs[:4]
    pts = refs[4 : 4 + pieces]
    augs = refs[4 + pieces : 4 + 2 * pieces]
    tiles_out = refs[4 + 2 * pieces]
    messages = len(message_rels(group)) + 1
    outs = refs[5 + 2 * pieces : 5 + 2 * pieces + messages]
    window, kept, u_win, level_row, level_col, acc, in_sems, out_sems = refs[5 + 2 * pieces + messages :]
    held = pts[0].shape[0]
    width = pts[0].shape[1]
    blocks_dev = held // PTS
    columns = augs[0].shape[0] - EXTRA
    height = acc.shape[1]
    copies = [
        pltpu.make_async_copy(
            pts[piece], window.at[pl.ds(piece * held, held), :], in_sems.at[piece]
        )
        for piece in range(pieces)
    ]
    for copy in copies:
        copy.start()

    pick = lax.broadcasted_iota(jnp.int32, (EXTRA, 128), 0)
    pick = jnp.where(jnp.logical_and(pick >= 1, pick <= 3), 1.0, 0.0).astype(jnp.bfloat16)
    for piece in range(pieces):
        for block in range(blocks_dev):
            place = piece * blocks_dev + block
            lanes = slice(block * PTS, (block + 1) * PTS)
            u_win[place] = augs[piece][:, lanes]
            tail = augs[piece][columns : columns + EXTRA, lanes]
            if piece < group:
                level_col[place] = lax.dot_general(
                    tail, pick, (((0,), (0,)), ((), ())), preferred_element_type=jnp.float32
                )
            tail = tail.astype(jnp.float32)
            level_row[place] = jnp.broadcast_to(tail[1:2] + tail[2:3] + tail[3:4], (8, PTS))
            acc[place] = jnp.zeros((height, PTS), jnp.float32)
    for block in range(blocks_dev):
        lanes = slice(block * PTS, (block + 1) * PTS)
        place_in = lax.broadcasted_iota(jnp.int32, (columns, PTS), 1)
        own = augs[0][0:columns, lanes].astype(jnp.float32)
        acc[block, 0:columns] = jnp.where(place_in < counts[block], own, 0.0)
        acc[block, columns:height] = jnp.ones((height - columns, PTS), jnp.float32)
    for copy in copies:
        copy.wait()

    n = n_ref[0]
    step = 256
    scale = 6.0 / width * LOG2E

    def body(index, carry):
        row, col = rows[index], cols[index]
        right = window[pl.ds(pl.multiple_of(col * PTS, PTS), PTS), :]
        right_level = level_row[col][0:1, :]
        for part in range(PTS // step):
            left = window[pl.ds(pl.multiple_of(row * PTS + part * step, step), step), :]
            cross = lax.dot_general(
                left, right, (((1,), (1,)), ((), ())), preferred_element_type=jnp.float32
            )
            left_level = level_col[row, part * step : (part + 1) * step, :]
            left_level = jnp.concatenate([left_level] * (PTS // 128), axis=1)
            value = jnp.exp2(cross * scale - left_level - right_level)
            kept[index, part * step : (part + 1) * step, :] = value.astype(jnp.bfloat16)
        pltpu.make_async_copy(kept.at[index], tiles_out.at[index], out_sems.at[index]).start()
        add_products(acc, kept[index], u_win[row], u_win[col], row, col)
        return carry

    lax.fori_loop(0, n, body, 0)
    write_products(group, blocks_dev, acc, outs)

    def finish(index, carry):
        pltpu.make_async_copy(kept.at[index], tiles_out.at[index], out_sems.at[index]).wait()
        return carry

    lax.fori_loop(0, n, finish, 0)


def first_turn(n, rows, cols, counts, pts, augs, group, cap):
    held, width = pts[0].shape
    blocks_dev = held // PTS
    places = (group + 1) * blocks_dev
    tall = augs[0].shape[0]
    height = tall - EXTRA + 8
    pieces = group + 1
    shapes = [jax.ShapeDtypeStruct((cap, PTS, PTS), jnp.bfloat16)]
    shapes += product_shapes(group, blocks_dev, height)

    def kernel(*refs):
        first_kernel(group, refs)

    return pl.pallas_call(
        kernel,
        out_shape=tuple(shapes),
        in_specs=[spec(SMEM)] * 4 + [spec(pl.ANY)] * pieces + [spec(VMEM)] * pieces,
        out_specs=(spec(pl.ANY),) + (spec(VMEM),) * (len(shapes) - 1),
        scratch_shapes=[
            VMEM((pieces * held, width), jnp.bfloat16),
            VMEM((cap, PTS, PTS), jnp.bfloat16),
            VMEM((places, tall, PTS), jnp.bfloat16),
            VMEM((places, 8, PTS), jnp.float32),
            VMEM((group * blocks_dev, PTS, 128), jnp.float32),
            VMEM((places, height, PTS), jnp.float32),
            pltpu.SemaphoreType.DMA((pieces,)),
            pltpu.SemaphoreType.DMA((cap,)),
        ],
        compiler_params=pltpu.CompilerParams(vmem_limit_bytes=48 * 2**20),
        name="first_turn",
    )(n, rows, cols, counts, *pts, *augs)


def scale_kernel(blocks_dev, has_degree, refs):
    degree_in = None if has_degree else refs[0]
    parts = refs[:-3] if has_degree else refs[1:-2]
    if has_degree:
        z_out, gram_out, degree_out = refs[-3:]
    else:
        z_out, gram_out = refs[-2:]
    columns = z_out.shape[0]
    gram = jnp.zeros((columns, columns), jnp.float32)
    for block in range(blocks_dev):
        lanes = slice(block * PTS, (block + 1) * PTS)
        total = parts[0][block]
        for part in parts[1:]:
            total = total + part[block]
        if has_degree:
            degree = total[columns : columns + 1, :]
            degree_out[:, lanes] = jnp.broadcast_to(degree, (8, PTS))
        else:
            degree = degree_in[0:1, lanes]
        z = total[0:columns] / degree
        z_out[:, lanes] = z
        gram = gram + lax.dot_general(
            z, z, (((1,), (1,)), ((), ())), precision=HIGHEST, preferred_element_type=jnp.float32
        )
    gram_out[...] = gram


def scaled_gram(parts, degree, columns):
    blocks_dev = parts[0].shape[0]
    for part in parts:
        blocks_dev = min(blocks_dev, part.shape[0])
    total = blocks_dev * PTS
    shapes = [
        jax.ShapeDtypeStruct((columns, total), jnp.float32),
        jax.ShapeDtypeStruct((columns, columns), jnp.float32),
    ]
    if degree is None:
        shapes.append(jax.ShapeDtypeStruct((8, total), jnp.float32))
        operands = list(parts)
    else:
        operands = [degree] + list(parts)

    def kernel(*refs):
        scale_kernel(blocks_dev, degree is None, refs)

    return pl.pallas_call(
        kernel,
        out_shape=tuple(shapes),
        in_specs=[spec(VMEM)] * len(operands),
        out_specs=(spec(VMEM),) * len(shapes),
        compiler_params=pltpu.CompilerParams(vmem_limit_bytes=32 * 2**20),
        name="scaled_gram",
    )(*operands)


def inverse_factor(gram):
    size = gram.shape[0]
    row_id = lax.broadcasted_iota(jnp.int32, (size, size), 0)
    col_id = lax.broadcasted_iota(jnp.int32, (size, size), 1)
    eye = jnp.where(row_id == col_id, 1.0, 0.0)
    whole = jnp.concatenate([gram, eye], axis=1)
    groups = [whole[8 * g : 8 * g + 8, :] for g in range(size // 8)]
    within = lax.broadcasted_iota(jnp.int32, (8, 2 * size), 0)
    for j in range(size):
        g, r = divmod(j, 8)
        top = groups[g][r : r + 1, :]
        factor = lax.rsqrt(top[:, j : j + 1])
        top = top * factor
        for other in range(g, size // 8):
            column = groups[other][:, j : j + 1] * factor
            fresh = groups[other] - column * top
            if other == g:
                fresh = jnp.where(within > r, fresh, jnp.where(within == r, top, groups[g]))
            groups[other] = fresh
    return jnp.concatenate(groups, axis=0)[:, size : 2 * size]


def second_kernel(group, refs):
    pieces = group + 1
    n_ref, rows, cols, counts, gram = refs[:5]
    zs = refs[5 : 5 + pieces]
    tiles = refs[5 + pieces]
    messages = len(message_rels(group)) + 1
    outs = refs[6 + pieces : 6 + pieces + messages]
    kept, u_win, acc, sems = refs[6 + pieces + messages :]
    columns, held = zs[0].shape
    blocks_dev = held // PTS
    n = n_ref[0]

    def fetch(index):
        return pltpu.make_async_copy(tiles.at[index], kept.at[index], sems.at[index])

    def begin(index, carry):
        fetch(index).start()
        return carry

    lax.fori_loop(0, n, begin, 0)
    inverse = inverse_factor(gram[...])
    for piece in range(pieces):
        for block in range(blocks_dev):
            place = piece * blocks_dev + block
            vec = jnp.dot(
                inverse,
                zs[piece][:, block * PTS : (block + 1) * PTS],
                precision=HIGHEST,
                preferred_element_type=jnp.float32,
            ).astype(jnp.bfloat16)
            u_win[place] = vec
            if piece == 0:
                place_in = lax.broadcasted_iota(jnp.int32, (columns, PTS), 1)
                acc[place] = jnp.where(place_in < counts[block], vec.astype(jnp.float32), 0.0)
            else:
                acc[place] = jnp.zeros((columns, PTS), jnp.float32)

    def body(index, carry):
        row, col = rows[index], cols[index]
        fetch(index).wait()
        add_products(acc, kept[index], u_win[row], u_win[col], row, col)
        return carry

    lax.fori_loop(0, n, body, 0)
    write_products(group, blocks_dev, acc, outs)


def next_turn(n, rows, cols, counts, gram, zs, tiles, group, cap):
    columns, held = zs[0].shape
    blocks_dev = held // PTS
    pieces = group + 1
    places = pieces * blocks_dev
    shapes = product_shapes(group, blocks_dev, columns)

    def kernel(*refs):
        second_kernel(group, refs)

    return pl.pallas_call(
        kernel,
        out_shape=tuple(shapes),
        in_specs=[spec(SMEM)] * 4 + [spec(VMEM)] * (1 + pieces) + [spec(pl.ANY)],
        out_specs=(spec(VMEM),) * len(shapes),
        scratch_shapes=[
            VMEM((cap, PTS, PTS), jnp.bfloat16),
            VMEM((places, columns, PTS), jnp.bfloat16),
            VMEM((places, columns, PTS), jnp.float32),
            pltpu.SemaphoreType.DMA((cap,)),
        ],
        compiler_params=pltpu.CompilerParams(vmem_limit_bytes=40 * 2**20),
        name="next_turn",
    )(n, rows, cols, counts, gram, *zs, tiles)


def embed_kernel(gram, z, out):
    out[...] = jnp.dot(
        inverse_factor(gram[...]), z[...], precision=HIGHEST, preferred_element_type=jnp.float32
    )


def embedding(gram, z):
    return pl.pallas_call(
        embed_kernel,
        out_shape=jax.ShapeDtypeStruct(z.shape, jnp.float32),
        in_specs=[spec(VMEM)] * 2,
        out_specs=spec(VMEM),
        name="embedding",
    )(gram, z)


def sum_products(messages, group, blocks_dev):
    rels = message_rels(group)
    parts = {}
    for names, message in zip(rels[1:], messages[1:-1]):
        for index, rel in enumerate(names):
            parts[rel] = [message[index * blocks_dev : (index + 1) * blocks_dev]]
    final = [messages[0], from_behind(messages[-1], "blk", 1)]
    for bit, names, message in zip(bits_of(group), rels[1:], messages[1:-1]):
        if bit > 1:
            message = jnp.concatenate([sum(parts[rel][1:], parts[rel][0]) for rel in names], 0)
        got = swap(message, "grp", bit)
        for index, rel in enumerate(names):
            target = rel ^ bit
            if target == 0:
                final.append(got)
            else:
                parts[target].append(got[index * blocks_dev : (index + 1) * blocks_dev])
    return final


def all_sum(value, axes):
    for axis in axes:
        for bit in bits_of(lax.axis_size(axis)):
            value = value + swap(value, axis, bit)
    return value


def per_device(points, counts, pair_rows, pair_cols, pair_live, start):
    group = lax.axis_size("grp")
    blocks_dev = counts.shape[0]
    columns = start.shape[0]
    slots = pair_rows.shape[0]
    cap = max(-(-slots // group), blocks_dev * blocks_dev * group)
    pts = gather_near(points, "grp") + [from_behind(points, "blk", -1)]
    aug, rows, cols, n = prepare(
        points, counts, pair_rows, pair_cols, pair_live, start, group, cap
    )
    augs = gather_near(aug, "grp") + [from_behind(aug, "blk", -1)]
    tiles, *messages = first_turn(n, rows, cols, counts, pts, augs, group, cap)
    z, gram, degree = scaled_gram(sum_products(messages, group, blocks_dev), None, columns)
    for turn in range(1, ITERS):
        zs = gather_near(z, "grp") + [from_behind(z, "blk", -1)]
        gram = all_sum(gram, ("grp", "blk"))
        messages = next_turn(n, rows, cols, counts, gram, zs, tiles, group, cap)
        z, gram = scaled_gram(sum_products(messages, group, blocks_dev), degree, columns)
    return embedding(all_sum(gram, ("grp", "blk")), z)


def solution(mesh):
    in_specs = (
        P(("blk", "grp"), None),
        P(("blk", "grp")),
        P("blk"),
        P("blk"),
        P("blk"),
        P(None, ("blk", "grp")),
    )
    out_specs = P(None, ("blk", "grp"))
    return jax.shard_map(
        per_device, mesh=mesh, in_specs=in_specs, out_specs=out_specs, check_vma=False
    )
```

time: 734 us -> 176 us (0.24)
  waiting for transfers between devices: 265 us -> 78.4 us
  blocking collectives: 120 us -> 0 us
  matrix products: 94.7 us -> 0 us
  other arithmetic: 95.2 us -> 0.74 us
  loops' own time: 64.5 us -> 0 us
  Pallas kernels: 0 us -> 48.1 us
  local copies, waits for them, and re-layouts: 57.1 us -> 10.1 us
  starting transfers between devices: 18.3 us -> 38.1 us
  between operations: 14 us -> 0.86 us
    ppermute x8 -> x5, waiting for transfers between devices: 195 us -> 14.4 us  [from_behind(): lax.ppermute(value, axis, [(source, source + steps) for source in range(i...]
    dot_general x98 -> x0, matrix products: 91.3 us -> none  [the longest x32 72.4 us: score(): lax.dot_general(left, right, (((1,), (1,)), ((), ())), preferred_element_...]
    psum x2 -> x0, blocking collectives: 79.2 us -> none  [per_device(): gram = lax.psum(partial_gram, ('blk', 'grp'))]
    another operation x34 -> x0, loops' own time: 64.5 us -> none  [the longest x32 43.5 us: turn_body(): return lax.cond(flag, add, lambda state: state, carry)]
    ppermute x0 -> x23, waiting for transfers between devices: none -> 64.1 us  [swap(): lax.ppermute(value, axis, [(source, source ^ bit) for source in range(cou...]
    reduce_sum x32 -> x0, other arithmetic: 56.2 us -> none  [score(): left_norm = jnp.sum(left_wide * left_wide, 1)]
    all_gather x1 -> x0, waiting for transfers between devices: 50.7 us -> none  [per_device(): lax.all_gather(points, 'grp', axis=0, tiled=True)]
    pallas_call x0 -> x6, Pallas kernels: none -> 48.1 us  [the longest x1 19.3 us: first_turn(): pl.pallas_call(kernel, out_shape=tuple(shapes), in_specs=[spec(SMEM)] * 4...]
  transfers between devices with their start and end apart: 11 -> 28, of which waited for: 9 -> 21; matrix products, arithmetic and copies ran while one was open for 1% -> 0% of each run, Pallas kernels for 0% -> 3%
where the time goes in v1:
time: 176 us
  waiting for transfers between devices  78.4 us (45%)
  Pallas kernels  48.1 us (27%)
  starting transfers between devices  38.1 us (22%)
  local copies, waits for them, and re-layouts  10.1 us (6%)
    ppermute x23, waiting for transfers between devices, swap(): lax.ppermute(value, axis, [(source, source ^ bit) for source in range(cou...  64.1 us
    ppermute x23, starting transfers between devices, swap(): lax.ppermute(value, axis, [(source, source ^ bit) for source in range(cou...  31.6 us
    pallas_call x1, Pallas kernels, first_turn(): pl.pallas_call(kernel, out_shape=tuple(shapes), in_specs=[spec(SMEM)] * 4...  19.3 us
    pallas_call x1, Pallas kernels, next_turn(): pl.pallas_call(kernel, out_shape=tuple(shapes), in_specs=[spec(SMEM)] * 4...  14.7 us
    ppermute x5, waiting for transfers between devices, from_behind(): lax.ppermute(value, axis, [(source, source + steps) for source in range(i...  14.4 us
    unnamed x24, local copies, waits for them, and re-layouts  10.1 us
    pallas_call x1, Pallas kernels, embedding(): pl.pallas_call(embed_kernel, out_shape=jax.ShapeDtypeStruct(z.shape, jnp....  7.44 us
    ppermute x5, starting transfers between devices, from_behind(): lax.ppermute(value, axis, [(source, source + steps) for source in range(i...  6.45 us
  transfers between devices with their start and end apart: 28, of which 21 were waited for; matrix products, arithmetic and copies ran while one was open for 0% of the time, Pallas kernels for 3%

profile of v1, /device:TPU:0, one launch (start us, length us, event | category | flops | bytes accessed | tf_op | source)
XLA Modules:
  0.0 176.3 jit_solution(5510727367930625211)
XLA Ops:
  0.0 2.9 %collective-permute-start.1 = (bf16[1024,768]{1,0:T(8,128)(2,1)}, bf16[1024,768]{1,0:T(8,128)(2,1)S(1)}, u32[]{:S(2)}, u32[]{:S(2)}) collective-permute-start(bf16[1024,768]{1,0:T(8,128)(2,1)} %refs_4_.1), channel_id=1, source_target_pairs={{0,2},{1,3},{2,0},{3,1},{4,6},{5,7},{6,4},{7,5},{8,10},{9,11},{10,... | collective-permute-start | bytes 4718600 | tf_op jit(solution)/shard_map/ppermute | solution.py:26
  2.9 1.3 collective-permute-start.3
  4.2 33.3 %collective-permute-done.1.refs_6_ = bf16[1024,768]{1,0:T(8,128)(2,1)S(1)} collective-permute-done((bf16[1024,768]{1,0:T(8,128)(2,1)}, bf16[1024,768]{1,0:T(8,128)(2,1)S(1)}, u32[]{:S(2)}, u32[]{:S(2)}) %collective-permute-start.1) | collective-permute-done | bytes 1572896 | tf_op jit(solution)/shard_map/ppermute | solution.py:26
  38.2 1.4 copy-done.1
  39.6 0.9 copy-done.4
  40.6 0.7 copy-done.5
  41.2 0.7 copy-done.7
  41.9 0.7 copy-done.8
  42.5 5.8 %prepare.1 = (bf16[80,1024]{1,0:T(8,128)(2,1)S(1)}, s32[16]{0:T(128)S(1)}, s32[16]{0:T(128)S(1)}, s32[1]{0:T(128)}) custom-call(bf16[1024,768]{1,0:T(8,128)(2,1)S(1)} %copy-done.1, s32[2]{0:T(128)S(1)} %copy-done.5, s32[64]{0:T(128)S(1)} %copy-done.7, s32[64]{0:T(128)S(1)} %copy-done.8, s32[1]{0:T(128)S(6)} %copy.7.live, f32[64,1024]{1,0:T(8,128)S(1)} %copy-done.4), custom_call_target="tpu_custom_call" | custom-call | tf_op jit(solution)/shard_map/prepare/pallas_call | solution.py:127
  48.3 1.3 collective-permute-start.7
  49.6 1.8 %collective-permute-start.5 = (bf16[80,1024]{1,0:T(8,128)(2,1)S(1)}, bf16[80,1024]{1,0:T(8,128)(2,1)S(1)}, u32[]{:S(2)}, u32[]{:S(2)}) collective-permute-start(bf16[80,1024]{1,0:T(8,128)(2,1)S(1)} %get-tuple-element.26.refs_9_), channel_id=1, source_target_pairs={{0,2},{1,3},{2,0},{3,1},{4,6},{5,7},{6,4},{7,5},{8,10},{9,11},{10,... | collective-permute-start | bytes 491528 | tf_op jit(solution)/shard_map/ppermute | solution.py:26
  51.4 5.4 %collective-permute-done.7.refs_13_ = bf16[80,1024]{1,0:T(8,128)(2,1)S(1)} collective-permute-done((bf16[80,1024]{1,0:T(8,128)(2,1)S(1)}, bf16[80,1024]{1,0:T(8,128)(2,1)S(1)}, u32[]{:S(2)}, u32[]{:S(2)}) %collective-permute-start.7) | collective-permute-done | bytes 163872 | tf_op jit(solution)/shard_map/ppermute | solution.py:32
  56.9 0.0 collective-permute-start.4
  56.9 0.0 collective-permute-done.5.refs_11_
  56.9 0.5 collective-permute-start.6
  57.4 0.9 collective-permute-done.4.refs_10_
  58.3 0.2 collective-permute-done.6.refs_12_
  58.5 0.0 collective-permute-done.refs_5_
  58.5 0.0 collective-permute-done.3.refs_8_
  58.5 1.2 copy-done.10
  59.7 0.5 copy-done.11
  60.2 19.3 %first_turn.1 = (bf16[16,512,512]{2,1,0:T(8,128)(2,1)}, f32[2,72,512]{2,1,0:T(8,128)S(1)}, f32[4,72,512]{2,1,0:T(8,128)S(1)}, f32[2,72,512]{2,1,0:T(8,128)S(1)}, f32[2,72,512]{2,1,0:T(8,128)S(1)}) custom-call(s32[1]{0:T(128)} %get-tuple-element.23.refs_0_, s32[16]{0:T(128)S(1)} %get-tuple-element.24.refs_1_, s32[16]{0:T(128)S(1)} %get-tuple-element.25.refs_2_, ...), custom_call_target="tpu_custom_call" | custom-call | tf_op jit(solution)/shard_map/first_turn/pallas_call | solution.py:268
  79.6 0.3 collective-permute-start.9
  79.9 1.3 collective-permute-start.8
  81.2 0.4 collective-permute-done.9.refs_2_
  81.7 1.8 %collective-permute-start.10 = (f32[2,72,512]{2,1,0:T(8,128)S(1)}, f32[2,72,512]{2,1,0:T(8,128)S(1)}, u32[]{:S(2)}, u32[]{:S(2)}) collective-permute-start(f32[2,72,512]{2,1,0:T(8,128)S(1)} %slice_add_fusion), channel_id=1, source_target_pairs={{0,2},{1,3},{2,0},{3,1},{4,6},{5,7},{6,4},{7,5},{8,10},{9,11},{10,... | collective-permute-start | bytes 884744 | tf_op jit(solution)/shard_map/ppermute | solution.py:26
  83.5 4.7 %collective-permute-done.8.refs_1_ = f32[2,72,512]{2,1,0:T(8,128)S(1)} collective-permute-done((f32[2,72,512]{2,1,0:T(8,128)S(1)}, f32[2,72,512]{2,1,0:T(8,128)S(1)}, u32[]{:S(2)}, u32[]{:S(2)}) %collective-permute-start.8) | collective-permute-done | bytes 294944 | tf_op jit(solution)/shard_map/ppermute | solution.py:32
  88.1 2.8 %collective-permute-done.10.refs_3_ = f32[2,72,512]{2,1,0:T(8,128)S(1)} collective-permute-done((f32[2,72,512]{2,1,0:T(8,128)S(1)}, f32[2,72,512]{2,1,0:T(8,128)S(1)}, u32[]{:S(2)}, u32[]{:S(2)}) %collective-permute-start.10) | collective-permute-done | bytes 294944 | tf_op jit(solution)/shard_map/ppermute | solution.py:26
  91.0 0.4 scaled_gram.2
  91.4 1.8 %collective-permute-start.17 = (f32[64,1024]{1,0:T(8,128)S(1)}, f32[64,1024]{1,0:T(8,128)S(1)}, u32[]{:S(2)}, u32[]{:S(2)}) collective-permute-start(f32[64,1024]{1,0:T(8,128)S(1)} %get-tuple-element.33.refs_5_), channel_id=1, source_target_pairs={{0,2},{1,3},{2,0},{3,1},{4,6},{5,7},{6,4},{7,5},{8,10},{9,11},{10,... | collective-permute-start | bytes 786440 | tf_op jit(solution)/shard_map/ppermute | solution.py:26
  93.1 1.3 collective-permute-start.19
  94.4 0.1 collective-permute-start.16
  94.5 4.6 %collective-permute-done.17.refs_7_ = f32[64,1024]{1,0:T(8,128)S(1)} collective-permute-done((f32[64,1024]{1,0:T(8,128)S(1)}, f32[64,1024]{1,0:T(8,128)S(1)}, u32[]{:S(2)}, u32[]{:S(2)}) %collective-permute-start.17) | collective-permute-done | bytes 262176 | tf_op jit(solution)/shard_map/ppermute | solution.py:26
  99.1 0.5 collective-permute-start.11
  99.6 1.1 collective-permute-done.11
  100.7 1.7 collective-permute-start.12
  102.4 2.2 %collective-permute-done.12 = f32[64,64]{1,0:T(8,128)S(1)} collective-permute-done((f32[64,64]{1,0:T(8,128)S(1)}, f32[64,64]{1,0:T(8,128)S(1)}, u32[]{:S(2)}, u32[]{:S(2)}) %collective-permute-start.12) | collective-permute-done | bytes 16416 | tf_op jit(solution)/shard_map/ppermute | solution.py:26
  104.6 2.1 %collective-permute-start.13 = (f32[64,64]{1,0:T(8,128)S(1)}, f32[64,64]{1,0:T(8,128)S(1)}, u32[]{:S(2)}, u32[]{:S(2)}) collective-permute-start(f32[64,64]{1,0:T(8,128)S(1)} %add.38), channel_id=1, source_target_pairs={{0,4},{4,0},{8,12},{12,8},{16,20},{20,16},{24,28},{28,24},{1,5},{5... | collective-permute-start | bytes 49160 | tf_op jit(solution)/shard_map/ppermute | solution.py:26
  106.8 1.9 %collective-permute-done.13 = f32[64,64]{1,0:T(8,128)S(1)} collective-permute-done((f32[64,64]{1,0:T(8,128)S(1)}, f32[64,64]{1,0:T(8,128)S(1)}, u32[]{:S(2)}, u32[]{:S(2)}) %collective-permute-start.13) | collective-permute-done | bytes 16416 | tf_op jit(solution)/shard_map/ppermute | solution.py:26
  108.7 3.6 %collective-permute-start.14 = (f32[64,64]{1,0:T(8,128)S(1)}, f32[64,64]{1,0:T(8,128)S(1)}, u32[]{:S(2)}, u32[]{:S(2)}) collective-permute-start(f32[64,64]{1,0:T(8,128)S(1)} %add.39), channel_id=1, source_target_pairs={{0,8},{4,12},{8,0},{12,4},{16,24},{20,28},{24,16},{28,20},{1,9},{5... | collective-permute-start | bytes 49160 | tf_op jit(solution)/shard_map/ppermute | solution.py:26
  112.2 1.9 %collective-permute-done.14 = f32[64,64]{1,0:T(8,128)S(1)} collective-permute-done((f32[64,64]{1,0:T(8,128)S(1)}, f32[64,64]{1,0:T(8,128)S(1)}, u32[]{:S(2)}, u32[]{:S(2)}) %collective-permute-start.14) | collective-permute-done | bytes 16416 | tf_op jit(solution)/shard_map/ppermute | solution.py:26
  114.1 3.1 %collective-permute-start.15 = (f32[64,64]{1,0:T(8,128)S(1)}, f32[64,64]{1,0:T(8,128)S(1)}, u32[]{:S(2)}, u32[]{:S(2)}) collective-permute-start(f32[64,64]{1,0:T(8,128)S(1)} %add.40), channel_id=1, source_target_pairs={{0,16},{4,20},{8,24},{12,28},{16,0},{20,4},{24,8},{28,12},{1,17},{... | collective-permute-start | bytes 49160 | tf_op jit(solution)/shard_map/ppermute | solution.py:26
  117.2 1.9 %collective-permute-done.15 = f32[64,64]{1,0:T(8,128)S(1)} collective-permute-done((f32[64,64]{1,0:T(8,128)S(1)}, f32[64,64]{1,0:T(8,128)S(1)}, u32[]{:S(2)}, u32[]{:S(2)}) %collective-permute-start.15) | collective-permute-done | bytes 16416 | tf_op jit(solution)/shard_map/ppermute | solution.py:26
  119.2 3.4 %copy-done = bf16[16,512,512]{2,1,0:T(8,128)(2,1)S(1)} copy-done((bf16[16,512,512]{2,1,0:T(8,128)(2,1)S(1)}, bf16[16,512,512]{2,1,0:T(8,128)(2,1)}, u32[]{:S(2)}) %copy-start) | copy-done | bytes 8388632
  122.5 14.7 %next_turn.1 = (f32[2,64,512]{2,1,0:T(8,128)S(1)}, f32[4,64,512]{2,1,0:T(8,128)S(1)}, f32[2,64,512]{2,1,0:T(8,128)S(1)}, f32[2,64,512]{2,1,0:T(8,128)S(1)}) custom-call(s32[1]{0:T(128)} %get-tuple-element.23.refs_0_, s32[16]{0:T(128)S(1)} %get-tuple-element.24.refs_1_, s32[16]{0:T(128)S(1)} %get-tuple-element.25.refs_2_, s32[2]{0:T(128)S(1)} %copy-done.6, ...), custom_call_target="tpu_custom_call" | custom-call | tf_op jit(solution)/shard_map/next_turn/pallas_call | solution.py:422
  137.3 0.1 collective-permute-start.21
  137.3 1.3 collective-permute-start.20
  138.7 0.6 collective-permute-done.21.refs_3_
  139.3 1.6 collective-permute-start.22
  140.9 4.3 %collective-permute-done.20.refs_2_ = f32[2,64,512]{2,1,0:T(8,128)S(1)} collective-permute-done((f32[2,64,512]{2,1,0:T(8,128)S(1)}, f32[2,64,512]{2,1,0:T(8,128)S(1)}, u32[]{:S(2)}, u32[]{:S(2)}) %collective-permute-start.20) | collective-permute-done | bytes 262176 | tf_op jit(solution)/shard_map/ppermute | solution.py:32
  145.1 2.6 %collective-permute-done.22.refs_4_ = f32[2,64,512]{2,1,0:T(8,128)S(1)} collective-permute-done((f32[2,64,512]{2,1,0:T(8,128)S(1)}, f32[2,64,512]{2,1,0:T(8,128)S(1)}, u32[]{:S(2)}, u32[]{:S(2)}) %collective-permute-start.22) | collective-permute-done | bytes 262176 | tf_op jit(solution)/shard_map/ppermute | solution.py:26
  147.7 0.4 scaled_gram.3
  148.1 0.7 copy-done.3
  148.8 1.2 collective-permute-done.23
  150.0 1.5 collective-permute-start.24
  151.5 2.4 %collective-permute-done.24 = f32[64,64]{1,0:T(8,128)S(1)} collective-permute-done((f32[64,64]{1,0:T(8,128)S(1)}, f32[64,64]{1,0:T(8,128)S(1)}, u32[]{:S(2)}, u32[]{:S(2)}) %collective-permute-start.24) | collective-permute-done | bytes 16416 | tf_op jit(solution)/shard_map/ppermute | solution.py:26
  153.9 2.6 %collective-permute-start.25 = (f32[64,64]{1,0:T(8,128)S(1)}, f32[64,64]{1,0:T(8,128)S(1)}, u32[]{:S(2)}, u32[]{:S(2)}) collective-permute-start(f32[64,64]{1,0:T(8,128)S(1)} %add.44), channel_id=1, source_target_pairs={{0,4},{4,0},{8,12},{12,8},{16,20},{20,16},{24,28},{28,24},{1,5},{5... | collective-permute-start | bytes 49160 | tf_op jit(solution)/shard_map/ppermute | solution.py:26
  156.5 1.9 %collective-permute-done.25 = f32[64,64]{1,0:T(8,128)S(1)} collective-permute-done((f32[64,64]{1,0:T(8,128)S(1)}, f32[64,64]{1,0:T(8,128)S(1)}, u32[]{:S(2)}, u32[]{:S(2)}) %collective-permute-start.25) | collective-permute-done | bytes 16416 | tf_op jit(solution)/shard_map/ppermute | solution.py:26
  158.4 3.1 %collective-permute-start.26 = (f32[64,64]{1,0:T(8,128)S(1)}, f32[64,64]{1,0:T(8,128)S(1)}, u32[]{:S(2)}, u32[]{:S(2)}) collective-permute-start(f32[64,64]{1,0:T(8,128)S(1)} %add.45), channel_id=1, source_target_pairs={{0,8},{4,12},{8,0},{12,4},{16,24},{20,28},{24,16},{28,20},{1,9},{5... | collective-permute-start | bytes 49160 | tf_op jit(solution)/shard_map/ppermute | solution.py:26
  161.5 1.9 %collective-permute-done.26 = f32[64,64]{1,0:T(8,128)S(1)} collective-permute-done((f32[64,64]{1,0:T(8,128)S(1)}, f32[64,64]{1,0:T(8,128)S(1)}, u32[]{:S(2)}, u32[]{:S(2)}) %collective-permute-start.26) | collective-permute-done | bytes 16416 | tf_op jit(solution)/shard_map/ppermute | solution.py:26
  163.4 2.5 %collective-permute-start.27 = (f32[64,64]{1,0:T(8,128)S(1)}, f32[64,64]{1,0:T(8,128)S(1)}, u32[]{:S(2)}, u32[]{:S(2)}) collective-permute-start(f32[64,64]{1,0:T(8,128)S(1)} %add.46), channel_id=1, source_target_pairs={{0,16},{4,20},{8,24},{12,28},{16,0},{20,4},{24,8},{28,12},{1,17},{... | collective-permute-start | bytes 49160 | tf_op jit(solution)/shard_map/ppermute | solution.py:26
  166.0 2.3 %collective-permute-done.27 = f32[64,64]{1,0:T(8,128)S(1)} collective-permute-done((f32[64,64]{1,0:T(8,128)S(1)}, f32[64,64]{1,0:T(8,128)S(1)}, u32[]{:S(2)}, u32[]{:S(2)}) %collective-permute-start.27) | collective-permute-done | bytes 16416 | tf_op jit(solution)/shard_map/ppermute | solution.py:26
  168.2 0.6 add.47.gram
  168.9 7.4 %embedding.1 = f32[64,1024]{1,0:T(8,128)} custom-call(f32[64,64]{1,0:T(8,128)} %add.47.gram, f32[64,1024]{1,0:T(8,128)} %copy-done.3), custom_call_target="tpu_custom_call" | custom-call | tf_op jit(solution)/shard_map/embedding/pallas_call | solution.py:445
  (34 shorter events, 0.2 us)
Async XLA Ops:
  0.0 60.2 %copy-start.6 = (s32[2]{0:T(128)S(1)}, s32[2]{0:T(128)}, u32[]{:S(2)}) copy-start(s32[2]{0:T(128)} %refs_3_.3) | copy-start | bytes 28
  0.0 37.5 %collective-permute-start.1 = (bf16[1024,768]{1,0:T(8,128)(2,1)}, bf16[1024,768]{1,0:T(8,128)(2,1)S(1)}, u32[]{:S(2)}, u32[]{:S(2)}) collective-permute-start(bf16[1024,768]{1,0:T(8,128)(2,1)} %refs_4_.1), channel_id=1, source_target_pairs={{0,2},{1,3},{2,0},{3,1},{4,6},{5,7},{6,4},{7,5},{8,10},{9,11},{10,... | collective-permute-start | bytes 4718600 | tf_op jit(solution)/shard_map/ppermute | solution.py:26
  2.9 55.6 %collective-permute-start = (bf16[1024,768]{1,0:T(8,128)(2,1)}, bf16[1024,768]{1,0:T(8,128)(2,1)S(1)}, u32[]{:S(2)}, u32[]{:S(2)}) collective-permute-start(bf16[1024,768]{1,0:T(8,128)(2,1)} %refs_4_.1), channel_id=1, source_target_pairs={{0,1},{1,0},{2,3},{3,2},{4,5},{5,4},{6,7},{7,6},{8,9},{9,8},{10,11... | collective-permute-start | bytes 4718600 | tf_op jit(solution)/shard_map/ppermute | solution.py:26
  2.9 55.6 %collective-permute-start.3 = (bf16[1024,768]{1,0:T(8,128)(2,1)}, bf16[1024,768]{1,0:T(8,128)(2,1)S(1)}, u32[]{:S(2)}, u32[]{:S(2)}) collective-permute-start(bf16[1024,768]{1,0:T(8,128)(2,1)} %refs_4_.1), channel_id=1, source_target_pairs={{4,0},{8,4},{12,8},{16,12},{20,16},{24,20},{28,24},{5,1},{9,5},{13... | collective-permute-start | bytes 4718600 | tf_op jit(solution)/shard_map/ppermute | solution.py:32
  37.5 21.0 %copy-start.9 = (bf16[1024,768]{1,0:T(8,128)(2,1)}, bf16[1024,768]{1,0:T(8,128)(2,1)S(1)}, u32[]{:S(2)}) copy-start(bf16[1024,768]{1,0:T(8,128)(2,1)S(1)} %collective-permute-done.1.refs_6_) | copy-start | bytes 4718596
  37.5 21.0 %collective-permute-start.2 = (bf16[1024,768]{1,0:T(8,128)(2,1)S(1)}, bf16[1024,768]{1,0:T(8,128)(2,1)S(1)}, u32[]{:S(2)}, u32[]{:S(2)}) collective-permute-start(bf16[1024,768]{1,0:T(8,128)(2,1)S(1)} %collective-permute-done.1.refs_6_), channel_id=1, source_target_pairs={{0,1},{1,0},{2,3},{3,2},{4,5},{5,4},{6,7},{7,6},{8,9},{9,8},{10,11... | collective-permute-start | bytes 4718600 | tf_op jit(solution)/shard_map/ppermute | solution.py:26
  38.2 1.4 copy-start.1
  39.6 0.9 copy-start.4
  40.6 0.7 copy-start.5
  41.2 0.7 copy-start.7
  41.9 0.7 copy-start.8
  42.5 17.7 %copy-start.2 = (bf16[1024,768]{1,0:T(8,128)(2,1)S(1)}, bf16[1024,768]{1,0:T(8,128)(2,1)}, u32[]{:S(2)}) copy-start(bf16[1024,768]{1,0:T(8,128)(2,1)} %refs_4_.1) | copy-start | bytes 4718596
  48.3 8.5 %collective-permute-start.7 = (bf16[80,1024]{1,0:T(8,128)(2,1)S(1)}, bf16[80,1024]{1,0:T(8,128)(2,1)S(1)}, u32[]{:S(2)}, u32[]{:S(2)}) collective-permute-start(bf16[80,1024]{1,0:T(8,128)(2,1)S(1)} %get-tuple-element.26.refs_9_), channel_id=1, source_target_pairs={{4,0},{8,4},{12,8},{16,12},{20,16},{24,20},{28,24},{5,1},{9,5},{13... | collective-permute-start | bytes 491528 | tf_op jit(solution)/shard_map/ppermute | solution.py:32
  49.6 7.2 %collective-permute-start.5 = (bf16[80,1024]{1,0:T(8,128)(2,1)S(1)}, bf16[80,1024]{1,0:T(8,128)(2,1)S(1)}, u32[]{:S(2)}, u32[]{:S(2)}) collective-permute-start(bf16[80,1024]{1,0:T(8,128)(2,1)S(1)} %get-tuple-element.26.refs_9_), channel_id=1, source_target_pairs={{0,2},{1,3},{2,0},{3,1},{4,6},{5,7},{6,4},{7,5},{8,10},{9,11},{10,... | collective-permute-start | bytes 491528 | tf_op jit(solution)/shard_map/ppermute | solution.py:26
  56.9 1.4 collective-permute-start.4
  56.9 1.6 collective-permute-start.6
  58.5 1.2 copy-start.10
  58.5 1.7 copy-start.11
  79.6 2.1 %collective-permute-start.9 = (f32[4,72,512]{2,1,0:T(8,128)S(1)}, f32[4,72,512]{2,1,0:T(8,128)S(1)}, u32[]{:S(2)}, u32[]{:S(2)}) collective-permute-start(f32[4,72,512]{2,1,0:T(8,128)S(1)} %get-tuple-element.29), channel_id=1, source_target_pairs={{0,1},{1,0},{2,3},{3,2},{4,5},{5,4},{6,7},{7,6},{8,9},{9,8},{10,11... | collective-permute-start | bytes 1769480 | tf_op jit(solution)/shard_map/ppermute | solution.py:26
  79.9 8.2 %collective-permute-start.8 = (f32[2,72,512]{2,1,0:T(8,128)S(1)}, f32[2,72,512]{2,1,0:T(8,128)S(1)}, u32[]{:S(2)}, u32[]{:S(2)}) collective-permute-start(f32[2,72,512]{2,1,0:T(8,128)S(1)} %get-tuple-element.28), channel_id=1, source_target_pairs={{0,4},{4,8},{8,12},{12,16},{16,20},{20,24},{24,28},{1,5},{5,9},{9,... | collective-permute-start | bytes 884744 | tf_op jit(solution)/shard_map/ppermute | solution.py:32
  81.7 9.3 %collective-permute-start.10 = (f32[2,72,512]{2,1,0:T(8,128)S(1)}, f32[2,72,512]{2,1,0:T(8,128)S(1)}, u32[]{:S(2)}, u32[]{:S(2)}) collective-permute-start(f32[2,72,512]{2,1,0:T(8,128)S(1)} %slice_add_fusion), channel_id=1, source_target_pairs={{0,2},{1,3},{2,0},{3,1},{4,6},{5,7},{6,4},{7,5},{8,10},{9,11},{10,... | collective-permute-start | bytes 884744 | tf_op jit(solution)/shard_map/ppermute | solution.py:26
  91.4 7.7 %collective-permute-start.17 = (f32[64,1024]{1,0:T(8,128)S(1)}, f32[64,1024]{1,0:T(8,128)S(1)}, u32[]{:S(2)}, u32[]{:S(2)}) collective-permute-start(f32[64,1024]{1,0:T(8,128)S(1)} %get-tuple-element.33.refs_5_), channel_id=1, source_target_pairs={{0,2},{1,3},{2,0},{3,1},{4,6},{5,7},{6,4},{7,5},{8,10},{9,11},{10,... | collective-permute-start | bytes 786440 | tf_op jit(solution)/shard_map/ppermute | solution.py:26
  93.1 26.0 %collective-permute-start.19 = (f32[64,1024]{1,0:T(8,128)S(1)}, f32[64,1024]{1,0:T(8,128)S(1)}, u32[]{:S(2)}, u32[]{:S(2)}) collective-permute-start(f32[64,1024]{1,0:T(8,128)S(1)} %get-tuple-element.33.refs_5_), channel_id=1, source_target_pairs={{4,0},{8,4},{12,8},{16,12},{20,16},{24,20},{28,24},{5,1},{9,5},{13... | collective-permute-start | bytes 786440 | tf_op jit(solution)/shard_map/ppermute | solution.py:32
  94.4 24.7 %collective-permute-start.16 = (f32[64,1024]{1,0:T(8,128)S(1)}, f32[64,1024]{1,0:T(8,128)S(1)}, u32[]{:S(2)}, u32[]{:S(2)}) collective-permute-start(f32[64,1024]{1,0:T(8,128)S(1)} %get-tuple-element.33.refs_5_), channel_id=1, source_target_pairs={{0,1},{1,0},{2,3},{3,2},{4,5},{5,4},{6,7},{7,6},{8,9},{9,8},{10,11... | collective-permute-start | bytes 786440 | tf_op jit(solution)/shard_map/ppermute | solution.py:26
  99.1 20.0 %collective-permute-start.18 = (f32[64,1024]{1,0:T(8,128)S(1)}, f32[64,1024]{1,0:T(8,128)S(1)}, u32[]{:S(2)}, u32[]{:S(2)}) collective-permute-start(f32[64,1024]{1,0:T(8,128)S(1)} %collective-permute-done.17.refs_7_), channel_id=1, source_target_pairs={{0,1},{1,0},{2,3},{3,2},{4,5},{5,4},{6,7},{7,6},{8,9},{9,8},{10,11... | collective-permute-start | bytes 786440 | tf_op jit(solution)/shard_map/ppermute | solution.py:26
  99.1 1.6 collective-permute-start.11
  100.7 3.9 %collective-permute-start.12 = (f32[64,64]{1,0:T(8,128)S(1)}, f32[64,64]{1,0:T(8,128)S(1)}, u32[]{:S(2)}, u32[]{:S(2)}) collective-permute-start(f32[64,64]{1,0:T(8,128)S(1)} %add.37), channel_id=1, source_target_pairs={{0,2},{1,3},{2,0},{3,1},{4,6},{5,7},{6,4},{7,5},{8,10},{9,11},{10,... | collective-permute-start | bytes 49160 | tf_op jit(solution)/shard_map/ppermute | solution.py:26
  104.6 4.0 %collective-permute-start.13 = (f32[64,64]{1,0:T(8,128)S(1)}, f32[64,64]{1,0:T(8,128)S(1)}, u32[]{:S(2)}, u32[]{:S(2)}) collective-permute-start(f32[64,64]{1,0:T(8,128)S(1)} %add.38), channel_id=1, source_target_pairs={{0,4},{4,0},{8,12},{12,8},{16,20},{20,16},{24,28},{28,24},{1,5},{5... | collective-permute-start | bytes 49160 | tf_op jit(solution)/shard_map/ppermute | solution.py:26
  108.7 5.5 %collective-permute-start.14 = (f32[64,64]{1,0:T(8,128)S(1)}, f32[64,64]{1,0:T(8,128)S(1)}, u32[]{:S(2)}, u32[]{:S(2)}) collective-permute-start(f32[64,64]{1,0:T(8,128)S(1)} %add.39), channel_id=1, source_target_pairs={{0,8},{4,12},{8,0},{12,4},{16,24},{20,28},{24,16},{28,20},{1,9},{5... | collective-permute-start | bytes 49160 | tf_op jit(solution)/shard_map/ppermute | solution.py:26
  114.1 5.0 %collective-permute-start.15 = (f32[64,64]{1,0:T(8,128)S(1)}, f32[64,64]{1,0:T(8,128)S(1)}, u32[]{:S(2)}, u32[]{:S(2)}) collective-permute-start(f32[64,64]{1,0:T(8,128)S(1)} %add.40), channel_id=1, source_target_pairs={{0,16},{4,20},{8,24},{12,28},{16,0},{20,4},{24,8},{28,12},{1,17},{... | collective-permute-start | bytes 49160 | tf_op jit(solution)/shard_map/ppermute | solution.py:26
  119.1 3.4 %copy-start = (bf16[16,512,512]{2,1,0:T(8,128)(2,1)S(1)}, bf16[16,512,512]{2,1,0:T(8,128)(2,1)}, u32[]{:S(2)}) copy-start(bf16[16,512,512]{2,1,0:T(8,128)(2,1)} %get-tuple-element.34.refs_10_) | copy-start | bytes 25165828
  137.3 2.0 %collective-permute-start.21 = (f32[4,64,512]{2,1,0:T(8,128)S(1)}, f32[4,64,512]{2,1,0:T(8,128)S(1)}, u32[]{:S(2)}, u32[]{:S(2)}) collective-permute-start(f32[4,64,512]{2,1,0:T(8,128)S(1)} %get-tuple-element.37), channel_id=1, source_target_pairs={{0,1},{1,0},{2,3},{3,2},{4,5},{5,4},{6,7},{7,6},{8,9},{9,8},{10,11... | collective-permute-start | bytes 1572872 | tf_op jit(solution)/shard_map/ppermute | solution.py:26
  137.3 7.8 %collective-permute-start.20 = (f32[2,64,512]{2,1,0:T(8,128)S(1)}, f32[2,64,512]{2,1,0:T(8,128)S(1)}, u32[]{:S(2)}, u32[]{:S(2)}) collective-permute-start(f32[2,64,512]{2,1,0:T(8,128)S(1)} %get-tuple-element.36), channel_id=1, source_target_pairs={{0,4},{4,8},{8,12},{12,16},{16,20},{20,24},{24,28},{1,5},{5,9},{9,... | collective-permute-start | bytes 786440 | tf_op jit(solution)/shard_map/ppermute | solution.py:32
  139.3 8.4 %collective-permute-start.22 = (f32[2,64,512]{2,1,0:T(8,128)S(1)}, f32[2,64,512]{2,1,0:T(8,128)S(1)}, u32[]{:S(2)}, u32[]{:S(2)}) collective-permute-start(f32[2,64,512]{2,1,0:T(8,128)S(1)} %slice_add_fusion.1), channel_id=1, source_target_pairs={{0,2},{1,3},{2,0},{3,1},{4,6},{5,7},{6,4},{7,5},{8,10},{9,11},{10,... | collective-permute-start | bytes 786440 | tf_op jit(solution)/shard_map/ppermute | solution.py:26
  148.1 0.7 copy-start.3
  148.8 1.2 collective-permute-start.23
  150.0 3.9 %collective-permute-start.24 = (f32[64,64]{1,0:T(8,128)S(1)}, f32[64,64]{1,0:T(8,128)S(1)}, u32[]{:S(2)}, u32[]{:S(2)}) collective-permute-start(f32[64,64]{1,0:T(8,128)S(1)} %add.43), channel_id=1, source_target_pairs={{0,2},{1,3},{2,0},{3,1},{4,6},{5,7},{6,4},{7,5},{8,10},{9,11},{10,... | collective-permute-start | bytes 49160 | tf_op jit(solution)/shard_map/ppermute | solution.py:26
  153.9 4.5 %collective-permute-start.25 = (f32[64,64]{1,0:T(8,128)S(1)}, f32[64,64]{1,0:T(8,128)S(1)}, u32[]{:S(2)}, u32[]{:S(2)}) collective-permute-start(f32[64,64]{1,0:T(8,128)S(1)} %add.44), channel_id=1, source_target_pairs={{0,4},{4,0},{8,12},{12,8},{16,20},{20,16},{24,28},{28,24},{1,5},{5... | collective-permute-start | bytes 49160 | tf_op jit(solution)/shard_map/ppermute | solution.py:26
  158.4 5.0 %collective-permute-start.26 = (f32[64,64]{1,0:T(8,128)S(1)}, f32[64,64]{1,0:T(8,128)S(1)}, u32[]{:S(2)}, u32[]{:S(2)}) collective-permute-start(f32[64,64]{1,0:T(8,128)S(1)} %add.45), channel_id=1, source_target_pairs={{0,8},{4,12},{8,0},{12,4},{16,24},{20,28},{24,16},{28,20},{1,9},{5... | collective-permute-start | bytes 49160 | tf_op jit(solution)/shard_map/ppermute | solution.py:26
  163.4 4.8 %collective-permute-start.27 = (f32[64,64]{1,0:T(8,128)S(1)}, f32[64,64]{1,0:T(8,128)S(1)}, u32[]{:S(2)}, u32[]{:S(2)}) collective-permute-start(f32[64,64]{1,0:T(8,128)S(1)} %add.46), channel_id=1, source_target_pairs={{0,16},{4,20},{8,24},{12,28},{16,0},{20,4},{24,8},{28,12},{1,17},{... | collective-permute-start | bytes 49160 | tf_op jit(solution)/shard_map/ppermute | solution.py:26

commit v2 on v1

--- a/solution.py
+++ b/solution.py
@@ -17,6 +17,10 @@
 HIGHEST = lax.Precision.HIGHEST
 
 
+def cost(flops, moved):
+    return pl.CostEstimate(flops=int(flops), bytes_accessed=int(moved), transcendentals=0)
+
+
 def spec(space):
     return pl.BlockSpec(memory_space=space)
 
@@ -41,11 +45,14 @@
     return bits
 
 
-def gather_near(value, axis):
+def gather_near(value, axis, before=()):
     held = {0: value}
     for bit in reversed(bits_of(lax.axis_size(axis))):
-        for rel in list(held):
-            held[rel ^ bit] = swap(held[rel], axis, bit)
+        source = dict(held)
+        for rel in source:
+            if rel and before:
+                source[rel] = lax.optimization_barrier((source[rel],) + tuple(before))[0]
+            held[rel ^ bit] = swap(source[rel], axis, bit)
     return [held[rel] for rel in range(len(held))]
 
 
@@ -135,6 +142,7 @@
         in_specs=[spec(VMEM), spec(SMEM), spec(SMEM), spec(SMEM), spec(SMEM), spec(VMEM)],
         out_specs=(spec(VMEM), spec(SMEM), spec(SMEM), spec(SMEM)),
         compiler_params=pltpu.CompilerParams(vmem_limit_bytes=32 * 2**20),
+        cost_estimate=cost(2**30, 2**24),
         name="prepare",
     )(points, counts, rows, cols, live, start)
 
@@ -182,20 +190,15 @@
     tiles_out = refs[4 + 2 * pieces]
     messages = len(message_rels(group)) + 1
     outs = refs[5 + 2 * pieces : 5 + 2 * pieces + messages]
-    window, kept, u_win, level_row, level_col, acc, in_sems, out_sems = refs[5 + 2 * pieces + messages :]
+    window, u_win, level_row, level_col, acc = refs[5 + 2 * pieces + messages :]
+    kept = tiles_out
     held = pts[0].shape[0]
     width = pts[0].shape[1]
     blocks_dev = held // PTS
     columns = augs[0].shape[0] - EXTRA
     height = acc.shape[1]
-    copies = [
-        pltpu.make_async_copy(
-            pts[piece], window.at[pl.ds(piece * held, held), :], in_sems.at[piece]
-        )
-        for piece in range(pieces)
-    ]
-    for copy in copies:
-        copy.start()
+    for piece in range(pieces):
+        window[piece * held : (piece + 1) * held, :] = pts[piece][...]
 
     pick = lax.broadcasted_iota(jnp.int32, (EXTRA, 128), 0)
     pick = jnp.where(jnp.logical_and(pick >= 1, pick <= 3), 1.0, 0.0).astype(jnp.bfloat16)
@@ -218,8 +221,6 @@
         own = augs[0][0:columns, lanes].astype(jnp.float32)
         acc[block, 0:columns] = jnp.where(place_in < counts[block], own, 0.0)
         acc[block, columns:height] = jnp.ones((height - columns, PTS), jnp.float32)
-    for copy in copies:
-        copy.wait()
 
     n = n_ref[0]
     step = 256
@@ -238,18 +239,11 @@
             left_level = jnp.concatenate([left_level] * (PTS // 128), axis=1)
             value = jnp.exp2(cross * scale - left_level - right_level)
             kept[index, part * step : (part + 1) * step, :] = value.astype(jnp.bfloat16)
-        pltpu.make_async_copy(kept.at[index], tiles_out.at[index], out_sems.at[index]).start()
         add_products(acc, kept[index], u_win[row], u_win[col], row, col)
         return carry
 
     lax.fori_loop(0, n, body, 0)
     write_products(group, blocks_dev, acc, outs)
-
-    def finish(index, carry):
-        pltpu.make_async_copy(kept.at[index], tiles_out.at[index], out_sems.at[index]).wait()
-        return carry
-
-    lax.fori_loop(0, n, finish, 0)
 
 
 def first_turn(n, rows, cols, counts, pts, augs, group, cap):
@@ -268,19 +262,17 @@
     return pl.pallas_call(
         kernel,
         out_shape=tuple(shapes),
-        in_specs=[spec(SMEM)] * 4 + [spec(pl.ANY)] * pieces + [spec(VMEM)] * pieces,
-        out_specs=(spec(pl.ANY),) + (spec(VMEM),) * (len(shapes) - 1),
+        in_specs=[spec(SMEM)] * 4 + [spec(VMEM)] * (2 * pieces),
+        out_specs=(spec(VMEM),) * len(shapes),
         scratch_shapes=[
             VMEM((pieces * held, width), jnp.bfloat16),
-            VMEM((cap, PTS, PTS), jnp.bfloat16),
             VMEM((places, tall, PTS), jnp.bfloat16),
             VMEM((places, 8, PTS), jnp.float32),
             VMEM((group * blocks_dev, PTS, 128), jnp.float32),
             VMEM((places, height, PTS), jnp.float32),
-            pltpu.SemaphoreType.DMA((pieces,)),
-            pltpu.SemaphoreType.DMA((cap,)),
         ],
-        compiler_params=pltpu.CompilerParams(vmem_limit_bytes=48 * 2**20),
+        compiler_params=pltpu.CompilerParams(vmem_limit_bytes=36 * 2**20),
+        cost_estimate=cost(2**33, 2**25),
         name="first_turn",
     )(n, rows, cols, counts, *pts, *augs)
 
@@ -336,6 +328,7 @@
         in_specs=[spec(VMEM)] * len(operands),
         out_specs=(spec(VMEM),) * len(shapes),
         compiler_params=pltpu.CompilerParams(vmem_limit_bytes=32 * 2**20),
+        cost_estimate=cost(2**26, 2**21),
         name="scaled_gram",
     )(*operands)
 
@@ -346,20 +339,41 @@
     col_id = lax.broadcasted_iota(jnp.int32, (size, size), 1)
     eye = jnp.where(row_id == col_id, 1.0, 0.0)
     whole = jnp.concatenate([gram, eye], axis=1)
-    groups = [whole[8 * g : 8 * g + 8, :] for g in range(size // 8)]
-    within = lax.broadcasted_iota(jnp.int32, (8, 2 * size), 0)
-    for j in range(size):
-        g, r = divmod(j, 8)
-        top = groups[g][r : r + 1, :]
-        factor = lax.rsqrt(top[:, j : j + 1])
-        top = top * factor
-        for other in range(g, size // 8):
-            column = groups[other][:, j : j + 1] * factor
-            fresh = groups[other] - column * top
-            if other == g:
-                fresh = jnp.where(within > r, fresh, jnp.where(within == r, top, groups[g]))
-            groups[other] = fresh
-    return jnp.concatenate(groups, axis=0)[:, size : 2 * size]
+    wide = 2 * size
+    count = size // 8
+    groups = [whole[8 * g : 8 * g + 8, :] for g in range(count)]
+    within = lax.broadcasted_iota(jnp.int32, (8, wide), 0)
+
+    def spread_row(value, row):
+        return jnp.broadcast_to(value[row : row + 1, :], (8, wide))
+
+    results = []
+    for g in range(count):
+        spread = [
+            [
+                jnp.broadcast_to(groups[other][:, 8 * g + k : 8 * g + k + 1], (8, wide))
+                for other in range(g, count)
+            ]
+            for k in range(8)
+        ]
+        pivots = jnp.ones((8, wide), jnp.float32)
+        for j in range(8):
+            column = spread[j]
+            pivot = spread_row(column[0], j)
+            pivots = jnp.where(within == j, pivot, pivots)
+            over = 1.0 / pivot
+            below = jnp.where(within > j, column[0], 0.0)
+            for k in range(j + 1, 8):
+                share = spread_row(column[0], k) * over
+                spread[k][0] = spread[k][0] - below * share
+                for other in range(1, count - g):
+                    spread[k][other] = spread[k][other] - column[other] * share
+            top = spread_row(groups[g], j) * over
+            groups[g] = groups[g] - below * top
+            for other in range(1, count - g):
+                groups[g + other] = groups[g + other] - column[other] * top
+        results.append(groups[g] * lax.rsqrt(pivots))
+    return jnp.concatenate(results, axis=0)[:, size:wide]
 
 
 def second_kernel(group, refs):
@@ -369,19 +383,11 @@
     tiles = refs[5 + pieces]
     messages = len(message_rels(group)) + 1
     outs = refs[6 + pieces : 6 + pieces + messages]
-    kept, u_win, acc, sems = refs[6 + pieces + messages :]
+    u_win, acc = refs[6 + pieces + messages :]
     columns, held = zs[0].shape
     blocks_dev = held // PTS
     n = n_ref[0]
 
-    def fetch(index):
-        return pltpu.make_async_copy(tiles.at[index], kept.at[index], sems.at[index])
-
-    def begin(index, carry):
-        fetch(index).start()
-        return carry
-
-    lax.fori_loop(0, n, begin, 0)
     inverse = inverse_factor(gram[...])
     for piece in range(pieces):
         for block in range(blocks_dev):
@@ -401,8 +407,7 @@
 
     def body(index, carry):
         row, col = rows[index], cols[index]
-        fetch(index).wait()
-        add_products(acc, kept[index], u_win[row], u_win[col], row, col)
+        add_products(acc, tiles[index], u_win[row], u_win[col], row, col)
         return carry
 
     lax.fori_loop(0, n, body, 0)
@@ -422,15 +427,14 @@
     return pl.pallas_call(
         kernel,
         out_shape=tuple(shapes),
-        in_specs=[spec(SMEM)] * 4 + [spec(VMEM)] * (1 + pieces) + [spec(pl.ANY)],
+        in_specs=[spec(SMEM)] * 4 + [spec(VMEM)] * (2 + pieces),
         out_specs=(spec(VMEM),) * len(shapes),
         scratch_shapes=[
-            VMEM((cap, PTS, PTS), jnp.bfloat16),
             VMEM((places, columns, PTS), jnp.bfloat16),
             VMEM((places, columns, PTS), jnp.float32),
-            pltpu.SemaphoreType.DMA((cap,)),
         ],
-        compiler_params=pltpu.CompilerParams(vmem_limit_bytes=40 * 2**20),
+        compiler_params=pltpu.CompilerParams(vmem_limit_bytes=24 * 2**20),
+        cost_estimate=cost(2**32, 2**24),
         name="next_turn",
     )(n, rows, cols, counts, gram, *zs, tiles)
 
@@ -447,6 +451,7 @@
         out_shape=jax.ShapeDtypeStruct(z.shape, jnp.float32),
         in_specs=[spec(VMEM)] * 2,
         out_specs=spec(VMEM),
+        cost_estimate=cost(2**30, 2**20),
         name="embedding",
     )(gram, z)
 
@@ -473,8 +478,14 @@
 
 def all_sum(value, axes):
     for axis in axes:
-        for bit in bits_of(lax.axis_size(axis)):
-            value = value + swap(value, axis, bit)
+        bits = bits_of(lax.axis_size(axis))
+        while bits:
+            now, bits = bits[:3], bits[3:]
+            base = now[0]
+            terms = [value] + [swap(value, axis, base * rel) for rel in range(1, 2 ** len(now))]
+            while len(terms) > 1:
+                terms = [left + right for left, right in zip(terms[::2], terms[1::2])]
+            value = terms[0]
     return value
 
 
@@ -484,11 +495,12 @@
     columns = start.shape[0]
     slots = pair_rows.shape[0]
     cap = max(-(-slots // group), blocks_dev * blocks_dev * group)
-    pts = gather_near(points, "grp") + [from_behind(points, "blk", -1)]
     aug, rows, cols, n = prepare(
         points, counts, pair_rows, pair_cols, pair_live, start, group, cap
     )
     augs = gather_near(aug, "grp") + [from_behind(aug, "blk", -1)]
+    far = from_behind(points, "blk", -1)
+    pts = gather_near(points, "grp", augs + [far]) + [far]
     tiles, *messages = first_turn(n, rows, cols, counts, pts, augs, group, cap)
     z, gram, degree = scaled_gram(sum_products(messages, group, blocks_dev), None, columns)
     for turn in range(1, ITERS):

time: 176 us -> 149 us (0.85); the launches traced: 176 us -> 147 us
  waiting for transfers between devices: 78.4 us -> 61.3 us
  Pallas kernels: 48.1 us -> 38 us
  local copies, waits for them, and re-layouts: 10.1 us -> 5.02 us
  starting transfers between devices: 38.1 us -> 41.1 us
    ppermute x23 -> x33, waiting for transfers between devices: 64.1 us -> 47.2 us  [swap(): lax.ppermute(value, axis, [(source, source ^ bit) for source in range(cou...]
    unnamed x24 -> x16, local copies, waits for them, and re-layouts: 10.1 us -> 5.02 us
    pallas_call x1, Pallas kernels: 14.7 us -> 10.4 us  [next_turn(): pl.pallas_call(kernel, out_shape=tuple(shapes), in_specs=[spec(SMEM)] * 4...]
    pallas_call x1, Pallas kernels: 7.44 us -> 4 us  [embedding(): pl.pallas_call(embed_kernel, out_shape=jax.ShapeDtypeStruct(z.shape, jnp....]
    ppermute x23 -> x33, starting transfers between devices: 31.6 us -> 34.7 us  [swap(): lax.ppermute(value, axis, [(source, source ^ bit) for source in range(cou...]
    pallas_call x1, Pallas kernels: 19.3 us -> 17 us  [first_turn(): pl.pallas_call(kernel, out_shape=tuple(shapes), in_specs=[spec(SMEM)] * 4...]
  transfers between devices with their start and end apart: 28 -> 38, of which waited for: 21 -> 18; matrix products, arithmetic and copies ran while one was open for 0% -> 0% of each run, Pallas kernels for 3% -> 4%
where the time goes in v2:
time: 149 us; the launch traced here: 147 us
  waiting for transfers between devices  61.3 us (41%)
  starting transfers between devices  41.1 us (28%)
  Pallas kernels  38 us (26%)
  local copies, waits for them, and re-layouts  5.02 us (3%)
    ppermute x33, waiting for transfers between devices, swap(): lax.ppermute(value, axis, [(source, source ^ bit) for source in range(cou...  47.2 us
    ppermute x33, starting transfers between devices, swap(): lax.ppermute(value, axis, [(source, source ^ bit) for source in range(cou...  34.7 us
    pallas_call x1, Pallas kernels, first_turn(): pl.pallas_call(kernel, out_shape=tuple(shapes), in_specs=[spec(SMEM)] * 4...  17 us
    ppermute x5, waiting for transfers between devices, from_behind(): lax.ppermute(value, axis, [(source, source + steps) for source in range(i...  14.1 us
    pallas_call x1, Pallas kernels, next_turn(): pl.pallas_call(kernel, out_shape=tuple(shapes), in_specs=[spec(SMEM)] * 4...  10.4 us
    ppermute x5, starting transfers between devices, from_behind(): lax.ppermute(value, axis, [(source, source + steps) for source in range(i...  6.45 us
    pallas_call x1, Pallas kernels, prepare(): pl.pallas_call(functools.partial(prepare_kernel, group, cap), out_shape=(...  5.79 us
    unnamed x16, local copies, waits for them, and re-layouts  5.02 us
  transfers between devices with their start and end apart: 38, of which 18 were waited for; matrix products, arithmetic and copies ran while one was open for 0% of the time, Pallas kernels for 4%

profile of v2, /device:TPU:0, one launch (start us, length us, event | category | flops | bytes accessed | tf_op | source)
XLA Modules:
  0.0 147.1 jit_solution(376518201564516625)
XLA Ops:
  0.0 2.9 %collective-permute-start.1 = (bf16[1024,768]{1,0:T(8,128)(2,1)}, bf16[1024,768]{1,0:T(8,128)(2,1)S(1)}, u32[]{:S(2)}, u32[]{:S(2)}) collective-permute-start(bf16[1024,768]{1,0:T(8,128)(2,1)} %refs_4_.1), channel_id=1, source_target_pairs={{0,2},{1,3},{2,0},{3,1},{4,6},{5,7},{6,4},{7,5},{8,10},{9,11},{10,... | collective-permute-start | bytes 4718600 | tf_op jit(solution)/shard_map/ppermute | solution.py:30
  2.9 1.3 collective-permute-start.6
  4.9 1.4 copy-done
  6.3 0.9 copy-done.2
  7.2 0.7 copy-done.4
  7.9 0.7 copy-done.5
  8.5 0.7 copy-done.6
  9.2 5.8 %prepare.1 = (bf16[80,1024]{1,0:T(8,128)(2,1)S(1)}, s32[16]{0:T(128)S(1)}, s32[16]{0:T(128)S(1)}, s32[1]{0:T(128)}) custom-call(bf16[1024,768]{1,0:T(8,128)(2,1)S(1)} %copy-done, s32[2]{0:T(128)S(1)} %copy-done.6, s32[64]{0:T(128)S(1)} %copy-done.4, s32[64]{0:T(128)S(1)} %copy-done.5, s32[1]{0:T(128)S(6)} %copy.7.live, f32[64,1024]{1,0:T(8,128)S(1)} %copy-done.2), custom_call_target="tpu_custom_call" | custom-call | flops 1073741824 | bytes 16777216 | tf_op jit(solution)/shard_map/prepare/pallas_call | solution.py:134
  15.0 0.1 collective-permute-start.3
  15.1 1.3 collective-permute-start.5
  16.4 0.1 collective-permute-start.2
  16.5 24.6 %collective-permute-done.3.refs_11_ = bf16[80,1024]{1,0:T(8,128)(2,1)S(1)} collective-permute-done((bf16[80,1024]{1,0:T(8,128)(2,1)S(1)}, bf16[80,1024]{1,0:T(8,128)(2,1)S(1)}, u32[]{:S(2)}, u32[]{:S(2)}) %collective-permute-start.3) | collective-permute-done | bytes 163872 | tf_op jit(solution)/shard_map/ppermute | solution.py:30
  41.1 3.3 %collective-permute-done.5.refs_13_ = bf16[80,1024]{1,0:T(8,128)(2,1)S(1)} collective-permute-done((bf16[80,1024]{1,0:T(8,128)(2,1)S(1)}, bf16[80,1024]{1,0:T(8,128)(2,1)S(1)}, u32[]{:S(2)}, u32[]{:S(2)}) %collective-permute-start.5) | collective-permute-done | bytes 163872 | tf_op jit(solution)/shard_map/ppermute | solution.py:36
  44.4 0.6 collective-permute-start.7
  45.0 2.8 %collective-permute-done.refs_5_ = bf16[1024,768]{1,0:T(8,128)(2,1)S(1)} collective-permute-done((bf16[1024,768]{1,0:T(8,128)(2,1)S(1)}, bf16[1024,768]{1,0:T(8,128)(2,1)S(1)}, u32[]{:S(2)}, u32[]{:S(2)}) %collective-permute-start) | collective-permute-done | bytes 1572896 | tf_op jit(solution)/shard_map/ppermute | solution.py:30
  47.8 2.2 %collective-permute-done.7.refs_7_ = bf16[1024,768]{1,0:T(8,128)(2,1)S(1)} collective-permute-done((bf16[1024,768]{1,0:T(8,128)(2,1)S(1)}, bf16[1024,768]{1,0:T(8,128)(2,1)S(1)}, u32[]{:S(2)}, u32[]{:S(2)}) %collective-permute-start.7) | collective-permute-done | bytes 1572896 | tf_op jit(solution)/shard_map/ppermute | solution.py:30
  50.1 17.0 %first_turn.1 = (bf16[16,512,512]{2,1,0:T(8,128)(2,1)S(1)}, f32[2,72,512]{2,1,0:T(8,128)S(1)}, f32[4,72,512]{2,1,0:T(8,128)S(1)}, f32[2,72,512]{2,1,0:T(8,128)S(1)}, f32[2,72,512]{2,1,0:T(8,128)S(1)}) custom-call(s32[1]{0:T(128)} %get-tuple-element.24.refs_0_, s32[16]{0:T(128)S(1)} %get-tuple-element.25.refs_1_, s32[16]{0:T(128)S(1)} %get-tuple-element.26.refs_2_, ...), custom_call_target="tpu_custom_call" | custom-call | flops 8589934592 | bytes 33554432 | tf_op jit(solution)/shard_map/first_turn/pallas_call | solution.py:262
  67.1 0.2 collective-permute-start.9
  67.3 1.3 collective-permute-start.8
  68.6 0.6 collective-permute-done.9.refs_2_
  69.2 0.4 collective-permute-start.10
  69.6 6.1 %collective-permute-done.8.refs_1_ = f32[2,72,512]{2,1,0:T(8,128)S(1)} collective-permute-done((f32[2,72,512]{2,1,0:T(8,128)S(1)}, f32[2,72,512]{2,1,0:T(8,128)S(1)}, u32[]{:S(2)}, u32[]{:S(2)}) %collective-permute-start.8) | collective-permute-done | bytes 294944 | tf_op jit(solution)/shard_map/ppermute | solution.py:36
  75.6 2.7 %collective-permute-done.10.refs_3_ = f32[2,72,512]{2,1,0:T(8,128)S(1)} collective-permute-done((f32[2,72,512]{2,1,0:T(8,128)S(1)}, f32[2,72,512]{2,1,0:T(8,128)S(1)}, u32[]{:S(2)}, u32[]{:S(2)}) %collective-permute-start.10) | collective-permute-done | bytes 294944 | tf_op jit(solution)/shard_map/ppermute | solution.py:30
  78.3 0.4 scaled_gram.2
  78.7 0.1 collective-permute-start.13
  78.8 0.9 collective-permute-start.12
  79.7 0.9 collective-permute-start.11
  80.6 0.3 collective-permute-start.22
  81.0 1.1 collective-permute-done.13
  82.1 0.7 collective-permute-done.12
  82.8 3.0 %collective-permute-start.20 = (f32[64,64]{1,0:T(8,128)S(1)}, f32[64,64]{1,0:T(8,128)S(1)}, u32[]{:S(2)}, u32[]{:S(2)}) collective-permute-start(f32[64,64]{1,0:T(8,128)S(1)} %add_add_fusion.3), channel_id=1, source_target_pairs={{0,28},{4,24},{8,20},{12,16},{16,12},{20,8},{24,4},{28,0},{1,29},{... | collective-permute-start | bytes 49160 | tf_op jit(solution)/shard_map/ppermute | solution.py:30
  85.9 0.4 collective-permute-start.19
  86.3 3.2 %collective-permute-start.18 = (f32[64,64]{1,0:T(8,128)S(1)}, f32[64,64]{1,0:T(8,128)S(1)}, u32[]{:S(2)}, u32[]{:S(2)}) collective-permute-start(f32[64,64]{1,0:T(8,128)S(1)} %add_add_fusion.3), channel_id=1, source_target_pairs={{0,20},{4,16},{8,28},{12,24},{16,4},{20,0},{24,12},{28,8},{1,21},{... | collective-permute-start | bytes 49160 | tf_op jit(solution)/shard_map/ppermute | solution.py:30
  89.4 1.1 collective-permute-start.17
  90.5 2.0 %collective-permute-start.16 = (f32[64,64]{1,0:T(8,128)S(1)}, f32[64,64]{1,0:T(8,128)S(1)}, u32[]{:S(2)}, u32[]{:S(2)}) collective-permute-start(f32[64,64]{1,0:T(8,128)S(1)} %add_add_fusion.3), channel_id=1, source_target_pairs={{0,12},{4,8},{8,4},{12,0},{16,28},{20,24},{24,20},{28,16},{1,13},{... | collective-permute-start | bytes 49160 | tf_op jit(solution)/shard_map/ppermute | solution.py:30
  92.6 1.3 collective-permute-start.24
  93.9 0.1 collective-permute-start.21
  94.0 0.5 collective-permute-start.23
  94.5 0.1 collective-permute-done.17
  94.6 3.6 %collective-permute-start.15 = (f32[64,64]{1,0:T(8,128)S(1)}, f32[64,64]{1,0:T(8,128)S(1)}, u32[]{:S(2)}, u32[]{:S(2)}) collective-permute-start(f32[64,64]{1,0:T(8,128)S(1)} %add_add_fusion.3), channel_id=1, source_target_pairs={{0,8},{4,12},{8,0},{12,4},{16,24},{20,28},{24,16},{28,20},{1,9},{5... | collective-permute-start | bytes 49160 | tf_op jit(solution)/shard_map/ppermute | solution.py:30
  98.2 4.7 %collective-permute-done.15 = f32[64,64]{1,0:T(8,128)S(1)} collective-permute-done((f32[64,64]{1,0:T(8,128)S(1)}, f32[64,64]{1,0:T(8,128)S(1)}, u32[]{:S(2)}, u32[]{:S(2)}) %collective-permute-start.15) | collective-permute-done | bytes 16416 | tf_op jit(solution)/shard_map/ppermute | solution.py:30
  103.0 10.4 %next_turn.1 = (f32[2,64,512]{2,1,0:T(8,128)S(1)}, f32[4,64,512]{2,1,0:T(8,128)S(1)}, f32[2,64,512]{2,1,0:T(8,128)S(1)}, f32[2,64,512]{2,1,0:T(8,128)S(1)}) custom-call(s32[1]{0:T(128)} %get-tuple-element.24.refs_0_, s32[16]{0:T(128)S(1)} %get-tuple-element.25.refs_1_, s32[16]{0:T(128)S(1)} %get-tuple-element.26.refs_2_, s32[2]{0:T(128)S(1)} %copy-done.7, ...), custom_call_target="tpu_custom_call" | custom-call | flops 4294967296 | bytes 16777216 | tf_op jit(solution)/shard_map/next_turn/pallas_call | solution.py:427
  113.5 1.3 collective-permute-start.25
  114.8 0.6 collective-permute-done.26.refs_3_
  115.4 1.1 collective-permute-start.27
  116.6 4.7 %collective-permute-done.25.refs_2_ = f32[2,64,512]{2,1,0:T(8,128)S(1)} collective-permute-done((f32[2,64,512]{2,1,0:T(8,128)S(1)}, f32[2,64,512]{2,1,0:T(8,128)S(1)}, u32[]{:S(2)}, u32[]{:S(2)}) %collective-permute-start.25) | collective-permute-done | bytes 262176 | tf_op jit(solution)/shard_map/ppermute | solution.py:36
  121.3 2.6 %collective-permute-done.27.refs_4_ = f32[2,64,512]{2,1,0:T(8,128)S(1)} collective-permute-done((f32[2,64,512]{2,1,0:T(8,128)S(1)}, f32[2,64,512]{2,1,0:T(8,128)S(1)}, u32[]{:S(2)}, u32[]{:S(2)}) %collective-permute-start.27) | collective-permute-done | bytes 262176 | tf_op jit(solution)/shard_map/ppermute | solution.py:30
  123.8 0.4 scaled_gram.3
  124.2 0.7 copy-done.3
  124.9 1.1 collective-permute-start.29
  126.0 0.8 collective-permute-start.28
  126.8 1.5 %collective-permute-done.30 = f32[64,64]{1,0:T(8,128)S(1)} collective-permute-done((f32[64,64]{1,0:T(8,128)S(1)}, f32[64,64]{1,0:T(8,128)S(1)}, u32[]{:S(2)}, u32[]{:S(2)}) %collective-permute-start.30) | collective-permute-done | bytes 16416 | tf_op jit(solution)/shard_map/ppermute | solution.py:30
  128.3 0.8 collective-permute-done.29
  129.1 0.9 collective-permute-start.37
  130.0 2.7 %collective-permute-start.36 = (f32[64,64]{1,0:T(8,128)S(1)}, f32[64,64]{1,0:T(8,128)S(1)}, u32[]{:S(2)}, u32[]{:S(2)}) collective-permute-start(f32[64,64]{1,0:T(8,128)S(1)} %add_add_fusion.1), channel_id=1, source_target_pairs={{0,24},{4,28},{8,16},{12,20},{16,8},{20,12},{24,0},{28,4},{1,25},{... | collective-permute-start | bytes 49160 | tf_op jit(solution)/shard_map/ppermute | solution.py:30
  132.7 1.8 %collective-permute-start.35 = (f32[64,64]{1,0:T(8,128)S(1)}, f32[64,64]{1,0:T(8,128)S(1)}, u32[]{:S(2)}, u32[]{:S(2)}) collective-permute-start(f32[64,64]{1,0:T(8,128)S(1)} %add_add_fusion.1), channel_id=1, source_target_pairs={{0,20},{4,16},{8,28},{12,24},{16,4},{20,0},{24,12},{28,8},{1,21},{... | collective-permute-start | bytes 49160 | tf_op jit(solution)/shard_map/ppermute | solution.py:30
  134.5 2.3 %collective-permute-start.34 = (f32[64,64]{1,0:T(8,128)S(1)}, f32[64,64]{1,0:T(8,128)S(1)}, u32[]{:S(2)}, u32[]{:S(2)}) collective-permute-start(f32[64,64]{1,0:T(8,128)S(1)} %add_add_fusion.1), channel_id=1, source_target_pairs={{0,16},{4,20},{8,24},{12,28},{16,0},{20,4},{24,8},{28,12},{1,17},{... | collective-permute-start | bytes 49160 | tf_op jit(solution)/shard_map/ppermute | solution.py:30
  136.8 0.8 collective-permute-start.33
  137.6 0.9 collective-permute-start.32
  138.5 1.7 %collective-permute-start.31 = (f32[64,64]{1,0:T(8,128)S(1)}, f32[64,64]{1,0:T(8,128)S(1)}, u32[]{:S(2)}, u32[]{:S(2)}) collective-permute-start(f32[64,64]{1,0:T(8,128)S(1)} %add_add_fusion.1), channel_id=1, source_target_pairs={{0,4},{4,0},{8,12},{12,8},{16,20},{20,16},{24,28},{28,24},{1,5},{5... | collective-permute-start | bytes 49160 | tf_op jit(solution)/shard_map/ppermute | solution.py:30
  140.3 1.3 collective-permute-done.33
  141.6 0.9 collective-permute-done.31
  142.4 0.6 add_add_fusion.gram
  143.1 4.0 %embedding.1 = f32[64,1024]{1,0:T(8,128)} custom-call(f32[64,64]{1,0:T(8,128)} %add_add_fusion.gram, f32[64,1024]{1,0:T(8,128)} %copy-done.3), custom_call_target="tpu_custom_call" | custom-call | flops 1073741824 | bytes 1048576 | tf_op jit(solution)/shard_map/embedding/pallas_call | solution.py:449
  (40 shorter events, 0.3 us)
Async XLA Ops:
  0.0 44.4 %collective-permute-start.1 = (bf16[1024,768]{1,0:T(8,128)(2,1)}, bf16[1024,768]{1,0:T(8,128)(2,1)S(1)}, u32[]{:S(2)}, u32[]{:S(2)}) collective-permute-start(bf16[1024,768]{1,0:T(8,128)(2,1)} %refs_4_.1), channel_id=1, source_target_pairs={{0,2},{1,3},{2,0},{3,1},{4,6},{5,7},{6,4},{7,5},{8,10},{9,11},{10,... | collective-permute-start | bytes 4718600 | tf_op jit(solution)/shard_map/ppermute | solution.py:30
  2.9 41.5 %collective-permute-start.6 = (bf16[1024,768]{1,0:T(8,128)(2,1)}, bf16[1024,768]{1,0:T(8,128)(2,1)S(1)}, u32[]{:S(2)}, u32[]{:S(2)}) collective-permute-start(bf16[1024,768]{1,0:T(8,128)(2,1)} %refs_4_.1), channel_id=1, source_target_pairs={{4,0},{8,4},{12,8},{16,12},{20,16},{24,20},{28,24},{5,1},{9,5},{13... | collective-permute-start | bytes 4718600 | tf_op jit(solution)/shard_map/ppermute | solution.py:36
  4.9 1.4 copy-start
  6.3 0.9 copy-start.2
  7.2 0.7 copy-start.4
  7.9 0.7 copy-start.5
  8.5 0.7 copy-start.6
  9.2 40.9 %copy-start.1 = (bf16[1024,768]{1,0:T(8,128)(2,1)S(1)}, bf16[1024,768]{1,0:T(8,128)(2,1)}, u32[]{:S(2)}) copy-start(bf16[1024,768]{1,0:T(8,128)(2,1)} %refs_4_.1) | copy-start | bytes 4718596
  9.2 40.9 %copy-start.7 = (s32[2]{0:T(128)S(1)}, s32[2]{0:T(128)}, u32[]{:S(2)}) copy-start(s32[2]{0:T(128)} %refs_3_.3) | copy-start | bytes 28
  15.0 26.1 %collective-permute-start.3 = (bf16[80,1024]{1,0:T(8,128)(2,1)S(1)}, bf16[80,1024]{1,0:T(8,128)(2,1)S(1)}, u32[]{:S(2)}, u32[]{:S(2)}) collective-permute-start(bf16[80,1024]{1,0:T(8,128)(2,1)S(1)} %get-tuple-element.27.refs_9_), channel_id=1, source_target_pairs={{0,2},{1,3},{2,0},{3,1},{4,6},{5,7},{6,4},{7,5},{8,10},{9,11},{10,... | collective-permute-start | bytes 491528 | tf_op jit(solution)/shard_map/ppermute | solution.py:30
  15.1 29.3 %collective-permute-start.5 = (bf16[80,1024]{1,0:T(8,128)(2,1)S(1)}, bf16[80,1024]{1,0:T(8,128)(2,1)S(1)}, u32[]{:S(2)}, u32[]{:S(2)}) collective-permute-start(bf16[80,1024]{1,0:T(8,128)(2,1)S(1)} %get-tuple-element.27.refs_9_), channel_id=1, source_target_pairs={{4,0},{8,4},{12,8},{16,12},{20,16},{24,20},{28,24},{5,1},{9,5},{13... | collective-permute-start | bytes 491528 | tf_op jit(solution)/shard_map/ppermute | solution.py:36
  16.4 28.0 %collective-permute-start.2 = (bf16[80,1024]{1,0:T(8,128)(2,1)S(1)}, bf16[80,1024]{1,0:T(8,128)(2,1)S(1)}, u32[]{:S(2)}, u32[]{:S(2)}) collective-permute-start(bf16[80,1024]{1,0:T(8,128)(2,1)S(1)} %get-tuple-element.27.refs_9_), channel_id=1, source_target_pairs={{0,1},{1,0},{2,3},{3,2},{4,5},{5,4},{6,7},{7,6},{8,9},{9,8},{10,11... | collective-permute-start | bytes 491528 | tf_op jit(solution)/shard_map/ppermute | solution.py:30
  41.1 3.4 %collective-permute-start.4 = (bf16[80,1024]{1,0:T(8,128)(2,1)S(1)}, bf16[80,1024]{1,0:T(8,128)(2,1)S(1)}, u32[]{:S(2)}, u32[]{:S(2)}) collective-permute-start(bf16[80,1024]{1,0:T(8,128)(2,1)S(1)} %collective-permute-done.3.refs_11_), channel_id=1, source_target_pairs={{0,1},{1,0},{2,3},{3,2},{4,5},{5,4},{6,7},{7,6},{8,9},{9,8},{10,11... | collective-permute-start | bytes 491528 | tf_op jit(solution)/shard_map/ppermute | solution.py:30
  44.4 3.4 %collective-permute-start = (bf16[1024,768]{1,0:T(8,128)(2,1)S(1)}, bf16[1024,768]{1,0:T(8,128)(2,1)S(1)}, u32[]{:S(2)}, u32[]{:S(2)}) collective-permute-start(bf16[1024,768]{1,0:T(8,128)(2,1)S(1)} %copy-done), channel_id=1, source_target_pairs={{0,1},{1,0},{2,3},{3,2},{4,5},{5,4},{6,7},{7,6},{8,9},{9,8},{10,11... | collective-permute-start | bytes 4718600 | tf_op jit(solution)/shard_map/ppermute | solution.py:30
  44.4 5.6 %collective-permute-start.7 = (bf16[1024,768]{1,0:T(8,128)(2,1)S(1)}, bf16[1024,768]{1,0:T(8,128)(2,1)S(1)}, u32[]{:S(2)}, u32[]{:S(2)}) collective-permute-start(bf16[1024,768]{1,0:T(8,128)(2,1)S(1)} %collective-permute-done.1.refs_6_), channel_id=1, source_target_pairs={{0,1},{1,0},{2,3},{3,2},{4,5},{5,4},{6,7},{7,6},{8,9},{9,8},{10,11... | collective-permute-start | bytes 4718600 | tf_op jit(solution)/shard_map/ppermute | solution.py:30
  67.1 2.1 %collective-permute-start.9 = (f32[4,72,512]{2,1,0:T(8,128)S(1)}, f32[4,72,512]{2,1,0:T(8,128)S(1)}, u32[]{:S(2)}, u32[]{:S(2)}) collective-permute-start(f32[4,72,512]{2,1,0:T(8,128)S(1)} %get-tuple-element.31), channel_id=1, source_target_pairs={{0,1},{1,0},{2,3},{3,2},{4,5},{5,4},{6,7},{7,6},{8,9},{9,8},{10,11... | collective-permute-start | bytes 1769480 | tf_op jit(solution)/shard_map/ppermute | solution.py:30
  67.3 8.3 %collective-permute-start.8 = (f32[2,72,512]{2,1,0:T(8,128)S(1)}, f32[2,72,512]{2,1,0:T(8,128)S(1)}, u32[]{:S(2)}, u32[]{:S(2)}) collective-permute-start(f32[2,72,512]{2,1,0:T(8,128)S(1)} %get-tuple-element.30), channel_id=1, source_target_pairs={{0,4},{4,8},{8,12},{12,16},{16,20},{20,24},{24,28},{1,5},{5,9},{9,... | collective-permute-start | bytes 884744 | tf_op jit(solution)/shard_map/ppermute | solution.py:36
  69.2 9.1 %collective-permute-start.10 = (f32[2,72,512]{2,1,0:T(8,128)S(1)}, f32[2,72,512]{2,1,0:T(8,128)S(1)}, u32[]{:S(2)}, u32[]{:S(2)}) collective-permute-start(f32[2,72,512]{2,1,0:T(8,128)S(1)} %slice_add_fusion), channel_id=1, source_target_pairs={{0,2},{1,3},{2,0},{3,1},{4,6},{5,7},{6,4},{7,5},{8,10},{9,11},{10,... | collective-permute-start | bytes 884744 | tf_op jit(solution)/shard_map/ppermute | solution.py:30
  78.7 3.4 %collective-permute-start.13 = (f32[64,64]{1,0:T(8,128)S(1)}, f32[64,64]{1,0:T(8,128)S(1)}, u32[]{:S(2)}, u32[]{:S(2)}) collective-permute-start(f32[64,64]{1,0:T(8,128)S(1)} %get-tuple-element.34), channel_id=1, source_target_pairs={{0,3},{1,2},{2,1},{3,0},{4,7},{5,6},{6,5},{7,4},{8,11},{9,10},{10,... | collective-permute-start | bytes 49160 | tf_op jit(solution)/shard_map/ppermute | solution.py:30
  78.8 4.0 %collective-permute-start.12 = (f32[64,64]{1,0:T(8,128)S(1)}, f32[64,64]{1,0:T(8,128)S(1)}, u32[]{:S(2)}, u32[]{:S(2)}) collective-permute-start(f32[64,64]{1,0:T(8,128)S(1)} %get-tuple-element.34), channel_id=1, source_target_pairs={{0,2},{1,3},{2,0},{3,1},{4,6},{5,7},{6,4},{7,5},{8,10},{9,11},{10,... | collective-permute-start | bytes 49160 | tf_op jit(solution)/shard_map/ppermute | solution.py:30
  79.7 3.1 %collective-permute-start.11 = (f32[64,64]{1,0:T(8,128)S(1)}, f32[64,64]{1,0:T(8,128)S(1)}, u32[]{:S(2)}, u32[]{:S(2)}) collective-permute-start(f32[64,64]{1,0:T(8,128)S(1)} %get-tuple-element.34), channel_id=1, source_target_pairs={{0,1},{1,0},{2,3},{3,2},{4,5},{5,4},{6,7},{7,6},{8,9},{9,8},{10,11... | collective-permute-start | bytes 49160 | tf_op jit(solution)/shard_map/ppermute | solution.py:30
  80.6 13.3 %collective-permute-start.22 = (f32[64,1024]{1,0:T(8,128)S(1)}, f32[64,1024]{1,0:T(8,128)S(1)}, u32[]{:S(2)}, u32[]{:S(2)}) collective-permute-start(f32[64,1024]{1,0:T(8,128)S(1)} %get-tuple-element.35.refs_5_), channel_id=1, source_target_pairs={{0,2},{1,3},{2,0},{3,1},{4,6},{5,7},{6,4},{7,5},{8,10},{9,11},{10,... | collective-permute-start | bytes 786440 | tf_op jit(solution)/shard_map/ppermute | solution.py:30
  82.8 7.7 %collective-permute-start.20 = (f32[64,64]{1,0:T(8,128)S(1)}, f32[64,64]{1,0:T(8,128)S(1)}, u32[]{:S(2)}, u32[]{:S(2)}) collective-permute-start(f32[64,64]{1,0:T(8,128)S(1)} %add_add_fusion.3), channel_id=1, source_target_pairs={{0,28},{4,24},{8,20},{12,16},{16,12},{20,8},{24,4},{28,0},{1,29},{... | collective-permute-start | bytes 49160 | tf_op jit(solution)/shard_map/ppermute | solution.py:30
  85.9 6.7 %collective-permute-start.19 = (f32[64,64]{1,0:T(8,128)S(1)}, f32[64,64]{1,0:T(8,128)S(1)}, u32[]{:S(2)}, u32[]{:S(2)}) collective-permute-start(f32[64,64]{1,0:T(8,128)S(1)} %add_add_fusion.3), channel_id=1, source_target_pairs={{0,24},{4,28},{8,16},{12,20},{16,8},{20,12},{24,0},{28,4},{1,25},{... | collective-permute-start | bytes 49160 | tf_op jit(solution)/shard_map/ppermute | solution.py:30
  86.3 7.6 %collective-permute-start.18 = (f32[64,64]{1,0:T(8,128)S(1)}, f32[64,64]{1,0:T(8,128)S(1)}, u32[]{:S(2)}, u32[]{:S(2)}) collective-permute-start(f32[64,64]{1,0:T(8,128)S(1)} %add_add_fusion.3), channel_id=1, source_target_pairs={{0,20},{4,16},{8,28},{12,24},{16,4},{20,0},{24,12},{28,8},{1,21},{... | collective-permute-start | bytes 49160 | tf_op jit(solution)/shard_map/ppermute | solution.py:30
  89.4 5.1 %collective-permute-start.17 = (f32[64,64]{1,0:T(8,128)S(1)}, f32[64,64]{1,0:T(8,128)S(1)}, u32[]{:S(2)}, u32[]{:S(2)}) collective-permute-start(f32[64,64]{1,0:T(8,128)S(1)} %add_add_fusion.3), channel_id=1, source_target_pairs={{0,16},{4,20},{8,24},{12,28},{16,0},{20,4},{24,8},{28,12},{1,17},{... | collective-permute-start | bytes 49160 | tf_op jit(solution)/shard_map/ppermute | solution.py:30
  90.5 7.6 %collective-permute-start.16 = (f32[64,64]{1,0:T(8,128)S(1)}, f32[64,64]{1,0:T(8,128)S(1)}, u32[]{:S(2)}, u32[]{:S(2)}) collective-permute-start(f32[64,64]{1,0:T(8,128)S(1)} %add_add_fusion.3), channel_id=1, source_target_pairs={{0,12},{4,8},{8,4},{12,0},{16,28},{20,24},{24,20},{28,16},{1,13},{... | collective-permute-start | bytes 49160 | tf_op jit(solution)/shard_map/ppermute | solution.py:30
  92.6 10.4 %collective-permute-start.24 = (f32[64,1024]{1,0:T(8,128)S(1)}, f32[64,1024]{1,0:T(8,128)S(1)}, u32[]{:S(2)}, u32[]{:S(2)}) collective-permute-start(f32[64,1024]{1,0:T(8,128)S(1)} %get-tuple-element.35.refs_5_), channel_id=1, source_target_pairs={{4,0},{8,4},{12,8},{16,12},{20,16},{24,20},{28,24},{5,1},{9,5},{13... | collective-permute-start | bytes 786440 | tf_op jit(solution)/shard_map/ppermute | solution.py:36
  93.9 9.1 %collective-permute-start.21 = (f32[64,1024]{1,0:T(8,128)S(1)}, f32[64,1024]{1,0:T(8,128)S(1)}, u32[]{:S(2)}, u32[]{:S(2)}) collective-permute-start(f32[64,1024]{1,0:T(8,128)S(1)} %get-tuple-element.35.refs_5_), channel_id=1, source_target_pairs={{0,1},{1,0},{2,3},{3,2},{4,5},{5,4},{6,7},{7,6},{8,9},{9,8},{10,11... | collective-permute-start | bytes 786440 | tf_op jit(solution)/shard_map/ppermute | solution.py:30
  94.0 9.0 %collective-permute-start.23 = (f32[64,1024]{1,0:T(8,128)S(1)}, f32[64,1024]{1,0:T(8,128)S(1)}, u32[]{:S(2)}, u32[]{:S(2)}) collective-permute-start(f32[64,1024]{1,0:T(8,128)S(1)} %collective-permute-done.22.refs_7_), channel_id=1, source_target_pairs={{0,1},{1,0},{2,3},{3,2},{4,5},{5,4},{6,7},{7,6},{8,9},{9,8},{10,11... | collective-permute-start | bytes 786440 | tf_op jit(solution)/shard_map/ppermute | solution.py:30
  94.6 8.3 %collective-permute-start.15 = (f32[64,64]{1,0:T(8,128)S(1)}, f32[64,64]{1,0:T(8,128)S(1)}, u32[]{:S(2)}, u32[]{:S(2)}) collective-permute-start(f32[64,64]{1,0:T(8,128)S(1)} %add_add_fusion.3), channel_id=1, source_target_pairs={{0,8},{4,12},{8,0},{12,4},{16,24},{20,28},{24,16},{28,20},{1,9},{5... | collective-permute-start | bytes 49160 | tf_op jit(solution)/shard_map/ppermute | solution.py:30
  98.2 4.7 %collective-permute-start.14 = (f32[64,64]{1,0:T(8,128)S(1)}, f32[64,64]{1,0:T(8,128)S(1)}, u32[]{:S(2)}, u32[]{:S(2)}) collective-permute-start(f32[64,64]{1,0:T(8,128)S(1)} %add_add_fusion.3), channel_id=1, source_target_pairs={{0,4},{4,0},{8,12},{12,8},{16,20},{20,16},{24,28},{28,24},{1,5},{5... | collective-permute-start | bytes 49160 | tf_op jit(solution)/shard_map/ppermute | solution.py:30
  113.4 2.0 %collective-permute-start.26 = (f32[4,64,512]{2,1,0:T(8,128)S(1)}, f32[4,64,512]{2,1,0:T(8,128)S(1)}, u32[]{:S(2)}, u32[]{:S(2)}) collective-permute-start(f32[4,64,512]{2,1,0:T(8,128)S(1)} %get-tuple-element.39), channel_id=1, source_target_pairs={{0,1},{1,0},{2,3},{3,2},{4,5},{5,4},{6,7},{7,6},{8,9},{9,8},{10,11... | collective-permute-start | bytes 1572872 | tf_op jit(solution)/shard_map/ppermute | solution.py:30
  113.5 7.8 %collective-permute-start.25 = (f32[2,64,512]{2,1,0:T(8,128)S(1)}, f32[2,64,512]{2,1,0:T(8,128)S(1)}, u32[]{:S(2)}, u32[]{:S(2)}) collective-permute-start(f32[2,64,512]{2,1,0:T(8,128)S(1)} %get-tuple-element.38), channel_id=1, source_target_pairs={{0,4},{4,8},{8,12},{12,16},{16,20},{20,24},{24,28},{1,5},{5,9},{9,... | collective-permute-start | bytes 786440 | tf_op jit(solution)/shard_map/ppermute | solution.py:36
  115.4 8.4 %collective-permute-start.27 = (f32[2,64,512]{2,1,0:T(8,128)S(1)}, f32[2,64,512]{2,1,0:T(8,128)S(1)}, u32[]{:S(2)}, u32[]{:S(2)}) collective-permute-start(f32[2,64,512]{2,1,0:T(8,128)S(1)} %slice_add_fusion.1), channel_id=1, source_target_pairs={{0,2},{1,3},{2,0},{3,1},{4,6},{5,7},{6,4},{7,5},{8,10},{9,11},{10,... | collective-permute-start | bytes 786440 | tf_op jit(solution)/shard_map/ppermute | solution.py:30
  124.2 0.7 copy-start.3
  124.9 3.3 %collective-permute-start.30 = (f32[64,64]{1,0:T(8,128)S(1)}, f32[64,64]{1,0:T(8,128)S(1)}, u32[]{:S(2)}, u32[]{:S(2)}) collective-permute-start(f32[64,64]{1,0:T(8,128)S(1)} %get-tuple-element.41), channel_id=1, source_target_pairs={{0,3},{1,2},{2,1},{3,0},{4,7},{5,6},{6,5},{7,4},{8,11},{9,10},{10,... | collective-permute-start | bytes 49160 | tf_op jit(solution)/shard_map/ppermute | solution.py:30
  124.9 4.1 %collective-permute-start.29 = (f32[64,64]{1,0:T(8,128)S(1)}, f32[64,64]{1,0:T(8,128)S(1)}, u32[]{:S(2)}, u32[]{:S(2)}) collective-permute-start(f32[64,64]{1,0:T(8,128)S(1)} %get-tuple-element.41), channel_id=1, source_target_pairs={{0,2},{1,3},{2,0},{3,1},{4,6},{5,7},{6,4},{7,5},{8,10},{9,11},{10,... | collective-permute-start | bytes 49160 | tf_op jit(solution)/shard_map/ppermute | solution.py:30
  126.0 3.0 %collective-permute-start.28 = (f32[64,64]{1,0:T(8,128)S(1)}, f32[64,64]{1,0:T(8,128)S(1)}, u32[]{:S(2)}, u32[]{:S(2)}) collective-permute-start(f32[64,64]{1,0:T(8,128)S(1)} %get-tuple-element.41), channel_id=1, source_target_pairs={{0,1},{1,0},{2,3},{3,2},{4,5},{5,4},{6,7},{7,6},{8,9},{9,8},{10,11... | collective-permute-start | bytes 49160 | tf_op jit(solution)/shard_map/ppermute | solution.py:30
  129.1 8.6 %collective-permute-start.37 = (f32[64,64]{1,0:T(8,128)S(1)}, f32[64,64]{1,0:T(8,128)S(1)}, u32[]{:S(2)}, u32[]{:S(2)}) collective-permute-start(f32[64,64]{1,0:T(8,128)S(1)} %add_add_fusion.1), channel_id=1, source_target_pairs={{0,28},{4,24},{8,20},{12,16},{16,12},{20,8},{24,4},{28,0},{1,29},{... | collective-permute-start | bytes 49160 | tf_op jit(solution)/shard_map/ppermute | solution.py:30
  130.0 8.5 %collective-permute-start.36 = (f32[64,64]{1,0:T(8,128)S(1)}, f32[64,64]{1,0:T(8,128)S(1)}, u32[]{:S(2)}, u32[]{:S(2)}) collective-permute-start(f32[64,64]{1,0:T(8,128)S(1)} %add_add_fusion.1), channel_id=1, source_target_pairs={{0,24},{4,28},{8,16},{12,20},{16,8},{20,12},{24,0},{28,4},{1,25},{... | collective-permute-start | bytes 49160 | tf_op jit(solution)/shard_map/ppermute | solution.py:30
  132.7 7.6 %collective-permute-start.35 = (f32[64,64]{1,0:T(8,128)S(1)}, f32[64,64]{1,0:T(8,128)S(1)}, u32[]{:S(2)}, u32[]{:S(2)}) collective-permute-start(f32[64,64]{1,0:T(8,128)S(1)} %add_add_fusion.1), channel_id=1, source_target_pairs={{0,20},{4,16},{8,28},{12,24},{16,4},{20,0},{24,12},{28,8},{1,21},{... | collective-permute-start | bytes 49160 | tf_op jit(solution)/shard_map/ppermute | solution.py:30
  134.5 5.8 %collective-permute-start.34 = (f32[64,64]{1,0:T(8,128)S(1)}, f32[64,64]{1,0:T(8,128)S(1)}, u32[]{:S(2)}, u32[]{:S(2)}) collective-permute-start(f32[64,64]{1,0:T(8,128)S(1)} %add_add_fusion.1), channel_id=1, source_target_pairs={{0,16},{4,20},{8,24},{12,28},{16,0},{20,4},{24,8},{28,12},{1,17},{... | collective-permute-start | bytes 49160 | tf_op jit(solution)/shard_map/ppermute | solution.py:30
  136.8 4.8 %collective-permute-start.33 = (f32[64,64]{1,0:T(8,128)S(1)}, f32[64,64]{1,0:T(8,128)S(1)}, u32[]{:S(2)}, u32[]{:S(2)}) collective-permute-start(f32[64,64]{1,0:T(8,128)S(1)} %add_add_fusion.1), channel_id=1, source_target_pairs={{0,12},{4,8},{8,4},{12,0},{16,28},{20,24},{24,20},{28,16},{1,13},{... | collective-permute-start | bytes 49160 | tf_op jit(solution)/shard_map/ppermute | solution.py:30
  137.6 4.0 %collective-permute-start.32 = (f32[64,64]{1,0:T(8,128)S(1)}, f32[64,64]{1,0:T(8,128)S(1)}, u32[]{:S(2)}, u32[]{:S(2)}) collective-permute-start(f32[64,64]{1,0:T(8,128)S(1)} %add_add_fusion.1), channel_id=1, source_target_pairs={{0,8},{4,12},{8,0},{12,4},{16,24},{20,28},{24,16},{28,20},{1,9},{5... | collective-permute-start | bytes 49160 | tf_op jit(solution)/shard_map/ppermute | solution.py:30
  138.5 3.9 %collective-permute-start.31 = (f32[64,64]{1,0:T(8,128)S(1)}, f32[64,64]{1,0:T(8,128)S(1)}, u32[]{:S(2)}, u32[]{:S(2)}) collective-permute-start(f32[64,64]{1,0:T(8,128)S(1)} %add_add_fusion.1), channel_id=1, source_target_pairs={{0,4},{4,0},{8,12},{12,8},{16,20},{20,16},{24,28},{28,24},{1,5},{5... | collective-permute-start | bytes 49160 | tf_op jit(solution)/shard_map/ppermute | solution.py:30

commit v3 on v2

--- a/solution.py
+++ b/solution.py
@@ -45,66 +45,27 @@
     return bits
 
 
-def gather_near(value, axis, before=()):
+def gather_near(value, axis):
     held = {0: value}
     for bit in reversed(bits_of(lax.axis_size(axis))):
-        source = dict(held)
-        for rel in source:
-            if rel and before:
-                source[rel] = lax.optimization_barrier((source[rel],) + tuple(before))[0]
-            held[rel ^ bit] = swap(source[rel], axis, bit)
+        for rel in list(held):
+            held[rel ^ bit] = swap(held[rel], axis, bit)
     return [held[rel] for rel in range(len(held))]
 
 
-def prepare_kernel(group, cap, pts, counts, rows, cols, live, start, aug, out_rows, out_cols, out_n):
+def gather_far_bits(value):
+    held = {0: value}
+    for bit in reversed(bits_of(lax.axis_size("grp"))[1:]):
+        for rel in list(held):
+            held[rel ^ bit] = swap(held[rel], "grp", bit)
+    held.pop(0)
+    return held
+
+
+def augment_kernel(pts, counts, start, aug):
     columns, total = start.shape
     width = pts.shape[1]
-    blocks_dev = total // PTS
-    slab = blocks_dev * group
-    slots = rows.shape[0]
-    member = lax.axis_index("grp")
-
-    def local_near(block):
-        return (lax.div(block, blocks_dev) ^ member) * blocks_dev + lax.rem(block, blocks_dev)
-
-    def count_far(slot, carry):
-        col = cols[slot]
-        far = jnp.logical_and(slot < live[0], col >= slab)
-        owner = lax.div(col - slab, blocks_dev)
-        return tuple(
-            old + jnp.where(jnp.logical_and(far, owner == device), 1, 0)
-            for device, old in enumerate(carry)
-        )
-
-    far_counts = lax.fori_loop(0, slots, count_far, (jnp.int32(0),) * group)
-    low = jnp.int32(0)
-    room = jnp.int32(0)
-    for device in range(group):
-        low = low + jnp.where(device < member, cap - far_counts[device], 0)
-        room = room + jnp.where(device == member, cap - far_counts[device], 0)
-
-    def place(slot, carry):
-        near_rank, filled = carry
-        row, col = rows[slot], cols[slot]
-        used = slot < live[0]
-        far = col >= slab
-        mine_far = jnp.logical_and(far, lax.div(col - slab, blocks_dev) == member)
-        mine_near = jnp.logical_and(
-            jnp.logical_not(far), jnp.logical_and(near_rank >= low, near_rank < low + room)
-        )
-        mine = jnp.logical_and(used, jnp.logical_or(mine_far, mine_near))
-
-        @pl.when(mine)
-        def _():
-            out_rows[filled] = local_near(row)
-            out_cols[filled] = jnp.where(far, slab + lax.rem(col - slab, blocks_dev), local_near(col))
-
-        near_rank = near_rank + jnp.where(jnp.logical_and(used, jnp.logical_not(far)), 1, 0)
-        return (near_rank, filled + jnp.where(mine, 1, 0))
-
-    out_n[0] = lax.fori_loop(0, slots, place, (jnp.int32(0), jnp.int32(0)))[1]
-
-    for block in range(blocks_dev):
+    for block in range(total // PTS):
         lanes = slice(block * PTS, (block + 1) * PTS)
         wide = pts[lanes, :].astype(jnp.float32)
         norm = lax.dot_general(
@@ -129,22 +90,95 @@
         aug[columns : columns + EXTRA, lanes] = tail.astype(jnp.bfloat16)
 
 
-def prepare(points, counts, rows, cols, live, start, group, cap):
+def augment(points, counts, start):
     columns, total = start.shape
     return pl.pallas_call(
-        functools.partial(prepare_kernel, group, cap),
+        augment_kernel,
+        out_shape=jax.ShapeDtypeStruct((columns + EXTRA, total), jnp.bfloat16),
+        in_specs=[spec(VMEM), spec(SMEM), spec(VMEM)],
+        out_specs=spec(VMEM),
+        cost_estimate=cost(2**30, 2**24),
+        compiler_params=pltpu.CompilerParams(vmem_limit_bytes=24 * 2**20),
+        name="augment",
+    )(points, counts, start)
+
+
+def is_early(place, group, blocks_dev):
+    near_by = jnp.logical_and(place < min(2, group) * blocks_dev, place < group * blocks_dev)
+    return jnp.logical_or(near_by, lax.rem(place, blocks_dev) < blocks_dev // 2)
+
+
+def listing_kernel(group, cap, blocks_dev, rows, cols, live, out_rows, out_cols, out_n):
+    slab = blocks_dev * group
+    slots = rows.shape[0]
+    member = lax.axis_index("grp")
+
+    def local_near(block):
+        return (lax.div(block, blocks_dev) ^ member) * blocks_dev + lax.rem(block, blocks_dev)
+
+    def count_far(slot, carry):
+        col = cols[slot]
+        far = jnp.logical_and(slot < live[0], col >= slab)
+        owner = lax.div(col - slab, blocks_dev)
+        return tuple(
+            old + jnp.where(jnp.logical_and(far, owner == device), 1, 0)
+            for device, old in enumerate(carry)
+        )
+
+    far_counts = lax.fori_loop(0, slots, count_far, (jnp.int32(0),) * group)
+    low = jnp.int32(0)
+    room = jnp.int32(0)
+    for device in range(group):
+        low = low + jnp.where(device < member, cap - far_counts[device], 0)
+        room = room + jnp.where(device == member, cap - far_counts[device], 0)
+
+    def place_those(wanted, filled):
+        def place(slot, carry):
+            near_rank, filled = carry
+            row, col = rows[slot], cols[slot]
+            used = slot < live[0]
+            far = col >= slab
+            mine_far = jnp.logical_and(far, lax.div(col - slab, blocks_dev) == member)
+            mine_near = jnp.logical_and(
+                jnp.logical_not(far), jnp.logical_and(near_rank >= low, near_rank < low + room)
+            )
+            row_place = local_near(row)
+            col_place = jnp.where(far, slab + lax.rem(col - slab, blocks_dev), local_near(col))
+            early = jnp.logical_and(
+                is_early(row_place, group, blocks_dev), is_early(col_place, group, blocks_dev)
+            )
+            mine = jnp.logical_and(used, jnp.logical_or(mine_far, mine_near))
+            mine = jnp.logical_and(mine, early if wanted else jnp.logical_not(early))
+
+            @pl.when(mine)
+            def _():
+                out_rows[filled] = row_place
+                out_cols[filled] = col_place
+
+            near_rank = near_rank + jnp.where(jnp.logical_and(used, jnp.logical_not(far)), 1, 0)
+            return (near_rank, filled + jnp.where(mine, 1, 0))
+
+        return lax.fori_loop(0, slots, place, (jnp.int32(0), filled))[1]
+
+    early_count = place_those(True, jnp.int32(0))
+    out_n[0] = jnp.int32(0)
+    out_n[1] = early_count
+    out_n[2] = place_those(False, early_count)
+
+
+def listing(rows, cols, live, group, cap, blocks_dev):
+    return pl.pallas_call(
+        functools.partial(listing_kernel, group, cap, blocks_dev),
         out_shape=(
-            jax.ShapeDtypeStruct((columns + EXTRA, total), jnp.bfloat16),
             jax.ShapeDtypeStruct((cap,), jnp.int32),
             jax.ShapeDtypeStruct((cap,), jnp.int32),
-            jax.ShapeDtypeStruct((1,), jnp.int32),
+            jax.ShapeDtypeStruct((3,), jnp.int32),
         ),
-        in_specs=[spec(VMEM), spec(SMEM), spec(SMEM), spec(SMEM), spec(SMEM), spec(VMEM)],
-        out_specs=(spec(VMEM), spec(SMEM), spec(SMEM), spec(SMEM)),
-        compiler_params=pltpu.CompilerParams(vmem_limit_bytes=32 * 2**20),
-        cost_estimate=cost(2**30, 2**24),
-        name="prepare",
-    )(points, counts, rows, cols, live, start)
+        in_specs=[spec(SMEM)] * 3,
+        out_specs=(spec(SMEM),) * 3,
+        cost_estimate=cost(2**20, 2**10),
+        name="listing",
+    )(rows, cols, live)
 
 
 def message_rels(group):
@@ -182,27 +216,13 @@
     acc[col] += to_col[:height]
 
 
-def first_kernel(group, refs):
-    pieces = group + 1
-    n_ref, rows, cols, counts = refs[:4]
-    pts = refs[4 : 4 + pieces]
-    augs = refs[4 + pieces : 4 + 2 * pieces]
-    tiles_out = refs[4 + 2 * pieces]
-    messages = len(message_rels(group)) + 1
-    outs = refs[5 + 2 * pieces : 5 + 2 * pieces + messages]
-    window, u_win, level_row, level_col, acc = refs[5 + 2 * pieces + messages :]
-    kept = tiles_out
-    held = pts[0].shape[0]
-    width = pts[0].shape[1]
-    blocks_dev = held // PTS
+def setup_first(group, augs, counts, u_win, level_row, level_col, acc):
     columns = augs[0].shape[0] - EXTRA
     height = acc.shape[1]
-    for piece in range(pieces):
-        window[piece * held : (piece + 1) * held, :] = pts[piece][...]
-
+    blocks_dev = augs[0].shape[1] // PTS
     pick = lax.broadcasted_iota(jnp.int32, (EXTRA, 128), 0)
     pick = jnp.where(jnp.logical_and(pick >= 1, pick <= 3), 1.0, 0.0).astype(jnp.bfloat16)
-    for piece in range(pieces):
+    for piece in range(group + 1):
         for block in range(blocks_dev):
             place = piece * blocks_dev + block
             lanes = slice(block * PTS, (block + 1) * PTS)
@@ -222,7 +242,9 @@
         acc[block, 0:columns] = jnp.where(place_in < counts[block], own, 0.0)
         acc[block, columns:height] = jnp.ones((height - columns, PTS), jnp.float32)
 
-    n = n_ref[0]
+
+def make_tiles(low, high, rows, cols, window, u_win, level_row, level_col, kept, acc):
+    width = window.shape[1]
     step = 256
     scale = 6.0 / width * LOG2E
 
@@ -242,39 +264,82 @@
         add_products(acc, kept[index], u_win[row], u_win[col], row, col)
         return carry
 
-    lax.fori_loop(0, n, body, 0)
-    write_products(group, blocks_dev, acc, outs)
-
-
-def first_turn(n, rows, cols, counts, pts, augs, group, cap):
-    held, width = pts[0].shape
-    blocks_dev = held // PTS
-    places = (group + 1) * blocks_dev
+    lax.fori_loop(low, high, body, 0)
+
+
+def early_tiles(places, n, rows, cols, counts, pts, augs, group, cap):
+    width = pts[0].shape[1]
+    blocks_dev = augs[0].shape[1] // PTS
+    total = (group + 1) * blocks_dev
     tall = augs[0].shape[0]
     height = tall - EXTRA + 8
-    pieces = group + 1
-    shapes = [jax.ShapeDtypeStruct((cap, PTS, PTS), jnp.bfloat16)]
+    shapes = (
+        jax.ShapeDtypeStruct((total, tall, PTS), jnp.bfloat16),
+        jax.ShapeDtypeStruct((total, 8, PTS), jnp.float32),
+        jax.ShapeDtypeStruct((group * blocks_dev, PTS, 128), jnp.float32),
+        jax.ShapeDtypeStruct((cap, PTS, PTS), jnp.bfloat16),
+        jax.ShapeDtypeStruct((total, height, PTS), jnp.float32),
+    )
+
+    def kernel(*refs):
+        n_ref, row_ref, col_ref, count_ref = refs[:4]
+        pt_refs = refs[4 : 4 + len(pts)]
+        aug_refs = refs[4 + len(pts) : 4 + len(pts) + len(augs)]
+        u_win, level_row, level_col, kept, acc, window = refs[4 + len(pts) + len(augs) :]
+        for place, piece in zip(places, pt_refs):
+            window[place * PTS : place * PTS + piece.shape[0], :] = piece[...]
+        setup_first(group, aug_refs, count_ref, u_win, level_row, level_col, acc)
+        make_tiles(
+            n_ref[0], n_ref[1], row_ref, col_ref, window, u_win, level_row, level_col, kept, acc
+        )
+
+    return pl.pallas_call(
+        kernel,
+        out_shape=shapes,
+        in_specs=[spec(SMEM)] * 4 + [spec(VMEM)] * (len(pts) + len(augs)),
+        out_specs=(spec(VMEM),) * len(shapes),
+        scratch_shapes=[VMEM((total * PTS, width), jnp.bfloat16)],
+        cost_estimate=cost(2**20, 2**20),
+        compiler_params=pltpu.CompilerParams(vmem_limit_bytes=20 * 2**20),
+        name="early_tiles",
+    )(n, rows, cols, counts, *pts, *augs)
+
+
+def late_tiles(places, n, rows, cols, pts, state, group, blocks_dev):
+    u_win, level_row, level_col, kept, acc = state
+    total, height = acc.shape[:2]
+    width = pts[0].shape[1]
+    shapes = [jax.ShapeDtypeStruct(kept.shape, kept.dtype)]
     shapes += product_shapes(group, blocks_dev, height)
+    first = 3 + len(pts)
 
     def kernel(*refs):
-        first_kernel(group, refs)
+        n_ref, row_ref, col_ref = refs[:3]
+        pt_refs = refs[3:first]
+        u_win, level_row, level_col, acc_in, kept = refs[first : first + 5]
+        outs = refs[first + 5 : -2]
+        window, acc = refs[-2:]
+        for place, piece in zip(places, pt_refs):
+            window[place * PTS : place * PTS + piece.shape[0], :] = piece[...]
+        acc[...] = acc_in[...]
+        make_tiles(
+            n_ref[1], n_ref[2], row_ref, col_ref, window, u_win, level_row, level_col, kept, acc
+        )
+        write_products(group, blocks_dev, acc, outs)
 
     return pl.pallas_call(
         kernel,
         out_shape=tuple(shapes),
-        in_specs=[spec(SMEM)] * 4 + [spec(VMEM)] * (2 * pieces),
+        in_specs=[spec(SMEM)] * 3 + [spec(VMEM)] * (len(pts) + 4),
         out_specs=(spec(VMEM),) * len(shapes),
         scratch_shapes=[
-            VMEM((pieces * held, width), jnp.bfloat16),
-            VMEM((places, tall, PTS), jnp.bfloat16),
-            VMEM((places, 8, PTS), jnp.float32),
-            VMEM((group * blocks_dev, PTS, 128), jnp.float32),
-            VMEM((places, height, PTS), jnp.float32),
+            VMEM((total * PTS, width), jnp.bfloat16),
+            VMEM((total, height, PTS), jnp.float32),
         ],
-        compiler_params=pltpu.CompilerParams(vmem_limit_bytes=36 * 2**20),
         cost_estimate=cost(2**33, 2**25),
-        name="first_turn",
-    )(n, rows, cols, counts, *pts, *augs)
+        compiler_params=pltpu.CompilerParams(vmem_limit_bytes=20 * 2**20),
+        name="late_tiles",
+    )(n, rows, cols, *pts, u_win, level_row, level_col, acc)
 
 
 def scale_kernel(blocks_dev, has_degree, refs):
@@ -380,14 +445,12 @@
     pieces = group + 1
     n_ref, rows, cols, counts, gram = refs[:5]
     zs = refs[5 : 5 + pieces]
-    tiles = refs[5 + pieces]
+    tiles = refs[5 + pieces : 7 + pieces]
     messages = len(message_rels(group)) + 1
-    outs = refs[6 + pieces : 6 + pieces + messages]
-    u_win, acc = refs[6 + pieces + messages :]
+    outs = refs[7 + pieces : 7 + pieces + messages]
+    u_win, acc = refs[7 + pieces + messages :]
     columns, held = zs[0].shape
     blocks_dev = held // PTS
-    n = n_ref[0]
-
     inverse = inverse_factor(gram[...])
     for piece in range(pieces):
         for block in range(blocks_dev):
@@ -405,12 +468,14 @@
             else:
                 acc[place] = jnp.zeros((columns, PTS), jnp.float32)
 
-    def body(index, carry):
-        row, col = rows[index], cols[index]
-        add_products(acc, tiles[index], u_win[row], u_win[col], row, col)
-        return carry
-
-    lax.fori_loop(0, n, body, 0)
+    for stage, kept in enumerate(tiles):
+
+        def body(index, carry):
+            row, col = rows[index], cols[index]
+            add_products(acc, kept[index], u_win[row], u_win[col], row, col)
+            return carry
+
+        lax.fori_loop(n_ref[stage], n_ref[stage + 1], body, 0)
     write_products(group, blocks_dev, acc, outs)
 
 
@@ -427,7 +492,7 @@
     return pl.pallas_call(
         kernel,
         out_shape=tuple(shapes),
-        in_specs=[spec(SMEM)] * 4 + [spec(VMEM)] * (2 + pieces),
+        in_specs=[spec(SMEM)] * 4 + [spec(VMEM)] * (3 + pieces),
         out_specs=(spec(VMEM),) * len(shapes),
         scratch_shapes=[
             VMEM((places, columns, PTS), jnp.bfloat16),
@@ -436,7 +501,7 @@
         compiler_params=pltpu.CompilerParams(vmem_limit_bytes=24 * 2**20),
         cost_estimate=cost(2**32, 2**24),
         name="next_turn",
-    )(n, rows, cols, counts, gram, *zs, tiles)
+    )(n, rows, cols, counts, gram, *zs, *tiles)
 
 
 def embed_kernel(gram, z, out):
@@ -476,17 +541,10 @@
     return final
 
 
-def all_sum(value, axes):
-    for axis in axes:
-        bits = bits_of(lax.axis_size(axis))
-        while bits:
-            now, bits = bits[:3], bits[3:]
-            base = now[0]
-            terms = [value] + [swap(value, axis, base * rel) for rel in range(1, 2 ** len(now))]
-            while len(terms) > 1:
-                terms = [left + right for left, right in zip(terms[::2], terms[1::2])]
-            value = terms[0]
-    return value
+def all_sum(value):
+    for bit in bits_of(lax.axis_size("grp")):
+        value = value + swap(value, "grp", bit)
+    return jnp.sum(lax.all_gather(value, "blk", axis=0, tiled=False), axis=0)
 
 
 def per_device(points, counts, pair_rows, pair_cols, pair_live, start):
@@ -495,20 +553,54 @@
     columns = start.shape[0]
     slots = pair_rows.shape[0]
     cap = max(-(-slots // group), blocks_dev * blocks_dev * group)
-    aug, rows, cols, n = prepare(
-        points, counts, pair_rows, pair_cols, pair_live, start, group, cap
-    )
-    augs = gather_near(aug, "grp") + [from_behind(aug, "blk", -1)]
-    far = from_behind(points, "blk", -1)
-    pts = gather_near(points, "grp", augs + [far]) + [far]
-    tiles, *messages = first_turn(n, rows, cols, counts, pts, augs, group, cap)
+    half = (blocks_dev // 2) * PTS
+    aug = augment(points, counts, start)
+    mate_aug = swap(aug, "grp", 1)
+    far_aug = from_behind(aug, "blk", -1)
+    cross_aug = gather_far_bits(aug)
+    chunks = [points[:half], points[half:]]
+    chunks[1] = lax.optimization_barrier((chunks[1], mate_aug))[0]
+    rows, cols, n = listing(pair_rows, pair_cols, pair_live, group, cap, blocks_dev)
+    far = [from_behind(chunk, "blk", -1) for chunk in chunks]
+    crossed = [gather_far_bits(chunk) for chunk in chunks]
+    there = (mate_aug, far[0], far_aug, *cross_aug.values(), *crossed[0].values())
+    tied = lax.optimization_barrier(there)
+    mate_aug, far[0], far_aug = tied[:3]
+    for index, rel in enumerate(cross_aug):
+        cross_aug[rel] = tied[3 + index]
+        crossed[0][rel] = tied[3 + len(cross_aug) + index]
+    augs = {0: aug, 1: mate_aug}
+    for rel, value in cross_aug.items():
+        augs[rel] = value
+        augs[rel ^ 1] = swap(value, "grp", 1)
+    augs = [augs[rel] for rel in range(group)] + [far_aug]
+    mate = swap(points, "grp", 1)
+
+    def placed(index):
+        offset = index * (blocks_dev // 2)
+        found = [(group * blocks_dev + offset, far[index])]
+        for rel, value in crossed[index].items():
+            found.append((rel * blocks_dev + offset, value))
+            found.append(((rel ^ 1) * blocks_dev + offset, swap(value, "grp", 1)))
+        return found
+
+    early = [(0, points), (blocks_dev, mate)] + placed(0)
+    places, pts = zip(*early)
+    state = early_tiles(places, n, rows, cols, counts, pts, augs, group, cap)
+    tied = lax.optimization_barrier((far[1], *crossed[1].values(), state[4]))
+    far[1] = tied[0]
+    crossed[1] = dict(zip(crossed[1], tied[1:-1]))
+    state = (*state[:4], tied[-1])
+    places, pts = zip(*(early + placed(1)))
+    late, *messages = late_tiles(places, n, rows, cols, pts, state, group, blocks_dev)
+    tiles = (state[3], late)
     z, gram, degree = scaled_gram(sum_products(messages, group, blocks_dev), None, columns)
     for turn in range(1, ITERS):
         zs = gather_near(z, "grp") + [from_behind(z, "blk", -1)]
-        gram = all_sum(gram, ("grp", "blk"))
+        gram = all_sum(gram)
         messages = next_turn(n, rows, cols, counts, gram, zs, tiles, group, cap)
         z, gram = scaled_gram(sum_products(messages, group, blocks_dev), degree, columns)
-    return embedding(all_sum(gram, ("grp", "blk")), z)
+    return embedding(all_sum(gram), z)
 
 
 def solution(mesh):

time: 149 us -> 207 us (1.39)
  blocking collectives: 0 us -> 64 us
  starting transfers between devices: 41.1 us -> 19.4 us
  local copies, waits for them, and re-layouts: 5.02 us -> 23.6 us
  waiting for transfers between devices: 61.3 us -> 53.4 us
  Pallas kernels: 38 us -> 43.5 us
    all_gather x0 -> x2, blocking collectives: none -> 64 us  [all_sum(): return jnp.sum(lax.all_gather(value, 'blk', axis=0, tiled=False), axis=0)]
    ppermute x33 -> x19, starting transfers between devices: 34.7 us -> 7.85 us  [swap(): lax.ppermute(value, axis, [(source, source ^ bit) for source in range(cou...]
    unnamed x16 -> x40, local copies, waits for them, and re-layouts: 5.02 us -> 21.1 us
    ppermute x33 -> x19, waiting for transfers between devices: 47.2 us -> 37.5 us  [swap(): lax.ppermute(value, axis, [(source, source ^ bit) for source in range(cou...]
    pallas_call x2 -> x4, Pallas kernels: 22.8 us -> 28.9 us  [the longest x1 11.8 us: late_tiles(): pl.pallas_call(kernel, out_shape=tuple(shapes), in_specs=[spec(SMEM)] * 3...]
    ppermute x5 -> x6, starting transfers between devices: 6.45 us -> 11.6 us  [from_behind(): lax.ppermute(value, axis, [(source, source + steps) for source in range(i...]
    slice x0 -> x1, local copies, waits for them, and re-layouts: none -> 2.5 us  [per_device(): chunks = [points[:half], points[half:]]]
    ppermute x5 -> x6, waiting for transfers between devices: 14.1 us -> 15.9 us  [from_behind(): lax.ppermute(value, axis, [(source, source + steps) for source in range(i...]
  transfers between devices with their start and end apart: 38 -> 25, of which waited for: 18 -> 12; matrix products, arithmetic and copies ran while one was open for 0% -> 0% of each run, Pallas kernels for 4% -> 8%
where the time goes in v3:
time: 207 us; the launch traced here: 206 us
  blocking collectives  64 us (31%)
  waiting for transfers between devices  53.4 us (26%)
  Pallas kernels  43.5 us (21%)
  local copies, waits for them, and re-layouts  23.6 us (11%)
  starting transfers between devices  19.4 us (9%)
    all_gather x2, blocking collectives, all_sum(): return jnp.sum(lax.all_gather(value, 'blk', axis=0, tiled=False), axis=0)  64 us
    ppermute x19, waiting for transfers between devices, swap(): lax.ppermute(value, axis, [(source, source ^ bit) for source in range(cou...  37.5 us
    unnamed x40, local copies, waits for them, and re-layouts  21.1 us
    ppermute x6, waiting for transfers between devices, from_behind(): lax.ppermute(value, axis, [(source, source + steps) for source in range(i...  15.9 us
    pallas_call x1, Pallas kernels, late_tiles(): pl.pallas_call(kernel, out_shape=tuple(shapes), in_specs=[spec(SMEM)] * 3...  11.8 us
    ppermute x6, starting transfers between devices, from_behind(): lax.ppermute(value, axis, [(source, source + steps) for source in range(i...  11.6 us
    pallas_call x1, Pallas kernels, next_turn(): pl.pallas_call(kernel, out_shape=tuple(shapes), in_specs=[spec(SMEM)] * 4...  9.8 us
    ppermute x19, starting transfers between devices, swap(): lax.ppermute(value, axis, [(source, source ^ bit) for source in range(cou...  7.85 us
  transfers between devices with their start and end apart: 25, of which 12 were waited for; matrix products, arithmetic and copies ran while one was open for 0% of the time, Pallas kernels for 8%

profile of v3, /device:TPU:0, one launch (start us, length us, event | category | flops | bytes accessed | tf_op | source)
XLA Modules:
  0.0 205.6 jit_solution(2938934246786238761)
XLA Ops:
  0.0 2.5 %fusion = (bf16[512,768]{1,0:T(8,128)(2,1)}, bf16[512,768]{1,0:T(8,128)(2,1)S(1)}) fusion(bf16[1024,768]{1,0:T(8,128)(2,1)} %refs_3_.4), kind=kLoop, calls=%fused_computation.2 | loop fusion | bytes 3145728 | tf_op jit(solution)/shard_map/slice | solution.py:561
  2.5 2.9 %collective-permute-start.5 = (bf16[512,768]{1,0:T(8,128)(2,1)S(1)}, bf16[512,768]{1,0:T(8,128)(2,1)}, u32[]{:S(2)}, u32[]{:S(2)}) collective-permute-start(bf16[512,768]{1,0:T(8,128)(2,1)S(1)} %get-tuple-element.68), channel_id=1, source_target_pairs={{0,2},{1,3},{2,0},{3,1},{4,6},{5,7},{6,4},{7,5},{8,10},{9,11},{10,... | collective-permute-start | bytes 2359304 | tf_op jit(solution)/shard_map/ppermute | solution.py:30
  5.5 1.3 collective-permute-start.2
  6.8 0.1 collective-permute-start
  6.9 3.1 %augment.1.refs_9_ = bf16[80,1024]{1,0:T(8,128)(2,1)S(1)} custom-call(bf16[1024,768]{1,0:T(8,128)(2,1)S(1)} %copy-done.4, s32[2]{0:T(128)S(1)} %copy-done.11, f32[64,1024]{1,0:T(8,128)S(1)} %copy-done.18), custom_call_target="tpu_custom_call" | custom-call | flops 1073741824 | bytes 16777216 | tf_op jit(solution)/shard_map/augment/pallas_call | solution.py:95
  10.0 0.1 collective-permute-start.4
  10.1 1.3 collective-permute-start.3
  11.4 15.1 %collective-permute-done.4.refs_11_ = bf16[80,1024]{1,0:T(8,128)(2,1)S(1)} collective-permute-done((bf16[80,1024]{1,0:T(8,128)(2,1)S(1)}, bf16[80,1024]{1,0:T(8,128)(2,1)S(1)}, u32[]{:S(2)}, u32[]{:S(2)}) %collective-permute-start.4) | collective-permute-done | bytes 163872 | tf_op jit(solution)/shard_map/ppermute | solution.py:30
  26.5 3.3 %collective-permute-done.3.refs_13_ = bf16[80,1024]{1,0:T(8,128)(2,1)S(1)} collective-permute-done((bf16[80,1024]{1,0:T(8,128)(2,1)S(1)}, bf16[80,1024]{1,0:T(8,128)(2,1)S(1)}, u32[]{:S(2)}, u32[]{:S(2)}) %collective-permute-start.3) | collective-permute-done | bytes 163872 | tf_op jit(solution)/shard_map/ppermute | solution.py:36
  29.9 0.7 copy-done.7
  30.5 0.0 collective-permute-done.1.refs_10_
  30.5 0.7 copy-done.9
  31.2 0.9 copy-done.5
  32.1 0.0 collective-permute-start.6
  32.1 0.3 collective-permute-start.8
  32.4 1.3 collective-permute-start.7
  33.7 0.3 collective-permute-start.9
  34.6 6.1 %listing.1 = (s32[16]{0:T(128)}, s32[16]{0:T(128)}, s32[3]{0:T(128)}) custom-call(s32[64]{0:T(128)} %rows.1, s32[64]{0:T(128)} %cols.1, s32[1]{0:T(128)S(6)} %copy.7.live), custom_call_target="tpu_custom_call" | custom-call | flops 1048576 | bytes 1024 | tf_op jit(solution)/shard_map/listing/pallas_call | solution.py:170
  40.8 0.0 collective-permute-done.6.refs_8_.refs_7_
  40.8 1.1 copy-done.6
  41.9 0.9 copy-done.8
  42.8 0.9 copy-done.10
  43.7 0.7 copy-done.12
  44.4 0.6 copy-done.14
  45.0 0.7 copy-done.16
  45.6 7.8 %early_tiles.1 = (bf16[10,80,512]{2,1,0:T(8,128)(2,1)S(1)}, f32[10,8,512]{2,1,0:T(8,128)S(1)}, f32[8,512,128]{2,1,0:T(8,128)S(1)}, bf16[16,512,512]{2,1,0:T(8,128)(2,1)S(1)}, f32[10,72,512]{2,1,0:T(8,128)S(1)}) custom-call(s32[3]{0:T(128)S(1)} %copy-done.16, s32[16]{0:T(128)S(1)} %copy-done.12, s32[16]{0:T(128)S(1)} %copy-done.14, s32[2]{0:T(128)S(1)} %copy-done.11, ...), custom_call_target="tpu_custom_call" | custom-call | flops 1048576 | bytes 1048576 | tf_op jit(solution)/shard_map/early_tiles/pallas_call | solution.py:296
  53.5 3.3 %copy-done = bf16[16,512,512]{2,1,0:T(8,128)(2,1)} copy-done((bf16[16,512,512]{2,1,0:T(8,128)(2,1)}, bf16[16,512,512]{2,1,0:T(8,128)(2,1)S(1)}, u32[]{:S(2)}) %copy-start) | copy-done | bytes 8388632
  56.8 0.0 collective-permute-done.8.refs_9_
  56.8 0.0 collective-permute-done.7.refs_8_
  56.8 2.1 %collective-permute-start.10 = (bf16[512,768]{1,0:T(8,128)(2,1)}, bf16[512,768]{1,0:T(8,128)(2,1)S(1)}, u32[]{:S(2)}, u32[]{:S(2)}) collective-permute-start(bf16[512,768]{1,0:T(8,128)(2,1)} %collective-permute-done.8.refs_9_), channel_id=1, source_target_pairs={{0,1},{1,0},{2,3},{3,2},{4,5},{5,4},{6,7},{7,6},{8,9},{9,8},{10,11... | collective-permute-start | bytes 2359304 | tf_op jit(solution)/shard_map/ppermute | solution.py:30
  58.9 2.1 %collective-permute-done.10.refs_10_ = bf16[512,768]{1,0:T(8,128)(2,1)S(1)} collective-permute-done((bf16[512,768]{1,0:T(8,128)(2,1)}, bf16[512,768]{1,0:T(8,128)(2,1)S(1)}, u32[]{:S(2)}, u32[]{:S(2)}) %collective-permute-start.10) | collective-permute-done | bytes 786464 | tf_op jit(solution)/shard_map/ppermute | solution.py:30
  61.0 11.8 %late_tiles.1 = (bf16[16,512,512]{2,1,0:T(8,128)(2,1)S(1)}, f32[2,72,512]{2,1,0:T(8,128)S(1)}, f32[4,72,512]{2,1,0:T(8,128)S(1)}, f32[2,72,512]{2,1,0:T(8,128)S(1)}, f32[2,72,512]{2,1,0:T(8,128)S(1)}) custom-call(s32[3]{0:T(128)S(1)} %copy-done.16, s32[16]{0:T(128)S(1)} %copy-done.12, s32[16]{0:T(128)S(1)} %copy-done.14, bf16[1024,768]{1,0:T(8,128)(2,1)S(1)} %copy-done.4, ...), custom_call_target="tpu_custom_call" | custom-call | flops 8589934592 | bytes 33554432 | tf_op jit(solution)/shard_map/late_tiles/pallas_call | solution.py:330
  72.9 3.2 %copy-done.2 = bf16[16,512,512]{2,1,0:T(8,128)(2,1)} copy-done((bf16[16,512,512]{2,1,0:T(8,128)(2,1)}, bf16[16,512,512]{2,1,0:T(8,128)(2,1)S(1)}, u32[]{:S(2)}) %copy-start.2) | copy-done | bytes 8388632
  76.1 0.0 collective-permute-start.12
  76.1 3.4 %collective-permute-start.11 = (f32[2,72,512]{2,1,0:T(8,128)S(1)}, f32[2,72,512]{2,1,0:T(8,128)S(1)}, u32[]{:S(2)}, u32[]{:S(2)}) collective-permute-start(f32[2,72,512]{2,1,0:T(8,128)S(1)} %get-tuple-element.53), channel_id=1, source_target_pairs={{0,4},{4,8},{8,12},{12,16},{16,20},{20,24},{24,28},{1,5},{5,9},{9,... | collective-permute-start | bytes 884744 | tf_op jit(solution)/shard_map/ppermute | solution.py:36
  79.6 0.3 collective-permute-start.13
  80.0 6.5 %collective-permute-done.11.refs_1_ = f32[2,72,512]{2,1,0:T(8,128)S(1)} collective-permute-done((f32[2,72,512]{2,1,0:T(8,128)S(1)}, f32[2,72,512]{2,1,0:T(8,128)S(1)}, u32[]{:S(2)}, u32[]{:S(2)}) %collective-permute-start.11) | collective-permute-done | bytes 294944 | tf_op jit(solution)/shard_map/ppermute | solution.py:36
  86.4 2.4 %collective-permute-done.13.refs_3_ = f32[2,72,512]{2,1,0:T(8,128)S(1)} collective-permute-done((f32[2,72,512]{2,1,0:T(8,128)S(1)}, f32[2,72,512]{2,1,0:T(8,128)S(1)}, u32[]{:S(2)}, u32[]{:S(2)}) %collective-permute-start.13) | collective-permute-done | bytes 294944 | tf_op jit(solution)/shard_map/ppermute | solution.py:30
  88.8 0.4 scaled_gram.2
  89.3 0.4 collective-permute-start.17
  89.6 1.3 collective-permute-start.19
  90.9 0.1 collective-permute-start.16
  91.0 6.0 %collective-permute-done.17.refs_7_ = f32[64,1024]{1,0:T(8,128)S(1)} collective-permute-done((f32[64,1024]{1,0:T(8,128)S(1)}, f32[64,1024]{1,0:T(8,128)S(1)}, u32[]{:S(2)}, u32[]{:S(2)}) %collective-permute-start.17) | collective-permute-done | bytes 262176 | tf_op jit(solution)/shard_map/ppermute | solution.py:30
  96.9 0.5 collective-permute-start.14
  97.4 1.1 collective-permute-done.14
  98.5 0.3 collective-permute-start.15
  98.9 3.6 %collective-permute-done.15 = f32[64,64]{1,0:T(8,128)S(1)} collective-permute-done((f32[64,64]{1,0:T(8,128)S(1)}, f32[64,64]{1,0:T(8,128)S(1)}, u32[]{:S(2)}, u32[]{:S(2)}) %collective-permute-start.15) | collective-permute-done | bytes 16416 | tf_op jit(solution)/shard_map/ppermute | solution.py:30
  102.4 33.2 %all-gather = f32[512,64]{1,0:T(8,128)S(1)} all-gather(f32[64,64]{1,0:T(8,128)S(1)} %add.20), channel_id=2, replica_groups=mesh['blk'=8,'grp'=4] {'blk'}, dimensions={0}, use_global_device_ids=true | all-gather | bytes 147456 | tf_op jit(solution)/shard_map/all_gather | solution.py:547
  135.7 3.4 %copy-done.1 = bf16[16,512,512]{2,1,0:T(8,128)(2,1)S(1)} copy-done((bf16[16,512,512]{2,1,0:T(8,128)(2,1)S(1)}, bf16[16,512,512]{2,1,0:T(8,128)(2,1)}, u32[]{:S(2)}) %copy-start.1) | copy-done | bytes 8388632
  139.1 3.4 %copy-done.3 = bf16[16,512,512]{2,1,0:T(8,128)(2,1)S(1)} copy-done((bf16[16,512,512]{2,1,0:T(8,128)(2,1)S(1)}, bf16[16,512,512]{2,1,0:T(8,128)(2,1)}, u32[]{:S(2)}) %copy-start.3) | copy-done | bytes 8388632
  142.5 9.8 %next_turn.1 = (f32[2,64,512]{2,1,0:T(8,128)S(1)}, f32[4,64,512]{2,1,0:T(8,128)S(1)}, f32[2,64,512]{2,1,0:T(8,128)S(1)}, f32[2,64,512]{2,1,0:T(8,128)S(1)}) custom-call(s32[3]{0:T(128)S(1)} %copy-done.17, s32[16]{0:T(128)S(1)} %copy-done.13, s32[16]{0:T(128)S(1)} %copy-done.15, s32[2]{0:T(128)S(1)} %copy-done.11, f32[64,64]{1,0:T(8,128)S(1)} %reduce_sum.18.refs_4_, ...), custom_call_target="tpu_custom_call" | custom-call | flops 4294967296 | bytes 16777216 | tf_op jit(solution)/shard_map/next_turn/pallas_call | solution.py:492
  152.3 0.1 collective-permute-start.21
  152.3 3.0 %collective-permute-start.20 = (f32[2,64,512]{2,1,0:T(8,128)S(1)}, f32[2,64,512]{2,1,0:T(8,128)S(1)}, u32[]{:S(2)}, u32[]{:S(2)}) collective-permute-start(f32[2,64,512]{2,1,0:T(8,128)S(1)} %get-tuple-element.62), channel_id=1, source_target_pairs={{0,4},{4,8},{8,12},{12,16},{16,20},{20,24},{24,28},{1,5},{5,9},{9,... | collective-permute-start | bytes 786440 | tf_op jit(solution)/shard_map/ppermute | solution.py:36
  155.5 0.1 collective-permute-start.22
  155.5 6.0 %collective-permute-done.20.refs_2_ = f32[2,64,512]{2,1,0:T(8,128)S(1)} collective-permute-done((f32[2,64,512]{2,1,0:T(8,128)S(1)}, f32[2,64,512]{2,1,0:T(8,128)S(1)}, u32[]{:S(2)}, u32[]{:S(2)}) %collective-permute-start.20) | collective-permute-done | bytes 262176 | tf_op jit(solution)/shard_map/ppermute | solution.py:36
  161.6 2.4 %collective-permute-done.22.refs_4_ = f32[2,64,512]{2,1,0:T(8,128)S(1)} collective-permute-done((f32[2,64,512]{2,1,0:T(8,128)S(1)}, f32[2,64,512]{2,1,0:T(8,128)S(1)}, u32[]{:S(2)}, u32[]{:S(2)}) %collective-permute-start.22) | collective-permute-done | bytes 262176 | tf_op jit(solution)/shard_map/ppermute | solution.py:30
  163.9 0.4 scaled_gram.3
  164.3 0.7 copy-done.19
  165.0 1.2 collective-permute-done.23
  166.3 0.3 collective-permute-start.24
  166.5 3.6 %collective-permute-done.24 = f32[64,64]{1,0:T(8,128)S(1)} collective-permute-done((f32[64,64]{1,0:T(8,128)S(1)}, f32[64,64]{1,0:T(8,128)S(1)}, u32[]{:S(2)}, u32[]{:S(2)}) %collective-permute-start.24) | collective-permute-done | bytes 16416 | tf_op jit(solution)/shard_map/ppermute | solution.py:30
  170.2 30.8 %all-gather.1 = f32[512,64]{1,0:T(8,128)S(1)} all-gather(f32[64,64]{1,0:T(8,128)S(1)} %add.23), channel_id=3, replica_groups=mesh['blk'=8,'grp'=4] {'blk'}, dimensions={0}, use_global_device_ids=true | all-gather | bytes 147456 | tf_op jit(solution)/shard_map/all_gather | solution.py:547
  201.0 0.6 reduce_sum.19.gram
  201.6 4.0 %embedding.1 = f32[64,1024]{1,0:T(8,128)} custom-call(f32[64,64]{1,0:T(8,128)} %reduce_sum.19.gram, f32[64,1024]{1,0:T(8,128)} %copy-done.19), custom_call_target="tpu_custom_call" | custom-call | flops 1073741824 | bytes 1048576 | tf_op jit(solution)/shard_map/embedding/pallas_call | solution.py:514
  (45 shorter events, 0.2 us)
Async XLA Ops:
  0.0 6.7 %copy-start.4 = (bf16[1024,768]{1,0:T(8,128)(2,1)S(1)}, bf16[1024,768]{1,0:T(8,128)(2,1)}, u32[]{:S(2)}) copy-start(bf16[1024,768]{1,0:T(8,128)(2,1)} %refs_3_.4) | copy-start | bytes 4718596
  0.0 6.8 %copy-start.11 = (s32[2]{0:T(128)S(1)}, s32[2]{0:T(128)}, u32[]{:S(2)}) copy-start(s32[2]{0:T(128)} %refs_3_.5) | copy-start | bytes 28
  0.0 6.8 %copy-start.18 = (f32[64,1024]{1,0:T(8,128)S(1)}, f32[64,1024]{1,0:T(8,128)}, u32[]{:S(2)}) copy-start(f32[64,1024]{1,0:T(8,128)} %start.1) | copy-start | bytes 786436
  2.5 28.7 %collective-permute-start.5 = (bf16[512,768]{1,0:T(8,128)(2,1)S(1)}, bf16[512,768]{1,0:T(8,128)(2,1)}, u32[]{:S(2)}, u32[]{:S(2)}) collective-permute-start(bf16[512,768]{1,0:T(8,128)(2,1)S(1)} %get-tuple-element.68), channel_id=1, source_target_pairs={{0,2},{1,3},{2,0},{3,1},{4,6},{5,7},{6,4},{7,5},{8,10},{9,11},{10,... | collective-permute-start | bytes 2359304 | tf_op jit(solution)/shard_map/ppermute | solution.py:30
  5.5 25.7 %collective-permute-start.2 = (bf16[512,768]{1,0:T(8,128)(2,1)S(1)}, bf16[512,768]{1,0:T(8,128)(2,1)S(1)}, u32[]{:S(2)}, u32[]{:S(2)}) collective-permute-start(bf16[512,768]{1,0:T(8,128)(2,1)S(1)} %get-tuple-element.68), channel_id=1, source_target_pairs={{4,0},{8,4},{12,8},{16,12},{20,16},{24,20},{28,24},{5,1},{9,5},{13... | collective-permute-start | bytes 2359304 | tf_op jit(solution)/shard_map/ppermute | solution.py:36
  6.8 34.0 %collective-permute-start = (bf16[1024,768]{1,0:T(8,128)(2,1)S(1)}, bf16[1024,768]{1,0:T(8,128)(2,1)S(1)}, u32[]{:S(2)}, u32[]{:S(2)}) collective-permute-start(bf16[1024,768]{1,0:T(8,128)(2,1)S(1)} %copy-done.4), channel_id=1, source_target_pairs={{0,1},{1,0},{2,3},{3,2},{4,5},{5,4},{6,7},{7,6},{8,9},{9,8},{10,11... | collective-permute-start | bytes 4718600 | tf_op jit(solution)/shard_map/ppermute | solution.py:30
  10.0 16.5 %collective-permute-start.4 = (bf16[80,1024]{1,0:T(8,128)(2,1)S(1)}, bf16[80,1024]{1,0:T(8,128)(2,1)S(1)}, u32[]{:S(2)}, u32[]{:S(2)}) collective-permute-start(bf16[80,1024]{1,0:T(8,128)(2,1)S(1)} %augment.1.refs_9_), channel_id=1, source_target_pairs={{0,2},{1,3},{2,0},{3,1},{4,6},{5,7},{6,4},{7,5},{8,10},{9,11},{10,... | collective-permute-start | bytes 491528 | tf_op jit(solution)/shard_map/ppermute | solution.py:30
  10.1 19.8 %collective-permute-start.3 = (bf16[80,1024]{1,0:T(8,128)(2,1)S(1)}, bf16[80,1024]{1,0:T(8,128)(2,1)S(1)}, u32[]{:S(2)}, u32[]{:S(2)}) collective-permute-start(bf16[80,1024]{1,0:T(8,128)(2,1)S(1)} %augment.1.refs_9_), channel_id=1, source_target_pairs={{4,0},{8,4},{12,8},{16,12},{20,16},{24,20},{28,24},{5,1},{9,5},{13... | collective-permute-start | bytes 491528 | tf_op jit(solution)/shard_map/ppermute | solution.py:36
  26.5 4.0 %collective-permute-start.1 = (bf16[80,1024]{1,0:T(8,128)(2,1)S(1)}, bf16[80,1024]{1,0:T(8,128)(2,1)S(1)}, u32[]{:S(2)}, u32[]{:S(2)}) collective-permute-start(bf16[80,1024]{1,0:T(8,128)(2,1)S(1)} %augment.1.refs_9_), channel_id=1, source_target_pairs={{0,1},{1,0},{2,3},{3,2},{4,5},{5,4},{6,7},{7,6},{8,9},{9,8},{10,11... | collective-permute-start | bytes 491528 | tf_op jit(solution)/shard_map/ppermute | solution.py:30
  29.8 0.7 copy-start.7
  30.5 0.7 copy-start.9
  31.2 0.9 copy-start.5
  32.1 8.7 %collective-permute-start.6 = (bf16[512,768]{1,0:T(8,128)(2,1)}, bf16[512,768]{1,0:T(8,128)(2,1)}, u32[]{:S(2)}, u32[]{:S(2)}) collective-permute-start(bf16[512,768]{1,0:T(8,128)(2,1)} %collective-permute-done.5.refs_7_.refs_6_), channel_id=1, source_target_pairs={{0,1},{1,0},{2,3},{3,2},{4,5},{5,4},{6,7},{7,6},{8,9},{9,8},{10,11... | collective-permute-start | bytes 2359304 | tf_op jit(solution)/shard_map/ppermute | solution.py:30
  32.1 24.7 %collective-permute-start.8 = (bf16[512,768]{1,0:T(8,128)(2,1)}, bf16[512,768]{1,0:T(8,128)(2,1)}, u32[]{:S(2)}, u32[]{:S(2)}) collective-permute-start(bf16[512,768]{1,0:T(8,128)(2,1)} %get-tuple-element.41), channel_id=1, source_target_pairs={{0,2},{1,3},{2,0},{3,1},{4,6},{5,7},{6,4},{7,5},{8,10},{9,11},{10,... | collective-permute-start | bytes 2359304 | tf_op jit(solution)/shard_map/ppermute | solution.py:30
  32.4 24.4 %collective-permute-start.7 = (bf16[512,768]{1,0:T(8,128)(2,1)}, bf16[512,768]{1,0:T(8,128)(2,1)}, u32[]{:S(2)}, u32[]{:S(2)}) collective-permute-start(bf16[512,768]{1,0:T(8,128)(2,1)} %get-tuple-element.41), channel_id=1, source_target_pairs={{4,0},{8,4},{12,8},{16,12},{20,16},{24,20},{28,24},{5,1},{9,5},{13... | collective-permute-start | bytes 2359304 | tf_op jit(solution)/shard_map/ppermute | solution.py:36
  33.7 7.1 %collective-permute-start.9 = (bf16[80,1024]{1,0:T(8,128)(2,1)S(1)}, bf16[80,1024]{1,0:T(8,128)(2,1)}, u32[]{:S(2)}, u32[]{:S(2)}) collective-permute-start(bf16[80,1024]{1,0:T(8,128)(2,1)S(1)} %collective-permute-done.4.refs_11_), channel_id=1, source_target_pairs={{0,1},{1,0},{2,3},{3,2},{4,5},{5,4},{6,7},{7,6},{8,9},{9,8},{10,11... | collective-permute-start | bytes 491528 | tf_op jit(solution)/shard_map/ppermute | solution.py:30
  40.8 1.1 copy-start.6
  41.9 0.9 copy-start.8
  42.8 0.9 copy-start.10
  43.7 0.7 copy-start.12
  44.4 0.6 copy-start.14
  45.0 0.7 copy-start.16
  53.5 3.3 %copy-start = (bf16[16,512,512]{2,1,0:T(8,128)(2,1)}, bf16[16,512,512]{2,1,0:T(8,128)(2,1)S(1)}, u32[]{:S(2)}) copy-start(bf16[16,512,512]{2,1,0:T(8,128)(2,1)S(1)} %get-tuple-element.59.refs_10_) | copy-start | bytes 25165828
  56.8 4.3 %collective-permute-start.10 = (bf16[512,768]{1,0:T(8,128)(2,1)}, bf16[512,768]{1,0:T(8,128)(2,1)S(1)}, u32[]{:S(2)}, u32[]{:S(2)}) collective-permute-start(bf16[512,768]{1,0:T(8,128)(2,1)} %collective-permute-done.8.refs_9_), channel_id=1, source_target_pairs={{0,1},{1,0},{2,3},{3,2},{4,5},{5,4},{6,7},{7,6},{8,9},{9,8},{10,11... | collective-permute-start | bytes 2359304 | tf_op jit(solution)/shard_map/ppermute | solution.py:30
  72.9 3.2 %copy-start.2 = (bf16[16,512,512]{2,1,0:T(8,128)(2,1)}, bf16[16,512,512]{2,1,0:T(8,128)(2,1)S(1)}, u32[]{:S(2)}) copy-start(bf16[16,512,512]{2,1,0:T(8,128)(2,1)S(1)} %get-tuple-element.60.refs_11_) | copy-start | bytes 25165828
  76.1 3.4 %collective-permute-start.12 = (f32[4,72,512]{2,1,0:T(8,128)S(1)}, f32[4,72,512]{2,1,0:T(8,128)S(1)}, u32[]{:S(2)}, u32[]{:S(2)}) collective-permute-start(f32[4,72,512]{2,1,0:T(8,128)S(1)} %get-tuple-element.54), channel_id=1, source_target_pairs={{0,1},{1,0},{2,3},{3,2},{4,5},{5,4},{6,7},{7,6},{8,9},{9,8},{10,11... | collective-permute-start | bytes 1769480 | tf_op jit(solution)/shard_map/ppermute | solution.py:30
  76.1 10.3 %collective-permute-start.11 = (f32[2,72,512]{2,1,0:T(8,128)S(1)}, f32[2,72,512]{2,1,0:T(8,128)S(1)}, u32[]{:S(2)}, u32[]{:S(2)}) collective-permute-start(f32[2,72,512]{2,1,0:T(8,128)S(1)} %get-tuple-element.53), channel_id=1, source_target_pairs={{0,4},{4,8},{8,12},{12,16},{16,20},{20,24},{24,28},{1,5},{5,9},{9,... | collective-permute-start | bytes 884744 | tf_op jit(solution)/shard_map/ppermute | solution.py:36
  79.6 56.1 %copy-start.13 = (s32[16]{0:T(128)S(1)}, s32[16]{0:T(128)}, u32[]{:S(2)}) copy-start(s32[16]{0:T(128)} %get-tuple-element.37.refs_1_) | copy-start | bytes 196
  79.6 56.1 %copy-start.15 = (s32[16]{0:T(128)S(1)}, s32[16]{0:T(128)}, u32[]{:S(2)}) copy-start(s32[16]{0:T(128)} %get-tuple-element.38.refs_2_) | copy-start | bytes 196
  79.6 56.1 %copy-start.17 = (s32[3]{0:T(128)S(1)}, s32[3]{0:T(128)}, u32[]{:S(2)}) copy-start(s32[3]{0:T(128)} %get-tuple-element.36.refs_0_) | copy-start | bytes 40
  79.6 9.2 %collective-permute-start.13 = (f32[2,72,512]{2,1,0:T(8,128)S(1)}, f32[2,72,512]{2,1,0:T(8,128)S(1)}, u32[]{:S(2)}, u32[]{:S(2)}) collective-permute-start(f32[2,72,512]{2,1,0:T(8,128)S(1)} %slice_add_fusion), channel_id=1, source_target_pairs={{0,2},{1,3},{2,0},{3,1},{4,6},{5,7},{6,4},{7,5},{8,10},{9,11},{10,... | collective-permute-start | bytes 884744 | tf_op jit(solution)/shard_map/ppermute | solution.py:30
  89.3 7.7 %collective-permute-start.17 = (f32[64,1024]{1,0:T(8,128)S(1)}, f32[64,1024]{1,0:T(8,128)S(1)}, u32[]{:S(2)}, u32[]{:S(2)}) collective-permute-start(f32[64,1024]{1,0:T(8,128)S(1)} %get-tuple-element.58.refs_5_), channel_id=1, source_target_pairs={{0,2},{1,3},{2,0},{3,1},{4,6},{5,7},{6,4},{7,5},{8,10},{9,11},{10,... | collective-permute-start | bytes 786440 | tf_op jit(solution)/shard_map/ppermute | solution.py:30
  89.6 46.0 %collective-permute-start.19 = (f32[64,1024]{1,0:T(8,128)S(1)}, f32[64,1024]{1,0:T(8,128)S(1)}, u32[]{:S(2)}, u32[]{:S(2)}) collective-permute-start(f32[64,1024]{1,0:T(8,128)S(1)} %get-tuple-element.58.refs_5_), channel_id=1, source_target_pairs={{4,0},{8,4},{12,8},{16,12},{20,16},{24,20},{28,24},{5,1},{9,5},{13... | collective-permute-start | bytes 786440 | tf_op jit(solution)/shard_map/ppermute | solution.py:36
  90.9 44.7 %collective-permute-start.16 = (f32[64,1024]{1,0:T(8,128)S(1)}, f32[64,1024]{1,0:T(8,128)S(1)}, u32[]{:S(2)}, u32[]{:S(2)}) collective-permute-start(f32[64,1024]{1,0:T(8,128)S(1)} %get-tuple-element.58.refs_5_), channel_id=1, source_target_pairs={{0,1},{1,0},{2,3},{3,2},{4,5},{5,4},{6,7},{7,6},{8,9},{9,8},{10,11... | collective-permute-start | bytes 786440 | tf_op jit(solution)/shard_map/ppermute | solution.py:30
  96.9 38.7 %collective-permute-start.18 = (f32[64,1024]{1,0:T(8,128)S(1)}, f32[64,1024]{1,0:T(8,128)S(1)}, u32[]{:S(2)}, u32[]{:S(2)}) collective-permute-start(f32[64,1024]{1,0:T(8,128)S(1)} %collective-permute-done.17.refs_7_), channel_id=1, source_target_pairs={{0,1},{1,0},{2,3},{3,2},{4,5},{5,4},{6,7},{7,6},{8,9},{9,8},{10,11... | collective-permute-start | bytes 786440 | tf_op jit(solution)/shard_map/ppermute | solution.py:30
  96.9 1.6 collective-permute-start.14
  98.5 3.9 %collective-permute-start.15 = (f32[64,64]{1,0:T(8,128)S(1)}, f32[64,64]{1,0:T(8,128)S(1)}, u32[]{:S(2)}, u32[]{:S(2)}) collective-permute-start(f32[64,64]{1,0:T(8,128)S(1)} %add.19), channel_id=1, source_target_pairs={{0,2},{1,3},{2,0},{3,1},{4,6},{5,7},{6,4},{7,5},{8,10},{9,11},{10,... | collective-permute-start | bytes 49160 | tf_op jit(solution)/shard_map/ppermute | solution.py:30
  135.7 3.4 %copy-start.1 = (bf16[16,512,512]{2,1,0:T(8,128)(2,1)S(1)}, bf16[16,512,512]{2,1,0:T(8,128)(2,1)}, u32[]{:S(2)}) copy-start(bf16[16,512,512]{2,1,0:T(8,128)(2,1)} %copy-done) | copy-start | bytes 25165828
  139.1 3.4 %copy-start.3 = (bf16[16,512,512]{2,1,0:T(8,128)(2,1)S(1)}, bf16[16,512,512]{2,1,0:T(8,128)(2,1)}, u32[]{:S(2)}) copy-start(bf16[16,512,512]{2,1,0:T(8,128)(2,1)} %copy-done.2) | copy-start | bytes 25165828
  152.3 3.1 %collective-permute-start.21 = (f32[4,64,512]{2,1,0:T(8,128)S(1)}, f32[4,64,512]{2,1,0:T(8,128)S(1)}, u32[]{:S(2)}, u32[]{:S(2)}) collective-permute-start(f32[4,64,512]{2,1,0:T(8,128)S(1)} %get-tuple-element.63), channel_id=1, source_target_pairs={{0,1},{1,0},{2,3},{3,2},{4,5},{5,4},{6,7},{7,6},{8,9},{9,8},{10,11... | collective-permute-start | bytes 1572872 | tf_op jit(solution)/shard_map/ppermute | solution.py:30
  152.3 9.2 %collective-permute-start.20 = (f32[2,64,512]{2,1,0:T(8,128)S(1)}, f32[2,64,512]{2,1,0:T(8,128)S(1)}, u32[]{:S(2)}, u32[]{:S(2)}) collective-permute-start(f32[2,64,512]{2,1,0:T(8,128)S(1)} %get-tuple-element.62), channel_id=1, source_target_pairs={{0,4},{4,8},{8,12},{12,16},{16,20},{20,24},{24,28},{1,5},{5,9},{9,... | collective-permute-start | bytes 786440 | tf_op jit(solution)/shard_map/ppermute | solution.py:36
  155.5 8.5 %collective-permute-start.22 = (f32[2,64,512]{2,1,0:T(8,128)S(1)}, f32[2,64,512]{2,1,0:T(8,128)S(1)}, u32[]{:S(2)}, u32[]{:S(2)}) collective-permute-start(f32[2,64,512]{2,1,0:T(8,128)S(1)} %slice_add_fusion.1), channel_id=1, source_target_pairs={{0,2},{1,3},{2,0},{3,1},{4,6},{5,7},{6,4},{7,5},{8,10},{9,11},{10,... | collective-permute-start | bytes 786440 | tf_op jit(solution)/shard_map/ppermute | solution.py:30
  164.3 0.7 copy-start.19
  165.0 1.2 collective-permute-start.23
  166.3 3.9 %collective-permute-start.24 = (f32[64,64]{1,0:T(8,128)S(1)}, f32[64,64]{1,0:T(8,128)S(1)}, u32[]{:S(2)}, u32[]{:S(2)}) collective-permute-start(f32[64,64]{1,0:T(8,128)S(1)} %add.22), channel_id=1, source_target_pairs={{0,2},{1,3},{2,0},{3,1},{4,6},{5,7},{6,4},{7,5},{8,10},{9,11},{10,... | collective-permute-start | bytes 49160 | tf_op jit(solution)/shard_map/ppermute | solution.py:30

commit v4 on v3

--- a/solution.py
+++ b/solution.py
@@ -98,7 +98,7 @@
         in_specs=[spec(VMEM), spec(SMEM), spec(VMEM)],
         out_specs=spec(VMEM),
         cost_estimate=cost(2**30, 2**24),
-        compiler_params=pltpu.CompilerParams(vmem_limit_bytes=24 * 2**20),
+        compiler_params=pltpu.CompilerParams(vmem_limit_bytes=8 * 2**20),
         name="augment",
     )(points, counts, start)
 
@@ -108,7 +108,7 @@
     return jnp.logical_or(near_by, lax.rem(place, blocks_dev) < blocks_dev // 2)
 
 
-def listing_kernel(group, cap, blocks_dev, rows, cols, live, out_rows, out_cols, out_n):
+def listing_kernel(group, cap, early_cap, blocks_dev, rows, cols, live, out_rows, out_cols, out_n):
     slab = blocks_dev * group
     slots = rows.shape[0]
     member = lax.axis_index("grp")
@@ -134,7 +134,7 @@
 
     def place_those(wanted, filled):
         def place(slot, carry):
-            near_rank, filled = carry
+            near_rank, early_rank, filled = carry
             row, col = rows[slot], cols[slot]
             used = slot < live[0]
             far = col >= slab
@@ -148,6 +148,10 @@
                 is_early(row_place, group, blocks_dev), is_early(col_place, group, blocks_dev)
             )
             mine = jnp.logical_and(used, jnp.logical_or(mine_far, mine_near))
+            early = jnp.logical_and(early, mine)
+            room_left = early_rank < early_cap
+            early_rank = early_rank + jnp.where(early, 1, 0)
+            early = jnp.logical_and(early, room_left)
             mine = jnp.logical_and(mine, early if wanted else jnp.logical_not(early))
 
             @pl.when(mine)
@@ -156,9 +160,9 @@
                 out_cols[filled] = col_place
 
             near_rank = near_rank + jnp.where(jnp.logical_and(used, jnp.logical_not(far)), 1, 0)
-            return (near_rank, filled + jnp.where(mine, 1, 0))
-
-        return lax.fori_loop(0, slots, place, (jnp.int32(0), filled))[1]
+            return (near_rank, early_rank, filled + jnp.where(mine, 1, 0))
+
+        return lax.fori_loop(0, slots, place, (jnp.int32(0), jnp.int32(0), filled))[2]
 
     early_count = place_those(True, jnp.int32(0))
     out_n[0] = jnp.int32(0)
@@ -166,9 +170,9 @@
     out_n[2] = place_those(False, early_count)
 
 
-def listing(rows, cols, live, group, cap, blocks_dev):
+def listing(rows, cols, live, group, cap, early_cap, blocks_dev):
     return pl.pallas_call(
-        functools.partial(listing_kernel, group, cap, blocks_dev),
+        functools.partial(listing_kernel, group, cap, early_cap, blocks_dev),
         out_shape=(
             jax.ShapeDtypeStruct((cap,), jnp.int32),
             jax.ShapeDtypeStruct((cap,), jnp.int32),
@@ -177,6 +181,7 @@
         in_specs=[spec(SMEM)] * 3,
         out_specs=(spec(SMEM),) * 3,
         cost_estimate=cost(2**20, 2**10),
+        compiler_params=pltpu.CompilerParams(vmem_limit_bytes=2**20),
         name="listing",
     )(rows, cols, live)
 
@@ -260,14 +265,14 @@
             left_level = level_col[row, part * step : (part + 1) * step, :]
             left_level = jnp.concatenate([left_level] * (PTS // 128), axis=1)
             value = jnp.exp2(cross * scale - left_level - right_level)
-            kept[index, part * step : (part + 1) * step, :] = value.astype(jnp.bfloat16)
-        add_products(acc, kept[index], u_win[row], u_win[col], row, col)
+            kept[index - low, part * step : (part + 1) * step, :] = value.astype(jnp.bfloat16)
+        add_products(acc, kept[index - low], u_win[row], u_win[col], row, col)
         return carry
 
     lax.fori_loop(low, high, body, 0)
 
 
-def early_tiles(places, n, rows, cols, counts, pts, augs, group, cap):
+def early_tiles(places, n, rows, cols, counts, pts, augs, group, early_cap):
     width = pts[0].shape[1]
     blocks_dev = augs[0].shape[1] // PTS
     total = (group + 1) * blocks_dev
@@ -277,7 +282,7 @@
         jax.ShapeDtypeStruct((total, tall, PTS), jnp.bfloat16),
         jax.ShapeDtypeStruct((total, 8, PTS), jnp.float32),
         jax.ShapeDtypeStruct((group * blocks_dev, PTS, 128), jnp.float32),
-        jax.ShapeDtypeStruct((cap, PTS, PTS), jnp.bfloat16),
+        jax.ShapeDtypeStruct((early_cap, PTS, PTS), jnp.bfloat16),
         jax.ShapeDtypeStruct((total, height, PTS), jnp.float32),
     )
 
@@ -300,16 +305,16 @@
         out_specs=(spec(VMEM),) * len(shapes),
         scratch_shapes=[VMEM((total * PTS, width), jnp.bfloat16)],
         cost_estimate=cost(2**20, 2**20),
-        compiler_params=pltpu.CompilerParams(vmem_limit_bytes=20 * 2**20),
+        compiler_params=pltpu.CompilerParams(vmem_limit_bytes=14 * 2**20),
         name="early_tiles",
     )(n, rows, cols, counts, *pts, *augs)
 
 
-def late_tiles(places, n, rows, cols, pts, state, group, blocks_dev):
-    u_win, level_row, level_col, kept, acc = state
+def late_tiles(places, n, rows, cols, pts, state, group, blocks_dev, cap):
+    u_win, level_row, level_col, _, acc = state
     total, height = acc.shape[:2]
     width = pts[0].shape[1]
-    shapes = [jax.ShapeDtypeStruct(kept.shape, kept.dtype)]
+    shapes = [jax.ShapeDtypeStruct((cap, PTS, PTS), jnp.bfloat16)]
     shapes += product_shapes(group, blocks_dev, height)
     first = 3 + len(pts)
 
@@ -337,7 +342,7 @@
             VMEM((total, height, PTS), jnp.float32),
         ],
         cost_estimate=cost(2**33, 2**25),
-        compiler_params=pltpu.CompilerParams(vmem_limit_bytes=20 * 2**20),
+        compiler_params=pltpu.CompilerParams(vmem_limit_bytes=14 * 2**20),
         name="late_tiles",
     )(n, rows, cols, *pts, u_win, level_row, level_col, acc)
 
@@ -392,7 +397,7 @@
         out_shape=tuple(shapes),
         in_specs=[spec(VMEM)] * len(operands),
         out_specs=(spec(VMEM),) * len(shapes),
-        compiler_params=pltpu.CompilerParams(vmem_limit_bytes=32 * 2**20),
+        compiler_params=pltpu.CompilerParams(vmem_limit_bytes=6 * 2**20),
         cost_estimate=cost(2**26, 2**21),
         name="scaled_gram",
     )(*operands)
@@ -469,13 +474,14 @@
                 acc[place] = jnp.zeros((columns, PTS), jnp.float32)
 
     for stage, kept in enumerate(tiles):
+        low = n_ref[stage]
 
         def body(index, carry):
             row, col = rows[index], cols[index]
-            add_products(acc, kept[index], u_win[row], u_win[col], row, col)
+            add_products(acc, kept[index - low], u_win[row], u_win[col], row, col)
             return carry
 
-        lax.fori_loop(n_ref[stage], n_ref[stage + 1], body, 0)
+        lax.fori_loop(low, n_ref[stage + 1], body, 0)
     write_products(group, blocks_dev, acc, outs)
 
 
@@ -498,7 +504,7 @@
             VMEM((places, columns, PTS), jnp.bfloat16),
             VMEM((places, columns, PTS), jnp.float32),
         ],
-        compiler_params=pltpu.CompilerParams(vmem_limit_bytes=24 * 2**20),
+        compiler_params=pltpu.CompilerParams(vmem_limit_bytes=10 * 2**20),
         cost_estimate=cost(2**32, 2**24),
         name="next_turn",
     )(n, rows, cols, counts, gram, *zs, *tiles)
@@ -517,6 +523,7 @@
         in_specs=[spec(VMEM)] * 2,
         out_specs=spec(VMEM),
         cost_estimate=cost(2**30, 2**20),
+        compiler_params=pltpu.CompilerParams(vmem_limit_bytes=4 * 2**20),
         name="embedding",
     )(gram, z)
 
@@ -542,9 +549,10 @@
 
 
 def all_sum(value):
-    for bit in bits_of(lax.axis_size("grp")):
-        value = value + swap(value, "grp", bit)
-    return jnp.sum(lax.all_gather(value, "blk", axis=0, tiled=False), axis=0)
+    for axis in ("grp", "blk"):
+        for bit in bits_of(lax.axis_size(axis)):
+            value = value + swap(value, axis, bit)
+    return value
 
 
 def per_device(points, counts, pair_rows, pair_cols, pair_live, start):
@@ -553,22 +561,30 @@
     columns = start.shape[0]
     slots = pair_rows.shape[0]
     cap = max(-(-slots // group), blocks_dev * blocks_dev * group)
+    early_cap = cap // 2
     half = (blocks_dev // 2) * PTS
-    aug = augment(points, counts, start)
+    rows, cols, n = listing(pair_rows, pair_cols, pair_live, group, cap, early_cap, blocks_dev)
+    mate = swap(points, "grp", 1)
+    first = points[:half]
+    far = [from_behind(first, "blk", -1)]
+    crossed = [gather_far_bits(first)]
+    ready, mate = lax.optimization_barrier((points, mate))
+    aug = augment(ready, counts, start)
     mate_aug = swap(aug, "grp", 1)
     far_aug = from_behind(aug, "blk", -1)
     cross_aug = gather_far_bits(aug)
-    chunks = [points[:half], points[half:]]
-    chunks[1] = lax.optimization_barrier((chunks[1], mate_aug))[0]
-    rows, cols, n = listing(pair_rows, pair_cols, pair_live, group, cap, blocks_dev)
-    far = [from_behind(chunk, "blk", -1) for chunk in chunks]
-    crossed = [gather_far_bits(chunk) for chunk in chunks]
-    there = (mate_aug, far[0], far_aug, *cross_aug.values(), *crossed[0].values())
-    tied = lax.optimization_barrier(there)
-    mate_aug, far[0], far_aug = tied[:3]
-    for index, rel in enumerate(cross_aug):
-        cross_aug[rel] = tied[3 + index]
-        crossed[0][rel] = tied[3 + len(cross_aug) + index]
+    second = lax.optimization_barrier((points, aug))[0][half:]
+    tied = lax.optimization_barrier(
+        (mate_aug, n, rows, cols, second, far[0], *crossed[0].values())
+    )
+    mate_aug, n, rows, cols, second, far[0] = tied[:6]
+    crossed[0] = dict(zip(crossed[0], tied[6:]))
+    far.append(from_behind(second, "blk", -1))
+    crossed.append(gather_far_bits(second))
+    tied = lax.optimization_barrier((far_aug, *cross_aug.values(), *crossed[0].values()))
+    far_aug = tied[0]
+    cross_aug = dict(zip(cross_aug, tied[1 : 1 + len(cross_aug)]))
+    crossed[0] = dict(zip(crossed[0], tied[1 + len(cross_aug) :]))
     augs = {0: aug, 1: mate_aug}
     for rel, value in cross_aug.items():
         augs[rel] = value
@@ -586,13 +602,13 @@
 
     early = [(0, points), (blocks_dev, mate)] + placed(0)
     places, pts = zip(*early)
-    state = early_tiles(places, n, rows, cols, counts, pts, augs, group, cap)
+    state = early_tiles(places, n, rows, cols, counts, pts, augs, group, early_cap)
     tied = lax.optimization_barrier((far[1], *crossed[1].values(), state[4]))
     far[1] = tied[0]
     crossed[1] = dict(zip(crossed[1], tied[1:-1]))
     state = (*state[:4], tied[-1])
     places, pts = zip(*(early + placed(1)))
-    late, *messages = late_tiles(places, n, rows, cols, pts, state, group, blocks_dev)
+    late, *messages = late_tiles(places, n, rows, cols, pts, state, group, blocks_dev, cap)
     tiles = (state[3], late)
     z, gram, degree = scaled_gram(sum_products(messages, group, blocks_dev), None, columns)
     for turn in range(1, ITERS):

time: 207 us -> 146 us (0.71); the launches traced: 206 us -> 148 us
  blocking collectives: 64 us -> 0 us
  local copies, waits for them, and re-layouts: 23.6 us -> 4.38 us
  waiting for transfers between devices: 53.4 us -> 70.7 us
  starting transfers between devices: 19.4 us -> 30.8 us
  Pallas kernels: 43.5 us -> 40.8 us
    all_gather x2 -> x0, blocking collectives: 64 us -> none  [all_sum(): return jnp.sum(lax.all_gather(value, 'blk', axis=0, tiled=False), axis=0)]
    unnamed x40 -> x14, local copies, waits for them, and re-layouts: 21.1 us -> 3.02 us
    ppermute x19 -> x25, starting transfers between devices: 7.85 us -> 23.1 us  [swap(): lax.ppermute(value, axis, [(source, source ^ bit) for source in range(cou...]
    ppermute x19 -> x25, waiting for transfers between devices: 37.5 us -> 49.8 us  [swap(): lax.ppermute(value, axis, [(source, source ^ bit) for source in range(cou...]
    ppermute x6, waiting for transfers between devices: 15.9 us -> 20.9 us  [from_behind(): lax.ppermute(value, axis, [(source, source + steps) for source in range(i...]
    ppermute x6, starting transfers between devices: 11.6 us -> 7.72 us  [from_behind(): lax.ppermute(value, axis, [(source, source + steps) for source in range(i...]
    pallas_call x1, Pallas kernels: 11.8 us -> 9.59 us  [late_tiles(): pl.pallas_call(kernel, out_shape=tuple(shapes), in_specs=[spec(SMEM)] * 3...]
  transfers between devices with their start and end apart: 25 -> 31, of which waited for: 12 -> 24; matrix products, arithmetic and copies ran while one was open for 0% -> 1% of each run, Pallas kernels for 8% -> 12%
where the time goes in v4:
time: 146 us; the launch traced here: 148 us
  waiting for transfers between devices  70.7 us (48%)
  Pallas kernels  40.8 us (28%)
  starting transfers between devices  30.8 us (21%)
  local copies, waits for them, and re-layouts  4.38 us (3%)
    ppermute x25, waiting for transfers between devices, swap(): lax.ppermute(value, axis, [(source, source ^ bit) for source in range(cou...  49.8 us
    ppermute x25, starting transfers between devices, swap(): lax.ppermute(value, axis, [(source, source ^ bit) for source in range(cou...  23.1 us
    ppermute x6, waiting for transfers between devices, from_behind(): lax.ppermute(value, axis, [(source, source + steps) for source in range(i...  20.9 us
    pallas_call x1, Pallas kernels, next_turn(): pl.pallas_call(kernel, out_shape=tuple(shapes), in_specs=[spec(SMEM)] * 4...  9.8 us
    pallas_call x1, Pallas kernels, late_tiles(): pl.pallas_call(kernel, out_shape=tuple(shapes), in_specs=[spec(SMEM)] * 3...  9.59 us
    pallas_call x1, Pallas kernels, early_tiles(): pl.pallas_call(kernel, out_shape=shapes, in_specs=[spec(SMEM)] * 4 + [spe...  7.92 us
    ppermute x6, starting transfers between devices, from_behind(): lax.ppermute(value, axis, [(source, source + steps) for source in range(i...  7.72 us
    pallas_call x1, Pallas kernels, listing(): pl.pallas_call(functools.partial(listing_kernel, group, cap, early_cap, b...  6.52 us
  transfers between devices with their start and end apart: 31, of which 24 were waited for; matrix products, arithmetic and copies ran while one was open for 1% of the time, Pallas kernels for 12%

profile of v4, /device:TPU:0, one launch (start us, length us, event | category | flops | bytes accessed | tf_op | source)
XLA Modules:
  0.0 147.7 jit_solution(12246896706040083788)
XLA Ops:
  0.0 0.5 collective-permute-start
  0.5 1.3 slice.13
  1.8 2.6 %collective-permute-start.3 = (bf16[512,768]{1,0:T(8,128)(2,1)S(1)}, bf16[512,768]{1,0:T(8,128)(2,1)S(1)}, u32[]{:S(2)}, u32[]{:S(2)}) collective-permute-start(bf16[512,768]{1,0:T(8,128)(2,1)S(1)} %slice.13), channel_id=1, source_target_pairs={{0,2},{1,3},{2,0},{3,1},{4,6},{5,7},{6,4},{7,5},{8,10},{9,11},{10,... | collective-permute-start | bytes 2359304 | tf_op jit(solution)/shard_map/ppermute | solution.py:30
  4.3 1.3 collective-permute-start.2
  5.6 1.4 copy-done
  7.0 0.7 copy-done.2
  7.7 0.9 copy-done.4
  8.6 3.1 %augment.1.refs_9_ = bf16[80,1024]{1,0:T(8,128)(2,1)S(1)} custom-call(bf16[1024,768]{1,0:T(8,128)(2,1)S(1)} %copy-done, s32[2]{0:T(128)S(1)} %copy-done.2, f32[64,1024]{1,0:T(8,128)S(1)} %copy-done.4), custom_call_target="tpu_custom_call" | custom-call | flops 1073741824 | bytes 16777216 | tf_op jit(solution)/shard_map/augment/pallas_call | solution.py:95
  11.8 0.3 collective-permute-start.1
  12.1 0.9 collective-permute-start.5
  12.9 1.3 collective-permute-start.4
  14.9 6.5 %listing.1 = (s32[16]{0:T(128)S(1)}, s32[16]{0:T(128)S(1)}, s32[3]{0:T(128)S(1)}) custom-call(s32[64]{0:T(128)S(1)} %copy-done.5, s32[64]{0:T(128)S(1)} %copy-done.6, s32[1]{0:T(128)S(6)} %copy.7.live), custom_call_target="tpu_custom_call" | custom-call | flops 1048576 | bytes 1024 | tf_op jit(solution)/shard_map/listing/pallas_call | solution.py:174
  21.5 1.2 collective-permute-done.3.refs_7_.refs_6_
  22.7 3.9 %collective-permute-done.2.refs_6_.refs_5_ = bf16[512,768]{1,0:T(8,128)(2,1)S(1)} collective-permute-done((bf16[512,768]{1,0:T(8,128)(2,1)S(1)}, bf16[512,768]{1,0:T(8,128)(2,1)S(1)}, u32[]{:S(2)}, u32[]{:S(2)}) %collective-permute-start.2) | collective-permute-done | bytes 786464 | tf_op jit(solution)/shard_map/ppermute | solution.py:36
  26.6 2.8 %collective-permute-done.4.refs_13_ = bf16[80,1024]{1,0:T(8,128)(2,1)S(1)} collective-permute-done((bf16[80,1024]{1,0:T(8,128)(2,1)S(1)}, bf16[80,1024]{1,0:T(8,128)(2,1)S(1)}, u32[]{:S(2)}, u32[]{:S(2)}) %collective-permute-start.4) | collective-permute-done | bytes 163872 | tf_op jit(solution)/shard_map/ppermute | solution.py:36
  29.4 0.3 collective-permute-start.8
  29.7 1.3 collective-permute-start.7
  31.0 0.3 collective-permute-start.9
  31.3 1.2 collective-permute-done.9.refs_12_
  32.5 7.9 %early_tiles.1 = (bf16[10,80,512]{2,1,0:T(8,128)(2,1)S(1)}, f32[10,8,512]{2,1,0:T(8,128)S(1)}, f32[8,512,128]{2,1,0:T(8,128)S(1)}, bf16[8,512,512]{2,1,0:T(8,128)(2,1)S(1)}, f32[10,72,512]{2,1,0:T(8,128)S(1)}) custom-call(s32[3]{0:T(128)S(1)} %get-tuple-element.47.refs_0_, s32[16]{0:T(128)S(1)} %get-tuple-element.48.refs_1_, ...), custom_call_target="tpu_custom_call" | custom-call | flops 1048576 | bytes 1048576 | tf_op jit(solution)/shard_map/early_tiles/pallas_call | solution.py:301
  40.4 8.9 %collective-permute-done.8.refs_9_ = bf16[512,768]{1,0:T(8,128)(2,1)S(1)} collective-permute-done((bf16[512,768]{1,0:T(8,128)(2,1)S(1)}, bf16[512,768]{1,0:T(8,128)(2,1)S(1)}, u32[]{:S(2)}, u32[]{:S(2)}) %collective-permute-start.8) | collective-permute-done | bytes 786464 | tf_op jit(solution)/shard_map/ppermute | solution.py:30
  49.3 2.8 %collective-permute-done.7.refs_8_ = bf16[512,768]{1,0:T(8,128)(2,1)S(1)} collective-permute-done((bf16[512,768]{1,0:T(8,128)(2,1)S(1)}, bf16[512,768]{1,0:T(8,128)(2,1)S(1)}, u32[]{:S(2)}, u32[]{:S(2)}) %collective-permute-start.7) | collective-permute-done | bytes 786464 | tf_op jit(solution)/shard_map/ppermute | solution.py:36
  52.2 2.3 %collective-permute-done.10.refs_10_ = bf16[512,768]{1,0:T(8,128)(2,1)S(1)} collective-permute-done((bf16[512,768]{1,0:T(8,128)(2,1)S(1)}, bf16[512,768]{1,0:T(8,128)(2,1)S(1)}, u32[]{:S(2)}, u32[]{:S(2)}) %collective-permute-start.10) | collective-permute-done | bytes 786464 | tf_op jit(solution)/shard_map/ppermute | solution.py:30
  54.4 9.6 %late_tiles.1 = (bf16[16,512,512]{2,1,0:T(8,128)(2,1)S(1)}, f32[2,72,512]{2,1,0:T(8,128)S(1)}, f32[4,72,512]{2,1,0:T(8,128)S(1)}, f32[2,72,512]{2,1,0:T(8,128)S(1)}, f32[2,72,512]{2,1,0:T(8,128)S(1)}) custom-call(s32[3]{0:T(128)S(1)} %get-tuple-element.47.refs_0_, s32[16]{0:T(128)S(1)} %get-tuple-element.48.refs_1_, s32[16]{0:T(128)S(1)} %get-tuple-element.49.refs_2_, ...), custom_call_target="tpu_custom_call" | custom-call | flops 8589934592 | bytes 33554432 | tf_op jit(solution)/shard_map/late_tiles/pallas_call | solution.py:335
  64.0 1.1 collective-permute-start.12
  65.2 1.3 collective-permute-start.11
  66.5 0.3 collective-permute-done.12.refs_2_
  66.9 0.1 collective-permute-start.13
  66.9 6.2 %collective-permute-done.11.refs_1_ = f32[2,72,512]{2,1,0:T(8,128)S(1)} collective-permute-done((f32[2,72,512]{2,1,0:T(8,128)S(1)}, f32[2,72,512]{2,1,0:T(8,128)S(1)}, u32[]{:S(2)}, u32[]{:S(2)}) %collective-permute-start.11) | collective-permute-done | bytes 294944 | tf_op jit(solution)/shard_map/ppermute | solution.py:36
  73.2 3.0 %collective-permute-done.13.refs_3_ = f32[2,72,512]{2,1,0:T(8,128)S(1)} collective-permute-done((f32[2,72,512]{2,1,0:T(8,128)S(1)}, f32[2,72,512]{2,1,0:T(8,128)S(1)}, u32[]{:S(2)}, u32[]{:S(2)}) %collective-permute-start.13) | collective-permute-done | bytes 294944 | tf_op jit(solution)/shard_map/ppermute | solution.py:30
  76.2 0.4 scaled_gram.2
  76.6 0.4 collective-permute-start.20
  77.0 1.3 collective-permute-start.22
  78.3 0.1 collective-permute-start.19
  78.3 6.1 %collective-permute-done.20.refs_7_ = f32[64,1024]{1,0:T(8,128)S(1)} collective-permute-done((f32[64,1024]{1,0:T(8,128)S(1)}, f32[64,1024]{1,0:T(8,128)S(1)}, u32[]{:S(2)}, u32[]{:S(2)}) %collective-permute-start.20) | collective-permute-done | bytes 262176 | tf_op jit(solution)/shard_map/ppermute | solution.py:30
  84.5 0.5 collective-permute-start.14
  85.0 1.1 collective-permute-done.14
  86.1 0.5 collective-permute-start.15
  86.6 3.4 %collective-permute-done.15 = f32[64,64]{1,0:T(8,128)S(1)} collective-permute-done((f32[64,64]{1,0:T(8,128)S(1)}, f32[64,64]{1,0:T(8,128)S(1)}, u32[]{:S(2)}, u32[]{:S(2)}) %collective-permute-start.15) | collective-permute-done | bytes 16416 | tf_op jit(solution)/shard_map/ppermute | solution.py:30
  90.0 3.8 %collective-permute-start.16 = (f32[64,64]{1,0:T(8,128)S(1)}, f32[64,64]{1,0:T(8,128)S(1)}, u32[]{:S(2)}, u32[]{:S(2)}) collective-permute-start(f32[64,64]{1,0:T(8,128)S(1)} %add.38), channel_id=1, source_target_pairs={{0,4},{4,0},{8,12},{12,8},{16,20},{20,16},{24,28},{28,24},{1,5},{5... | collective-permute-start | bytes 49160 | tf_op jit(solution)/shard_map/ppermute | solution.py:30
  93.8 1.9 %collective-permute-done.16 = f32[64,64]{1,0:T(8,128)S(1)} collective-permute-done((f32[64,64]{1,0:T(8,128)S(1)}, f32[64,64]{1,0:T(8,128)S(1)}, u32[]{:S(2)}, u32[]{:S(2)}) %collective-permute-start.16) | collective-permute-done | bytes 16416 | tf_op jit(solution)/shard_map/ppermute | solution.py:30
  95.7 1.9 %collective-permute-start.17 = (f32[64,64]{1,0:T(8,128)S(1)}, f32[64,64]{1,0:T(8,128)S(1)}, u32[]{:S(2)}, u32[]{:S(2)}) collective-permute-start(f32[64,64]{1,0:T(8,128)S(1)} %add.39), channel_id=1, source_target_pairs={{0,8},{4,12},{8,0},{12,4},{16,24},{20,28},{24,16},{28,20},{1,9},{5... | collective-permute-start | bytes 49160 | tf_op jit(solution)/shard_map/ppermute | solution.py:30
  97.6 2.0 %collective-permute-done.17 = f32[64,64]{1,0:T(8,128)S(1)} collective-permute-done((f32[64,64]{1,0:T(8,128)S(1)}, f32[64,64]{1,0:T(8,128)S(1)}, u32[]{:S(2)}, u32[]{:S(2)}) %collective-permute-start.17) | collective-permute-done | bytes 16416 | tf_op jit(solution)/shard_map/ppermute | solution.py:30
  99.6 1.9 %collective-permute-start.18 = (f32[64,64]{1,0:T(8,128)S(1)}, f32[64,64]{1,0:T(8,128)S(1)}, u32[]{:S(2)}, u32[]{:S(2)}) collective-permute-start(f32[64,64]{1,0:T(8,128)S(1)} %add.40), channel_id=1, source_target_pairs={{0,16},{4,20},{8,24},{12,28},{16,0},{20,4},{24,8},{28,12},{1,17},{... | collective-permute-start | bytes 49160 | tf_op jit(solution)/shard_map/ppermute | solution.py:30
  101.5 2.9 %collective-permute-done.18 = f32[64,64]{1,0:T(8,128)S(1)} collective-permute-done((f32[64,64]{1,0:T(8,128)S(1)}, f32[64,64]{1,0:T(8,128)S(1)}, u32[]{:S(2)}, u32[]{:S(2)}) %collective-permute-start.18) | collective-permute-done | bytes 16416 | tf_op jit(solution)/shard_map/ppermute | solution.py:30
  104.4 9.8 %next_turn.1 = (f32[2,64,512]{2,1,0:T(8,128)S(1)}, f32[4,64,512]{2,1,0:T(8,128)S(1)}, f32[2,64,512]{2,1,0:T(8,128)S(1)}, f32[2,64,512]{2,1,0:T(8,128)S(1)}) custom-call(s32[3]{0:T(128)S(1)} %get-tuple-element.47.refs_0_, s32[16]{0:T(128)S(1)} %get-tuple-element.48.refs_1_, s32[16]{0:T(128)S(1)} %get-tuple-element.49.refs_2_, s32[2]{0:T(128)S(1)} %copy-done.3, ...), custom_call_target="tpu_custom_call" | custom-call | flops 4294967296 | bytes 16777216 | tf_op jit(solution)/shard_map/next_turn/pallas_call | solution.py:498
  114.2 0.1 collective-permute-start.24
  114.3 1.3 collective-permute-start.23
  115.6 0.6 collective-permute-done.24.refs_3_
  116.3 0.7 collective-permute-start.25
  117.0 5.1 %collective-permute-done.23.refs_2_ = f32[2,64,512]{2,1,0:T(8,128)S(1)} collective-permute-done((f32[2,64,512]{2,1,0:T(8,128)S(1)}, f32[2,64,512]{2,1,0:T(8,128)S(1)}, u32[]{:S(2)}, u32[]{:S(2)}) %collective-permute-start.23) | collective-permute-done | bytes 262176 | tf_op jit(solution)/shard_map/ppermute | solution.py:36
  122.1 2.6 %collective-permute-done.25.refs_4_ = f32[2,64,512]{2,1,0:T(8,128)S(1)} collective-permute-done((f32[2,64,512]{2,1,0:T(8,128)S(1)}, f32[2,64,512]{2,1,0:T(8,128)S(1)}, u32[]{:S(2)}, u32[]{:S(2)}) %collective-permute-start.25) | collective-permute-done | bytes 262176 | tf_op jit(solution)/shard_map/ppermute | solution.py:30
  124.7 0.4 scaled_gram.3
  125.1 0.1 collective-permute-start.26
  125.2 1.2 collective-permute-done.26
  126.4 0.6 collective-permute-start.27
  127.0 3.3 %collective-permute-done.27 = f32[64,64]{1,0:T(8,128)S(1)} collective-permute-done((f32[64,64]{1,0:T(8,128)S(1)}, f32[64,64]{1,0:T(8,128)S(1)}, u32[]{:S(2)}, u32[]{:S(2)}) %collective-permute-start.27) | collective-permute-done | bytes 16416 | tf_op jit(solution)/shard_map/ppermute | solution.py:30
  130.3 3.7 %collective-permute-start.28 = (f32[64,64]{1,0:T(8,128)S(1)}, f32[64,64]{1,0:T(8,128)S(1)}, u32[]{:S(2)}, u32[]{:S(2)}) collective-permute-start(f32[64,64]{1,0:T(8,128)S(1)} %add.44), channel_id=1, source_target_pairs={{0,4},{4,0},{8,12},{12,8},{16,20},{20,16},{24,28},{28,24},{1,5},{5... | collective-permute-start | bytes 49160 | tf_op jit(solution)/shard_map/ppermute | solution.py:30
  134.0 1.9 %collective-permute-done.28 = f32[64,64]{1,0:T(8,128)S(1)} collective-permute-done((f32[64,64]{1,0:T(8,128)S(1)}, f32[64,64]{1,0:T(8,128)S(1)}, u32[]{:S(2)}, u32[]{:S(2)}) %collective-permute-start.28) | collective-permute-done | bytes 16416 | tf_op jit(solution)/shard_map/ppermute | solution.py:30
  135.9 1.6 %collective-permute-start.29 = (f32[64,64]{1,0:T(8,128)S(1)}, f32[64,64]{1,0:T(8,128)S(1)}, u32[]{:S(2)}, u32[]{:S(2)}) collective-permute-start(f32[64,64]{1,0:T(8,128)S(1)} %add.45), channel_id=1, source_target_pairs={{0,8},{4,12},{8,0},{12,4},{16,24},{20,28},{24,16},{28,20},{1,9},{5... | collective-permute-start | bytes 49160 | tf_op jit(solution)/shard_map/ppermute | solution.py:30
  137.5 2.3 %collective-permute-done.29 = f32[64,64]{1,0:T(8,128)S(1)} collective-permute-done((f32[64,64]{1,0:T(8,128)S(1)}, f32[64,64]{1,0:T(8,128)S(1)}, u32[]{:S(2)}, u32[]{:S(2)}) %collective-permute-start.29) | collective-permute-done | bytes 16416 | tf_op jit(solution)/shard_map/ppermute | solution.py:30
  139.8 1.3 collective-permute-start.30
  141.1 3.5 %collective-permute-done.30 = f32[64,64]{1,0:T(8,128)S(1)} collective-permute-done((f32[64,64]{1,0:T(8,128)S(1)}, f32[64,64]{1,0:T(8,128)S(1)}, u32[]{:S(2)}, u32[]{:S(2)}) %collective-permute-start.30) | collective-permute-done | bytes 16416 | tf_op jit(solution)/shard_map/ppermute | solution.py:30
  144.7 3.0 %embedding.1 = f32[64,1024]{1,0:T(8,128)} custom-call(f32[64,64]{1,0:T(8,128)S(1)} %add.47.gram, f32[64,1024]{1,0:T(8,128)S(1)} %get-tuple-element.78.z), custom_call_target="tpu_custom_call" | custom-call | flops 1073741824 | bytes 1048576 | tf_op jit(solution)/shard_map/embedding/pallas_call | solution.py:520
  (34 shorter events, 0.2 us)
Async XLA Ops:
  0.0 5.6 %collective-permute-start = (bf16[1024,768]{1,0:T(8,128)(2,1)}, bf16[1024,768]{1,0:T(8,128)(2,1)S(1)}, u32[]{:S(2)}, u32[]{:S(2)}) collective-permute-start(bf16[1024,768]{1,0:T(8,128)(2,1)} %refs_3_.4), channel_id=1, source_target_pairs={{0,1},{1,0},{2,3},{3,2},{4,5},{5,4},{6,7},{7,6},{8,9},{9,8},{10,11... | collective-permute-start | bytes 4718600 | tf_op jit(solution)/shard_map/ppermute | solution.py:30
  0.5 21.0 %copy-start.1 = (bf16[1024,768]{1,0:T(8,128)(2,1)S(1)}, bf16[1024,768]{1,0:T(8,128)(2,1)}, u32[]{:S(2)}) copy-start(bf16[1024,768]{1,0:T(8,128)(2,1)} %refs_3_.4) | copy-start | bytes 4718596
  1.8 20.9 %collective-permute-start.3 = (bf16[512,768]{1,0:T(8,128)(2,1)S(1)}, bf16[512,768]{1,0:T(8,128)(2,1)S(1)}, u32[]{:S(2)}, u32[]{:S(2)}) collective-permute-start(bf16[512,768]{1,0:T(8,128)(2,1)S(1)} %slice.13), channel_id=1, source_target_pairs={{0,2},{1,3},{2,0},{3,1},{4,6},{5,7},{6,4},{7,5},{8,10},{9,11},{10,... | collective-permute-start | bytes 2359304 | tf_op jit(solution)/shard_map/ppermute | solution.py:30
  4.3 22.3 %collective-permute-start.2 = (bf16[512,768]{1,0:T(8,128)(2,1)S(1)}, bf16[512,768]{1,0:T(8,128)(2,1)S(1)}, u32[]{:S(2)}, u32[]{:S(2)}) collective-permute-start(bf16[512,768]{1,0:T(8,128)(2,1)S(1)} %slice.13), channel_id=1, source_target_pairs={{4,0},{8,4},{12,8},{16,12},{20,16},{24,20},{28,24},{5,1},{9,5},{13... | collective-permute-start | bytes 2359304 | tf_op jit(solution)/shard_map/ppermute | solution.py:36
  5.6 1.4 copy-start
  7.0 0.7 copy-start.2
  7.7 0.9 copy-start.4
  8.6 6.2 %copy-start.5 = (s32[64]{0:T(128)S(1)}, s32[64]{0:T(128)}, u32[]{:S(2)}) copy-start(s32[64]{0:T(128)} %rows.1) | copy-start | bytes 772
  8.6 6.2 %copy-start.6 = (s32[64]{0:T(128)S(1)}, s32[64]{0:T(128)}, u32[]{:S(2)}) copy-start(s32[64]{0:T(128)} %cols.1) | copy-start | bytes 772
  8.6 23.8 %copy-start.3 = (s32[2]{0:T(128)S(1)}, s32[2]{0:T(128)}, u32[]{:S(2)}) copy-start(s32[2]{0:T(128)} %refs_3_.5) | copy-start | bytes 28
  11.8 14.8 %collective-permute-start.1 = (bf16[80,1024]{1,0:T(8,128)(2,1)S(1)}, bf16[80,1024]{1,0:T(8,128)(2,1)S(1)}, u32[]{:S(2)}, u32[]{:S(2)}) collective-permute-start(bf16[80,1024]{1,0:T(8,128)(2,1)S(1)} %augment.1.refs_9_), channel_id=1, source_target_pairs={{0,1},{1,0},{2,3},{3,2},{4,5},{5,4},{6,7},{7,6},{8,9},{9,8},{10,11... | collective-permute-start | bytes 491528 | tf_op jit(solution)/shard_map/ppermute | solution.py:30
  12.1 14.5 %collective-permute-start.5 = (bf16[80,1024]{1,0:T(8,128)(2,1)S(1)}, bf16[80,1024]{1,0:T(8,128)(2,1)S(1)}, u32[]{:S(2)}, u32[]{:S(2)}) collective-permute-start(bf16[80,1024]{1,0:T(8,128)(2,1)S(1)} %augment.1.refs_9_), channel_id=1, source_target_pairs={{0,2},{1,3},{2,0},{3,1},{4,6},{5,7},{6,4},{7,5},{8,10},{9,11},{10,... | collective-permute-start | bytes 491528 | tf_op jit(solution)/shard_map/ppermute | solution.py:30
  12.9 16.5 %collective-permute-start.4 = (bf16[80,1024]{1,0:T(8,128)(2,1)S(1)}, bf16[80,1024]{1,0:T(8,128)(2,1)S(1)}, u32[]{:S(2)}, u32[]{:S(2)}) collective-permute-start(bf16[80,1024]{1,0:T(8,128)(2,1)S(1)} %augment.1.refs_9_), channel_id=1, source_target_pairs={{4,0},{8,4},{12,8},{16,12},{20,16},{24,20},{28,24},{5,1},{9,5},{13... | collective-permute-start | bytes 491528 | tf_op jit(solution)/shard_map/ppermute | solution.py:36
  29.4 3.1 %collective-permute-start.6 = (bf16[512,768]{1,0:T(8,128)(2,1)S(1)}, bf16[512,768]{1,0:T(8,128)(2,1)S(1)}, u32[]{:S(2)}, u32[]{:S(2)}) collective-permute-start(bf16[512,768]{1,0:T(8,128)(2,1)S(1)} %collective-permute-done.3.refs_7_.refs_6_), channel_id=1, source_target_pairs={{0,1},{1,0},{2,3},{3,2},{4,5},{5,4},{6,7},{7,6},{8,9},{9,8},{10,11... | collective-permute-start | bytes 2359304 | tf_op jit(solution)/shard_map/ppermute | solution.py:30
  29.4 20.0 %collective-permute-start.8 = (bf16[512,768]{1,0:T(8,128)(2,1)S(1)}, bf16[512,768]{1,0:T(8,128)(2,1)S(1)}, u32[]{:S(2)}, u32[]{:S(2)}) collective-permute-start(bf16[512,768]{1,0:T(8,128)(2,1)S(1)} %slice.12), channel_id=1, source_target_pairs={{0,2},{1,3},{2,0},{3,1},{4,6},{5,7},{6,4},{7,5},{8,10},{9,11},{10,... | collective-permute-start | bytes 2359304 | tf_op jit(solution)/shard_map/ppermute | solution.py:30
  29.7 22.5 %collective-permute-start.7 = (bf16[512,768]{1,0:T(8,128)(2,1)S(1)}, bf16[512,768]{1,0:T(8,128)(2,1)S(1)}, u32[]{:S(2)}, u32[]{:S(2)}) collective-permute-start(bf16[512,768]{1,0:T(8,128)(2,1)S(1)} %slice.12), channel_id=1, source_target_pairs={{4,0},{8,4},{12,8},{16,12},{20,16},{24,20},{28,24},{5,1},{9,5},{13... | collective-permute-start | bytes 2359304 | tf_op jit(solution)/shard_map/ppermute | solution.py:36
  31.0 1.5 collective-permute-start.9
  52.2 2.3 %collective-permute-start.10 = (bf16[512,768]{1,0:T(8,128)(2,1)S(1)}, bf16[512,768]{1,0:T(8,128)(2,1)S(1)}, u32[]{:S(2)}, u32[]{:S(2)}) collective-permute-start(bf16[512,768]{1,0:T(8,128)(2,1)S(1)} %collective-permute-done.8.refs_9_), channel_id=1, source_target_pairs={{0,1},{1,0},{2,3},{3,2},{4,5},{5,4},{6,7},{7,6},{8,9},{9,8},{10,11... | collective-permute-start | bytes 2359304 | tf_op jit(solution)/shard_map/ppermute | solution.py:30
  64.0 2.8 %collective-permute-start.12 = (f32[4,72,512]{2,1,0:T(8,128)S(1)}, f32[4,72,512]{2,1,0:T(8,128)S(1)}, u32[]{:S(2)}, u32[]{:S(2)}) collective-permute-start(f32[4,72,512]{2,1,0:T(8,128)S(1)} %get-tuple-element.66), channel_id=1, source_target_pairs={{0,1},{1,0},{2,3},{3,2},{4,5},{5,4},{6,7},{7,6},{8,9},{9,8},{10,11... | collective-permute-start | bytes 1769480 | tf_op jit(solution)/shard_map/ppermute | solution.py:30
  65.2 8.0 %collective-permute-start.11 = (f32[2,72,512]{2,1,0:T(8,128)S(1)}, f32[2,72,512]{2,1,0:T(8,128)S(1)}, u32[]{:S(2)}, u32[]{:S(2)}) collective-permute-start(f32[2,72,512]{2,1,0:T(8,128)S(1)} %get-tuple-element.65), channel_id=1, source_target_pairs={{0,4},{4,8},{8,12},{12,16},{16,20},{20,24},{24,28},{1,5},{5,9},{9,... | collective-permute-start | bytes 884744 | tf_op jit(solution)/shard_map/ppermute | solution.py:36
  66.9 9.4 %collective-permute-start.13 = (f32[2,72,512]{2,1,0:T(8,128)S(1)}, f32[2,72,512]{2,1,0:T(8,128)S(1)}, u32[]{:S(2)}, u32[]{:S(2)}) collective-permute-start(f32[2,72,512]{2,1,0:T(8,128)S(1)} %slice_add_fusion), channel_id=1, source_target_pairs={{0,2},{1,3},{2,0},{3,1},{4,6},{5,7},{6,4},{7,5},{8,10},{9,11},{10,... | collective-permute-start | bytes 884744 | tf_op jit(solution)/shard_map/ppermute | solution.py:30
  76.6 7.8 %collective-permute-start.20 = (f32[64,1024]{1,0:T(8,128)S(1)}, f32[64,1024]{1,0:T(8,128)S(1)}, u32[]{:S(2)}, u32[]{:S(2)}) collective-permute-start(f32[64,1024]{1,0:T(8,128)S(1)} %get-tuple-element.70.refs_5_), channel_id=1, source_target_pairs={{0,2},{1,3},{2,0},{3,1},{4,6},{5,7},{6,4},{7,5},{8,10},{9,11},{10,... | collective-permute-start | bytes 786440 | tf_op jit(solution)/shard_map/ppermute | solution.py:30
  77.0 27.4 %collective-permute-start.22 = (f32[64,1024]{1,0:T(8,128)S(1)}, f32[64,1024]{1,0:T(8,128)S(1)}, u32[]{:S(2)}, u32[]{:S(2)}) collective-permute-start(f32[64,1024]{1,0:T(8,128)S(1)} %get-tuple-element.70.refs_5_), channel_id=1, source_target_pairs={{4,0},{8,4},{12,8},{16,12},{20,16},{24,20},{28,24},{5,1},{9,5},{13... | collective-permute-start | bytes 786440 | tf_op jit(solution)/shard_map/ppermute | solution.py:36
  78.3 26.2 %collective-permute-start.19 = (f32[64,1024]{1,0:T(8,128)S(1)}, f32[64,1024]{1,0:T(8,128)S(1)}, u32[]{:S(2)}, u32[]{:S(2)}) collective-permute-start(f32[64,1024]{1,0:T(8,128)S(1)} %get-tuple-element.70.refs_5_), channel_id=1, source_target_pairs={{0,1},{1,0},{2,3},{3,2},{4,5},{5,4},{6,7},{7,6},{8,9},{9,8},{10,11... | collective-permute-start | bytes 786440 | tf_op jit(solution)/shard_map/ppermute | solution.py:30
  84.5 20.0 %collective-permute-start.21 = (f32[64,1024]{1,0:T(8,128)S(1)}, f32[64,1024]{1,0:T(8,128)S(1)}, u32[]{:S(2)}, u32[]{:S(2)}) collective-permute-start(f32[64,1024]{1,0:T(8,128)S(1)} %collective-permute-done.20.refs_7_), channel_id=1, source_target_pairs={{0,1},{1,0},{2,3},{3,2},{4,5},{5,4},{6,7},{7,6},{8,9},{9,8},{10,11... | collective-permute-start | bytes 786440 | tf_op jit(solution)/shard_map/ppermute | solution.py:30
  84.5 1.6 %collective-permute-start.14 = (f32[64,64]{1,0:T(8,128)S(1)}, f32[64,64]{1,0:T(8,128)S(1)}, u32[]{:S(2)}, u32[]{:S(2)}) collective-permute-start(f32[64,64]{1,0:T(8,128)S(1)} %get-tuple-element.69), channel_id=1, source_target_pairs={{0,1},{1,0},{2,3},{3,2},{4,5},{5,4},{6,7},{7,6},{8,9},{9,8},{10,11... | collective-permute-start | bytes 49160 | tf_op jit(solution)/shard_map/ppermute | solution.py:30
  86.1 3.9 %collective-permute-start.15 = (f32[64,64]{1,0:T(8,128)S(1)}, f32[64,64]{1,0:T(8,128)S(1)}, u32[]{:S(2)}, u32[]{:S(2)}) collective-permute-start(f32[64,64]{1,0:T(8,128)S(1)} %add.37), channel_id=1, source_target_pairs={{0,2},{1,3},{2,0},{3,1},{4,6},{5,7},{6,4},{7,5},{8,10},{9,11},{10,... | collective-permute-start | bytes 49160 | tf_op jit(solution)/shard_map/ppermute | solution.py:30
  90.0 5.7 %collective-permute-start.16 = (f32[64,64]{1,0:T(8,128)S(1)}, f32[64,64]{1,0:T(8,128)S(1)}, u32[]{:S(2)}, u32[]{:S(2)}) collective-permute-start(f32[64,64]{1,0:T(8,128)S(1)} %add.38), channel_id=1, source_target_pairs={{0,4},{4,0},{8,12},{12,8},{16,20},{20,16},{24,28},{28,24},{1,5},{5... | collective-permute-start | bytes 49160 | tf_op jit(solution)/shard_map/ppermute | solution.py:30
  95.7 3.9 %collective-permute-start.17 = (f32[64,64]{1,0:T(8,128)S(1)}, f32[64,64]{1,0:T(8,128)S(1)}, u32[]{:S(2)}, u32[]{:S(2)}) collective-permute-start(f32[64,64]{1,0:T(8,128)S(1)} %add.39), channel_id=1, source_target_pairs={{0,8},{4,12},{8,0},{12,4},{16,24},{20,28},{24,16},{28,20},{1,9},{5... | collective-permute-start | bytes 49160 | tf_op jit(solution)/shard_map/ppermute | solution.py:30
  99.6 4.8 %collective-permute-start.18 = (f32[64,64]{1,0:T(8,128)S(1)}, f32[64,64]{1,0:T(8,128)S(1)}, u32[]{:S(2)}, u32[]{:S(2)}) collective-permute-start(f32[64,64]{1,0:T(8,128)S(1)} %add.40), channel_id=1, source_target_pairs={{0,16},{4,20},{8,24},{12,28},{16,0},{20,4},{24,8},{28,12},{1,17},{... | collective-permute-start | bytes 49160 | tf_op jit(solution)/shard_map/ppermute | solution.py:30
  114.2 2.0 %collective-permute-start.24 = (f32[4,64,512]{2,1,0:T(8,128)S(1)}, f32[4,64,512]{2,1,0:T(8,128)S(1)}, u32[]{:S(2)}, u32[]{:S(2)}) collective-permute-start(f32[4,64,512]{2,1,0:T(8,128)S(1)} %get-tuple-element.75), channel_id=1, source_target_pairs={{0,1},{1,0},{2,3},{3,2},{4,5},{5,4},{6,7},{7,6},{8,9},{9,8},{10,11... | collective-permute-start | bytes 1572872 | tf_op jit(solution)/shard_map/ppermute | solution.py:30
  114.3 7.8 %collective-permute-start.23 = (f32[2,64,512]{2,1,0:T(8,128)S(1)}, f32[2,64,512]{2,1,0:T(8,128)S(1)}, u32[]{:S(2)}, u32[]{:S(2)}) collective-permute-start(f32[2,64,512]{2,1,0:T(8,128)S(1)} %get-tuple-element.74), channel_id=1, source_target_pairs={{0,4},{4,8},{8,12},{12,16},{16,20},{20,24},{24,28},{1,5},{5,9},{9,... | collective-permute-start | bytes 786440 | tf_op jit(solution)/shard_map/ppermute | solution.py:36
  116.3 8.4 %collective-permute-start.25 = (f32[2,64,512]{2,1,0:T(8,128)S(1)}, f32[2,64,512]{2,1,0:T(8,128)S(1)}, u32[]{:S(2)}, u32[]{:S(2)}) collective-permute-start(f32[2,64,512]{2,1,0:T(8,128)S(1)} %slice_add_fusion.1), channel_id=1, source_target_pairs={{0,2},{1,3},{2,0},{3,1},{4,6},{5,7},{6,4},{7,5},{8,10},{9,11},{10,... | collective-permute-start | bytes 786440 | tf_op jit(solution)/shard_map/ppermute | solution.py:30
  125.1 1.3 collective-permute-start.26
  126.4 3.9 %collective-permute-start.27 = (f32[64,64]{1,0:T(8,128)S(1)}, f32[64,64]{1,0:T(8,128)S(1)}, u32[]{:S(2)}, u32[]{:S(2)}) collective-permute-start(f32[64,64]{1,0:T(8,128)S(1)} %add.43), channel_id=1, source_target_pairs={{0,2},{1,3},{2,0},{3,1},{4,6},{5,7},{6,4},{7,5},{8,10},{9,11},{10,... | collective-permute-start | bytes 49160 | tf_op jit(solution)/shard_map/ppermute | solution.py:30
  130.3 5.6 %collective-permute-start.28 = (f32[64,64]{1,0:T(8,128)S(1)}, f32[64,64]{1,0:T(8,128)S(1)}, u32[]{:S(2)}, u32[]{:S(2)}) collective-permute-start(f32[64,64]{1,0:T(8,128)S(1)} %add.44), channel_id=1, source_target_pairs={{0,4},{4,0},{8,12},{12,8},{16,20},{20,16},{24,28},{28,24},{1,5},{5... | collective-permute-start | bytes 49160 | tf_op jit(solution)/shard_map/ppermute | solution.py:30
  135.9 3.9 %collective-permute-start.29 = (f32[64,64]{1,0:T(8,128)S(1)}, f32[64,64]{1,0:T(8,128)S(1)}, u32[]{:S(2)}, u32[]{:S(2)}) collective-permute-start(f32[64,64]{1,0:T(8,128)S(1)} %add.45), channel_id=1, source_target_pairs={{0,8},{4,12},{8,0},{12,4},{16,24},{20,28},{24,16},{28,20},{1,9},{5... | collective-permute-start | bytes 49160 | tf_op jit(solution)/shard_map/ppermute | solution.py:30
  139.8 4.8 %collective-permute-start.30 = (f32[64,64]{1,0:T(8,128)S(1)}, f32[64,64]{1,0:T(8,128)S(1)}, u32[]{:S(2)}, u32[]{:S(2)}) collective-permute-start(f32[64,64]{1,0:T(8,128)S(1)} %add.46), channel_id=1, source_target_pairs={{0,16},{4,20},{8,24},{12,28},{16,0},{20,4},{24,8},{28,12},{1,17},{... | collective-permute-start | bytes 49160 | tf_op jit(solution)/shard_map/ppermute | solution.py:30

commit v5 on v4

v5 whole, which is shorter than its diff:
```python
import functools

import jax
import jax.numpy as jnp
from jax import lax
from jax.experimental import pallas as pl
from jax.experimental.pallas import tpu as pltpu
from jax.sharding import PartitionSpec as P

PTS = 512
ITERS = 2
LOG2E = 1.4426950408889634
DEAD = 65536.0
EXTRA = 16
VMEM = pltpu.VMEM
SMEM = pltpu.SMEM
HIGHEST = lax.Precision.HIGHEST


def cost(flops, moved):
    return pl.CostEstimate(flops=int(flops), bytes_accessed=int(moved), transcendentals=0)


def spec(space):
    return pl.BlockSpec(memory_space=space)


def swap(value, axis, bit):
    count = lax.axis_size(axis)
    return lax.ppermute(value, axis, [(source, source ^ bit) for source in range(count)])


def from_behind(value, axis, steps):
    count = lax.axis_size(axis)
    initial, last = (max(0, -steps), min(count, count - steps))
    return lax.ppermute(value, axis, [(source, source + steps) for source in range(initial, last)])


def bits_of(count):
    bits = []
    bit = 1
    while bit < count:
        bits.append(bit)
        bit *= 2
    return bits


def gather_near(value, axis):
    held = {0: value}
    for bit in reversed(bits_of(lax.axis_size(axis))):
        for rel in list(held):
            held[rel ^ bit] = swap(held[rel], axis, bit)
    return [held[rel] for rel in range(len(held))]


def gather_far_bits(value):
    held = {0: value}
    for bit in reversed(bits_of(lax.axis_size("grp"))[1:]):
        for rel in list(held):
            held[rel ^ bit] = swap(held[rel], "grp", bit)
    held.pop(0)
    return held


def opening_kernel(start, counts, out):
    columns, total = start.shape
    for block in range(total // PTS):
        lanes = slice(block * PTS, (block + 1) * PTS)
        used = lax.broadcasted_iota(jnp.int32, (columns, PTS), 1) < counts[block]
        out[0:columns, lanes] = jnp.where(used, start[:, lanes], 0.0).astype(jnp.bfloat16)
        which = lax.broadcasted_iota(jnp.int32, (EXTRA, PTS), 0)
        place_in = lax.broadcasted_iota(jnp.int32, (EXTRA, PTS), 1)
        ones = jnp.logical_and(which == 0, place_in < counts[block])
        out[columns : columns + EXTRA, lanes] = jnp.where(ones, 1.0, 0.0).astype(jnp.bfloat16)


def opening(start, counts):
    columns, total = start.shape
    return pl.pallas_call(
        opening_kernel,
        out_shape=jax.ShapeDtypeStruct((columns + EXTRA, total), jnp.bfloat16),
        in_specs=[spec(VMEM), spec(SMEM)],
        out_specs=spec(VMEM),
        cost_estimate=cost(2**20, 2**19),
        compiler_params=pltpu.CompilerParams(vmem_limit_bytes=2 * 2**20),
        name="opening",
    )(start, counts)


def is_early(place, group, blocks_dev):
    near_by = jnp.logical_and(place < min(2, group) * blocks_dev, place < group * blocks_dev)
    return jnp.logical_or(near_by, lax.rem(place, blocks_dev) < blocks_dev // 2)


def listing_kernel(group, cap, early_cap, blocks_dev, rows, cols, live, out_rows, out_cols, out_n):
    slab = blocks_dev * group
    slots = rows.shape[0]
    member = lax.axis_index("grp")

    def local_near(block):
        return (lax.div(block, blocks_dev) ^ member) * blocks_dev + lax.rem(block, blocks_dev)

    def count_far(slot, carry):
        col = cols[slot]
        far = jnp.logical_and(slot < live[0], col >= slab)
        owner = lax.div(col - slab, blocks_dev)
        return tuple(
            old + jnp.where(jnp.logical_and(far, owner == device), 1, 0)
            for device, old in enumerate(carry)
        )

    far_counts = lax.fori_loop(0, slots, count_far, (jnp.int32(0),) * group)
    low = jnp.int32(0)
    room = jnp.int32(0)
    for device in range(group):
        low = low + jnp.where(device < member, cap - far_counts[device], 0)
        room = room + jnp.where(device == member, cap - far_counts[device], 0)

    def place_those(wanted, filled):
        def place(slot, carry):
            near_rank, early_rank, filled = carry
            row, col = rows[slot], cols[slot]
            used = slot < live[0]
            far = col >= slab
            mine_far = jnp.logical_and(far, lax.div(col - slab, blocks_dev) == member)
            mine_near = jnp.logical_and(
                jnp.logical_not(far), jnp.logical_and(near_rank >= low, near_rank < low + room)
            )
            row_place = local_near(row)
            col_place = jnp.where(far, slab + lax.rem(col - slab, blocks_dev), local_near(col))
            early = jnp.logical_and(
                is_early(row_place, group, blocks_dev), is_early(col_place, group, blocks_dev)
            )
            mine = jnp.logical_and(used, jnp.logical_or(mine_far, mine_near))
            early = jnp.logical_and(early, mine)
            room_left = early_rank < early_cap
            early_rank = early_rank + jnp.where(early, 1, 0)
            early = jnp.logical_and(early, room_left)
            mine = jnp.logical_and(mine, early if wanted else jnp.logical_not(early))

            @pl.when(mine)
            def _():
                out_rows[filled] = row_place
                out_cols[filled] = col_place

            near_rank = near_rank + jnp.where(jnp.logical_and(used, jnp.logical_not(far)), 1, 0)
            return (near_rank, early_rank, filled + jnp.where(mine, 1, 0))

        return lax.fori_loop(0, slots, place, (jnp.int32(0), jnp.int32(0), filled))[2]

    early_count = place_those(True, jnp.int32(0))
    out_n[0] = jnp.int32(0)
    out_n[1] = early_count
    out_n[2] = place_those(False, early_count)


def listing(rows, cols, live, group, cap, early_cap, blocks_dev):
    return pl.pallas_call(
        functools.partial(listing_kernel, group, cap, early_cap, blocks_dev),
        out_shape=(
            jax.ShapeDtypeStruct((cap,), jnp.int32),
            jax.ShapeDtypeStruct((cap,), jnp.int32),
            jax.ShapeDtypeStruct((3,), jnp.int32),
        ),
        in_specs=[spec(SMEM)] * 3,
        out_specs=(spec(SMEM),) * 3,
        cost_estimate=cost(2**20, 2**10),
        compiler_params=pltpu.CompilerParams(vmem_limit_bytes=2**20),
        name="listing",
    )(rows, cols, live)


def message_rels(group):
    groups = [[0]]
    for bit in bits_of(group):
        groups.append([rel for rel in range(group) if rel & bit and rel % bit == 0])
    return groups


def product_shapes(group, blocks_dev, height):
    shapes = [
        jax.ShapeDtypeStruct((len(rels) * blocks_dev, height, PTS), jnp.float32)
        for rels in message_rels(group)
    ]
    shapes.append(jax.ShapeDtypeStruct((blocks_dev, height, PTS), jnp.float32))
    return shapes


def write_products(group, blocks_dev, acc, outs):
    for rels, out in zip(message_rels(group), outs[:-1]):
        for index, rel in enumerate(rels):
            for block in range(blocks_dev):
                out[index * blocks_dev + block] = acc[rel * blocks_dev + block]
    for block in range(blocks_dev):
        outs[-1][block] = acc[group * blocks_dev + block]


def set_levels(place, window, level_row, level_col, scale):
    block = window[place * PTS : (place + 1) * PTS, :]
    width = block.shape[1]
    part = jnp.zeros((PTS, 128), jnp.float32)
    for lane in range(0, width, 128):
        wide = block[:, lane : lane + 128].astype(jnp.float32)
        part = part + wide * wide
    level_row[place] = scale * lax.dot_general(
        jnp.ones((8, 128), jnp.float32),
        part,
        (((1,), (1,)), ((), ())),
        precision=HIGHEST,
        preferred_element_type=jnp.float32,
    )
    if place < level_col.shape[0]:
        total = jnp.sum(part, axis=1, keepdims=True) * scale
        level_col[place] = jnp.broadcast_to(total, (PTS, 128))


def make_tiles(low, high, rows, cols, window, level_row, level_col, kept):
    width = window.shape[1]
    step = 256
    scale = 6.0 / width * LOG2E

    def body(index, carry):
        row, col = rows[index], cols[index]
        right = window[pl.ds(pl.multiple_of(col * PTS, PTS), PTS), :]
        right_level = level_row[col][0:1, :]
        for part in range(PTS // step):
            left = window[pl.ds(pl.multiple_of(row * PTS + part * step, step), step), :]
            cross = lax.dot_general(
                left, right, (((1,), (1,)), ((), ())), preferred_element_type=jnp.float32
            )
            left_level = level_col[row, part * step : (part + 1) * step, :]
            left_level = jnp.concatenate([left_level] * (PTS // 128), axis=1)
            value = jnp.exp2(cross * scale - left_level - right_level)
            kept[index - low, part * step : (part + 1) * step, :] = value.astype(jnp.bfloat16)
        return carry

    lax.fori_loop(low, high, body, 0)


def build_tiles(stage, fresh, places, n, rows, cols, pts, levels, group, blocks_dev, cap, name):
    width = pts[0].shape[1]
    total = (group + 1) * blocks_dev
    near = group * blocks_dev
    level_shapes = [
        jax.ShapeDtypeStruct((total, 8, PTS), jnp.float32),
        jax.ShapeDtypeStruct((near, PTS, 128), jnp.float32),
    ]
    shapes = [jax.ShapeDtypeStruct((cap, PTS, PTS), jnp.bfloat16)] + level_shapes

    def kernel(*refs):
        n_ref, row_ref, col_ref = refs[:3]
        pt_refs = refs[3 : 3 + len(pts)]
        level_refs = refs[3 + len(pts) : 3 + len(pts) + len(levels)]
        kept, level_row, level_col, window = refs[3 + len(pts) + len(levels) :]
        for place, piece in zip(places, pt_refs):
            window[place * PTS : place * PTS + piece.shape[0], :] = piece[...]
        for index, (place, piece) in enumerate(zip(places, pt_refs)):
            for block in range(place, place + piece.shape[0] // PTS):
                if index < fresh:
                    set_levels(block, window, level_row, level_col, 3.0 / width * LOG2E)
                else:
                    level_row[block] = level_refs[0][block]
                    if block < near:
                        level_col[block] = level_refs[1][block]
        make_tiles(
            n_ref[stage], n_ref[stage + 1], row_ref, col_ref, window, level_row, level_col, kept
        )

    return pl.pallas_call(
        kernel,
        out_shape=tuple(shapes),
        in_specs=[spec(SMEM)] * 3 + [spec(VMEM)] * (len(pts) + len(levels)),
        out_specs=(spec(VMEM),) * len(shapes),
        scratch_shapes=[VMEM((total * PTS, width), jnp.bfloat16)],
        cost_estimate=cost(2**20 if stage == 0 else 2**32, 2**20),
        compiler_params=pltpu.CompilerParams(vmem_limit_bytes=14 * 2**20),
        name=name,
    )(n, rows, cols, *pts, *levels)


def products(n, rows, cols, vecs, tiles, group, blocks_dev, height, folds):
    pieces = group + 1
    places = pieces * blocks_dev
    tall = vecs[0].shape[0]
    shapes = product_shapes(group, blocks_dev, height)

    def fold(value):
        out = value[:height]
        for index in range(1, folds):
            out = out + value[index * height : (index + 1) * height]
        return out

    def kernel(*refs):
        n_ref, row_ref, col_ref = refs[:3]
        vec_refs = refs[3 : 3 + pieces]
        tile_refs = refs[3 + pieces : 3 + pieces + len(tiles)]
        outs = refs[3 + pieces + len(tiles) : -2]
        u_win, acc = refs[-2:]
        for piece in range(pieces):
            for block in range(blocks_dev):
                lanes = slice(block * PTS, (block + 1) * PTS)
                u_win[piece * blocks_dev + block] = vec_refs[piece][:, lanes]
                acc[piece * blocks_dev + block] = jnp.zeros((height, PTS), jnp.float32)
        for stage, kept in enumerate(tile_refs):
            low = n_ref[stage]

            def body(index, carry):
                row, col = row_ref[index], col_ref[index]
                tile = kept[index - low]
                to_row = lax.dot_general(
                    u_win[col], tile, (((1,), (1,)), ((), ())), preferred_element_type=jnp.float32
                )
                acc[row] += fold(to_row)
                to_col = jnp.dot(u_win[row], tile, preferred_element_type=jnp.float32)
                acc[col] += fold(to_col)
                return carry

            lax.fori_loop(low, n_ref[stage + 1], body, 0)
        write_products(group, blocks_dev, acc, outs)

    return pl.pallas_call(
        kernel,
        out_shape=tuple(shapes),
        in_specs=[spec(SMEM)] * 3 + [spec(VMEM)] * (pieces + len(tiles)),
        out_specs=(spec(VMEM),) * len(shapes),
        scratch_shapes=[
            VMEM((places, tall, PTS), jnp.bfloat16),
            VMEM((places, height, PTS), jnp.float32),
        ],
        cost_estimate=cost(2**32, 2**24),
        compiler_params=pltpu.CompilerParams(vmem_limit_bytes=10 * 2**20),
        name="products",
    )(n, rows, cols, *vecs, *tiles)


def scaled_gram(parts, own, counts, degree, inverse, split):
    columns = own.shape[0] if degree is not None else own.shape[0] - EXTRA
    total = own.shape[1]
    first = degree is None
    shapes = [
        jax.ShapeDtypeStruct((columns, total), jnp.float32),
        jax.ShapeDtypeStruct((columns, columns), jnp.float32),
    ]
    if split:
        shapes.append(jax.ShapeDtypeStruct((2 * columns, total), jnp.bfloat16))
    if first:
        shapes.append(jax.ShapeDtypeStruct((8, total), jnp.float32))
    operands = list(parts) + [own]
    operands += [] if first else [degree]
    operands += [] if inverse is None else [inverse]

    def kernel(count_ref, *refs):
        ins = list(refs[: len(operands)])
        outs = list(refs[len(operands) :])
        part_refs = ins[: len(parts)]
        own_ref = ins[len(parts)]
        z_out, gram_out = outs[:2]
        gram = jnp.zeros((columns, columns), jnp.float32)
        for block in range(total // PTS):
            lanes = slice(block * PTS, (block + 1) * PTS)
            sums = part_refs[0][block]
            for part in part_refs[1:]:
                sums = sums + part[block]
            if first:
                level = 1.0 + sums[columns : columns + 1, :]
                outs[-1][:, lanes] = jnp.broadcast_to(level, (8, PTS))
            else:
                level = ins[len(parts) + 1][0:1, lanes]
            used = lax.broadcasted_iota(jnp.int32, (columns, PTS), 1) < count_ref[block]
            held = own_ref[0:columns, lanes].astype(jnp.float32)
            z = (held + jnp.where(used, sums[0:columns], 0.0)) / level
            if inverse is not None:
                z = jnp.dot(
                    ins[-1][...], z, precision=HIGHEST, preferred_element_type=jnp.float32
                )
            z_out[:, lanes] = z
            if split:
                high = z.astype(jnp.bfloat16)
                outs[2][0:columns, lanes] = high
                rest = z - high.astype(jnp.float32)
                outs[2][columns : 2 * columns, lanes] = rest.astype(jnp.bfloat16)
            gram = gram + lax.dot_general(
                z, z, (((1,), (1,)), ((), ())), precision=HIGHEST, preferred_element_type=jnp.float32
            )
        gram_out[...] = gram

    return pl.pallas_call(
        kernel,
        out_shape=tuple(shapes),
        in_specs=[spec(SMEM)] + [spec(VMEM)] * len(operands),
        out_specs=(spec(VMEM),) * len(shapes),
        cost_estimate=cost(2**26, 2**21),
        compiler_params=pltpu.CompilerParams(vmem_limit_bytes=6 * 2**20),
        name="scaled_gram",
    )(counts, *operands)


def inverse_factor(gram):
    size = gram.shape[0]
    row_id = lax.broadcasted_iota(jnp.int32, (size, size), 0)
    col_id = lax.broadcasted_iota(jnp.int32, (size, size), 1)
    eye = jnp.where(row_id == col_id, 1.0, 0.0)
    whole = jnp.concatenate([gram, eye], axis=1)
    wide = 2 * size
    count = size // 8
    groups = [whole[8 * g : 8 * g + 8, :] for g in range(count)]
    within = lax.broadcasted_iota(jnp.int32, (8, wide), 0)

    def spread_row(value, row):
        return jnp.broadcast_to(value[row : row + 1, :], (8, wide))

    results = []
    for g in range(count):
        spread = [
            [
                jnp.broadcast_to(groups[other][:, 8 * g + k : 8 * g + k + 1], (8, wide))
                for other in range(g, count)
            ]
            for k in range(8)
        ]
        pivots = jnp.ones((8, wide), jnp.float32)
        for j in range(8):
            column = spread[j]
            pivot = spread_row(column[0], j)
            pivots = jnp.where(within == j, pivot, pivots)
            over = 1.0 / pivot
            below = jnp.where(within > j, column[0], 0.0)
            for k in range(j + 1, 8):
                share = spread_row(column[0], k) * over
                spread[k][0] = spread[k][0] - below * share
                for other in range(1, count - g):
                    spread[k][other] = spread[k][other] - column[other] * share
            top = spread_row(groups[g], j) * over
            groups[g] = groups[g] - below * top
            for other in range(1, count - g):
                groups[g + other] = groups[g + other] - column[other] * top
        results.append(groups[g] * lax.rsqrt(pivots))
    return jnp.concatenate(results, axis=0)[:, size:wide]


def factor_kernel(gram, out):
    out[...] = inverse_factor(gram[...])


def factor(gram):
    return pl.pallas_call(
        factor_kernel,
        out_shape=jax.ShapeDtypeStruct(gram.shape, jnp.float32),
        in_specs=[spec(VMEM)],
        out_specs=spec(VMEM),
        cost_estimate=cost(2**31, 2**16),
        compiler_params=pltpu.CompilerParams(vmem_limit_bytes=2 * 2**20),
        name="factor",
    )(gram)


def embed_kernel(gram, z, out):
    out[...] = jnp.dot(
        inverse_factor(gram[...]), z[...], precision=HIGHEST, preferred_element_type=jnp.float32
    )


def embedding(gram, z):
    return pl.pallas_call(
        embed_kernel,
        out_shape=jax.ShapeDtypeStruct(z.shape, jnp.float32),
        in_specs=[spec(VMEM)] * 2,
        out_specs=spec(VMEM),
        cost_estimate=cost(2**30, 2**20),
        compiler_params=pltpu.CompilerParams(vmem_limit_bytes=4 * 2**20),
        name="embedding",
    )(gram, z)


def sum_products(messages, group, blocks_dev):
    rels = message_rels(group)
    parts = {}
    for names, message in zip(rels[1:], messages[1:-1]):
        for index, rel in enumerate(names):
            parts[rel] = [message[index * blocks_dev : (index + 1) * blocks_dev]]
    final = [messages[0], from_behind(messages[-1], "blk", 1)]
    for bit, names, message in zip(bits_of(group), rels[1:], messages[1:-1]):
        if bit > 1:
            message = jnp.concatenate([sum(parts[rel][1:], parts[rel][0]) for rel in names], 0)
        got = swap(message, "grp", bit)
        for index, rel in enumerate(names):
            target = rel ^ bit
            if target == 0:
                final.append(got)
            else:
                parts[target].append(got[index * blocks_dev : (index + 1) * blocks_dev])
    return final


def sum_stages():
    return [(axis, bit) for axis in ("grp", "blk") for bit in bits_of(lax.axis_size(axis))]


def all_sum(value, stages):
    for axis, bit in stages:
        value = value + swap(value, axis, bit)
    return value


def per_device(points, counts, pair_rows, pair_cols, pair_live, start):
    group = lax.axis_size("grp")
    blocks_dev = counts.shape[0]
    columns = start.shape[0]
    slots = pair_rows.shape[0]
    cap = max(-(-slots // group), blocks_dev * blocks_dev * group)
    early_cap = cap // 2
    half = (blocks_dev // 2) * PTS

    rows, cols, n = listing(pair_rows, pair_cols, pair_live, group, cap, early_cap, blocks_dev)
    mate = swap(points, "grp", 1)
    chunks = [points[:half], points[half:]]
    far = [from_behind(chunk, "blk", -1) for chunk in chunks]
    crossed = [gather_far_bits(chunk) for chunk in chunks]
    begin, mate = lax.optimization_barrier((start, mate))
    vec = opening(begin, counts)
    tied = lax.optimization_barrier((vec, n, rows, cols, far[0], *crossed[0].values()))
    vec, n, rows, cols, far[0] = tied[:5]
    crossed[0] = dict(zip(crossed[0], tied[5:]))
    cross_vec = gather_far_bits(vec)
    far_vec = from_behind(vec, "blk", -1)
    mate_vec = swap(vec, "grp", 1)

    def placed(index):
        offset = index * (blocks_dev // 2)
        found = [(group * blocks_dev + offset, far[index])]
        for rel, value in crossed[index].items():
            found.append((rel * blocks_dev + offset, value))
            found.append(((rel ^ 1) * blocks_dev + offset, swap(value, "grp", 1)))
        return found

    def tiles_of(stage, fresh, pieces, levels, size, name):
        places, pts = zip(*pieces)
        return build_tiles(
            stage, fresh, places, n, rows, cols, pts, levels, group, blocks_dev, size, name
        )

    early = [(0, points), (blocks_dev, mate)] + placed(0)
    early_kept, *levels = tiles_of(0, len(early), early, (), early_cap, "early_tiles")
    tied = lax.optimization_barrier((far[1], levels[0], *crossed[1].values()))
    far[1], levels[0] = tied[:2]
    crossed[1] = dict(zip(crossed[1], tied[2:]))
    late = placed(1)
    late_kept, _, _ = tiles_of(1, len(late), late + early, levels, cap, "late_tiles")
    tied = lax.optimization_barrier((late_kept, *cross_vec.values()))
    kept = (early_kept, tied[0])
    cross_vec = dict(zip(cross_vec, tied[1:]))

    vecs = {0: vec, 1: mate_vec}
    for rel, value in cross_vec.items():
        vecs[rel] = value
        vecs[rel ^ 1] = swap(value, "grp", 1)
    vecs = [vecs[rel] for rel in range(group)] + [far_vec]
    messages = products(n, rows, cols, vecs, kept, group, blocks_dev, columns + 8, 1)
    z, gram, parts, degree = scaled_gram(
        sum_products(messages, group, blocks_dev), vec, counts, None, None, True
    )
    for turn in range(1, ITERS):
        stages = sum_stages()
        far_part = from_behind(parts, "blk", -1)
        crossed = gather_far_bits(parts)
        gram = all_sum(gram, stages[:1])
        gram, *tied = lax.optimization_barrier((gram, *crossed.values()))
        vecs = {0: parts, 1: swap(parts, "grp", 1)}
        for rel, value in zip(crossed, tied):
            vecs[rel] = value
            vecs[rel ^ 1] = swap(value, "grp", 1)
        vecs = [vecs[rel] for rel in range(group)] + [far_part]
        gram = all_sum(gram, stages[1:2])
        gram, *vecs = lax.optimization_barrier((gram, *vecs))
        messages = products(n, rows, cols, vecs, kept, group, blocks_dev, columns, 2)
        sums = sum_products(messages, group, blocks_dev)
        inverse = factor(all_sum(gram, stages[2:]))
        z, gram, *parts = scaled_gram(sums, z, counts, degree, inverse, turn + 1 < ITERS)
        parts = parts[0] if parts else None
    return embedding(all_sum(gram, sum_stages()), z)


def solution(mesh):
    in_specs = (
        P(("blk", "grp"), None),
        P(("blk", "grp")),
        P("blk"),
        P("blk"),
        P("blk"),
        P(None, ("blk", "grp")),
    )
    out_specs = P(None, ("blk", "grp"))
    return jax.shard_map(
        per_device, mesh=mesh, in_specs=in_specs, out_specs=out_specs, check_vma=False
    )
```

time: 146 us -> 148 us (1.014)
  Pallas kernels: 40.8 us -> 44.7 us
  waiting for transfers between devices: 70.7 us -> 66.8 us
  starting transfers between devices: 30.8 us -> 34.2 us
  local copies, waits for them, and re-layouts: 4.38 us -> 1.52 us
    ppermute x25, waiting for transfers between devices: 49.8 us -> 36.1 us  [swap(): lax.ppermute(value, axis, [(source, source ^ bit) for source in range(cou...]
    ppermute x6, waiting for transfers between devices: 20.9 us -> 30.6 us  [from_behind(): lax.ppermute(value, axis, [(source, source + steps) for source in range(i...]
    ppermute x6, starting transfers between devices: 7.72 us -> 15.5 us  [from_behind(): lax.ppermute(value, axis, [(source, source + steps) for source in range(i...]
    ppermute x25, starting transfers between devices: 23.1 us -> 18.7 us  [swap(): lax.ppermute(value, axis, [(source, source ^ bit) for source in range(cou...]
    pallas_call x6 -> x8, Pallas kernels: 31.2 us -> 35.1 us  [the longest x2 16.2 us: build_tiles(): pl.pallas_call(kernel, out_shape=tuple(shapes), in_specs=[spec(SMEM)] * 3...]
    unnamed x14 -> x10, local copies, waits for them, and re-layouts: 3.02 us -> 0.02 us
  transfers between devices with their start and end apart: 31 -> 31, of which waited for: 24 -> 16; matrix products, arithmetic and copies ran while one was open for 1% -> 1% of each run, Pallas kernels for 12% -> 17%
where the time goes in v5:
time: 148 us
  waiting for transfers between devices  66.8 us (45%)
  Pallas kernels  44.7 us (30%)
  starting transfers between devices  34.2 us (23%)
  local copies, waits for them, and re-layouts  1.52 us (1%)
    ppermute x25, waiting for transfers between devices, swap(): lax.ppermute(value, axis, [(source, source ^ bit) for source in range(cou...  36.1 us
    ppermute x6, waiting for transfers between devices, from_behind(): lax.ppermute(value, axis, [(source, source + steps) for source in range(i...  30.6 us
    ppermute x25, starting transfers between devices, swap(): lax.ppermute(value, axis, [(source, source ^ bit) for source in range(cou...  18.7 us
    pallas_call x2, Pallas kernels, build_tiles(): pl.pallas_call(kernel, out_shape=tuple(shapes), in_specs=[spec(SMEM)] * 3...  16.2 us
    ppermute x6, starting transfers between devices, from_behind(): lax.ppermute(value, axis, [(source, source + steps) for source in range(i...  15.5 us
    pallas_call x2, Pallas kernels, products(): pl.pallas_call(kernel, out_shape=tuple(shapes), in_specs=[spec(SMEM)] * 3...  13.9 us
    pallas_call x1, Pallas kernels, listing(): pl.pallas_call(functools.partial(listing_kernel, group, cap, early_cap, b...  6.52 us
    pallas_call x1, Pallas kernels, embedding(): pl.pallas_call(embed_kernel, out_shape=jax.ShapeDtypeStruct(z.shape, jnp....  3.01 us
  transfers between devices with their start and end apart: 31, of which 16 were waited for; matrix products, arithmetic and copies ran while one was open for 1% of the time, Pallas kernels for 17%

profile of v5, /device:TPU:0, one launch (start us, length us, event | category | flops | bytes accessed | tf_op | source)
XLA Modules:
  0.0 148.2 jit_solution(8460765546442410586)
XLA Ops:
  0.0 0.5 collective-permute-start
  0.5 1.5 %fusion = (bf16[512,768]{1,0:T(8,128)(2,1)S(1)}, bf16[512,768]{1,0:T(8,128)(2,1)S(1)}) fusion(bf16[1024,768]{1,0:T(8,128)(2,1)} %refs_6_.1), kind=kLoop, calls=%fused_computation.2 | loop fusion | bytes 3145728 | tf_op jit(solution)/shard_map/slice | solution.py:516
  2.1 1.3 collective-permute-start.1
  3.4 2.7 %collective-permute-start.2 = (bf16[512,768]{1,0:T(8,128)(2,1)S(1)}, bf16[512,768]{1,0:T(8,128)(2,1)S(1)}, u32[]{:S(2)}, u32[]{:S(2)}) collective-permute-start(bf16[512,768]{1,0:T(8,128)(2,1)S(1)} %get-tuple-element.90), channel_id=1, source_target_pairs={{0,2},{1,3},{2,0},{3,1},{4,6},{5,7},{6,4},{7,5},{8,10},{9,11},{10,... | collective-permute-start | bytes 2359304 | tf_op jit(solution)/shard_map/ppermute | solution.py:30
  6.7 6.5 %listing.1 = (s32[16]{0:T(128)S(1)}, s32[16]{0:T(128)S(1)}, s32[3]{0:T(128)S(1)}) custom-call(s32[64]{0:T(128)S(1)} %copy-done.3, s32[64]{0:T(128)S(1)} %copy-done.4, s32[1]{0:T(128)S(6)} %copy.7.live), custom_call_target="tpu_custom_call" | custom-call | flops 1048576 | bytes 1024 | tf_op jit(solution)/shard_map/listing/pallas_call | solution.py:158
  13.2 0.0 collective-permute-done.refs_4_.refs_7_
  13.3 0.6 opening.1.refs_3_.refs_4_
  13.8 10.8 %collective-permute-done.1.refs_5_.refs_8_ = bf16[512,768]{1,0:T(8,128)(2,1)S(1)} collective-permute-done((bf16[512,768]{1,0:T(8,128)(2,1)S(1)}, bf16[512,768]{1,0:T(8,128)(2,1)S(1)}, u32[]{:S(2)}, u32[]{:S(2)}) %collective-permute-start.1) | collective-permute-done | bytes 786464 | tf_op jit(solution)/shard_map/ppermute | solution.py:36
  24.7 0.0 collective-permute-done.2.refs_6_.refs_9_
  24.7 0.0 collective-permute-start.5
  24.7 1.3 collective-permute-start.4
  25.9 1.8 %collective-permute-start.6 = (bf16[512,768]{1,0:T(8,128)(2,1)S(1)}, bf16[512,768]{1,0:T(8,128)(2,1)S(1)}, u32[]{:S(2)}, u32[]{:S(2)}) collective-permute-start(bf16[512,768]{1,0:T(8,128)(2,1)S(1)} %get-tuple-element.89), channel_id=1, source_target_pairs={{0,2},{1,3},{2,0},{3,1},{4,6},{5,7},{6,4},{7,5},{8,10},{9,11},{10,... | collective-permute-start | bytes 2359304 | tf_op jit(solution)/shard_map/ppermute | solution.py:30
  27.7 6.6 %early_tiles.1 = (bf16[8,512,512]{2,1,0:T(8,128)(2,1)S(1)}, f32[10,8,512]{2,1,0:T(8,128)S(1)}, f32[8,512,128]{2,1,0:T(8,128)S(1)}) custom-call(s32[3]{0:T(128)S(1)} %get-tuple-element.51.refs_0_, s32[16]{0:T(128)S(1)} %get-tuple-element.52.refs_1_, s32[16]{0:T(128)S(1)} %get-tuple-element.53.refs_2_, bf16[1024,768]{1,0:T(8,128)(2,1)S(1)} %copy-done, ...), custom_call_target="tpu_custom_call" | custom-call | flops 1048576 | bytes 1048576 | tf_op jit(solution)/shard_map/early_tiles/pallas_call | solution.py:269
  34.3 13.1 %collective-permute-done.4.refs_3_ = bf16[512,768]{1,0:T(8,128)(2,1)S(1)} collective-permute-done((bf16[512,768]{1,0:T(8,128)(2,1)S(1)}, bf16[512,768]{1,0:T(8,128)(2,1)S(1)}, u32[]{:S(2)}, u32[]{:S(2)}) %collective-permute-start.4) | collective-permute-done | bytes 786464 | tf_op jit(solution)/shard_map/ppermute | solution.py:36
  47.4 1.5 %collective-permute-start.8 = (bf16[80,1024]{1,0:T(8,128)(2,1)S(1)}, bf16[80,1024]{1,0:T(8,128)(2,1)S(1)}, u32[]{:S(2)}, u32[]{:S(2)}) collective-permute-start(bf16[80,1024]{1,0:T(8,128)(2,1)S(1)} %opening.1.refs_3_.refs_4_), channel_id=1, source_target_pairs={{0,2},{1,3},{2,0},{3,1},{4,6},{5,7},{6,4},{7,5},{8,10},{9,11},{10,... | collective-permute-start | bytes 491528 | tf_op jit(solution)/shard_map/ppermute | solution.py:30
  48.9 1.3 collective-permute-start.10
  50.2 0.3 collective-permute-start.3
  50.5 9.6 %late_tiles.1 = (bf16[16,512,512]{2,1,0:T(8,128)(2,1)S(1)}, f32[10,8,512]{2,1,0:T(8,128)}, f32[8,512,128]{2,1,0:T(8,128)}) custom-call(s32[3]{0:T(128)S(1)} %get-tuple-element.51.refs_0_, s32[16]{0:T(128)S(1)} %get-tuple-element.52.refs_1_, s32[16]{0:T(128)S(1)} %get-tuple-element.53.refs_2_, bf16[512,768]{1,0:T(8,128)(2,1)S(1)} %collective-permute-done.4.refs_3_, ...), custom_call_target="tpu_custom_call" | custom-call | flops 4294967296 | bytes 1048576 | tf_op jit(solution)/shard_map/late_tiles/pallas_call | solution.py:269
  60.1 0.0 collective-permute-done.8.refs_5_
  60.1 0.3 collective-permute-start.9
  60.4 0.0 collective-permute-done.10.refs_7_
  60.4 0.0 collective-permute-done.3.refs_4_
  60.4 1.1 collective-permute-done.9.refs_6_
  61.5 6.9 %products.2 = (f32[2,72,512]{2,1,0:T(8,128)S(1)}, f32[4,72,512]{2,1,0:T(8,128)S(1)}, f32[2,72,512]{2,1,0:T(8,128)S(1)}, f32[2,72,512]{2,1,0:T(8,128)S(1)}) custom-call(s32[3]{0:T(128)S(1)} %get-tuple-element.51.refs_0_, s32[16]{0:T(128)S(1)} %get-tuple-element.52.refs_1_, s32[16]{0:T(128)S(1)} %get-tuple-element.53.refs_2_, ...), custom_call_target="tpu_custom_call" | custom-call | flops 4294967296 | bytes 16777216 | tf_op jit(solution)/shard_map/products/pallas_call | solution.py:321
  68.4 0.3 collective-permute-start.12
  68.7 5.7 %collective-permute-start.11 = (f32[2,72,512]{2,1,0:T(8,128)S(1)}, f32[2,72,512]{2,1,0:T(8,128)S(1)}, u32[]{:S(2)}, u32[]{:S(2)}) collective-permute-start(f32[2,72,512]{2,1,0:T(8,128)S(1)} %get-tuple-element.68), channel_id=1, source_target_pairs={{0,4},{4,8},{8,12},{12,16},{16,20},{20,24},{24,28},{1,5},{5,9},{9,... | collective-permute-start | bytes 884744 | tf_op jit(solution)/shard_map/ppermute | solution.py:36
  74.5 0.1 collective-permute-start.13
  74.5 6.6 %collective-permute-done.11.refs_1_ = f32[2,72,512]{2,1,0:T(8,128)S(1)} collective-permute-done((f32[2,72,512]{2,1,0:T(8,128)S(1)}, f32[2,72,512]{2,1,0:T(8,128)S(1)}, u32[]{:S(2)}, u32[]{:S(2)}) %collective-permute-start.11) | collective-permute-done | bytes 294944 | tf_op jit(solution)/shard_map/ppermute | solution.py:36
  81.2 2.4 %collective-permute-done.13.refs_3_ = f32[2,72,512]{2,1,0:T(8,128)S(1)} collective-permute-done((f32[2,72,512]{2,1,0:T(8,128)S(1)}, f32[2,72,512]{2,1,0:T(8,128)S(1)}, u32[]{:S(2)}, u32[]{:S(2)}) %collective-permute-start.13) | collective-permute-done | bytes 294944 | tf_op jit(solution)/shard_map/ppermute | solution.py:30
  83.5 1.0 scaled_gram.2
  84.5 0.4 collective-permute-start.15
  84.8 0.0 collective-permute-start.14
  84.8 0.5 collective-permute-start.17
  85.3 1.3 collective-permute-start.19
  86.6 0.0 collective-permute-done.14
  86.7 5.3 %collective-permute-done.15.refs_5_ = bf16[128,1024]{1,0:T(8,128)(2,1)S(1)} collective-permute-done((bf16[128,1024]{1,0:T(8,128)(2,1)S(1)}, bf16[128,1024]{1,0:T(8,128)(2,1)S(1)}, u32[]{:S(2)}, u32[]{:S(2)}) %collective-permute-start.15) | collective-permute-done | bytes 262176 | tf_op jit(solution)/shard_map/ppermute | solution.py:30
  92.0 0.0 collective-permute-start.18
  92.0 0.6 collective-permute-start.16
  92.6 3.3 %collective-permute-done.16 = f32[64,64]{1,0:T(8,128)S(1)} collective-permute-done((f32[64,64]{1,0:T(8,128)S(1)}, f32[64,64]{1,0:T(8,128)S(1)}, u32[]{:S(2)}, u32[]{:S(2)}) %collective-permute-start.16) | collective-permute-done | bytes 16416 | tf_op jit(solution)/shard_map/ppermute | solution.py:30
  95.9 0.0 collective-permute-done.17.refs_4_
  95.9 0.1 collective-permute-done.19.refs_7_
  96.0 7.1 %products.3 = (f32[2,64,512]{2,1,0:T(8,128)S(1)}, f32[4,64,512]{2,1,0:T(8,128)S(1)}, f32[2,64,512]{2,1,0:T(8,128)S(1)}, f32[2,64,512]{2,1,0:T(8,128)S(1)}) custom-call(s32[3]{0:T(128)S(1)} %get-tuple-element.51.refs_0_, s32[16]{0:T(128)S(1)} %get-tuple-element.52.refs_1_, s32[16]{0:T(128)S(1)} %get-tuple-element.53.refs_2_, ...), custom_call_target="tpu_custom_call" | custom-call | flops 4294967296 | bytes 16777216 | tf_op jit(solution)/shard_map/products/pallas_call | solution.py:321
  103.1 0.1 collective-permute-start.21
  103.2 4.7 %collective-permute-start.20 = (f32[2,64,512]{2,1,0:T(8,128)S(1)}, f32[2,64,512]{2,1,0:T(8,128)S(1)}, u32[]{:S(2)}, u32[]{:S(2)}) collective-permute-start(f32[2,64,512]{2,1,0:T(8,128)S(1)} %get-tuple-element.81), channel_id=1, source_target_pairs={{0,4},{4,8},{8,12},{12,16},{16,20},{20,24},{24,28},{1,5},{5,9},{9,... | collective-permute-start | bytes 786440 | tf_op jit(solution)/shard_map/ppermute | solution.py:36
  108.0 1.1 collective-permute-start.22
  109.1 0.2 collective-permute-start.23
  109.3 5.3 %collective-permute-done.23 = f32[64,64]{1,0:T(8,128)S(1)} collective-permute-done((f32[64,64]{1,0:T(8,128)S(1)}, f32[64,64]{1,0:T(8,128)S(1)}, u32[]{:S(2)}, u32[]{:S(2)}) %collective-permute-start.23) | collective-permute-done | bytes 16416 | tf_op jit(solution)/shard_map/ppermute | solution.py:30
  114.6 2.2 %collective-permute-start.24 = (f32[64,64]{1,0:T(8,128)S(1)}, f32[64,64]{1,0:T(8,128)S(1)}, u32[]{:S(2)}, u32[]{:S(2)}) collective-permute-start(f32[64,64]{1,0:T(8,128)S(1)} %add.40), channel_id=1, source_target_pairs={{0,8},{4,12},{8,0},{12,4},{16,24},{20,28},{24,16},{28,20},{1,9},{5... | collective-permute-start | bytes 49160 | tf_op jit(solution)/shard_map/ppermute | solution.py:30
  116.9 1.9 %collective-permute-done.24 = f32[64,64]{1,0:T(8,128)S(1)} collective-permute-done((f32[64,64]{1,0:T(8,128)S(1)}, f32[64,64]{1,0:T(8,128)S(1)}, u32[]{:S(2)}, u32[]{:S(2)}) %collective-permute-start.24) | collective-permute-done | bytes 16416 | tf_op jit(solution)/shard_map/ppermute | solution.py:30
  118.7 0.6 collective-permute-start.25
  119.4 4.2 %collective-permute-done.25 = f32[64,64]{1,0:T(8,128)S(1)} collective-permute-done((f32[64,64]{1,0:T(8,128)S(1)}, f32[64,64]{1,0:T(8,128)S(1)}, u32[]{:S(2)}, u32[]{:S(2)}) %collective-permute-start.25) | collective-permute-done | bytes 16416 | tf_op jit(solution)/shard_map/ppermute | solution.py:30
  123.6 2.0 %factor.1.refs_6_ = f32[64,64]{1,0:T(8,128)S(1)} custom-call(f32[64,64]{1,0:T(8,128)S(1)} %add.42.gram), custom_call_target="tpu_custom_call" | custom-call | flops 2147483648 | bytes 65536 | tf_op jit(solution)/shard_map/factor/pallas_call | solution.py:446
  125.5 1.5 %scaled_gram.3 = (f32[64,1024]{1,0:T(8,128)S(1)}, f32[64,64]{1,0:T(8,128)S(1)}) custom-call(s32[2]{0:T(128)S(1)} %copy-done.2, f32[2,64,512]{2,1,0:T(8,128)S(1)} %get-tuple-element.80.refs_0_, f32[2,64,512]{2,1,0:T(8,128)S(1)} %collective-permute-done.20.refs_1_, f32[4,64,512]{2,1,0:T(8,128)S(1)} %collective-permute-done.21.refs_2_, ...), custom_call_target="tpu_custom_call" | custom-call | flops 67108864 | bytes 2097152 | tf_op jit(solution)/shard_map/scaled_gram/pallas_call | solution.py:387
  127.1 0.1 collective-permute-start.26
  127.1 1.2 collective-permute-done.26
  128.3 1.0 collective-permute-start.27
  129.3 2.9 %collective-permute-done.27 = f32[64,64]{1,0:T(8,128)S(1)} collective-permute-done((f32[64,64]{1,0:T(8,128)S(1)}, f32[64,64]{1,0:T(8,128)S(1)}, u32[]{:S(2)}, u32[]{:S(2)}) %collective-permute-start.27) | collective-permute-done | bytes 16416 | tf_op jit(solution)/shard_map/ppermute | solution.py:30
  132.3 2.3 %collective-permute-start.28 = (f32[64,64]{1,0:T(8,128)S(1)}, f32[64,64]{1,0:T(8,128)S(1)}, u32[]{:S(2)}, u32[]{:S(2)}) collective-permute-start(f32[64,64]{1,0:T(8,128)S(1)} %add.44), channel_id=1, source_target_pairs={{0,4},{4,0},{8,12},{12,8},{16,20},{20,16},{24,28},{28,24},{1,5},{5... | collective-permute-start | bytes 49160 | tf_op jit(solution)/shard_map/ppermute | solution.py:30
  134.6 1.9 %collective-permute-done.28 = f32[64,64]{1,0:T(8,128)S(1)} collective-permute-done((f32[64,64]{1,0:T(8,128)S(1)}, f32[64,64]{1,0:T(8,128)S(1)}, u32[]{:S(2)}, u32[]{:S(2)}) %collective-permute-start.28) | collective-permute-done | bytes 16416 | tf_op jit(solution)/shard_map/ppermute | solution.py:30
  136.5 1.8 %collective-permute-start.29 = (f32[64,64]{1,0:T(8,128)S(1)}, f32[64,64]{1,0:T(8,128)S(1)}, u32[]{:S(2)}, u32[]{:S(2)}) collective-permute-start(f32[64,64]{1,0:T(8,128)S(1)} %add.45), channel_id=1, source_target_pairs={{0,8},{4,12},{8,0},{12,4},{16,24},{20,28},{24,16},{28,20},{1,9},{5... | collective-permute-start | bytes 49160 | tf_op jit(solution)/shard_map/ppermute | solution.py:30
  138.2 2.2 %collective-permute-done.29 = f32[64,64]{1,0:T(8,128)S(1)} collective-permute-done((f32[64,64]{1,0:T(8,128)S(1)}, f32[64,64]{1,0:T(8,128)S(1)}, u32[]{:S(2)}, u32[]{:S(2)}) %collective-permute-start.29) | collective-permute-done | bytes 16416 | tf_op jit(solution)/shard_map/ppermute | solution.py:30
  140.4 0.4 collective-permute-start.30
  140.8 4.4 %collective-permute-done.30 = f32[64,64]{1,0:T(8,128)S(1)} collective-permute-done((f32[64,64]{1,0:T(8,128)S(1)}, f32[64,64]{1,0:T(8,128)S(1)}, u32[]{:S(2)}, u32[]{:S(2)}) %collective-permute-start.30) | collective-permute-done | bytes 16416 | tf_op jit(solution)/shard_map/ppermute | solution.py:30
  145.2 3.0 %embedding.1 = f32[64,1024]{1,0:T(8,128)} custom-call(f32[64,64]{1,0:T(8,128)S(1)} %add.47.gram, f32[64,1024]{1,0:T(8,128)S(1)} %get-tuple-element.88.z), custom_call_target="tpu_custom_call" | custom-call | flops 1073741824 | bytes 1048576 | tf_op jit(solution)/shard_map/embedding/pallas_call | solution.py:464
  (31 shorter events, 0.2 us)
Async XLA Ops:
  0.0 27.7 %copy-start = (bf16[1024,768]{1,0:T(8,128)(2,1)S(1)}, bf16[1024,768]{1,0:T(8,128)(2,1)}, u32[]{:S(2)}) copy-start(bf16[1024,768]{1,0:T(8,128)(2,1)} %refs_6_.1) | copy-start | bytes 4718596
  0.0 6.7 %copy-start.3 = (s32[64]{0:T(128)S(1)}, s32[64]{0:T(128)}, u32[]{:S(2)}) copy-start(s32[64]{0:T(128)} %rows.1) | copy-start | bytes 772
  0.0 6.7 %copy-start.4 = (s32[64]{0:T(128)S(1)}, s32[64]{0:T(128)}, u32[]{:S(2)}) copy-start(s32[64]{0:T(128)} %cols.1) | copy-start | bytes 772
  0.0 13.2 %copy-start.1 = (f32[64,1024]{1,0:T(8,128)S(1)}, f32[64,1024]{1,0:T(8,128)}, u32[]{:S(2)}) copy-start(f32[64,1024]{1,0:T(8,128)} %start) | copy-start | bytes 786436
  0.0 13.2 %copy-start.2 = (s32[2]{0:T(128)S(1)}, s32[2]{0:T(128)}, u32[]{:S(2)}) copy-start(s32[2]{0:T(128)} %count_ref.3) | copy-start | bytes 28
  0.0 13.2 %collective-permute-start = (bf16[1024,768]{1,0:T(8,128)(2,1)}, bf16[1024,768]{1,0:T(8,128)(2,1)S(1)}, u32[]{:S(2)}, u32[]{:S(2)}) collective-permute-start(bf16[1024,768]{1,0:T(8,128)(2,1)} %refs_6_.1), channel_id=1, source_target_pairs={{0,1},{1,0},{2,3},{3,2},{4,5},{5,4},{6,7},{7,6},{8,9},{9,8},{10,11... | collective-permute-start | bytes 4718600 | tf_op jit(solution)/shard_map/ppermute | solution.py:30
  2.1 22.6 %collective-permute-start.1 = (bf16[512,768]{1,0:T(8,128)(2,1)S(1)}, bf16[512,768]{1,0:T(8,128)(2,1)S(1)}, u32[]{:S(2)}, u32[]{:S(2)}) collective-permute-start(bf16[512,768]{1,0:T(8,128)(2,1)S(1)} %get-tuple-element.90), channel_id=1, source_target_pairs={{4,0},{8,4},{12,8},{16,12},{20,16},{24,20},{28,24},{5,1},{9,5},{13... | collective-permute-start | bytes 2359304 | tf_op jit(solution)/shard_map/ppermute | solution.py:36
  3.4 21.3 %collective-permute-start.2 = (bf16[512,768]{1,0:T(8,128)(2,1)S(1)}, bf16[512,768]{1,0:T(8,128)(2,1)S(1)}, u32[]{:S(2)}, u32[]{:S(2)}) collective-permute-start(bf16[512,768]{1,0:T(8,128)(2,1)S(1)} %get-tuple-element.90), channel_id=1, source_target_pairs={{0,2},{1,3},{2,0},{3,1},{4,6},{5,7},{6,4},{7,5},{8,10},{9,11},{10,... | collective-permute-start | bytes 2359304 | tf_op jit(solution)/shard_map/ppermute | solution.py:30
  24.7 3.1 %collective-permute-start.5 = (bf16[512,768]{1,0:T(8,128)(2,1)S(1)}, bf16[512,768]{1,0:T(8,128)(2,1)S(1)}, u32[]{:S(2)}, u32[]{:S(2)}) collective-permute-start(bf16[512,768]{1,0:T(8,128)(2,1)S(1)} %collective-permute-done.2.refs_6_.refs_9_), channel_id=1, source_target_pairs={{0,1},{1,0},{2,3},{3,2},{4,5},{5,4},{6,7},{7,6},{8,9},{9,8},{10,11... | collective-permute-start | bytes 2359304 | tf_op jit(solution)/shard_map/ppermute | solution.py:30
  24.7 22.7 %collective-permute-start.4 = (bf16[512,768]{1,0:T(8,128)(2,1)S(1)}, bf16[512,768]{1,0:T(8,128)(2,1)S(1)}, u32[]{:S(2)}, u32[]{:S(2)}) collective-permute-start(bf16[512,768]{1,0:T(8,128)(2,1)S(1)} %get-tuple-element.89), channel_id=1, source_target_pairs={{4,0},{8,4},{12,8},{16,12},{20,16},{24,20},{28,24},{5,1},{9,5},{13... | collective-permute-start | bytes 2359304 | tf_op jit(solution)/shard_map/ppermute | solution.py:36
  25.9 21.4 %collective-permute-start.6 = (bf16[512,768]{1,0:T(8,128)(2,1)S(1)}, bf16[512,768]{1,0:T(8,128)(2,1)S(1)}, u32[]{:S(2)}, u32[]{:S(2)}) collective-permute-start(bf16[512,768]{1,0:T(8,128)(2,1)S(1)} %get-tuple-element.89), channel_id=1, source_target_pairs={{0,2},{1,3},{2,0},{3,1},{4,6},{5,7},{6,4},{7,5},{8,10},{9,11},{10,... | collective-permute-start | bytes 2359304 | tf_op jit(solution)/shard_map/ppermute | solution.py:30
  47.4 3.1 %collective-permute-start.7 = (bf16[512,768]{1,0:T(8,128)(2,1)S(1)}, bf16[512,768]{1,0:T(8,128)(2,1)S(1)}, u32[]{:S(2)}, u32[]{:S(2)}) collective-permute-start(bf16[512,768]{1,0:T(8,128)(2,1)S(1)} %collective-permute-done.6.refs_4_), channel_id=1, source_target_pairs={{0,1},{1,0},{2,3},{3,2},{4,5},{5,4},{6,7},{7,6},{8,9},{9,8},{10,11... | collective-permute-start | bytes 2359304 | tf_op jit(solution)/shard_map/ppermute | solution.py:30
  47.4 12.7 %collective-permute-start.8 = (bf16[80,1024]{1,0:T(8,128)(2,1)S(1)}, bf16[80,1024]{1,0:T(8,128)(2,1)S(1)}, u32[]{:S(2)}, u32[]{:S(2)}) collective-permute-start(bf16[80,1024]{1,0:T(8,128)(2,1)S(1)} %opening.1.refs_3_.refs_4_), channel_id=1, source_target_pairs={{0,2},{1,3},{2,0},{3,1},{4,6},{5,7},{6,4},{7,5},{8,10},{9,11},{10,... | collective-permute-start | bytes 491528 | tf_op jit(solution)/shard_map/ppermute | solution.py:30
  48.9 11.5 %collective-permute-start.10 = (bf16[80,1024]{1,0:T(8,128)(2,1)S(1)}, bf16[80,1024]{1,0:T(8,128)(2,1)S(1)}, u32[]{:S(2)}, u32[]{:S(2)}) collective-permute-start(bf16[80,1024]{1,0:T(8,128)(2,1)S(1)} %opening.1.refs_3_.refs_4_), channel_id=1, source_target_pairs={{4,0},{8,4},{12,8},{16,12},{20,16},{24,20},{28,24},{5,1},{9,5},{13... | collective-permute-start | bytes 491528 | tf_op jit(solution)/shard_map/ppermute | solution.py:36
  50.2 10.2 %collective-permute-start.3 = (bf16[80,1024]{1,0:T(8,128)(2,1)S(1)}, bf16[80,1024]{1,0:T(8,128)(2,1)S(1)}, u32[]{:S(2)}, u32[]{:S(2)}) collective-permute-start(bf16[80,1024]{1,0:T(8,128)(2,1)S(1)} %opening.1.refs_3_.refs_4_), channel_id=1, source_target_pairs={{0,1},{1,0},{2,3},{3,2},{4,5},{5,4},{6,7},{7,6},{8,9},{9,8},{10,11... | collective-permute-start | bytes 491528 | tf_op jit(solution)/shard_map/ppermute | solution.py:30
  60.1 1.4 collective-permute-start.9
  68.4 6.0 %collective-permute-start.12 = (f32[4,72,512]{2,1,0:T(8,128)S(1)}, f32[4,72,512]{2,1,0:T(8,128)S(1)}, u32[]{:S(2)}, u32[]{:S(2)}) collective-permute-start(f32[4,72,512]{2,1,0:T(8,128)S(1)} %get-tuple-element.69), channel_id=1, source_target_pairs={{0,1},{1,0},{2,3},{3,2},{4,5},{5,4},{6,7},{7,6},{8,9},{9,8},{10,11... | collective-permute-start | bytes 1769480 | tf_op jit(solution)/shard_map/ppermute | solution.py:30
  68.7 12.4 %collective-permute-start.11 = (f32[2,72,512]{2,1,0:T(8,128)S(1)}, f32[2,72,512]{2,1,0:T(8,128)S(1)}, u32[]{:S(2)}, u32[]{:S(2)}) collective-permute-start(f32[2,72,512]{2,1,0:T(8,128)S(1)} %get-tuple-element.68), channel_id=1, source_target_pairs={{0,4},{4,8},{8,12},{12,16},{16,20},{20,24},{24,28},{1,5},{5,9},{9,... | collective-permute-start | bytes 884744 | tf_op jit(solution)/shard_map/ppermute | solution.py:36
  74.5 9.0 %collective-permute-start.13 = (f32[2,72,512]{2,1,0:T(8,128)S(1)}, f32[2,72,512]{2,1,0:T(8,128)S(1)}, u32[]{:S(2)}, u32[]{:S(2)}) collective-permute-start(f32[2,72,512]{2,1,0:T(8,128)S(1)} %slice_add_fusion), channel_id=1, source_target_pairs={{0,2},{1,3},{2,0},{3,1},{4,6},{5,7},{6,4},{7,5},{8,10},{9,11},{10,... | collective-permute-start | bytes 884744 | tf_op jit(solution)/shard_map/ppermute | solution.py:30
  84.5 7.5 %collective-permute-start.15 = (bf16[128,1024]{1,0:T(8,128)(2,1)S(1)}, bf16[128,1024]{1,0:T(8,128)(2,1)S(1)}, u32[]{:S(2)}, u32[]{:S(2)}) collective-permute-start(bf16[128,1024]{1,0:T(8,128)(2,1)S(1)} %get-tuple-element.75.refs_3_), channel_id=1, source_target_pairs={{0,2},{1,3},{2,0},{3,1},{4,6},{5,7},{6,4},{7,5},{8,10},{9,11},{10,... | collective-permute-start | bytes 786440 | tf_op jit(solution)/shard_map/ppermute | solution.py:30
  84.8 1.8 %collective-permute-start.14 = (f32[64,64]{1,0:T(8,128)S(1)}, f32[64,64]{1,0:T(8,128)S(1)}, u32[]{:S(2)}, u32[]{:S(2)}) collective-permute-start(f32[64,64]{1,0:T(8,128)S(1)} %get-tuple-element.71), channel_id=1, source_target_pairs={{0,1},{1,0},{2,3},{3,2},{4,5},{5,4},{6,7},{7,6},{8,9},{9,8},{10,11... | collective-permute-start | bytes 49160 | tf_op jit(solution)/shard_map/ppermute | solution.py:30
  84.8 11.1 %collective-permute-start.17 = (bf16[128,1024]{1,0:T(8,128)(2,1)S(1)}, bf16[128,1024]{1,0:T(8,128)(2,1)S(1)}, u32[]{:S(2)}, u32[]{:S(2)}) collective-permute-start(bf16[128,1024]{1,0:T(8,128)(2,1)S(1)} %get-tuple-element.75.refs_3_), channel_id=1, source_target_pairs={{0,1},{1,0},{2,3},{3,2},{4,5},{5,4},{6,7},{7,6},{8,9},{9,8},{10,11... | collective-permute-start | bytes 786440 | tf_op jit(solution)/shard_map/ppermute | solution.py:30
  85.3 10.7 %collective-permute-start.19 = (bf16[128,1024]{1,0:T(8,128)(2,1)S(1)}, bf16[128,1024]{1,0:T(8,128)(2,1)S(1)}, u32[]{:S(2)}, u32[]{:S(2)}) collective-permute-start(bf16[128,1024]{1,0:T(8,128)(2,1)S(1)} %get-tuple-element.75.refs_3_), channel_id=1, source_target_pairs={{4,0},{8,4},{12,8},{16,12},{20,16},{24,20},{28,24},{5,1},{9,5},{13... | collective-permute-start | bytes 786440 | tf_op jit(solution)/shard_map/ppermute | solution.py:36
  92.0 4.0 %collective-permute-start.18 = (bf16[128,1024]{1,0:T(8,128)(2,1)S(1)}, bf16[128,1024]{1,0:T(8,128)(2,1)S(1)}, u32[]{:S(2)}, u32[]{:S(2)}) collective-permute-start(bf16[128,1024]{1,0:T(8,128)(2,1)S(1)} %collective-permute-done.15.refs_5_), channel_id=1, source_target_pairs={{0,1},{1,0},{2,3},{3,2},{4,5},{5,4},{6,7},{7,6},{8,9},{9,8},{10,11... | collective-permute-start | bytes 786440 | tf_op jit(solution)/shard_map/ppermute | solution.py:30
  92.0 3.9 %collective-permute-start.16 = (f32[64,64]{1,0:T(8,128)S(1)}, f32[64,64]{1,0:T(8,128)S(1)}, u32[]{:S(2)}, u32[]{:S(2)}) collective-permute-start(f32[64,64]{1,0:T(8,128)S(1)} %add.37), channel_id=1, source_target_pairs={{0,2},{1,3},{2,0},{3,1},{4,6},{5,7},{6,4},{7,5},{8,10},{9,11},{10,... | collective-permute-start | bytes 49160 | tf_op jit(solution)/shard_map/ppermute | solution.py:30
  103.1 4.8 %collective-permute-start.21 = (f32[4,64,512]{2,1,0:T(8,128)S(1)}, f32[4,64,512]{2,1,0:T(8,128)S(1)}, u32[]{:S(2)}, u32[]{:S(2)}) collective-permute-start(f32[4,64,512]{2,1,0:T(8,128)S(1)} %get-tuple-element.82), channel_id=1, source_target_pairs={{0,1},{1,0},{2,3},{3,2},{4,5},{5,4},{6,7},{7,6},{8,9},{9,8},{10,11... | collective-permute-start | bytes 1572872 | tf_op jit(solution)/shard_map/ppermute | solution.py:30
  103.2 22.4 %collective-permute-start.20 = (f32[2,64,512]{2,1,0:T(8,128)S(1)}, f32[2,64,512]{2,1,0:T(8,128)S(1)}, u32[]{:S(2)}, u32[]{:S(2)}) collective-permute-start(f32[2,64,512]{2,1,0:T(8,128)S(1)} %get-tuple-element.81), channel_id=1, source_target_pairs={{0,4},{4,8},{8,12},{12,16},{16,20},{20,24},{24,28},{1,5},{5,9},{9,... | collective-permute-start | bytes 786440 | tf_op jit(solution)/shard_map/ppermute | solution.py:36
  108.0 17.6 %collective-permute-start.22 = (f32[2,64,512]{2,1,0:T(8,128)S(1)}, f32[2,64,512]{2,1,0:T(8,128)S(1)}, u32[]{:S(2)}, u32[]{:S(2)}) collective-permute-start(f32[2,64,512]{2,1,0:T(8,128)S(1)} %slice_add_fusion.1), channel_id=1, source_target_pairs={{0,2},{1,3},{2,0},{3,1},{4,6},{5,7},{6,4},{7,5},{8,10},{9,11},{10,... | collective-permute-start | bytes 786440 | tf_op jit(solution)/shard_map/ppermute | solution.py:30
  109.1 5.6 %collective-permute-start.23 = (f32[64,64]{1,0:T(8,128)S(1)}, f32[64,64]{1,0:T(8,128)S(1)}, u32[]{:S(2)}, u32[]{:S(2)}) collective-permute-start(f32[64,64]{1,0:T(8,128)S(1)} %add.38), channel_id=1, source_target_pairs={{0,4},{4,0},{8,12},{12,8},{16,20},{20,16},{24,28},{28,24},{1,5},{5... | collective-permute-start | bytes 49160 | tf_op jit(solution)/shard_map/ppermute | solution.py:30
  114.6 4.1 %collective-permute-start.24 = (f32[64,64]{1,0:T(8,128)S(1)}, f32[64,64]{1,0:T(8,128)S(1)}, u32[]{:S(2)}, u32[]{:S(2)}) collective-permute-start(f32[64,64]{1,0:T(8,128)S(1)} %add.40), channel_id=1, source_target_pairs={{0,8},{4,12},{8,0},{12,4},{16,24},{20,28},{24,16},{28,20},{1,9},{5... | collective-permute-start | bytes 49160 | tf_op jit(solution)/shard_map/ppermute | solution.py:30
  118.7 4.8 %collective-permute-start.25 = (f32[64,64]{1,0:T(8,128)S(1)}, f32[64,64]{1,0:T(8,128)S(1)}, u32[]{:S(2)}, u32[]{:S(2)}) collective-permute-start(f32[64,64]{1,0:T(8,128)S(1)} %add.41), channel_id=1, source_target_pairs={{0,16},{4,20},{8,24},{12,28},{16,0},{20,4},{24,8},{28,12},{1,17},{... | collective-permute-start | bytes 49160 | tf_op jit(solution)/shard_map/ppermute | solution.py:30
  127.1 1.3 collective-permute-start.26
  128.3 3.9 %collective-permute-start.27 = (f32[64,64]{1,0:T(8,128)S(1)}, f32[64,64]{1,0:T(8,128)S(1)}, u32[]{:S(2)}, u32[]{:S(2)}) collective-permute-start(f32[64,64]{1,0:T(8,128)S(1)} %add.43), channel_id=1, source_target_pairs={{0,2},{1,3},{2,0},{3,1},{4,6},{5,7},{6,4},{7,5},{8,10},{9,11},{10,... | collective-permute-start | bytes 49160 | tf_op jit(solution)/shard_map/ppermute | solution.py:30
  132.3 4.2 %collective-permute-start.28 = (f32[64,64]{1,0:T(8,128)S(1)}, f32[64,64]{1,0:T(8,128)S(1)}, u32[]{:S(2)}, u32[]{:S(2)}) collective-permute-start(f32[64,64]{1,0:T(8,128)S(1)} %add.44), channel_id=1, source_target_pairs={{0,4},{4,0},{8,12},{12,8},{16,20},{20,16},{24,28},{28,24},{1,5},{5... | collective-permute-start | bytes 49160 | tf_op jit(solution)/shard_map/ppermute | solution.py:30
  136.5 3.9 %collective-permute-start.29 = (f32[64,64]{1,0:T(8,128)S(1)}, f32[64,64]{1,0:T(8,128)S(1)}, u32[]{:S(2)}, u32[]{:S(2)}) collective-permute-start(f32[64,64]{1,0:T(8,128)S(1)} %add.45), channel_id=1, source_target_pairs={{0,8},{4,12},{8,0},{12,4},{16,24},{20,28},{24,16},{28,20},{1,9},{5... | collective-permute-start | bytes 49160 | tf_op jit(solution)/shard_map/ppermute | solution.py:30
  140.4 4.8 %collective-permute-start.30 = (f32[64,64]{1,0:T(8,128)S(1)}, f32[64,64]{1,0:T(8,128)S(1)}, u32[]{:S(2)}, u32[]{:S(2)}) collective-permute-start(f32[64,64]{1,0:T(8,128)S(1)} %add.46), channel_id=1, source_target_pairs={{0,16},{4,20},{8,24},{12,28},{16,0},{20,4},{24,8},{28,12},{1,17},{... | collective-permute-start | bytes 49160 | tf_op jit(solution)/shard_map/ppermute | solution.py:30

commit v6 on v5

--- a/solution.py
+++ b/solution.py
@@ -88,8 +88,10 @@
 
 
 def is_early(place, group, blocks_dev):
-    near_by = jnp.logical_and(place < min(2, group) * blocks_dev, place < group * blocks_dev)
-    return jnp.logical_or(near_by, lax.rem(place, blocks_dev) < blocks_dev // 2)
+    near_by = place < min(2, group) * blocks_dev
+    direct = lax.rem(lax.div(place, blocks_dev), 2) == 0
+    first_half = lax.rem(place, blocks_dev) < blocks_dev // 2
+    return jnp.logical_or(near_by, jnp.logical_and(direct, first_half))
 
 
 def listing_kernel(group, cap, early_cap, blocks_dev, rows, cols, live, out_rows, out_cols, out_n):
@@ -214,27 +216,37 @@
         level_col[place] = jnp.broadcast_to(total, (PTS, 128))
 
 
-def make_tiles(low, high, rows, cols, window, level_row, level_col, kept):
+def make_tiles(low, high, rows, cols, window, level_row, level_col, kept, buffers):
     width = window.shape[1]
-    step = 256
     scale = 6.0 / width * LOG2E
-
-    def body(index, carry):
+    count = high - low
+    spare = kept.shape[0] - 1
+
+    def cross(tile, buffer):
+        index = low + jnp.minimum(tile, count - 1)
+        left = window[pl.ds(pl.multiple_of(rows[index] * PTS, PTS), PTS), :]
+        right = window[pl.ds(pl.multiple_of(cols[index] * PTS, PTS), PTS), :]
+        buffer[...] = lax.dot_general(
+            left, right, (((1,), (1,)), ((), ())), preferred_element_type=jnp.float32
+        )
+
+    def finish(tile, buffer):
+        valid = jnp.logical_and(tile >= 0, tile < count)
+        index = low + jnp.clip(tile, 0, count - 1)
         row, col = rows[index], cols[index]
-        right = window[pl.ds(pl.multiple_of(col * PTS, PTS), PTS), :]
         right_level = level_row[col][0:1, :]
-        for part in range(PTS // step):
-            left = window[pl.ds(pl.multiple_of(row * PTS + part * step, step), step), :]
-            cross = lax.dot_general(
-                left, right, (((1,), (1,)), ((), ())), preferred_element_type=jnp.float32
-            )
-            left_level = level_col[row, part * step : (part + 1) * step, :]
-            left_level = jnp.concatenate([left_level] * (PTS // 128), axis=1)
-            value = jnp.exp2(cross * scale - left_level - right_level)
-            kept[index - low, part * step : (part + 1) * step, :] = value.astype(jnp.bfloat16)
+        left_level = jnp.concatenate([level_col[row]] * (PTS // 128), axis=1)
+        value = jnp.exp2(buffer[...] * scale - left_level - right_level)
+        kept[jnp.where(valid, tile, spare)] = value.astype(jnp.bfloat16)
+
+    def body(pair, carry):
+        cross(2 * pair, buffers[0])
+        finish(2 * pair - 1, buffers[1])
+        cross(2 * pair + 1, buffers[1])
+        finish(2 * pair, buffers[0])
         return carry
 
-    lax.fori_loop(low, high, body, 0)
+    lax.fori_loop(0, jnp.where(count > 0, lax.div(count, 2) + 1, 0), body, 0)
 
 
 def build_tiles(stage, fresh, places, n, rows, cols, pts, levels, group, blocks_dev, cap, name):
@@ -245,13 +257,13 @@
         jax.ShapeDtypeStruct((total, 8, PTS), jnp.float32),
         jax.ShapeDtypeStruct((near, PTS, 128), jnp.float32),
     ]
-    shapes = [jax.ShapeDtypeStruct((cap, PTS, PTS), jnp.bfloat16)] + level_shapes
+    shapes = [jax.ShapeDtypeStruct((cap + 1, PTS, PTS), jnp.bfloat16)] + level_shapes
 
     def kernel(*refs):
         n_ref, row_ref, col_ref = refs[:3]
         pt_refs = refs[3 : 3 + len(pts)]
         level_refs = refs[3 + len(pts) : 3 + len(pts) + len(levels)]
-        kept, level_row, level_col, window = refs[3 + len(pts) + len(levels) :]
+        kept, level_row, level_col, window, *buffers = refs[3 + len(pts) + len(levels) :]
         for place, piece in zip(places, pt_refs):
             window[place * PTS : place * PTS + piece.shape[0], :] = piece[...]
         for index, (place, piece) in enumerate(zip(places, pt_refs)):
@@ -262,8 +274,18 @@
                     level_row[block] = level_refs[0][block]
                     if block < near:
                         level_col[block] = level_refs[1][block]
+        for buffer in buffers:
+            buffer[...] = jnp.zeros((PTS, PTS), jnp.float32)
         make_tiles(
-            n_ref[stage], n_ref[stage + 1], row_ref, col_ref, window, level_row, level_col, kept
+            n_ref[stage],
+            n_ref[stage + 1],
+            row_ref,
+            col_ref,
+            window,
+            level_row,
+            level_col,
+            kept,
+            buffers,
         )
 
     return pl.pallas_call(
@@ -271,7 +293,8 @@
         out_shape=tuple(shapes),
         in_specs=[spec(SMEM)] * 3 + [spec(VMEM)] * (len(pts) + len(levels)),
         out_specs=(spec(VMEM),) * len(shapes),
-        scratch_shapes=[VMEM((total * PTS, width), jnp.bfloat16)],
+        scratch_shapes=[VMEM((total * PTS, width), jnp.bfloat16)]
+        + [VMEM((PTS, PTS), jnp.float32)] * 2,
         cost_estimate=cost(2**20 if stage == 0 else 2**32, 2**20),
         compiler_params=pltpu.CompilerParams(vmem_limit_bytes=14 * 2**20),
         name=name,
@@ -493,12 +516,23 @@
 
 
 def sum_stages():
-    return [(axis, bit) for axis in ("grp", "blk") for bit in bits_of(lax.axis_size(axis))]
+    bits = bits_of(lax.axis_size("blk") * lax.axis_size("grp"))
+    return [bits[:1]] + [bits[first : first + 2] for first in range(1, len(bits), 2)]
 
 
 def all_sum(value, stages):
-    for axis, bit in stages:
-        value = value + swap(value, axis, bit)
+    count = lax.axis_size("blk") * lax.axis_size("grp")
+    for bits in stages:
+        moves = [0]
+        for bit in bits:
+            moves += [move ^ bit for move in moves]
+        terms = [value] + [
+            lax.ppermute(value, ("blk", "grp"), [(source, source ^ move) for source in range(count)])
+            for move in moves[1:]
+        ]
+        while len(terms) > 1:
+            terms = [left + right for left, right in zip(terms[::2], terms[1::2])]
+        value = terms[0]
     return value
 
 
@@ -525,13 +559,19 @@
     far_vec = from_behind(vec, "blk", -1)
     mate_vec = swap(vec, "grp", 1)
 
-    def placed(index):
+    def arrived(index):
         offset = index * (blocks_dev // 2)
         found = [(group * blocks_dev + offset, far[index])]
-        for rel, value in crossed[index].items():
-            found.append((rel * blocks_dev + offset, value))
-            found.append(((rel ^ 1) * blocks_dev + offset, swap(value, "grp", 1)))
-        return found
+        return found + [
+            (rel * blocks_dev + offset, value) for rel, value in crossed[index].items()
+        ]
+
+    def passed_on(index):
+        offset = index * (blocks_dev // 2)
+        return [
+            ((rel ^ 1) * blocks_dev + offset, swap(value, "grp", 1))
+            for rel, value in crossed[index].items()
+        ]
 
     def tiles_of(stage, fresh, pieces, levels, size, name):
         places, pts = zip(*pieces)
@@ -539,12 +579,12 @@
             stage, fresh, places, n, rows, cols, pts, levels, group, blocks_dev, size, name
         )
 
-    early = [(0, points), (blocks_dev, mate)] + placed(0)
+    early = [(0, points), (blocks_dev, mate)] + arrived(0)
     early_kept, *levels = tiles_of(0, len(early), early, (), early_cap, "early_tiles")
     tied = lax.optimization_barrier((far[1], levels[0], *crossed[1].values()))
     far[1], levels[0] = tied[:2]
     crossed[1] = dict(zip(crossed[1], tied[2:]))
-    late = placed(1)
+    late = passed_on(0) + arrived(1) + passed_on(1)
     late_kept, _, _ = tiles_of(1, len(late), late + early, levels, cap, "late_tiles")
     tied = lax.optimization_barrier((late_kept, *cross_vec.values()))
     kept = (early_kept, tied[0])
@@ -573,8 +613,10 @@
         gram = all_sum(gram, stages[1:2])
         gram, *vecs = lax.optimization_barrier((gram, *vecs))
         messages = products(n, rows, cols, vecs, kept, group, blocks_dev, columns, 2)
+        gram = all_sum(gram, stages[2:])
+        gram, *messages = lax.optimization_barrier((gram, *messages))
         sums = sum_products(messages, group, blocks_dev)
-        inverse = factor(all_sum(gram, stages[2:]))
+        inverse = factor(gram)
         z, gram, *parts = scaled_gram(sums, z, counts, degree, inverse, turn + 1 < ITERS)
         parts = parts[0] if parts else None
     return embedding(all_sum(gram, sum_stages()), z)

time: 148 us -> 141 us (0.953)
  waiting for transfers between devices: 66.8 us -> 49.8 us
  starting transfers between devices: 34.2 us -> 42.3 us
    ppermute x25 -> x15, waiting for transfers between devices: 36.1 us -> 10.6 us  [swap(): lax.ppermute(value, axis, [(source, source ^ bit) for source in range(cou...]
    ppermute x0 -> x14, starting transfers between devices: none -> 17.8 us  [all_sum(): lax.ppermute(value, ('blk', 'grp'), [(source, source ^ move) for source i...]
    ppermute x0 -> x14, waiting for transfers between devices: none -> 12.5 us  [all_sum(): lax.ppermute(value, ('blk', 'grp'), [(source, source ^ move) for source i...]
    ppermute x25 -> x15, starting transfers between devices: 18.7 us -> 10.3 us  [swap(): lax.ppermute(value, axis, [(source, source ^ bit) for source in range(cou...]
    ppermute x6, waiting for transfers between devices: 30.6 us -> 26.7 us  [from_behind(): lax.ppermute(value, axis, [(source, source + steps) for source in range(i...]
  transfers between devices with their start and end apart: 31 -> 35, of which waited for: 16 -> 16; matrix products, arithmetic and copies ran while one was open for 1% -> 1% of each run, Pallas kernels for 17% -> 24%
where the time goes in v6:
time: 141 us
  waiting for transfers between devices  49.8 us (35%)
  Pallas kernels  46.1 us (33%)
  starting transfers between devices  42.3 us (30%)
  local copies, waits for them, and re-layouts  1.52 us (1%)
    ppermute x6, waiting for transfers between devices, from_behind(): lax.ppermute(value, axis, [(source, source + steps) for source in range(i...  26.7 us
    ppermute x14, starting transfers between devices, all_sum(): lax.ppermute(value, ('blk', 'grp'), [(source, source ^ move) for source i...  17.8 us
    pallas_call x2, Pallas kernels, build_tiles(): pl.pallas_call(kernel, out_shape=tuple(shapes), in_specs=[spec(SMEM)] * 3...  16.8 us
    ppermute x6, starting transfers between devices, from_behind(): lax.ppermute(value, axis, [(source, source + steps) for source in range(i...  14.2 us
    pallas_call x2, Pallas kernels, products(): pl.pallas_call(kernel, out_shape=tuple(shapes), in_specs=[spec(SMEM)] * 3...  13.9 us
    ppermute x14, waiting for transfers between devices, all_sum(): lax.ppermute(value, ('blk', 'grp'), [(source, source ^ move) for source i...  12.5 us
    ppermute x15, waiting for transfers between devices, swap(): lax.ppermute(value, axis, [(source, source ^ bit) for source in range(cou...  10.6 us
    ppermute x15, starting transfers between devices, swap(): lax.ppermute(value, axis, [(source, source ^ bit) for source in range(cou...  10.3 us
  transfers between devices with their start and end apart: 35, of which 16 were waited for; matrix products, arithmetic and copies ran while one was open for 1% of the time, Pallas kernels for 24%

profile of v6, /device:TPU:0, one launch (start us, length us, event | category | flops | bytes accessed | tf_op | source)
XLA Modules:
  0.0 140.8 jit_solution(9427902888505369457)
XLA Ops:
  0.0 0.5 collective-permute-start
  0.5 1.5 %fusion = (bf16[512,768]{1,0:T(8,128)(2,1)S(1)}, bf16[512,768]{1,0:T(8,128)(2,1)S(1)}) fusion(bf16[1024,768]{1,0:T(8,128)(2,1)} %refs_7_.1), kind=kLoop, calls=%fused_computation.6 | loop fusion | bytes 3145728 | tf_op jit(solution)/shard_map/slice | solution.py:550
  2.1 1.3 collective-permute-start.1
  3.4 2.7 %collective-permute-start.2 = (bf16[512,768]{1,0:T(8,128)(2,1)S(1)}, bf16[512,768]{1,0:T(8,128)(2,1)S(1)}, u32[]{:S(2)}, u32[]{:S(2)}) collective-permute-start(bf16[512,768]{1,0:T(8,128)(2,1)S(1)} %get-tuple-element.100), channel_id=1, source_target_pairs={{0,2},{1,3},{2,0},{3,1},{4,6},{5,7},{6,4},{7,5},{8,10},{9,11},{10,... | collective-permute-start | bytes 2359304 | tf_op jit(solution)/shard_map/ppermute | solution.py:30
  6.0 1.3 collective-permute-start.5
  7.3 0.1 collective-permute-start.6
  8.1 7.3 %listing.1 = (s32[16]{0:T(128)S(1)}, s32[16]{0:T(128)S(1)}, s32[3]{0:T(128)S(1)}) custom-call(s32[64]{0:T(128)S(1)} %copy-done.3, s32[64]{0:T(128)S(1)} %copy-done.4, s32[1]{0:T(128)S(6)} %copy.7.live), custom_call_target="tpu_custom_call" | custom-call | flops 1048576 | bytes 1024 | tf_op jit(solution)/shard_map/listing/pallas_call | solution.py:160
  15.3 0.0 collective-permute-done.refs_4_.refs_8_
  15.4 0.6 opening.1.refs_3_.refs_4_
  15.9 9.0 %collective-permute-done.1.refs_5_.refs_9_ = bf16[512,768]{1,0:T(8,128)(2,1)S(1)} collective-permute-done((bf16[512,768]{1,0:T(8,128)(2,1)S(1)}, bf16[512,768]{1,0:T(8,128)(2,1)S(1)}, u32[]{:S(2)}, u32[]{:S(2)}) %collective-permute-start.1) | collective-permute-done | bytes 786464 | tf_op jit(solution)/shard_map/ppermute | solution.py:36
  25.0 0.0 collective-permute-done.2.refs_6_.refs_10_
  25.0 7.9 %early_tiles.1 = (bf16[9,512,512]{2,1,0:T(8,128)(2,1)S(1)}, f32[10,8,512]{2,1,0:T(8,128)S(1)}, f32[8,512,128]{2,1,0:T(8,128)S(1)}) custom-call(s32[3]{0:T(128)S(1)} %get-tuple-element.56.refs_0_, s32[16]{0:T(128)S(1)} %get-tuple-element.57.refs_1_, s32[16]{0:T(128)S(1)} %get-tuple-element.58.refs_2_, bf16[1024,768]{1,0:T(8,128)(2,1)S(1)} %copy-done, ...), custom_call_target="tpu_custom_call" | custom-call | flops 1048576 | bytes 1048576 | tf_op jit(solution)/shard_map/early_tiles/pallas_call | solution.py:291
  32.9 8.6 %collective-permute-done.5.refs_4_ = bf16[512,768]{1,0:T(8,128)(2,1)S(1)} collective-permute-done((bf16[512,768]{1,0:T(8,128)(2,1)S(1)}, bf16[512,768]{1,0:T(8,128)(2,1)S(1)}, u32[]{:S(2)}, u32[]{:S(2)}) %collective-permute-start.5) | collective-permute-done | bytes 786464 | tf_op jit(solution)/shard_map/ppermute | solution.py:36
  41.5 0.5 collective-permute-start.4
  42.0 1.7 %collective-permute-start.8 = (bf16[80,1024]{1,0:T(8,128)(2,1)S(1)}, bf16[80,1024]{1,0:T(8,128)(2,1)S(1)}, u32[]{:S(2)}, u32[]{:S(2)}) collective-permute-start(bf16[80,1024]{1,0:T(8,128)(2,1)S(1)} %opening.1.refs_3_.refs_4_), channel_id=1, source_target_pairs={{0,2},{1,3},{2,0},{3,1},{4,6},{5,7},{6,4},{7,5},{8,10},{9,11},{10,... | collective-permute-start | bytes 491528 | tf_op jit(solution)/shard_map/ppermute | solution.py:30
  43.7 1.3 collective-permute-start.10
  45.0 0.1 collective-permute-start.3
  45.1 8.9 %late_tiles.1 = (bf16[17,512,512]{2,1,0:T(8,128)(2,1)S(1)}, f32[10,8,512]{2,1,0:T(8,128)}, f32[8,512,128]{2,1,0:T(8,128)}) custom-call(s32[3]{0:T(128)S(1)} %get-tuple-element.56.refs_0_, s32[16]{0:T(128)S(1)} %get-tuple-element.57.refs_1_, s32[16]{0:T(128)S(1)} %get-tuple-element.58.refs_2_, bf16[512,768]{1,0:T(8,128)(2,1)S(1)} %collective-permute-done.4.refs_3_, ...), custom_call_target="tpu_custom_call" | custom-call | flops 4294967296 | bytes 1048576 | tf_op jit(solution)/shard_map/late_tiles/pallas_call | solution.py:291
  54.1 1.5 %collective-permute-start.9 = (bf16[80,1024]{1,0:T(8,128)(2,1)S(1)}, bf16[80,1024]{1,0:T(8,128)(2,1)S(1)}, u32[]{:S(2)}, u32[]{:S(2)}) collective-permute-start(bf16[80,1024]{1,0:T(8,128)(2,1)S(1)} %collective-permute-done.8.refs_5_), channel_id=1, source_target_pairs={{0,1},{1,0},{2,3},{3,2},{4,5},{5,4},{6,7},{7,6},{8,9},{9,8},{10,11... | collective-permute-start | bytes 491528 | tf_op jit(solution)/shard_map/ppermute | solution.py:30
  55.6 0.0 collective-permute-done.10.refs_7_
  55.6 0.0 collective-permute-done.3.refs_4_
  55.6 1.0 collective-permute-done.9.refs_6_
  56.6 6.9 %products.2 = (f32[2,72,512]{2,1,0:T(8,128)S(1)}, f32[4,72,512]{2,1,0:T(8,128)S(1)}, f32[2,72,512]{2,1,0:T(8,128)S(1)}, f32[2,72,512]{2,1,0:T(8,128)S(1)}) custom-call(s32[3]{0:T(128)S(1)} %get-tuple-element.56.refs_0_, s32[16]{0:T(128)S(1)} %get-tuple-element.57.refs_1_, s32[16]{0:T(128)S(1)} %get-tuple-element.58.refs_2_, ...), custom_call_target="tpu_custom_call" | custom-call | flops 4294967296 | bytes 16777216 | tf_op jit(solution)/shard_map/products/pallas_call | solution.py:344
  63.5 0.4 collective-permute-start.12
  63.9 6.0 %collective-permute-start.11 = (f32[2,72,512]{2,1,0:T(8,128)S(1)}, f32[2,72,512]{2,1,0:T(8,128)S(1)}, u32[]{:S(2)}, u32[]{:S(2)}) collective-permute-start(f32[2,72,512]{2,1,0:T(8,128)S(1)} %get-tuple-element.73), channel_id=1, source_target_pairs={{0,4},{4,8},{8,12},{12,16},{16,20},{20,24},{24,28},{1,5},{5,9},{9,... | collective-permute-start | bytes 884744 | tf_op jit(solution)/shard_map/ppermute | solution.py:36
  70.0 0.6 collective-permute-start.13
  70.6 5.9 %collective-permute-done.11.refs_1_ = f32[2,72,512]{2,1,0:T(8,128)S(1)} collective-permute-done((f32[2,72,512]{2,1,0:T(8,128)S(1)}, f32[2,72,512]{2,1,0:T(8,128)S(1)}, u32[]{:S(2)}, u32[]{:S(2)}) %collective-permute-start.11) | collective-permute-done | bytes 294944 | tf_op jit(solution)/shard_map/ppermute | solution.py:36
  76.5 2.4 %collective-permute-done.13.refs_3_ = f32[2,72,512]{2,1,0:T(8,128)S(1)} collective-permute-done((f32[2,72,512]{2,1,0:T(8,128)S(1)}, f32[2,72,512]{2,1,0:T(8,128)S(1)}, u32[]{:S(2)}, u32[]{:S(2)}) %collective-permute-start.13) | collective-permute-done | bytes 294944 | tf_op jit(solution)/shard_map/ppermute | solution.py:30
  78.8 1.0 scaled_gram.2
  79.8 0.8 collective-permute-start.15
  80.7 0.0 collective-permute-start.14
  80.7 0.5 collective-permute-start.19
  81.2 1.3 collective-permute-start.21
  82.5 0.0 collective-permute-done.14
  82.5 4.6 %collective-permute-done.15.refs_5_ = bf16[128,1024]{1,0:T(8,128)(2,1)S(1)} collective-permute-done((bf16[128,1024]{1,0:T(8,128)(2,1)S(1)}, bf16[128,1024]{1,0:T(8,128)(2,1)S(1)}, u32[]{:S(2)}, u32[]{:S(2)}) %collective-permute-start.15) | collective-permute-done | bytes 262176 | tf_op jit(solution)/shard_map/ppermute | solution.py:30
  87.1 1.0 collective-permute-start.16
  88.1 1.5 %collective-permute-start.17 = (f32[64,64]{1,0:T(8,128)S(1)}, f32[64,64]{1,0:T(8,128)S(1)}, u32[]{:S(2)}, u32[]{:S(2)}) collective-permute-start(f32[64,64]{1,0:T(8,128)S(1)} %add.49), channel_id=1, source_target_pairs={{0,4},{1,5},{2,6},{3,7},{4,0},{5,1},{6,2},{7,3},{8,12},{9,13},{10,... | collective-permute-start | bytes 49160 | tf_op jit(solution)/shard_map/ppermute | solution.py:530
  89.6 1.4 %collective-permute-done.16 = f32[64,64]{1,0:T(8,128)S(1)} collective-permute-done((f32[64,64]{1,0:T(8,128)S(1)}, f32[64,64]{1,0:T(8,128)S(1)}, u32[]{:S(2)}, u32[]{:S(2)}) %collective-permute-start.16) | collective-permute-done | bytes 16416 | tf_op jit(solution)/shard_map/ppermute | solution.py:530
  91.0 1.9 %collective-permute-start.18 = (f32[64,64]{1,0:T(8,128)S(1)}, f32[64,64]{1,0:T(8,128)S(1)}, u32[]{:S(2)}, u32[]{:S(2)}) collective-permute-start(f32[64,64]{1,0:T(8,128)S(1)} %add.49), channel_id=1, source_target_pairs={{0,6},{1,7},{2,4},{3,5},{4,2},{5,3},{6,0},{7,1},{8,14},{9,15},{10,... | collective-permute-start | bytes 49160 | tf_op jit(solution)/shard_map/ppermute | solution.py:530
  92.9 2.9 %collective-permute-done.18 = f32[64,64]{1,0:T(8,128)S(1)} collective-permute-done((f32[64,64]{1,0:T(8,128)S(1)}, f32[64,64]{1,0:T(8,128)S(1)}, u32[]{:S(2)}, u32[]{:S(2)}) %collective-permute-start.18) | collective-permute-done | bytes 16416 | tf_op jit(solution)/shard_map/ppermute | solution.py:530
  95.9 1.8 %collective-permute-start.22 = (f32[64,64]{1,0:T(8,128)S(1)}, f32[64,64]{1,0:T(8,128)S(1)}, u32[]{:S(2)}, u32[]{:S(2)}) collective-permute-start(f32[64,64]{1,0:T(8,128)S(1)} %add_add_fusion.3), channel_id=1, source_target_pairs={{0,8},{1,9},{2,10},{3,11},{4,12},{5,13},{6,14},{7,15},{8,0},{9,1},... | collective-permute-start | bytes 49160 | tf_op jit(solution)/shard_map/ppermute | solution.py:530
  97.7 3.5 %collective-permute-start.23 = (f32[64,64]{1,0:T(8,128)S(1)}, f32[64,64]{1,0:T(8,128)S(1)}, u32[]{:S(2)}, u32[]{:S(2)}) collective-permute-start(f32[64,64]{1,0:T(8,128)S(1)} %add_add_fusion.3), channel_id=1, source_target_pairs={{0,16},{1,17},{2,18},{3,19},{4,20},{5,21},{6,22},{7,23},{8,24},{9,... | collective-permute-start | bytes 49160 | tf_op jit(solution)/shard_map/ppermute | solution.py:530
  101.2 7.1 %products.3 = (f32[2,64,512]{2,1,0:T(8,128)S(1)}, f32[4,64,512]{2,1,0:T(8,128)S(1)}, f32[2,64,512]{2,1,0:T(8,128)S(1)}, f32[2,64,512]{2,1,0:T(8,128)S(1)}) custom-call(s32[3]{0:T(128)S(1)} %get-tuple-element.56.refs_0_, s32[16]{0:T(128)S(1)} %get-tuple-element.57.refs_1_, s32[16]{0:T(128)S(1)} %get-tuple-element.58.refs_2_, ...), custom_call_target="tpu_custom_call" | custom-call | flops 4294967296 | bytes 16777216 | tf_op jit(solution)/shard_map/products/pallas_call | solution.py:344
  108.3 0.1 collective-permute-start.26
  108.4 3.1 %collective-permute-start.25 = (f32[2,64,512]{2,1,0:T(8,128)S(1)}, f32[2,64,512]{2,1,0:T(8,128)S(1)}, u32[]{:S(2)}, u32[]{:S(2)}) collective-permute-start(f32[2,64,512]{2,1,0:T(8,128)S(1)} %get-tuple-element.91), channel_id=1, source_target_pairs={{0,4},{4,8},{8,12},{12,16},{16,20},{20,24},{24,28},{1,5},{5,9},{9,... | collective-permute-start | bytes 786440 | tf_op jit(solution)/shard_map/ppermute | solution.py:36
  111.5 0.7 collective-permute-start.27
  112.3 2.0 %factor.1.refs_6_ = f32[64,64]{1,0:T(8,128)S(1)} custom-call(f32[64,64]{1,0:T(8,128)S(1)} %add_add_fusion.2.gram), custom_call_target="tpu_custom_call" | custom-call | flops 2147483648 | bytes 65536 | tf_op jit(solution)/shard_map/factor/pallas_call | solution.py:469
  114.2 3.2 %collective-permute-done.25.refs_1_ = f32[2,64,512]{2,1,0:T(8,128)S(1)} collective-permute-done((f32[2,64,512]{2,1,0:T(8,128)S(1)}, f32[2,64,512]{2,1,0:T(8,128)S(1)}, u32[]{:S(2)}, u32[]{:S(2)}) %collective-permute-start.25) | collective-permute-done | bytes 262176 | tf_op jit(solution)/shard_map/ppermute | solution.py:36
  117.5 2.5 %collective-permute-done.27.refs_3_ = f32[2,64,512]{2,1,0:T(8,128)S(1)} collective-permute-done((f32[2,64,512]{2,1,0:T(8,128)S(1)}, f32[2,64,512]{2,1,0:T(8,128)S(1)}, u32[]{:S(2)}, u32[]{:S(2)}) %collective-permute-start.27) | collective-permute-done | bytes 262176 | tf_op jit(solution)/shard_map/ppermute | solution.py:30
  120.0 1.5 %scaled_gram.3 = (f32[64,1024]{1,0:T(8,128)S(1)}, f32[64,64]{1,0:T(8,128)S(1)}) custom-call(s32[2]{0:T(128)S(1)} %copy-done.2, f32[2,64,512]{2,1,0:T(8,128)S(1)} %get-tuple-element.90.refs_0_, f32[2,64,512]{2,1,0:T(8,128)S(1)} %collective-permute-done.25.refs_1_, f32[4,64,512]{2,1,0:T(8,128)S(1)} %collective-permute-done.26.refs_2_, ...), custom_call_target="tpu_custom_call" | custom-call | flops 67108864 | bytes 2097152 | tf_op jit(solution)/shard_map/scaled_gram/pallas_call | solution.py:410
  121.5 0.1 collective-permute-start.28
  121.6 1.2 collective-permute-done.28
  122.8 0.7 collective-permute-start.29
  123.5 1.0 collective-permute-start.30
  124.5 1.8 %collective-permute-start.31 = (f32[64,64]{1,0:T(8,128)S(1)}, f32[64,64]{1,0:T(8,128)S(1)}, u32[]{:S(2)}, u32[]{:S(2)}) collective-permute-start(f32[64,64]{1,0:T(8,128)S(1)} %add.57), channel_id=1, source_target_pairs={{0,6},{1,7},{2,4},{3,5},{4,2},{5,3},{6,0},{7,1},{8,14},{9,15},{10,... | collective-permute-start | bytes 49160 | tf_op jit(solution)/shard_map/ppermute | solution.py:530
  126.3 0.4 collective-permute-done.29
  126.7 0.7 collective-permute-done.30
  127.4 1.9 %collective-permute-done.31 = f32[64,64]{1,0:T(8,128)S(1)} collective-permute-done((f32[64,64]{1,0:T(8,128)S(1)}, f32[64,64]{1,0:T(8,128)S(1)}, u32[]{:S(2)}, u32[]{:S(2)}) %collective-permute-start.31) | collective-permute-done | bytes 16416 | tf_op jit(solution)/shard_map/ppermute | solution.py:530
  129.3 0.1 collective-permute-start.32
  129.4 2.7 %collective-permute-start.33 = (f32[64,64]{1,0:T(8,128)S(1)}, f32[64,64]{1,0:T(8,128)S(1)}, u32[]{:S(2)}, u32[]{:S(2)}) collective-permute-start(f32[64,64]{1,0:T(8,128)S(1)} %add_add_fusion.1), channel_id=1, source_target_pairs={{0,16},{1,17},{2,18},{3,19},{4,20},{5,21},{6,22},{7,23},{8,24},{9,... | collective-permute-start | bytes 49160 | tf_op jit(solution)/shard_map/ppermute | solution.py:530
  132.1 1.6 %collective-permute-start.34 = (f32[64,64]{1,0:T(8,128)S(1)}, f32[64,64]{1,0:T(8,128)S(1)}, u32[]{:S(2)}, u32[]{:S(2)}) collective-permute-start(f32[64,64]{1,0:T(8,128)S(1)} %add_add_fusion.1), channel_id=1, source_target_pairs={{0,24},{1,25},{2,26},{3,27},{4,28},{5,29},{6,30},{7,31},{8,16},{9,... | collective-permute-start | bytes 49160 | tf_op jit(solution)/shard_map/ppermute | solution.py:530
  133.7 0.5 collective-permute-done.33
  134.2 3.6 %collective-permute-done.34 = f32[64,64]{1,0:T(8,128)S(1)} collective-permute-done((f32[64,64]{1,0:T(8,128)S(1)}, f32[64,64]{1,0:T(8,128)S(1)}, u32[]{:S(2)}, u32[]{:S(2)}) %collective-permute-start.34) | collective-permute-done | bytes 16416 | tf_op jit(solution)/shard_map/ppermute | solution.py:530
  137.8 3.0 %embedding.1 = f32[64,1024]{1,0:T(8,128)} custom-call(f32[64,64]{1,0:T(8,128)S(1)} %add_add_fusion.gram, f32[64,1024]{1,0:T(8,128)S(1)} %get-tuple-element.98.z), custom_call_target="tpu_custom_call" | custom-call | flops 1073741824 | bytes 1048576 | tf_op jit(solution)/shard_map/embedding/pallas_call | solution.py:487
  (35 shorter events, 0.2 us)
Async XLA Ops:
  0.0 25.0 %copy-start = (bf16[1024,768]{1,0:T(8,128)(2,1)S(1)}, bf16[1024,768]{1,0:T(8,128)(2,1)}, u32[]{:S(2)}) copy-start(bf16[1024,768]{1,0:T(8,128)(2,1)} %refs_7_.1) | copy-start | bytes 4718596
  0.0 8.1 %copy-start.3 = (s32[64]{0:T(128)S(1)}, s32[64]{0:T(128)}, u32[]{:S(2)}) copy-start(s32[64]{0:T(128)} %rows.1) | copy-start | bytes 772
  0.0 8.1 %copy-start.4 = (s32[64]{0:T(128)S(1)}, s32[64]{0:T(128)}, u32[]{:S(2)}) copy-start(s32[64]{0:T(128)} %cols.1) | copy-start | bytes 772
  0.0 15.3 %copy-start.1 = (f32[64,1024]{1,0:T(8,128)S(1)}, f32[64,1024]{1,0:T(8,128)}, u32[]{:S(2)}) copy-start(f32[64,1024]{1,0:T(8,128)} %start) | copy-start | bytes 786436
  0.0 15.4 %copy-start.2 = (s32[2]{0:T(128)S(1)}, s32[2]{0:T(128)}, u32[]{:S(2)}) copy-start(s32[2]{0:T(128)} %count_ref.3) | copy-start | bytes 28
  0.0 15.3 %collective-permute-start = (bf16[1024,768]{1,0:T(8,128)(2,1)}, bf16[1024,768]{1,0:T(8,128)(2,1)S(1)}, u32[]{:S(2)}, u32[]{:S(2)}) collective-permute-start(bf16[1024,768]{1,0:T(8,128)(2,1)} %refs_7_.1), channel_id=1, source_target_pairs={{0,1},{1,0},{2,3},{3,2},{4,5},{5,4},{6,7},{7,6},{8,9},{9,8},{10,11... | collective-permute-start | bytes 4718600 | tf_op jit(solution)/shard_map/ppermute | solution.py:30
  2.1 22.9 %collective-permute-start.1 = (bf16[512,768]{1,0:T(8,128)(2,1)S(1)}, bf16[512,768]{1,0:T(8,128)(2,1)S(1)}, u32[]{:S(2)}, u32[]{:S(2)}) collective-permute-start(bf16[512,768]{1,0:T(8,128)(2,1)S(1)} %get-tuple-element.100), channel_id=1, source_target_pairs={{4,0},{8,4},{12,8},{16,12},{20,16},{24,20},{28,24},{5,1},{9,5},{13... | collective-permute-start | bytes 2359304 | tf_op jit(solution)/shard_map/ppermute | solution.py:36
  3.4 21.6 %collective-permute-start.2 = (bf16[512,768]{1,0:T(8,128)(2,1)S(1)}, bf16[512,768]{1,0:T(8,128)(2,1)S(1)}, u32[]{:S(2)}, u32[]{:S(2)}) collective-permute-start(bf16[512,768]{1,0:T(8,128)(2,1)S(1)} %get-tuple-element.100), channel_id=1, source_target_pairs={{0,2},{1,3},{2,0},{3,1},{4,6},{5,7},{6,4},{7,5},{8,10},{9,11},{10,... | collective-permute-start | bytes 2359304 | tf_op jit(solution)/shard_map/ppermute | solution.py:30
  6.0 35.5 %collective-permute-start.5 = (bf16[512,768]{1,0:T(8,128)(2,1)S(1)}, bf16[512,768]{1,0:T(8,128)(2,1)S(1)}, u32[]{:S(2)}, u32[]{:S(2)}) collective-permute-start(bf16[512,768]{1,0:T(8,128)(2,1)S(1)} %get-tuple-element.99), channel_id=1, source_target_pairs={{4,0},{8,4},{12,8},{16,12},{20,16},{24,20},{28,24},{5,1},{9,5},{13... | collective-permute-start | bytes 2359304 | tf_op jit(solution)/shard_map/ppermute | solution.py:36
  7.3 34.2 %collective-permute-start.6 = (bf16[512,768]{1,0:T(8,128)(2,1)S(1)}, bf16[512,768]{1,0:T(8,128)(2,1)S(1)}, u32[]{:S(2)}, u32[]{:S(2)}) collective-permute-start(bf16[512,768]{1,0:T(8,128)(2,1)S(1)} %get-tuple-element.99), channel_id=1, source_target_pairs={{0,2},{1,3},{2,0},{3,1},{4,6},{5,7},{6,4},{7,5},{8,10},{9,11},{10,... | collective-permute-start | bytes 2359304 | tf_op jit(solution)/shard_map/ppermute | solution.py:30
  41.5 3.6 %collective-permute-start.7 = (bf16[512,768]{1,0:T(8,128)(2,1)S(1)}, bf16[512,768]{1,0:T(8,128)(2,1)S(1)}, u32[]{:S(2)}, u32[]{:S(2)}) collective-permute-start(bf16[512,768]{1,0:T(8,128)(2,1)S(1)} %collective-permute-done.6.refs_5_), channel_id=1, source_target_pairs={{0,1},{1,0},{2,3},{3,2},{4,5},{5,4},{6,7},{7,6},{8,9},{9,8},{10,11... | collective-permute-start | bytes 2359304 | tf_op jit(solution)/shard_map/ppermute | solution.py:30
  41.5 3.6 %collective-permute-start.4 = (bf16[512,768]{1,0:T(8,128)(2,1)S(1)}, bf16[512,768]{1,0:T(8,128)(2,1)S(1)}, u32[]{:S(2)}, u32[]{:S(2)}) collective-permute-start(bf16[512,768]{1,0:T(8,128)(2,1)S(1)} %collective-permute-done.2.refs_6_.refs_10_), channel_id=1, source_target_pairs={{0,1},{1,0},{2,3},{3,2},{4,5},{5,4},{6,7},{7,6},{8,9},{9,8},{10,11... | collective-permute-start | bytes 2359304 | tf_op jit(solution)/shard_map/ppermute | solution.py:30
  42.0 12.0 %collective-permute-start.8 = (bf16[80,1024]{1,0:T(8,128)(2,1)S(1)}, bf16[80,1024]{1,0:T(8,128)(2,1)S(1)}, u32[]{:S(2)}, u32[]{:S(2)}) collective-permute-start(bf16[80,1024]{1,0:T(8,128)(2,1)S(1)} %opening.1.refs_3_.refs_4_), channel_id=1, source_target_pairs={{0,2},{1,3},{2,0},{3,1},{4,6},{5,7},{6,4},{7,5},{8,10},{9,11},{10,... | collective-permute-start | bytes 491528 | tf_op jit(solution)/shard_map/ppermute | solution.py:30
  43.7 11.9 %collective-permute-start.10 = (bf16[80,1024]{1,0:T(8,128)(2,1)S(1)}, bf16[80,1024]{1,0:T(8,128)(2,1)S(1)}, u32[]{:S(2)}, u32[]{:S(2)}) collective-permute-start(bf16[80,1024]{1,0:T(8,128)(2,1)S(1)} %opening.1.refs_3_.refs_4_), channel_id=1, source_target_pairs={{4,0},{8,4},{12,8},{16,12},{20,16},{24,20},{28,24},{5,1},{9,5},{13... | collective-permute-start | bytes 491528 | tf_op jit(solution)/shard_map/ppermute | solution.py:36
  45.0 10.6 %collective-permute-start.3 = (bf16[80,1024]{1,0:T(8,128)(2,1)S(1)}, bf16[80,1024]{1,0:T(8,128)(2,1)S(1)}, u32[]{:S(2)}, u32[]{:S(2)}) collective-permute-start(bf16[80,1024]{1,0:T(8,128)(2,1)S(1)} %opening.1.refs_3_.refs_4_), channel_id=1, source_target_pairs={{0,1},{1,0},{2,3},{3,2},{4,5},{5,4},{6,7},{7,6},{8,9},{9,8},{10,11... | collective-permute-start | bytes 491528 | tf_op jit(solution)/shard_map/ppermute | solution.py:30
  54.1 2.6 %collective-permute-start.9 = (bf16[80,1024]{1,0:T(8,128)(2,1)S(1)}, bf16[80,1024]{1,0:T(8,128)(2,1)S(1)}, u32[]{:S(2)}, u32[]{:S(2)}) collective-permute-start(bf16[80,1024]{1,0:T(8,128)(2,1)S(1)} %collective-permute-done.8.refs_5_), channel_id=1, source_target_pairs={{0,1},{1,0},{2,3},{3,2},{4,5},{5,4},{6,7},{7,6},{8,9},{9,8},{10,11... | collective-permute-start | bytes 491528 | tf_op jit(solution)/shard_map/ppermute | solution.py:30
  63.5 6.5 %collective-permute-start.12 = (f32[4,72,512]{2,1,0:T(8,128)S(1)}, f32[4,72,512]{2,1,0:T(8,128)S(1)}, u32[]{:S(2)}, u32[]{:S(2)}) collective-permute-start(f32[4,72,512]{2,1,0:T(8,128)S(1)} %get-tuple-element.74), channel_id=1, source_target_pairs={{0,1},{1,0},{2,3},{3,2},{4,5},{5,4},{6,7},{7,6},{8,9},{9,8},{10,11... | collective-permute-start | bytes 1769480 | tf_op jit(solution)/shard_map/ppermute | solution.py:30
  63.9 12.6 %collective-permute-start.11 = (f32[2,72,512]{2,1,0:T(8,128)S(1)}, f32[2,72,512]{2,1,0:T(8,128)S(1)}, u32[]{:S(2)}, u32[]{:S(2)}) collective-permute-start(f32[2,72,512]{2,1,0:T(8,128)S(1)} %get-tuple-element.73), channel_id=1, source_target_pairs={{0,4},{4,8},{8,12},{12,16},{16,20},{20,24},{24,28},{1,5},{5,9},{9,... | collective-permute-start | bytes 884744 | tf_op jit(solution)/shard_map/ppermute | solution.py:36
  70.0 8.8 %collective-permute-start.13 = (f32[2,72,512]{2,1,0:T(8,128)S(1)}, f32[2,72,512]{2,1,0:T(8,128)S(1)}, u32[]{:S(2)}, u32[]{:S(2)}) collective-permute-start(f32[2,72,512]{2,1,0:T(8,128)S(1)} %slice_add_fusion), channel_id=1, source_target_pairs={{0,2},{1,3},{2,0},{3,1},{4,6},{5,7},{6,4},{7,5},{8,10},{9,11},{10,... | collective-permute-start | bytes 884744 | tf_op jit(solution)/shard_map/ppermute | solution.py:30
  79.8 7.3 %collective-permute-start.15 = (bf16[128,1024]{1,0:T(8,128)(2,1)S(1)}, bf16[128,1024]{1,0:T(8,128)(2,1)S(1)}, u32[]{:S(2)}, u32[]{:S(2)}) collective-permute-start(bf16[128,1024]{1,0:T(8,128)(2,1)S(1)} %get-tuple-element.81.refs_3_), channel_id=1, source_target_pairs={{0,2},{1,3},{2,0},{3,1},{4,6},{5,7},{6,4},{7,5},{8,10},{9,11},{10,... | collective-permute-start | bytes 786440 | tf_op jit(solution)/shard_map/ppermute | solution.py:30
  80.7 1.8 %collective-permute-start.14 = (f32[64,64]{1,0:T(8,128)S(1)}, f32[64,64]{1,0:T(8,128)S(1)}, u32[]{:S(2)}, u32[]{:S(2)}) collective-permute-start(f32[64,64]{1,0:T(8,128)S(1)} %get-tuple-element.76), channel_id=1, source_target_pairs={{0,1},{1,0},{2,3},{3,2},{4,5},{5,4},{6,7},{7,6},{8,9},{9,8},{10,11... | collective-permute-start | bytes 49160 | tf_op jit(solution)/shard_map/ppermute | solution.py:530
  80.7 15.2 %collective-permute-start.19 = (bf16[128,1024]{1,0:T(8,128)(2,1)S(1)}, bf16[128,1024]{1,0:T(8,128)(2,1)S(1)}, u32[]{:S(2)}, u32[]{:S(2)}) collective-permute-start(bf16[128,1024]{1,0:T(8,128)(2,1)S(1)} %get-tuple-element.81.refs_3_), channel_id=1, source_target_pairs={{0,1},{1,0},{2,3},{3,2},{4,5},{5,4},{6,7},{7,6},{8,9},{9,8},{10,11... | collective-permute-start | bytes 786440 | tf_op jit(solution)/shard_map/ppermute | solution.py:30
  81.2 14.7 %collective-permute-start.21 = (bf16[128,1024]{1,0:T(8,128)(2,1)S(1)}, bf16[128,1024]{1,0:T(8,128)(2,1)S(1)}, u32[]{:S(2)}, u32[]{:S(2)}) collective-permute-start(bf16[128,1024]{1,0:T(8,128)(2,1)S(1)} %get-tuple-element.81.refs_3_), channel_id=1, source_target_pairs={{4,0},{8,4},{12,8},{16,12},{20,16},{24,20},{28,24},{5,1},{9,5},{13... | collective-permute-start | bytes 786440 | tf_op jit(solution)/shard_map/ppermute | solution.py:36
  87.1 8.8 %collective-permute-start.20 = (bf16[128,1024]{1,0:T(8,128)(2,1)S(1)}, bf16[128,1024]{1,0:T(8,128)(2,1)S(1)}, u32[]{:S(2)}, u32[]{:S(2)}) collective-permute-start(bf16[128,1024]{1,0:T(8,128)(2,1)S(1)} %collective-permute-done.15.refs_5_), channel_id=1, source_target_pairs={{0,1},{1,0},{2,3},{3,2},{4,5},{5,4},{6,7},{7,6},{8,9},{9,8},{10,11... | collective-permute-start | bytes 786440 | tf_op jit(solution)/shard_map/ppermute | solution.py:30
  87.1 3.9 %collective-permute-start.16 = (f32[64,64]{1,0:T(8,128)S(1)}, f32[64,64]{1,0:T(8,128)S(1)}, u32[]{:S(2)}, u32[]{:S(2)}) collective-permute-start(f32[64,64]{1,0:T(8,128)S(1)} %add.49), channel_id=1, source_target_pairs={{0,2},{1,3},{2,0},{3,1},{4,6},{5,7},{6,4},{7,5},{8,10},{9,11},{10,... | collective-permute-start | bytes 49160 | tf_op jit(solution)/shard_map/ppermute | solution.py:530
  88.1 4.8 %collective-permute-start.17 = (f32[64,64]{1,0:T(8,128)S(1)}, f32[64,64]{1,0:T(8,128)S(1)}, u32[]{:S(2)}, u32[]{:S(2)}) collective-permute-start(f32[64,64]{1,0:T(8,128)S(1)} %add.49), channel_id=1, source_target_pairs={{0,4},{1,5},{2,6},{3,7},{4,0},{5,1},{6,2},{7,3},{8,12},{9,13},{10,... | collective-permute-start | bytes 49160 | tf_op jit(solution)/shard_map/ppermute | solution.py:530
  91.0 4.8 %collective-permute-start.18 = (f32[64,64]{1,0:T(8,128)S(1)}, f32[64,64]{1,0:T(8,128)S(1)}, u32[]{:S(2)}, u32[]{:S(2)}) collective-permute-start(f32[64,64]{1,0:T(8,128)S(1)} %add.49), channel_id=1, source_target_pairs={{0,6},{1,7},{2,4},{3,5},{4,2},{5,3},{6,0},{7,1},{8,14},{9,15},{10,... | collective-permute-start | bytes 49160 | tf_op jit(solution)/shard_map/ppermute | solution.py:530
  95.9 12.4 %collective-permute-start.22 = (f32[64,64]{1,0:T(8,128)S(1)}, f32[64,64]{1,0:T(8,128)S(1)}, u32[]{:S(2)}, u32[]{:S(2)}) collective-permute-start(f32[64,64]{1,0:T(8,128)S(1)} %add_add_fusion.3), channel_id=1, source_target_pairs={{0,8},{1,9},{2,10},{3,11},{4,12},{5,13},{6,14},{7,15},{8,0},{9,1},... | collective-permute-start | bytes 49160 | tf_op jit(solution)/shard_map/ppermute | solution.py:530
  97.7 10.6 %collective-permute-start.23 = (f32[64,64]{1,0:T(8,128)S(1)}, f32[64,64]{1,0:T(8,128)S(1)}, u32[]{:S(2)}, u32[]{:S(2)}) collective-permute-start(f32[64,64]{1,0:T(8,128)S(1)} %add_add_fusion.3), channel_id=1, source_target_pairs={{0,16},{1,17},{2,18},{3,19},{4,20},{5,21},{6,22},{7,23},{8,24},{9,... | collective-permute-start | bytes 49160 | tf_op jit(solution)/shard_map/ppermute | solution.py:530
  101.2 7.1 %collective-permute-start.24 = (f32[64,64]{1,0:T(8,128)S(1)}, f32[64,64]{1,0:T(8,128)S(1)}, u32[]{:S(2)}, u32[]{:S(2)}) collective-permute-start(f32[64,64]{1,0:T(8,128)S(1)} %add_add_fusion.3), channel_id=1, source_target_pairs={{0,24},{1,25},{2,26},{3,27},{4,28},{5,29},{6,30},{7,31},{8,16},{9,... | collective-permute-start | bytes 49160 | tf_op jit(solution)/shard_map/ppermute | solution.py:530
  108.3 3.2 %collective-permute-start.26 = (f32[4,64,512]{2,1,0:T(8,128)S(1)}, f32[4,64,512]{2,1,0:T(8,128)S(1)}, u32[]{:S(2)}, u32[]{:S(2)}) collective-permute-start(f32[4,64,512]{2,1,0:T(8,128)S(1)} %get-tuple-element.92), channel_id=1, source_target_pairs={{0,1},{1,0},{2,3},{3,2},{4,5},{5,4},{6,7},{7,6},{8,9},{9,8},{10,11... | collective-permute-start | bytes 1572872 | tf_op jit(solution)/shard_map/ppermute | solution.py:30
  108.4 9.1 %collective-permute-start.25 = (f32[2,64,512]{2,1,0:T(8,128)S(1)}, f32[2,64,512]{2,1,0:T(8,128)S(1)}, u32[]{:S(2)}, u32[]{:S(2)}) collective-permute-start(f32[2,64,512]{2,1,0:T(8,128)S(1)} %get-tuple-element.91), channel_id=1, source_target_pairs={{0,4},{4,8},{8,12},{12,16},{16,20},{20,24},{24,28},{1,5},{5,9},{9,... | collective-permute-start | bytes 786440 | tf_op jit(solution)/shard_map/ppermute | solution.py:36
  111.5 8.5 %collective-permute-start.27 = (f32[2,64,512]{2,1,0:T(8,128)S(1)}, f32[2,64,512]{2,1,0:T(8,128)S(1)}, u32[]{:S(2)}, u32[]{:S(2)}) collective-permute-start(f32[2,64,512]{2,1,0:T(8,128)S(1)} %slice_add_fusion.1), channel_id=1, source_target_pairs={{0,2},{1,3},{2,0},{3,1},{4,6},{5,7},{6,4},{7,5},{8,10},{9,11},{10,... | collective-permute-start | bytes 786440 | tf_op jit(solution)/shard_map/ppermute | solution.py:30
  121.5 1.3 collective-permute-start.28
  122.8 3.9 %collective-permute-start.29 = (f32[64,64]{1,0:T(8,128)S(1)}, f32[64,64]{1,0:T(8,128)S(1)}, u32[]{:S(2)}, u32[]{:S(2)}) collective-permute-start(f32[64,64]{1,0:T(8,128)S(1)} %add.57), channel_id=1, source_target_pairs={{0,2},{1,3},{2,0},{3,1},{4,6},{5,7},{6,4},{7,5},{8,10},{9,11},{10,... | collective-permute-start | bytes 49160 | tf_op jit(solution)/shard_map/ppermute | solution.py:530
  123.5 3.9 %collective-permute-start.30 = (f32[64,64]{1,0:T(8,128)S(1)}, f32[64,64]{1,0:T(8,128)S(1)}, u32[]{:S(2)}, u32[]{:S(2)}) collective-permute-start(f32[64,64]{1,0:T(8,128)S(1)} %add.57), channel_id=1, source_target_pairs={{0,4},{1,5},{2,6},{3,7},{4,0},{5,1},{6,2},{7,3},{8,12},{9,13},{10,... | collective-permute-start | bytes 49160 | tf_op jit(solution)/shard_map/ppermute | solution.py:530
  124.5 4.8 %collective-permute-start.31 = (f32[64,64]{1,0:T(8,128)S(1)}, f32[64,64]{1,0:T(8,128)S(1)}, u32[]{:S(2)}, u32[]{:S(2)}) collective-permute-start(f32[64,64]{1,0:T(8,128)S(1)} %add.57), channel_id=1, source_target_pairs={{0,6},{1,7},{2,4},{3,5},{4,2},{5,3},{6,0},{7,1},{8,14},{9,15},{10,... | collective-permute-start | bytes 49160 | tf_op jit(solution)/shard_map/ppermute | solution.py:530
  129.3 4.5 %collective-permute-start.32 = (f32[64,64]{1,0:T(8,128)S(1)}, f32[64,64]{1,0:T(8,128)S(1)}, u32[]{:S(2)}, u32[]{:S(2)}) collective-permute-start(f32[64,64]{1,0:T(8,128)S(1)} %add_add_fusion.1), channel_id=1, source_target_pairs={{0,8},{1,9},{2,10},{3,11},{4,12},{5,13},{6,14},{7,15},{8,0},{9,1},... | collective-permute-start | bytes 49160 | tf_op jit(solution)/shard_map/ppermute | solution.py:530
  129.4 4.9 %collective-permute-start.33 = (f32[64,64]{1,0:T(8,128)S(1)}, f32[64,64]{1,0:T(8,128)S(1)}, u32[]{:S(2)}, u32[]{:S(2)}) collective-permute-start(f32[64,64]{1,0:T(8,128)S(1)} %add_add_fusion.1), channel_id=1, source_target_pairs={{0,16},{1,17},{2,18},{3,19},{4,20},{5,21},{6,22},{7,23},{8,24},{9,... | collective-permute-start | bytes 49160 | tf_op jit(solution)/shard_map/ppermute | solution.py:530
  132.1 5.7 %collective-permute-start.34 = (f32[64,64]{1,0:T(8,128)S(1)}, f32[64,64]{1,0:T(8,128)S(1)}, u32[]{:S(2)}, u32[]{:S(2)}) collective-permute-start(f32[64,64]{1,0:T(8,128)S(1)} %add_add_fusion.1), channel_id=1, source_target_pairs={{0,24},{1,25},{2,26},{3,27},{4,28},{5,29},{6,30},{7,31},{8,16},{9,... | collective-permute-start | bytes 49160 | tf_op jit(solution)/shard_map/ppermute | solution.py:530

commit v7 on v6

--- a/solution.py
+++ b/solution.py
@@ -94,7 +94,9 @@
     return jnp.logical_or(near_by, jnp.logical_and(direct, first_half))
 
 
-def listing_kernel(group, cap, early_cap, blocks_dev, rows, cols, live, out_rows, out_cols, out_n):
+def listing_kernel(
+    group, cap, early_cap, blocks_dev, rows, cols, live, out_rows, out_cols, out_n, tiles, sources, targets, bounds
+):
     slab = blocks_dev * group
     slots = rows.shape[0]
     member = lax.axis_index("grp")
@@ -151,9 +153,39 @@
         return lax.fori_loop(0, slots, place, (jnp.int32(0), jnp.int32(0), filled))[2]
 
     early_count = place_those(True, jnp.int32(0))
+    count = place_those(False, early_count)
     out_n[0] = jnp.int32(0)
     out_n[1] = early_count
-    out_n[2] = place_those(False, early_count)
+    out_n[2] = count
+
+    home = min(2, group) * blocks_dev
+    bounds[0] = jnp.int32(0)
+    filled = jnp.int32(0)
+    for kind in range(3):
+        for to_row in (True, False):
+
+            def enter(index, filled):
+                source = (out_cols if to_row else out_rows)[index]
+                target = (out_rows if to_row else out_cols)[index]
+                if kind == 0:
+                    wanted = source < home
+                elif kind == 1:
+                    wanted = jnp.logical_and(source >= home, target >= blocks_dev)
+                else:
+                    wanted = jnp.logical_and(source >= home, target < blocks_dev)
+
+                @pl.when(wanted)
+                def _():
+                    tiles[filled] = jnp.where(
+                        index < early_count, index, early_cap + index - early_count
+                    )
+                    sources[filled] = source
+                    targets[filled] = target
+
+                return filled + jnp.where(wanted, 1, 0)
+
+            filled = lax.fori_loop(0, count, enter, filled)
+            bounds[2 * kind + (1 if to_row else 2)] = filled
 
 
 def listing(rows, cols, live, group, cap, early_cap, blocks_dev):
@@ -163,38 +195,17 @@
             jax.ShapeDtypeStruct((cap,), jnp.int32),
             jax.ShapeDtypeStruct((cap,), jnp.int32),
             jax.ShapeDtypeStruct((3,), jnp.int32),
+            jax.ShapeDtypeStruct((2 * cap,), jnp.int32),
+            jax.ShapeDtypeStruct((2 * cap,), jnp.int32),
+            jax.ShapeDtypeStruct((2 * cap,), jnp.int32),
+            jax.ShapeDtypeStruct((7,), jnp.int32),
         ),
         in_specs=[spec(SMEM)] * 3,
-        out_specs=(spec(SMEM),) * 3,
+        out_specs=(spec(SMEM),) * 7,
         cost_estimate=cost(2**20, 2**10),
         compiler_params=pltpu.CompilerParams(vmem_limit_bytes=2**20),
         name="listing",
     )(rows, cols, live)
-
-
-def message_rels(group):
-    groups = [[0]]
-    for bit in bits_of(group):
-        groups.append([rel for rel in range(group) if rel & bit and rel % bit == 0])
-    return groups
-
-
-def product_shapes(group, blocks_dev, height):
-    shapes = [
-        jax.ShapeDtypeStruct((len(rels) * blocks_dev, height, PTS), jnp.float32)
-        for rels in message_rels(group)
-    ]
-    shapes.append(jax.ShapeDtypeStruct((blocks_dev, height, PTS), jnp.float32))
-    return shapes
-
-
-def write_products(group, blocks_dev, acc, outs):
-    for rels, out in zip(message_rels(group), outs[:-1]):
-        for index, rel in enumerate(rels):
-            for block in range(blocks_dev):
-                out[index * blocks_dev + block] = acc[rel * blocks_dev + block]
-    for block in range(blocks_dev):
-        outs[-1][block] = acc[group * blocks_dev + block]
 
 
 def set_levels(place, window, level_row, level_col, scale):
@@ -216,7 +227,7 @@
         level_col[place] = jnp.broadcast_to(total, (PTS, 128))
 
 
-def make_tiles(low, high, rows, cols, window, level_row, level_col, kept, buffers):
+def make_tiles(low, high, rows, cols, window, level_row, level_col, kept, skip, buffers):
     width = window.shape[1]
     scale = 6.0 / width * LOG2E
     count = high - low
@@ -237,7 +248,7 @@
         right_level = level_row[col][0:1, :]
         left_level = jnp.concatenate([level_col[row]] * (PTS // 128), axis=1)
         value = jnp.exp2(buffer[...] * scale - left_level - right_level)
-        kept[jnp.where(valid, tile, spare)] = value.astype(jnp.bfloat16)
+        kept[jnp.where(valid, skip + tile, spare)] = value.astype(jnp.bfloat16)
 
     def body(pair, carry):
         cross(2 * pair, buffers[0])
@@ -249,7 +260,10 @@
     lax.fori_loop(0, jnp.where(count > 0, lax.div(count, 2) + 1, 0), body, 0)
 
 
-def build_tiles(stage, fresh, places, n, rows, cols, pts, levels, group, blocks_dev, cap, name):
+def build_tiles(
+    stage, fresh, places, n, rows, cols, pts, levels, before, group, blocks_dev, cap, name
+):
+    skip = before[0].shape[0] - 1 if before else 0
     width = pts[0].shape[1]
     total = (group + 1) * blocks_dev
     near = group * blocks_dev
@@ -257,13 +271,22 @@
         jax.ShapeDtypeStruct((total, 8, PTS), jnp.float32),
         jax.ShapeDtypeStruct((near, PTS, 128), jnp.float32),
     ]
-    shapes = [jax.ShapeDtypeStruct((cap + 1, PTS, PTS), jnp.bfloat16)] + level_shapes
+    shapes = [jax.ShapeDtypeStruct((skip + cap + 1, PTS, PTS), jnp.bfloat16)] + level_shapes
 
     def kernel(*refs):
         n_ref, row_ref, col_ref = refs[:3]
         pt_refs = refs[3 : 3 + len(pts)]
         level_refs = refs[3 + len(pts) : 3 + len(pts) + len(levels)]
-        kept, level_row, level_col, window, *buffers = refs[3 + len(pts) + len(levels) :]
+        before_refs = refs[3 + len(pts) + len(levels) : 3 + len(pts) + len(levels) + len(before)]
+        own_refs = refs[3 + len(pts) + len(levels) + len(before) :]
+        kept, level_row, level_col, window, left_buffer, right_buffer, *sems = own_refs
+        buffers = (left_buffer, right_buffer)
+        copies = [
+            pltpu.make_async_copy(ref.at[pl.ds(0, skip)], kept.at[pl.ds(0, skip)], sem)
+            for ref, sem in zip(before_refs, sems)
+        ]
+        for copy in copies:
+            copy.start()
         for place, piece in zip(places, pt_refs):
             window[place * PTS : place * PTS + piece.shape[0], :] = piece[...]
         for index, (place, piece) in enumerate(zip(places, pt_refs)):
@@ -285,27 +308,37 @@
             level_row,
             level_col,
             kept,
+            skip,
             buffers,
         )
+        for copy in copies:
+            copy.wait()
 
     return pl.pallas_call(
         kernel,
         out_shape=tuple(shapes),
-        in_specs=[spec(SMEM)] * 3 + [spec(VMEM)] * (len(pts) + len(levels)),
+        in_specs=[spec(SMEM)] * 3 + [spec(VMEM)] * (len(pts) + len(levels) + len(before)),
         out_specs=(spec(VMEM),) * len(shapes),
         scratch_shapes=[VMEM((total * PTS, width), jnp.bfloat16)]
-        + [VMEM((PTS, PTS), jnp.float32)] * 2,
+        + [VMEM((PTS, PTS), jnp.float32)] * 2
+        + [pltpu.SemaphoreType.DMA] * len(before),
         cost_estimate=cost(2**20 if stage == 0 else 2**32, 2**20),
         compiler_params=pltpu.CompilerParams(vmem_limit_bytes=14 * 2**20),
         name=name,
-    )(n, rows, cols, *pts, *levels)
-
-
-def products(n, rows, cols, vecs, tiles, group, blocks_dev, height, folds):
-    pieces = group + 1
-    places = pieces * blocks_dev
-    tall = vecs[0].shape[0]
-    shapes = product_shapes(group, blocks_dev, height)
+    )(n, rows, cols, *pts, *levels, *before)
+
+
+def products(entries, kinds, vecs, tiles, start, targets, height, folds):
+    firsts = sorted(vecs)
+    tall, held = vecs[firsts[0]].shape
+    blocks_dev = held // PTS
+    begun = sorted(start)
+    source_low, source_high = firsts[0], firsts[-1] + blocks_dev
+    low = min(first for first, _ in targets)
+    high = max(last for _, last in targets)
+    shapes = [
+        jax.ShapeDtypeStruct((last - first, height, PTS), jnp.float32) for first, last in targets
+    ]
 
     def fold(value):
         out = value[:height]
@@ -314,46 +347,87 @@
         return out
 
     def kernel(*refs):
-        n_ref, row_ref, col_ref = refs[:3]
-        vec_refs = refs[3 : 3 + pieces]
-        tile_refs = refs[3 + pieces : 3 + pieces + len(tiles)]
-        outs = refs[3 + pieces + len(tiles) : -2]
+        tile_ref, source_ref, target_ref, bounds = refs[:4]
+        vec_refs = refs[4 : 4 + len(firsts)]
+        kept = refs[4 + len(firsts)]
+        start_refs = refs[5 + len(firsts) : 5 + len(firsts) + len(begun)]
+        outs = refs[5 + len(firsts) + len(begun) : -2]
         u_win, acc = refs[-2:]
-        for piece in range(pieces):
+        for first, ref in zip(firsts, vec_refs):
             for block in range(blocks_dev):
                 lanes = slice(block * PTS, (block + 1) * PTS)
-                u_win[piece * blocks_dev + block] = vec_refs[piece][:, lanes]
-                acc[piece * blocks_dev + block] = jnp.zeros((height, PTS), jnp.float32)
-        for stage, kept in enumerate(tile_refs):
-            low = n_ref[stage]
-
-            def body(index, carry):
-                row, col = row_ref[index], col_ref[index]
-                tile = kept[index - low]
-                to_row = lax.dot_general(
-                    u_win[col], tile, (((1,), (1,)), ((), ())), preferred_element_type=jnp.float32
-                )
-                acc[row] += fold(to_row)
-                to_col = jnp.dot(u_win[row], tile, preferred_element_type=jnp.float32)
-                acc[col] += fold(to_col)
-                return carry
-
-            lax.fori_loop(low, n_ref[stage + 1], body, 0)
-        write_products(group, blocks_dev, acc, outs)
+                u_win[first - source_low + block] = ref[:, lanes]
+        if begun:
+            for first, ref in zip(begun, start_refs):
+                acc[first - low : first - low + ref.shape[0]] = ref[...]
+        else:
+            for place in range(high - low):
+                acc[place] = jnp.zeros((height, PTS), jnp.float32)
+
+        def to_row(index, carry):
+            value = lax.dot_general(
+                u_win[source_ref[index] - source_low],
+                kept[tile_ref[index]],
+                (((1,), (1,)), ((), ())),
+                preferred_element_type=jnp.float32,
+            )
+            acc[target_ref[index] - low] += fold(value)
+            return carry
+
+        def to_col(index, carry):
+            value = jnp.dot(
+                u_win[source_ref[index] - source_low],
+                kept[tile_ref[index]],
+                preferred_element_type=jnp.float32,
+            )
+            acc[target_ref[index] - low] += fold(value)
+            return carry
+
+        for kind in kinds:
+            lax.fori_loop(bounds[2 * kind], bounds[2 * kind + 1], to_row, 0)
+            lax.fori_loop(bounds[2 * kind + 1], bounds[2 * kind + 2], to_col, 0)
+        for (first, last), out in zip(targets, outs):
+            out[...] = acc[first - low : last - low]
 
     return pl.pallas_call(
         kernel,
-        out_shape=tuple(shapes),
-        in_specs=[spec(SMEM)] * 3 + [spec(VMEM)] * (pieces + len(tiles)),
-        out_specs=(spec(VMEM),) * len(shapes),
+        out_shape=shapes,
+        in_specs=[spec(SMEM)] * 4 + [spec(VMEM)] * (len(firsts) + 1 + len(begun)),
+        out_specs=[spec(VMEM)] * len(shapes),
         scratch_shapes=[
-            VMEM((places, tall, PTS), jnp.bfloat16),
-            VMEM((places, height, PTS), jnp.float32),
+            VMEM((source_high - source_low, tall, PTS), jnp.bfloat16),
+            VMEM((high - low, height, PTS), jnp.float32),
         ],
-        cost_estimate=cost(2**32, 2**24),
+        cost_estimate=cost(2**31 if kinds == (1,) else 2**20, 2**20),
         compiler_params=pltpu.CompilerParams(vmem_limit_bytes=10 * 2**20),
         name="products",
-    )(n, rows, cols, *vecs, *tiles)
+    )(*entries, *[vecs[first] for first in firsts], tiles, *[start[first] for first in begun])
+
+
+def urgent_ranges(group, blocks_dev):
+    return [(rel * blocks_dev, (rel + 1) * blocks_dev) for rel in range(1, group + 1)]
+
+
+def send_urgent(results, at_home, group):
+    final = [from_behind(results[-1], "blk", 1)]
+    parts = {rel: value for rel, value in zip(range(1, group), results)}
+    for bit in bits_of(group):
+        for rel in reversed([rel for rel in parts if rel & bit and rel % bit == 0]):
+            value = parts.pop(rel)
+            if bit > 1:
+                value, at_home = lax.optimization_barrier((value, at_home))
+            got = swap(value, "grp", bit)
+            if rel ^ bit:
+                parts[rel ^ bit] = parts[rel ^ bit] + got
+            else:
+                final.append(got)
+    return final, at_home
+
+
+def finish_home(entries, vecs, tiles, start, blocks_dev, height, folds):
+    return list(
+        products(entries, (2,), vecs, tiles, start, [(0, blocks_dev)], height, folds)
+    )
 
 
 def scaled_gram(parts, own, counts, degree, inverse, split):
@@ -495,36 +569,15 @@
     )(gram, z)
 
 
-def sum_products(messages, group, blocks_dev):
-    rels = message_rels(group)
-    parts = {}
-    for names, message in zip(rels[1:], messages[1:-1]):
-        for index, rel in enumerate(names):
-            parts[rel] = [message[index * blocks_dev : (index + 1) * blocks_dev]]
-    final = [messages[0], from_behind(messages[-1], "blk", 1)]
-    for bit, names, message in zip(bits_of(group), rels[1:], messages[1:-1]):
-        if bit > 1:
-            message = jnp.concatenate([sum(parts[rel][1:], parts[rel][0]) for rel in names], 0)
-        got = swap(message, "grp", bit)
-        for index, rel in enumerate(names):
-            target = rel ^ bit
-            if target == 0:
-                final.append(got)
-            else:
-                parts[target].append(got[index * blocks_dev : (index + 1) * blocks_dev])
-    return final
-
-
 def sum_stages():
-    bits = bits_of(lax.axis_size("blk") * lax.axis_size("grp"))
-    return [bits[:1]] + [bits[first : first + 2] for first in range(1, len(bits), 2)]
+    return bits_of(lax.axis_size("blk") * lax.axis_size("grp"))
 
 
 def all_sum(value, stages):
     count = lax.axis_size("blk") * lax.axis_size("grp")
     for bits in stages:
         moves = [0]
-        for bit in bits:
+        for bit in bits if isinstance(bits, list) else [bits]:
             moves += [move ^ bit for move in moves]
         terms = [value] + [
             lax.ppermute(value, ("blk", "grp"), [(source, source ^ move) for source in range(count)])
@@ -545,7 +598,11 @@
     early_cap = cap // 2
     half = (blocks_dev // 2) * PTS
 
-    rows, cols, n = listing(pair_rows, pair_cols, pair_live, group, cap, early_cap, blocks_dev)
+    home = min(2, group) * blocks_dev
+
+    rows, cols, n, *entries = listing(
+        pair_rows, pair_cols, pair_live, group, cap, early_cap, blocks_dev
+    )
     mate = swap(points, "grp", 1)
     chunks = [points[:half], points[half:]]
     far = [from_behind(chunk, "blk", -1) for chunk in chunks]
@@ -573,53 +630,91 @@
             for rel, value in crossed[index].items()
         ]
 
-    def tiles_of(stage, fresh, pieces, levels, size, name):
+    def tiles_of(stage, fresh, pieces, levels, before, size, name):
         places, pts = zip(*pieces)
         return build_tiles(
-            stage, fresh, places, n, rows, cols, pts, levels, group, blocks_dev, size, name
+            stage, fresh, places, n, rows, cols, pts, levels, before, group, blocks_dev, size, name
         )
 
     early = [(0, points), (blocks_dev, mate)] + arrived(0)
-    early_kept, *levels = tiles_of(0, len(early), early, (), early_cap, "early_tiles")
-    tied = lax.optimization_barrier((far[1], levels[0], *crossed[1].values()))
-    far[1], levels[0] = tied[:2]
-    crossed[1] = dict(zip(crossed[1], tied[2:]))
-    late = passed_on(0) + arrived(1) + passed_on(1)
-    late_kept, _, _ = tiles_of(1, len(late), late + early, levels, cap, "late_tiles")
-    tied = lax.optimization_barrier((late_kept, *cross_vec.values()))
-    kept = (early_kept, tied[0])
+    early_kept, *levels = tiles_of(0, len(early), early, (), (), early_cap, "early_tiles")
+    passed = passed_on(0)
+    tied = lax.optimization_barrier(
+        (far[1], levels[0], mate_vec, *[value for _, value in passed], *crossed[1].values())
+    )
+    far[1], levels[0], mate_vec = tied[:3]
+    passed = [(place, value) for (place, _), value in zip(passed, tied[3:])]
+    crossed[1] = dict(zip(crossed[1], tied[3 + len(passed) :]))
+    late = passed_on(1)
+    late = passed + arrived(1) + late
+    kept, _, _ = tiles_of(1, len(late), late + early, levels, (early_kept,), cap, "late_tiles")
+
+    tied = lax.optimization_barrier((kept, *cross_vec.values()))
+    kept = tied[0]
     cross_vec = dict(zip(cross_vec, tied[1:]))
 
-    vecs = {0: vec, 1: mate_vec}
-    for rel, value in cross_vec.items():
-        vecs[rel] = value
-        vecs[rel ^ 1] = swap(value, "grp", 1)
-    vecs = [vecs[rel] for rel in range(group)] + [far_vec]
-    messages = products(n, rows, cols, vecs, kept, group, blocks_dev, columns + 8, 1)
-    z, gram, parts, degree = scaled_gram(
-        sum_products(messages, group, blocks_dev), vec, counts, None, None, True
+    def window_of(own, mate, crossed, far):
+        found = {0: own, blocks_dev: mate, group * blocks_dev: far}
+        for rel, value in crossed.items():
+            found[rel * blocks_dev] = value
+            found[(rel ^ 1) * blocks_dev] = swap(value, "grp", 1)
+        return found
+
+    def beyond(vecs):
+        return {place: value for place, value in vecs.items() if place >= home}
+
+    vecs = window_of(vec, mate_vec, cross_vec, far_vec)
+    urgent = urgent_ranges(group, blocks_dev)
+    height = columns + 8
+    at_home, *results = products(
+        entries,
+        (0,),
+        {0: vec, blocks_dev: mate_vec},
+        kept,
+        {},
+        [(0, blocks_dev)] + urgent,
+        height,
+        1,
     )
+    begun = {first: value for (first, _), value in zip(urgent, results)}
+    results = products(entries, (1,), beyond(vecs), kept, begun, urgent, height, 1)
+    sums, at_home = send_urgent(results, at_home, group)
+    sums = finish_home(entries, beyond(vecs), kept, {0: at_home}, blocks_dev, height, 1) + sums
+    z, gram, parts, degree = scaled_gram(sums, vec, counts, None, None, True)
     for turn in range(1, ITERS):
         stages = sum_stages()
         far_part = from_behind(parts, "blk", -1)
         crossed = gather_far_bits(parts)
+        mate_part = swap(parts, "grp", 1)
+        at_home, *results = products(
+            entries,
+            (0,),
+            {0: parts, blocks_dev: mate_part},
+            kept,
+            {},
+            [(0, blocks_dev)] + urgent,
+            columns,
+            2,
+        )
         gram = all_sum(gram, stages[:1])
-        gram, *tied = lax.optimization_barrier((gram, *crossed.values()))
-        vecs = {0: parts, 1: swap(parts, "grp", 1)}
-        for rel, value in zip(crossed, tied):
-            vecs[rel] = value
-            vecs[rel ^ 1] = swap(value, "grp", 1)
-        vecs = [vecs[rel] for rel in range(group)] + [far_part]
+        gram, at_home, *tied = lax.optimization_barrier((gram, at_home, *crossed.values()))
+        crossed = dict(zip(crossed, tied))
+        vecs = beyond(window_of(parts, mate_part, crossed, far_part))
         gram = all_sum(gram, stages[1:2])
-        gram, *vecs = lax.optimization_barrier((gram, *vecs))
-        messages = products(n, rows, cols, vecs, kept, group, blocks_dev, columns, 2)
-        gram = all_sum(gram, stages[2:])
-        gram, *messages = lax.optimization_barrier((gram, *messages))
-        sums = sum_products(messages, group, blocks_dev)
-        inverse = factor(gram)
+        gram, *tied = lax.optimization_barrier((gram, *vecs.values()))
+        vecs = dict(zip(vecs, tied))
+        begun = {first: value for (first, _), value in zip(urgent, results)}
+        results = products(entries, (1,), vecs, kept, begun, urgent, columns, 2)
+        gram = all_sum(gram, stages[2:3])
+        gram, *results = lax.optimization_barrier((gram, *results))
+        sums, at_home = send_urgent(results, at_home, group)
+        sums = finish_home(entries, vecs, kept, {0: at_home}, blocks_dev, columns, 2) + sums
+        inverse = factor(all_sum(gram, stages[3:]))
         z, gram, *parts = scaled_gram(sums, z, counts, degree, inverse, turn + 1 < ITERS)
         parts = parts[0] if parts else None
-    return embedding(all_sum(gram, sum_stages()), z)
+    stages = sum_stages()
+    pairs = [stages[:1]] + [stages[first : first + 2] for first in range(1, len(stages), 2)]
+    return embedding(all_sum(gram, pairs), z)
 
 
 def solution(mesh):

time: 141 us -> 140 us (level)
  Pallas kernels: 46.1 us -> 53.8 us
  starting transfers between devices: 42.3 us -> 38.2 us
  waiting for transfers between devices: 49.8 us -> 45.8 us
    pallas_call x2 -> x6, Pallas kernels: 13.9 us -> 21.3 us  [products(): pl.pallas_call(kernel, out_shape=shapes, in_specs=[spec(SMEM)] * 4 + [spe...]
    ppermute x6, starting transfers between devices: 14.2 us -> 7.73 us  [from_behind(): lax.ppermute(value, axis, [(source, source + steps) for source in range(i...]
    ppermute x15 -> x17, waiting for transfers between devices: 10.6 us -> 5.42 us  [swap(): lax.ppermute(value, axis, [(source, source ^ bit) for source in range(cou...]
    ppermute x14 -> x12, waiting for transfers between devices: 12.5 us -> 17.2 us  [all_sum(): lax.ppermute(value, ('blk', 'grp'), [(source, source ^ move) for source i...]
    ppermute x6, waiting for transfers between devices: 26.7 us -> 23.1 us  [from_behind(): lax.ppermute(value, axis, [(source, source + steps) for source in range(i...]
    ppermute x15 -> x17, starting transfers between devices: 10.3 us -> 11.8 us  [swap(): lax.ppermute(value, axis, [(source, source ^ bit) for source in range(cou...]
    ppermute x14 -> x12, starting transfers between devices: 17.8 us -> 18.6 us  [all_sum(): lax.ppermute(value, ('blk', 'grp'), [(source, source ^ move) for source i...]
  transfers between devices with their start and end apart: 35 -> 35, of which waited for: 16 -> 14; matrix products, arithmetic and copies ran while one was open for 1% -> 1% of each run, Pallas kernels for 24% -> 31%
where the time goes in v7:
time: 140 us
  Pallas kernels  53.8 us (38%)
  waiting for transfers between devices  45.8 us (33%)
  starting transfers between devices  38.2 us (27%)
  local copies, waits for them, and re-layouts  1.52 us (1%)
    ppermute x6, waiting for transfers between devices, from_behind(): lax.ppermute(value, axis, [(source, source + steps) for source in range(i...  23.1 us
    pallas_call x6, Pallas kernels, products(): pl.pallas_call(kernel, out_shape=shapes, in_specs=[spec(SMEM)] * 4 + [spe...  21.3 us
    ppermute x12, starting transfers between devices, all_sum(): lax.ppermute(value, ('blk', 'grp'), [(source, source ^ move) for source i...  18.6 us
    ppermute x12, waiting for transfers between devices, all_sum(): lax.ppermute(value, ('blk', 'grp'), [(source, source ^ move) for source i...  17.2 us
    pallas_call x2, Pallas kernels, build_tiles(): pl.pallas_call(kernel, out_shape=tuple(shapes), in_specs=[spec(SMEM)] * 3...  16.1 us
    ppermute x17, starting transfers between devices, swap(): lax.ppermute(value, axis, [(source, source ^ bit) for source in range(cou...  11.8 us
    pallas_call x1, Pallas kernels, listing(): pl.pallas_call(functools.partial(listing_kernel, group, cap, early_cap, b...  8.38 us
    ppermute x6, starting transfers between devices, from_behind(): lax.ppermute(value, axis, [(source, source + steps) for source in range(i...  7.73 us
  transfers between devices with their start and end apart: 35, of which 14 were waited for; matrix products, arithmetic and copies ran while one was open for 1% of the time, Pallas kernels for 31%

profile of v7, /device:TPU:0, one launch (start us, length us, event | category | flops | bytes accessed | tf_op | source)
XLA Modules:
  0.0 140.4 jit_solution(5825287813645720147)
XLA Ops:
  0.0 0.5 collective-permute-start
  0.5 1.5 %fusion = (bf16[512,768]{1,0:T(8,128)(2,1)S(1)}, bf16[512,768]{1,0:T(8,128)(2,1)S(1)}) fusion(bf16[1024,768]{1,0:T(8,128)(2,1)} %refs_7_.1), kind=kLoop, calls=%fused_computation.2 | loop fusion | bytes 3145728 | tf_op jit(solution)/shard_map/slice | solution.py:607
  2.1 1.3 collective-permute-start.1
  3.4 2.7 %collective-permute-start.2 = (bf16[512,768]{1,0:T(8,128)(2,1)S(1)}, bf16[512,768]{1,0:T(8,128)(2,1)S(1)}, u32[]{:S(2)}, u32[]{:S(2)}) collective-permute-start(bf16[512,768]{1,0:T(8,128)(2,1)S(1)} %get-tuple-element.138), channel_id=1, source_target_pairs={{0,2},{1,3},{2,0},{3,1},{4,6},{5,7},{6,4},{7,5},{8,10},{9,11},{10,... | collective-permute-start | bytes 2359304 | tf_op jit(solution)/shard_map/ppermute | solution.py:30
  6.0 1.3 collective-permute-start.3
  7.3 0.1 collective-permute-start.6
  8.1 8.4 %listing.1 = (s32[16]{0:T(128)S(1)}, s32[16]{0:T(128)S(1)}, s32[3]{0:T(128)S(1)}, s32[32]{0:T(128)S(1)}, s32[32]{0:T(128)S(1)}, /*index=5*/s32[32]{0:T(128)S(1)}, s32[7]{0:T(128)S(1)}) custom-call(s32[64]{0:T(128)S(1)} %copy-done.3, s32[64]{0:T(128)S(1)} %copy-done.4, s32[1]{0:T(128)S(6)} %copy.7.live), custom_call_target="tpu_custom_call" | custom-call | flops 1048576 | bytes 1024 | tf_op jit(solution)/shard_map/listing/pallas_call | solution.py:192
  16.5 0.6 opening.1.refs_4_
  17.1 7.9 %collective-permute-done.1.refs_5_.refs_9_ = bf16[512,768]{1,0:T(8,128)(2,1)S(1)} collective-permute-done((bf16[512,768]{1,0:T(8,128)(2,1)S(1)}, bf16[512,768]{1,0:T(8,128)(2,1)S(1)}, u32[]{:S(2)}, u32[]{:S(2)}) %collective-permute-start.1) | collective-permute-done | bytes 786464 | tf_op jit(solution)/shard_map/ppermute | solution.py:36
  25.0 0.5 collective-permute-start.4
  25.5 5.8 %early_tiles.1 = (bf16[9,512,512]{2,1,0:T(8,128)(2,1)S(1)}, f32[10,8,512]{2,1,0:T(8,128)S(1)}, f32[8,512,128]{2,1,0:T(8,128)S(1)}) custom-call(s32[3]{0:T(128)S(1)} %get-tuple-element.79.refs_0_, s32[16]{0:T(128)S(1)} %get-tuple-element.80.refs_1_, s32[16]{0:T(128)S(1)} %get-tuple-element.81.refs_2_, bf16[1024,768]{1,0:T(8,128)(2,1)S(1)} %copy-done, ...), custom_call_target="tpu_custom_call" | custom-call | flops 1048576 | bytes 1048576 | tf_op jit(solution)/shard_map/early_tiles/pallas_call | solution.py:317
  31.2 10.3 %collective-permute-done.3.refs_4_ = bf16[512,768]{1,0:T(8,128)(2,1)S(1)} collective-permute-done((bf16[512,768]{1,0:T(8,128)(2,1)S(1)}, bf16[512,768]{1,0:T(8,128)(2,1)S(1)}, u32[]{:S(2)}, u32[]{:S(2)}) %collective-permute-start.3) | collective-permute-done | bytes 786464 | tf_op jit(solution)/shard_map/ppermute | solution.py:36
  41.5 0.0 collective-permute-done.6.refs_5_
  41.5 0.0 collective-permute-done.4.refs_5_
  41.5 0.0 collective-permute-done.5.refs_3_
  41.5 0.1 collective-permute-start.7
  41.6 1.8 %collective-permute-start.8 = (bf16[80,1024]{1,0:T(8,128)(2,1)S(1)}, bf16[80,1024]{1,0:T(8,128)(2,1)S(1)}, u32[]{:S(2)}, u32[]{:S(2)}) collective-permute-start(bf16[80,1024]{1,0:T(8,128)(2,1)S(1)} %opening.1.refs_4_), channel_id=1, source_target_pairs={{0,2},{1,3},{2,0},{3,1},{4,6},{5,7},{6,4},{7,5},{8,10},{9,11},{10,... | collective-permute-start | bytes 491528 | tf_op jit(solution)/shard_map/ppermute | solution.py:30
  43.4 1.3 collective-permute-start.10
  44.7 10.3 %late_tiles.1 = (bf16[25,512,512]{2,1,0:T(8,128)(2,1)S(1)}, f32[10,8,512]{2,1,0:T(8,128)}, f32[8,512,128]{2,1,0:T(8,128)}) custom-call(s32[3]{0:T(128)S(1)} %get-tuple-element.79.refs_0_, s32[16]{0:T(128)S(1)} %get-tuple-element.80.refs_1_, s32[16]{0:T(128)S(1)} %get-tuple-element.81.refs_2_, bf16[512,768]{1,0:T(8,128)(2,1)S(1)} %collective-permute-done.5.refs_3_, ...), custom_call_target="tpu_custom_call" | custom-call | flops 4294967296 | bytes 1048576 | tf_op jit(solution)/shard_map/late_tiles/pallas_call | solution.py:317
  55.0 0.0 collective-permute-done.8.refs_4_
  55.0 0.2 collective-permute-start.9
  55.3 3.5 %products.6 = (f32[2,72,512]{2,1,0:T(8,128)S(1)}, f32[2,72,512]{2,1,0:T(8,128)S(1)}, f32[2,72,512]{2,1,0:T(8,128)S(1)}, f32[2,72,512]{2,1,0:T(8,128)S(1)}, f32[2,72,512]{2,1,0:T(8,128)S(1)}) custom-call(s32[32]{0:T(128)S(1)} %get-tuple-element.71.refs_0_, s32[32]{0:T(128)S(1)} %get-tuple-element.72.refs_1_, s32[32]{0:T(128)S(1)} %get-tuple-element.73.refs_2_, ...), custom_call_target="tpu_custom_call" | custom-call | flops 1048576 | bytes 1048576 | tf_op jit(solution)/shard_map/products/pallas_call | solution.py:392
  58.8 4.6 %products.7 = (f32[2,72,512]{2,1,0:T(8,128)S(1)}, f32[2,72,512]{2,1,0:T(8,128)S(1)}, f32[2,72,512]{2,1,0:T(8,128)S(1)}, f32[2,72,512]{2,1,0:T(8,128)S(1)}) custom-call(s32[32]{0:T(128)S(1)} %get-tuple-element.71.refs_0_, s32[32]{0:T(128)S(1)} %get-tuple-element.72.refs_1_, s32[32]{0:T(128)S(1)} %get-tuple-element.73.refs_2_, ...), custom_call_target="tpu_custom_call" | custom-call | flops 2147483648 | bytes 1048576 | tf_op jit(solution)/shard_map/products/pallas_call | solution.py:392
  63.4 0.7 collective-permute-start.11
  64.1 1.3 collective-permute-start.12
  65.4 0.1 collective-permute-start.13
  65.6 1.1 collective-permute-start.14
  66.7 2.1 %products.8.refs_0_ = f32[2,72,512]{2,1,0:T(8,128)S(1)} custom-call(s32[32]{0:T(128)S(1)} %get-tuple-element.71.refs_0_, s32[32]{0:T(128)S(1)} %get-tuple-element.72.refs_1_, s32[32]{0:T(128)S(1)} %get-tuple-element.73.refs_2_, s32[7]{0:T(128)S(1)} %get-tuple-element.74.refs_3_, bf16[80,1024]{1,0:T(8,128)(2,1)S(1)} %collective-permute-done.8.refs_4_, ...), custom_call_target="tpu_custom_call" | custom-call | flops 1048576 | bytes 1048576 | tf_op jit(solution)/shard_map/products/pallas_call | solution.py:392
  68.8 3.4 %collective-permute-done.12.refs_1_ = f32[2,72,512]{2,1,0:T(8,128)S(1)} collective-permute-done((f32[2,72,512]{2,1,0:T(8,128)S(1)}, f32[2,72,512]{2,1,0:T(8,128)S(1)}, u32[]{:S(2)}, u32[]{:S(2)}) %collective-permute-start.12) | collective-permute-done | bytes 294944 | tf_op jit(solution)/shard_map/ppermute | solution.py:36
  72.1 2.9 %collective-permute-done.14.refs_3_ = f32[2,72,512]{2,1,0:T(8,128)S(1)} collective-permute-done((f32[2,72,512]{2,1,0:T(8,128)S(1)}, f32[2,72,512]{2,1,0:T(8,128)S(1)}, u32[]{:S(2)}, u32[]{:S(2)}) %collective-permute-start.14) | collective-permute-done | bytes 294944 | tf_op jit(solution)/shard_map/ppermute | solution.py:30
  75.0 1.0 scaled_gram.2
  76.0 0.1 collective-permute-start.16
  76.1 1.0 collective-permute-start.17
  77.1 0.2 collective-permute-start.15
  77.2 1.3 collective-permute-start.19
  78.5 3.8 %products.9 = (f32[2,64,512]{2,1,0:T(8,128)S(1)}, f32[2,64,512]{2,1,0:T(8,128)S(1)}, f32[2,64,512]{2,1,0:T(8,128)S(1)}, f32[2,64,512]{2,1,0:T(8,128)S(1)}, f32[2,64,512]{2,1,0:T(8,128)S(1)}) custom-call(s32[32]{0:T(128)S(1)} %get-tuple-element.71.refs_0_, s32[32]{0:T(128)S(1)} %get-tuple-element.72.refs_1_, s32[32]{0:T(128)S(1)} %get-tuple-element.73.refs_2_, ...), custom_call_target="tpu_custom_call" | custom-call | flops 1048576 | bytes 1048576 | tf_op jit(solution)/shard_map/products/pallas_call | solution.py:392
  82.3 2.5 %collective-permute-done.17.refs_4_ = bf16[128,1024]{1,0:T(8,128)(2,1)S(1)} collective-permute-done((bf16[128,1024]{1,0:T(8,128)(2,1)S(1)}, bf16[128,1024]{1,0:T(8,128)(2,1)S(1)}, u32[]{:S(2)}, u32[]{:S(2)}) %collective-permute-start.17) | collective-permute-done | bytes 262176 | tf_op jit(solution)/shard_map/ppermute | solution.py:30
  84.8 0.9 collective-permute-start.18
  85.7 3.0 %collective-permute-done.18 = f32[64,64]{1,0:T(8,128)S(1)} collective-permute-done((f32[64,64]{1,0:T(8,128)S(1)}, f32[64,64]{1,0:T(8,128)S(1)}, u32[]{:S(2)}, u32[]{:S(2)}) %collective-permute-start.18) | collective-permute-done | bytes 16416 | tf_op jit(solution)/shard_map/ppermute | solution.py:583
  88.7 1.6 %collective-permute-done.19.refs_6_ = bf16[128,1024]{1,0:T(8,128)(2,1)S(1)} collective-permute-done((bf16[128,1024]{1,0:T(8,128)(2,1)S(1)}, bf16[128,1024]{1,0:T(8,128)(2,1)S(1)}, u32[]{:S(2)}, u32[]{:S(2)}) %collective-permute-start.19) | collective-permute-done | bytes 262176 | tf_op jit(solution)/shard_map/ppermute | solution.py:36
  90.3 3.5 %collective-permute-start.21 = (f32[64,64]{1,0:T(8,128)S(1)}, f32[64,64]{1,0:T(8,128)S(1)}, u32[]{:S(2)}, u32[]{:S(2)}) collective-permute-start(f32[64,64]{1,0:T(8,128)S(1)} %add.44), channel_id=1, source_target_pairs={{0,4},{1,5},{2,6},{3,7},{4,0},{5,1},{6,2},{7,3},{8,12},{9,13},{10,... | collective-permute-start | bytes 49160 | tf_op jit(solution)/shard_map/ppermute | solution.py:583
  93.8 5.0 %products.10 = (f32[2,64,512]{2,1,0:T(8,128)S(1)}, f32[2,64,512]{2,1,0:T(8,128)S(1)}, f32[2,64,512]{2,1,0:T(8,128)S(1)}, f32[2,64,512]{2,1,0:T(8,128)S(1)}) custom-call(s32[32]{0:T(128)S(1)} %get-tuple-element.71.refs_0_, s32[32]{0:T(128)S(1)} %get-tuple-element.72.refs_1_, s32[32]{0:T(128)S(1)} %get-tuple-element.73.refs_2_, ...), custom_call_target="tpu_custom_call" | custom-call | flops 2147483648 | bytes 1048576 | tf_op jit(solution)/shard_map/products/pallas_call | solution.py:392
  98.8 0.1 collective-permute-start.22
  98.9 1.3 collective-permute-start.23
  100.2 0.6 collective-permute-start.24
  100.8 2.3 %collective-permute-start.25 = (f32[2,64,512]{2,1,0:T(8,128)S(1)}, f32[2,64,512]{2,1,0:T(8,128)S(1)}, u32[]{:S(2)}, u32[]{:S(2)}) collective-permute-start(f32[2,64,512]{2,1,0:T(8,128)S(1)} %add.46), channel_id=1, source_target_pairs={{0,2},{1,3},{2,0},{3,1},{4,6},{5,7},{6,4},{7,5},{8,10},{9,11},{10,... | collective-permute-start | bytes 786440 | tf_op jit(solution)/shard_map/ppermute | solution.py:30
  103.2 1.4 collective-permute-start.26
  104.5 2.5 %collective-permute-done.26 = f32[64,64]{1,0:T(8,128)S(1)} collective-permute-done((f32[64,64]{1,0:T(8,128)S(1)}, f32[64,64]{1,0:T(8,128)S(1)}, u32[]{:S(2)}, u32[]{:S(2)}) %collective-permute-start.26) | collective-permute-done | bytes 16416 | tf_op jit(solution)/shard_map/ppermute | solution.py:583
  107.1 1.5 %collective-permute-start.27 = (f32[64,64]{1,0:T(8,128)S(1)}, f32[64,64]{1,0:T(8,128)S(1)}, u32[]{:S(2)}, u32[]{:S(2)}) collective-permute-start(f32[64,64]{1,0:T(8,128)S(1)} %add.47), channel_id=1, source_target_pairs={{0,16},{1,17},{2,18},{3,19},{4,20},{5,21},{6,22},{7,23},{8,24},{9,... | collective-permute-start | bytes 49160 | tf_op jit(solution)/shard_map/ppermute | solution.py:583
  108.6 3.3 %collective-permute-done.27 = f32[64,64]{1,0:T(8,128)S(1)} collective-permute-done((f32[64,64]{1,0:T(8,128)S(1)}, f32[64,64]{1,0:T(8,128)S(1)}, u32[]{:S(2)}, u32[]{:S(2)}) %collective-permute-start.27) | collective-permute-done | bytes 16416 | tf_op jit(solution)/shard_map/ppermute | solution.py:583
  111.9 2.0 %factor.1.refs_6_ = f32[64,64]{1,0:T(8,128)S(1)} custom-call(f32[64,64]{1,0:T(8,128)S(1)} %add.48.gram), custom_call_target="tpu_custom_call" | custom-call | flops 2147483648 | bytes 65536 | tf_op jit(solution)/shard_map/factor/pallas_call | solution.py:543
  113.9 2.4 %products.11.refs_0_ = f32[2,64,512]{2,1,0:T(8,128)S(1)} custom-call(s32[32]{0:T(128)S(1)} %get-tuple-element.71.refs_0_, s32[32]{0:T(128)S(1)} %get-tuple-element.72.refs_1_, s32[32]{0:T(128)S(1)} %get-tuple-element.73.refs_2_, s32[7]{0:T(128)S(1)} %get-tuple-element.74.refs_3_, bf16[128,1024]{1,0:T(8,128)(2,1)S(1)} %collective-permute-done.17.refs_4_, ...), custom_call_target="tpu_custom_call" | custom-call | flops 1048576 | bytes 1048576 | tf_op jit(solution)/shard_map/products/pallas_call | solution.py:392
  116.3 1.5 %scaled_gram.3 = (f32[64,1024]{1,0:T(8,128)S(1)}, f32[64,64]{1,0:T(8,128)S(1)}) custom-call(s32[2]{0:T(128)S(1)} %copy-done.2, f32[2,64,512]{2,1,0:T(8,128)S(1)} %products.11.refs_0_, f32[2,64,512]{2,1,0:T(8,128)S(1)} %collective-permute-done.23.refs_1_, f32[2,64,512]{2,1,0:T(8,128)S(1)} %collective-permute-done.24.refs_2_, ...), custom_call_target="tpu_custom_call" | custom-call | flops 67108864 | bytes 2097152 | tf_op jit(solution)/shard_map/scaled_gram/pallas_call | solution.py:484
  117.8 0.1 collective-permute-start.28
  117.9 1.2 collective-permute-done.28
  119.1 3.1 %collective-permute-start.30 = (f32[64,64]{1,0:T(8,128)S(1)}, f32[64,64]{1,0:T(8,128)S(1)}, u32[]{:S(2)}, u32[]{:S(2)}) collective-permute-start(f32[64,64]{1,0:T(8,128)S(1)} %add.49), channel_id=1, source_target_pairs={{0,4},{1,5},{2,6},{3,7},{4,0},{5,1},{6,2},{7,3},{8,12},{9,13},{10,... | collective-permute-start | bytes 49160 | tf_op jit(solution)/shard_map/ppermute | solution.py:583
  122.2 1.5 %collective-permute-start.29 = (f32[64,64]{1,0:T(8,128)S(1)}, f32[64,64]{1,0:T(8,128)S(1)}, u32[]{:S(2)}, u32[]{:S(2)}) collective-permute-start(f32[64,64]{1,0:T(8,128)S(1)} %add.49), channel_id=1, source_target_pairs={{0,2},{1,3},{2,0},{3,1},{4,6},{5,7},{6,4},{7,5},{8,10},{9,11},{10,... | collective-permute-start | bytes 49160 | tf_op jit(solution)/shard_map/ppermute | solution.py:583
  123.7 0.4 collective-permute-done.30
  124.1 2.9 %collective-permute-done.31 = f32[64,64]{1,0:T(8,128)S(1)} collective-permute-done((f32[64,64]{1,0:T(8,128)S(1)}, f32[64,64]{1,0:T(8,128)S(1)}, u32[]{:S(2)}, u32[]{:S(2)}) %collective-permute-start.31) | collective-permute-done | bytes 16416 | tf_op jit(solution)/shard_map/ppermute | solution.py:583
  127.0 2.0 %collective-permute-start.33 = (f32[64,64]{1,0:T(8,128)S(1)}, f32[64,64]{1,0:T(8,128)S(1)}, u32[]{:S(2)}, u32[]{:S(2)}) collective-permute-start(f32[64,64]{1,0:T(8,128)S(1)} %add_add_fusion.1), channel_id=1, source_target_pairs={{0,16},{1,17},{2,18},{3,19},{4,20},{5,21},{6,22},{7,23},{8,24},{9,... | collective-permute-start | bytes 49160 | tf_op jit(solution)/shard_map/ppermute | solution.py:583
  129.0 4.5 %collective-permute-start.34 = (f32[64,64]{1,0:T(8,128)S(1)}, f32[64,64]{1,0:T(8,128)S(1)}, u32[]{:S(2)}, u32[]{:S(2)}) collective-permute-start(f32[64,64]{1,0:T(8,128)S(1)} %add_add_fusion.1), channel_id=1, source_target_pairs={{0,24},{1,25},{2,26},{3,27},{4,28},{5,29},{6,30},{7,31},{8,16},{9,... | collective-permute-start | bytes 49160 | tf_op jit(solution)/shard_map/ppermute | solution.py:583
  133.5 2.3 %collective-permute-done.34 = f32[64,64]{1,0:T(8,128)S(1)} collective-permute-done((f32[64,64]{1,0:T(8,128)S(1)}, f32[64,64]{1,0:T(8,128)S(1)}, u32[]{:S(2)}, u32[]{:S(2)}) %collective-permute-start.34) | collective-permute-done | bytes 16416 | tf_op jit(solution)/shard_map/ppermute | solution.py:583
  135.8 1.6 %collective-permute-done.32 = f32[64,64]{1,0:T(8,128)S(1)} collective-permute-done((f32[64,64]{1,0:T(8,128)S(1)}, f32[64,64]{1,0:T(8,128)S(1)}, u32[]{:S(2)}, u32[]{:S(2)}) %collective-permute-start.32) | collective-permute-done | bytes 16416 | tf_op jit(solution)/shard_map/ppermute | solution.py:583
  137.4 3.0 %embedding.1 = f32[64,1024]{1,0:T(8,128)} custom-call(f32[64,64]{1,0:T(8,128)S(1)} %add_add_fusion.gram, f32[64,1024]{1,0:T(8,128)S(1)} %get-tuple-element.136.z), custom_call_target="tpu_custom_call" | custom-call | flops 1073741824 | bytes 1048576 | tf_op jit(solution)/shard_map/embedding/pallas_call | solution.py:561
  (41 shorter events, 0.2 us)
Async XLA Ops:
  0.0 25.5 %copy-start = (bf16[1024,768]{1,0:T(8,128)(2,1)S(1)}, bf16[1024,768]{1,0:T(8,128)(2,1)}, u32[]{:S(2)}) copy-start(bf16[1024,768]{1,0:T(8,128)(2,1)} %refs_7_.1) | copy-start | bytes 4718596
  0.0 8.1 %copy-start.3 = (s32[64]{0:T(128)S(1)}, s32[64]{0:T(128)}, u32[]{:S(2)}) copy-start(s32[64]{0:T(128)} %rows.1) | copy-start | bytes 772
  0.0 8.1 %copy-start.4 = (s32[64]{0:T(128)S(1)}, s32[64]{0:T(128)}, u32[]{:S(2)}) copy-start(s32[64]{0:T(128)} %cols.1) | copy-start | bytes 772
  0.0 16.5 %copy-start.1 = (f32[64,1024]{1,0:T(8,128)S(1)}, f32[64,1024]{1,0:T(8,128)}, u32[]{:S(2)}) copy-start(f32[64,1024]{1,0:T(8,128)} %start) | copy-start | bytes 786436
  0.0 16.5 %copy-start.2 = (s32[2]{0:T(128)S(1)}, s32[2]{0:T(128)}, u32[]{:S(2)}) copy-start(s32[2]{0:T(128)} %count_ref.3) | copy-start | bytes 28
  0.0 16.4 %collective-permute-start = (bf16[1024,768]{1,0:T(8,128)(2,1)}, bf16[1024,768]{1,0:T(8,128)(2,1)S(1)}, u32[]{:S(2)}, u32[]{:S(2)}) collective-permute-start(bf16[1024,768]{1,0:T(8,128)(2,1)} %refs_7_.1), channel_id=1, source_target_pairs={{0,1},{1,0},{2,3},{3,2},{4,5},{5,4},{6,7},{7,6},{8,9},{9,8},{10,11... | collective-permute-start | bytes 4718600 | tf_op jit(solution)/shard_map/ppermute | solution.py:30
  2.1 22.9 %collective-permute-start.1 = (bf16[512,768]{1,0:T(8,128)(2,1)S(1)}, bf16[512,768]{1,0:T(8,128)(2,1)S(1)}, u32[]{:S(2)}, u32[]{:S(2)}) collective-permute-start(bf16[512,768]{1,0:T(8,128)(2,1)S(1)} %get-tuple-element.138), channel_id=1, source_target_pairs={{4,0},{8,4},{12,8},{16,12},{20,16},{24,20},{28,24},{5,1},{9,5},{13... | collective-permute-start | bytes 2359304 | tf_op jit(solution)/shard_map/ppermute | solution.py:36
  3.4 21.6 %collective-permute-start.2 = (bf16[512,768]{1,0:T(8,128)(2,1)S(1)}, bf16[512,768]{1,0:T(8,128)(2,1)S(1)}, u32[]{:S(2)}, u32[]{:S(2)}) collective-permute-start(bf16[512,768]{1,0:T(8,128)(2,1)S(1)} %get-tuple-element.138), channel_id=1, source_target_pairs={{0,2},{1,3},{2,0},{3,1},{4,6},{5,7},{6,4},{7,5},{8,10},{9,11},{10,... | collective-permute-start | bytes 2359304 | tf_op jit(solution)/shard_map/ppermute | solution.py:30
  6.0 35.5 %collective-permute-start.3 = (bf16[512,768]{1,0:T(8,128)(2,1)S(1)}, bf16[512,768]{1,0:T(8,128)(2,1)S(1)}, u32[]{:S(2)}, u32[]{:S(2)}) collective-permute-start(bf16[512,768]{1,0:T(8,128)(2,1)S(1)} %get-tuple-element.137), channel_id=1, source_target_pairs={{4,0},{8,4},{12,8},{16,12},{20,16},{24,20},{28,24},{5,1},{9,5},{13... | collective-permute-start | bytes 2359304 | tf_op jit(solution)/shard_map/ppermute | solution.py:36
  7.3 34.2 %collective-permute-start.6 = (bf16[512,768]{1,0:T(8,128)(2,1)S(1)}, bf16[512,768]{1,0:T(8,128)(2,1)S(1)}, u32[]{:S(2)}, u32[]{:S(2)}) collective-permute-start(bf16[512,768]{1,0:T(8,128)(2,1)S(1)} %get-tuple-element.137), channel_id=1, source_target_pairs={{0,2},{1,3},{2,0},{3,1},{4,6},{5,7},{6,4},{7,5},{8,10},{9,11},{10,... | collective-permute-start | bytes 2359304 | tf_op jit(solution)/shard_map/ppermute | solution.py:30
  25.0 16.6 %collective-permute-start.5 = (bf16[512,768]{1,0:T(8,128)(2,1)S(1)}, bf16[512,768]{1,0:T(8,128)(2,1)S(1)}, u32[]{:S(2)}, u32[]{:S(2)}) collective-permute-start(bf16[512,768]{1,0:T(8,128)(2,1)S(1)} %collective-permute-done.2.refs_6_.refs_10_), channel_id=1, source_target_pairs={{0,1},{1,0},{2,3},{3,2},{4,5},{5,4},{6,7},{7,6},{8,9},{9,8},{10,11... | collective-permute-start | bytes 2359304 | tf_op jit(solution)/shard_map/ppermute | solution.py:30
  25.0 16.5 %collective-permute-start.4 = (bf16[80,1024]{1,0:T(8,128)(2,1)S(1)}, bf16[80,1024]{1,0:T(8,128)(2,1)S(1)}, u32[]{:S(2)}, u32[]{:S(2)}) collective-permute-start(bf16[80,1024]{1,0:T(8,128)(2,1)S(1)} %opening.1.refs_4_), channel_id=1, source_target_pairs={{0,1},{1,0},{2,3},{3,2},{4,5},{5,4},{6,7},{7,6},{8,9},{9,8},{10,11... | collective-permute-start | bytes 491528 | tf_op jit(solution)/shard_map/ppermute | solution.py:30
  41.5 3.1 %collective-permute-start.7 = (bf16[512,768]{1,0:T(8,128)(2,1)S(1)}, bf16[512,768]{1,0:T(8,128)(2,1)S(1)}, u32[]{:S(2)}, u32[]{:S(2)}) collective-permute-start(bf16[512,768]{1,0:T(8,128)(2,1)S(1)} %collective-permute-done.6.refs_5_), channel_id=1, source_target_pairs={{0,1},{1,0},{2,3},{3,2},{4,5},{5,4},{6,7},{7,6},{8,9},{9,8},{10,11... | collective-permute-start | bytes 2359304 | tf_op jit(solution)/shard_map/ppermute | solution.py:30
  41.6 13.4 %collective-permute-start.8 = (bf16[80,1024]{1,0:T(8,128)(2,1)S(1)}, bf16[80,1024]{1,0:T(8,128)(2,1)S(1)}, u32[]{:S(2)}, u32[]{:S(2)}) collective-permute-start(bf16[80,1024]{1,0:T(8,128)(2,1)S(1)} %opening.1.refs_4_), channel_id=1, source_target_pairs={{0,2},{1,3},{2,0},{3,1},{4,6},{5,7},{6,4},{7,5},{8,10},{9,11},{10,... | collective-permute-start | bytes 491528 | tf_op jit(solution)/shard_map/ppermute | solution.py:30
  43.4 15.4 %collective-permute-start.10 = (bf16[80,1024]{1,0:T(8,128)(2,1)S(1)}, bf16[80,1024]{1,0:T(8,128)(2,1)S(1)}, u32[]{:S(2)}, u32[]{:S(2)}) collective-permute-start(bf16[80,1024]{1,0:T(8,128)(2,1)S(1)} %opening.1.refs_4_), channel_id=1, source_target_pairs={{4,0},{8,4},{12,8},{16,12},{20,16},{24,20},{28,24},{5,1},{9,5},{13... | collective-permute-start | bytes 491528 | tf_op jit(solution)/shard_map/ppermute | solution.py:36
  55.0 3.8 %collective-permute-start.9 = (bf16[80,1024]{1,0:T(8,128)(2,1)S(1)}, bf16[80,1024]{1,0:T(8,128)(2,1)S(1)}, u32[]{:S(2)}, u32[]{:S(2)}) collective-permute-start(bf16[80,1024]{1,0:T(8,128)(2,1)S(1)} %collective-permute-done.8.refs_4_), channel_id=1, source_target_pairs={{0,1},{1,0},{2,3},{3,2},{4,5},{5,4},{6,7},{7,6},{8,9},{9,8},{10,11... | collective-permute-start | bytes 491528 | tf_op jit(solution)/shard_map/ppermute | solution.py:30
  63.4 2.1 %collective-permute-start.11 = (f32[2,72,512]{2,1,0:T(8,128)S(1)}, f32[2,72,512]{2,1,0:T(8,128)S(1)}, u32[]{:S(2)}, u32[]{:S(2)}) collective-permute-start(f32[2,72,512]{2,1,0:T(8,128)S(1)} %get-tuple-element.102), channel_id=1, source_target_pairs={{0,1},{1,0},{2,3},{3,2},{4,5},{5,4},{6,7},{7,6},{8,9},{9,8},{10,11... | collective-permute-start | bytes 884744 | tf_op jit(solution)/shard_map/ppermute | solution.py:30
  64.1 8.0 %collective-permute-start.12 = (f32[2,72,512]{2,1,0:T(8,128)S(1)}, f32[2,72,512]{2,1,0:T(8,128)S(1)}, u32[]{:S(2)}, u32[]{:S(2)}) collective-permute-start(f32[2,72,512]{2,1,0:T(8,128)S(1)} %get-tuple-element.105), channel_id=1, source_target_pairs={{0,4},{4,8},{8,12},{12,16},{16,20},{20,24},{24,28},{1,5},{5,9},{9,... | collective-permute-start | bytes 884744 | tf_op jit(solution)/shard_map/ppermute | solution.py:36
  65.4 6.7 %collective-permute-start.13 = (f32[2,72,512]{2,1,0:T(8,128)S(1)}, f32[2,72,512]{2,1,0:T(8,128)S(1)}, u32[]{:S(2)}, u32[]{:S(2)}) collective-permute-start(f32[2,72,512]{2,1,0:T(8,128)S(1)} %get-tuple-element.106), channel_id=1, source_target_pairs={{0,1},{1,0},{2,3},{3,2},{4,5},{5,4},{6,7},{7,6},{8,9},{9,8},{10,11... | collective-permute-start | bytes 884744 | tf_op jit(solution)/shard_map/ppermute | solution.py:30
  65.6 9.5 %collective-permute-start.14 = (f32[2,72,512]{2,1,0:T(8,128)S(1)}, f32[2,72,512]{2,1,0:T(8,128)S(1)}, u32[]{:S(2)}, u32[]{:S(2)}) collective-permute-start(f32[2,72,512]{2,1,0:T(8,128)S(1)} %add.42), channel_id=1, source_target_pairs={{0,2},{1,3},{2,0},{3,1},{4,6},{5,7},{6,4},{7,5},{8,10},{9,11},{10,... | collective-permute-start | bytes 884744 | tf_op jit(solution)/shard_map/ppermute | solution.py:30
  76.0 2.5 %collective-permute-start.16 = (bf16[128,1024]{1,0:T(8,128)(2,1)S(1)}, bf16[128,1024]{1,0:T(8,128)(2,1)S(1)}, u32[]{:S(2)}, u32[]{:S(2)}) collective-permute-start(bf16[128,1024]{1,0:T(8,128)(2,1)S(1)} %get-tuple-element.109.refs_4_), channel_id=1, source_target_pairs={{0,1},{1,0},{2,3},{3,2},{4,5},{5,4},{6,7},{7,6},{8,9},{9,8},{10,11... | collective-permute-start | bytes 786440 | tf_op jit(solution)/shard_map/ppermute | solution.py:30
  76.1 8.7 %collective-permute-start.17 = (bf16[128,1024]{1,0:T(8,128)(2,1)S(1)}, bf16[128,1024]{1,0:T(8,128)(2,1)S(1)}, u32[]{:S(2)}, u32[]{:S(2)}) collective-permute-start(bf16[128,1024]{1,0:T(8,128)(2,1)S(1)} %get-tuple-element.109.refs_4_), channel_id=1, source_target_pairs={{0,2},{1,3},{2,0},{3,1},{4,6},{5,7},{6,4},{7,5},{8,10},{9,11},{10,... | collective-permute-start | bytes 786440 | tf_op jit(solution)/shard_map/ppermute | solution.py:30
  77.1 1.5 %collective-permute-start.15 = (f32[64,64]{1,0:T(8,128)S(1)}, f32[64,64]{1,0:T(8,128)S(1)}, u32[]{:S(2)}, u32[]{:S(2)}) collective-permute-start(f32[64,64]{1,0:T(8,128)S(1)} %get-tuple-element.108), channel_id=1, source_target_pairs={{0,1},{1,0},{2,3},{3,2},{4,5},{5,4},{6,7},{7,6},{8,9},{9,8},{10,11... | collective-permute-start | bytes 49160 | tf_op jit(solution)/shard_map/ppermute | solution.py:583
  77.2 13.1 %collective-permute-start.19 = (bf16[128,1024]{1,0:T(8,128)(2,1)S(1)}, bf16[128,1024]{1,0:T(8,128)(2,1)S(1)}, u32[]{:S(2)}, u32[]{:S(2)}) collective-permute-start(bf16[128,1024]{1,0:T(8,128)(2,1)S(1)} %get-tuple-element.109.refs_4_), channel_id=1, source_target_pairs={{4,0},{8,4},{12,8},{16,12},{20,16},{24,20},{28,24},{5,1},{9,5},{13... | collective-permute-start | bytes 786440 | tf_op jit(solution)/shard_map/ppermute | solution.py:36
  84.8 5.5 %collective-permute-start.20 = (bf16[128,1024]{1,0:T(8,128)(2,1)S(1)}, bf16[128,1024]{1,0:T(8,128)(2,1)S(1)}, u32[]{:S(2)}, u32[]{:S(2)}) collective-permute-start(bf16[128,1024]{1,0:T(8,128)(2,1)S(1)} %collective-permute-done.17.refs_4_), channel_id=1, source_target_pairs={{0,1},{1,0},{2,3},{3,2},{4,5},{5,4},{6,7},{7,6},{8,9},{9,8},{10,11... | collective-permute-start | bytes 786440 | tf_op jit(solution)/shard_map/ppermute | solution.py:30
  84.8 3.9 %collective-permute-start.18 = (f32[64,64]{1,0:T(8,128)S(1)}, f32[64,64]{1,0:T(8,128)S(1)}, u32[]{:S(2)}, u32[]{:S(2)}) collective-permute-start(f32[64,64]{1,0:T(8,128)S(1)} %add.43), channel_id=1, source_target_pairs={{0,2},{1,3},{2,0},{3,1},{4,6},{5,7},{6,4},{7,5},{8,10},{9,11},{10,... | collective-permute-start | bytes 49160 | tf_op jit(solution)/shard_map/ppermute | solution.py:583
  90.3 8.5 %collective-permute-start.21 = (f32[64,64]{1,0:T(8,128)S(1)}, f32[64,64]{1,0:T(8,128)S(1)}, u32[]{:S(2)}, u32[]{:S(2)}) collective-permute-start(f32[64,64]{1,0:T(8,128)S(1)} %add.44), channel_id=1, source_target_pairs={{0,4},{1,5},{2,6},{3,7},{4,0},{5,1},{6,2},{7,3},{8,12},{9,13},{10,... | collective-permute-start | bytes 49160 | tf_op jit(solution)/shard_map/ppermute | solution.py:583
  98.8 1.9 %collective-permute-start.22 = (f32[2,64,512]{2,1,0:T(8,128)S(1)}, f32[2,64,512]{2,1,0:T(8,128)S(1)}, u32[]{:S(2)}, u32[]{:S(2)}) collective-permute-start(f32[2,64,512]{2,1,0:T(8,128)S(1)} %get-tuple-element.126), channel_id=1, source_target_pairs={{0,1},{1,0},{2,3},{3,2},{4,5},{5,4},{6,7},{7,6},{8,9},{9,8},{10,11... | collective-permute-start | bytes 786440 | tf_op jit(solution)/shard_map/ppermute | solution.py:30
  98.9 17.4 %collective-permute-start.23 = (f32[2,64,512]{2,1,0:T(8,128)S(1)}, f32[2,64,512]{2,1,0:T(8,128)S(1)}, u32[]{:S(2)}, u32[]{:S(2)}) collective-permute-start(f32[2,64,512]{2,1,0:T(8,128)S(1)} %get-tuple-element.129), channel_id=1, source_target_pairs={{0,4},{4,8},{8,12},{12,16},{16,20},{20,24},{24,28},{1,5},{5,9},{9,... | collective-permute-start | bytes 786440 | tf_op jit(solution)/shard_map/ppermute | solution.py:36
  100.2 16.1 %collective-permute-start.24 = (f32[2,64,512]{2,1,0:T(8,128)S(1)}, f32[2,64,512]{2,1,0:T(8,128)S(1)}, u32[]{:S(2)}, u32[]{:S(2)}) collective-permute-start(f32[2,64,512]{2,1,0:T(8,128)S(1)} %get-tuple-element.130), channel_id=1, source_target_pairs={{0,1},{1,0},{2,3},{3,2},{4,5},{5,4},{6,7},{7,6},{8,9},{9,8},{10,11... | collective-permute-start | bytes 786440 | tf_op jit(solution)/shard_map/ppermute | solution.py:30
  100.8 15.5 %collective-permute-start.25 = (f32[2,64,512]{2,1,0:T(8,128)S(1)}, f32[2,64,512]{2,1,0:T(8,128)S(1)}, u32[]{:S(2)}, u32[]{:S(2)}) collective-permute-start(f32[2,64,512]{2,1,0:T(8,128)S(1)} %add.46), channel_id=1, source_target_pairs={{0,2},{1,3},{2,0},{3,1},{4,6},{5,7},{6,4},{7,5},{8,10},{9,11},{10,... | collective-permute-start | bytes 786440 | tf_op jit(solution)/shard_map/ppermute | solution.py:30
  103.2 3.9 %collective-permute-start.26 = (f32[64,64]{1,0:T(8,128)S(1)}, f32[64,64]{1,0:T(8,128)S(1)}, u32[]{:S(2)}, u32[]{:S(2)}) collective-permute-start(f32[64,64]{1,0:T(8,128)S(1)} %add.45), channel_id=1, source_target_pairs={{0,8},{1,9},{2,10},{3,11},{4,12},{5,13},{6,14},{7,15},{8,0},{9,1},... | collective-permute-start | bytes 49160 | tf_op jit(solution)/shard_map/ppermute | solution.py:583
  107.1 4.8 %collective-permute-start.27 = (f32[64,64]{1,0:T(8,128)S(1)}, f32[64,64]{1,0:T(8,128)S(1)}, u32[]{:S(2)}, u32[]{:S(2)}) collective-permute-start(f32[64,64]{1,0:T(8,128)S(1)} %add.47), channel_id=1, source_target_pairs={{0,16},{1,17},{2,18},{3,19},{4,20},{5,21},{6,22},{7,23},{8,24},{9,... | collective-permute-start | bytes 49160 | tf_op jit(solution)/shard_map/ppermute | solution.py:583
  117.8 1.3 collective-permute-start.28
  119.1 5.0 %collective-permute-start.30 = (f32[64,64]{1,0:T(8,128)S(1)}, f32[64,64]{1,0:T(8,128)S(1)}, u32[]{:S(2)}, u32[]{:S(2)}) collective-permute-start(f32[64,64]{1,0:T(8,128)S(1)} %add.49), channel_id=1, source_target_pairs={{0,4},{1,5},{2,6},{3,7},{4,0},{5,1},{6,2},{7,3},{8,12},{9,13},{10,... | collective-permute-start | bytes 49160 | tf_op jit(solution)/shard_map/ppermute | solution.py:583
  122.2 4.8 %collective-permute-start.31 = (f32[64,64]{1,0:T(8,128)S(1)}, f32[64,64]{1,0:T(8,128)S(1)}, u32[]{:S(2)}, u32[]{:S(2)}) collective-permute-start(f32[64,64]{1,0:T(8,128)S(1)} %add.49), channel_id=1, source_target_pairs={{0,6},{1,7},{2,4},{3,5},{4,2},{5,3},{6,0},{7,1},{8,14},{9,15},{10,... | collective-permute-start | bytes 49160 | tf_op jit(solution)/shard_map/ppermute | solution.py:583
  122.2 4.8 %collective-permute-start.29 = (f32[64,64]{1,0:T(8,128)S(1)}, f32[64,64]{1,0:T(8,128)S(1)}, u32[]{:S(2)}, u32[]{:S(2)}) collective-permute-start(f32[64,64]{1,0:T(8,128)S(1)} %add.49), channel_id=1, source_target_pairs={{0,2},{1,3},{2,0},{3,1},{4,6},{5,7},{6,4},{7,5},{8,10},{9,11},{10,... | collective-permute-start | bytes 49160 | tf_op jit(solution)/shard_map/ppermute | solution.py:583
  127.0 6.5 %collective-permute-start.33 = (f32[64,64]{1,0:T(8,128)S(1)}, f32[64,64]{1,0:T(8,128)S(1)}, u32[]{:S(2)}, u32[]{:S(2)}) collective-permute-start(f32[64,64]{1,0:T(8,128)S(1)} %add_add_fusion.1), channel_id=1, source_target_pairs={{0,16},{1,17},{2,18},{3,19},{4,20},{5,21},{6,22},{7,23},{8,24},{9,... | collective-permute-start | bytes 49160 | tf_op jit(solution)/shard_map/ppermute | solution.py:583
  129.0 6.8 %collective-permute-start.34 = (f32[64,64]{1,0:T(8,128)S(1)}, f32[64,64]{1,0:T(8,128)S(1)}, u32[]{:S(2)}, u32[]{:S(2)}) collective-permute-start(f32[64,64]{1,0:T(8,128)S(1)} %add_add_fusion.1), channel_id=1, source_target_pairs={{0,24},{1,25},{2,26},{3,27},{4,28},{5,29},{6,30},{7,31},{8,16},{9,... | collective-permute-start | bytes 49160 | tf_op jit(solution)/shard_map/ppermute | solution.py:583
  133.5 3.9 %collective-permute-start.32 = (f32[64,64]{1,0:T(8,128)S(1)}, f32[64,64]{1,0:T(8,128)S(1)}, u32[]{:S(2)}, u32[]{:S(2)}) collective-permute-start(f32[64,64]{1,0:T(8,128)S(1)} %add_add_fusion.1), channel_id=1, source_target_pairs={{0,8},{1,9},{2,10},{3,11},{4,12},{5,13},{6,14},{7,15},{8,0},{9,1},... | collective-permute-start | bytes 49160 | tf_op jit(solution)/shard_map/ppermute | solution.py:583

commit v8 on v7

--- a/solution.py
+++ b/solution.py
@@ -87,76 +87,100 @@
     )(start, counts)
 
 
-def is_early(place, group, blocks_dev):
-    near_by = place < min(2, group) * blocks_dev
-    direct = lax.rem(lax.div(place, blocks_dev), 2) == 0
+def stage_of(place, group, blocks_dev):
+    piece = lax.div(place, blocks_dev)
     first_half = lax.rem(place, blocks_dev) < blocks_dev // 2
-    return jnp.logical_or(near_by, jnp.logical_and(direct, first_half))
+    later = jnp.where(first_half, jnp.where(lax.rem(piece, 2) == 0, 0, 1), 2)
+    return jnp.where(piece < min(2, group), 0, later)
 
 
 def listing_kernel(
-    group, cap, early_cap, blocks_dev, rows, cols, live, out_rows, out_cols, out_n, tiles, sources, targets, bounds
+    group,
+    cap,
+    blocks_dev,
+    rows,
+    cols,
+    live,
+    out_rows,
+    out_cols,
+    out_n,
+    tiles,
+    sources,
+    targets,
+    bounds,
+    owners,
 ):
     slab = blocks_dev * group
     slots = rows.shape[0]
     member = lax.axis_index("grp")
 
-    def local_near(block):
-        return (lax.div(block, blocks_dev) ^ member) * blocks_dev + lax.rem(block, blocks_dev)
+    def local_near(block, device):
+        return (lax.div(block, blocks_dev) ^ device) * blocks_dev + lax.rem(block, blocks_dev)
+
+    def local_far(block):
+        return slab + lax.rem(block - slab, blocks_dev)
 
     def count_far(slot, carry):
         col = cols[slot]
         far = jnp.logical_and(slot < live[0], col >= slab)
         owner = lax.div(col - slab, blocks_dev)
+        owners[slot] = jnp.where(far, owner, -1)
         return tuple(
             old + jnp.where(jnp.logical_and(far, owner == device), 1, 0)
             for device, old in enumerate(carry)
         )
 
-    far_counts = lax.fori_loop(0, slots, count_far, (jnp.int32(0),) * group)
-    low = jnp.int32(0)
-    room = jnp.int32(0)
-    for device in range(group):
-        low = low + jnp.where(device < member, cap - far_counts[device], 0)
-        room = room + jnp.where(device == member, cap - far_counts[device], 0)
+    loads = lax.fori_loop(0, slots, count_far, (jnp.int32(0),) * group)
+
+    def give(slot, loads):
+        row, col = rows[slot], cols[slot]
+        near = jnp.logical_and(slot < live[0], col < slab)
+        best = jnp.int32(2**30)
+        owner = jnp.int32(0)
+        for device in range(group):
+            stage = jnp.maximum(
+                stage_of(local_near(row, device), group, blocks_dev),
+                stage_of(local_near(col, device), group, blocks_dev),
+            )
+            score = loads[device] + 64 * stage + jnp.where(loads[device] < cap, 0, 2**20)
+            owner = jnp.where(score < best, device, owner)
+            best = jnp.minimum(score, best)
+
+        @pl.when(near)
+        def _():
+            owners[slot] = owner
+
+        return tuple(
+            load + jnp.where(jnp.logical_and(near, owner == device), 1, 0)
+            for device, load in enumerate(loads)
+        )
+
+    lax.fori_loop(0, slots, give, loads)
 
     def place_those(wanted, filled):
-        def place(slot, carry):
-            near_rank, early_rank, filled = carry
+        def place(slot, filled):
             row, col = rows[slot], cols[slot]
-            used = slot < live[0]
-            far = col >= slab
-            mine_far = jnp.logical_and(far, lax.div(col - slab, blocks_dev) == member)
-            mine_near = jnp.logical_and(
-                jnp.logical_not(far), jnp.logical_and(near_rank >= low, near_rank < low + room)
+            row_place = local_near(row, member)
+            col_place = jnp.where(col >= slab, local_far(col), local_near(col, member))
+            stage = jnp.maximum(
+                stage_of(row_place, group, blocks_dev), stage_of(col_place, group, blocks_dev)
             )
-            row_place = local_near(row)
-            col_place = jnp.where(far, slab + lax.rem(col - slab, blocks_dev), local_near(col))
-            early = jnp.logical_and(
-                is_early(row_place, group, blocks_dev), is_early(col_place, group, blocks_dev)
-            )
-            mine = jnp.logical_and(used, jnp.logical_or(mine_far, mine_near))
-            early = jnp.logical_and(early, mine)
-            room_left = early_rank < early_cap
-            early_rank = early_rank + jnp.where(early, 1, 0)
-            early = jnp.logical_and(early, room_left)
-            mine = jnp.logical_and(mine, early if wanted else jnp.logical_not(early))
+            mine = jnp.logical_and(owners[slot] == member, stage == wanted)
 
             @pl.when(mine)
             def _():
                 out_rows[filled] = row_place
                 out_cols[filled] = col_place
 
-            near_rank = near_rank + jnp.where(jnp.logical_and(used, jnp.logical_not(far)), 1, 0)
-            return (near_rank, early_rank, filled + jnp.where(mine, 1, 0))
-
-        return lax.fori_loop(0, slots, place, (jnp.int32(0), jnp.int32(0), filled))[2]
-
-    early_count = place_those(True, jnp.int32(0))
-    count = place_those(False, early_count)
-    out_n[0] = jnp.int32(0)
-    out_n[1] = early_count
-    out_n[2] = count
+            return filled + jnp.where(mine, 1, 0)
+
+        return lax.fori_loop(0, slots, place, filled)
+
+    count = jnp.int32(0)
+    out_n[0] = count
+    for wanted in range(3):
+        count = place_those(wanted, count)
+        out_n[wanted + 1] = count
 
     home = min(2, group) * blocks_dev
     bounds[0] = jnp.int32(0)
@@ -176,9 +200,7 @@
 
                 @pl.when(wanted)
                 def _():
-                    tiles[filled] = jnp.where(
-                        index < early_count, index, early_cap + index - early_count
-                    )
+                    tiles[filled] = index
                     sources[filled] = source
                     targets[filled] = target
 
@@ -188,13 +210,13 @@
             bounds[2 * kind + (1 if to_row else 2)] = filled
 
 
-def listing(rows, cols, live, group, cap, early_cap, blocks_dev):
+def listing(rows, cols, live, group, cap, blocks_dev):
     return pl.pallas_call(
-        functools.partial(listing_kernel, group, cap, early_cap, blocks_dev),
+        functools.partial(listing_kernel, group, cap, blocks_dev),
         out_shape=(
             jax.ShapeDtypeStruct((cap,), jnp.int32),
             jax.ShapeDtypeStruct((cap,), jnp.int32),
-            jax.ShapeDtypeStruct((3,), jnp.int32),
+            jax.ShapeDtypeStruct((4,), jnp.int32),
             jax.ShapeDtypeStruct((2 * cap,), jnp.int32),
             jax.ShapeDtypeStruct((2 * cap,), jnp.int32),
             jax.ShapeDtypeStruct((2 * cap,), jnp.int32),
@@ -202,6 +224,7 @@
         ),
         in_specs=[spec(SMEM)] * 3,
         out_specs=(spec(SMEM),) * 7,
+        scratch_shapes=[SMEM((rows.shape[0],), jnp.int32)],
         cost_estimate=cost(2**20, 2**10),
         compiler_params=pltpu.CompilerParams(vmem_limit_bytes=2**20),
         name="listing",
@@ -227,7 +250,7 @@
         level_col[place] = jnp.broadcast_to(total, (PTS, 128))
 
 
-def make_tiles(low, high, rows, cols, window, level_row, level_col, kept, skip, buffers):
+def make_tiles(low, high, rows, cols, window, level_row, level_col, kept, buffers):
     width = window.shape[1]
     scale = 6.0 / width * LOG2E
     count = high - low
@@ -248,7 +271,7 @@
         right_level = level_row[col][0:1, :]
         left_level = jnp.concatenate([level_col[row]] * (PTS // 128), axis=1)
         value = jnp.exp2(buffer[...] * scale - left_level - right_level)
-        kept[jnp.where(valid, skip + tile, spare)] = value.astype(jnp.bfloat16)
+        kept[jnp.where(valid, index, spare)] = value.astype(jnp.bfloat16)
 
     def body(pair, carry):
         cross(2 * pair, buffers[0])
@@ -257,75 +280,65 @@
         finish(2 * pair, buffers[0])
         return carry
 
+    @pl.when(count > 0)
+    def _():
+        buffers[1][...] = jnp.zeros((PTS, PTS), jnp.float32)
+
     lax.fori_loop(0, jnp.where(count > 0, lax.div(count, 2) + 1, 0), body, 0)
 
 
-def build_tiles(
-    stage, fresh, places, n, rows, cols, pts, levels, before, group, blocks_dev, cap, name
-):
-    skip = before[0].shape[0] - 1 if before else 0
+def build_tiles(stage, fresh, n, rows, cols, state, group, blocks_dev, cap, name):
+    places = list(fresh)
+    pts = list(fresh.values())
     width = pts[0].shape[1]
     total = (group + 1) * blocks_dev
     near = group * blocks_dev
-    level_shapes = [
+    shapes = [
+        jax.ShapeDtypeStruct((total * PTS, width), jnp.bfloat16),
         jax.ShapeDtypeStruct((total, 8, PTS), jnp.float32),
         jax.ShapeDtypeStruct((near, PTS, 128), jnp.float32),
     ]
-    shapes = [jax.ShapeDtypeStruct((skip + cap + 1, PTS, PTS), jnp.bfloat16)] + level_shapes
+    makes = stage is not None
+    if makes:
+        shapes.append(jax.ShapeDtypeStruct((cap + 1, PTS, PTS), jnp.bfloat16))
+    state = state[: len(shapes)]
+    scalars = (n, rows, cols) if makes else ()
+    first = len(scalars) + len(pts)
 
     def kernel(*refs):
-        n_ref, row_ref, col_ref = refs[:3]
-        pt_refs = refs[3 : 3 + len(pts)]
-        level_refs = refs[3 + len(pts) : 3 + len(pts) + len(levels)]
-        before_refs = refs[3 + len(pts) + len(levels) : 3 + len(pts) + len(levels) + len(before)]
-        own_refs = refs[3 + len(pts) + len(levels) + len(before) :]
-        kept, level_row, level_col, window, left_buffer, right_buffer, *sems = own_refs
-        buffers = (left_buffer, right_buffer)
-        copies = [
-            pltpu.make_async_copy(ref.at[pl.ds(0, skip)], kept.at[pl.ds(0, skip)], sem)
-            for ref, sem in zip(before_refs, sems)
-        ]
-        for copy in copies:
-            copy.start()
+        pt_refs = refs[len(scalars) : first]
+        window, level_row, level_col, *rest = refs[first + len(state) :]
         for place, piece in zip(places, pt_refs):
-            window[place * PTS : place * PTS + piece.shape[0], :] = piece[...]
-        for index, (place, piece) in enumerate(zip(places, pt_refs)):
-            for block in range(place, place + piece.shape[0] // PTS):
-                if index < fresh:
-                    set_levels(block, window, level_row, level_col, 3.0 / width * LOG2E)
-                else:
-                    level_row[block] = level_refs[0][block]
-                    if block < near:
-                        level_col[block] = level_refs[1][block]
-        for buffer in buffers:
-            buffer[...] = jnp.zeros((PTS, PTS), jnp.float32)
-        make_tiles(
-            n_ref[stage],
-            n_ref[stage + 1],
-            row_ref,
-            col_ref,
-            window,
-            level_row,
-            level_col,
-            kept,
-            skip,
-            buffers,
-        )
-        for copy in copies:
-            copy.wait()
+            blocks = piece.shape[0] // PTS
+            window[place * PTS : (place + blocks) * PTS, :] = piece[...]
+            for block in range(place, place + blocks):
+                set_levels(block, window, level_row, level_col, 3.0 / width * LOG2E)
+        if makes:
+            n_ref, row_ref, col_ref = refs[:3]
+            kept, *buffers = rest
+            make_tiles(
+                n_ref[stage],
+                n_ref[stage + 1],
+                row_ref,
+                col_ref,
+                window,
+                level_row,
+                level_col,
+                kept,
+                buffers,
+            )
 
     return pl.pallas_call(
         kernel,
-        out_shape=tuple(shapes),
-        in_specs=[spec(SMEM)] * 3 + [spec(VMEM)] * (len(pts) + len(levels) + len(before)),
-        out_specs=(spec(VMEM),) * len(shapes),
-        scratch_shapes=[VMEM((total * PTS, width), jnp.bfloat16)]
-        + [VMEM((PTS, PTS), jnp.float32)] * 2
-        + [pltpu.SemaphoreType.DMA] * len(before),
-        cost_estimate=cost(2**20 if stage == 0 else 2**32, 2**20),
-        compiler_params=pltpu.CompilerParams(vmem_limit_bytes=14 * 2**20),
+        out_shape=shapes,
+        in_specs=[spec(SMEM)] * len(scalars) + [spec(VMEM)] * (len(pts) + len(state)),
+        out_specs=[spec(VMEM)] * len(shapes),
+        input_output_aliases={first + index: index for index in range(len(state))},
+        scratch_shapes=[VMEM((PTS, PTS), jnp.float32)] * (2 if makes else 0),
+        cost_estimate=cost(2**32 if stage == 2 else 2**20, 2**20),
+        compiler_params=pltpu.CompilerParams(vmem_limit_bytes=6 * 2**20),
         name=name,
-    )(n, rows, cols, *pts, *levels, *before)
+    )(*scalars, *pts, *state)
 
 
 def products(entries, kinds, vecs, tiles, start, targets, height, folds):
@@ -361,31 +374,40 @@
             for first, ref in zip(begun, start_refs):
                 acc[first - low : first - low + ref.shape[0]] = ref[...]
         else:
-            for place in range(high - low):
+            for place in range(high - low + 1):
                 acc[place] = jnp.zeros((height, PTS), jnp.float32)
 
-        def to_row(index, carry):
-            value = lax.dot_general(
-                u_win[source_ref[index] - source_low],
-                kept[tile_ref[index]],
-                (((1,), (1,)), ((), ())),
-                preferred_element_type=jnp.float32,
-            )
-            acc[target_ref[index] - low] += fold(value)
-            return carry
-
-        def to_col(index, carry):
-            value = jnp.dot(
-                u_win[source_ref[index] - source_low],
-                kept[tile_ref[index]],
-                preferred_element_type=jnp.float32,
-            )
-            acc[target_ref[index] - low] += fold(value)
-            return carry
+        spare = high - low
+        unroll = 4
+
+        def several(begin, end, transposed):
+            def body(step, carry):
+                done = []
+                for lane in range(unroll):
+                    index = begin + step * unroll + lane
+                    valid = index < end
+                    index = jnp.minimum(index, end - 1)
+                    vec = u_win[source_ref[index] - source_low]
+                    tile = kept[tile_ref[index]]
+                    if transposed:
+                        value = lax.dot_general(
+                            vec,
+                            tile,
+                            (((1,), (1,)), ((), ())),
+                            preferred_element_type=jnp.float32,
+                        )
+                    else:
+                        value = jnp.dot(vec, tile, preferred_element_type=jnp.float32)
+                    done.append((jnp.where(valid, target_ref[index] - low, spare), fold(value)))
+                for target, value in done:
+                    acc[target] += value
+                return carry
+
+            lax.fori_loop(0, lax.div(end - begin + unroll - 1, unroll), body, 0)
 
         for kind in kinds:
-            lax.fori_loop(bounds[2 * kind], bounds[2 * kind + 1], to_row, 0)
-            lax.fori_loop(bounds[2 * kind + 1], bounds[2 * kind + 2], to_col, 0)
+            several(bounds[2 * kind], bounds[2 * kind + 1], True)
+            several(bounds[2 * kind + 1], bounds[2 * kind + 2], False)
         for (first, last), out in zip(targets, outs):
             out[...] = acc[first - low : last - low]
 
@@ -396,7 +418,7 @@
         out_specs=[spec(VMEM)] * len(shapes),
         scratch_shapes=[
             VMEM((source_high - source_low, tall, PTS), jnp.bfloat16),
-            VMEM((high - low, height, PTS), jnp.float32),
+            VMEM((high - low + 1, height, PTS), jnp.float32),
         ],
         cost_estimate=cost(2**31 if kinds == (1,) else 2**20, 2**20),
         compiler_params=pltpu.CompilerParams(vmem_limit_bytes=10 * 2**20),
@@ -573,6 +595,10 @@
     return bits_of(lax.axis_size("blk") * lax.axis_size("grp"))
 
 
+def pairs_of(bits):
+    return [bits[first : first + 2] for first in range(0, len(bits), 2)]
+
+
 def all_sum(value, stages):
     count = lax.axis_size("blk") * lax.axis_size("grp")
     for bits in stages:
@@ -595,13 +621,12 @@
     columns = start.shape[0]
     slots = pair_rows.shape[0]
     cap = max(-(-slots // group), blocks_dev * blocks_dev * group)
-    early_cap = cap // 2
     half = (blocks_dev // 2) * PTS
 
     home = min(2, group) * blocks_dev
 
     rows, cols, n, *entries = listing(
-        pair_rows, pair_cols, pair_live, group, cap, early_cap, blocks_dev
+        pair_rows, pair_cols, pair_live, group, cap, blocks_dev
     )
     mate = swap(points, "grp", 1)
     chunks = [points[:half], points[half:]]
@@ -616,39 +641,35 @@
     far_vec = from_behind(vec, "blk", -1)
     mate_vec = swap(vec, "grp", 1)
 
-    def arrived(index):
+    def direct(index):
         offset = index * (blocks_dev // 2)
-        found = [(group * blocks_dev + offset, far[index])]
-        return found + [
-            (rel * blocks_dev + offset, value) for rel, value in crossed[index].items()
-        ]
+        found = {group * blocks_dev + offset: far[index]}
+        for rel, value in crossed[index].items():
+            found[rel * blocks_dev + offset] = value
+        return found
 
     def passed_on(index):
         offset = index * (blocks_dev // 2)
-        return [
-            ((rel ^ 1) * blocks_dev + offset, swap(value, "grp", 1))
+        return {
+            (rel ^ 1) * blocks_dev + offset: swap(value, "grp", 1)
             for rel, value in crossed[index].items()
-        ]
-
-    def tiles_of(stage, fresh, pieces, levels, before, size, name):
-        places, pts = zip(*pieces)
-        return build_tiles(
-            stage, fresh, places, n, rows, cols, pts, levels, before, group, blocks_dev, size, name
+        }
+
+    def build(stage, fresh, state, name):
+        return list(
+            build_tiles(stage, fresh, n, rows, cols, state, group, blocks_dev, cap, name)
         )
 
-    early = [(0, points), (blocks_dev, mate)] + arrived(0)
-    early_kept, *levels = tiles_of(0, len(early), early, (), (), early_cap, "early_tiles")
-    passed = passed_on(0)
-    tied = lax.optimization_barrier(
-        (far[1], levels[0], mate_vec, *[value for _, value in passed], *crossed[1].values())
-    )
-    far[1], levels[0], mate_vec = tied[:3]
-    passed = [(place, value) for (place, _), value in zip(passed, tied[3:])]
-    crossed[1] = dict(zip(crossed[1], tied[3 + len(passed) :]))
-    late = passed_on(1)
-    late = passed + arrived(1) + late
-    kept, _, _ = tiles_of(1, len(late), late + early, levels, (early_kept,), cap, "late_tiles")
-
+    state = build(0, {0: points, blocks_dev: mate, **direct(0)}, (), "first_tiles")
+    tied = lax.optimization_barrier((far[1], mate_vec, state[1], *crossed[1].values()))
+    far[1], mate_vec, state[1] = tied[:3]
+    crossed[1] = dict(zip(crossed[1], tied[3:]))
+    state = build(1, passed_on(0), state, "second_tiles")
+    last = passed_on(1)
+    *grown, kept = state
+    state = build(None, direct(1), grown, "more_blocks") + [kept]
+    state = build(2, last, state, "last_tiles")
+    kept = state[-1]
     tied = lax.optimization_barrier((kept, *cross_vec.values()))
     kept = tied[0]
     cross_vec = dict(zip(cross_vec, tied[1:]))
@@ -709,12 +730,11 @@
         gram, *results = lax.optimization_barrier((gram, *results))
         sums, at_home = send_urgent(results, at_home, group)
         sums = finish_home(entries, vecs, kept, {0: at_home}, blocks_dev, columns, 2) + sums
-        inverse = factor(all_sum(gram, stages[3:]))
+        inverse = factor(all_sum(gram, pairs_of(stages[3:])))
         z, gram, *parts = scaled_gram(sums, z, counts, degree, inverse, turn + 1 < ITERS)
         parts = parts[0] if parts else None
     stages = sum_stages()
-    pairs = [stages[:1]] + [stages[first : first + 2] for first in range(1, len(stages), 2)]
-    return embedding(all_sum(gram, pairs), z)
+    return embedding(all_sum(gram, stages[:1] + pairs_of(stages[1:])), z)
 
 
 def solution(mesh):

time: 140 us -> 132 us (0.943)
  waiting for transfers between devices: 45.8 us -> 32.5 us
  local copies, waits for them, and re-layouts: 1.52 us -> 5.79 us
    ppermute x6, waiting for transfers between devices: 23.1 us -> 11.2 us  [from_behind(): lax.ppermute(value, axis, [(source, source + steps) for source in range(i...]
    ppermute x6, starting transfers between devices: 7.73 us -> 15.4 us  [from_behind(): lax.ppermute(value, axis, [(source, source + steps) for source in range(i...]
    ppermute x12 -> x13, waiting for transfers between devices: 17.2 us -> 11 us  [all_sum(): lax.ppermute(value, ('blk', 'grp'), [(source, source ^ move) for source i...]
    pallas_call x3 -> x5, Pallas kernels: 24.5 us -> 30.5 us  [the longest x4 16.2 us: build_tiles(): pl.pallas_call(kernel, out_shape=shapes, in_specs=[spec(SMEM)] * len(scal...]
    pallas_call x6, Pallas kernels: 21.3 us -> 15.6 us  [products(): pl.pallas_call(kernel, out_shape=shapes, in_specs=[spec(SMEM)] * 4 + [spe...]
    ppermute x12 -> x13, starting transfers between devices: 18.6 us -> 13.2 us  [all_sum(): lax.ppermute(value, ('blk', 'grp'), [(source, source ^ move) for source i...]
    ppermute x17, waiting for transfers between devices: 5.42 us -> 10.3 us  [swap(): lax.ppermute(value, axis, [(source, source ^ bit) for source in range(cou...]
    unnamed x10 -> x12, local copies, waits for them, and re-layouts: 0.02 us -> 4.32 us
  transfers between devices with their start and end apart: 35 -> 36, of which waited for: 14 -> 14; matrix products, arithmetic and copies ran while one was open for 1% -> 1% of each run, Pallas kernels for 31% -> 35%
where the time goes in v8:
time: 132 us; the launch traced here: 131 us
  Pallas kernels  54.1 us (41%)
  starting transfers between devices  37.5 us (28%)
  waiting for transfers between devices  32.5 us (25%)
  local copies, waits for them, and re-layouts  5.79 us (4%)
    pallas_call x4, Pallas kernels, build_tiles(): pl.pallas_call(kernel, out_shape=shapes, in_specs=[spec(SMEM)] * len(scal...  16.2 us
    pallas_call x6, Pallas kernels, products(): pl.pallas_call(kernel, out_shape=shapes, in_specs=[spec(SMEM)] * 4 + [spe...  15.6 us
    ppermute x6, starting transfers between devices, from_behind(): lax.ppermute(value, axis, [(source, source + steps) for source in range(i...  15.4 us
    pallas_call x1, Pallas kernels, listing(): pl.pallas_call(functools.partial(listing_kernel, group, cap, blocks_dev),...  14.3 us
    ppermute x13, starting transfers between devices, all_sum(): lax.ppermute(value, ('blk', 'grp'), [(source, source ^ move) for source i...  13.2 us
    ppermute x6, waiting for transfers between devices, from_behind(): lax.ppermute(value, axis, [(source, source + steps) for source in range(i...  11.2 us
    ppermute x13, waiting for transfers between devices, all_sum(): lax.ppermute(value, ('blk', 'grp'), [(source, source ^ move) for source i...  11 us
    ppermute x17, waiting for transfers between devices, swap(): lax.ppermute(value, axis, [(source, source ^ bit) for source in range(cou...  10.3 us
  transfers between devices with their start and end apart: 36, of which 14 were waited for; matrix products, arithmetic and copies ran while one was open for 1% of the time, Pallas kernels for 35%

profile of v8, /device:TPU:0, one launch (start us, length us, event | category | flops | bytes accessed | tf_op | source)
XLA Modules:
  0.0 131.1 jit_solution(15691050765642789127)
XLA Ops:
  0.0 0.5 collective-permute-start
  0.5 1.5 %fusion = (bf16[512,768]{1,0:T(8,128)(2,1)S(1)}, bf16[512,768]{1,0:T(8,128)(2,1)S(1)}) fusion(bf16[1024,768]{1,0:T(8,128)(2,1)} %refs_3_.1), kind=kLoop, calls=%fused_computation.3 | loop fusion | bytes 3145728 | tf_op jit(solution)/shard_map/slice | solution.py:632
  1.9 1.3 collective-permute-start.1
  3.2 2.6 %collective-permute-start.2 = (bf16[512,768]{1,0:T(8,128)(2,1)S(1)}, bf16[512,768]{1,0:T(8,128)(2,1)S(1)}, u32[]{:S(2)}, u32[]{:S(2)}) collective-permute-start(bf16[512,768]{1,0:T(8,128)(2,1)S(1)} %get-tuple-element.152), channel_id=1, source_target_pairs={{0,2},{1,3},{2,0},{3,1},{4,6},{5,7},{6,4},{7,5},{8,10},{9,11},{10,... | collective-permute-start | bytes 2359304 | tf_op jit(solution)/shard_map/ppermute | solution.py:30
  5.8 1.3 collective-permute-start.3
  7.1 0.1 collective-permute-start.5
  7.8 0.6 copy-done.4
  8.5 0.7 copy-done.5
  9.1 14.3 %listing.1 = (s32[16]{0:T(128)S(1)}, s32[16]{0:T(128)S(1)}, s32[4]{0:T(128)S(1)}, s32[32]{0:T(128)S(1)}, s32[32]{0:T(128)S(1)}, /*index=5*/s32[32]{0:T(128)S(1)}, s32[7]{0:T(128)S(1)}) custom-call(s32[64]{0:T(128)S(1)} %copy-done.4, s32[64]{0:T(128)S(1)} %copy-done.5, s32[1]{0:T(128)S(6)} %copy.29.live), custom_call_target="tpu_custom_call" | custom-call | flops 1048576 | bytes 1024 | tf_op jit(solution)/shard_map/listing/pallas_call | solution.py:214
  23.4 0.9 copy-done.1
  24.4 0.7 copy-done.2
  25.0 0.6 opening.1.refs_4_
  25.6 0.3 collective-permute-start.4
  25.9 0.3 collective-permute-start.7
  26.2 1.4 %copy-done = bf16[1024,768]{1,0:T(8,128)(2,1)S(1)} copy-done((bf16[1024,768]{1,0:T(8,128)(2,1)S(1)}, bf16[1024,768]{1,0:T(8,128)(2,1)}, u32[]{:S(2)}) %copy-start) | copy-done | bytes 1572888
  27.6 8.0 %first_tiles.1 = (bf16[5120,768]{1,0:T(8,128)(2,1)S(1)}, f32[10,8,512]{2,1,0:T(8,128)S(1)}, f32[8,512,128]{2,1,0:T(8,128)S(1)}, bf16[17,512,512]{2,1,0:T(8,128)(2,1)S(1)}) custom-call(s32[4]{0:T(128)S(1)} %get-tuple-element.86.refs_0_, s32[16]{0:T(128)S(1)} %get-tuple-element.87.refs_1_, s32[16]{0:T(128)S(1)} %get-tuple-element.88.refs_2_, ...), custom_call_target="tpu_custom_call" | custom-call | flops 1048576 | bytes 1048576 | tf_op jit(solution)/shard_map/first_tiles/pallas_call | solution.py:331
  35.6 5.8 %collective-permute-done.3.refs_0_ = bf16[512,768]{1,0:T(8,128)(2,1)S(1)} collective-permute-done((bf16[512,768]{1,0:T(8,128)(2,1)S(1)}, bf16[512,768]{1,0:T(8,128)(2,1)S(1)}, u32[]{:S(2)}, u32[]{:S(2)}) %collective-permute-start.3) | collective-permute-done | bytes 786464 | tf_op jit(solution)/shard_map/ppermute | solution.py:36
  41.4 1.8 %collective-permute-start.8 = (bf16[80,1024]{1,0:T(8,128)(2,1)S(1)}, bf16[80,1024]{1,0:T(8,128)(2,1)S(1)}, u32[]{:S(2)}, u32[]{:S(2)}) collective-permute-start(bf16[80,1024]{1,0:T(8,128)(2,1)S(1)} %opening.1.refs_4_), channel_id=1, source_target_pairs={{0,2},{1,3},{2,0},{3,1},{4,6},{5,7},{6,4},{7,5},{8,10},{9,11},{10,... | collective-permute-start | bytes 491528 | tf_op jit(solution)/shard_map/ppermute | solution.py:30
  43.2 1.3 collective-permute-start.10
  44.5 2.1 %second_tiles.1 = (bf16[5120,768]{1,0:T(8,128)(2,1)S(1)}, f32[10,8,512]{2,1,0:T(8,128)S(1)}, f32[8,512,128]{2,1,0:T(8,128)S(1)}, bf16[17,512,512]{2,1,0:T(8,128)(2,1)S(1)}) custom-call(s32[4]{0:T(128)S(1)} %get-tuple-element.86.refs_0_, s32[16]{0:T(128)S(1)} %get-tuple-element.87.refs_1_, ...), custom_call_target="tpu_custom_call", output_to_operand_aliasing={{0}: (4, {}), {1}: (5, {}), {2}: (6, {}), {3}: (7, {})} | custom-call | flops 1048576 | bytes 1048576 | tf_op jit(solution)/shard_map/second_tiles/pallas_call | solution.py:331
  46.6 0.8 more_blocks.1
  47.4 5.4 %last_tiles.1 = (bf16[5120,768]{1,0:T(8,128)(2,1)S(1)}, f32[10,8,512]{2,1,0:T(8,128)S(1)}, f32[8,512,128]{2,1,0:T(8,128)S(1)}, bf16[17,512,512]{2,1,0:T(8,128)(2,1)S(1)}) custom-call(s32[4]{0:T(128)S(1)} %get-tuple-element.86.refs_0_, s32[16]{0:T(128)S(1)} %get-tuple-element.87.refs_1_, ...), custom_call_target="tpu_custom_call", output_to_operand_aliasing={{0}: (4, {}), {1}: (5, {}), {2}: (6, {}), {3}: (7, {})} | custom-call | flops 4294967296 | bytes 1048576 | tf_op jit(solution)/shard_map/last_tiles/pallas_call | solution.py:331
  52.8 0.2 collective-permute-start.9
  53.0 3.0 %products.6 = (f32[2,72,512]{2,1,0:T(8,128)S(1)}, f32[2,72,512]{2,1,0:T(8,128)S(1)}, f32[2,72,512]{2,1,0:T(8,128)S(1)}, f32[2,72,512]{2,1,0:T(8,128)S(1)}, f32[2,72,512]{2,1,0:T(8,128)S(1)}) custom-call(s32[32]{0:T(128)S(1)} %get-tuple-element.78.refs_0_, s32[32]{0:T(128)S(1)} %get-tuple-element.79.refs_1_, s32[32]{0:T(128)S(1)} %get-tuple-element.80.refs_2_, ...), custom_call_target="tpu_custom_call" | custom-call | flops 1048576 | bytes 1048576 | tf_op jit(solution)/shard_map/products/pallas_call | solution.py:414
  56.0 3.3 %products.7 = (f32[2,72,512]{2,1,0:T(8,128)S(1)}, f32[2,72,512]{2,1,0:T(8,128)S(1)}, f32[2,72,512]{2,1,0:T(8,128)S(1)}, f32[2,72,512]{2,1,0:T(8,128)S(1)}) custom-call(s32[32]{0:T(128)S(1)} %get-tuple-element.78.refs_0_, s32[32]{0:T(128)S(1)} %get-tuple-element.79.refs_1_, s32[32]{0:T(128)S(1)} %get-tuple-element.80.refs_2_, ...), custom_call_target="tpu_custom_call" | custom-call | flops 2147483648 | bytes 1048576 | tf_op jit(solution)/shard_map/products/pallas_call | solution.py:414
  59.3 1.2 collective-permute-start.11
  60.5 6.0 %collective-permute-start.12 = (f32[2,72,512]{2,1,0:T(8,128)S(1)}, f32[2,72,512]{2,1,0:T(8,128)S(1)}, u32[]{:S(2)}, u32[]{:S(2)}) collective-permute-start(f32[2,72,512]{2,1,0:T(8,128)S(1)} %get-tuple-element.119), channel_id=1, source_target_pairs={{0,4},{4,8},{8,12},{12,16},{16,20},{20,24},{24,28},{1,5},{5,9},{9,... | collective-permute-start | bytes 884744 | tf_op jit(solution)/shard_map/ppermute | solution.py:36
  66.7 0.6 collective-permute-start.14
  67.3 1.4 %products.8.refs_0_ = f32[2,72,512]{2,1,0:T(8,128)S(1)} custom-call(s32[32]{0:T(128)S(1)} %get-tuple-element.78.refs_0_, s32[32]{0:T(128)S(1)} %get-tuple-element.79.refs_1_, s32[32]{0:T(128)S(1)} %get-tuple-element.80.refs_2_, s32[7]{0:T(128)S(1)} %get-tuple-element.81.refs_3_, bf16[80,1024]{1,0:T(8,128)(2,1)S(1)} %collective-permute-done.8.refs_4_, ...), custom_call_target="tpu_custom_call" | custom-call | flops 1048576 | bytes 1048576 | tf_op jit(solution)/shard_map/products/pallas_call | solution.py:414
  68.7 4.3 %collective-permute-done.12.refs_1_ = f32[2,72,512]{2,1,0:T(8,128)S(1)} collective-permute-done((f32[2,72,512]{2,1,0:T(8,128)S(1)}, f32[2,72,512]{2,1,0:T(8,128)S(1)}, u32[]{:S(2)}, u32[]{:S(2)}) %collective-permute-start.12) | collective-permute-done | bytes 294944 | tf_op jit(solution)/shard_map/ppermute | solution.py:36
  73.0 3.2 %collective-permute-done.14.refs_3_ = f32[2,72,512]{2,1,0:T(8,128)S(1)} collective-permute-done((f32[2,72,512]{2,1,0:T(8,128)S(1)}, f32[2,72,512]{2,1,0:T(8,128)S(1)}, u32[]{:S(2)}, u32[]{:S(2)}) %collective-permute-start.14) | collective-permute-done | bytes 294944 | tf_op jit(solution)/shard_map/ppermute | solution.py:30
  76.2 1.0 scaled_gram.2
  77.2 0.6 collective-permute-start.17
  77.8 0.2 collective-permute-start.15
  78.0 1.3 collective-permute-start.19
  79.3 3.2 %products.9 = (f32[2,64,512]{2,1,0:T(8,128)S(1)}, f32[2,64,512]{2,1,0:T(8,128)S(1)}, f32[2,64,512]{2,1,0:T(8,128)S(1)}, f32[2,64,512]{2,1,0:T(8,128)S(1)}, f32[2,64,512]{2,1,0:T(8,128)S(1)}) custom-call(s32[32]{0:T(128)S(1)} %get-tuple-element.78.refs_0_, s32[32]{0:T(128)S(1)} %get-tuple-element.79.refs_1_, s32[32]{0:T(128)S(1)} %get-tuple-element.80.refs_2_, ...), custom_call_target="tpu_custom_call" | custom-call | flops 1048576 | bytes 1048576 | tf_op jit(solution)/shard_map/products/pallas_call | solution.py:414
  82.5 3.5 %collective-permute-done.17.refs_4_ = bf16[128,1024]{1,0:T(8,128)(2,1)S(1)} collective-permute-done((bf16[128,1024]{1,0:T(8,128)(2,1)S(1)}, bf16[128,1024]{1,0:T(8,128)(2,1)S(1)}, u32[]{:S(2)}, u32[]{:S(2)}) %collective-permute-start.17) | collective-permute-done | bytes 262176 | tf_op jit(solution)/shard_map/ppermute | solution.py:30
  85.9 0.5 collective-permute-start.18
  86.5 3.4 %collective-permute-done.18 = f32[64,64]{1,0:T(8,128)S(1)} collective-permute-done((f32[64,64]{1,0:T(8,128)S(1)}, f32[64,64]{1,0:T(8,128)S(1)}, u32[]{:S(2)}, u32[]{:S(2)}) %collective-permute-start.18) | collective-permute-done | bytes 16416 | tf_op jit(solution)/shard_map/ppermute | solution.py:609
  90.0 3.3 %products.10 = (f32[2,64,512]{2,1,0:T(8,128)S(1)}, f32[2,64,512]{2,1,0:T(8,128)S(1)}, f32[2,64,512]{2,1,0:T(8,128)S(1)}, f32[2,64,512]{2,1,0:T(8,128)S(1)}) custom-call(s32[32]{0:T(128)S(1)} %get-tuple-element.78.refs_0_, s32[32]{0:T(128)S(1)} %get-tuple-element.79.refs_1_, s32[32]{0:T(128)S(1)} %get-tuple-element.80.refs_2_, ...), custom_call_target="tpu_custom_call" | custom-call | flops 2147483648 | bytes 1048576 | tf_op jit(solution)/shard_map/products/pallas_call | solution.py:414
  93.3 0.6 collective-permute-done.21
  93.9 1.4 %collective-permute-start.26 = (f32[64,64]{1,0:T(8,128)S(1)}, f32[64,64]{1,0:T(8,128)S(1)}, u32[]{:S(2)}, u32[]{:S(2)}) collective-permute-start(f32[64,64]{1,0:T(8,128)S(1)} %add.48), channel_id=1, source_target_pairs={{0,8},{1,9},{2,10},{3,11},{4,12},{5,13},{6,14},{7,15},{8,0},{9,1},... | collective-permute-start | bytes 49160 | tf_op jit(solution)/shard_map/ppermute | solution.py:609
  95.3 1.1 collective-permute-start.27
  96.4 1.9 %collective-permute-start.28 = (f32[64,64]{1,0:T(8,128)S(1)}, f32[64,64]{1,0:T(8,128)S(1)}, u32[]{:S(2)}, u32[]{:S(2)}) collective-permute-start(f32[64,64]{1,0:T(8,128)S(1)} %add.48), channel_id=1, source_target_pairs={{0,24},{1,25},{2,26},{3,27},{4,28},{5,29},{6,30},{7,31},{8,16},{9,... | collective-permute-start | bytes 49160 | tf_op jit(solution)/shard_map/ppermute | solution.py:609
  98.3 4.2 %collective-permute-start.23 = (f32[2,64,512]{2,1,0:T(8,128)S(1)}, f32[2,64,512]{2,1,0:T(8,128)S(1)}, u32[]{:S(2)}, u32[]{:S(2)}) collective-permute-start(f32[2,64,512]{2,1,0:T(8,128)S(1)} %get-tuple-element.143), channel_id=1, source_target_pairs={{0,4},{4,8},{8,12},{12,16},{16,20},{20,24},{24,28},{1,5},{5,9},{9,... | collective-permute-start | bytes 786440 | tf_op jit(solution)/shard_map/ppermute | solution.py:36
  102.7 0.6 collective-permute-start.25
  103.3 2.0 %factor.1.refs_6_ = f32[64,64]{1,0:T(8,128)S(1)} custom-call(f32[64,64]{1,0:T(8,128)S(1)} %add_add_fusion.2.gram), custom_call_target="tpu_custom_call" | custom-call | flops 2147483648 | bytes 65536 | tf_op jit(solution)/shard_map/factor/pallas_call | solution.py:565
  105.3 1.5 %products.11.refs_0_ = f32[2,64,512]{2,1,0:T(8,128)S(1)} custom-call(s32[32]{0:T(128)S(1)} %get-tuple-element.78.refs_0_, s32[32]{0:T(128)S(1)} %get-tuple-element.79.refs_1_, s32[32]{0:T(128)S(1)} %get-tuple-element.80.refs_2_, s32[7]{0:T(128)S(1)} %get-tuple-element.81.refs_3_, bf16[128,1024]{1,0:T(8,128)(2,1)S(1)} %collective-permute-done.17.refs_4_, ...), custom_call_target="tpu_custom_call" | custom-call | flops 1048576 | bytes 1048576 | tf_op jit(solution)/shard_map/products/pallas_call | solution.py:414
  106.8 1.1 collective-permute-done.23.refs_1_
  107.9 3.6 %collective-permute-done.25.refs_3_ = f32[2,64,512]{2,1,0:T(8,128)S(1)} collective-permute-done((f32[2,64,512]{2,1,0:T(8,128)S(1)}, f32[2,64,512]{2,1,0:T(8,128)S(1)}, u32[]{:S(2)}, u32[]{:S(2)}) %collective-permute-start.25) | collective-permute-done | bytes 262176 | tf_op jit(solution)/shard_map/ppermute | solution.py:30
  111.5 1.5 %scaled_gram.3 = (f32[64,1024]{1,0:T(8,128)S(1)}, f32[64,64]{1,0:T(8,128)S(1)}) custom-call(s32[2]{0:T(128)S(1)} %copy-done.3, f32[2,64,512]{2,1,0:T(8,128)S(1)} %products.11.refs_0_, f32[2,64,512]{2,1,0:T(8,128)S(1)} %collective-permute-done.23.refs_1_, f32[2,64,512]{2,1,0:T(8,128)S(1)} %collective-permute-done.24.refs_2_, ...), custom_call_target="tpu_custom_call" | custom-call | flops 67108864 | bytes 2097152 | tf_op jit(solution)/shard_map/scaled_gram/pallas_call | solution.py:506
  113.0 1.2 collective-permute-done.29
  114.2 0.5 collective-permute-start.30
  114.8 0.3 collective-permute-start.31
  115.1 2.6 %collective-permute-start.32 = (f32[64,64]{1,0:T(8,128)S(1)}, f32[64,64]{1,0:T(8,128)S(1)}, u32[]{:S(2)}, u32[]{:S(2)}) collective-permute-start(f32[64,64]{1,0:T(8,128)S(1)} %add.53), channel_id=1, source_target_pairs={{0,6},{1,7},{2,4},{3,5},{4,2},{5,3},{6,0},{7,1},{8,14},{9,15},{10,... | collective-permute-start | bytes 49160 | tf_op jit(solution)/shard_map/ppermute | solution.py:609
  117.7 0.4 collective-permute-done.30
  118.2 0.7 collective-permute-done.31
  118.9 1.0 collective-permute-done.32
  119.9 1.9 %collective-permute-start.33 = (f32[64,64]{1,0:T(8,128)S(1)}, f32[64,64]{1,0:T(8,128)S(1)}, u32[]{:S(2)}, u32[]{:S(2)}) collective-permute-start(f32[64,64]{1,0:T(8,128)S(1)} %add_add_fusion.1), channel_id=1, source_target_pairs={{0,8},{1,9},{2,10},{3,11},{4,12},{5,13},{6,14},{7,15},{8,0},{9,1},... | collective-permute-start | bytes 49160 | tf_op jit(solution)/shard_map/ppermute | solution.py:609
  121.8 0.5 collective-permute-start.34
  122.3 2.0 %collective-permute-start.35 = (f32[64,64]{1,0:T(8,128)S(1)}, f32[64,64]{1,0:T(8,128)S(1)}, u32[]{:S(2)}, u32[]{:S(2)}) collective-permute-start(f32[64,64]{1,0:T(8,128)S(1)} %add_add_fusion.1), channel_id=1, source_target_pairs={{0,24},{1,25},{2,26},{3,27},{4,28},{5,29},{6,30},{7,31},{8,16},{9,... | collective-permute-start | bytes 49160 | tf_op jit(solution)/shard_map/ppermute | solution.py:609
  124.4 2.3 %collective-permute-done.34 = f32[64,64]{1,0:T(8,128)S(1)} collective-permute-done((f32[64,64]{1,0:T(8,128)S(1)}, f32[64,64]{1,0:T(8,128)S(1)}, u32[]{:S(2)}, u32[]{:S(2)}) %collective-permute-start.34) | collective-permute-done | bytes 16416 | tf_op jit(solution)/shard_map/ppermute | solution.py:609
  126.6 1.4 %collective-permute-done.35 = f32[64,64]{1,0:T(8,128)S(1)} collective-permute-done((f32[64,64]{1,0:T(8,128)S(1)}, f32[64,64]{1,0:T(8,128)S(1)}, u32[]{:S(2)}, u32[]{:S(2)}) %collective-permute-start.35) | collective-permute-done | bytes 16416 | tf_op jit(solution)/shard_map/ppermute | solution.py:609
  128.1 3.0 %embedding.1 = f32[64,1024]{1,0:T(8,128)} custom-call(f32[64,64]{1,0:T(8,128)S(1)} %add_add_fusion.gram, f32[64,1024]{1,0:T(8,128)S(1)} %get-tuple-element.150.z), custom_call_target="tpu_custom_call" | custom-call | flops 1073741824 | bytes 1048576 | tf_op jit(solution)/shard_map/embedding/pallas_call | solution.py:583
  (46 shorter events, 0.6 us)
Async XLA Ops:
  0.0 23.4 %collective-permute-start = (bf16[1024,768]{1,0:T(8,128)(2,1)}, bf16[1024,768]{1,0:T(8,128)(2,1)S(1)}, u32[]{:S(2)}, u32[]{:S(2)}) collective-permute-start(bf16[1024,768]{1,0:T(8,128)(2,1)} %refs_3_.1), channel_id=1, source_target_pairs={{0,1},{1,0},{2,3},{3,2},{4,5},{5,4},{6,7},{7,6},{8,9},{9,8},{10,11... | collective-permute-start | bytes 4718600 | tf_op jit(solution)/shard_map/ppermute | solution.py:30
  1.9 23.7 %collective-permute-start.1 = (bf16[512,768]{1,0:T(8,128)(2,1)S(1)}, bf16[512,768]{1,0:T(8,128)(2,1)S(1)}, u32[]{:S(2)}, u32[]{:S(2)}) collective-permute-start(bf16[512,768]{1,0:T(8,128)(2,1)S(1)} %get-tuple-element.152), channel_id=1, source_target_pairs={{4,0},{8,4},{12,8},{16,12},{20,16},{24,20},{28,24},{5,1},{9,5},{13... | collective-permute-start | bytes 2359304 | tf_op jit(solution)/shard_map/ppermute | solution.py:36
  3.2 22.4 %collective-permute-start.2 = (bf16[512,768]{1,0:T(8,128)(2,1)S(1)}, bf16[512,768]{1,0:T(8,128)(2,1)S(1)}, u32[]{:S(2)}, u32[]{:S(2)}) collective-permute-start(bf16[512,768]{1,0:T(8,128)(2,1)S(1)} %get-tuple-element.152), channel_id=1, source_target_pairs={{0,2},{1,3},{2,0},{3,1},{4,6},{5,7},{6,4},{7,5},{8,10},{9,11},{10,... | collective-permute-start | bytes 2359304 | tf_op jit(solution)/shard_map/ppermute | solution.py:30
  5.8 35.6 %collective-permute-start.3 = (bf16[512,768]{1,0:T(8,128)(2,1)S(1)}, bf16[512,768]{1,0:T(8,128)(2,1)S(1)}, u32[]{:S(2)}, u32[]{:S(2)}) collective-permute-start(bf16[512,768]{1,0:T(8,128)(2,1)S(1)} %get-tuple-element.151), channel_id=1, source_target_pairs={{4,0},{8,4},{12,8},{16,12},{20,16},{24,20},{28,24},{5,1},{9,5},{13... | collective-permute-start | bytes 2359304 | tf_op jit(solution)/shard_map/ppermute | solution.py:36
  7.1 34.3 %collective-permute-start.5 = (bf16[512,768]{1,0:T(8,128)(2,1)S(1)}, bf16[512,768]{1,0:T(8,128)(2,1)S(1)}, u32[]{:S(2)}, u32[]{:S(2)}) collective-permute-start(bf16[512,768]{1,0:T(8,128)(2,1)S(1)} %get-tuple-element.151), channel_id=1, source_target_pairs={{0,2},{1,3},{2,0},{3,1},{4,6},{5,7},{6,4},{7,5},{8,10},{9,11},{10,... | collective-permute-start | bytes 2359304 | tf_op jit(solution)/shard_map/ppermute | solution.py:30
  7.8 0.7 copy-start.4
  8.5 0.7 copy-start.5
  23.4 1.0 copy-start.1
  24.4 0.7 copy-start.2
  25.6 15.8 %collective-permute-start.4 = (bf16[80,1024]{1,0:T(8,128)(2,1)S(1)}, bf16[80,1024]{1,0:T(8,128)(2,1)S(1)}, u32[]{:S(2)}, u32[]{:S(2)}) collective-permute-start(bf16[80,1024]{1,0:T(8,128)(2,1)S(1)} %opening.1.refs_4_), channel_id=1, source_target_pairs={{0,1},{1,0},{2,3},{3,2},{4,5},{5,4},{6,7},{7,6},{8,9},{9,8},{10,11... | collective-permute-start | bytes 491528 | tf_op jit(solution)/shard_map/ppermute | solution.py:30
  25.9 18.6 %collective-permute-start.7 = (bf16[512,768]{1,0:T(8,128)(2,1)S(1)}, bf16[512,768]{1,0:T(8,128)(2,1)S(1)}, u32[]{:S(2)}, u32[]{:S(2)}) collective-permute-start(bf16[512,768]{1,0:T(8,128)(2,1)S(1)} %collective-permute-done.2.refs_6_), channel_id=1, source_target_pairs={{0,1},{1,0},{2,3},{3,2},{4,5},{5,4},{6,7},{7,6},{8,9},{9,8},{10,11... | collective-permute-start | bytes 2359304 | tf_op jit(solution)/shard_map/ppermute | solution.py:30
  26.2 1.4 %copy-start = (bf16[1024,768]{1,0:T(8,128)(2,1)S(1)}, bf16[1024,768]{1,0:T(8,128)(2,1)}, u32[]{:S(2)}) copy-start(bf16[1024,768]{1,0:T(8,128)(2,1)} %refs_3_.1) | copy-start | bytes 4718596
  41.4 6.0 %collective-permute-start.6 = (bf16[512,768]{1,0:T(8,128)(2,1)S(1)}, bf16[512,768]{1,0:T(8,128)(2,1)S(1)}, u32[]{:S(2)}, u32[]{:S(2)}) collective-permute-start(bf16[512,768]{1,0:T(8,128)(2,1)S(1)} %collective-permute-done.5.refs_1_), channel_id=1, source_target_pairs={{0,1},{1,0},{2,3},{3,2},{4,5},{5,4},{6,7},{7,6},{8,9},{9,8},{10,11... | collective-permute-start | bytes 2359304 | tf_op jit(solution)/shard_map/ppermute | solution.py:30
  41.4 11.3 %collective-permute-start.8 = (bf16[80,1024]{1,0:T(8,128)(2,1)S(1)}, bf16[80,1024]{1,0:T(8,128)(2,1)S(1)}, u32[]{:S(2)}, u32[]{:S(2)}) collective-permute-start(bf16[80,1024]{1,0:T(8,128)(2,1)S(1)} %opening.1.refs_4_), channel_id=1, source_target_pairs={{0,2},{1,3},{2,0},{3,1},{4,6},{5,7},{6,4},{7,5},{8,10},{9,11},{10,... | collective-permute-start | bytes 491528 | tf_op jit(solution)/shard_map/ppermute | solution.py:30
  43.2 12.8 %collective-permute-start.10 = (bf16[80,1024]{1,0:T(8,128)(2,1)S(1)}, bf16[80,1024]{1,0:T(8,128)(2,1)S(1)}, u32[]{:S(2)}, u32[]{:S(2)}) collective-permute-start(bf16[80,1024]{1,0:T(8,128)(2,1)S(1)} %opening.1.refs_4_), channel_id=1, source_target_pairs={{4,0},{8,4},{12,8},{16,12},{20,16},{24,20},{28,24},{5,1},{9,5},{13... | collective-permute-start | bytes 491528 | tf_op jit(solution)/shard_map/ppermute | solution.py:36
  52.8 3.3 %collective-permute-start.9 = (bf16[80,1024]{1,0:T(8,128)(2,1)S(1)}, bf16[80,1024]{1,0:T(8,128)(2,1)S(1)}, u32[]{:S(2)}, u32[]{:S(2)}) collective-permute-start(bf16[80,1024]{1,0:T(8,128)(2,1)S(1)} %collective-permute-done.8.refs_4_), channel_id=1, source_target_pairs={{0,1},{1,0},{2,3},{3,2},{4,5},{5,4},{6,7},{7,6},{8,9},{9,8},{10,11... | collective-permute-start | bytes 491528 | tf_op jit(solution)/shard_map/ppermute | solution.py:30
  59.3 16.9 %copy-start.3 = (s32[2]{0:T(128)S(1)}, s32[2]{0:T(128)}, u32[]{:S(2)}) copy-start(s32[2]{0:T(128)} %count_ref.3) | copy-start | bytes 28
  59.3 7.3 %collective-permute-start.11 = (f32[2,72,512]{2,1,0:T(8,128)S(1)}, f32[2,72,512]{2,1,0:T(8,128)S(1)}, u32[]{:S(2)}, u32[]{:S(2)}) collective-permute-start(f32[2,72,512]{2,1,0:T(8,128)S(1)} %get-tuple-element.116), channel_id=1, source_target_pairs={{0,1},{1,0},{2,3},{3,2},{4,5},{5,4},{6,7},{7,6},{8,9},{9,8},{10,11... | collective-permute-start | bytes 884744 | tf_op jit(solution)/shard_map/ppermute | solution.py:30
  60.5 12.5 %collective-permute-start.12 = (f32[2,72,512]{2,1,0:T(8,128)S(1)}, f32[2,72,512]{2,1,0:T(8,128)S(1)}, u32[]{:S(2)}, u32[]{:S(2)}) collective-permute-start(f32[2,72,512]{2,1,0:T(8,128)S(1)} %get-tuple-element.119), channel_id=1, source_target_pairs={{0,4},{4,8},{8,12},{12,16},{16,20},{20,24},{24,28},{1,5},{5,9},{9,... | collective-permute-start | bytes 884744 | tf_op jit(solution)/shard_map/ppermute | solution.py:36
  66.6 6.4 %collective-permute-start.13 = (f32[2,72,512]{2,1,0:T(8,128)S(1)}, f32[2,72,512]{2,1,0:T(8,128)S(1)}, u32[]{:S(2)}, u32[]{:S(2)}) collective-permute-start(f32[2,72,512]{2,1,0:T(8,128)S(1)} %get-tuple-element.120), channel_id=1, source_target_pairs={{0,1},{1,0},{2,3},{3,2},{4,5},{5,4},{6,7},{7,6},{8,9},{9,8},{10,11... | collective-permute-start | bytes 884744 | tf_op jit(solution)/shard_map/ppermute | solution.py:30
  66.7 9.5 %collective-permute-start.14 = (f32[2,72,512]{2,1,0:T(8,128)S(1)}, f32[2,72,512]{2,1,0:T(8,128)S(1)}, u32[]{:S(2)}, u32[]{:S(2)}) collective-permute-start(f32[2,72,512]{2,1,0:T(8,128)S(1)} %add.45), channel_id=1, source_target_pairs={{0,2},{1,3},{2,0},{3,1},{4,6},{5,7},{6,4},{7,5},{8,10},{9,11},{10,... | collective-permute-start | bytes 884744 | tf_op jit(solution)/shard_map/ppermute | solution.py:30
  77.1 2.2 %collective-permute-start.16 = (bf16[128,1024]{1,0:T(8,128)(2,1)S(1)}, bf16[128,1024]{1,0:T(8,128)(2,1)S(1)}, u32[]{:S(2)}, u32[]{:S(2)}) collective-permute-start(bf16[128,1024]{1,0:T(8,128)(2,1)S(1)} %get-tuple-element.123.refs_4_), channel_id=1, source_target_pairs={{0,1},{1,0},{2,3},{3,2},{4,5},{5,4},{6,7},{7,6},{8,9},{9,8},{10,11... | collective-permute-start | bytes 786440 | tf_op jit(solution)/shard_map/ppermute | solution.py:30
  77.2 8.7 %collective-permute-start.17 = (bf16[128,1024]{1,0:T(8,128)(2,1)S(1)}, bf16[128,1024]{1,0:T(8,128)(2,1)S(1)}, u32[]{:S(2)}, u32[]{:S(2)}) collective-permute-start(bf16[128,1024]{1,0:T(8,128)(2,1)S(1)} %get-tuple-element.123.refs_4_), channel_id=1, source_target_pairs={{0,2},{1,3},{2,0},{3,1},{4,6},{5,7},{6,4},{7,5},{8,10},{9,11},{10,... | collective-permute-start | bytes 786440 | tf_op jit(solution)/shard_map/ppermute | solution.py:30
  77.8 1.5 %collective-permute-start.15 = (f32[64,64]{1,0:T(8,128)S(1)}, f32[64,64]{1,0:T(8,128)S(1)}, u32[]{:S(2)}, u32[]{:S(2)}) collective-permute-start(f32[64,64]{1,0:T(8,128)S(1)} %get-tuple-element.122), channel_id=1, source_target_pairs={{0,1},{1,0},{2,3},{3,2},{4,5},{5,4},{6,7},{7,6},{8,9},{9,8},{10,11... | collective-permute-start | bytes 49160 | tf_op jit(solution)/shard_map/ppermute | solution.py:609
  78.0 11.9 %collective-permute-start.19 = (bf16[128,1024]{1,0:T(8,128)(2,1)S(1)}, bf16[128,1024]{1,0:T(8,128)(2,1)S(1)}, u32[]{:S(2)}, u32[]{:S(2)}) collective-permute-start(bf16[128,1024]{1,0:T(8,128)(2,1)S(1)} %get-tuple-element.123.refs_4_), channel_id=1, source_target_pairs={{4,0},{8,4},{12,8},{16,12},{20,16},{24,20},{28,24},{5,1},{9,5},{13... | collective-permute-start | bytes 786440 | tf_op jit(solution)/shard_map/ppermute | solution.py:36
  85.9 3.9 %collective-permute-start.20 = (bf16[128,1024]{1,0:T(8,128)(2,1)S(1)}, bf16[128,1024]{1,0:T(8,128)(2,1)S(1)}, u32[]{:S(2)}, u32[]{:S(2)}) collective-permute-start(bf16[128,1024]{1,0:T(8,128)(2,1)S(1)} %collective-permute-done.17.refs_4_), channel_id=1, source_target_pairs={{0,1},{1,0},{2,3},{3,2},{4,5},{5,4},{6,7},{7,6},{8,9},{9,8},{10,11... | collective-permute-start | bytes 786440 | tf_op jit(solution)/shard_map/ppermute | solution.py:30
  85.9 3.9 %collective-permute-start.18 = (f32[64,64]{1,0:T(8,128)S(1)}, f32[64,64]{1,0:T(8,128)S(1)}, u32[]{:S(2)}, u32[]{:S(2)}) collective-permute-start(f32[64,64]{1,0:T(8,128)S(1)} %add.46), channel_id=1, source_target_pairs={{0,2},{1,3},{2,0},{3,1},{4,6},{5,7},{6,4},{7,5},{8,10},{9,11},{10,... | collective-permute-start | bytes 49160 | tf_op jit(solution)/shard_map/ppermute | solution.py:609
  89.9 4.0 %collective-permute-start.21 = (f32[64,64]{1,0:T(8,128)S(1)}, f32[64,64]{1,0:T(8,128)S(1)}, u32[]{:S(2)}, u32[]{:S(2)}) collective-permute-start(f32[64,64]{1,0:T(8,128)S(1)} %add.47), channel_id=1, source_target_pairs={{0,4},{1,5},{2,6},{3,7},{4,0},{5,1},{6,2},{7,3},{8,12},{9,13},{10,... | collective-permute-start | bytes 49160 | tf_op jit(solution)/shard_map/ppermute | solution.py:609
  93.9 8.7 %collective-permute-start.22 = (f32[2,64,512]{2,1,0:T(8,128)S(1)}, f32[2,64,512]{2,1,0:T(8,128)S(1)}, u32[]{:S(2)}, u32[]{:S(2)}) collective-permute-start(f32[2,64,512]{2,1,0:T(8,128)S(1)} %get-tuple-element.140), channel_id=1, source_target_pairs={{0,1},{1,0},{2,3},{3,2},{4,5},{5,4},{6,7},{7,6},{8,9},{9,8},{10,11... | collective-permute-start | bytes 786440 | tf_op jit(solution)/shard_map/ppermute | solution.py:30
  93.9 8.8 %collective-permute-start.26 = (f32[64,64]{1,0:T(8,128)S(1)}, f32[64,64]{1,0:T(8,128)S(1)}, u32[]{:S(2)}, u32[]{:S(2)}) collective-permute-start(f32[64,64]{1,0:T(8,128)S(1)} %add.48), channel_id=1, source_target_pairs={{0,8},{1,9},{2,10},{3,11},{4,12},{5,13},{6,14},{7,15},{8,0},{9,1},... | collective-permute-start | bytes 49160 | tf_op jit(solution)/shard_map/ppermute | solution.py:609
  95.3 8.0 %collective-permute-start.27 = (f32[64,64]{1,0:T(8,128)S(1)}, f32[64,64]{1,0:T(8,128)S(1)}, u32[]{:S(2)}, u32[]{:S(2)}) collective-permute-start(f32[64,64]{1,0:T(8,128)S(1)} %add.48), channel_id=1, source_target_pairs={{0,16},{1,17},{2,18},{3,19},{4,20},{5,21},{6,22},{7,23},{8,24},{9,... | collective-permute-start | bytes 49160 | tf_op jit(solution)/shard_map/ppermute | solution.py:609
  96.4 6.9 %collective-permute-start.28 = (f32[64,64]{1,0:T(8,128)S(1)}, f32[64,64]{1,0:T(8,128)S(1)}, u32[]{:S(2)}, u32[]{:S(2)}) collective-permute-start(f32[64,64]{1,0:T(8,128)S(1)} %add.48), channel_id=1, source_target_pairs={{0,24},{1,25},{2,26},{3,27},{4,28},{5,29},{6,30},{7,31},{8,16},{9,... | collective-permute-start | bytes 49160 | tf_op jit(solution)/shard_map/ppermute | solution.py:609
  98.3 9.5 %collective-permute-start.23 = (f32[2,64,512]{2,1,0:T(8,128)S(1)}, f32[2,64,512]{2,1,0:T(8,128)S(1)}, u32[]{:S(2)}, u32[]{:S(2)}) collective-permute-start(f32[2,64,512]{2,1,0:T(8,128)S(1)} %get-tuple-element.143), channel_id=1, source_target_pairs={{0,4},{4,8},{8,12},{12,16},{16,20},{20,24},{24,28},{1,5},{5,9},{9,... | collective-permute-start | bytes 786440 | tf_op jit(solution)/shard_map/ppermute | solution.py:36
  102.6 5.3 %collective-permute-start.24 = (f32[2,64,512]{2,1,0:T(8,128)S(1)}, f32[2,64,512]{2,1,0:T(8,128)S(1)}, u32[]{:S(2)}, u32[]{:S(2)}) collective-permute-start(f32[2,64,512]{2,1,0:T(8,128)S(1)} %get-tuple-element.144), channel_id=1, source_target_pairs={{0,1},{1,0},{2,3},{3,2},{4,5},{5,4},{6,7},{7,6},{8,9},{9,8},{10,11... | collective-permute-start | bytes 786440 | tf_op jit(solution)/shard_map/ppermute | solution.py:30
  102.7 8.8 %collective-permute-start.25 = (f32[2,64,512]{2,1,0:T(8,128)S(1)}, f32[2,64,512]{2,1,0:T(8,128)S(1)}, u32[]{:S(2)}, u32[]{:S(2)}) collective-permute-start(f32[2,64,512]{2,1,0:T(8,128)S(1)} %add.49), channel_id=1, source_target_pairs={{0,2},{1,3},{2,0},{3,1},{4,6},{5,7},{6,4},{7,5},{8,10},{9,11},{10,... | collective-permute-start | bytes 786440 | tf_op jit(solution)/shard_map/ppermute | solution.py:30
  113.0 1.3 collective-permute-start.29
  114.2 3.9 %collective-permute-start.30 = (f32[64,64]{1,0:T(8,128)S(1)}, f32[64,64]{1,0:T(8,128)S(1)}, u32[]{:S(2)}, u32[]{:S(2)}) collective-permute-start(f32[64,64]{1,0:T(8,128)S(1)} %add.53), channel_id=1, source_target_pairs={{0,2},{1,3},{2,0},{3,1},{4,6},{5,7},{6,4},{7,5},{8,10},{9,11},{10,... | collective-permute-start | bytes 49160 | tf_op jit(solution)/shard_map/ppermute | solution.py:609
  114.8 4.1 %collective-permute-start.31 = (f32[64,64]{1,0:T(8,128)S(1)}, f32[64,64]{1,0:T(8,128)S(1)}, u32[]{:S(2)}, u32[]{:S(2)}) collective-permute-start(f32[64,64]{1,0:T(8,128)S(1)} %add.53), channel_id=1, source_target_pairs={{0,4},{1,5},{2,6},{3,7},{4,0},{5,1},{6,2},{7,3},{8,12},{9,13},{10,... | collective-permute-start | bytes 49160 | tf_op jit(solution)/shard_map/ppermute | solution.py:609
  115.1 4.8 %collective-permute-start.32 = (f32[64,64]{1,0:T(8,128)S(1)}, f32[64,64]{1,0:T(8,128)S(1)}, u32[]{:S(2)}, u32[]{:S(2)}) collective-permute-start(f32[64,64]{1,0:T(8,128)S(1)} %add.53), channel_id=1, source_target_pairs={{0,6},{1,7},{2,4},{3,5},{4,2},{5,3},{6,0},{7,1},{8,14},{9,15},{10,... | collective-permute-start | bytes 49160 | tf_op jit(solution)/shard_map/ppermute | solution.py:609
  119.9 4.5 %collective-permute-start.33 = (f32[64,64]{1,0:T(8,128)S(1)}, f32[64,64]{1,0:T(8,128)S(1)}, u32[]{:S(2)}, u32[]{:S(2)}) collective-permute-start(f32[64,64]{1,0:T(8,128)S(1)} %add_add_fusion.1), channel_id=1, source_target_pairs={{0,8},{1,9},{2,10},{3,11},{4,12},{5,13},{6,14},{7,15},{8,0},{9,1},... | collective-permute-start | bytes 49160 | tf_op jit(solution)/shard_map/ppermute | solution.py:609
  121.8 4.8 %collective-permute-start.34 = (f32[64,64]{1,0:T(8,128)S(1)}, f32[64,64]{1,0:T(8,128)S(1)}, u32[]{:S(2)}, u32[]{:S(2)}) collective-permute-start(f32[64,64]{1,0:T(8,128)S(1)} %add_add_fusion.1), channel_id=1, source_target_pairs={{0,16},{1,17},{2,18},{3,19},{4,20},{5,21},{6,22},{7,23},{8,24},{9,... | collective-permute-start | bytes 49160 | tf_op jit(solution)/shard_map/ppermute | solution.py:609
  122.3 5.7 %collective-permute-start.35 = (f32[64,64]{1,0:T(8,128)S(1)}, f32[64,64]{1,0:T(8,128)S(1)}, u32[]{:S(2)}, u32[]{:S(2)}) collective-permute-start(f32[64,64]{1,0:T(8,128)S(1)} %add_add_fusion.1), channel_id=1, source_target_pairs={{0,24},{1,25},{2,26},{3,27},{4,28},{5,29},{6,30},{7,31},{8,16},{9,... | collective-permute-start | bytes 49160 | tf_op jit(solution)/shard_map/ppermute | solution.py:609

commit v9 on v8

--- a/solution.py
+++ b/solution.py
@@ -431,19 +431,20 @@
 
 
 def send_urgent(results, at_home, group):
-    final = [from_behind(results[-1], "blk", 1)]
-    parts = {rel: value for rel, value in zip(range(1, group), results)}
+    final = []
+    *near, far = results
+    parts = {rel: value for rel, value in zip(range(1, group), near)}
     for bit in bits_of(group):
         for rel in reversed([rel for rel in parts if rel & bit and rel % bit == 0]):
             value = parts.pop(rel)
             if bit > 1:
-                value, at_home = lax.optimization_barrier((value, at_home))
+                value, far, at_home = lax.optimization_barrier((value, far, at_home))
             got = swap(value, "grp", bit)
             if rel ^ bit:
                 parts[rel ^ bit] = parts[rel ^ bit] + got
             else:
                 final.append(got)
-    return final, at_home
+    return final + [from_behind(far, "blk", 1)], at_home
 
 
 def finish_home(entries, vecs, tiles, start, blocks_dev, height, folds):
@@ -650,10 +651,12 @@
 
     def passed_on(index):
         offset = index * (blocks_dev // 2)
-        return {
-            (rel ^ 1) * blocks_dev + offset: swap(value, "grp", 1)
-            for rel, value in crossed[index].items()
-        }
+        found = {}
+        for rel, value in crossed[index].items():
+            cut = value.shape[0] // (1 if index else 2)
+            parts = [swap(value[at : at + cut], "grp", 1) for at in range(0, value.shape[0], cut)]
+            found[(rel ^ 1) * blocks_dev + offset] = jnp.concatenate(parts, 0)
+        return found
 
     def build(stage, fresh, state, name):
         return list(
@@ -661,10 +664,10 @@
         )
 
     state = build(0, {0: points, blocks_dev: mate, **direct(0)}, (), "first_tiles")
+    state = build(1, passed_on(0), state, "second_tiles")
     tied = lax.optimization_barrier((far[1], mate_vec, state[1], *crossed[1].values()))
     far[1], mate_vec, state[1] = tied[:3]
     crossed[1] = dict(zip(crossed[1], tied[3:]))
-    state = build(1, passed_on(0), state, "second_tiles")
     last = passed_on(1)
     *grown, kept = state
     state = build(None, direct(1), grown, "more_blocks") + [kept]
@@ -718,7 +721,9 @@
             2,
         )
         gram = all_sum(gram, stages[:1])
-        gram, at_home, *tied = lax.optimization_barrier((gram, at_home, *crossed.values()))
+        gram, at_home = lax.optimization_barrier((gram, at_home))
+        gram = all_sum(gram, pairs_of(stages[3:]))
+        gram, far_part, *tied = lax.optimization_barrier((gram, far_part, *crossed.values()))
         crossed = dict(zip(crossed, tied))
         vecs = beyond(window_of(parts, mate_part, crossed, far_part))
         gram = all_sum(gram, stages[1:2])
@@ -730,7 +735,7 @@
         gram, *results = lax.optimization_barrier((gram, *results))
         sums, at_home = send_urgent(results, at_home, group)
         sums = finish_home(entries, vecs, kept, {0: at_home}, blocks_dev, columns, 2) + sums
-        inverse = factor(all_sum(gram, pairs_of(stages[3:])))
+        inverse = factor(gram)
         z, gram, *parts = scaled_gram(sums, z, counts, degree, inverse, turn + 1 < ITERS)
         parts = parts[0] if parts else None
     stages = sum_stages()

time: 132 us -> 134 us (1.015); the launches traced: 131 us -> 135 us
  starting transfers between devices: 37.5 us -> 45.2 us
  local copies, waits for them, and re-layouts: 5.79 us -> 1.57 us
  Pallas kernels: 54.1 us -> 55.7 us
    ppermute x13, starting transfers between devices: 13.2 us -> 21.6 us  [all_sum(): lax.ppermute(value, ('blk', 'grp'), [(source, source ^ move) for source i...]
    ppermute x17 -> x18, waiting for transfers between devices: 10.3 us -> 4.41 us  [swap(): lax.ppermute(value, axis, [(source, source ^ bit) for source in range(cou...]
    ppermute x13, waiting for transfers between devices: 11 us -> 16.2 us  [all_sum(): lax.ppermute(value, ('blk', 'grp'), [(source, source ^ move) for source i...]
    unnamed x12 -> x10, local copies, waits for them, and re-layouts: 4.32 us -> 0.02 us
    ppermute x6, starting transfers between devices: 15.4 us -> 12.8 us  [from_behind(): lax.ppermute(value, axis, [(source, source + steps) for source in range(i...]
    ppermute x17 -> x18, starting transfers between devices: 8.88 us -> 10.8 us  [swap(): lax.ppermute(value, axis, [(source, source ^ bit) for source in range(cou...]
    pallas_call x6, Pallas kernels: 15.6 us -> 17.2 us  [products(): pl.pallas_call(kernel, out_shape=shapes, in_specs=[spec(SMEM)] * 4 + [spe...]
  transfers between devices with their start and end apart: 36 -> 37, of which waited for: 14 -> 17; matrix products, arithmetic and copies ran while one was open for 1% -> 1% of each run, Pallas kernels for 35% -> 35%
where the time goes in v9:
time: 134 us; the launch traced here: 135 us
  Pallas kernels  55.7 us (42%)
  starting transfers between devices  45.2 us (34%)
  waiting for transfers between devices  31.6 us (24%)
  local copies, waits for them, and re-layouts  1.57 us (1%)
    ppermute x13, starting transfers between devices, all_sum(): lax.ppermute(value, ('blk', 'grp'), [(source, source ^ move) for source i...  21.6 us
    pallas_call x6, Pallas kernels, products(): pl.pallas_call(kernel, out_shape=shapes, in_specs=[spec(SMEM)] * 4 + [spe...  17.2 us
    pallas_call x4, Pallas kernels, build_tiles(): pl.pallas_call(kernel, out_shape=shapes, in_specs=[spec(SMEM)] * len(scal...  16.2 us
    ppermute x13, waiting for transfers between devices, all_sum(): lax.ppermute(value, ('blk', 'grp'), [(source, source ^ move) for source i...  16.2 us
    pallas_call x1, Pallas kernels, listing(): pl.pallas_call(functools.partial(listing_kernel, group, cap, blocks_dev),...  14.3 us
    ppermute x6, starting transfers between devices, from_behind(): lax.ppermute(value, axis, [(source, source + steps) for source in range(i...  12.8 us
    ppermute x6, waiting for transfers between devices, from_behind(): lax.ppermute(value, axis, [(source, source + steps) for source in range(i...  11 us
    ppermute x18, starting transfers between devices, swap(): lax.ppermute(value, axis, [(source, source ^ bit) for source in range(cou...  10.8 us
  transfers between devices with their start and end apart: 37, of which 17 were waited for; matrix products, arithmetic and copies ran while one was open for 1% of the time, Pallas kernels for 35%

profile of v9, /device:TPU:0, one launch (start us, length us, event | category | flops | bytes accessed | tf_op | source)
XLA Modules:
  0.0 135.2 jit_solution(9408661852779218244)
XLA Ops:
  0.0 0.5 collective-permute-start
  0.5 1.5 %fusion = (bf16[512,768]{1,0:T(8,128)(2,1)S(1)}, bf16[512,768]{1,0:T(8,128)(2,1)S(1)}) fusion(bf16[1024,768]{1,0:T(8,128)(2,1)} %refs_3_.1), kind=kLoop, calls=%fused_computation.4 | loop fusion | bytes 3145728 | tf_op jit(solution)/shard_map/slice | solution.py:633
  2.1 1.3 collective-permute-start.1
  3.4 2.7 %collective-permute-start.2 = (bf16[512,768]{1,0:T(8,128)(2,1)S(1)}, bf16[512,768]{1,0:T(8,128)(2,1)S(1)}, u32[]{:S(2)}, u32[]{:S(2)}) collective-permute-start(bf16[512,768]{1,0:T(8,128)(2,1)S(1)} %get-tuple-element.160), channel_id=1, source_target_pairs={{0,2},{1,3},{2,0},{3,1},{4,6},{5,7},{6,4},{7,5},{8,10},{9,11},{10,... | collective-permute-start | bytes 2359304 | tf_op jit(solution)/shard_map/ppermute | solution.py:30
  6.0 1.3 collective-permute-start.3
  7.3 0.1 collective-permute-start.7
  8.1 14.3 %listing.1 = (s32[16]{0:T(128)S(1)}, s32[16]{0:T(128)S(1)}, s32[4]{0:T(128)S(1)}, s32[32]{0:T(128)S(1)}, s32[32]{0:T(128)S(1)}, /*index=5*/s32[32]{0:T(128)S(1)}, s32[7]{0:T(128)S(1)}) custom-call(s32[64]{0:T(128)S(1)} %copy-done.3, s32[64]{0:T(128)S(1)} %copy-done.4, s32[1]{0:T(128)S(6)} %copy.29.live), custom_call_target="tpu_custom_call" | custom-call | flops 1048576 | bytes 1024 | tf_op jit(solution)/shard_map/listing/pallas_call | solution.py:214
  22.4 0.6 opening.1.refs_4_
  23.0 2.0 %collective-permute-done.1.refs_5_ = bf16[512,768]{1,0:T(8,128)(2,1)S(1)} collective-permute-done((bf16[512,768]{1,0:T(8,128)(2,1)S(1)}, bf16[512,768]{1,0:T(8,128)(2,1)S(1)}, u32[]{:S(2)}, u32[]{:S(2)}) %collective-permute-start.1) | collective-permute-done | bytes 786464 | tf_op jit(solution)/shard_map/ppermute | solution.py:36
  25.1 0.5 collective-permute-start.6
  25.6 0.1 collective-permute-start.4
  25.7 7.9 %first_tiles.1 = (bf16[5120,768]{1,0:T(8,128)(2,1)S(1)}, f32[10,8,512]{2,1,0:T(8,128)S(1)}, f32[8,512,128]{2,1,0:T(8,128)S(1)}, bf16[17,512,512]{2,1,0:T(8,128)(2,1)S(1)}) custom-call(s32[4]{0:T(128)S(1)} %get-tuple-element.90.refs_0_, s32[16]{0:T(128)S(1)} %get-tuple-element.91.refs_1_, s32[16]{0:T(128)S(1)} %get-tuple-element.92.refs_2_, ...), custom_call_target="tpu_custom_call" | custom-call | flops 1048576 | bytes 1048576 | tf_op jit(solution)/shard_map/first_tiles/pallas_call | solution.py:331
  33.7 2.1 %second_tiles.1 = (bf16[5120,768]{1,0:T(8,128)(2,1)S(1)}, f32[10,8,512]{2,1,0:T(8,128)S(1)}, f32[8,512,128]{2,1,0:T(8,128)S(1)}, bf16[17,512,512]{2,1,0:T(8,128)(2,1)S(1)}) custom-call(s32[4]{0:T(128)S(1)} %get-tuple-element.90.refs_0_, s32[16]{0:T(128)S(1)} %get-tuple-element.91.refs_1_, ...), custom_call_target="tpu_custom_call", output_to_operand_aliasing={{0}: (4, {}), {1}: (5, {}), {2}: (6, {}), {3}: (7, {})} | custom-call | flops 1048576 | bytes 1048576 | tf_op jit(solution)/shard_map/second_tiles/pallas_call | solution.py:331
  35.8 5.7 %collective-permute-done.3.refs_0_ = bf16[512,768]{1,0:T(8,128)(2,1)S(1)} collective-permute-done((bf16[512,768]{1,0:T(8,128)(2,1)S(1)}, bf16[512,768]{1,0:T(8,128)(2,1)S(1)}, u32[]{:S(2)}, u32[]{:S(2)}) %collective-permute-start.3) | collective-permute-done | bytes 786464 | tf_op jit(solution)/shard_map/ppermute | solution.py:36
  41.5 1.8 %collective-permute-start.9 = (bf16[80,1024]{1,0:T(8,128)(2,1)S(1)}, bf16[80,1024]{1,0:T(8,128)(2,1)S(1)}, u32[]{:S(2)}, u32[]{:S(2)}) collective-permute-start(bf16[80,1024]{1,0:T(8,128)(2,1)S(1)} %opening.1.refs_4_), channel_id=1, source_target_pairs={{0,2},{1,3},{2,0},{3,1},{4,6},{5,7},{6,4},{7,5},{8,10},{9,11},{10,... | collective-permute-start | bytes 491528 | tf_op jit(solution)/shard_map/ppermute | solution.py:30
  43.3 1.3 collective-permute-start.11
  44.6 0.8 more_blocks.1
  45.3 5.4 %last_tiles.1 = (bf16[5120,768]{1,0:T(8,128)(2,1)S(1)}, f32[10,8,512]{2,1,0:T(8,128)S(1)}, f32[8,512,128]{2,1,0:T(8,128)S(1)}, bf16[17,512,512]{2,1,0:T(8,128)(2,1)S(1)}) custom-call(s32[4]{0:T(128)S(1)} %get-tuple-element.90.refs_0_, s32[16]{0:T(128)S(1)} %get-tuple-element.91.refs_1_, ...), custom_call_target="tpu_custom_call", output_to_operand_aliasing={{0}: (4, {}), {1}: (5, {}), {2}: (6, {}), {3}: (7, {})} | custom-call | flops 4294967296 | bytes 1048576 | tf_op jit(solution)/shard_map/last_tiles/pallas_call | solution.py:331
  50.7 1.3 collective-permute-start.10
  52.1 2.8 %products.6 = (f32[2,72,512]{2,1,0:T(8,128)S(1)}, f32[2,72,512]{2,1,0:T(8,128)S(1)}, f32[2,72,512]{2,1,0:T(8,128)S(1)}, f32[2,72,512]{2,1,0:T(8,128)S(1)}, f32[2,72,512]{2,1,0:T(8,128)S(1)}) custom-call(s32[32]{0:T(128)S(1)} %get-tuple-element.82.refs_0_, s32[32]{0:T(128)S(1)} %get-tuple-element.83.refs_1_, s32[32]{0:T(128)S(1)} %get-tuple-element.84.refs_2_, ...), custom_call_target="tpu_custom_call" | custom-call | flops 1048576 | bytes 1048576 | tf_op jit(solution)/shard_map/products/pallas_call | solution.py:414
  54.8 3.5 %products.7 = (f32[2,72,512]{2,1,0:T(8,128)S(1)}, f32[2,72,512]{2,1,0:T(8,128)S(1)}, f32[2,72,512]{2,1,0:T(8,128)S(1)}, f32[2,72,512]{2,1,0:T(8,128)S(1)}) custom-call(s32[32]{0:T(128)S(1)} %get-tuple-element.82.refs_0_, s32[32]{0:T(128)S(1)} %get-tuple-element.83.refs_1_, s32[32]{0:T(128)S(1)} %get-tuple-element.84.refs_2_, ...), custom_call_target="tpu_custom_call" | custom-call | flops 2147483648 | bytes 1048576 | tf_op jit(solution)/shard_map/products/pallas_call | solution.py:414
  58.4 0.8 collective-permute-start.12
  59.2 0.1 collective-permute-start.13
  59.3 1.1 collective-permute-done.12
  60.5 0.7 collective-permute-start.14
  61.2 4.7 %collective-permute-start.15 = (f32[2,72,512]{2,1,0:T(8,128)S(1)}, f32[2,72,512]{2,1,0:T(8,128)S(1)}, u32[]{:S(2)}, u32[]{:S(2)}) collective-permute-start(f32[2,72,512]{2,1,0:T(8,128)S(1)} %get-tuple-element.126), channel_id=1, source_target_pairs={{0,4},{4,8},{8,12},{12,16},{16,20},{20,24},{24,28},{1,5},{5,9},{9,... | collective-permute-start | bytes 884744 | tf_op jit(solution)/shard_map/ppermute | solution.py:36
  65.9 2.2 %products.8.refs_0_ = f32[2,72,512]{2,1,0:T(8,128)S(1)} custom-call(s32[32]{0:T(128)S(1)} %get-tuple-element.82.refs_0_, s32[32]{0:T(128)S(1)} %get-tuple-element.83.refs_1_, s32[32]{0:T(128)S(1)} %get-tuple-element.84.refs_2_, s32[7]{0:T(128)S(1)} %get-tuple-element.85.refs_3_, bf16[80,1024]{1,0:T(8,128)(2,1)S(1)} %collective-permute-done.9.refs_4_, ...), custom_call_target="tpu_custom_call" | custom-call | flops 1048576 | bytes 1048576 | tf_op jit(solution)/shard_map/products/pallas_call | solution.py:414
  68.1 1.7 %collective-permute-done.14.refs_2_ = f32[2,72,512]{2,1,0:T(8,128)S(1)} collective-permute-done((f32[2,72,512]{2,1,0:T(8,128)S(1)}, f32[2,72,512]{2,1,0:T(8,128)S(1)}, u32[]{:S(2)}, u32[]{:S(2)}) %collective-permute-start.14) | collective-permute-done | bytes 294944 | tf_op jit(solution)/shard_map/ppermute | solution.py:30
  69.8 2.5 %collective-permute-done.15.refs_3_ = f32[2,72,512]{2,1,0:T(8,128)S(1)} collective-permute-done((f32[2,72,512]{2,1,0:T(8,128)S(1)}, f32[2,72,512]{2,1,0:T(8,128)S(1)}, u32[]{:S(2)}, u32[]{:S(2)}) %collective-permute-start.15) | collective-permute-done | bytes 294944 | tf_op jit(solution)/shard_map/ppermute | solution.py:36
  72.4 0.9 scaled_gram.2
  73.4 1.3 collective-permute-start.21
  74.7 0.7 collective-permute-start.22
  75.5 0.2 collective-permute-start.16
  75.7 1.0 collective-permute-done.16
  76.7 2.8 %products.9 = (f32[2,64,512]{2,1,0:T(8,128)S(1)}, f32[2,64,512]{2,1,0:T(8,128)S(1)}, f32[2,64,512]{2,1,0:T(8,128)S(1)}, f32[2,64,512]{2,1,0:T(8,128)S(1)}, f32[2,64,512]{2,1,0:T(8,128)S(1)}) custom-call(s32[32]{0:T(128)S(1)} %get-tuple-element.82.refs_0_, s32[32]{0:T(128)S(1)} %get-tuple-element.83.refs_1_, s32[32]{0:T(128)S(1)} %get-tuple-element.84.refs_2_, ...), custom_call_target="tpu_custom_call" | custom-call | flops 1048576 | bytes 1048576 | tf_op jit(solution)/shard_map/products/pallas_call | solution.py:414
  79.5 6.9 %collective-permute-start.18 = (f32[64,64]{1,0:T(8,128)S(1)}, f32[64,64]{1,0:T(8,128)S(1)}, u32[]{:S(2)}, u32[]{:S(2)}) collective-permute-start(f32[64,64]{1,0:T(8,128)S(1)} %add.46), channel_id=1, source_target_pairs={{0,8},{1,9},{2,10},{3,11},{4,12},{5,13},{6,14},{7,15},{8,0},{9,1},... | collective-permute-start | bytes 49160 | tf_op jit(solution)/shard_map/ppermute | solution.py:610
  86.3 2.4 %collective-permute-start.20 = (f32[64,64]{1,0:T(8,128)S(1)}, f32[64,64]{1,0:T(8,128)S(1)}, u32[]{:S(2)}, u32[]{:S(2)}) collective-permute-start(f32[64,64]{1,0:T(8,128)S(1)} %add.46), channel_id=1, source_target_pairs={{0,24},{1,25},{2,26},{3,27},{4,28},{5,29},{6,30},{7,31},{8,16},{9,... | collective-permute-start | bytes 49160 | tf_op jit(solution)/shard_map/ppermute | solution.py:610
  88.8 2.5 %collective-permute-done.19 = f32[64,64]{1,0:T(8,128)S(1)} collective-permute-done((f32[64,64]{1,0:T(8,128)S(1)}, f32[64,64]{1,0:T(8,128)S(1)}, u32[]{:S(2)}, u32[]{:S(2)}) %collective-permute-start.19) | collective-permute-done | bytes 16416 | tf_op jit(solution)/shard_map/ppermute | solution.py:610
  91.3 0.8 collective-permute-done.20
  92.2 1.4 %collective-permute-start.23 = (f32[64,64]{1,0:T(8,128)S(1)}, f32[64,64]{1,0:T(8,128)S(1)}, u32[]{:S(2)}, u32[]{:S(2)}) collective-permute-start(f32[64,64]{1,0:T(8,128)S(1)} %add_add_fusion.2), channel_id=1, source_target_pairs={{0,2},{1,3},{2,0},{3,1},{4,6},{5,7},{6,4},{7,5},{8,10},{9,11},{10,... | collective-permute-start | bytes 49160 | tf_op jit(solution)/shard_map/ppermute | solution.py:610
  93.6 2.6 %collective-permute-done.23 = f32[64,64]{1,0:T(8,128)S(1)} collective-permute-done((f32[64,64]{1,0:T(8,128)S(1)}, f32[64,64]{1,0:T(8,128)S(1)}, u32[]{:S(2)}, u32[]{:S(2)}) %collective-permute-start.23) | collective-permute-done | bytes 16416 | tf_op jit(solution)/shard_map/ppermute | solution.py:610
  96.2 2.2 %collective-permute-start.25 = (f32[64,64]{1,0:T(8,128)S(1)}, f32[64,64]{1,0:T(8,128)S(1)}, u32[]{:S(2)}, u32[]{:S(2)}) collective-permute-start(f32[64,64]{1,0:T(8,128)S(1)} %add.50), channel_id=1, source_target_pairs={{0,4},{1,5},{2,6},{3,7},{4,0},{5,1},{6,2},{7,3},{8,12},{9,13},{10,... | collective-permute-start | bytes 49160 | tf_op jit(solution)/shard_map/ppermute | solution.py:610
  98.4 3.6 %products.10 = (f32[2,64,512]{2,1,0:T(8,128)S(1)}, f32[2,64,512]{2,1,0:T(8,128)S(1)}, f32[2,64,512]{2,1,0:T(8,128)S(1)}, f32[2,64,512]{2,1,0:T(8,128)S(1)}) custom-call(s32[32]{0:T(128)S(1)} %get-tuple-element.82.refs_0_, s32[32]{0:T(128)S(1)} %get-tuple-element.83.refs_1_, s32[32]{0:T(128)S(1)} %get-tuple-element.84.refs_2_, ...), custom_call_target="tpu_custom_call" | custom-call | flops 2147483648 | bytes 1048576 | tf_op jit(solution)/shard_map/products/pallas_call | solution.py:414
  102.1 0.5 collective-permute-start.27
  102.6 1.0 collective-permute-done.26
  103.7 0.6 collective-permute-start.28
  104.3 3.0 %collective-permute-start.29 = (f32[2,64,512]{2,1,0:T(8,128)S(1)}, f32[2,64,512]{2,1,0:T(8,128)S(1)}, u32[]{:S(2)}, u32[]{:S(2)}) collective-permute-start(f32[2,64,512]{2,1,0:T(8,128)S(1)} %get-tuple-element.153), channel_id=1, source_target_pairs={{0,4},{4,8},{8,12},{12,16},{16,20},{20,24},{24,28},{1,5},{5,9},{9,... | collective-permute-start | bytes 786440 | tf_op jit(solution)/shard_map/ppermute | solution.py:36
  107.3 2.0 %factor.1.refs_6_ = f32[64,64]{1,0:T(8,128)S(1)} custom-call(f32[64,64]{1,0:T(8,128)S(1)} %add.51.gram), custom_call_target="tpu_custom_call" | custom-call | flops 2147483648 | bytes 65536 | tf_op jit(solution)/shard_map/factor/pallas_call | solution.py:566
  109.3 2.3 %products.11.refs_0_ = f32[2,64,512]{2,1,0:T(8,128)S(1)} custom-call(s32[32]{0:T(128)S(1)} %get-tuple-element.82.refs_0_, s32[32]{0:T(128)S(1)} %get-tuple-element.83.refs_1_, s32[32]{0:T(128)S(1)} %get-tuple-element.84.refs_2_, s32[7]{0:T(128)S(1)} %get-tuple-element.85.refs_3_, bf16[128,1024]{1,0:T(8,128)(2,1)S(1)} %collective-permute-done.22.refs_4_, ...), custom_call_target="tpu_custom_call" | custom-call | flops 1048576 | bytes 1048576 | tf_op jit(solution)/shard_map/products/pallas_call | solution.py:414
  111.6 0.5 collective-permute-done.28.refs_2_
  112.1 0.8 collective-permute-done.29.refs_3_
  112.9 1.5 %scaled_gram.3 = (f32[64,1024]{1,0:T(8,128)S(1)}, f32[64,64]{1,0:T(8,128)S(1)}) custom-call(s32[2]{0:T(128)S(1)} %copy-done.2, f32[2,64,512]{2,1,0:T(8,128)S(1)} %products.11.refs_0_, f32[2,64,512]{2,1,0:T(8,128)S(1)} %collective-permute-done.27.refs_1_, f32[2,64,512]{2,1,0:T(8,128)S(1)} %collective-permute-done.28.refs_2_, ...), custom_call_target="tpu_custom_call" | custom-call | flops 67108864 | bytes 2097152 | tf_op jit(solution)/shard_map/scaled_gram/pallas_call | solution.py:507
  114.5 1.2 collective-permute-done.30
  115.7 0.8 collective-permute-start.31
  116.5 2.6 %collective-permute-start.32 = (f32[64,64]{1,0:T(8,128)S(1)}, f32[64,64]{1,0:T(8,128)S(1)}, u32[]{:S(2)}, u32[]{:S(2)}) collective-permute-start(f32[64,64]{1,0:T(8,128)S(1)} %add.53), channel_id=1, source_target_pairs={{0,4},{1,5},{2,6},{3,7},{4,0},{5,1},{6,2},{7,3},{8,12},{9,13},{10,... | collective-permute-start | bytes 49160 | tf_op jit(solution)/shard_map/ppermute | solution.py:610
  119.1 0.5 collective-permute-start.33
  119.6 1.4 %collective-permute-done.32 = f32[64,64]{1,0:T(8,128)S(1)} collective-permute-done((f32[64,64]{1,0:T(8,128)S(1)}, f32[64,64]{1,0:T(8,128)S(1)}, u32[]{:S(2)}, u32[]{:S(2)}) %collective-permute-start.32) | collective-permute-done | bytes 16416 | tf_op jit(solution)/shard_map/ppermute | solution.py:610
  121.0 2.9 %collective-permute-done.33 = f32[64,64]{1,0:T(8,128)S(1)} collective-permute-done((f32[64,64]{1,0:T(8,128)S(1)}, f32[64,64]{1,0:T(8,128)S(1)}, u32[]{:S(2)}, u32[]{:S(2)}) %collective-permute-start.33) | collective-permute-done | bytes 16416 | tf_op jit(solution)/shard_map/ppermute | solution.py:610
  123.9 2.0 %collective-permute-start.34 = (f32[64,64]{1,0:T(8,128)S(1)}, f32[64,64]{1,0:T(8,128)S(1)}, u32[]{:S(2)}, u32[]{:S(2)}) collective-permute-start(f32[64,64]{1,0:T(8,128)S(1)} %add_add_fusion.1), channel_id=1, source_target_pairs={{0,8},{1,9},{2,10},{3,11},{4,12},{5,13},{6,14},{7,15},{8,0},{9,1},... | collective-permute-start | bytes 49160 | tf_op jit(solution)/shard_map/ppermute | solution.py:610
  125.9 0.6 collective-permute-start.35
  126.5 1.9 %collective-permute-start.36 = (f32[64,64]{1,0:T(8,128)S(1)}, f32[64,64]{1,0:T(8,128)S(1)}, u32[]{:S(2)}, u32[]{:S(2)}) collective-permute-start(f32[64,64]{1,0:T(8,128)S(1)} %add_add_fusion.1), channel_id=1, source_target_pairs={{0,24},{1,25},{2,26},{3,27},{4,28},{5,29},{6,30},{7,31},{8,16},{9,... | collective-permute-start | bytes 49160 | tf_op jit(solution)/shard_map/ppermute | solution.py:610
  128.4 2.3 %collective-permute-done.35 = f32[64,64]{1,0:T(8,128)S(1)} collective-permute-done((f32[64,64]{1,0:T(8,128)S(1)}, f32[64,64]{1,0:T(8,128)S(1)}, u32[]{:S(2)}, u32[]{:S(2)}) %collective-permute-start.35) | collective-permute-done | bytes 16416 | tf_op jit(solution)/shard_map/ppermute | solution.py:610
  130.7 1.5 %collective-permute-done.36 = f32[64,64]{1,0:T(8,128)S(1)} collective-permute-done((f32[64,64]{1,0:T(8,128)S(1)}, f32[64,64]{1,0:T(8,128)S(1)}, u32[]{:S(2)}, u32[]{:S(2)}) %collective-permute-start.36) | collective-permute-done | bytes 16416 | tf_op jit(solution)/shard_map/ppermute | solution.py:610
  132.2 3.0 %embedding.1 = f32[64,1024]{1,0:T(8,128)} custom-call(f32[64,64]{1,0:T(8,128)S(1)} %add_add_fusion.gram, f32[64,1024]{1,0:T(8,128)S(1)} %get-tuple-element.158.z), custom_call_target="tpu_custom_call" | custom-call | flops 1073741824 | bytes 1048576 | tf_op jit(solution)/shard_map/embedding/pallas_call | solution.py:584
  (48 shorter events, 0.7 us)
Async XLA Ops:
  0.0 25.7 %copy-start = (bf16[1024,768]{1,0:T(8,128)(2,1)S(1)}, bf16[1024,768]{1,0:T(8,128)(2,1)}, u32[]{:S(2)}) copy-start(bf16[1024,768]{1,0:T(8,128)(2,1)} %refs_3_.1) | copy-start | bytes 4718596
  0.0 8.1 %copy-start.3 = (s32[64]{0:T(128)S(1)}, s32[64]{0:T(128)}, u32[]{:S(2)}) copy-start(s32[64]{0:T(128)} %rows.1) | copy-start | bytes 772
  0.0 8.1 %copy-start.4 = (s32[64]{0:T(128)S(1)}, s32[64]{0:T(128)}, u32[]{:S(2)}) copy-start(s32[64]{0:T(128)} %cols.1) | copy-start | bytes 772
  0.0 22.4 %copy-start.1 = (f32[64,1024]{1,0:T(8,128)S(1)}, f32[64,1024]{1,0:T(8,128)}, u32[]{:S(2)}) copy-start(f32[64,1024]{1,0:T(8,128)} %start) | copy-start | bytes 786436
  0.0 22.4 %copy-start.2 = (s32[2]{0:T(128)S(1)}, s32[2]{0:T(128)}, u32[]{:S(2)}) copy-start(s32[2]{0:T(128)} %count_ref.3) | copy-start | bytes 28
  0.0 22.4 %collective-permute-start = (bf16[1024,768]{1,0:T(8,128)(2,1)}, bf16[1024,768]{1,0:T(8,128)(2,1)S(1)}, u32[]{:S(2)}, u32[]{:S(2)}) collective-permute-start(bf16[1024,768]{1,0:T(8,128)(2,1)} %refs_3_.1), channel_id=1, source_target_pairs={{0,1},{1,0},{2,3},{3,2},{4,5},{5,4},{6,7},{7,6},{8,9},{9,8},{10,11... | collective-permute-start | bytes 4718600 | tf_op jit(solution)/shard_map/ppermute | solution.py:30
  2.1 22.9 %collective-permute-start.1 = (bf16[512,768]{1,0:T(8,128)(2,1)S(1)}, bf16[512,768]{1,0:T(8,128)(2,1)S(1)}, u32[]{:S(2)}, u32[]{:S(2)}) collective-permute-start(bf16[512,768]{1,0:T(8,128)(2,1)S(1)} %get-tuple-element.160), channel_id=1, source_target_pairs={{4,0},{8,4},{12,8},{16,12},{20,16},{24,20},{28,24},{5,1},{9,5},{13... | collective-permute-start | bytes 2359304 | tf_op jit(solution)/shard_map/ppermute | solution.py:36
  3.4 21.6 %collective-permute-start.2 = (bf16[512,768]{1,0:T(8,128)(2,1)S(1)}, bf16[512,768]{1,0:T(8,128)(2,1)S(1)}, u32[]{:S(2)}, u32[]{:S(2)}) collective-permute-start(bf16[512,768]{1,0:T(8,128)(2,1)S(1)} %get-tuple-element.160), channel_id=1, source_target_pairs={{0,2},{1,3},{2,0},{3,1},{4,6},{5,7},{6,4},{7,5},{8,10},{9,11},{10,... | collective-permute-start | bytes 2359304 | tf_op jit(solution)/shard_map/ppermute | solution.py:30
  6.0 35.5 %collective-permute-start.3 = (bf16[512,768]{1,0:T(8,128)(2,1)S(1)}, bf16[512,768]{1,0:T(8,128)(2,1)S(1)}, u32[]{:S(2)}, u32[]{:S(2)}) collective-permute-start(bf16[512,768]{1,0:T(8,128)(2,1)S(1)} %get-tuple-element.159), channel_id=1, source_target_pairs={{4,0},{8,4},{12,8},{16,12},{20,16},{24,20},{28,24},{5,1},{9,5},{13... | collective-permute-start | bytes 2359304 | tf_op jit(solution)/shard_map/ppermute | solution.py:36
  7.3 34.2 %collective-permute-start.7 = (bf16[512,768]{1,0:T(8,128)(2,1)S(1)}, bf16[512,768]{1,0:T(8,128)(2,1)S(1)}, u32[]{:S(2)}, u32[]{:S(2)}) collective-permute-start(bf16[512,768]{1,0:T(8,128)(2,1)S(1)} %get-tuple-element.159), channel_id=1, source_target_pairs={{0,2},{1,3},{2,0},{3,1},{4,6},{5,7},{6,4},{7,5},{8,10},{9,11},{10,... | collective-permute-start | bytes 2359304 | tf_op jit(solution)/shard_map/ppermute | solution.py:30
  25.0 8.6 %collective-permute-start.5 = (bf16[256,768]{1,0:T(8,128)(2,1)S(1)}, bf16[256,768]{1,0:T(8,128)(2,1)S(1)}, u32[]{:S(2)}, u32[]{:S(2)}) collective-permute-start(bf16[256,768]{1,0:T(8,128)(2,1)S(1)} %get-tuple-element.161), channel_id=1, source_target_pairs={{0,1},{1,0},{2,3},{3,2},{4,5},{5,4},{6,7},{7,6},{8,9},{9,8},{10,11... | collective-permute-start | bytes 1179656 | tf_op jit(solution)/shard_map/ppermute | solution.py:30
  25.1 8.5 %collective-permute-start.6 = (bf16[256,768]{1,0:T(8,128)(2,1)S(1)}, bf16[256,768]{1,0:T(8,128)(2,1)S(1)}, u32[]{:S(2)}, u32[]{:S(2)}) collective-permute-start(bf16[256,768]{1,0:T(8,128)(2,1)S(1)} %get-tuple-element.162), channel_id=1, source_target_pairs={{0,1},{1,0},{2,3},{3,2},{4,5},{5,4},{6,7},{7,6},{8,9},{9,8},{10,11... | collective-permute-start | bytes 1179656 | tf_op jit(solution)/shard_map/ppermute | solution.py:30
  25.6 15.9 %collective-permute-start.4 = (bf16[80,1024]{1,0:T(8,128)(2,1)S(1)}, bf16[80,1024]{1,0:T(8,128)(2,1)S(1)}, u32[]{:S(2)}, u32[]{:S(2)}) collective-permute-start(bf16[80,1024]{1,0:T(8,128)(2,1)S(1)} %opening.1.refs_4_), channel_id=1, source_target_pairs={{0,1},{1,0},{2,3},{3,2},{4,5},{5,4},{6,7},{7,6},{8,9},{9,8},{10,11... | collective-permute-start | bytes 491528 | tf_op jit(solution)/shard_map/ppermute | solution.py:30
  41.5 3.8 %collective-permute-start.8 = (bf16[512,768]{1,0:T(8,128)(2,1)S(1)}, bf16[512,768]{1,0:T(8,128)(2,1)S(1)}, u32[]{:S(2)}, u32[]{:S(2)}) collective-permute-start(bf16[512,768]{1,0:T(8,128)(2,1)S(1)} %collective-permute-done.7.refs_1_), channel_id=1, source_target_pairs={{0,1},{1,0},{2,3},{3,2},{4,5},{5,4},{6,7},{7,6},{8,9},{9,8},{10,11... | collective-permute-start | bytes 2359304 | tf_op jit(solution)/shard_map/ppermute | solution.py:30
  41.5 9.2 %collective-permute-start.9 = (bf16[80,1024]{1,0:T(8,128)(2,1)S(1)}, bf16[80,1024]{1,0:T(8,128)(2,1)S(1)}, u32[]{:S(2)}, u32[]{:S(2)}) collective-permute-start(bf16[80,1024]{1,0:T(8,128)(2,1)S(1)} %opening.1.refs_4_), channel_id=1, source_target_pairs={{0,2},{1,3},{2,0},{3,1},{4,6},{5,7},{6,4},{7,5},{8,10},{9,11},{10,... | collective-permute-start | bytes 491528 | tf_op jit(solution)/shard_map/ppermute | solution.py:30
  43.3 11.5 %collective-permute-start.11 = (bf16[80,1024]{1,0:T(8,128)(2,1)S(1)}, bf16[80,1024]{1,0:T(8,128)(2,1)S(1)}, u32[]{:S(2)}, u32[]{:S(2)}) collective-permute-start(bf16[80,1024]{1,0:T(8,128)(2,1)S(1)} %opening.1.refs_4_), channel_id=1, source_target_pairs={{4,0},{8,4},{12,8},{16,12},{20,16},{24,20},{28,24},{5,1},{9,5},{13... | collective-permute-start | bytes 491528 | tf_op jit(solution)/shard_map/ppermute | solution.py:36
  50.7 4.1 %collective-permute-start.10 = (bf16[80,1024]{1,0:T(8,128)(2,1)S(1)}, bf16[80,1024]{1,0:T(8,128)(2,1)S(1)}, u32[]{:S(2)}, u32[]{:S(2)}) collective-permute-start(bf16[80,1024]{1,0:T(8,128)(2,1)S(1)} %collective-permute-done.9.refs_4_), channel_id=1, source_target_pairs={{0,1},{1,0},{2,3},{3,2},{4,5},{5,4},{6,7},{7,6},{8,9},{9,8},{10,11... | collective-permute-start | bytes 491528 | tf_op jit(solution)/shard_map/ppermute | solution.py:30
  58.4 2.0 %collective-permute-start.12 = (f32[2,72,512]{2,1,0:T(8,128)S(1)}, f32[2,72,512]{2,1,0:T(8,128)S(1)}, u32[]{:S(2)}, u32[]{:S(2)}) collective-permute-start(f32[2,72,512]{2,1,0:T(8,128)S(1)} %get-tuple-element.120), channel_id=1, source_target_pairs={{0,1},{1,0},{2,3},{3,2},{4,5},{5,4},{6,7},{7,6},{8,9},{9,8},{10,11... | collective-permute-start | bytes 884744 | tf_op jit(solution)/shard_map/ppermute | solution.py:30
  59.2 8.9 %collective-permute-start.13 = (f32[2,72,512]{2,1,0:T(8,128)S(1)}, f32[2,72,512]{2,1,0:T(8,128)S(1)}, u32[]{:S(2)}, u32[]{:S(2)}) collective-permute-start(f32[2,72,512]{2,1,0:T(8,128)S(1)} %get-tuple-element.124), channel_id=1, source_target_pairs={{0,1},{1,0},{2,3},{3,2},{4,5},{5,4},{6,7},{7,6},{8,9},{9,8},{10,11... | collective-permute-start | bytes 884744 | tf_op jit(solution)/shard_map/ppermute | solution.py:30
  60.5 9.4 %collective-permute-start.14 = (f32[2,72,512]{2,1,0:T(8,128)S(1)}, f32[2,72,512]{2,1,0:T(8,128)S(1)}, u32[]{:S(2)}, u32[]{:S(2)}) collective-permute-start(f32[2,72,512]{2,1,0:T(8,128)S(1)} %add.45), channel_id=1, source_target_pairs={{0,2},{1,3},{2,0},{3,1},{4,6},{5,7},{6,4},{7,5},{8,10},{9,11},{10,... | collective-permute-start | bytes 884744 | tf_op jit(solution)/shard_map/ppermute | solution.py:30
  61.2 11.2 %collective-permute-start.15 = (f32[2,72,512]{2,1,0:T(8,128)S(1)}, f32[2,72,512]{2,1,0:T(8,128)S(1)}, u32[]{:S(2)}, u32[]{:S(2)}) collective-permute-start(f32[2,72,512]{2,1,0:T(8,128)S(1)} %get-tuple-element.126), channel_id=1, source_target_pairs={{0,4},{4,8},{8,12},{12,16},{16,20},{20,24},{24,28},{1,5},{5,9},{9,... | collective-permute-start | bytes 884744 | tf_op jit(solution)/shard_map/ppermute | solution.py:36
  73.3 3.3 %collective-permute-start.17 = (bf16[128,1024]{1,0:T(8,128)(2,1)S(1)}, bf16[128,1024]{1,0:T(8,128)(2,1)S(1)}, u32[]{:S(2)}, u32[]{:S(2)}) collective-permute-start(bf16[128,1024]{1,0:T(8,128)(2,1)S(1)} %get-tuple-element.128.refs_4_), channel_id=1, source_target_pairs={{0,1},{1,0},{2,3},{3,2},{4,5},{5,4},{6,7},{7,6},{8,9},{9,8},{10,11... | collective-permute-start | bytes 786440 | tf_op jit(solution)/shard_map/ppermute | solution.py:30
  73.4 18.7 %collective-permute-start.21 = (bf16[128,1024]{1,0:T(8,128)(2,1)S(1)}, bf16[128,1024]{1,0:T(8,128)(2,1)S(1)}, u32[]{:S(2)}, u32[]{:S(2)}) collective-permute-start(bf16[128,1024]{1,0:T(8,128)(2,1)S(1)} %get-tuple-element.128.refs_4_), channel_id=1, source_target_pairs={{4,0},{8,4},{12,8},{16,12},{20,16},{24,20},{28,24},{5,1},{9,5},{13... | collective-permute-start | bytes 786440 | tf_op jit(solution)/shard_map/ppermute | solution.py:36
  74.7 17.4 %collective-permute-start.22 = (bf16[128,1024]{1,0:T(8,128)(2,1)S(1)}, bf16[128,1024]{1,0:T(8,128)(2,1)S(1)}, u32[]{:S(2)}, u32[]{:S(2)}) collective-permute-start(bf16[128,1024]{1,0:T(8,128)(2,1)S(1)} %get-tuple-element.128.refs_4_), channel_id=1, source_target_pairs={{0,2},{1,3},{2,0},{3,1},{4,6},{5,7},{6,4},{7,5},{8,10},{9,11},{10,... | collective-permute-start | bytes 786440 | tf_op jit(solution)/shard_map/ppermute | solution.py:30
  75.5 1.2 collective-permute-start.16
  79.5 9.3 %collective-permute-start.18 = (f32[64,64]{1,0:T(8,128)S(1)}, f32[64,64]{1,0:T(8,128)S(1)}, u32[]{:S(2)}, u32[]{:S(2)}) collective-permute-start(f32[64,64]{1,0:T(8,128)S(1)} %add.46), channel_id=1, source_target_pairs={{0,8},{1,9},{2,10},{3,11},{4,12},{5,13},{6,14},{7,15},{8,0},{9,1},... | collective-permute-start | bytes 49160 | tf_op jit(solution)/shard_map/ppermute | solution.py:610
  86.3 4.9 %collective-permute-start.19 = (f32[64,64]{1,0:T(8,128)S(1)}, f32[64,64]{1,0:T(8,128)S(1)}, u32[]{:S(2)}, u32[]{:S(2)}) collective-permute-start(f32[64,64]{1,0:T(8,128)S(1)} %add.46), channel_id=1, source_target_pairs={{0,16},{1,17},{2,18},{3,19},{4,20},{5,21},{6,22},{7,23},{8,24},{9,... | collective-permute-start | bytes 49160 | tf_op jit(solution)/shard_map/ppermute | solution.py:610
  86.3 5.7 %collective-permute-start.20 = (f32[64,64]{1,0:T(8,128)S(1)}, f32[64,64]{1,0:T(8,128)S(1)}, u32[]{:S(2)}, u32[]{:S(2)}) collective-permute-start(f32[64,64]{1,0:T(8,128)S(1)} %add.46), channel_id=1, source_target_pairs={{0,24},{1,25},{2,26},{3,27},{4,28},{5,29},{6,30},{7,31},{8,16},{9,... | collective-permute-start | bytes 49160 | tf_op jit(solution)/shard_map/ppermute | solution.py:610
  92.1 4.1 %collective-permute-start.24 = (bf16[128,1024]{1,0:T(8,128)(2,1)S(1)}, bf16[128,1024]{1,0:T(8,128)(2,1)S(1)}, u32[]{:S(2)}, u32[]{:S(2)}) collective-permute-start(bf16[128,1024]{1,0:T(8,128)(2,1)S(1)} %collective-permute-done.22.refs_4_), channel_id=1, source_target_pairs={{0,1},{1,0},{2,3},{3,2},{4,5},{5,4},{6,7},{7,6},{8,9},{9,8},{10,11... | collective-permute-start | bytes 786440 | tf_op jit(solution)/shard_map/ppermute | solution.py:30
  92.2 4.0 %collective-permute-start.23 = (f32[64,64]{1,0:T(8,128)S(1)}, f32[64,64]{1,0:T(8,128)S(1)}, u32[]{:S(2)}, u32[]{:S(2)}) collective-permute-start(f32[64,64]{1,0:T(8,128)S(1)} %add_add_fusion.2), channel_id=1, source_target_pairs={{0,2},{1,3},{2,0},{3,1},{4,6},{5,7},{6,4},{7,5},{8,10},{9,11},{10,... | collective-permute-start | bytes 49160 | tf_op jit(solution)/shard_map/ppermute | solution.py:610
  96.2 5.9 %collective-permute-start.25 = (f32[64,64]{1,0:T(8,128)S(1)}, f32[64,64]{1,0:T(8,128)S(1)}, u32[]{:S(2)}, u32[]{:S(2)}) collective-permute-start(f32[64,64]{1,0:T(8,128)S(1)} %add.50), channel_id=1, source_target_pairs={{0,4},{1,5},{2,6},{3,7},{4,0},{5,1},{6,2},{7,3},{8,12},{9,13},{10,... | collective-permute-start | bytes 49160 | tf_op jit(solution)/shard_map/ppermute | solution.py:610
  102.1 1.6 %collective-permute-start.26 = (f32[2,64,512]{2,1,0:T(8,128)S(1)}, f32[2,64,512]{2,1,0:T(8,128)S(1)}, u32[]{:S(2)}, u32[]{:S(2)}) collective-permute-start(f32[2,64,512]{2,1,0:T(8,128)S(1)} %get-tuple-element.147), channel_id=1, source_target_pairs={{0,1},{1,0},{2,3},{3,2},{4,5},{5,4},{6,7},{7,6},{8,9},{9,8},{10,11... | collective-permute-start | bytes 786440 | tf_op jit(solution)/shard_map/ppermute | solution.py:30
  102.1 9.5 %collective-permute-start.27 = (f32[2,64,512]{2,1,0:T(8,128)S(1)}, f32[2,64,512]{2,1,0:T(8,128)S(1)}, u32[]{:S(2)}, u32[]{:S(2)}) collective-permute-start(f32[2,64,512]{2,1,0:T(8,128)S(1)} %get-tuple-element.151), channel_id=1, source_target_pairs={{0,1},{1,0},{2,3},{3,2},{4,5},{5,4},{6,7},{7,6},{8,9},{9,8},{10,11... | collective-permute-start | bytes 786440 | tf_op jit(solution)/shard_map/ppermute | solution.py:30
  103.7 8.4 %collective-permute-start.28 = (f32[2,64,512]{2,1,0:T(8,128)S(1)}, f32[2,64,512]{2,1,0:T(8,128)S(1)}, u32[]{:S(2)}, u32[]{:S(2)}) collective-permute-start(f32[2,64,512]{2,1,0:T(8,128)S(1)} %add.52), channel_id=1, source_target_pairs={{0,2},{1,3},{2,0},{3,1},{4,6},{5,7},{6,4},{7,5},{8,10},{9,11},{10,... | collective-permute-start | bytes 786440 | tf_op jit(solution)/shard_map/ppermute | solution.py:30
  104.3 8.6 %collective-permute-start.29 = (f32[2,64,512]{2,1,0:T(8,128)S(1)}, f32[2,64,512]{2,1,0:T(8,128)S(1)}, u32[]{:S(2)}, u32[]{:S(2)}) collective-permute-start(f32[2,64,512]{2,1,0:T(8,128)S(1)} %get-tuple-element.153), channel_id=1, source_target_pairs={{0,4},{4,8},{8,12},{12,16},{16,20},{20,24},{24,28},{1,5},{5,9},{9,... | collective-permute-start | bytes 786440 | tf_op jit(solution)/shard_map/ppermute | solution.py:36
  114.4 1.3 collective-permute-start.30
  115.7 4.0 %collective-permute-start.31 = (f32[64,64]{1,0:T(8,128)S(1)}, f32[64,64]{1,0:T(8,128)S(1)}, u32[]{:S(2)}, u32[]{:S(2)}) collective-permute-start(f32[64,64]{1,0:T(8,128)S(1)} %add.53), channel_id=1, source_target_pairs={{0,2},{1,3},{2,0},{3,1},{4,6},{5,7},{6,4},{7,5},{8,10},{9,11},{10,... | collective-permute-start | bytes 49160 | tf_op jit(solution)/shard_map/ppermute | solution.py:610
  116.5 4.5 %collective-permute-start.32 = (f32[64,64]{1,0:T(8,128)S(1)}, f32[64,64]{1,0:T(8,128)S(1)}, u32[]{:S(2)}, u32[]{:S(2)}) collective-permute-start(f32[64,64]{1,0:T(8,128)S(1)} %add.53), channel_id=1, source_target_pairs={{0,4},{1,5},{2,6},{3,7},{4,0},{5,1},{6,2},{7,3},{8,12},{9,13},{10,... | collective-permute-start | bytes 49160 | tf_op jit(solution)/shard_map/ppermute | solution.py:610
  119.1 4.8 %collective-permute-start.33 = (f32[64,64]{1,0:T(8,128)S(1)}, f32[64,64]{1,0:T(8,128)S(1)}, u32[]{:S(2)}, u32[]{:S(2)}) collective-permute-start(f32[64,64]{1,0:T(8,128)S(1)} %add.53), channel_id=1, source_target_pairs={{0,6},{1,7},{2,4},{3,5},{4,2},{5,3},{6,0},{7,1},{8,14},{9,15},{10,... | collective-permute-start | bytes 49160 | tf_op jit(solution)/shard_map/ppermute | solution.py:610
  123.9 4.5 %collective-permute-start.34 = (f32[64,64]{1,0:T(8,128)S(1)}, f32[64,64]{1,0:T(8,128)S(1)}, u32[]{:S(2)}, u32[]{:S(2)}) collective-permute-start(f32[64,64]{1,0:T(8,128)S(1)} %add_add_fusion.1), channel_id=1, source_target_pairs={{0,8},{1,9},{2,10},{3,11},{4,12},{5,13},{6,14},{7,15},{8,0},{9,1},... | collective-permute-start | bytes 49160 | tf_op jit(solution)/shard_map/ppermute | solution.py:610
  125.9 4.8 %collective-permute-start.35 = (f32[64,64]{1,0:T(8,128)S(1)}, f32[64,64]{1,0:T(8,128)S(1)}, u32[]{:S(2)}, u32[]{:S(2)}) collective-permute-start(f32[64,64]{1,0:T(8,128)S(1)} %add_add_fusion.1), channel_id=1, source_target_pairs={{0,16},{1,17},{2,18},{3,19},{4,20},{5,21},{6,22},{7,23},{8,24},{9,... | collective-permute-start | bytes 49160 | tf_op jit(solution)/shard_map/ppermute | solution.py:610
  126.5 5.7 %collective-permute-start.36 = (f32[64,64]{1,0:T(8,128)S(1)}, f32[64,64]{1,0:T(8,128)S(1)}, u32[]{:S(2)}, u32[]{:S(2)}) collective-permute-start(f32[64,64]{1,0:T(8,128)S(1)} %add_add_fusion.1), channel_id=1, source_target_pairs={{0,24},{1,25},{2,26},{3,27},{4,28},{5,29},{6,30},{7,31},{8,16},{9,... | collective-permute-start | bytes 49160 | tf_op jit(solution)/shard_map/ppermute | solution.py:610

commit v10 on v9

--- a/solution.py
+++ b/solution.py
@@ -345,13 +345,21 @@
     firsts = sorted(vecs)
     tall, held = vecs[firsts[0]].shape
     blocks_dev = held // PTS
-    begun = sorted(start)
+    begun = list(start)
     source_low, source_high = firsts[0], firsts[-1] + blocks_dev
-    low = min(first for first, _ in targets)
-    high = max(last for _, last in targets)
+    low = min(first for ranges in targets for first, _ in ranges)
+    high = max(last for ranges in targets for _, last in ranges)
     shapes = [
-        jax.ShapeDtypeStruct((last - first, height, PTS), jnp.float32) for first, last in targets
+        jax.ShapeDtypeStruct((sum(last - first for first, last in ranges), height, PTS), jnp.float32)
+        for ranges in targets
     ]
+
+    def pieces(refs):
+        for ranges, ref in zip(targets, refs):
+            at = 0
+            for first, last in ranges:
+                yield ref, slice(at, at + last - first), slice(first - low, last - low)
+                at += last - first
 
     def fold(value):
         out = value[:height]
@@ -371,8 +379,8 @@
                 lanes = slice(block * PTS, (block + 1) * PTS)
                 u_win[first - source_low + block] = ref[:, lanes]
         if begun:
-            for first, ref in zip(begun, start_refs):
-                acc[first - low : first - low + ref.shape[0]] = ref[...]
+            for ref, inside, places in pieces(start_refs):
+                acc[places] = ref[inside]
         else:
             for place in range(high - low + 1):
                 acc[place] = jnp.zeros((height, PTS), jnp.float32)
@@ -408,8 +416,8 @@
         for kind in kinds:
             several(bounds[2 * kind], bounds[2 * kind + 1], True)
             several(bounds[2 * kind + 1], bounds[2 * kind + 2], False)
-        for (first, last), out in zip(targets, outs):
-            out[...] = acc[first - low : last - low]
+        for out, inside, places in pieces(outs):
+            out[inside] = acc[places]
 
     return pl.pallas_call(
         kernel,
@@ -423,33 +431,45 @@
         cost_estimate=cost(2**31 if kinds == (1,) else 2**20, 2**20),
         compiler_params=pltpu.CompilerParams(vmem_limit_bytes=10 * 2**20),
         name="products",
-    )(*entries, *[vecs[first] for first in firsts], tiles, *[start[first] for first in begun])
+    )(*entries, *[vecs[first] for first in firsts], tiles, *begun)
 
 
 def urgent_ranges(group, blocks_dev):
-    return [(rel * blocks_dev, (rel + 1) * blocks_dev) for rel in range(1, group + 1)]
-
-
-def send_urgent(results, at_home, group):
+    messages = [
+        [rel for rel in range(group) if rel & bit and rel % bit == 0] for bit in bits_of(group)
+    ]
+    return [
+        [(rel * blocks_dev, (rel + 1) * blocks_dev) for rel in rels]
+        for rels in messages + [[group]]
+    ]
+
+
+def send_urgent(results, later, group, blocks_dev):
     final = []
-    *near, far = results
-    parts = {rel: value for rel, value in zip(range(1, group), near)}
-    for bit in bits_of(group):
-        for rel in reversed([rel for rel in parts if rel & bit and rel % bit == 0]):
-            value = parts.pop(rel)
-            if bit > 1:
-                value, far, at_home = lax.optimization_barrier((value, far, at_home))
-            got = swap(value, "grp", bit)
+    *messages, far = results
+    parts = {}
+    for bit, message in zip(bits_of(group), messages):
+        rels = [rel for rel in range(group) if rel & bit and rel % bit == 0]
+        for index, rel in enumerate(rels):
+            if rel in parts:
+                held = message[index * blocks_dev : (index + 1) * blocks_dev]
+                message = held + parts[rel] if len(rels) == 1 else message.at[
+                    index * blocks_dev : (index + 1) * blocks_dev
+                ].add(parts[rel])
+        if bit > 1:
+            message, far, *later = lax.optimization_barrier((message, far, *later))
+        got = swap(message, "grp", bit)
+        final.append(got)
+        for index, rel in enumerate(rels):
             if rel ^ bit:
-                parts[rel ^ bit] = parts[rel ^ bit] + got
-            else:
-                final.append(got)
-    return final + [from_behind(far, "blk", 1)], at_home
+                piece = got[index * blocks_dev : (index + 1) * blocks_dev]
+                parts[rel ^ bit] = parts[rel ^ bit] + piece if rel ^ bit in parts else piece
+    return final + [from_behind(far, "blk", 1)], later
 
 
 def finish_home(entries, vecs, tiles, start, blocks_dev, height, folds):
     return list(
-        products(entries, (2,), vecs, tiles, start, [(0, blocks_dev)], height, folds)
+        products(entries, (2,), vecs, tiles, [start], [[(0, blocks_dev)]], height, folds)
     )
 
 
@@ -568,7 +588,7 @@
         out_shape=jax.ShapeDtypeStruct(gram.shape, jnp.float32),
         in_specs=[spec(VMEM)],
         out_specs=spec(VMEM),
-        cost_estimate=cost(2**31, 2**16),
+        cost_estimate=cost(2**16, 2**16),
         compiler_params=pltpu.CompilerParams(vmem_limit_bytes=2 * 2**20),
         name="factor",
     )(gram)
@@ -695,46 +715,46 @@
         (0,),
         {0: vec, blocks_dev: mate_vec},
         kept,
-        {},
-        [(0, blocks_dev)] + urgent,
+        (),
+        [[(0, blocks_dev)]] + urgent,
         height,
         1,
     )
-    begun = {first: value for (first, _), value in zip(urgent, results)}
-    results = products(entries, (1,), beyond(vecs), kept, begun, urgent, height, 1)
-    sums, at_home = send_urgent(results, at_home, group)
-    sums = finish_home(entries, beyond(vecs), kept, {0: at_home}, blocks_dev, height, 1) + sums
+    results = products(entries, (1,), beyond(vecs), kept, results, urgent, height, 1)
+    sums, (at_home,) = send_urgent(results, (at_home,), group, blocks_dev)
+    sums = finish_home(entries, beyond(vecs), kept, at_home, blocks_dev, height, 1) + sums
     z, gram, parts, degree = scaled_gram(sums, vec, counts, None, None, True)
     for turn in range(1, ITERS):
         stages = sum_stages()
-        far_part = from_behind(parts, "blk", -1)
         crossed = gather_far_bits(parts)
         mate_part = swap(parts, "grp", 1)
+        gram = all_sum(gram, stages[:1])
+        gram, far_part = lax.optimization_barrier((gram, parts))
+        far_part = from_behind(far_part, "blk", -1)
         at_home, *results = products(
             entries,
             (0,),
             {0: parts, blocks_dev: mate_part},
             kept,
-            {},
-            [(0, blocks_dev)] + urgent,
+            (),
+            [[(0, blocks_dev)]] + urgent,
             columns,
             2,
         )
-        gram = all_sum(gram, stages[:1])
-        gram, at_home = lax.optimization_barrier((gram, at_home))
-        gram = all_sum(gram, pairs_of(stages[3:]))
-        gram, far_part, *tied = lax.optimization_barrier((gram, far_part, *crossed.values()))
+        at_home, far_part, *tied = lax.optimization_barrier(
+            (at_home, far_part, *crossed.values())
+        )
         crossed = dict(zip(crossed, tied))
         vecs = beyond(window_of(parts, mate_part, crossed, far_part))
         gram = all_sum(gram, stages[1:2])
         gram, *tied = lax.optimization_barrier((gram, *vecs.values()))
         vecs = dict(zip(vecs, tied))
-        begun = {first: value for (first, _), value in zip(urgent, results)}
-        results = products(entries, (1,), vecs, kept, begun, urgent, columns, 2)
+        results = products(entries, (1,), vecs, kept, results, urgent, columns, 2)
         gram = all_sum(gram, stages[2:3])
         gram, *results = lax.optimization_barrier((gram, *results))
-        sums, at_home = send_urgent(results, at_home, group)
-        sums = finish_home(entries, vecs, kept, {0: at_home}, blocks_dev, columns, 2) + sums
+        sums, (at_home, gram) = send_urgent(results, (at_home, gram), group, blocks_dev)
+        gram = all_sum(gram, pairs_of(stages[3:]))
+        sums = finish_home(entries, vecs, kept, at_home, blocks_dev, columns, 2) + sums
         inverse = factor(gram)
         z, gram, *parts = scaled_gram(sums, z, counts, degree, inverse, turn + 1 < ITERS)
         parts = parts[0] if parts else None

time: 134 us -> 140 us (1.045); the launches traced: 135 us -> 139 us
  waiting for transfers between devices: 31.6 us -> 44.1 us
  starting transfers between devices: 45.2 us -> 36.2 us
    ppermute x18 -> x16, waiting for transfers between devices: 4.41 us -> 12.9 us  [swap(): lax.ppermute(value, axis, [(source, source ^ bit) for source in range(cou...]
    ppermute x6, starting transfers between devices: 12.8 us -> 8.08 us  [from_behind(): lax.ppermute(value, axis, [(source, source + steps) for source in range(i...]
    ppermute x6, waiting for transfers between devices: 11 us -> 14.9 us  [from_behind(): lax.ppermute(value, axis, [(source, source + steps) for source in range(i...]
    ppermute x13, starting transfers between devices: 21.6 us -> 18.2 us  [all_sum(): lax.ppermute(value, ('blk', 'grp'), [(source, source ^ move) for source i...]
    ppermute x18 -> x16, starting transfers between devices: 10.8 us -> 9.95 us  [swap(): lax.ppermute(value, axis, [(source, source ^ bit) for source in range(cou...]
  transfers between devices with their start and end apart: 37 -> 35, of which waited for: 17 -> 15; matrix products, arithmetic and copies ran while one was open for 1% -> 1% of each run, Pallas kernels for 35% -> 33%
where the time goes in v10:
time: 140 us; the launch traced here: 139 us
  Pallas kernels  55.7 us (40%)
  waiting for transfers between devices  44.1 us (32%)
  starting transfers between devices  36.2 us (26%)
  local copies, waits for them, and re-layouts  1.57 us (1%)
    ppermute x13, starting transfers between devices, all_sum(): lax.ppermute(value, ('blk', 'grp'), [(source, source ^ move) for source i...  18.2 us
    pallas_call x6, Pallas kernels, products(): pl.pallas_call(kernel, out_shape=shapes, in_specs=[spec(SMEM)] * 4 + [spe...  17.2 us
    ppermute x13, waiting for transfers between devices, all_sum(): lax.ppermute(value, ('blk', 'grp'), [(source, source ^ move) for source i...  16.3 us
    pallas_call x4, Pallas kernels, build_tiles(): pl.pallas_call(kernel, out_shape=shapes, in_specs=[spec(SMEM)] * len(scal...  16.2 us
    ppermute x6, waiting for transfers between devices, from_behind(): lax.ppermute(value, axis, [(source, source + steps) for source in range(i...  14.9 us
    pallas_call x1, Pallas kernels, listing(): pl.pallas_call(functools.partial(listing_kernel, group, cap, blocks_dev),...  14.3 us
    ppermute x16, waiting for transfers between devices, swap(): lax.ppermute(value, axis, [(source, source ^ bit) for source in range(cou...  12.9 us
    ppermute x16, starting transfers between devices, swap(): lax.ppermute(value, axis, [(source, source ^ bit) for source in range(cou...  9.95 us
  transfers between devices with their start and end apart: 35, of which 15 were waited for; matrix products, arithmetic and copies ran while one was open for 1% of the time, Pallas kernels for 33%

profile of v10, /device:TPU:0, one launch (start us, length us, event | category | flops | bytes accessed | tf_op | source)
XLA Modules:
  0.0 138.8 jit_solution(14950680591243994923)
XLA Ops:
  0.0 0.5 collective-permute-start
  0.5 1.5 %fusion = (bf16[512,768]{1,0:T(8,128)(2,1)S(1)}, bf16[512,768]{1,0:T(8,128)(2,1)S(1)}) fusion(bf16[1024,768]{1,0:T(8,128)(2,1)} %refs_3_.1), kind=kLoop, calls=%fused_computation.6 | loop fusion | bytes 3145728 | tf_op jit(solution)/shard_map/slice | solution.py:653
  2.1 1.3 collective-permute-start.1
  3.4 2.7 %collective-permute-start.2 = (bf16[512,768]{1,0:T(8,128)(2,1)S(1)}, bf16[512,768]{1,0:T(8,128)(2,1)S(1)}, u32[]{:S(2)}, u32[]{:S(2)}) collective-permute-start(bf16[512,768]{1,0:T(8,128)(2,1)S(1)} %get-tuple-element.152), channel_id=1, source_target_pairs={{0,2},{1,3},{2,0},{3,1},{4,6},{5,7},{6,4},{7,5},{8,10},{9,11},{10,... | collective-permute-start | bytes 2359304 | tf_op jit(solution)/shard_map/ppermute | solution.py:30
  6.0 1.3 collective-permute-start.3
  7.3 0.1 collective-permute-start.7
  8.1 14.3 %listing.1 = (s32[16]{0:T(128)S(1)}, s32[16]{0:T(128)S(1)}, s32[4]{0:T(128)S(1)}, s32[32]{0:T(128)S(1)}, s32[32]{0:T(128)S(1)}, /*index=5*/s32[32]{0:T(128)S(1)}, s32[7]{0:T(128)S(1)}) custom-call(s32[64]{0:T(128)S(1)} %copy-done.3, s32[64]{0:T(128)S(1)} %copy-done.4, s32[1]{0:T(128)S(6)} %copy.29.live), custom_call_target="tpu_custom_call" | custom-call | flops 1048576 | bytes 1024 | tf_op jit(solution)/shard_map/listing/pallas_call | solution.py:214
  22.4 0.6 opening.1.refs_4_
  23.0 2.0 %collective-permute-done.1.refs_5_ = bf16[512,768]{1,0:T(8,128)(2,1)S(1)} collective-permute-done((bf16[512,768]{1,0:T(8,128)(2,1)S(1)}, bf16[512,768]{1,0:T(8,128)(2,1)S(1)}, u32[]{:S(2)}, u32[]{:S(2)}) %collective-permute-start.1) | collective-permute-done | bytes 786464 | tf_op jit(solution)/shard_map/ppermute | solution.py:36
  25.0 0.1 collective-permute-start.5
  25.1 0.5 collective-permute-start.6
  25.6 0.1 collective-permute-start.4
  25.7 7.9 %first_tiles.1 = (bf16[5120,768]{1,0:T(8,128)(2,1)S(1)}, f32[10,8,512]{2,1,0:T(8,128)S(1)}, f32[8,512,128]{2,1,0:T(8,128)S(1)}, bf16[17,512,512]{2,1,0:T(8,128)(2,1)S(1)}) custom-call(s32[4]{0:T(128)S(1)} %get-tuple-element.86.refs_0_, s32[16]{0:T(128)S(1)} %get-tuple-element.87.refs_1_, s32[16]{0:T(128)S(1)} %get-tuple-element.88.refs_2_, ...), custom_call_target="tpu_custom_call" | custom-call | flops 1048576 | bytes 1048576 | tf_op jit(solution)/shard_map/first_tiles/pallas_call | solution.py:331
  33.7 2.1 %second_tiles.1 = (bf16[5120,768]{1,0:T(8,128)(2,1)S(1)}, f32[10,8,512]{2,1,0:T(8,128)S(1)}, f32[8,512,128]{2,1,0:T(8,128)S(1)}, bf16[17,512,512]{2,1,0:T(8,128)(2,1)S(1)}) custom-call(s32[4]{0:T(128)S(1)} %get-tuple-element.86.refs_0_, s32[16]{0:T(128)S(1)} %get-tuple-element.87.refs_1_, ...), custom_call_target="tpu_custom_call", output_to_operand_aliasing={{0}: (4, {}), {1}: (5, {}), {2}: (6, {}), {3}: (7, {})} | custom-call | flops 1048576 | bytes 1048576 | tf_op jit(solution)/shard_map/second_tiles/pallas_call | solution.py:331
  35.8 5.7 %collective-permute-done.3.refs_0_ = bf16[512,768]{1,0:T(8,128)(2,1)S(1)} collective-permute-done((bf16[512,768]{1,0:T(8,128)(2,1)S(1)}, bf16[512,768]{1,0:T(8,128)(2,1)S(1)}, u32[]{:S(2)}, u32[]{:S(2)}) %collective-permute-start.3) | collective-permute-done | bytes 786464 | tf_op jit(solution)/shard_map/ppermute | solution.py:36
  41.5 1.8 %collective-permute-start.9 = (bf16[80,1024]{1,0:T(8,128)(2,1)S(1)}, bf16[80,1024]{1,0:T(8,128)(2,1)S(1)}, u32[]{:S(2)}, u32[]{:S(2)}) collective-permute-start(bf16[80,1024]{1,0:T(8,128)(2,1)S(1)} %opening.1.refs_4_), channel_id=1, source_target_pairs={{0,2},{1,3},{2,0},{3,1},{4,6},{5,7},{6,4},{7,5},{8,10},{9,11},{10,... | collective-permute-start | bytes 491528 | tf_op jit(solution)/shard_map/ppermute | solution.py:30
  43.3 1.3 collective-permute-start.11
  44.6 0.8 more_blocks.1
  45.3 5.4 %last_tiles.1 = (bf16[5120,768]{1,0:T(8,128)(2,1)S(1)}, f32[10,8,512]{2,1,0:T(8,128)S(1)}, f32[8,512,128]{2,1,0:T(8,128)S(1)}, bf16[17,512,512]{2,1,0:T(8,128)(2,1)S(1)}) custom-call(s32[4]{0:T(128)S(1)} %get-tuple-element.86.refs_0_, s32[16]{0:T(128)S(1)} %get-tuple-element.87.refs_1_, ...), custom_call_target="tpu_custom_call", output_to_operand_aliasing={{0}: (4, {}), {1}: (5, {}), {2}: (6, {}), {3}: (7, {})} | custom-call | flops 4294967296 | bytes 1048576 | tf_op jit(solution)/shard_map/last_tiles/pallas_call | solution.py:331
  50.7 1.3 collective-permute-start.10
  52.1 3.0 %products.6 = (f32[2,72,512]{2,1,0:T(8,128)S(1)}, f32[4,72,512]{2,1,0:T(8,128)S(1)}, f32[2,72,512]{2,1,0:T(8,128)S(1)}, f32[2,72,512]{2,1,0:T(8,128)S(1)}) custom-call(s32[32]{0:T(128)S(1)} %get-tuple-element.78.refs_0_, s32[32]{0:T(128)S(1)} %get-tuple-element.79.refs_1_, s32[32]{0:T(128)S(1)} %get-tuple-element.80.refs_2_, ...), custom_call_target="tpu_custom_call" | custom-call | flops 1048576 | bytes 1048576 | tf_op jit(solution)/shard_map/products/pallas_call | solution.py:422
  55.1 4.0 %products.7 = (f32[4,72,512]{2,1,0:T(8,128)S(1)}, f32[2,72,512]{2,1,0:T(8,128)S(1)}, f32[2,72,512]{2,1,0:T(8,128)S(1)}) custom-call(s32[32]{0:T(128)S(1)} %get-tuple-element.78.refs_0_, s32[32]{0:T(128)S(1)} %get-tuple-element.79.refs_1_, s32[32]{0:T(128)S(1)} %get-tuple-element.80.refs_2_, s32[7]{0:T(128)S(1)} %get-tuple-element.81.refs_3_, ...), custom_call_target="tpu_custom_call" | custom-call | flops 2147483648 | bytes 1048576 | tf_op jit(solution)/shard_map/products/pallas_call | solution.py:422
  59.1 0.1 collective-permute-start.12
  59.2 2.0 %collective-permute-done.12.refs_1_ = f32[4,72,512]{2,1,0:T(8,128)S(1)} collective-permute-done((f32[4,72,512]{2,1,0:T(8,128)S(1)}, f32[4,72,512]{2,1,0:T(8,128)S(1)}, u32[]{:S(2)}, u32[]{:S(2)}) %collective-permute-start.12) | collective-permute-done | bytes 589856 | tf_op jit(solution)/shard_map/ppermute | solution.py:30
  61.3 0.4 collective-permute-start.13
  61.6 1.3 collective-permute-start.14
  62.9 1.4 %products.8.refs_0_ = f32[2,72,512]{2,1,0:T(8,128)S(1)} custom-call(s32[32]{0:T(128)S(1)} %get-tuple-element.78.refs_0_, s32[32]{0:T(128)S(1)} %get-tuple-element.79.refs_1_, s32[32]{0:T(128)S(1)} %get-tuple-element.80.refs_2_, s32[7]{0:T(128)S(1)} %get-tuple-element.81.refs_3_, bf16[80,1024]{1,0:T(8,128)(2,1)S(1)} %collective-permute-done.9.refs_4_, ...), custom_call_target="tpu_custom_call" | custom-call | flops 1048576 | bytes 1048576 | tf_op jit(solution)/shard_map/products/pallas_call | solution.py:422
  64.4 6.0 %collective-permute-done.13.refs_2_ = f32[2,72,512]{2,1,0:T(8,128)S(1)} collective-permute-done((f32[2,72,512]{2,1,0:T(8,128)S(1)}, f32[2,72,512]{2,1,0:T(8,128)S(1)}, u32[]{:S(2)}, u32[]{:S(2)}) %collective-permute-start.13) | collective-permute-done | bytes 294944 | tf_op jit(solution)/shard_map/ppermute | solution.py:30
  70.4 0.9 scaled_gram.2
  71.3 0.1 collective-permute-start.15
  71.4 0.5 collective-permute-start.17
  71.9 0.8 collective-permute-start.19
  72.7 1.3 collective-permute-start.18
  74.0 3.1 %products.9 = (f32[2,64,512]{2,1,0:T(8,128)S(1)}, f32[4,64,512]{2,1,0:T(8,128)S(1)}, f32[2,64,512]{2,1,0:T(8,128)S(1)}, f32[2,64,512]{2,1,0:T(8,128)S(1)}) custom-call(s32[32]{0:T(128)S(1)} %get-tuple-element.78.refs_0_, s32[32]{0:T(128)S(1)} %get-tuple-element.79.refs_1_, s32[32]{0:T(128)S(1)} %get-tuple-element.80.refs_2_, ...), custom_call_target="tpu_custom_call" | custom-call | flops 1048576 | bytes 1048576 | tf_op jit(solution)/shard_map/products/pallas_call | solution.py:422
  77.2 3.0 %collective-permute-done.19.refs_4_ = bf16[128,1024]{1,0:T(8,128)(2,1)S(1)} collective-permute-done((bf16[128,1024]{1,0:T(8,128)(2,1)S(1)}, bf16[128,1024]{1,0:T(8,128)(2,1)S(1)}, u32[]{:S(2)}, u32[]{:S(2)}) %collective-permute-start.19) | collective-permute-done | bytes 262176 | tf_op jit(solution)/shard_map/ppermute | solution.py:30
  80.2 7.2 %collective-permute-done.18.refs_6_ = bf16[128,1024]{1,0:T(8,128)(2,1)S(1)} collective-permute-done((bf16[128,1024]{1,0:T(8,128)(2,1)S(1)}, bf16[128,1024]{1,0:T(8,128)(2,1)S(1)}, u32[]{:S(2)}, u32[]{:S(2)}) %collective-permute-start.18) | collective-permute-done | bytes 262176 | tf_op jit(solution)/shard_map/ppermute | solution.py:36
  87.4 1.0 collective-permute-start.16
  88.5 2.9 %collective-permute-done.16 = f32[64,64]{1,0:T(8,128)S(1)} collective-permute-done((f32[64,64]{1,0:T(8,128)S(1)}, f32[64,64]{1,0:T(8,128)S(1)}, u32[]{:S(2)}, u32[]{:S(2)}) %collective-permute-start.16) | collective-permute-done | bytes 16416 | tf_op jit(solution)/shard_map/ppermute | solution.py:630
  91.3 3.4 %collective-permute-start.21 = (f32[64,64]{1,0:T(8,128)S(1)}, f32[64,64]{1,0:T(8,128)S(1)}, u32[]{:S(2)}, u32[]{:S(2)}) collective-permute-start(f32[64,64]{1,0:T(8,128)S(1)} %add.47), channel_id=1, source_target_pairs={{0,4},{1,5},{2,6},{3,7},{4,0},{5,1},{6,2},{7,3},{8,12},{9,13},{10,... | collective-permute-start | bytes 49160 | tf_op jit(solution)/shard_map/ppermute | solution.py:630
  94.8 4.1 %products.10 = (f32[4,64,512]{2,1,0:T(8,128)S(1)}, f32[2,64,512]{2,1,0:T(8,128)S(1)}, f32[2,64,512]{2,1,0:T(8,128)S(1)}) custom-call(s32[32]{0:T(128)S(1)} %get-tuple-element.78.refs_0_, s32[32]{0:T(128)S(1)} %get-tuple-element.79.refs_1_, s32[32]{0:T(128)S(1)} %get-tuple-element.80.refs_2_, s32[7]{0:T(128)S(1)} %get-tuple-element.81.refs_3_, ...), custom_call_target="tpu_custom_call" | custom-call | flops 2147483648 | bytes 1048576 | tf_op jit(solution)/shard_map/products/pallas_call | solution.py:422
  98.9 0.1 collective-permute-start.22
  99.0 1.9 %collective-permute-done.22.refs_1_ = f32[4,64,512]{2,1,0:T(8,128)S(1)} collective-permute-done((f32[4,64,512]{2,1,0:T(8,128)S(1)}, f32[4,64,512]{2,1,0:T(8,128)S(1)}, u32[]{:S(2)}, u32[]{:S(2)}) %collective-permute-start.22) | collective-permute-done | bytes 524320 | tf_op jit(solution)/shard_map/ppermute | solution.py:30
  101.0 1.1 collective-permute-start.23
  102.0 1.6 %collective-permute-start.24 = (f32[2,64,512]{2,1,0:T(8,128)S(1)}, f32[2,64,512]{2,1,0:T(8,128)S(1)}, u32[]{:S(2)}, u32[]{:S(2)}) collective-permute-start(f32[2,64,512]{2,1,0:T(8,128)S(1)} %get-tuple-element.145), channel_id=1, source_target_pairs={{0,4},{4,8},{8,12},{12,16},{16,20},{20,24},{24,28},{1,5},{5,9},{9,... | collective-permute-start | bytes 786440 | tf_op jit(solution)/shard_map/ppermute | solution.py:36
  103.7 0.9 collective-permute-start.25
  104.6 3.5 %collective-permute-start.27 = (f32[64,64]{1,0:T(8,128)S(1)}, f32[64,64]{1,0:T(8,128)S(1)}, u32[]{:S(2)}, u32[]{:S(2)}) collective-permute-start(f32[64,64]{1,0:T(8,128)S(1)} %add.48), channel_id=1, source_target_pairs={{0,24},{1,25},{2,26},{3,27},{4,28},{5,29},{6,30},{7,31},{8,16},{9,... | collective-permute-start | bytes 49160 | tf_op jit(solution)/shard_map/ppermute | solution.py:630
  108.1 1.3 collective-permute-done.26
  109.4 1.1 collective-permute-done.27
  110.5 1.5 %products.11.refs_0_ = f32[2,64,512]{2,1,0:T(8,128)S(1)} custom-call(s32[32]{0:T(128)S(1)} %get-tuple-element.78.refs_0_, s32[32]{0:T(128)S(1)} %get-tuple-element.79.refs_1_, s32[32]{0:T(128)S(1)} %get-tuple-element.80.refs_2_, s32[7]{0:T(128)S(1)} %get-tuple-element.81.refs_3_, bf16[128,1024]{1,0:T(8,128)(2,1)S(1)} %collective-permute-done.19.refs_4_, ...), custom_call_target="tpu_custom_call" | custom-call | flops 1048576 | bytes 1048576 | tf_op jit(solution)/shard_map/products/pallas_call | solution.py:422
  112.0 2.0 %factor.1.refs_6_ = f32[64,64]{1,0:T(8,128)S(1)} custom-call(f32[64,64]{1,0:T(8,128)S(1)} %add_add_fusion.2.gram), custom_call_target="tpu_custom_call" | custom-call | flops 65536 | bytes 65536 | tf_op jit(solution)/shard_map/factor/pallas_call | solution.py:586
  113.9 1.5 %scaled_gram.3 = (f32[64,1024]{1,0:T(8,128)S(1)}, f32[64,64]{1,0:T(8,128)S(1)}) custom-call(s32[2]{0:T(128)S(1)} %copy-done.2, f32[2,64,512]{2,1,0:T(8,128)S(1)} %products.11.refs_0_, f32[4,64,512]{2,1,0:T(8,128)S(1)} %collective-permute-done.22.refs_1_, f32[2,64,512]{2,1,0:T(8,128)S(1)} %collective-permute-done.23.refs_2_, ...), custom_call_target="tpu_custom_call" | custom-call | flops 67108864 | bytes 2097152 | tf_op jit(solution)/shard_map/scaled_gram/pallas_call | solution.py:527
  115.5 0.1 collective-permute-start.28
  115.5 1.2 collective-permute-done.28
  116.7 0.9 collective-permute-start.29
  117.6 3.5 %collective-permute-start.30 = (f32[64,64]{1,0:T(8,128)S(1)}, f32[64,64]{1,0:T(8,128)S(1)}, u32[]{:S(2)}, u32[]{:S(2)}) collective-permute-start(f32[64,64]{1,0:T(8,128)S(1)} %add.53), channel_id=1, source_target_pairs={{0,4},{1,5},{2,6},{3,7},{4,0},{5,1},{6,2},{7,3},{8,12},{9,13},{10,... | collective-permute-start | bytes 49160 | tf_op jit(solution)/shard_map/ppermute | solution.py:630
  121.1 0.3 collective-permute-start.31
  121.4 1.6 %collective-permute-done.30 = f32[64,64]{1,0:T(8,128)S(1)} collective-permute-done((f32[64,64]{1,0:T(8,128)S(1)}, f32[64,64]{1,0:T(8,128)S(1)}, u32[]{:S(2)}, u32[]{:S(2)}) %collective-permute-start.30) | collective-permute-done | bytes 16416 | tf_op jit(solution)/shard_map/ppermute | solution.py:630
  123.0 2.9 %collective-permute-done.31 = f32[64,64]{1,0:T(8,128)S(1)} collective-permute-done((f32[64,64]{1,0:T(8,128)S(1)}, f32[64,64]{1,0:T(8,128)S(1)}, u32[]{:S(2)}, u32[]{:S(2)}) %collective-permute-start.31) | collective-permute-done | bytes 16416 | tf_op jit(solution)/shard_map/ppermute | solution.py:630
  125.9 0.6 collective-permute-start.32
  126.5 3.5 %collective-permute-start.33 = (f32[64,64]{1,0:T(8,128)S(1)}, f32[64,64]{1,0:T(8,128)S(1)}, u32[]{:S(2)}, u32[]{:S(2)}) collective-permute-start(f32[64,64]{1,0:T(8,128)S(1)} %add_add_fusion.1), channel_id=1, source_target_pairs={{0,16},{1,17},{2,18},{3,19},{4,20},{5,21},{6,22},{7,23},{8,24},{9,... | collective-permute-start | bytes 49160 | tf_op jit(solution)/shard_map/ppermute | solution.py:630
  130.0 0.4 collective-permute-start.34
  130.4 1.5 %collective-permute-done.33 = f32[64,64]{1,0:T(8,128)S(1)} collective-permute-done((f32[64,64]{1,0:T(8,128)S(1)}, f32[64,64]{1,0:T(8,128)S(1)}, u32[]{:S(2)}, u32[]{:S(2)}) %collective-permute-start.33) | collective-permute-done | bytes 16416 | tf_op jit(solution)/shard_map/ppermute | solution.py:630
  131.9 3.8 %collective-permute-done.34 = f32[64,64]{1,0:T(8,128)S(1)} collective-permute-done((f32[64,64]{1,0:T(8,128)S(1)}, f32[64,64]{1,0:T(8,128)S(1)}, u32[]{:S(2)}, u32[]{:S(2)}) %collective-permute-start.34) | collective-permute-done | bytes 16416 | tf_op jit(solution)/shard_map/ppermute | solution.py:630
  135.8 3.0 %embedding.1 = f32[64,1024]{1,0:T(8,128)} custom-call(f32[64,64]{1,0:T(8,128)S(1)} %add_add_fusion.gram, f32[64,1024]{1,0:T(8,128)S(1)} %get-tuple-element.150.z), custom_call_target="tpu_custom_call" | custom-call | flops 1073741824 | bytes 1048576 | tf_op jit(solution)/shard_map/embedding/pallas_call | solution.py:604
  (44 shorter events, 0.3 us)
Async XLA Ops:
  0.0 25.7 %copy-start = (bf16[1024,768]{1,0:T(8,128)(2,1)S(1)}, bf16[1024,768]{1,0:T(8,128)(2,1)}, u32[]{:S(2)}) copy-start(bf16[1024,768]{1,0:T(8,128)(2,1)} %refs_3_.1) | copy-start | bytes 4718596
  0.0 8.1 %copy-start.3 = (s32[64]{0:T(128)S(1)}, s32[64]{0:T(128)}, u32[]{:S(2)}) copy-start(s32[64]{0:T(128)} %rows.1) | copy-start | bytes 772
  0.0 8.1 %copy-start.4 = (s32[64]{0:T(128)S(1)}, s32[64]{0:T(128)}, u32[]{:S(2)}) copy-start(s32[64]{0:T(128)} %cols.1) | copy-start | bytes 772
  0.0 22.4 %copy-start.1 = (f32[64,1024]{1,0:T(8,128)S(1)}, f32[64,1024]{1,0:T(8,128)}, u32[]{:S(2)}) copy-start(f32[64,1024]{1,0:T(8,128)} %start) | copy-start | bytes 786436
  0.0 22.4 %copy-start.2 = (s32[2]{0:T(128)S(1)}, s32[2]{0:T(128)}, u32[]{:S(2)}) copy-start(s32[2]{0:T(128)} %count_ref.3) | copy-start | bytes 28
  0.0 22.4 %collective-permute-start = (bf16[1024,768]{1,0:T(8,128)(2,1)}, bf16[1024,768]{1,0:T(8,128)(2,1)S(1)}, u32[]{:S(2)}, u32[]{:S(2)}) collective-permute-start(bf16[1024,768]{1,0:T(8,128)(2,1)} %refs_3_.1), channel_id=1, source_target_pairs={{0,1},{1,0},{2,3},{3,2},{4,5},{5,4},{6,7},{7,6},{8,9},{9,8},{10,11... | collective-permute-start | bytes 4718600 | tf_op jit(solution)/shard_map/ppermute | solution.py:30
  2.1 22.9 %collective-permute-start.1 = (bf16[512,768]{1,0:T(8,128)(2,1)S(1)}, bf16[512,768]{1,0:T(8,128)(2,1)S(1)}, u32[]{:S(2)}, u32[]{:S(2)}) collective-permute-start(bf16[512,768]{1,0:T(8,128)(2,1)S(1)} %get-tuple-element.152), channel_id=1, source_target_pairs={{4,0},{8,4},{12,8},{16,12},{20,16},{24,20},{28,24},{5,1},{9,5},{13... | collective-permute-start | bytes 2359304 | tf_op jit(solution)/shard_map/ppermute | solution.py:36
  3.4 21.6 %collective-permute-start.2 = (bf16[512,768]{1,0:T(8,128)(2,1)S(1)}, bf16[512,768]{1,0:T(8,128)(2,1)S(1)}, u32[]{:S(2)}, u32[]{:S(2)}) collective-permute-start(bf16[512,768]{1,0:T(8,128)(2,1)S(1)} %get-tuple-element.152), channel_id=1, source_target_pairs={{0,2},{1,3},{2,0},{3,1},{4,6},{5,7},{6,4},{7,5},{8,10},{9,11},{10,... | collective-permute-start | bytes 2359304 | tf_op jit(solution)/shard_map/ppermute | solution.py:30
  6.0 35.5 %collective-permute-start.3 = (bf16[512,768]{1,0:T(8,128)(2,1)S(1)}, bf16[512,768]{1,0:T(8,128)(2,1)S(1)}, u32[]{:S(2)}, u32[]{:S(2)}) collective-permute-start(bf16[512,768]{1,0:T(8,128)(2,1)S(1)} %get-tuple-element.151), channel_id=1, source_target_pairs={{4,0},{8,4},{12,8},{16,12},{20,16},{24,20},{28,24},{5,1},{9,5},{13... | collective-permute-start | bytes 2359304 | tf_op jit(solution)/shard_map/ppermute | solution.py:36
  7.3 34.2 %collective-permute-start.7 = (bf16[512,768]{1,0:T(8,128)(2,1)S(1)}, bf16[512,768]{1,0:T(8,128)(2,1)S(1)}, u32[]{:S(2)}, u32[]{:S(2)}) collective-permute-start(bf16[512,768]{1,0:T(8,128)(2,1)S(1)} %get-tuple-element.151), channel_id=1, source_target_pairs={{0,2},{1,3},{2,0},{3,1},{4,6},{5,7},{6,4},{7,5},{8,10},{9,11},{10,... | collective-permute-start | bytes 2359304 | tf_op jit(solution)/shard_map/ppermute | solution.py:30
  25.0 8.6 %collective-permute-start.5 = (bf16[256,768]{1,0:T(8,128)(2,1)S(1)}, bf16[256,768]{1,0:T(8,128)(2,1)S(1)}, u32[]{:S(2)}, u32[]{:S(2)}) collective-permute-start(bf16[256,768]{1,0:T(8,128)(2,1)S(1)} %get-tuple-element.153), channel_id=1, source_target_pairs={{0,1},{1,0},{2,3},{3,2},{4,5},{5,4},{6,7},{7,6},{8,9},{9,8},{10,11... | collective-permute-start | bytes 1179656 | tf_op jit(solution)/shard_map/ppermute | solution.py:30
  25.1 8.5 %collective-permute-start.6 = (bf16[256,768]{1,0:T(8,128)(2,1)S(1)}, bf16[256,768]{1,0:T(8,128)(2,1)S(1)}, u32[]{:S(2)}, u32[]{:S(2)}) collective-permute-start(bf16[256,768]{1,0:T(8,128)(2,1)S(1)} %get-tuple-element.154), channel_id=1, source_target_pairs={{0,1},{1,0},{2,3},{3,2},{4,5},{5,4},{6,7},{7,6},{8,9},{9,8},{10,11... | collective-permute-start | bytes 1179656 | tf_op jit(solution)/shard_map/ppermute | solution.py:30
  25.6 15.9 %collective-permute-start.4 = (bf16[80,1024]{1,0:T(8,128)(2,1)S(1)}, bf16[80,1024]{1,0:T(8,128)(2,1)S(1)}, u32[]{:S(2)}, u32[]{:S(2)}) collective-permute-start(bf16[80,1024]{1,0:T(8,128)(2,1)S(1)} %opening.1.refs_4_), channel_id=1, source_target_pairs={{0,1},{1,0},{2,3},{3,2},{4,5},{5,4},{6,7},{7,6},{8,9},{9,8},{10,11... | collective-permute-start | bytes 491528 | tf_op jit(solution)/shard_map/ppermute | solution.py:30
  41.5 3.8 %collective-permute-start.8 = (bf16[512,768]{1,0:T(8,128)(2,1)S(1)}, bf16[512,768]{1,0:T(8,128)(2,1)S(1)}, u32[]{:S(2)}, u32[]{:S(2)}) collective-permute-start(bf16[512,768]{1,0:T(8,128)(2,1)S(1)} %collective-permute-done.7.refs_1_), channel_id=1, source_target_pairs={{0,1},{1,0},{2,3},{3,2},{4,5},{5,4},{6,7},{7,6},{8,9},{9,8},{10,11... | collective-permute-start | bytes 2359304 | tf_op jit(solution)/shard_map/ppermute | solution.py:30
  41.5 9.2 %collective-permute-start.9 = (bf16[80,1024]{1,0:T(8,128)(2,1)S(1)}, bf16[80,1024]{1,0:T(8,128)(2,1)S(1)}, u32[]{:S(2)}, u32[]{:S(2)}) collective-permute-start(bf16[80,1024]{1,0:T(8,128)(2,1)S(1)} %opening.1.refs_4_), channel_id=1, source_target_pairs={{0,2},{1,3},{2,0},{3,1},{4,6},{5,7},{6,4},{7,5},{8,10},{9,11},{10,... | collective-permute-start | bytes 491528 | tf_op jit(solution)/shard_map/ppermute | solution.py:30
  43.3 11.8 %collective-permute-start.11 = (bf16[80,1024]{1,0:T(8,128)(2,1)S(1)}, bf16[80,1024]{1,0:T(8,128)(2,1)S(1)}, u32[]{:S(2)}, u32[]{:S(2)}) collective-permute-start(bf16[80,1024]{1,0:T(8,128)(2,1)S(1)} %opening.1.refs_4_), channel_id=1, source_target_pairs={{4,0},{8,4},{12,8},{16,12},{20,16},{24,20},{28,24},{5,1},{9,5},{13... | collective-permute-start | bytes 491528 | tf_op jit(solution)/shard_map/ppermute | solution.py:36
  50.7 4.4 %collective-permute-start.10 = (bf16[80,1024]{1,0:T(8,128)(2,1)S(1)}, bf16[80,1024]{1,0:T(8,128)(2,1)S(1)}, u32[]{:S(2)}, u32[]{:S(2)}) collective-permute-start(bf16[80,1024]{1,0:T(8,128)(2,1)S(1)} %collective-permute-done.9.refs_4_), channel_id=1, source_target_pairs={{0,1},{1,0},{2,3},{3,2},{4,5},{5,4},{6,7},{7,6},{8,9},{9,8},{10,11... | collective-permute-start | bytes 491528 | tf_op jit(solution)/shard_map/ppermute | solution.py:30
  59.1 2.1 %collective-permute-start.12 = (f32[4,72,512]{2,1,0:T(8,128)S(1)}, f32[4,72,512]{2,1,0:T(8,128)S(1)}, u32[]{:S(2)}, u32[]{:S(2)}) collective-permute-start(f32[4,72,512]{2,1,0:T(8,128)S(1)} %get-tuple-element.115), channel_id=1, source_target_pairs={{0,1},{1,0},{2,3},{3,2},{4,5},{5,4},{6,7},{7,6},{8,9},{9,8},{10,11... | collective-permute-start | bytes 1769480 | tf_op jit(solution)/shard_map/ppermute | solution.py:30
  61.3 9.1 %collective-permute-start.13 = (f32[2,72,512]{2,1,0:T(8,128)S(1)}, f32[2,72,512]{2,1,0:T(8,128)S(1)}, u32[]{:S(2)}, u32[]{:S(2)}) collective-permute-start(f32[2,72,512]{2,1,0:T(8,128)S(1)} %slice_add_fusion), channel_id=1, source_target_pairs={{0,2},{1,3},{2,0},{3,1},{4,6},{5,7},{6,4},{7,5},{8,10},{9,11},{10,... | collective-permute-start | bytes 884744 | tf_op jit(solution)/shard_map/ppermute | solution.py:30
  61.6 8.7 %collective-permute-start.14 = (f32[2,72,512]{2,1,0:T(8,128)S(1)}, f32[2,72,512]{2,1,0:T(8,128)S(1)}, u32[]{:S(2)}, u32[]{:S(2)}) collective-permute-start(f32[2,72,512]{2,1,0:T(8,128)S(1)} %get-tuple-element.120), channel_id=1, source_target_pairs={{0,4},{4,8},{8,12},{12,16},{16,20},{20,24},{24,28},{1,5},{5,9},{9,... | collective-permute-start | bytes 884744 | tf_op jit(solution)/shard_map/ppermute | solution.py:36
  71.3 1.4 %collective-permute-start.15 = (f32[64,64]{1,0:T(8,128)S(1)}, f32[64,64]{1,0:T(8,128)S(1)}, u32[]{:S(2)}, u32[]{:S(2)}) collective-permute-start(f32[64,64]{1,0:T(8,128)S(1)} %get-tuple-element.121), channel_id=1, source_target_pairs={{0,1},{1,0},{2,3},{3,2},{4,5},{5,4},{6,7},{7,6},{8,9},{9,8},{10,11... | collective-permute-start | bytes 49160 | tf_op jit(solution)/shard_map/ppermute | solution.py:630
  71.4 2.6 %collective-permute-start.17 = (bf16[128,1024]{1,0:T(8,128)(2,1)S(1)}, bf16[128,1024]{1,0:T(8,128)(2,1)S(1)}, u32[]{:S(2)}, u32[]{:S(2)}) collective-permute-start(bf16[128,1024]{1,0:T(8,128)(2,1)S(1)} %get-tuple-element.125.refs_4_), channel_id=1, source_target_pairs={{0,1},{1,0},{2,3},{3,2},{4,5},{5,4},{6,7},{7,6},{8,9},{9,8},{10,11... | collective-permute-start | bytes 786440 | tf_op jit(solution)/shard_map/ppermute | solution.py:30
  71.9 8.3 %collective-permute-start.19 = (bf16[128,1024]{1,0:T(8,128)(2,1)S(1)}, bf16[128,1024]{1,0:T(8,128)(2,1)S(1)}, u32[]{:S(2)}, u32[]{:S(2)}) collective-permute-start(bf16[128,1024]{1,0:T(8,128)(2,1)S(1)} %get-tuple-element.125.refs_4_), channel_id=1, source_target_pairs={{0,2},{1,3},{2,0},{3,1},{4,6},{5,7},{6,4},{7,5},{8,10},{9,11},{10,... | collective-permute-start | bytes 786440 | tf_op jit(solution)/shard_map/ppermute | solution.py:30
  72.7 14.7 %collective-permute-start.18 = (bf16[128,1024]{1,0:T(8,128)(2,1)S(1)}, bf16[128,1024]{1,0:T(8,128)(2,1)S(1)}, u32[]{:S(2)}, u32[]{:S(2)}) collective-permute-start(bf16[128,1024]{1,0:T(8,128)(2,1)S(1)} %get-tuple-element.125.refs_4_), channel_id=1, source_target_pairs={{4,0},{8,4},{12,8},{16,12},{20,16},{24,20},{28,24},{5,1},{9,5},{13... | collective-permute-start | bytes 786440 | tf_op jit(solution)/shard_map/ppermute | solution.py:36
  87.4 3.9 %collective-permute-start.20 = (bf16[128,1024]{1,0:T(8,128)(2,1)S(1)}, bf16[128,1024]{1,0:T(8,128)(2,1)S(1)}, u32[]{:S(2)}, u32[]{:S(2)}) collective-permute-start(bf16[128,1024]{1,0:T(8,128)(2,1)S(1)} %collective-permute-done.19.refs_4_), channel_id=1, source_target_pairs={{0,1},{1,0},{2,3},{3,2},{4,5},{5,4},{6,7},{7,6},{8,9},{9,8},{10,11... | collective-permute-start | bytes 786440 | tf_op jit(solution)/shard_map/ppermute | solution.py:30
  87.4 3.9 %collective-permute-start.16 = (f32[64,64]{1,0:T(8,128)S(1)}, f32[64,64]{1,0:T(8,128)S(1)}, u32[]{:S(2)}, u32[]{:S(2)}) collective-permute-start(f32[64,64]{1,0:T(8,128)S(1)} %add.46), channel_id=1, source_target_pairs={{0,2},{1,3},{2,0},{3,1},{4,6},{5,7},{6,4},{7,5},{8,10},{9,11},{10,... | collective-permute-start | bytes 49160 | tf_op jit(solution)/shard_map/ppermute | solution.py:630
  91.3 7.6 %collective-permute-start.21 = (f32[64,64]{1,0:T(8,128)S(1)}, f32[64,64]{1,0:T(8,128)S(1)}, u32[]{:S(2)}, u32[]{:S(2)}) collective-permute-start(f32[64,64]{1,0:T(8,128)S(1)} %add.47), channel_id=1, source_target_pairs={{0,4},{1,5},{2,6},{3,7},{4,0},{5,1},{6,2},{7,3},{8,12},{9,13},{10,... | collective-permute-start | bytes 49160 | tf_op jit(solution)/shard_map/ppermute | solution.py:630
  98.9 2.0 %collective-permute-start.22 = (f32[4,64,512]{2,1,0:T(8,128)S(1)}, f32[4,64,512]{2,1,0:T(8,128)S(1)}, u32[]{:S(2)}, u32[]{:S(2)}) collective-permute-start(f32[4,64,512]{2,1,0:T(8,128)S(1)} %get-tuple-element.139), channel_id=1, source_target_pairs={{0,1},{1,0},{2,3},{3,2},{4,5},{5,4},{6,7},{7,6},{8,9},{9,8},{10,11... | collective-permute-start | bytes 1572872 | tf_op jit(solution)/shard_map/ppermute | solution.py:30
  101.0 13.0 %collective-permute-start.23 = (f32[2,64,512]{2,1,0:T(8,128)S(1)}, f32[2,64,512]{2,1,0:T(8,128)S(1)}, u32[]{:S(2)}, u32[]{:S(2)}) collective-permute-start(f32[2,64,512]{2,1,0:T(8,128)S(1)} %slice_add_fusion.1), channel_id=1, source_target_pairs={{0,2},{1,3},{2,0},{3,1},{4,6},{5,7},{6,4},{7,5},{8,10},{9,11},{10,... | collective-permute-start | bytes 786440 | tf_op jit(solution)/shard_map/ppermute | solution.py:30
  102.0 11.9 %collective-permute-start.24 = (f32[2,64,512]{2,1,0:T(8,128)S(1)}, f32[2,64,512]{2,1,0:T(8,128)S(1)}, u32[]{:S(2)}, u32[]{:S(2)}) collective-permute-start(f32[2,64,512]{2,1,0:T(8,128)S(1)} %get-tuple-element.145), channel_id=1, source_target_pairs={{0,4},{4,8},{8,12},{12,16},{16,20},{20,24},{24,28},{1,5},{5,9},{9,... | collective-permute-start | bytes 786440 | tf_op jit(solution)/shard_map/ppermute | solution.py:36
  103.7 4.5 %collective-permute-start.25 = (f32[64,64]{1,0:T(8,128)S(1)}, f32[64,64]{1,0:T(8,128)S(1)}, u32[]{:S(2)}, u32[]{:S(2)}) collective-permute-start(f32[64,64]{1,0:T(8,128)S(1)} %add.48), channel_id=1, source_target_pairs={{0,8},{1,9},{2,10},{3,11},{4,12},{5,13},{6,14},{7,15},{8,0},{9,1},... | collective-permute-start | bytes 49160 | tf_op jit(solution)/shard_map/ppermute | solution.py:630
  104.6 4.8 %collective-permute-start.26 = (f32[64,64]{1,0:T(8,128)S(1)}, f32[64,64]{1,0:T(8,128)S(1)}, u32[]{:S(2)}, u32[]{:S(2)}) collective-permute-start(f32[64,64]{1,0:T(8,128)S(1)} %add.48), channel_id=1, source_target_pairs={{0,16},{1,17},{2,18},{3,19},{4,20},{5,21},{6,22},{7,23},{8,24},{9,... | collective-permute-start | bytes 49160 | tf_op jit(solution)/shard_map/ppermute | solution.py:630
  104.6 5.9 %collective-permute-start.27 = (f32[64,64]{1,0:T(8,128)S(1)}, f32[64,64]{1,0:T(8,128)S(1)}, u32[]{:S(2)}, u32[]{:S(2)}) collective-permute-start(f32[64,64]{1,0:T(8,128)S(1)} %add.48), channel_id=1, source_target_pairs={{0,24},{1,25},{2,26},{3,27},{4,28},{5,29},{6,30},{7,31},{8,16},{9,... | collective-permute-start | bytes 49160 | tf_op jit(solution)/shard_map/ppermute | solution.py:630
  115.5 1.3 collective-permute-start.28
  116.7 4.6 %collective-permute-start.29 = (f32[64,64]{1,0:T(8,128)S(1)}, f32[64,64]{1,0:T(8,128)S(1)}, u32[]{:S(2)}, u32[]{:S(2)}) collective-permute-start(f32[64,64]{1,0:T(8,128)S(1)} %add.53), channel_id=1, source_target_pairs={{0,2},{1,3},{2,0},{3,1},{4,6},{5,7},{6,4},{7,5},{8,10},{9,11},{10,... | collective-permute-start | bytes 49160 | tf_op jit(solution)/shard_map/ppermute | solution.py:630
  117.6 5.4 %collective-permute-start.30 = (f32[64,64]{1,0:T(8,128)S(1)}, f32[64,64]{1,0:T(8,128)S(1)}, u32[]{:S(2)}, u32[]{:S(2)}) collective-permute-start(f32[64,64]{1,0:T(8,128)S(1)} %add.53), channel_id=1, source_target_pairs={{0,4},{1,5},{2,6},{3,7},{4,0},{5,1},{6,2},{7,3},{8,12},{9,13},{10,... | collective-permute-start | bytes 49160 | tf_op jit(solution)/shard_map/ppermute | solution.py:630
  121.1 4.8 %collective-permute-start.31 = (f32[64,64]{1,0:T(8,128)S(1)}, f32[64,64]{1,0:T(8,128)S(1)}, u32[]{:S(2)}, u32[]{:S(2)}) collective-permute-start(f32[64,64]{1,0:T(8,128)S(1)} %add.53), channel_id=1, source_target_pairs={{0,6},{1,7},{2,4},{3,5},{4,2},{5,3},{6,0},{7,1},{8,14},{9,15},{10,... | collective-permute-start | bytes 49160 | tf_op jit(solution)/shard_map/ppermute | solution.py:630
  125.9 4.5 %collective-permute-start.32 = (f32[64,64]{1,0:T(8,128)S(1)}, f32[64,64]{1,0:T(8,128)S(1)}, u32[]{:S(2)}, u32[]{:S(2)}) collective-permute-start(f32[64,64]{1,0:T(8,128)S(1)} %add_add_fusion.1), channel_id=1, source_target_pairs={{0,8},{1,9},{2,10},{3,11},{4,12},{5,13},{6,14},{7,15},{8,0},{9,1},... | collective-permute-start | bytes 49160 | tf_op jit(solution)/shard_map/ppermute | solution.py:630
  126.5 5.4 %collective-permute-start.33 = (f32[64,64]{1,0:T(8,128)S(1)}, f32[64,64]{1,0:T(8,128)S(1)}, u32[]{:S(2)}, u32[]{:S(2)}) collective-permute-start(f32[64,64]{1,0:T(8,128)S(1)} %add_add_fusion.1), channel_id=1, source_target_pairs={{0,16},{1,17},{2,18},{3,19},{4,20},{5,21},{6,22},{7,23},{8,24},{9,... | collective-permute-start | bytes 49160 | tf_op jit(solution)/shard_map/ppermute | solution.py:630
  130.0 5.7 %collective-permute-start.34 = (f32[64,64]{1,0:T(8,128)S(1)}, f32[64,64]{1,0:T(8,128)S(1)}, u32[]{:S(2)}, u32[]{:S(2)}) collective-permute-start(f32[64,64]{1,0:T(8,128)S(1)} %add_add_fusion.1), channel_id=1, source_target_pairs={{0,24},{1,25},{2,26},{3,27},{4,28},{5,29},{6,30},{7,31},{8,16},{9,... | collective-permute-start | bytes 49160 | tf_op jit(solution)/shard_map/ppermute | solution.py:630

commit v11 on v10

--- a/solution.py
+++ b/solution.py
@@ -726,11 +726,10 @@
     z, gram, parts, degree = scaled_gram(sums, vec, counts, None, None, True)
     for turn in range(1, ITERS):
         stages = sum_stages()
+        far_part = from_behind(parts, "blk", -1)
         crossed = gather_far_bits(parts)
         mate_part = swap(parts, "grp", 1)
         gram = all_sum(gram, stages[:1])
-        gram, far_part = lax.optimization_barrier((gram, parts))
-        far_part = from_behind(far_part, "blk", -1)
         at_home, *results = products(
             entries,
             (0,),
@@ -741,8 +740,8 @@
             columns,
             2,
         )
-        at_home, far_part, *tied = lax.optimization_barrier(
-            (at_home, far_part, *crossed.values())
+        gram, at_home, far_part, *tied = lax.optimization_barrier(
+            (gram, at_home, far_part, *crossed.values())
         )
         crossed = dict(zip(crossed, tied))
         vecs = beyond(window_of(parts, mate_part, crossed, far_part))
@@ -752,8 +751,9 @@
         results = products(entries, (1,), vecs, kept, results, urgent, columns, 2)
         gram = all_sum(gram, stages[2:3])
         gram, *results = lax.optimization_barrier((gram, *results))
+        gram = all_sum(gram, stages[3:4])
         sums, (at_home, gram) = send_urgent(results, (at_home, gram), group, blocks_dev)
-        gram = all_sum(gram, pairs_of(stages[3:]))
+        gram = all_sum(gram, stages[4:])
         sums = finish_home(entries, vecs, kept, at_home, blocks_dev, columns, 2) + sums
         inverse = factor(gram)
         z, gram, *parts = scaled_gram(sums, z, counts, degree, inverse, turn + 1 < ITERS)

time: 140 us -> 136 us (0.971); the launches traced: 139 us -> 138 us
  waiting for transfers between devices: 44.1 us -> 38.7 us
  starting transfers between devices: 36.2 us -> 38.8 us
  Pallas kernels: 55.7 us -> 57.2 us
    ppermute x16, waiting for transfers between devices: 12.9 us -> 7.57 us  [swap(): lax.ppermute(value, axis, [(source, source ^ bit) for source in range(cou...]
    ppermute x6, starting transfers between devices: 8.08 us -> 11.1 us  [from_behind(): lax.ppermute(value, axis, [(source, source + steps) for source in range(i...]
    ppermute x6, waiting for transfers between devices: 14.9 us -> 12.8 us  [from_behind(): lax.ppermute(value, axis, [(source, source + steps) for source in range(i...]
    ppermute x13 -> x12, waiting for transfers between devices: 16.3 us -> 18.4 us  [all_sum(): lax.ppermute(value, ('blk', 'grp'), [(source, source ^ move) for source i...]
    ppermute x16, starting transfers between devices: 9.95 us -> 8.32 us  [swap(): lax.ppermute(value, axis, [(source, source ^ bit) for source in range(cou...]
    pallas_call x6, Pallas kernels: 17.2 us -> 18.7 us  [products(): pl.pallas_call(kernel, out_shape=shapes, in_specs=[spec(SMEM)] * 4 + [spe...]
    ppermute x13 -> x12, starting transfers between devices: 18.2 us -> 19.4 us  [all_sum(): lax.ppermute(value, ('blk', 'grp'), [(source, source ^ move) for source i...]
  transfers between devices with their start and end apart: 35 -> 34, of which waited for: 15 -> 15; matrix products, arithmetic and copies ran while one was open for 1% -> 1% of each run, Pallas kernels for 33% -> 35%
where the time goes in v11:
time: 136 us; the launch traced here: 138 us
  Pallas kernels  57.2 us (42%)
  starting transfers between devices  38.8 us (29%)
  waiting for transfers between devices  38.7 us (28%)
  local copies, waits for them, and re-layouts  1.57 us (1%)
    ppermute x12, starting transfers between devices, all_sum(): lax.ppermute(value, ('blk', 'grp'), [(source, source ^ move) for source i...  19.4 us
    pallas_call x6, Pallas kernels, products(): pl.pallas_call(kernel, out_shape=shapes, in_specs=[spec(SMEM)] * 4 + [spe...  18.7 us
    ppermute x12, waiting for transfers between devices, all_sum(): lax.ppermute(value, ('blk', 'grp'), [(source, source ^ move) for source i...  18.4 us
    pallas_call x4, Pallas kernels, build_tiles(): pl.pallas_call(kernel, out_shape=shapes, in_specs=[spec(SMEM)] * len(scal...  16.2 us
    pallas_call x1, Pallas kernels, listing(): pl.pallas_call(functools.partial(listing_kernel, group, cap, blocks_dev),...  14.3 us
    ppermute x6, waiting for transfers between devices, from_behind(): lax.ppermute(value, axis, [(source, source + steps) for source in range(i...  12.8 us
    ppermute x6, starting transfers between devices, from_behind(): lax.ppermute(value, axis, [(source, source + steps) for source in range(i...  11.1 us
    ppermute x16, starting transfers between devices, swap(): lax.ppermute(value, axis, [(source, source ^ bit) for source in range(cou...  8.32 us
  transfers between devices with their start and end apart: 34, of which 15 were waited for; matrix products, arithmetic and copies ran while one was open for 1% of the time, Pallas kernels for 35%

profile of v11, /device:TPU:0, one launch (start us, length us, event | category | flops | bytes accessed | tf_op | source)
XLA Modules:
  0.0 137.6 jit_solution(8006500330739091309)
XLA Ops:
  0.0 0.5 collective-permute-start
  0.5 1.5 %fusion = (bf16[512,768]{1,0:T(8,128)(2,1)S(1)}, bf16[512,768]{1,0:T(8,128)(2,1)S(1)}) fusion(bf16[1024,768]{1,0:T(8,128)(2,1)} %refs_3_.1), kind=kLoop, calls=%fused_computation.5 | loop fusion | bytes 3145728 | tf_op jit(solution)/shard_map/slice | solution.py:653
  2.1 1.3 collective-permute-start.1
  3.4 2.7 %collective-permute-start.2 = (bf16[512,768]{1,0:T(8,128)(2,1)S(1)}, bf16[512,768]{1,0:T(8,128)(2,1)S(1)}, u32[]{:S(2)}, u32[]{:S(2)}) collective-permute-start(bf16[512,768]{1,0:T(8,128)(2,1)S(1)} %get-tuple-element.150), channel_id=1, source_target_pairs={{0,2},{1,3},{2,0},{3,1},{4,6},{5,7},{6,4},{7,5},{8,10},{9,11},{10,... | collective-permute-start | bytes 2359304 | tf_op jit(solution)/shard_map/ppermute | solution.py:30
  6.0 1.3 collective-permute-start.3
  7.3 0.1 collective-permute-start.7
  8.1 14.3 %listing.1 = (s32[16]{0:T(128)S(1)}, s32[16]{0:T(128)S(1)}, s32[4]{0:T(128)S(1)}, s32[32]{0:T(128)S(1)}, s32[32]{0:T(128)S(1)}, /*index=5*/s32[32]{0:T(128)S(1)}, s32[7]{0:T(128)S(1)}) custom-call(s32[64]{0:T(128)S(1)} %copy-done.3, s32[64]{0:T(128)S(1)} %copy-done.4, s32[1]{0:T(128)S(6)} %copy.29.live), custom_call_target="tpu_custom_call" | custom-call | flops 1048576 | bytes 1024 | tf_op jit(solution)/shard_map/listing/pallas_call | solution.py:214
  22.4 0.6 opening.1.refs_4_
  23.0 2.0 %collective-permute-done.1.refs_5_ = bf16[512,768]{1,0:T(8,128)(2,1)S(1)} collective-permute-done((bf16[512,768]{1,0:T(8,128)(2,1)S(1)}, bf16[512,768]{1,0:T(8,128)(2,1)S(1)}, u32[]{:S(2)}, u32[]{:S(2)}) %collective-permute-start.1) | collective-permute-done | bytes 786464 | tf_op jit(solution)/shard_map/ppermute | solution.py:36
  25.0 0.1 fusion.1
  25.0 0.1 collective-permute-start.5
  25.1 0.5 collective-permute-start.6
  25.6 0.1 collective-permute-start.4
  25.7 7.9 %first_tiles.1 = (bf16[5120,768]{1,0:T(8,128)(2,1)S(1)}, f32[10,8,512]{2,1,0:T(8,128)S(1)}, f32[8,512,128]{2,1,0:T(8,128)S(1)}, bf16[17,512,512]{2,1,0:T(8,128)(2,1)S(1)}) custom-call(s32[4]{0:T(128)S(1)} %get-tuple-element.85.refs_0_, s32[16]{0:T(128)S(1)} %get-tuple-element.86.refs_1_, s32[16]{0:T(128)S(1)} %get-tuple-element.87.refs_2_, ...), custom_call_target="tpu_custom_call" | custom-call | flops 1048576 | bytes 1048576 | tf_op jit(solution)/shard_map/first_tiles/pallas_call | solution.py:331
  33.6 0.1 pad_maximum_fusion.refs_3_
  33.7 1.0 second_tiles.1
  34.7 6.8 %collective-permute-done.3.refs_0_ = bf16[512,768]{1,0:T(8,128)(2,1)S(1)} collective-permute-done((bf16[512,768]{1,0:T(8,128)(2,1)S(1)}, bf16[512,768]{1,0:T(8,128)(2,1)S(1)}, u32[]{:S(2)}, u32[]{:S(2)}) %collective-permute-start.3) | collective-permute-done | bytes 786464 | tf_op jit(solution)/shard_map/ppermute | solution.py:36
  41.5 1.8 %collective-permute-start.9 = (bf16[80,1024]{1,0:T(8,128)(2,1)S(1)}, bf16[80,1024]{1,0:T(8,128)(2,1)S(1)}, u32[]{:S(2)}, u32[]{:S(2)}) collective-permute-start(bf16[80,1024]{1,0:T(8,128)(2,1)S(1)} %opening.1.refs_4_), channel_id=1, source_target_pairs={{0,2},{1,3},{2,0},{3,1},{4,6},{5,7},{6,4},{7,5},{8,10},{9,11},{10,... | collective-permute-start | bytes 491528 | tf_op jit(solution)/shard_map/ppermute | solution.py:30
  43.3 1.3 collective-permute-start.11
  44.6 0.8 more_blocks.1
  45.3 6.5 %last_tiles.1 = (bf16[5120,768]{1,0:T(8,128)(2,1)S(1)}, f32[10,8,512]{2,1,0:T(8,128)S(1)}, f32[8,512,128]{2,1,0:T(8,128)S(1)}, bf16[17,512,512]{2,1,0:T(8,128)(2,1)S(1)}) custom-call(s32[4]{0:T(128)S(1)} %get-tuple-element.85.refs_0_, s32[16]{0:T(128)S(1)} %get-tuple-element.86.refs_1_, ...), custom_call_target="tpu_custom_call", output_to_operand_aliasing={{0}: (4, {}), {1}: (5, {}), {2}: (6, {}), {3}: (7, {})} | custom-call | flops 4294967296 | bytes 1048576 | tf_op jit(solution)/shard_map/last_tiles/pallas_call | solution.py:331
  51.8 0.2 collective-permute-start.10
  52.1 3.0 %products.6 = (f32[2,72,512]{2,1,0:T(8,128)S(1)}, f32[4,72,512]{2,1,0:T(8,128)S(1)}, f32[2,72,512]{2,1,0:T(8,128)S(1)}, f32[2,72,512]{2,1,0:T(8,128)S(1)}) custom-call(s32[32]{0:T(128)S(1)} %get-tuple-element.77.refs_0_, s32[32]{0:T(128)S(1)} %get-tuple-element.78.refs_1_, s32[32]{0:T(128)S(1)} %get-tuple-element.79.refs_2_, ...), custom_call_target="tpu_custom_call" | custom-call | flops 1048576 | bytes 1048576 | tf_op jit(solution)/shard_map/products/pallas_call | solution.py:422
  55.1 4.0 %products.7 = (f32[4,72,512]{2,1,0:T(8,128)S(1)}, f32[2,72,512]{2,1,0:T(8,128)S(1)}, f32[2,72,512]{2,1,0:T(8,128)S(1)}) custom-call(s32[32]{0:T(128)S(1)} %get-tuple-element.77.refs_0_, s32[32]{0:T(128)S(1)} %get-tuple-element.78.refs_1_, s32[32]{0:T(128)S(1)} %get-tuple-element.79.refs_2_, s32[7]{0:T(128)S(1)} %get-tuple-element.80.refs_3_, ...), custom_call_target="tpu_custom_call" | custom-call | flops 2147483648 | bytes 1048576 | tf_op jit(solution)/shard_map/products/pallas_call | solution.py:422
  59.1 0.1 collective-permute-start.12
  59.2 2.0 %collective-permute-done.12.refs_1_ = f32[4,72,512]{2,1,0:T(8,128)S(1)} collective-permute-done((f32[4,72,512]{2,1,0:T(8,128)S(1)}, f32[4,72,512]{2,1,0:T(8,128)S(1)}, u32[]{:S(2)}, u32[]{:S(2)}) %collective-permute-start.12) | collective-permute-done | bytes 589856 | tf_op jit(solution)/shard_map/ppermute | solution.py:30
  61.3 0.1 collective-permute-start.13
  61.3 1.3 collective-permute-start.14
  62.7 2.2 %products.8.refs_0_ = f32[2,72,512]{2,1,0:T(8,128)S(1)} custom-call(s32[32]{0:T(128)S(1)} %get-tuple-element.77.refs_0_, s32[32]{0:T(128)S(1)} %get-tuple-element.78.refs_1_, s32[32]{0:T(128)S(1)} %get-tuple-element.79.refs_2_, s32[7]{0:T(128)S(1)} %get-tuple-element.80.refs_3_, bf16[80,1024]{1,0:T(8,128)(2,1)S(1)} %collective-permute-done.9.refs_4_, ...), custom_call_target="tpu_custom_call" | custom-call | flops 1048576 | bytes 1048576 | tf_op jit(solution)/shard_map/products/pallas_call | solution.py:422
  64.8 5.5 %collective-permute-done.13.refs_2_ = f32[2,72,512]{2,1,0:T(8,128)S(1)} collective-permute-done((f32[2,72,512]{2,1,0:T(8,128)S(1)}, f32[2,72,512]{2,1,0:T(8,128)S(1)}, u32[]{:S(2)}, u32[]{:S(2)}) %collective-permute-start.13) | collective-permute-done | bytes 294944 | tf_op jit(solution)/shard_map/ppermute | solution.py:30
  70.4 0.9 scaled_gram.2
  71.3 0.1 collective-permute-start.16
  71.4 1.3 collective-permute-start.17
  72.7 0.9 collective-permute-start.18
  73.6 0.2 collective-permute-start.15
  73.8 1.0 collective-permute-done.15
  74.8 3.1 %products.9 = (f32[2,64,512]{2,1,0:T(8,128)S(1)}, f32[4,64,512]{2,1,0:T(8,128)S(1)}, f32[2,64,512]{2,1,0:T(8,128)S(1)}, f32[2,64,512]{2,1,0:T(8,128)S(1)}) custom-call(s32[32]{0:T(128)S(1)} %get-tuple-element.77.refs_0_, s32[32]{0:T(128)S(1)} %get-tuple-element.78.refs_1_, s32[32]{0:T(128)S(1)} %get-tuple-element.79.refs_2_, ...), custom_call_target="tpu_custom_call" | custom-call | flops 1048576 | bytes 1048576 | tf_op jit(solution)/shard_map/products/pallas_call | solution.py:422
  78.0 4.0 %collective-permute-done.17.refs_6_ = bf16[128,1024]{1,0:T(8,128)(2,1)S(1)} collective-permute-done((bf16[128,1024]{1,0:T(8,128)(2,1)S(1)}, bf16[128,1024]{1,0:T(8,128)(2,1)S(1)}, u32[]{:S(2)}, u32[]{:S(2)}) %collective-permute-start.17) | collective-permute-done | bytes 262176 | tf_op jit(solution)/shard_map/ppermute | solution.py:36
  82.0 1.6 %collective-permute-start.19 = (f32[64,64]{1,0:T(8,128)S(1)}, f32[64,64]{1,0:T(8,128)S(1)}, u32[]{:S(2)}, u32[]{:S(2)}) collective-permute-start(f32[64,64]{1,0:T(8,128)S(1)} %add.43), channel_id=1, source_target_pairs={{0,2},{1,3},{2,0},{3,1},{4,6},{5,7},{6,4},{7,5},{8,10},{9,11},{10,... | collective-permute-start | bytes 49160 | tf_op jit(solution)/shard_map/ppermute | solution.py:630
  83.6 2.4 %collective-permute-done.19 = f32[64,64]{1,0:T(8,128)S(1)} collective-permute-done((f32[64,64]{1,0:T(8,128)S(1)}, f32[64,64]{1,0:T(8,128)S(1)}, u32[]{:S(2)}, u32[]{:S(2)}) %collective-permute-start.19) | collective-permute-done | bytes 16416 | tf_op jit(solution)/shard_map/ppermute | solution.py:630
  85.9 5.0 %collective-permute-start.21 = (f32[64,64]{1,0:T(8,128)S(1)}, f32[64,64]{1,0:T(8,128)S(1)}, u32[]{:S(2)}, u32[]{:S(2)}) collective-permute-start(f32[64,64]{1,0:T(8,128)S(1)} %add.44), channel_id=1, source_target_pairs={{0,4},{1,5},{2,6},{3,7},{4,0},{5,1},{6,2},{7,3},{8,12},{9,13},{10,... | collective-permute-start | bytes 49160 | tf_op jit(solution)/shard_map/ppermute | solution.py:630
  90.9 4.1 %products.10 = (f32[4,64,512]{2,1,0:T(8,128)S(1)}, f32[2,64,512]{2,1,0:T(8,128)S(1)}, f32[2,64,512]{2,1,0:T(8,128)S(1)}) custom-call(s32[32]{0:T(128)S(1)} %get-tuple-element.77.refs_0_, s32[32]{0:T(128)S(1)} %get-tuple-element.78.refs_1_, s32[32]{0:T(128)S(1)} %get-tuple-element.79.refs_2_, s32[7]{0:T(128)S(1)} %get-tuple-element.80.refs_3_, ...), custom_call_target="tpu_custom_call" | custom-call | flops 2147483648 | bytes 1048576 | tf_op jit(solution)/shard_map/products/pallas_call | solution.py:422
  95.1 0.1 collective-permute-start.22
  95.2 1.7 %collective-permute-start.23 = (f32[64,64]{1,0:T(8,128)S(1)}, f32[64,64]{1,0:T(8,128)S(1)}, u32[]{:S(2)}, u32[]{:S(2)}) collective-permute-start(f32[64,64]{1,0:T(8,128)S(1)} %add.45), channel_id=1, source_target_pairs={{0,8},{1,9},{2,10},{3,11},{4,12},{5,13},{6,14},{7,15},{8,0},{9,1},... | collective-permute-start | bytes 49160 | tf_op jit(solution)/shard_map/ppermute | solution.py:630
  96.8 2.3 %collective-permute-done.23 = f32[64,64]{1,0:T(8,128)S(1)} collective-permute-done((f32[64,64]{1,0:T(8,128)S(1)}, f32[64,64]{1,0:T(8,128)S(1)}, u32[]{:S(2)}, u32[]{:S(2)}) %collective-permute-start.23) | collective-permute-done | bytes 16416 | tf_op jit(solution)/shard_map/ppermute | solution.py:630
  99.2 1.2 collective-permute-start.24
  100.4 4.7 %collective-permute-start.25 = (f32[2,64,512]{2,1,0:T(8,128)S(1)}, f32[2,64,512]{2,1,0:T(8,128)S(1)}, u32[]{:S(2)}, u32[]{:S(2)}) collective-permute-start(f32[2,64,512]{2,1,0:T(8,128)S(1)} %get-tuple-element.143), channel_id=1, source_target_pairs={{0,4},{4,8},{8,12},{12,16},{16,20},{20,24},{24,28},{1,5},{5,9},{9,... | collective-permute-start | bytes 786440 | tf_op jit(solution)/shard_map/ppermute | solution.py:36
  105.1 1.3 collective-permute-start.26
  106.4 3.6 %collective-permute-done.26 = f32[64,64]{1,0:T(8,128)S(1)} collective-permute-done((f32[64,64]{1,0:T(8,128)S(1)}, f32[64,64]{1,0:T(8,128)S(1)}, u32[]{:S(2)}, u32[]{:S(2)}) %collective-permute-start.26) | collective-permute-done | bytes 16416 | tf_op jit(solution)/shard_map/ppermute | solution.py:630
  110.0 2.3 %products.11.refs_0_ = f32[2,64,512]{2,1,0:T(8,128)S(1)} custom-call(s32[32]{0:T(128)S(1)} %get-tuple-element.77.refs_0_, s32[32]{0:T(128)S(1)} %get-tuple-element.78.refs_1_, s32[32]{0:T(128)S(1)} %get-tuple-element.79.refs_2_, s32[7]{0:T(128)S(1)} %get-tuple-element.80.refs_3_, bf16[128,1024]{1,0:T(8,128)(2,1)S(1)} %collective-permute-done.18.refs_4_, ...), custom_call_target="tpu_custom_call" | custom-call | flops 1048576 | bytes 1048576 | tf_op jit(solution)/shard_map/products/pallas_call | solution.py:422
  112.3 2.0 %factor.1.refs_6_ = f32[64,64]{1,0:T(8,128)S(1)} custom-call(f32[64,64]{1,0:T(8,128)S(1)} %add.48.gram), custom_call_target="tpu_custom_call" | custom-call | flops 65536 | bytes 65536 | tf_op jit(solution)/shard_map/factor/pallas_call | solution.py:586
  114.2 1.5 %scaled_gram.3 = (f32[64,1024]{1,0:T(8,128)S(1)}, f32[64,64]{1,0:T(8,128)S(1)}) custom-call(s32[2]{0:T(128)S(1)} %copy-done.2, f32[2,64,512]{2,1,0:T(8,128)S(1)} %products.11.refs_0_, f32[4,64,512]{2,1,0:T(8,128)S(1)} %collective-permute-done.22.refs_1_, f32[2,64,512]{2,1,0:T(8,128)S(1)} %collective-permute-done.24.refs_2_, ...), custom_call_target="tpu_custom_call" | custom-call | flops 67108864 | bytes 2097152 | tf_op jit(solution)/shard_map/scaled_gram/pallas_call | solution.py:527
  115.8 0.1 collective-permute-start.27
  115.8 1.2 collective-permute-done.27
  117.1 0.9 collective-permute-start.29
  117.9 2.6 %collective-permute-start.30 = (f32[64,64]{1,0:T(8,128)S(1)}, f32[64,64]{1,0:T(8,128)S(1)}, u32[]{:S(2)}, u32[]{:S(2)}) collective-permute-start(f32[64,64]{1,0:T(8,128)S(1)} %add.49), channel_id=1, source_target_pairs={{0,6},{1,7},{2,4},{3,5},{4,2},{5,3},{6,0},{7,1},{8,14},{9,15},{10,... | collective-permute-start | bytes 49160 | tf_op jit(solution)/shard_map/ppermute | solution.py:630
  120.5 0.4 collective-permute-done.28
  121.0 0.1 collective-permute-done.29
  121.0 1.7 %collective-permute-done.30 = f32[64,64]{1,0:T(8,128)S(1)} collective-permute-done((f32[64,64]{1,0:T(8,128)S(1)}, f32[64,64]{1,0:T(8,128)S(1)}, u32[]{:S(2)}, u32[]{:S(2)}) %collective-permute-start.30) | collective-permute-done | bytes 16416 | tf_op jit(solution)/shard_map/ppermute | solution.py:630
  122.8 3.4 %collective-permute-start.31 = (f32[64,64]{1,0:T(8,128)S(1)}, f32[64,64]{1,0:T(8,128)S(1)}, u32[]{:S(2)}, u32[]{:S(2)}) collective-permute-start(f32[64,64]{1,0:T(8,128)S(1)} %add_add_fusion.1), channel_id=1, source_target_pairs={{0,8},{1,9},{2,10},{3,11},{4,12},{5,13},{6,14},{7,15},{8,0},{9,1},... | collective-permute-start | bytes 49160 | tf_op jit(solution)/shard_map/ppermute | solution.py:630
  126.1 2.7 %collective-permute-start.32 = (f32[64,64]{1,0:T(8,128)S(1)}, f32[64,64]{1,0:T(8,128)S(1)}, u32[]{:S(2)}, u32[]{:S(2)}) collective-permute-start(f32[64,64]{1,0:T(8,128)S(1)} %add_add_fusion.1), channel_id=1, source_target_pairs={{0,16},{1,17},{2,18},{3,19},{4,20},{5,21},{6,22},{7,23},{8,24},{9,... | collective-permute-start | bytes 49160 | tf_op jit(solution)/shard_map/ppermute | solution.py:630
  128.8 2.1 %collective-permute-done.32 = f32[64,64]{1,0:T(8,128)S(1)} collective-permute-done((f32[64,64]{1,0:T(8,128)S(1)}, f32[64,64]{1,0:T(8,128)S(1)}, u32[]{:S(2)}, u32[]{:S(2)}) %collective-permute-start.32) | collective-permute-done | bytes 16416 | tf_op jit(solution)/shard_map/ppermute | solution.py:630
  130.9 3.6 %collective-permute-done.33 = f32[64,64]{1,0:T(8,128)S(1)} collective-permute-done((f32[64,64]{1,0:T(8,128)S(1)}, f32[64,64]{1,0:T(8,128)S(1)}, u32[]{:S(2)}, u32[]{:S(2)}) %collective-permute-start.33) | collective-permute-done | bytes 16416 | tf_op jit(solution)/shard_map/ppermute | solution.py:630
  134.5 3.0 %embedding.1 = f32[64,1024]{1,0:T(8,128)} custom-call(f32[64,64]{1,0:T(8,128)S(1)} %add_add_fusion.gram, f32[64,1024]{1,0:T(8,128)S(1)} %get-tuple-element.148.z), custom_call_target="tpu_custom_call" | custom-call | flops 1073741824 | bytes 1048576 | tf_op jit(solution)/shard_map/embedding/pallas_call | solution.py:604
  (43 shorter events, 0.2 us)
Async XLA Ops:
  0.0 25.7 %copy-start = (bf16[1024,768]{1,0:T(8,128)(2,1)S(1)}, bf16[1024,768]{1,0:T(8,128)(2,1)}, u32[]{:S(2)}) copy-start(bf16[1024,768]{1,0:T(8,128)(2,1)} %refs_3_.1) | copy-start | bytes 4718596
  0.0 8.1 %copy-start.3 = (s32[64]{0:T(128)S(1)}, s32[64]{0:T(128)}, u32[]{:S(2)}) copy-start(s32[64]{0:T(128)} %rows.1) | copy-start | bytes 772
  0.0 8.1 %copy-start.4 = (s32[64]{0:T(128)S(1)}, s32[64]{0:T(128)}, u32[]{:S(2)}) copy-start(s32[64]{0:T(128)} %cols.1) | copy-start | bytes 772
  0.0 22.4 %copy-start.1 = (f32[64,1024]{1,0:T(8,128)S(1)}, f32[64,1024]{1,0:T(8,128)}, u32[]{:S(2)}) copy-start(f32[64,1024]{1,0:T(8,128)} %start) | copy-start | bytes 786436
  0.0 22.4 %copy-start.2 = (s32[2]{0:T(128)S(1)}, s32[2]{0:T(128)}, u32[]{:S(2)}) copy-start(s32[2]{0:T(128)} %count_ref.3) | copy-start | bytes 28
  0.0 22.4 %collective-permute-start = (bf16[1024,768]{1,0:T(8,128)(2,1)}, bf16[1024,768]{1,0:T(8,128)(2,1)S(1)}, u32[]{:S(2)}, u32[]{:S(2)}) collective-permute-start(bf16[1024,768]{1,0:T(8,128)(2,1)} %refs_3_.1), channel_id=1, source_target_pairs={{0,1},{1,0},{2,3},{3,2},{4,5},{5,4},{6,7},{7,6},{8,9},{9,8},{10,11... | collective-permute-start | bytes 4718600 | tf_op jit(solution)/shard_map/ppermute | solution.py:30
  2.1 22.9 %collective-permute-start.1 = (bf16[512,768]{1,0:T(8,128)(2,1)S(1)}, bf16[512,768]{1,0:T(8,128)(2,1)S(1)}, u32[]{:S(2)}, u32[]{:S(2)}) collective-permute-start(bf16[512,768]{1,0:T(8,128)(2,1)S(1)} %get-tuple-element.150), channel_id=1, source_target_pairs={{4,0},{8,4},{12,8},{16,12},{20,16},{24,20},{28,24},{5,1},{9,5},{13... | collective-permute-start | bytes 2359304 | tf_op jit(solution)/shard_map/ppermute | solution.py:36
  3.4 21.6 %collective-permute-start.2 = (bf16[512,768]{1,0:T(8,128)(2,1)S(1)}, bf16[512,768]{1,0:T(8,128)(2,1)S(1)}, u32[]{:S(2)}, u32[]{:S(2)}) collective-permute-start(bf16[512,768]{1,0:T(8,128)(2,1)S(1)} %get-tuple-element.150), channel_id=1, source_target_pairs={{0,2},{1,3},{2,0},{3,1},{4,6},{5,7},{6,4},{7,5},{8,10},{9,11},{10,... | collective-permute-start | bytes 2359304 | tf_op jit(solution)/shard_map/ppermute | solution.py:30
  6.0 35.5 %collective-permute-start.3 = (bf16[512,768]{1,0:T(8,128)(2,1)S(1)}, bf16[512,768]{1,0:T(8,128)(2,1)S(1)}, u32[]{:S(2)}, u32[]{:S(2)}) collective-permute-start(bf16[512,768]{1,0:T(8,128)(2,1)S(1)} %get-tuple-element.149), channel_id=1, source_target_pairs={{4,0},{8,4},{12,8},{16,12},{20,16},{24,20},{28,24},{5,1},{9,5},{13... | collective-permute-start | bytes 2359304 | tf_op jit(solution)/shard_map/ppermute | solution.py:36
  7.3 34.2 %collective-permute-start.7 = (bf16[512,768]{1,0:T(8,128)(2,1)S(1)}, bf16[512,768]{1,0:T(8,128)(2,1)S(1)}, u32[]{:S(2)}, u32[]{:S(2)}) collective-permute-start(bf16[512,768]{1,0:T(8,128)(2,1)S(1)} %get-tuple-element.149), channel_id=1, source_target_pairs={{0,2},{1,3},{2,0},{3,1},{4,6},{5,7},{6,4},{7,5},{8,10},{9,11},{10,... | collective-permute-start | bytes 2359304 | tf_op jit(solution)/shard_map/ppermute | solution.py:30
  25.0 8.6 %collective-permute-start.5 = (bf16[256,768]{1,0:T(8,128)(2,1)S(1)}, bf16[256,768]{1,0:T(8,128)(2,1)S(1)}, u32[]{:S(2)}, u32[]{:S(2)}) collective-permute-start(bf16[256,768]{1,0:T(8,128)(2,1)S(1)} %get-tuple-element.151), channel_id=1, source_target_pairs={{0,1},{1,0},{2,3},{3,2},{4,5},{5,4},{6,7},{7,6},{8,9},{9,8},{10,11... | collective-permute-start | bytes 1179656 | tf_op jit(solution)/shard_map/ppermute | solution.py:30
  25.1 8.5 %collective-permute-start.6 = (bf16[256,768]{1,0:T(8,128)(2,1)S(1)}, bf16[256,768]{1,0:T(8,128)(2,1)S(1)}, u32[]{:S(2)}, u32[]{:S(2)}) collective-permute-start(bf16[256,768]{1,0:T(8,128)(2,1)S(1)} %get-tuple-element.152), channel_id=1, source_target_pairs={{0,1},{1,0},{2,3},{3,2},{4,5},{5,4},{6,7},{7,6},{8,9},{9,8},{10,11... | collective-permute-start | bytes 1179656 | tf_op jit(solution)/shard_map/ppermute | solution.py:30
  25.6 15.9 %collective-permute-start.4 = (bf16[80,1024]{1,0:T(8,128)(2,1)S(1)}, bf16[80,1024]{1,0:T(8,128)(2,1)S(1)}, u32[]{:S(2)}, u32[]{:S(2)}) collective-permute-start(bf16[80,1024]{1,0:T(8,128)(2,1)S(1)} %opening.1.refs_4_), channel_id=1, source_target_pairs={{0,1},{1,0},{2,3},{3,2},{4,5},{5,4},{6,7},{7,6},{8,9},{9,8},{10,11... | collective-permute-start | bytes 491528 | tf_op jit(solution)/shard_map/ppermute | solution.py:30
  41.5 3.8 %collective-permute-start.8 = (bf16[512,768]{1,0:T(8,128)(2,1)S(1)}, bf16[512,768]{1,0:T(8,128)(2,1)S(1)}, u32[]{:S(2)}, u32[]{:S(2)}) collective-permute-start(bf16[512,768]{1,0:T(8,128)(2,1)S(1)} %collective-permute-done.7.refs_1_), channel_id=1, source_target_pairs={{0,1},{1,0},{2,3},{3,2},{4,5},{5,4},{6,7},{7,6},{8,9},{9,8},{10,11... | collective-permute-start | bytes 2359304 | tf_op jit(solution)/shard_map/ppermute | solution.py:30
  41.5 10.3 %collective-permute-start.9 = (bf16[80,1024]{1,0:T(8,128)(2,1)S(1)}, bf16[80,1024]{1,0:T(8,128)(2,1)S(1)}, u32[]{:S(2)}, u32[]{:S(2)}) collective-permute-start(bf16[80,1024]{1,0:T(8,128)(2,1)S(1)} %opening.1.refs_4_), channel_id=1, source_target_pairs={{0,2},{1,3},{2,0},{3,1},{4,6},{5,7},{6,4},{7,5},{8,10},{9,11},{10,... | collective-permute-start | bytes 491528 | tf_op jit(solution)/shard_map/ppermute | solution.py:30
  43.3 11.8 %collective-permute-start.11 = (bf16[80,1024]{1,0:T(8,128)(2,1)S(1)}, bf16[80,1024]{1,0:T(8,128)(2,1)S(1)}, u32[]{:S(2)}, u32[]{:S(2)}) collective-permute-start(bf16[80,1024]{1,0:T(8,128)(2,1)S(1)} %opening.1.refs_4_), channel_id=1, source_target_pairs={{4,0},{8,4},{12,8},{16,12},{20,16},{24,20},{28,24},{5,1},{9,5},{13... | collective-permute-start | bytes 491528 | tf_op jit(solution)/shard_map/ppermute | solution.py:36
  51.8 3.3 %collective-permute-start.10 = (bf16[80,1024]{1,0:T(8,128)(2,1)S(1)}, bf16[80,1024]{1,0:T(8,128)(2,1)S(1)}, u32[]{:S(2)}, u32[]{:S(2)}) collective-permute-start(bf16[80,1024]{1,0:T(8,128)(2,1)S(1)} %collective-permute-done.9.refs_4_), channel_id=1, source_target_pairs={{0,1},{1,0},{2,3},{3,2},{4,5},{5,4},{6,7},{7,6},{8,9},{9,8},{10,11... | collective-permute-start | bytes 491528 | tf_op jit(solution)/shard_map/ppermute | solution.py:30
  59.1 2.1 %collective-permute-start.12 = (f32[4,72,512]{2,1,0:T(8,128)S(1)}, f32[4,72,512]{2,1,0:T(8,128)S(1)}, u32[]{:S(2)}, u32[]{:S(2)}) collective-permute-start(f32[4,72,512]{2,1,0:T(8,128)S(1)} %get-tuple-element.114), channel_id=1, source_target_pairs={{0,1},{1,0},{2,3},{3,2},{4,5},{5,4},{6,7},{7,6},{8,9},{9,8},{10,11... | collective-permute-start | bytes 1769480 | tf_op jit(solution)/shard_map/ppermute | solution.py:30
  61.3 9.1 %collective-permute-start.13 = (f32[2,72,512]{2,1,0:T(8,128)S(1)}, f32[2,72,512]{2,1,0:T(8,128)S(1)}, u32[]{:S(2)}, u32[]{:S(2)}) collective-permute-start(f32[2,72,512]{2,1,0:T(8,128)S(1)} %slice_add_fusion), channel_id=1, source_target_pairs={{0,2},{1,3},{2,0},{3,1},{4,6},{5,7},{6,4},{7,5},{8,10},{9,11},{10,... | collective-permute-start | bytes 884744 | tf_op jit(solution)/shard_map/ppermute | solution.py:30
  61.3 9.0 %collective-permute-start.14 = (f32[2,72,512]{2,1,0:T(8,128)S(1)}, f32[2,72,512]{2,1,0:T(8,128)S(1)}, u32[]{:S(2)}, u32[]{:S(2)}) collective-permute-start(f32[2,72,512]{2,1,0:T(8,128)S(1)} %get-tuple-element.119), channel_id=1, source_target_pairs={{0,4},{4,8},{8,12},{12,16},{16,20},{20,24},{24,28},{1,5},{5,9},{9,... | collective-permute-start | bytes 884744 | tf_op jit(solution)/shard_map/ppermute | solution.py:36
  71.3 3.5 %collective-permute-start.16 = (bf16[128,1024]{1,0:T(8,128)(2,1)S(1)}, bf16[128,1024]{1,0:T(8,128)(2,1)S(1)}, u32[]{:S(2)}, u32[]{:S(2)}) collective-permute-start(bf16[128,1024]{1,0:T(8,128)(2,1)S(1)} %get-tuple-element.121.refs_4_), channel_id=1, source_target_pairs={{0,1},{1,0},{2,3},{3,2},{4,5},{5,4},{6,7},{7,6},{8,9},{9,8},{10,11... | collective-permute-start | bytes 786440 | tf_op jit(solution)/shard_map/ppermute | solution.py:30
  71.4 10.6 %collective-permute-start.17 = (bf16[128,1024]{1,0:T(8,128)(2,1)S(1)}, bf16[128,1024]{1,0:T(8,128)(2,1)S(1)}, u32[]{:S(2)}, u32[]{:S(2)}) collective-permute-start(bf16[128,1024]{1,0:T(8,128)(2,1)S(1)} %get-tuple-element.121.refs_4_), channel_id=1, source_target_pairs={{4,0},{8,4},{12,8},{16,12},{20,16},{24,20},{28,24},{5,1},{9,5},{13... | collective-permute-start | bytes 786440 | tf_op jit(solution)/shard_map/ppermute | solution.py:36
  72.7 9.3 %collective-permute-start.18 = (bf16[128,1024]{1,0:T(8,128)(2,1)S(1)}, bf16[128,1024]{1,0:T(8,128)(2,1)S(1)}, u32[]{:S(2)}, u32[]{:S(2)}) collective-permute-start(bf16[128,1024]{1,0:T(8,128)(2,1)S(1)} %get-tuple-element.121.refs_4_), channel_id=1, source_target_pairs={{0,2},{1,3},{2,0},{3,1},{4,6},{5,7},{6,4},{7,5},{8,10},{9,11},{10,... | collective-permute-start | bytes 786440 | tf_op jit(solution)/shard_map/ppermute | solution.py:30
  73.6 1.2 collective-permute-start.15
  82.0 3.9 %collective-permute-start.20 = (bf16[128,1024]{1,0:T(8,128)(2,1)S(1)}, bf16[128,1024]{1,0:T(8,128)(2,1)S(1)}, u32[]{:S(2)}, u32[]{:S(2)}) collective-permute-start(bf16[128,1024]{1,0:T(8,128)(2,1)S(1)} %collective-permute-done.18.refs_4_), channel_id=1, source_target_pairs={{0,1},{1,0},{2,3},{3,2},{4,5},{5,4},{6,7},{7,6},{8,9},{9,8},{10,11... | collective-permute-start | bytes 786440 | tf_op jit(solution)/shard_map/ppermute | solution.py:30
  82.0 3.9 %collective-permute-start.19 = (f32[64,64]{1,0:T(8,128)S(1)}, f32[64,64]{1,0:T(8,128)S(1)}, u32[]{:S(2)}, u32[]{:S(2)}) collective-permute-start(f32[64,64]{1,0:T(8,128)S(1)} %add.43), channel_id=1, source_target_pairs={{0,2},{1,3},{2,0},{3,1},{4,6},{5,7},{6,4},{7,5},{8,10},{9,11},{10,... | collective-permute-start | bytes 49160 | tf_op jit(solution)/shard_map/ppermute | solution.py:630
  85.9 9.1 %collective-permute-start.21 = (f32[64,64]{1,0:T(8,128)S(1)}, f32[64,64]{1,0:T(8,128)S(1)}, u32[]{:S(2)}, u32[]{:S(2)}) collective-permute-start(f32[64,64]{1,0:T(8,128)S(1)} %add.44), channel_id=1, source_target_pairs={{0,4},{1,5},{2,6},{3,7},{4,0},{5,1},{6,2},{7,3},{8,12},{9,13},{10,... | collective-permute-start | bytes 49160 | tf_op jit(solution)/shard_map/ppermute | solution.py:630
  95.1 4.1 %collective-permute-start.22 = (f32[4,64,512]{2,1,0:T(8,128)S(1)}, f32[4,64,512]{2,1,0:T(8,128)S(1)}, u32[]{:S(2)}, u32[]{:S(2)}) collective-permute-start(f32[4,64,512]{2,1,0:T(8,128)S(1)} %get-tuple-element.137), channel_id=1, source_target_pairs={{0,1},{1,0},{2,3},{3,2},{4,5},{5,4},{6,7},{7,6},{8,9},{9,8},{10,11... | collective-permute-start | bytes 1572872 | tf_op jit(solution)/shard_map/ppermute | solution.py:30
  95.2 4.0 %collective-permute-start.23 = (f32[64,64]{1,0:T(8,128)S(1)}, f32[64,64]{1,0:T(8,128)S(1)}, u32[]{:S(2)}, u32[]{:S(2)}) collective-permute-start(f32[64,64]{1,0:T(8,128)S(1)} %add.45), channel_id=1, source_target_pairs={{0,8},{1,9},{2,10},{3,11},{4,12},{5,13},{6,14},{7,15},{8,0},{9,1},... | collective-permute-start | bytes 49160 | tf_op jit(solution)/shard_map/ppermute | solution.py:630
  99.2 15.0 %collective-permute-start.24 = (f32[2,64,512]{2,1,0:T(8,128)S(1)}, f32[2,64,512]{2,1,0:T(8,128)S(1)}, u32[]{:S(2)}, u32[]{:S(2)}) collective-permute-start(f32[2,64,512]{2,1,0:T(8,128)S(1)} %slice_add_fusion.1), channel_id=1, source_target_pairs={{0,2},{1,3},{2,0},{3,1},{4,6},{5,7},{6,4},{7,5},{8,10},{9,11},{10,... | collective-permute-start | bytes 786440 | tf_op jit(solution)/shard_map/ppermute | solution.py:30
  100.4 13.8 %collective-permute-start.25 = (f32[2,64,512]{2,1,0:T(8,128)S(1)}, f32[2,64,512]{2,1,0:T(8,128)S(1)}, u32[]{:S(2)}, u32[]{:S(2)}) collective-permute-start(f32[2,64,512]{2,1,0:T(8,128)S(1)} %get-tuple-element.143), channel_id=1, source_target_pairs={{0,4},{4,8},{8,12},{12,16},{16,20},{20,24},{24,28},{1,5},{5,9},{9,... | collective-permute-start | bytes 786440 | tf_op jit(solution)/shard_map/ppermute | solution.py:36
  105.1 4.9 %collective-permute-start.26 = (f32[64,64]{1,0:T(8,128)S(1)}, f32[64,64]{1,0:T(8,128)S(1)}, u32[]{:S(2)}, u32[]{:S(2)}) collective-permute-start(f32[64,64]{1,0:T(8,128)S(1)} %add.47), channel_id=1, source_target_pairs={{0,16},{1,17},{2,18},{3,19},{4,20},{5,21},{6,22},{7,23},{8,24},{9,... | collective-permute-start | bytes 49160 | tf_op jit(solution)/shard_map/ppermute | solution.py:630
  115.8 1.3 collective-permute-start.27
  117.0 3.9 %collective-permute-start.28 = (f32[64,64]{1,0:T(8,128)S(1)}, f32[64,64]{1,0:T(8,128)S(1)}, u32[]{:S(2)}, u32[]{:S(2)}) collective-permute-start(f32[64,64]{1,0:T(8,128)S(1)} %add.49), channel_id=1, source_target_pairs={{0,2},{1,3},{2,0},{3,1},{4,6},{5,7},{6,4},{7,5},{8,10},{9,11},{10,... | collective-permute-start | bytes 49160 | tf_op jit(solution)/shard_map/ppermute | solution.py:630
  117.1 4.0 %collective-permute-start.29 = (f32[64,64]{1,0:T(8,128)S(1)}, f32[64,64]{1,0:T(8,128)S(1)}, u32[]{:S(2)}, u32[]{:S(2)}) collective-permute-start(f32[64,64]{1,0:T(8,128)S(1)} %add.49), channel_id=1, source_target_pairs={{0,4},{1,5},{2,6},{3,7},{4,0},{5,1},{6,2},{7,3},{8,12},{9,13},{10,... | collective-permute-start | bytes 49160 | tf_op jit(solution)/shard_map/ppermute | solution.py:630
  117.9 4.8 %collective-permute-start.30 = (f32[64,64]{1,0:T(8,128)S(1)}, f32[64,64]{1,0:T(8,128)S(1)}, u32[]{:S(2)}, u32[]{:S(2)}) collective-permute-start(f32[64,64]{1,0:T(8,128)S(1)} %add.49), channel_id=1, source_target_pairs={{0,6},{1,7},{2,4},{3,5},{4,2},{5,3},{6,0},{7,1},{8,14},{9,15},{10,... | collective-permute-start | bytes 49160 | tf_op jit(solution)/shard_map/ppermute | solution.py:630
  122.8 6.1 %collective-permute-start.31 = (f32[64,64]{1,0:T(8,128)S(1)}, f32[64,64]{1,0:T(8,128)S(1)}, u32[]{:S(2)}, u32[]{:S(2)}) collective-permute-start(f32[64,64]{1,0:T(8,128)S(1)} %add_add_fusion.1), channel_id=1, source_target_pairs={{0,8},{1,9},{2,10},{3,11},{4,12},{5,13},{6,14},{7,15},{8,0},{9,1},... | collective-permute-start | bytes 49160 | tf_op jit(solution)/shard_map/ppermute | solution.py:630
  126.1 4.8 %collective-permute-start.32 = (f32[64,64]{1,0:T(8,128)S(1)}, f32[64,64]{1,0:T(8,128)S(1)}, u32[]{:S(2)}, u32[]{:S(2)}) collective-permute-start(f32[64,64]{1,0:T(8,128)S(1)} %add_add_fusion.1), channel_id=1, source_target_pairs={{0,16},{1,17},{2,18},{3,19},{4,20},{5,21},{6,22},{7,23},{8,24},{9,... | collective-permute-start | bytes 49160 | tf_op jit(solution)/shard_map/ppermute | solution.py:630
  128.8 5.7 %collective-permute-start.33 = (f32[64,64]{1,0:T(8,128)S(1)}, f32[64,64]{1,0:T(8,128)S(1)}, u32[]{:S(2)}, u32[]{:S(2)}) collective-permute-start(f32[64,64]{1,0:T(8,128)S(1)} %add_add_fusion.1), channel_id=1, source_target_pairs={{0,24},{1,25},{2,26},{3,27},{4,28},{5,29},{6,30},{7,31},{8,16},{9,... | collective-permute-start | bytes 49160 | tf_op jit(solution)/shard_map/ppermute | solution.py:630

commit v12 on v11

--- a/solution.py
+++ b/solution.py
@@ -448,6 +448,7 @@
     final = []
     *messages, far = results
     parts = {}
+    behind = None
     for bit, message in zip(bits_of(group), messages):
         rels = [rel for rel in range(group) if rel & bit and rel % bit == 0]
         for index, rel in enumerate(rels):
@@ -457,14 +458,19 @@
                     index * blocks_dev : (index + 1) * blocks_dev
                 ].add(parts[rel])
         if bit > 1:
-            message, far, *later = lax.optimization_barrier((message, far, *later))
+            message, *later = lax.optimization_barrier((message, *later))
         got = swap(message, "grp", bit)
+        if behind is None:
+            got, far = lax.optimization_barrier((got, far))
+            behind = from_behind(far, "blk", 1)
         final.append(got)
         for index, rel in enumerate(rels):
             if rel ^ bit:
                 piece = got[index * blocks_dev : (index + 1) * blocks_dev]
                 parts[rel ^ bit] = parts[rel ^ bit] + piece if rel ^ bit in parts else piece
-    return final + [from_behind(far, "blk", 1)], later
+    if behind is None:
+        behind = from_behind(far, "blk", 1)
+    return [behind] + final, later
 
 
 def finish_home(entries, vecs, tiles, start, blocks_dev, height, folds):
@@ -620,7 +626,7 @@
     return [bits[first : first + 2] for first in range(0, len(bits), 2)]
 
 
-def all_sum(value, stages):
+def all_sum(value, stages, beside=None):
     count = lax.axis_size("blk") * lax.axis_size("grp")
     for bits in stages:
         moves = [0]
@@ -630,10 +636,12 @@
             lax.ppermute(value, ("blk", "grp"), [(source, source ^ move) for source in range(count)])
             for move in moves[1:]
         ]
+        if beside is not None:
+            terms[0], beside = lax.optimization_barrier((terms[0], beside))
         while len(terms) > 1:
             terms = [left + right for left, right in zip(terms[::2], terms[1::2])]
         value = terms[0]
-    return value
+    return value if beside is None else (value, beside)
 
 
 def per_device(points, counts, pair_rows, pair_cols, pair_live, start):
@@ -740,9 +748,7 @@
             columns,
             2,
         )
-        gram, at_home, far_part, *tied = lax.optimization_barrier(
-            (gram, at_home, far_part, *crossed.values())
-        )
+        gram, at_home, *tied = lax.optimization_barrier((gram, at_home, *crossed.values()))
         crossed = dict(zip(crossed, tied))
         vecs = beyond(window_of(parts, mate_part, crossed, far_part))
         gram = all_sum(gram, stages[1:2])
@@ -753,8 +759,10 @@
         gram, *results = lax.optimization_barrier((gram, *results))
         gram = all_sum(gram, stages[3:4])
         sums, (at_home, gram) = send_urgent(results, (at_home, gram), group, blocks_dev)
-        gram = all_sum(gram, stages[4:])
-        sums = finish_home(entries, vecs, kept, at_home, blocks_dev, columns, 2) + sums
+        gram = all_sum(gram, stages[4:-1])
+        own = finish_home(entries, vecs, kept, at_home, blocks_dev, columns, 2)
+        gram, own[0] = all_sum(gram, stages[4:][-1:], own[0])
+        sums = own + sums
         inverse = factor(gram)
         z, gram, *parts = scaled_gram(sums, z, counts, degree, inverse, turn + 1 < ITERS)
         parts = parts[0] if parts else None

time: 136 us -> 132 us (0.971)
  waiting for transfers between devices: 38.7 us -> 32.3 us
  starting transfers between devices: 38.8 us -> 41.9 us
  Pallas kernels: 57.2 us -> 55.7 us
    ppermute x6, waiting for transfers between devices: 12.8 us -> 7.69 us  [from_behind(): lax.ppermute(value, axis, [(source, source + steps) for source in range(i...]
    ppermute x12, waiting for transfers between devices: 18.4 us -> 15 us  [all_sum(): lax.ppermute(value, ('blk', 'grp'), [(source, source ^ move) for source i...]
    ppermute x12, starting transfers between devices: 19.4 us -> 21.7 us  [all_sum(): lax.ppermute(value, ('blk', 'grp'), [(source, source ^ move) for source i...]
    ppermute x16, waiting for transfers between devices: 7.57 us -> 9.64 us  [swap(): lax.ppermute(value, axis, [(source, source ^ bit) for source in range(cou...]
    ppermute x16, starting transfers between devices: 8.32 us -> 10.1 us  [swap(): lax.ppermute(value, axis, [(source, source ^ bit) for source in range(cou...]
    pallas_call x6, Pallas kernels: 18.7 us -> 17.2 us  [products(): pl.pallas_call(kernel, out_shape=shapes, in_specs=[spec(SMEM)] * 4 + [spe...]
  transfers between devices with their start and end apart: 34 -> 34, of which waited for: 15 -> 14; matrix products, arithmetic and copies ran while one was open for 1% -> 1% of each run, Pallas kernels for 35% -> 35%
where the time goes in v12:
time: 132 us; the launch traced here: 133 us
  Pallas kernels  55.7 us (42%)
  starting transfers between devices  41.9 us (32%)
  waiting for transfers between devices  32.3 us (24%)
  local copies, waits for them, and re-layouts  1.57 us (1%)
    ppermute x12, starting transfers between devices, all_sum(): lax.ppermute(value, ('blk', 'grp'), [(source, source ^ move) for source i...  21.7 us
    pallas_call x6, Pallas kernels, products(): pl.pallas_call(kernel, out_shape=shapes, in_specs=[spec(SMEM)] * 4 + [spe...  17.2 us
    pallas_call x4, Pallas kernels, build_tiles(): pl.pallas_call(kernel, out_shape=shapes, in_specs=[spec(SMEM)] * len(scal...  16.2 us
    ppermute x12, waiting for transfers between devices, all_sum(): lax.ppermute(value, ('blk', 'grp'), [(source, source ^ move) for source i...  15 us
    pallas_call x1, Pallas kernels, listing(): pl.pallas_call(functools.partial(listing_kernel, group, cap, blocks_dev),...  14.3 us
    ppermute x6, starting transfers between devices, from_behind(): lax.ppermute(value, axis, [(source, source + steps) for source in range(i...  10.1 us
    ppermute x16, starting transfers between devices, swap(): lax.ppermute(value, axis, [(source, source ^ bit) for source in range(cou...  10.1 us
    ppermute x16, waiting for transfers between devices, swap(): lax.ppermute(value, axis, [(source, source ^ bit) for source in range(cou...  9.64 us
  transfers between devices with their start and end apart: 34, of which 14 were waited for; matrix products, arithmetic and copies ran while one was open for 1% of the time, Pallas kernels for 35%

profile of v12, /device:TPU:0, one launch (start us, length us, event | category | flops | bytes accessed | tf_op | source)
XLA Modules:
  0.0 132.7 jit_solution(10509762626096257748)
XLA Ops:
  0.0 0.5 collective-permute-start
  0.5 1.5 %fusion = (bf16[512,768]{1,0:T(8,128)(2,1)S(1)}, bf16[512,768]{1,0:T(8,128)(2,1)S(1)}) fusion(bf16[1024,768]{1,0:T(8,128)(2,1)} %refs_3_.1), kind=kLoop, calls=%fused_computation.5 | loop fusion | bytes 3145728 | tf_op jit(solution)/shard_map/slice | solution.py:661
  2.1 1.3 collective-permute-start.1
  3.4 2.7 %collective-permute-start.2 = (bf16[512,768]{1,0:T(8,128)(2,1)S(1)}, bf16[512,768]{1,0:T(8,128)(2,1)S(1)}, u32[]{:S(2)}, u32[]{:S(2)}) collective-permute-start(bf16[512,768]{1,0:T(8,128)(2,1)S(1)} %get-tuple-element.156), channel_id=1, source_target_pairs={{0,2},{1,3},{2,0},{3,1},{4,6},{5,7},{6,4},{7,5},{8,10},{9,11},{10,... | collective-permute-start | bytes 2359304 | tf_op jit(solution)/shard_map/ppermute | solution.py:30
  6.0 1.3 collective-permute-start.3
  7.3 0.1 collective-permute-start.7
  8.1 14.3 %listing.1 = (s32[16]{0:T(128)S(1)}, s32[16]{0:T(128)S(1)}, s32[4]{0:T(128)S(1)}, s32[32]{0:T(128)S(1)}, s32[32]{0:T(128)S(1)}, /*index=5*/s32[32]{0:T(128)S(1)}, s32[7]{0:T(128)S(1)}) custom-call(s32[64]{0:T(128)S(1)} %copy-done.3, s32[64]{0:T(128)S(1)} %copy-done.4, s32[1]{0:T(128)S(6)} %copy.29.live), custom_call_target="tpu_custom_call" | custom-call | flops 1048576 | bytes 1024 | tf_op jit(solution)/shard_map/listing/pallas_call | solution.py:214
  22.4 0.6 opening.1.refs_4_
  23.0 2.0 %collective-permute-done.1.refs_5_ = bf16[512,768]{1,0:T(8,128)(2,1)S(1)} collective-permute-done((bf16[512,768]{1,0:T(8,128)(2,1)S(1)}, bf16[512,768]{1,0:T(8,128)(2,1)S(1)}, u32[]{:S(2)}, u32[]{:S(2)}) %collective-permute-start.1) | collective-permute-done | bytes 786464 | tf_op jit(solution)/shard_map/ppermute | solution.py:36
  25.0 0.1 fusion.1
  25.0 0.1 collective-permute-start.5
  25.1 0.5 collective-permute-start.6
  25.6 0.1 collective-permute-start.4
  25.7 7.9 %first_tiles.1 = (bf16[5120,768]{1,0:T(8,128)(2,1)S(1)}, f32[10,8,512]{2,1,0:T(8,128)S(1)}, f32[8,512,128]{2,1,0:T(8,128)S(1)}, bf16[17,512,512]{2,1,0:T(8,128)(2,1)S(1)}) custom-call(s32[4]{0:T(128)S(1)} %get-tuple-element.88.refs_0_, s32[16]{0:T(128)S(1)} %get-tuple-element.89.refs_1_, s32[16]{0:T(128)S(1)} %get-tuple-element.90.refs_2_, ...), custom_call_target="tpu_custom_call" | custom-call | flops 1048576 | bytes 1048576 | tf_op jit(solution)/shard_map/first_tiles/pallas_call | solution.py:331
  33.6 0.1 pad_maximum_fusion.refs_3_
  33.7 2.1 %second_tiles.1 = (bf16[5120,768]{1,0:T(8,128)(2,1)S(1)}, f32[10,8,512]{2,1,0:T(8,128)S(1)}, f32[8,512,128]{2,1,0:T(8,128)S(1)}, bf16[17,512,512]{2,1,0:T(8,128)(2,1)S(1)}) custom-call(s32[4]{0:T(128)S(1)} %get-tuple-element.88.refs_0_, s32[16]{0:T(128)S(1)} %get-tuple-element.89.refs_1_, ...), custom_call_target="tpu_custom_call", output_to_operand_aliasing={{0}: (4, {}), {1}: (5, {}), {2}: (6, {}), {3}: (7, {})} | custom-call | flops 1048576 | bytes 1048576 | tf_op jit(solution)/shard_map/second_tiles/pallas_call | solution.py:331
  35.8 5.7 %collective-permute-done.3.refs_0_ = bf16[512,768]{1,0:T(8,128)(2,1)S(1)} collective-permute-done((bf16[512,768]{1,0:T(8,128)(2,1)S(1)}, bf16[512,768]{1,0:T(8,128)(2,1)S(1)}, u32[]{:S(2)}, u32[]{:S(2)}) %collective-permute-start.3) | collective-permute-done | bytes 786464 | tf_op jit(solution)/shard_map/ppermute | solution.py:36
  41.5 1.8 %collective-permute-start.9 = (bf16[80,1024]{1,0:T(8,128)(2,1)S(1)}, bf16[80,1024]{1,0:T(8,128)(2,1)S(1)}, u32[]{:S(2)}, u32[]{:S(2)}) collective-permute-start(bf16[80,1024]{1,0:T(8,128)(2,1)S(1)} %opening.1.refs_4_), channel_id=1, source_target_pairs={{0,2},{1,3},{2,0},{3,1},{4,6},{5,7},{6,4},{7,5},{8,10},{9,11},{10,... | collective-permute-start | bytes 491528 | tf_op jit(solution)/shard_map/ppermute | solution.py:30
  43.3 1.3 collective-permute-start.11
  44.6 0.8 more_blocks.1
  45.3 5.4 %last_tiles.1 = (bf16[5120,768]{1,0:T(8,128)(2,1)S(1)}, f32[10,8,512]{2,1,0:T(8,128)S(1)}, f32[8,512,128]{2,1,0:T(8,128)S(1)}, bf16[17,512,512]{2,1,0:T(8,128)(2,1)S(1)}) custom-call(s32[4]{0:T(128)S(1)} %get-tuple-element.88.refs_0_, s32[16]{0:T(128)S(1)} %get-tuple-element.89.refs_1_, ...), custom_call_target="tpu_custom_call", output_to_operand_aliasing={{0}: (4, {}), {1}: (5, {}), {2}: (6, {}), {3}: (7, {})} | custom-call | flops 4294967296 | bytes 1048576 | tf_op jit(solution)/shard_map/last_tiles/pallas_call | solution.py:331
  50.7 0.2 collective-permute-start.10
  51.0 3.0 %products.6 = (f32[2,72,512]{2,1,0:T(8,128)S(1)}, f32[4,72,512]{2,1,0:T(8,128)S(1)}, f32[2,72,512]{2,1,0:T(8,128)S(1)}, f32[2,72,512]{2,1,0:T(8,128)S(1)}) custom-call(s32[32]{0:T(128)S(1)} %get-tuple-element.80.refs_0_, s32[32]{0:T(128)S(1)} %get-tuple-element.81.refs_1_, s32[32]{0:T(128)S(1)} %get-tuple-element.82.refs_2_, ...), custom_call_target="tpu_custom_call" | custom-call | flops 1048576 | bytes 1048576 | tf_op jit(solution)/shard_map/products/pallas_call | solution.py:422
  54.0 4.0 %products.7 = (f32[4,72,512]{2,1,0:T(8,128)S(1)}, f32[2,72,512]{2,1,0:T(8,128)S(1)}, f32[2,72,512]{2,1,0:T(8,128)S(1)}) custom-call(s32[32]{0:T(128)S(1)} %get-tuple-element.80.refs_0_, s32[32]{0:T(128)S(1)} %get-tuple-element.81.refs_1_, s32[32]{0:T(128)S(1)} %get-tuple-element.82.refs_2_, s32[7]{0:T(128)S(1)} %get-tuple-element.83.refs_3_, ...), custom_call_target="tpu_custom_call" | custom-call | flops 2147483648 | bytes 1048576 | tf_op jit(solution)/shard_map/products/pallas_call | solution.py:422
  58.0 0.4 collective-permute-start.12
  58.5 1.6 %collective-permute-done.12.refs_2_ = f32[4,72,512]{2,1,0:T(8,128)S(1)} collective-permute-done((f32[4,72,512]{2,1,0:T(8,128)S(1)}, f32[4,72,512]{2,1,0:T(8,128)S(1)}, u32[]{:S(2)}, u32[]{:S(2)}) %collective-permute-start.12) | collective-permute-done | bytes 589856 | tf_op jit(solution)/shard_map/ppermute | solution.py:30
  60.2 1.5 %collective-permute-start.14 = (f32[2,72,512]{2,1,0:T(8,128)S(1)}, f32[2,72,512]{2,1,0:T(8,128)S(1)}, u32[]{:S(2)}, u32[]{:S(2)}) collective-permute-start(f32[2,72,512]{2,1,0:T(8,128)S(1)} %slice_add_fusion), channel_id=1, source_target_pairs={{0,2},{1,3},{2,0},{3,1},{4,6},{5,7},{6,4},{7,5},{8,10},{9,11},{10,... | collective-permute-start | bytes 884744 | tf_op jit(solution)/shard_map/ppermute | solution.py:30
  61.6 1.3 collective-permute-start.13
  62.9 1.4 %products.8.refs_0_ = f32[2,72,512]{2,1,0:T(8,128)S(1)} custom-call(s32[32]{0:T(128)S(1)} %get-tuple-element.80.refs_0_, s32[32]{0:T(128)S(1)} %get-tuple-element.81.refs_1_, s32[32]{0:T(128)S(1)} %get-tuple-element.82.refs_2_, s32[7]{0:T(128)S(1)} %get-tuple-element.83.refs_3_, bf16[80,1024]{1,0:T(8,128)(2,1)S(1)} %collective-permute-done.9.refs_4_, ...), custom_call_target="tpu_custom_call" | custom-call | flops 1048576 | bytes 1048576 | tf_op jit(solution)/shard_map/products/pallas_call | solution.py:422
  64.4 5.1 %collective-permute-done.14.refs_3_ = f32[2,72,512]{2,1,0:T(8,128)S(1)} collective-permute-done((f32[2,72,512]{2,1,0:T(8,128)S(1)}, f32[2,72,512]{2,1,0:T(8,128)S(1)}, u32[]{:S(2)}, u32[]{:S(2)}) %collective-permute-start.14) | collective-permute-done | bytes 294944 | tf_op jit(solution)/shard_map/ppermute | solution.py:30
  69.5 1.0 scaled_gram.2
  70.5 0.1 collective-permute-start.16
  70.5 1.3 collective-permute-start.17
  71.8 0.2 collective-permute-start.15
  72.0 1.3 collective-permute-start.19
  73.3 3.1 %products.9 = (f32[2,64,512]{2,1,0:T(8,128)S(1)}, f32[4,64,512]{2,1,0:T(8,128)S(1)}, f32[2,64,512]{2,1,0:T(8,128)S(1)}, f32[2,64,512]{2,1,0:T(8,128)S(1)}) custom-call(s32[32]{0:T(128)S(1)} %get-tuple-element.80.refs_0_, s32[32]{0:T(128)S(1)} %get-tuple-element.81.refs_1_, s32[32]{0:T(128)S(1)} %get-tuple-element.82.refs_2_, ...), custom_call_target="tpu_custom_call" | custom-call | flops 1048576 | bytes 1048576 | tf_op jit(solution)/shard_map/products/pallas_call | solution.py:422
  76.4 2.8 %collective-permute-done.17.refs_4_ = bf16[128,1024]{1,0:T(8,128)(2,1)S(1)} collective-permute-done((bf16[128,1024]{1,0:T(8,128)(2,1)S(1)}, bf16[128,1024]{1,0:T(8,128)(2,1)S(1)}, u32[]{:S(2)}, u32[]{:S(2)}) %collective-permute-start.17) | collective-permute-done | bytes 262176 | tf_op jit(solution)/shard_map/ppermute | solution.py:30
  79.3 1.2 collective-permute-start.18
  80.5 2.7 %collective-permute-done.18 = f32[64,64]{1,0:T(8,128)S(1)} collective-permute-done((f32[64,64]{1,0:T(8,128)S(1)}, f32[64,64]{1,0:T(8,128)S(1)}, u32[]{:S(2)}, u32[]{:S(2)}) %collective-permute-start.18) | collective-permute-done | bytes 16416 | tf_op jit(solution)/shard_map/ppermute | solution.py:636
  83.2 2.5 %collective-permute-start.21 = (f32[64,64]{1,0:T(8,128)S(1)}, f32[64,64]{1,0:T(8,128)S(1)}, u32[]{:S(2)}, u32[]{:S(2)}) collective-permute-start(f32[64,64]{1,0:T(8,128)S(1)} %add.44), channel_id=1, source_target_pairs={{0,4},{1,5},{2,6},{3,7},{4,0},{5,1},{6,2},{7,3},{8,12},{9,13},{10,... | collective-permute-start | bytes 49160 | tf_op jit(solution)/shard_map/ppermute | solution.py:636
  85.7 4.1 %products.10 = (f32[4,64,512]{2,1,0:T(8,128)S(1)}, f32[2,64,512]{2,1,0:T(8,128)S(1)}, f32[2,64,512]{2,1,0:T(8,128)S(1)}) custom-call(s32[32]{0:T(128)S(1)} %get-tuple-element.80.refs_0_, s32[32]{0:T(128)S(1)} %get-tuple-element.81.refs_1_, s32[32]{0:T(128)S(1)} %get-tuple-element.82.refs_2_, s32[7]{0:T(128)S(1)} %get-tuple-element.83.refs_3_, ...), custom_call_target="tpu_custom_call" | custom-call | flops 2147483648 | bytes 1048576 | tf_op jit(solution)/shard_map/products/pallas_call | solution.py:422
  89.9 0.1 collective-permute-start.22
  89.9 2.0 %collective-permute-start.23 = (f32[64,64]{1,0:T(8,128)S(1)}, f32[64,64]{1,0:T(8,128)S(1)}, u32[]{:S(2)}, u32[]{:S(2)}) collective-permute-start(f32[64,64]{1,0:T(8,128)S(1)} %add.45), channel_id=1, source_target_pairs={{0,8},{1,9},{2,10},{3,11},{4,12},{5,13},{6,14},{7,15},{8,0},{9,1},... | collective-permute-start | bytes 49160 | tf_op jit(solution)/shard_map/ppermute | solution.py:636
  91.9 2.0 %collective-permute-done.23 = f32[64,64]{1,0:T(8,128)S(1)} collective-permute-done((f32[64,64]{1,0:T(8,128)S(1)}, f32[64,64]{1,0:T(8,128)S(1)}, u32[]{:S(2)}, u32[]{:S(2)}) %collective-permute-start.23) | collective-permute-done | bytes 16416 | tf_op jit(solution)/shard_map/ppermute | solution.py:636
  94.0 0.8 collective-permute-start.25
  94.8 3.7 %collective-permute-start.24 = (f32[2,64,512]{2,1,0:T(8,128)S(1)}, f32[2,64,512]{2,1,0:T(8,128)S(1)}, u32[]{:S(2)}, u32[]{:S(2)}) collective-permute-start(f32[2,64,512]{2,1,0:T(8,128)S(1)} %get-tuple-element.148), channel_id=1, source_target_pairs={{0,4},{4,8},{8,12},{12,16},{16,20},{20,24},{24,28},{1,5},{5,9},{9,... | collective-permute-start | bytes 786440 | tf_op jit(solution)/shard_map/ppermute | solution.py:36
  98.5 5.8 %collective-permute-start.26 = (f32[64,64]{1,0:T(8,128)S(1)}, f32[64,64]{1,0:T(8,128)S(1)}, u32[]{:S(2)}, u32[]{:S(2)}) collective-permute-start(f32[64,64]{1,0:T(8,128)S(1)} %add.47), channel_id=1, source_target_pairs={{0,16},{1,17},{2,18},{3,19},{4,20},{5,21},{6,22},{7,23},{8,24},{9,... | collective-permute-start | bytes 49160 | tf_op jit(solution)/shard_map/ppermute | solution.py:636
  104.3 1.5 %products.11.refs_0_ = f32[2,64,512]{2,1,0:T(8,128)S(1)} custom-call(s32[32]{0:T(128)S(1)} %get-tuple-element.80.refs_0_, s32[32]{0:T(128)S(1)} %get-tuple-element.81.refs_1_, s32[32]{0:T(128)S(1)} %get-tuple-element.82.refs_2_, s32[7]{0:T(128)S(1)} %get-tuple-element.83.refs_3_, bf16[128,1024]{1,0:T(8,128)(2,1)S(1)} %collective-permute-done.17.refs_4_, ...), custom_call_target="tpu_custom_call" | custom-call | flops 1048576 | bytes 1048576 | tf_op jit(solution)/shard_map/products/pallas_call | solution.py:422
  105.8 0.4 collective-permute-done.26
  106.2 2.0 %factor.1.refs_6_ = f32[64,64]{1,0:T(8,128)S(1)} custom-call(f32[64,64]{1,0:T(8,128)S(1)} %add.48.gram), custom_call_target="tpu_custom_call" | custom-call | flops 65536 | bytes 65536 | tf_op jit(solution)/shard_map/factor/pallas_call | solution.py:592
  108.2 1.5 %scaled_gram.3 = (f32[64,1024]{1,0:T(8,128)S(1)}, f32[64,64]{1,0:T(8,128)S(1)}) custom-call(s32[2]{0:T(128)S(1)} %copy-done.2, f32[2,64,512]{2,1,0:T(8,128)S(1)} %products.11.refs_0_, f32[2,64,512]{2,1,0:T(8,128)S(1)} %collective-permute-done.24.refs_1_, f32[4,64,512]{2,1,0:T(8,128)S(1)} %collective-permute-done.22.refs_2_, ...), custom_call_target="tpu_custom_call" | custom-call | flops 67108864 | bytes 2097152 | tf_op jit(solution)/shard_map/scaled_gram/pallas_call | solution.py:533
  109.7 0.1 collective-permute-start.27
  109.8 1.2 collective-permute-done.27
  111.0 0.9 collective-permute-start.28
  111.8 0.8 collective-permute-start.29
  112.6 1.9 %collective-permute-start.30 = (f32[64,64]{1,0:T(8,128)S(1)}, f32[64,64]{1,0:T(8,128)S(1)}, u32[]{:S(2)}, u32[]{:S(2)}) collective-permute-start(f32[64,64]{1,0:T(8,128)S(1)} %add.49), channel_id=1, source_target_pairs={{0,6},{1,7},{2,4},{3,5},{4,2},{5,3},{6,0},{7,1},{8,14},{9,15},{10,... | collective-permute-start | bytes 49160 | tf_op jit(solution)/shard_map/ppermute | solution.py:636
  114.5 0.4 collective-permute-done.28
  114.9 0.9 collective-permute-done.29
  115.8 1.7 %collective-permute-done.30 = f32[64,64]{1,0:T(8,128)S(1)} collective-permute-done((f32[64,64]{1,0:T(8,128)S(1)}, f32[64,64]{1,0:T(8,128)S(1)}, u32[]{:S(2)}, u32[]{:S(2)}) %collective-permute-start.30) | collective-permute-done | bytes 16416 | tf_op jit(solution)/shard_map/ppermute | solution.py:636
  117.4 3.1 %collective-permute-start.31 = (f32[64,64]{1,0:T(8,128)S(1)}, f32[64,64]{1,0:T(8,128)S(1)}, u32[]{:S(2)}, u32[]{:S(2)}) collective-permute-start(f32[64,64]{1,0:T(8,128)S(1)} %add_add_fusion.1), channel_id=1, source_target_pairs={{0,8},{1,9},{2,10},{3,11},{4,12},{5,13},{6,14},{7,15},{8,0},{9,1},... | collective-permute-start | bytes 49160 | tf_op jit(solution)/shard_map/ppermute | solution.py:636
  120.5 3.4 %collective-permute-start.32 = (f32[64,64]{1,0:T(8,128)S(1)}, f32[64,64]{1,0:T(8,128)S(1)}, u32[]{:S(2)}, u32[]{:S(2)}) collective-permute-start(f32[64,64]{1,0:T(8,128)S(1)} %add_add_fusion.1), channel_id=1, source_target_pairs={{0,16},{1,17},{2,18},{3,19},{4,20},{5,21},{6,22},{7,23},{8,24},{9,... | collective-permute-start | bytes 49160 | tf_op jit(solution)/shard_map/ppermute | solution.py:636
  123.9 2.0 %collective-permute-done.32 = f32[64,64]{1,0:T(8,128)S(1)} collective-permute-done((f32[64,64]{1,0:T(8,128)S(1)}, f32[64,64]{1,0:T(8,128)S(1)}, u32[]{:S(2)}, u32[]{:S(2)}) %collective-permute-start.32) | collective-permute-done | bytes 16416 | tf_op jit(solution)/shard_map/ppermute | solution.py:636
  126.0 3.7 %collective-permute-done.33 = f32[64,64]{1,0:T(8,128)S(1)} collective-permute-done((f32[64,64]{1,0:T(8,128)S(1)}, f32[64,64]{1,0:T(8,128)S(1)}, u32[]{:S(2)}, u32[]{:S(2)}) %collective-permute-start.33) | collective-permute-done | bytes 16416 | tf_op jit(solution)/shard_map/ppermute | solution.py:636
  129.7 3.0 %embedding.1 = f32[64,1024]{1,0:T(8,128)} custom-call(f32[64,64]{1,0:T(8,128)S(1)} %add_add_fusion.gram, f32[64,1024]{1,0:T(8,128)S(1)} %get-tuple-element.154.z), custom_call_target="tpu_custom_call" | custom-call | flops 1073741824 | bytes 1048576 | tf_op jit(solution)/shard_map/embedding/pallas_call | solution.py:610
  (43 shorter events, 0.2 us)
Async XLA Ops:
  0.0 25.7 %copy-start = (bf16[1024,768]{1,0:T(8,128)(2,1)S(1)}, bf16[1024,768]{1,0:T(8,128)(2,1)}, u32[]{:S(2)}) copy-start(bf16[1024,768]{1,0:T(8,128)(2,1)} %refs_3_.1) | copy-start | bytes 4718596
  0.0 8.1 %copy-start.3 = (s32[64]{0:T(128)S(1)}, s32[64]{0:T(128)}, u32[]{:S(2)}) copy-start(s32[64]{0:T(128)} %rows.1) | copy-start | bytes 772
  0.0 8.1 %copy-start.4 = (s32[64]{0:T(128)S(1)}, s32[64]{0:T(128)}, u32[]{:S(2)}) copy-start(s32[64]{0:T(128)} %cols.1) | copy-start | bytes 772
  0.0 22.4 %copy-start.1 = (f32[64,1024]{1,0:T(8,128)S(1)}, f32[64,1024]{1,0:T(8,128)}, u32[]{:S(2)}) copy-start(f32[64,1024]{1,0:T(8,128)} %start) | copy-start | bytes 786436
  0.0 22.4 %copy-start.2 = (s32[2]{0:T(128)S(1)}, s32[2]{0:T(128)}, u32[]{:S(2)}) copy-start(s32[2]{0:T(128)} %count_ref.3) | copy-start | bytes 28
  0.0 22.4 %collective-permute-start = (bf16[1024,768]{1,0:T(8,128)(2,1)}, bf16[1024,768]{1,0:T(8,128)(2,1)S(1)}, u32[]{:S(2)}, u32[]{:S(2)}) collective-permute-start(bf16[1024,768]{1,0:T(8,128)(2,1)} %refs_3_.1), channel_id=1, source_target_pairs={{0,1},{1,0},{2,3},{3,2},{4,5},{5,4},{6,7},{7,6},{8,9},{9,8},{10,11... | collective-permute-start | bytes 4718600 | tf_op jit(solution)/shard_map/ppermute | solution.py:30
  2.1 22.9 %collective-permute-start.1 = (bf16[512,768]{1,0:T(8,128)(2,1)S(1)}, bf16[512,768]{1,0:T(8,128)(2,1)S(1)}, u32[]{:S(2)}, u32[]{:S(2)}) collective-permute-start(bf16[512,768]{1,0:T(8,128)(2,1)S(1)} %get-tuple-element.156), channel_id=1, source_target_pairs={{4,0},{8,4},{12,8},{16,12},{20,16},{24,20},{28,24},{5,1},{9,5},{13... | collective-permute-start | bytes 2359304 | tf_op jit(solution)/shard_map/ppermute | solution.py:36
  3.4 21.6 %collective-permute-start.2 = (bf16[512,768]{1,0:T(8,128)(2,1)S(1)}, bf16[512,768]{1,0:T(8,128)(2,1)S(1)}, u32[]{:S(2)}, u32[]{:S(2)}) collective-permute-start(bf16[512,768]{1,0:T(8,128)(2,1)S(1)} %get-tuple-element.156), channel_id=1, source_target_pairs={{0,2},{1,3},{2,0},{3,1},{4,6},{5,7},{6,4},{7,5},{8,10},{9,11},{10,... | collective-permute-start | bytes 2359304 | tf_op jit(solution)/shard_map/ppermute | solution.py:30
  6.0 35.5 %collective-permute-start.3 = (bf16[512,768]{1,0:T(8,128)(2,1)S(1)}, bf16[512,768]{1,0:T(8,128)(2,1)S(1)}, u32[]{:S(2)}, u32[]{:S(2)}) collective-permute-start(bf16[512,768]{1,0:T(8,128)(2,1)S(1)} %get-tuple-element.155), channel_id=1, source_target_pairs={{4,0},{8,4},{12,8},{16,12},{20,16},{24,20},{28,24},{5,1},{9,5},{13... | collective-permute-start | bytes 2359304 | tf_op jit(solution)/shard_map/ppermute | solution.py:36
  7.3 34.2 %collective-permute-start.7 = (bf16[512,768]{1,0:T(8,128)(2,1)S(1)}, bf16[512,768]{1,0:T(8,128)(2,1)S(1)}, u32[]{:S(2)}, u32[]{:S(2)}) collective-permute-start(bf16[512,768]{1,0:T(8,128)(2,1)S(1)} %get-tuple-element.155), channel_id=1, source_target_pairs={{0,2},{1,3},{2,0},{3,1},{4,6},{5,7},{6,4},{7,5},{8,10},{9,11},{10,... | collective-permute-start | bytes 2359304 | tf_op jit(solution)/shard_map/ppermute | solution.py:30
  25.0 8.6 %collective-permute-start.5 = (bf16[256,768]{1,0:T(8,128)(2,1)S(1)}, bf16[256,768]{1,0:T(8,128)(2,1)S(1)}, u32[]{:S(2)}, u32[]{:S(2)}) collective-permute-start(bf16[256,768]{1,0:T(8,128)(2,1)S(1)} %get-tuple-element.157), channel_id=1, source_target_pairs={{0,1},{1,0},{2,3},{3,2},{4,5},{5,4},{6,7},{7,6},{8,9},{9,8},{10,11... | collective-permute-start | bytes 1179656 | tf_op jit(solution)/shard_map/ppermute | solution.py:30
  25.1 8.5 %collective-permute-start.6 = (bf16[256,768]{1,0:T(8,128)(2,1)S(1)}, bf16[256,768]{1,0:T(8,128)(2,1)S(1)}, u32[]{:S(2)}, u32[]{:S(2)}) collective-permute-start(bf16[256,768]{1,0:T(8,128)(2,1)S(1)} %get-tuple-element.158), channel_id=1, source_target_pairs={{0,1},{1,0},{2,3},{3,2},{4,5},{5,4},{6,7},{7,6},{8,9},{9,8},{10,11... | collective-permute-start | bytes 1179656 | tf_op jit(solution)/shard_map/ppermute | solution.py:30
  25.6 15.9 %collective-permute-start.4 = (bf16[80,1024]{1,0:T(8,128)(2,1)S(1)}, bf16[80,1024]{1,0:T(8,128)(2,1)S(1)}, u32[]{:S(2)}, u32[]{:S(2)}) collective-permute-start(bf16[80,1024]{1,0:T(8,128)(2,1)S(1)} %opening.1.refs_4_), channel_id=1, source_target_pairs={{0,1},{1,0},{2,3},{3,2},{4,5},{5,4},{6,7},{7,6},{8,9},{9,8},{10,11... | collective-permute-start | bytes 491528 | tf_op jit(solution)/shard_map/ppermute | solution.py:30
  41.5 3.8 %collective-permute-start.8 = (bf16[512,768]{1,0:T(8,128)(2,1)S(1)}, bf16[512,768]{1,0:T(8,128)(2,1)S(1)}, u32[]{:S(2)}, u32[]{:S(2)}) collective-permute-start(bf16[512,768]{1,0:T(8,128)(2,1)S(1)} %collective-permute-done.7.refs_1_), channel_id=1, source_target_pairs={{0,1},{1,0},{2,3},{3,2},{4,5},{5,4},{6,7},{7,6},{8,9},{9,8},{10,11... | collective-permute-start | bytes 2359304 | tf_op jit(solution)/shard_map/ppermute | solution.py:30
  41.5 9.2 %collective-permute-start.9 = (bf16[80,1024]{1,0:T(8,128)(2,1)S(1)}, bf16[80,1024]{1,0:T(8,128)(2,1)S(1)}, u32[]{:S(2)}, u32[]{:S(2)}) collective-permute-start(bf16[80,1024]{1,0:T(8,128)(2,1)S(1)} %opening.1.refs_4_), channel_id=1, source_target_pairs={{0,2},{1,3},{2,0},{3,1},{4,6},{5,7},{6,4},{7,5},{8,10},{9,11},{10,... | collective-permute-start | bytes 491528 | tf_op jit(solution)/shard_map/ppermute | solution.py:30
  43.3 10.7 %collective-permute-start.11 = (bf16[80,1024]{1,0:T(8,128)(2,1)S(1)}, bf16[80,1024]{1,0:T(8,128)(2,1)S(1)}, u32[]{:S(2)}, u32[]{:S(2)}) collective-permute-start(bf16[80,1024]{1,0:T(8,128)(2,1)S(1)} %opening.1.refs_4_), channel_id=1, source_target_pairs={{4,0},{8,4},{12,8},{16,12},{20,16},{24,20},{28,24},{5,1},{9,5},{13... | collective-permute-start | bytes 491528 | tf_op jit(solution)/shard_map/ppermute | solution.py:36
  50.7 3.3 %collective-permute-start.10 = (bf16[80,1024]{1,0:T(8,128)(2,1)S(1)}, bf16[80,1024]{1,0:T(8,128)(2,1)S(1)}, u32[]{:S(2)}, u32[]{:S(2)}) collective-permute-start(bf16[80,1024]{1,0:T(8,128)(2,1)S(1)} %collective-permute-done.9.refs_4_), channel_id=1, source_target_pairs={{0,1},{1,0},{2,3},{3,2},{4,5},{5,4},{6,7},{7,6},{8,9},{9,8},{10,11... | collective-permute-start | bytes 491528 | tf_op jit(solution)/shard_map/ppermute | solution.py:30
  58.0 2.1 %collective-permute-start.12 = (f32[4,72,512]{2,1,0:T(8,128)S(1)}, f32[4,72,512]{2,1,0:T(8,128)S(1)}, u32[]{:S(2)}, u32[]{:S(2)}) collective-permute-start(f32[4,72,512]{2,1,0:T(8,128)S(1)} %get-tuple-element.117), channel_id=1, source_target_pairs={{0,1},{1,0},{2,3},{3,2},{4,5},{5,4},{6,7},{7,6},{8,9},{9,8},{10,11... | collective-permute-start | bytes 1769480 | tf_op jit(solution)/shard_map/ppermute | solution.py:30
  60.2 9.3 %collective-permute-start.14 = (f32[2,72,512]{2,1,0:T(8,128)S(1)}, f32[2,72,512]{2,1,0:T(8,128)S(1)}, u32[]{:S(2)}, u32[]{:S(2)}) collective-permute-start(f32[2,72,512]{2,1,0:T(8,128)S(1)} %slice_add_fusion), channel_id=1, source_target_pairs={{0,2},{1,3},{2,0},{3,1},{4,6},{5,7},{6,4},{7,5},{8,10},{9,11},{10,... | collective-permute-start | bytes 884744 | tf_op jit(solution)/shard_map/ppermute | solution.py:30
  61.6 7.9 %collective-permute-start.13 = (f32[2,72,512]{2,1,0:T(8,128)S(1)}, f32[2,72,512]{2,1,0:T(8,128)S(1)}, u32[]{:S(2)}, u32[]{:S(2)}) collective-permute-start(f32[2,72,512]{2,1,0:T(8,128)S(1)} %get-tuple-element.122), channel_id=1, source_target_pairs={{0,4},{4,8},{8,12},{12,16},{16,20},{20,24},{24,28},{1,5},{5,9},{9,... | collective-permute-start | bytes 884744 | tf_op jit(solution)/shard_map/ppermute | solution.py:36
  70.5 2.8 %collective-permute-start.16 = (bf16[128,1024]{1,0:T(8,128)(2,1)S(1)}, bf16[128,1024]{1,0:T(8,128)(2,1)S(1)}, u32[]{:S(2)}, u32[]{:S(2)}) collective-permute-start(bf16[128,1024]{1,0:T(8,128)(2,1)S(1)} %get-tuple-element.125.refs_4_), channel_id=1, source_target_pairs={{0,1},{1,0},{2,3},{3,2},{4,5},{5,4},{6,7},{7,6},{8,9},{9,8},{10,11... | collective-permute-start | bytes 786440 | tf_op jit(solution)/shard_map/ppermute | solution.py:30
  70.5 8.7 %collective-permute-start.17 = (bf16[128,1024]{1,0:T(8,128)(2,1)S(1)}, bf16[128,1024]{1,0:T(8,128)(2,1)S(1)}, u32[]{:S(2)}, u32[]{:S(2)}) collective-permute-start(bf16[128,1024]{1,0:T(8,128)(2,1)S(1)} %get-tuple-element.125.refs_4_), channel_id=1, source_target_pairs={{0,2},{1,3},{2,0},{3,1},{4,6},{5,7},{6,4},{7,5},{8,10},{9,11},{10,... | collective-permute-start | bytes 786440 | tf_op jit(solution)/shard_map/ppermute | solution.py:30
  71.8 1.5 %collective-permute-start.15 = (f32[64,64]{1,0:T(8,128)S(1)}, f32[64,64]{1,0:T(8,128)S(1)}, u32[]{:S(2)}, u32[]{:S(2)}) collective-permute-start(f32[64,64]{1,0:T(8,128)S(1)} %get-tuple-element.124), channel_id=1, source_target_pairs={{0,1},{1,0},{2,3},{3,2},{4,5},{5,4},{6,7},{7,6},{8,9},{9,8},{10,11... | collective-permute-start | bytes 49160 | tf_op jit(solution)/shard_map/ppermute | solution.py:636
  72.0 11.2 %collective-permute-start.19 = (bf16[128,1024]{1,0:T(8,128)(2,1)S(1)}, bf16[128,1024]{1,0:T(8,128)(2,1)S(1)}, u32[]{:S(2)}, u32[]{:S(2)}) collective-permute-start(bf16[128,1024]{1,0:T(8,128)(2,1)S(1)} %get-tuple-element.125.refs_4_), channel_id=1, source_target_pairs={{4,0},{8,4},{12,8},{16,12},{20,16},{24,20},{28,24},{5,1},{9,5},{13... | collective-permute-start | bytes 786440 | tf_op jit(solution)/shard_map/ppermute | solution.py:36
  79.3 3.9 %collective-permute-start.20 = (bf16[128,1024]{1,0:T(8,128)(2,1)S(1)}, bf16[128,1024]{1,0:T(8,128)(2,1)S(1)}, u32[]{:S(2)}, u32[]{:S(2)}) collective-permute-start(bf16[128,1024]{1,0:T(8,128)(2,1)S(1)} %collective-permute-done.17.refs_4_), channel_id=1, source_target_pairs={{0,1},{1,0},{2,3},{3,2},{4,5},{5,4},{6,7},{7,6},{8,9},{9,8},{10,11... | collective-permute-start | bytes 786440 | tf_op jit(solution)/shard_map/ppermute | solution.py:30
  79.3 3.9 %collective-permute-start.18 = (f32[64,64]{1,0:T(8,128)S(1)}, f32[64,64]{1,0:T(8,128)S(1)}, u32[]{:S(2)}, u32[]{:S(2)}) collective-permute-start(f32[64,64]{1,0:T(8,128)S(1)} %add.43), channel_id=1, source_target_pairs={{0,2},{1,3},{2,0},{3,1},{4,6},{5,7},{6,4},{7,5},{8,10},{9,11},{10,... | collective-permute-start | bytes 49160 | tf_op jit(solution)/shard_map/ppermute | solution.py:636
  83.2 6.6 %collective-permute-start.21 = (f32[64,64]{1,0:T(8,128)S(1)}, f32[64,64]{1,0:T(8,128)S(1)}, u32[]{:S(2)}, u32[]{:S(2)}) collective-permute-start(f32[64,64]{1,0:T(8,128)S(1)} %add.44), channel_id=1, source_target_pairs={{0,4},{1,5},{2,6},{3,7},{4,0},{5,1},{6,2},{7,3},{8,12},{9,13},{10,... | collective-permute-start | bytes 49160 | tf_op jit(solution)/shard_map/ppermute | solution.py:636
  89.9 4.1 %collective-permute-start.22 = (f32[4,64,512]{2,1,0:T(8,128)S(1)}, f32[4,64,512]{2,1,0:T(8,128)S(1)}, u32[]{:S(2)}, u32[]{:S(2)}) collective-permute-start(f32[4,64,512]{2,1,0:T(8,128)S(1)} %get-tuple-element.140), channel_id=1, source_target_pairs={{0,1},{1,0},{2,3},{3,2},{4,5},{5,4},{6,7},{7,6},{8,9},{9,8},{10,11... | collective-permute-start | bytes 1572872 | tf_op jit(solution)/shard_map/ppermute | solution.py:30
  89.9 4.0 %collective-permute-start.23 = (f32[64,64]{1,0:T(8,128)S(1)}, f32[64,64]{1,0:T(8,128)S(1)}, u32[]{:S(2)}, u32[]{:S(2)}) collective-permute-start(f32[64,64]{1,0:T(8,128)S(1)} %add.45), channel_id=1, source_target_pairs={{0,8},{1,9},{2,10},{3,11},{4,12},{5,13},{6,14},{7,15},{8,0},{9,1},... | collective-permute-start | bytes 49160 | tf_op jit(solution)/shard_map/ppermute | solution.py:636
  94.0 14.2 %collective-permute-start.25 = (f32[2,64,512]{2,1,0:T(8,128)S(1)}, f32[2,64,512]{2,1,0:T(8,128)S(1)}, u32[]{:S(2)}, u32[]{:S(2)}) collective-permute-start(f32[2,64,512]{2,1,0:T(8,128)S(1)} %slice_add_fusion.1), channel_id=1, source_target_pairs={{0,2},{1,3},{2,0},{3,1},{4,6},{5,7},{6,4},{7,5},{8,10},{9,11},{10,... | collective-permute-start | bytes 786440 | tf_op jit(solution)/shard_map/ppermute | solution.py:30
  94.8 13.4 %collective-permute-start.24 = (f32[2,64,512]{2,1,0:T(8,128)S(1)}, f32[2,64,512]{2,1,0:T(8,128)S(1)}, u32[]{:S(2)}, u32[]{:S(2)}) collective-permute-start(f32[2,64,512]{2,1,0:T(8,128)S(1)} %get-tuple-element.148), channel_id=1, source_target_pairs={{0,4},{4,8},{8,12},{12,16},{16,20},{20,24},{24,28},{1,5},{5,9},{9,... | collective-permute-start | bytes 786440 | tf_op jit(solution)/shard_map/ppermute | solution.py:36
  98.5 7.7 %collective-permute-start.26 = (f32[64,64]{1,0:T(8,128)S(1)}, f32[64,64]{1,0:T(8,128)S(1)}, u32[]{:S(2)}, u32[]{:S(2)}) collective-permute-start(f32[64,64]{1,0:T(8,128)S(1)} %add.47), channel_id=1, source_target_pairs={{0,16},{1,17},{2,18},{3,19},{4,20},{5,21},{6,22},{7,23},{8,24},{9,... | collective-permute-start | bytes 49160 | tf_op jit(solution)/shard_map/ppermute | solution.py:636
  109.7 1.3 collective-permute-start.27
  111.0 3.9 %collective-permute-start.28 = (f32[64,64]{1,0:T(8,128)S(1)}, f32[64,64]{1,0:T(8,128)S(1)}, u32[]{:S(2)}, u32[]{:S(2)}) collective-permute-start(f32[64,64]{1,0:T(8,128)S(1)} %add.49), channel_id=1, source_target_pairs={{0,2},{1,3},{2,0},{3,1},{4,6},{5,7},{6,4},{7,5},{8,10},{9,11},{10,... | collective-permute-start | bytes 49160 | tf_op jit(solution)/shard_map/ppermute | solution.py:636
  111.8 3.9 %collective-permute-start.29 = (f32[64,64]{1,0:T(8,128)S(1)}, f32[64,64]{1,0:T(8,128)S(1)}, u32[]{:S(2)}, u32[]{:S(2)}) collective-permute-start(f32[64,64]{1,0:T(8,128)S(1)} %add.49), channel_id=1, source_target_pairs={{0,4},{1,5},{2,6},{3,7},{4,0},{5,1},{6,2},{7,3},{8,12},{9,13},{10,... | collective-permute-start | bytes 49160 | tf_op jit(solution)/shard_map/ppermute | solution.py:636
  112.6 4.8 %collective-permute-start.30 = (f32[64,64]{1,0:T(8,128)S(1)}, f32[64,64]{1,0:T(8,128)S(1)}, u32[]{:S(2)}, u32[]{:S(2)}) collective-permute-start(f32[64,64]{1,0:T(8,128)S(1)} %add.49), channel_id=1, source_target_pairs={{0,6},{1,7},{2,4},{3,5},{4,2},{5,3},{6,0},{7,1},{8,14},{9,15},{10,... | collective-permute-start | bytes 49160 | tf_op jit(solution)/shard_map/ppermute | solution.py:636
  117.4 6.5 %collective-permute-start.31 = (f32[64,64]{1,0:T(8,128)S(1)}, f32[64,64]{1,0:T(8,128)S(1)}, u32[]{:S(2)}, u32[]{:S(2)}) collective-permute-start(f32[64,64]{1,0:T(8,128)S(1)} %add_add_fusion.1), channel_id=1, source_target_pairs={{0,8},{1,9},{2,10},{3,11},{4,12},{5,13},{6,14},{7,15},{8,0},{9,1},... | collective-permute-start | bytes 49160 | tf_op jit(solution)/shard_map/ppermute | solution.py:636
  120.5 5.4 %collective-permute-start.32 = (f32[64,64]{1,0:T(8,128)S(1)}, f32[64,64]{1,0:T(8,128)S(1)}, u32[]{:S(2)}, u32[]{:S(2)}) collective-permute-start(f32[64,64]{1,0:T(8,128)S(1)} %add_add_fusion.1), channel_id=1, source_target_pairs={{0,16},{1,17},{2,18},{3,19},{4,20},{5,21},{6,22},{7,23},{8,24},{9,... | collective-permute-start | bytes 49160 | tf_op jit(solution)/shard_map/ppermute | solution.py:636
  123.9 5.7 %collective-permute-start.33 = (f32[64,64]{1,0:T(8,128)S(1)}, f32[64,64]{1,0:T(8,128)S(1)}, u32[]{:S(2)}, u32[]{:S(2)}) collective-permute-start(f32[64,64]{1,0:T(8,128)S(1)} %add_add_fusion.1), channel_id=1, source_target_pairs={{0,24},{1,25},{2,26},{3,27},{4,28},{5,29},{6,30},{7,31},{8,16},{9,... | collective-permute-start | bytes 49160 | tf_op jit(solution)/shard_map/ppermute | solution.py:636

commit v13 on v12

--- a/solution.py
+++ b/solution.py
@@ -620,6 +620,15 @@
 
 def sum_stages():
     return bits_of(lax.axis_size("blk") * lax.axis_size("grp"))
+
+
+def sum_by_shares(value):
+    axes = ("blk", "grp")
+    count = lax.axis_size("blk") * lax.axis_size("grp")
+    shares = value.reshape(count, value.size // count)
+    share = jnp.sum(lax.all_to_all(shares, axes, 0, 0, tiled=True), axis=0, keepdims=True)
+    shares = jnp.broadcast_to(share, shares.shape)
+    return lax.all_to_all(shares, axes, 0, 0, tiled=True).reshape(value.shape)
 
 
 def pairs_of(bits):
@@ -766,8 +775,9 @@
         inverse = factor(gram)
         z, gram, *parts = scaled_gram(sums, z, counts, degree, inverse, turn + 1 < ITERS)
         parts = parts[0] if parts else None
-    stages = sum_stages()
-    return embedding(all_sum(gram, stages[:1] + pairs_of(stages[1:])), z)
+    half = columns // 2
+    gram = sum_by_shares(jnp.concatenate([gram[:half], gram[half:]], axis=1))
+    return embedding(jnp.concatenate([gram[:, :columns], gram[:, columns:]], axis=0), z)
 
 
 def solution(mesh):

time: 132 us -> 134 us (1.015)
  blocking collectives: 0 us -> 25.1 us
  starting transfers between devices: 41.9 us -> 26.5 us
  waiting for transfers between devices: 32.3 us -> 24.4 us
    all_to_all x0 -> x2, blocking collectives: none -> 25.1 us  [the longest x1 16.3 us: sum_by_shares(): lax.all_to_all(shares, axes, 0, 0, tiled=True)]
    ppermute x12 -> x5, starting transfers between devices: 21.7 us -> 8.09 us  [all_sum(): lax.ppermute(value, ('blk', 'grp'), [(source, source ^ move) for source i...]
    ppermute x12 -> x5, waiting for transfers between devices: 15 us -> 6.37 us  [all_sum(): lax.ppermute(value, ('blk', 'grp'), [(source, source ^ move) for source i...]
    ppermute x6, starting transfers between devices: 10.1 us -> 8.05 us  [from_behind(): lax.ppermute(value, axis, [(source, source + steps) for source in range(i...]
  transfers between devices with their start and end apart: 34 -> 27, of which waited for: 14 -> 8; matrix products, arithmetic and copies ran while one was open for 1% -> 1% of each run, Pallas kernels for 35% -> 34%
where the time goes in v13:
time: 134 us; the launch traced here: 135 us
  Pallas kernels  55.7 us (42%)
  starting transfers between devices  26.5 us (20%)
  blocking collectives  25.1 us (19%)
  waiting for transfers between devices  24.4 us (18%)
  local copies, waits for them, and re-layouts  1.66 us (1%)
    pallas_call x6, Pallas kernels, products(): pl.pallas_call(kernel, out_shape=shapes, in_specs=[spec(SMEM)] * 4 + [spe...  17.2 us
    all_to_all x1, blocking collectives, sum_by_shares(): lax.all_to_all(shares, axes, 0, 0, tiled=True)  16.3 us
    pallas_call x4, Pallas kernels, build_tiles(): pl.pallas_call(kernel, out_shape=shapes, in_specs=[spec(SMEM)] * len(scal...  16.2 us
    pallas_call x1, Pallas kernels, listing(): pl.pallas_call(functools.partial(listing_kernel, group, cap, blocks_dev),...  14.3 us
    ppermute x16, starting transfers between devices, swap(): lax.ppermute(value, axis, [(source, source ^ bit) for source in range(cou...  10.4 us
    ppermute x16, waiting for transfers between devices, swap(): lax.ppermute(value, axis, [(source, source ^ bit) for source in range(cou...  10.3 us
    all_to_all x1, blocking collectives, sum_by_shares(): return lax.all_to_all(shares, axes, 0, 0, tiled=True).reshape(value.shape)  8.84 us
    ppermute x5, starting transfers between devices, all_sum(): lax.ppermute(value, ('blk', 'grp'), [(source, source ^ move) for source i...  8.09 us
  transfers between devices with their start and end apart: 27, of which 8 were waited for; matrix products, arithmetic and copies ran while one was open for 1% of the time, Pallas kernels for 34%

profile of v13, /device:TPU:0, one launch (start us, length us, event | category | flops | bytes accessed | tf_op | source)
XLA Modules:
  0.0 134.7 jit_solution(3421096352308991164)
XLA Ops:
  0.0 0.5 collective-permute-start
  0.5 1.5 %fusion = (bf16[512,768]{1,0:T(8,128)(2,1)S(1)}, bf16[512,768]{1,0:T(8,128)(2,1)S(1)}) fusion(bf16[1024,768]{1,0:T(8,128)(2,1)} %refs_3_.1), kind=kLoop, calls=%fused_computation.5 | loop fusion | bytes 3145728 | tf_op jit(solution)/shard_map/slice | solution.py:670
  2.1 1.3 collective-permute-start.1
  3.4 2.7 %collective-permute-start.2 = (bf16[512,768]{1,0:T(8,128)(2,1)S(1)}, bf16[512,768]{1,0:T(8,128)(2,1)S(1)}, u32[]{:S(2)}, u32[]{:S(2)}) collective-permute-start(bf16[512,768]{1,0:T(8,128)(2,1)S(1)} %get-tuple-element.156), channel_id=1, source_target_pairs={{0,2},{1,3},{2,0},{3,1},{4,6},{5,7},{6,4},{7,5},{8,10},{9,11},{10,... | collective-permute-start | bytes 2359304 | tf_op jit(solution)/shard_map/ppermute | solution.py:30
  6.0 1.3 collective-permute-start.3
  7.3 0.1 collective-permute-start.7
  8.1 14.3 %listing.1 = (s32[16]{0:T(128)S(1)}, s32[16]{0:T(128)S(1)}, s32[4]{0:T(128)S(1)}, s32[32]{0:T(128)S(1)}, s32[32]{0:T(128)S(1)}, /*index=5*/s32[32]{0:T(128)S(1)}, s32[7]{0:T(128)S(1)}) custom-call(s32[64]{0:T(128)S(1)} %copy-done.3, s32[64]{0:T(128)S(1)} %copy-done.4, s32[1]{0:T(128)S(6)} %copy.30.live), custom_call_target="tpu_custom_call" | custom-call | flops 1048576 | bytes 1024 | tf_op jit(solution)/shard_map/listing/pallas_call | solution.py:214
  22.4 0.6 opening.1.refs_4_
  23.0 2.0 %collective-permute-done.1.refs_5_ = bf16[512,768]{1,0:T(8,128)(2,1)S(1)} collective-permute-done((bf16[512,768]{1,0:T(8,128)(2,1)S(1)}, bf16[512,768]{1,0:T(8,128)(2,1)S(1)}, u32[]{:S(2)}, u32[]{:S(2)}) %collective-permute-start.1) | collective-permute-done | bytes 786464 | tf_op jit(solution)/shard_map/ppermute | solution.py:36
  25.0 0.1 fusion.1
  25.0 0.1 collective-permute-start.5
  25.1 0.5 collective-permute-start.6
  25.6 0.1 collective-permute-start.4
  25.7 6.8 %first_tiles.1 = (bf16[5120,768]{1,0:T(8,128)(2,1)S(1)}, f32[10,8,512]{2,1,0:T(8,128)S(1)}, f32[8,512,128]{2,1,0:T(8,128)S(1)}, bf16[17,512,512]{2,1,0:T(8,128)(2,1)S(1)}) custom-call(s32[4]{0:T(128)S(1)} %get-tuple-element.88.refs_0_, s32[16]{0:T(128)S(1)} %get-tuple-element.89.refs_1_, s32[16]{0:T(128)S(1)} %get-tuple-element.90.refs_2_, ...), custom_call_target="tpu_custom_call" | custom-call | flops 1048576 | bytes 1048576 | tf_op jit(solution)/shard_map/first_tiles/pallas_call | solution.py:331
  32.5 0.0 collective-permute-done.6
  32.5 0.1 pad_maximum_fusion.refs_3_
  32.6 3.2 %second_tiles.1 = (bf16[5120,768]{1,0:T(8,128)(2,1)S(1)}, f32[10,8,512]{2,1,0:T(8,128)S(1)}, f32[8,512,128]{2,1,0:T(8,128)S(1)}, bf16[17,512,512]{2,1,0:T(8,128)(2,1)S(1)}) custom-call(s32[4]{0:T(128)S(1)} %get-tuple-element.88.refs_0_, s32[16]{0:T(128)S(1)} %get-tuple-element.89.refs_1_, ...), custom_call_target="tpu_custom_call", output_to_operand_aliasing={{0}: (4, {}), {1}: (5, {}), {2}: (6, {}), {3}: (7, {})} | custom-call | flops 1048576 | bytes 1048576 | tf_op jit(solution)/shard_map/second_tiles/pallas_call | solution.py:331
  35.8 5.7 %collective-permute-done.3.refs_0_ = bf16[512,768]{1,0:T(8,128)(2,1)S(1)} collective-permute-done((bf16[512,768]{1,0:T(8,128)(2,1)S(1)}, bf16[512,768]{1,0:T(8,128)(2,1)S(1)}, u32[]{:S(2)}, u32[]{:S(2)}) %collective-permute-start.3) | collective-permute-done | bytes 786464 | tf_op jit(solution)/shard_map/ppermute | solution.py:36
  41.5 0.0 collective-permute-done.7.refs_1_
  41.5 0.0 collective-permute-done.4.refs_5_
  41.5 0.0 collective-permute-start.8
  41.5 1.8 %collective-permute-start.9 = (bf16[80,1024]{1,0:T(8,128)(2,1)S(1)}, bf16[80,1024]{1,0:T(8,128)(2,1)S(1)}, u32[]{:S(2)}, u32[]{:S(2)}) collective-permute-start(bf16[80,1024]{1,0:T(8,128)(2,1)S(1)} %opening.1.refs_4_), channel_id=1, source_target_pairs={{0,2},{1,3},{2,0},{3,1},{4,6},{5,7},{6,4},{7,5},{8,10},{9,11},{10,... | collective-permute-start | bytes 491528 | tf_op jit(solution)/shard_map/ppermute | solution.py:30
  43.3 1.3 collective-permute-start.11
  44.6 0.8 more_blocks.1
  45.3 5.4 %last_tiles.1 = (bf16[5120,768]{1,0:T(8,128)(2,1)S(1)}, f32[10,8,512]{2,1,0:T(8,128)S(1)}, f32[8,512,128]{2,1,0:T(8,128)S(1)}, bf16[17,512,512]{2,1,0:T(8,128)(2,1)S(1)}) custom-call(s32[4]{0:T(128)S(1)} %get-tuple-element.88.refs_0_, s32[16]{0:T(128)S(1)} %get-tuple-element.89.refs_1_, ...), custom_call_target="tpu_custom_call", output_to_operand_aliasing={{0}: (4, {}), {1}: (5, {}), {2}: (6, {}), {3}: (7, {})} | custom-call | flops 4294967296 | bytes 1048576 | tf_op jit(solution)/shard_map/last_tiles/pallas_call | solution.py:331
  50.7 1.3 collective-permute-start.10
  52.1 3.0 %products.6 = (f32[2,72,512]{2,1,0:T(8,128)S(1)}, f32[4,72,512]{2,1,0:T(8,128)S(1)}, f32[2,72,512]{2,1,0:T(8,128)S(1)}, f32[2,72,512]{2,1,0:T(8,128)S(1)}) custom-call(s32[32]{0:T(128)S(1)} %get-tuple-element.80.refs_0_, s32[32]{0:T(128)S(1)} %get-tuple-element.81.refs_1_, s32[32]{0:T(128)S(1)} %get-tuple-element.82.refs_2_, ...), custom_call_target="tpu_custom_call" | custom-call | flops 1048576 | bytes 1048576 | tf_op jit(solution)/shard_map/products/pallas_call | solution.py:422
  55.1 0.0 collective-permute-done.10.refs_5_
  55.1 4.0 %products.7 = (f32[4,72,512]{2,1,0:T(8,128)S(1)}, f32[2,72,512]{2,1,0:T(8,128)S(1)}, f32[2,72,512]{2,1,0:T(8,128)S(1)}) custom-call(s32[32]{0:T(128)S(1)} %get-tuple-element.80.refs_0_, s32[32]{0:T(128)S(1)} %get-tuple-element.81.refs_1_, s32[32]{0:T(128)S(1)} %get-tuple-element.82.refs_2_, s32[7]{0:T(128)S(1)} %get-tuple-element.83.refs_3_, ...), custom_call_target="tpu_custom_call" | custom-call | flops 2147483648 | bytes 1048576 | tf_op jit(solution)/shard_map/products/pallas_call | solution.py:422
  59.1 0.1 collective-permute-start.12
  59.2 2.0 %collective-permute-done.12.refs_2_ = f32[4,72,512]{2,1,0:T(8,128)S(1)} collective-permute-done((f32[4,72,512]{2,1,0:T(8,128)S(1)}, f32[4,72,512]{2,1,0:T(8,128)S(1)}, u32[]{:S(2)}, u32[]{:S(2)}) %collective-permute-start.12) | collective-permute-done | bytes 589856 | tf_op jit(solution)/shard_map/ppermute | solution.py:30
  61.3 1.0 collective-permute-start.14
  62.2 1.3 collective-permute-start.13
  63.5 1.4 %products.8.refs_0_ = f32[2,72,512]{2,1,0:T(8,128)S(1)} custom-call(s32[32]{0:T(128)S(1)} %get-tuple-element.80.refs_0_, s32[32]{0:T(128)S(1)} %get-tuple-element.81.refs_1_, s32[32]{0:T(128)S(1)} %get-tuple-element.82.refs_2_, s32[7]{0:T(128)S(1)} %get-tuple-element.83.refs_3_, bf16[80,1024]{1,0:T(8,128)(2,1)S(1)} %collective-permute-done.9.refs_4_, ...), custom_call_target="tpu_custom_call" | custom-call | flops 1048576 | bytes 1048576 | tf_op jit(solution)/shard_map/products/pallas_call | solution.py:422
  65.0 5.4 %collective-permute-done.14.refs_3_ = f32[2,72,512]{2,1,0:T(8,128)S(1)} collective-permute-done((f32[2,72,512]{2,1,0:T(8,128)S(1)}, f32[2,72,512]{2,1,0:T(8,128)S(1)}, u32[]{:S(2)}, u32[]{:S(2)}) %collective-permute-start.14) | collective-permute-done | bytes 294944 | tf_op jit(solution)/shard_map/ppermute | solution.py:30
  70.4 0.0 collective-permute-done.13.refs_1_
  70.4 0.9 scaled_gram.2
  71.3 0.1 collective-permute-start.16
  71.4 1.2 collective-permute-start.17
  72.6 0.2 collective-permute-start.15
  72.8 1.3 collective-permute-start.19
  74.1 3.1 %products.9 = (f32[2,64,512]{2,1,0:T(8,128)S(1)}, f32[4,64,512]{2,1,0:T(8,128)S(1)}, f32[2,64,512]{2,1,0:T(8,128)S(1)}, f32[2,64,512]{2,1,0:T(8,128)S(1)}) custom-call(s32[32]{0:T(128)S(1)} %get-tuple-element.80.refs_0_, s32[32]{0:T(128)S(1)} %get-tuple-element.81.refs_1_, s32[32]{0:T(128)S(1)} %get-tuple-element.82.refs_2_, ...), custom_call_target="tpu_custom_call" | custom-call | flops 1048576 | bytes 1048576 | tf_op jit(solution)/shard_map/products/pallas_call | solution.py:422
  77.3 2.9 %collective-permute-done.17.refs_4_ = bf16[128,1024]{1,0:T(8,128)(2,1)S(1)} collective-permute-done((bf16[128,1024]{1,0:T(8,128)(2,1)S(1)}, bf16[128,1024]{1,0:T(8,128)(2,1)S(1)}, u32[]{:S(2)}, u32[]{:S(2)}) %collective-permute-start.17) | collective-permute-done | bytes 262176 | tf_op jit(solution)/shard_map/ppermute | solution.py:30
  80.1 0.0 collective-permute-start.20
  80.1 1.1 collective-permute-start.18
  81.3 2.8 %collective-permute-done.18 = f32[64,64]{1,0:T(8,128)S(1)} collective-permute-done((f32[64,64]{1,0:T(8,128)S(1)}, f32[64,64]{1,0:T(8,128)S(1)}, u32[]{:S(2)}, u32[]{:S(2)}) %collective-permute-start.18) | collective-permute-done | bytes 16416 | tf_op jit(solution)/shard_map/ppermute | solution.py:645
  84.1 2.5 %collective-permute-start.21 = (f32[64,64]{1,0:T(8,128)S(1)}, f32[64,64]{1,0:T(8,128)S(1)}, u32[]{:S(2)}, u32[]{:S(2)}) collective-permute-start(f32[64,64]{1,0:T(8,128)S(1)} %add.23), channel_id=1, source_target_pairs={{0,4},{1,5},{2,6},{3,7},{4,0},{5,1},{6,2},{7,3},{8,12},{9,13},{10,... | collective-permute-start | bytes 49160 | tf_op jit(solution)/shard_map/ppermute | solution.py:645
  86.5 4.1 %products.10 = (f32[4,64,512]{2,1,0:T(8,128)S(1)}, f32[2,64,512]{2,1,0:T(8,128)S(1)}, f32[2,64,512]{2,1,0:T(8,128)S(1)}) custom-call(s32[32]{0:T(128)S(1)} %get-tuple-element.80.refs_0_, s32[32]{0:T(128)S(1)} %get-tuple-element.81.refs_1_, s32[32]{0:T(128)S(1)} %get-tuple-element.82.refs_2_, s32[7]{0:T(128)S(1)} %get-tuple-element.83.refs_3_, ...), custom_call_target="tpu_custom_call" | custom-call | flops 2147483648 | bytes 1048576 | tf_op jit(solution)/shard_map/products/pallas_call | solution.py:422
  90.7 0.1 collective-permute-start.22
  90.8 0.8 collective-permute-start.23
  91.6 3.1 %collective-permute-done.23 = f32[64,64]{1,0:T(8,128)S(1)} collective-permute-done((f32[64,64]{1,0:T(8,128)S(1)}, f32[64,64]{1,0:T(8,128)S(1)}, u32[]{:S(2)}, u32[]{:S(2)}) %collective-permute-start.23) | collective-permute-done | bytes 16416 | tf_op jit(solution)/shard_map/ppermute | solution.py:645
  94.8 1.0 collective-permute-start.25
  95.7 1.6 %collective-permute-start.24 = (f32[2,64,512]{2,1,0:T(8,128)S(1)}, f32[2,64,512]{2,1,0:T(8,128)S(1)}, u32[]{:S(2)}, u32[]{:S(2)}) collective-permute-start(f32[2,64,512]{2,1,0:T(8,128)S(1)} %get-tuple-element.148), channel_id=1, source_target_pairs={{0,4},{4,8},{8,12},{12,16},{16,20},{20,24},{24,28},{1,5},{5,9},{9,... | collective-permute-start | bytes 786440 | tf_op jit(solution)/shard_map/ppermute | solution.py:36
  97.4 3.5 %collective-permute-start.26 = (f32[64,64]{1,0:T(8,128)S(1)}, f32[64,64]{1,0:T(8,128)S(1)}, u32[]{:S(2)}, u32[]{:S(2)}) collective-permute-start(f32[64,64]{1,0:T(8,128)S(1)} %add.26), channel_id=1, source_target_pairs={{0,16},{1,17},{2,18},{3,19},{4,20},{5,21},{6,22},{7,23},{8,24},{9,... | collective-permute-start | bytes 49160 | tf_op jit(solution)/shard_map/ppermute | solution.py:645
  100.9 1.5 %products.11.refs_0_ = f32[2,64,512]{2,1,0:T(8,128)S(1)} custom-call(s32[32]{0:T(128)S(1)} %get-tuple-element.80.refs_0_, s32[32]{0:T(128)S(1)} %get-tuple-element.81.refs_1_, s32[32]{0:T(128)S(1)} %get-tuple-element.82.refs_2_, s32[7]{0:T(128)S(1)} %get-tuple-element.83.refs_3_, bf16[128,1024]{1,0:T(8,128)(2,1)S(1)} %collective-permute-done.17.refs_4_, ...), custom_call_target="tpu_custom_call" | custom-call | flops 1048576 | bytes 1048576 | tf_op jit(solution)/shard_map/products/pallas_call | solution.py:422
  102.3 0.5 collective-permute-done.26
  102.8 2.0 %factor.1.refs_6_ = f32[64,64]{1,0:T(8,128)S(1)} custom-call(f32[64,64]{1,0:T(8,128)S(1)} %add.27.gram), custom_call_target="tpu_custom_call" | custom-call | flops 65536 | bytes 65536 | tf_op jit(solution)/shard_map/factor/pallas_call | solution.py:592
  104.8 1.5 %scaled_gram.3 = (f32[64,1024]{1,0:T(8,128)S(1)}, f32[64,64]{1,0:T(8,128)S(1)}) custom-call(s32[2]{0:T(128)S(1)} %copy-done.2, f32[2,64,512]{2,1,0:T(8,128)S(1)} %products.11.refs_0_, f32[2,64,512]{2,1,0:T(8,128)S(1)} %collective-permute-done.24.refs_1_, f32[4,64,512]{2,1,0:T(8,128)S(1)} %collective-permute-done.22.refs_2_, ...), custom_call_target="tpu_custom_call" | custom-call | flops 67108864 | bytes 2097152 | tf_op jit(solution)/shard_map/scaled_gram/pallas_call | solution.py:533
  106.3 0.1 pad_maximum_fusion.2
  106.4 16.3 %all_to_all.18 = f32[32,1,128]{2,1,0:T(1,128)S(1)} all-to-all(f32[32,1,128]{2,1,0:T(1,128)S(1)} %bitcast.5), channel_id=1, replica_groups=mesh['blk'=8,'grp'=4] {'blk','grp'}, dimensions={0} | all-to-all | bytes 32768 | tf_op jit(solution)/shard_map/all_to_all | solution.py:629
  122.7 0.1 reduce_sum.9
  122.7 8.8 %all_to_all.19 = f32[32,1,128]{2,1,0:T(1,128)S(1)} all-to-all(f32[32,1,128]{2,1,0:T(1,128)S(1)} %broadcast_in_dim.2), channel_id=1, replica_groups=mesh['blk'=8,'grp'=4] {'blk','grp'}, dimensions={0} | all-to-all | bytes 32768 | tf_op jit(solution)/shard_map/all_to_all | solution.py:631
  131.6 0.1 fusion.3
  131.6 3.0 %embedding.1 = f32[64,1024]{1,0:T(8,128)} custom-call(f32[64,64]{1,0:T(8,128)S(1)} %pad_maximum_fusion.1.gram, f32[64,1024]{1,0:T(8,128)S(1)} %get-tuple-element.154.z), custom_call_target="tpu_custom_call" | custom-call | flops 1073741824 | bytes 1048576 | tf_op jit(solution)/shard_map/embedding/pallas_call | solution.py:610
  (34 shorter events, 0.2 us)
Async XLA Ops:
  0.0 25.7 %copy-start = (bf16[1024,768]{1,0:T(8,128)(2,1)S(1)}, bf16[1024,768]{1,0:T(8,128)(2,1)}, u32[]{:S(2)}) copy-start(bf16[1024,768]{1,0:T(8,128)(2,1)} %refs_3_.1) | copy-start | bytes 4718596
  0.0 8.1 %copy-start.3 = (s32[64]{0:T(128)S(1)}, s32[64]{0:T(128)}, u32[]{:S(2)}) copy-start(s32[64]{0:T(128)} %rows.1) | copy-start | bytes 772
  0.0 8.1 %copy-start.4 = (s32[64]{0:T(128)S(1)}, s32[64]{0:T(128)}, u32[]{:S(2)}) copy-start(s32[64]{0:T(128)} %cols.1) | copy-start | bytes 772
  0.0 22.4 %copy-start.1 = (f32[64,1024]{1,0:T(8,128)S(1)}, f32[64,1024]{1,0:T(8,128)}, u32[]{:S(2)}) copy-start(f32[64,1024]{1,0:T(8,128)} %start) | copy-start | bytes 786436
  0.0 22.4 %copy-start.2 = (s32[2]{0:T(128)S(1)}, s32[2]{0:T(128)}, u32[]{:S(2)}) copy-start(s32[2]{0:T(128)} %count_ref.3) | copy-start | bytes 28
  0.0 22.4 %collective-permute-start = (bf16[1024,768]{1,0:T(8,128)(2,1)}, bf16[1024,768]{1,0:T(8,128)(2,1)S(1)}, u32[]{:S(2)}, u32[]{:S(2)}) collective-permute-start(bf16[1024,768]{1,0:T(8,128)(2,1)} %refs_3_.1), channel_id=1, source_target_pairs={{0,1},{1,0},{2,3},{3,2},{4,5},{5,4},{6,7},{7,6},{8,9},{9,8},{10,11... | collective-permute-start | bytes 4718600 | tf_op jit(solution)/shard_map/ppermute | solution.py:30
  2.1 22.9 %collective-permute-start.1 = (bf16[512,768]{1,0:T(8,128)(2,1)S(1)}, bf16[512,768]{1,0:T(8,128)(2,1)S(1)}, u32[]{:S(2)}, u32[]{:S(2)}) collective-permute-start(bf16[512,768]{1,0:T(8,128)(2,1)S(1)} %get-tuple-element.156), channel_id=1, source_target_pairs={{4,0},{8,4},{12,8},{16,12},{20,16},{24,20},{28,24},{5,1},{9,5},{13... | collective-permute-start | bytes 2359304 | tf_op jit(solution)/shard_map/ppermute | solution.py:36
  3.4 21.6 %collective-permute-start.2 = (bf16[512,768]{1,0:T(8,128)(2,1)S(1)}, bf16[512,768]{1,0:T(8,128)(2,1)S(1)}, u32[]{:S(2)}, u32[]{:S(2)}) collective-permute-start(bf16[512,768]{1,0:T(8,128)(2,1)S(1)} %get-tuple-element.156), channel_id=1, source_target_pairs={{0,2},{1,3},{2,0},{3,1},{4,6},{5,7},{6,4},{7,5},{8,10},{9,11},{10,... | collective-permute-start | bytes 2359304 | tf_op jit(solution)/shard_map/ppermute | solution.py:30
  6.0 35.5 %collective-permute-start.3 = (bf16[512,768]{1,0:T(8,128)(2,1)S(1)}, bf16[512,768]{1,0:T(8,128)(2,1)S(1)}, u32[]{:S(2)}, u32[]{:S(2)}) collective-permute-start(bf16[512,768]{1,0:T(8,128)(2,1)S(1)} %get-tuple-element.155), channel_id=1, source_target_pairs={{4,0},{8,4},{12,8},{16,12},{20,16},{24,20},{28,24},{5,1},{9,5},{13... | collective-permute-start | bytes 2359304 | tf_op jit(solution)/shard_map/ppermute | solution.py:36
  7.3 34.2 %collective-permute-start.7 = (bf16[512,768]{1,0:T(8,128)(2,1)S(1)}, bf16[512,768]{1,0:T(8,128)(2,1)S(1)}, u32[]{:S(2)}, u32[]{:S(2)}) collective-permute-start(bf16[512,768]{1,0:T(8,128)(2,1)S(1)} %get-tuple-element.155), channel_id=1, source_target_pairs={{0,2},{1,3},{2,0},{3,1},{4,6},{5,7},{6,4},{7,5},{8,10},{9,11},{10,... | collective-permute-start | bytes 2359304 | tf_op jit(solution)/shard_map/ppermute | solution.py:30
  25.0 7.5 %collective-permute-start.5 = (bf16[256,768]{1,0:T(8,128)(2,1)S(1)}, bf16[256,768]{1,0:T(8,128)(2,1)S(1)}, u32[]{:S(2)}, u32[]{:S(2)}) collective-permute-start(bf16[256,768]{1,0:T(8,128)(2,1)S(1)} %get-tuple-element.157), channel_id=1, source_target_pairs={{0,1},{1,0},{2,3},{3,2},{4,5},{5,4},{6,7},{7,6},{8,9},{9,8},{10,11... | collective-permute-start | bytes 1179656 | tf_op jit(solution)/shard_map/ppermute | solution.py:30
  25.1 7.4 %collective-permute-start.6 = (bf16[256,768]{1,0:T(8,128)(2,1)S(1)}, bf16[256,768]{1,0:T(8,128)(2,1)S(1)}, u32[]{:S(2)}, u32[]{:S(2)}) collective-permute-start(bf16[256,768]{1,0:T(8,128)(2,1)S(1)} %get-tuple-element.158), channel_id=1, source_target_pairs={{0,1},{1,0},{2,3},{3,2},{4,5},{5,4},{6,7},{7,6},{8,9},{9,8},{10,11... | collective-permute-start | bytes 1179656 | tf_op jit(solution)/shard_map/ppermute | solution.py:30
  25.6 15.9 %collective-permute-start.4 = (bf16[80,1024]{1,0:T(8,128)(2,1)S(1)}, bf16[80,1024]{1,0:T(8,128)(2,1)S(1)}, u32[]{:S(2)}, u32[]{:S(2)}) collective-permute-start(bf16[80,1024]{1,0:T(8,128)(2,1)S(1)} %opening.1.refs_4_), channel_id=1, source_target_pairs={{0,1},{1,0},{2,3},{3,2},{4,5},{5,4},{6,7},{7,6},{8,9},{9,8},{10,11... | collective-permute-start | bytes 491528 | tf_op jit(solution)/shard_map/ppermute | solution.py:30
  41.5 3.8 %collective-permute-start.8 = (bf16[512,768]{1,0:T(8,128)(2,1)S(1)}, bf16[512,768]{1,0:T(8,128)(2,1)S(1)}, u32[]{:S(2)}, u32[]{:S(2)}) collective-permute-start(bf16[512,768]{1,0:T(8,128)(2,1)S(1)} %collective-permute-done.7.refs_1_), channel_id=1, source_target_pairs={{0,1},{1,0},{2,3},{3,2},{4,5},{5,4},{6,7},{7,6},{8,9},{9,8},{10,11... | collective-permute-start | bytes 2359304 | tf_op jit(solution)/shard_map/ppermute | solution.py:30
  41.5 9.2 %collective-permute-start.9 = (bf16[80,1024]{1,0:T(8,128)(2,1)S(1)}, bf16[80,1024]{1,0:T(8,128)(2,1)S(1)}, u32[]{:S(2)}, u32[]{:S(2)}) collective-permute-start(bf16[80,1024]{1,0:T(8,128)(2,1)S(1)} %opening.1.refs_4_), channel_id=1, source_target_pairs={{0,2},{1,3},{2,0},{3,1},{4,6},{5,7},{6,4},{7,5},{8,10},{9,11},{10,... | collective-permute-start | bytes 491528 | tf_op jit(solution)/shard_map/ppermute | solution.py:30
  43.3 11.8 %collective-permute-start.11 = (bf16[80,1024]{1,0:T(8,128)(2,1)S(1)}, bf16[80,1024]{1,0:T(8,128)(2,1)S(1)}, u32[]{:S(2)}, u32[]{:S(2)}) collective-permute-start(bf16[80,1024]{1,0:T(8,128)(2,1)S(1)} %opening.1.refs_4_), channel_id=1, source_target_pairs={{4,0},{8,4},{12,8},{16,12},{20,16},{24,20},{28,24},{5,1},{9,5},{13... | collective-permute-start | bytes 491528 | tf_op jit(solution)/shard_map/ppermute | solution.py:36
  50.7 4.4 %collective-permute-start.10 = (bf16[80,1024]{1,0:T(8,128)(2,1)S(1)}, bf16[80,1024]{1,0:T(8,128)(2,1)S(1)}, u32[]{:S(2)}, u32[]{:S(2)}) collective-permute-start(bf16[80,1024]{1,0:T(8,128)(2,1)S(1)} %collective-permute-done.9.refs_4_), channel_id=1, source_target_pairs={{0,1},{1,0},{2,3},{3,2},{4,5},{5,4},{6,7},{7,6},{8,9},{9,8},{10,11... | collective-permute-start | bytes 491528 | tf_op jit(solution)/shard_map/ppermute | solution.py:30
  59.1 2.1 %collective-permute-start.12 = (f32[4,72,512]{2,1,0:T(8,128)S(1)}, f32[4,72,512]{2,1,0:T(8,128)S(1)}, u32[]{:S(2)}, u32[]{:S(2)}) collective-permute-start(f32[4,72,512]{2,1,0:T(8,128)S(1)} %get-tuple-element.117), channel_id=1, source_target_pairs={{0,1},{1,0},{2,3},{3,2},{4,5},{5,4},{6,7},{7,6},{8,9},{9,8},{10,11... | collective-permute-start | bytes 1769480 | tf_op jit(solution)/shard_map/ppermute | solution.py:30
  61.3 9.1 %collective-permute-start.14 = (f32[2,72,512]{2,1,0:T(8,128)S(1)}, f32[2,72,512]{2,1,0:T(8,128)S(1)}, u32[]{:S(2)}, u32[]{:S(2)}) collective-permute-start(f32[2,72,512]{2,1,0:T(8,128)S(1)} %slice_add_fusion), channel_id=1, source_target_pairs={{0,2},{1,3},{2,0},{3,1},{4,6},{5,7},{6,4},{7,5},{8,10},{9,11},{10,... | collective-permute-start | bytes 884744 | tf_op jit(solution)/shard_map/ppermute | solution.py:30
  62.2 8.1 %collective-permute-start.13 = (f32[2,72,512]{2,1,0:T(8,128)S(1)}, f32[2,72,512]{2,1,0:T(8,128)S(1)}, u32[]{:S(2)}, u32[]{:S(2)}) collective-permute-start(f32[2,72,512]{2,1,0:T(8,128)S(1)} %get-tuple-element.122), channel_id=1, source_target_pairs={{0,4},{4,8},{8,12},{12,16},{16,20},{20,24},{24,28},{1,5},{5,9},{9,... | collective-permute-start | bytes 884744 | tf_op jit(solution)/shard_map/ppermute | solution.py:36
  71.3 2.8 %collective-permute-start.16 = (bf16[128,1024]{1,0:T(8,128)(2,1)S(1)}, bf16[128,1024]{1,0:T(8,128)(2,1)S(1)}, u32[]{:S(2)}, u32[]{:S(2)}) collective-permute-start(bf16[128,1024]{1,0:T(8,128)(2,1)S(1)} %get-tuple-element.125.refs_4_), channel_id=1, source_target_pairs={{0,1},{1,0},{2,3},{3,2},{4,5},{5,4},{6,7},{7,6},{8,9},{9,8},{10,11... | collective-permute-start | bytes 786440 | tf_op jit(solution)/shard_map/ppermute | solution.py:30
  71.4 8.7 %collective-permute-start.17 = (bf16[128,1024]{1,0:T(8,128)(2,1)S(1)}, bf16[128,1024]{1,0:T(8,128)(2,1)S(1)}, u32[]{:S(2)}, u32[]{:S(2)}) collective-permute-start(bf16[128,1024]{1,0:T(8,128)(2,1)S(1)} %get-tuple-element.125.refs_4_), channel_id=1, source_target_pairs={{0,2},{1,3},{2,0},{3,1},{4,6},{5,7},{6,4},{7,5},{8,10},{9,11},{10,... | collective-permute-start | bytes 786440 | tf_op jit(solution)/shard_map/ppermute | solution.py:30
  72.6 1.5 %collective-permute-start.15 = (f32[64,64]{1,0:T(8,128)S(1)}, f32[64,64]{1,0:T(8,128)S(1)}, u32[]{:S(2)}, u32[]{:S(2)}) collective-permute-start(f32[64,64]{1,0:T(8,128)S(1)} %get-tuple-element.124), channel_id=1, source_target_pairs={{0,1},{1,0},{2,3},{3,2},{4,5},{5,4},{6,7},{7,6},{8,9},{9,8},{10,11... | collective-permute-start | bytes 49160 | tf_op jit(solution)/shard_map/ppermute | solution.py:645
  72.8 11.3 %collective-permute-start.19 = (bf16[128,1024]{1,0:T(8,128)(2,1)S(1)}, bf16[128,1024]{1,0:T(8,128)(2,1)S(1)}, u32[]{:S(2)}, u32[]{:S(2)}) collective-permute-start(bf16[128,1024]{1,0:T(8,128)(2,1)S(1)} %get-tuple-element.125.refs_4_), channel_id=1, source_target_pairs={{4,0},{8,4},{12,8},{16,12},{20,16},{24,20},{28,24},{5,1},{9,5},{13... | collective-permute-start | bytes 786440 | tf_op jit(solution)/shard_map/ppermute | solution.py:36
  80.1 3.9 %collective-permute-start.20 = (bf16[128,1024]{1,0:T(8,128)(2,1)S(1)}, bf16[128,1024]{1,0:T(8,128)(2,1)S(1)}, u32[]{:S(2)}, u32[]{:S(2)}) collective-permute-start(bf16[128,1024]{1,0:T(8,128)(2,1)S(1)} %collective-permute-done.17.refs_4_), channel_id=1, source_target_pairs={{0,1},{1,0},{2,3},{3,2},{4,5},{5,4},{6,7},{7,6},{8,9},{9,8},{10,11... | collective-permute-start | bytes 786440 | tf_op jit(solution)/shard_map/ppermute | solution.py:30
  80.1 3.9 %collective-permute-start.18 = (f32[64,64]{1,0:T(8,128)S(1)}, f32[64,64]{1,0:T(8,128)S(1)}, u32[]{:S(2)}, u32[]{:S(2)}) collective-permute-start(f32[64,64]{1,0:T(8,128)S(1)} %add.22), channel_id=1, source_target_pairs={{0,2},{1,3},{2,0},{3,1},{4,6},{5,7},{6,4},{7,5},{8,10},{9,11},{10,... | collective-permute-start | bytes 49160 | tf_op jit(solution)/shard_map/ppermute | solution.py:645
  84.1 6.6 %collective-permute-start.21 = (f32[64,64]{1,0:T(8,128)S(1)}, f32[64,64]{1,0:T(8,128)S(1)}, u32[]{:S(2)}, u32[]{:S(2)}) collective-permute-start(f32[64,64]{1,0:T(8,128)S(1)} %add.23), channel_id=1, source_target_pairs={{0,4},{1,5},{2,6},{3,7},{4,0},{5,1},{6,2},{7,3},{8,12},{9,13},{10,... | collective-permute-start | bytes 49160 | tf_op jit(solution)/shard_map/ppermute | solution.py:645
  90.7 4.1 %collective-permute-start.22 = (f32[4,64,512]{2,1,0:T(8,128)S(1)}, f32[4,64,512]{2,1,0:T(8,128)S(1)}, u32[]{:S(2)}, u32[]{:S(2)}) collective-permute-start(f32[4,64,512]{2,1,0:T(8,128)S(1)} %get-tuple-element.140), channel_id=1, source_target_pairs={{0,1},{1,0},{2,3},{3,2},{4,5},{5,4},{6,7},{7,6},{8,9},{9,8},{10,11... | collective-permute-start | bytes 1572872 | tf_op jit(solution)/shard_map/ppermute | solution.py:30
  90.8 4.0 %collective-permute-start.23 = (f32[64,64]{1,0:T(8,128)S(1)}, f32[64,64]{1,0:T(8,128)S(1)}, u32[]{:S(2)}, u32[]{:S(2)}) collective-permute-start(f32[64,64]{1,0:T(8,128)S(1)} %add.24), channel_id=1, source_target_pairs={{0,8},{1,9},{2,10},{3,11},{4,12},{5,13},{6,14},{7,15},{8,0},{9,1},... | collective-permute-start | bytes 49160 | tf_op jit(solution)/shard_map/ppermute | solution.py:645
  94.8 10.0 %collective-permute-start.25 = (f32[2,64,512]{2,1,0:T(8,128)S(1)}, f32[2,64,512]{2,1,0:T(8,128)S(1)}, u32[]{:S(2)}, u32[]{:S(2)}) collective-permute-start(f32[2,64,512]{2,1,0:T(8,128)S(1)} %slice_add_fusion.1), channel_id=1, source_target_pairs={{0,2},{1,3},{2,0},{3,1},{4,6},{5,7},{6,4},{7,5},{8,10},{9,11},{10,... | collective-permute-start | bytes 786440 | tf_op jit(solution)/shard_map/ppermute | solution.py:30
  95.7 9.0 %collective-permute-start.24 = (f32[2,64,512]{2,1,0:T(8,128)S(1)}, f32[2,64,512]{2,1,0:T(8,128)S(1)}, u32[]{:S(2)}, u32[]{:S(2)}) collective-permute-start(f32[2,64,512]{2,1,0:T(8,128)S(1)} %get-tuple-element.148), channel_id=1, source_target_pairs={{0,4},{4,8},{8,12},{12,16},{16,20},{20,24},{24,28},{1,5},{5,9},{9,... | collective-permute-start | bytes 786440 | tf_op jit(solution)/shard_map/ppermute | solution.py:36
  97.4 5.4 %collective-permute-start.26 = (f32[64,64]{1,0:T(8,128)S(1)}, f32[64,64]{1,0:T(8,128)S(1)}, u32[]{:S(2)}, u32[]{:S(2)}) collective-permute-start(f32[64,64]{1,0:T(8,128)S(1)} %add.26), channel_id=1, source_target_pairs={{0,16},{1,17},{2,18},{3,19},{4,20},{5,21},{6,22},{7,23},{8,24},{9,... | collective-permute-start | bytes 49160 | tf_op jit(solution)/shard_map/ppermute | solution.py:645

commit v14 on v12

--- a/solution.py
+++ b/solution.py
@@ -620,6 +620,12 @@
 
 def sum_stages():
     return bits_of(lax.axis_size("blk") * lax.axis_size("grp"))
+
+
+def sum_over(value, axis):
+    count = lax.axis_size(axis)
+    copies = jnp.broadcast_to(value[None], (count,) + value.shape)
+    return jnp.sum(lax.all_to_all(copies, axis, 0, 0, tiled=True), axis=0)
 
 
 def pairs_of(bits):
@@ -766,8 +772,10 @@
         inverse = factor(gram)
         z, gram, *parts = scaled_gram(sums, z, counts, degree, inverse, turn + 1 < ITERS)
         parts = parts[0] if parts else None
-    stages = sum_stages()
-    return embedding(all_sum(gram, stages[:1] + pairs_of(stages[1:])), z)
+    half = columns // 2
+    gram = jnp.concatenate([gram[:half], gram[half:]], axis=1)
+    gram = sum_over(sum_over(gram, "grp"), "blk")
+    return embedding(jnp.concatenate([gram[:, :columns], gram[:, columns:]], axis=0), z)
 
 
 def solution(mesh):

time: 132 us -> 137 us (1.038); the launches traced: 133 us -> 136 us
  blocking collectives: 0 us -> 21.4 us
  starting transfers between devices: 41.9 us -> 32.2 us
  waiting for transfers between devices: 32.3 us -> 23.3 us
    all_to_all x0 -> x2, blocking collectives: none -> 21.4 us  [sum_over(): return jnp.sum(lax.all_to_all(copies, axis, 0, 0, tiled=True), axis=0)]
    ppermute x12 -> x5, waiting for transfers between devices: 15 us -> 5.1 us  [all_sum(): lax.ppermute(value, ('blk', 'grp'), [(source, source ^ move) for source i...]
    ppermute x12 -> x5, starting transfers between devices: 21.7 us -> 12.1 us  [all_sum(): lax.ppermute(value, ('blk', 'grp'), [(source, source ^ move) for source i...]
  transfers between devices with their start and end apart: 34 -> 27, of which waited for: 14 -> 7; matrix products, arithmetic and copies ran while one was open for 1% -> 1% of each run, Pallas kernels for 35% -> 35%
where the time goes in v14:
time: 137 us; the launch traced here: 136 us
  Pallas kernels  55.7 us (41%)
  starting transfers between devices  32.2 us (24%)
  waiting for transfers between devices  23.3 us (17%)
  blocking collectives  21.4 us (16%)
  local copies, waits for them, and re-layouts  1.67 us (1%)
    all_to_all x2, blocking collectives, sum_over(): return jnp.sum(lax.all_to_all(copies, axis, 0, 0, tiled=True), axis=0)  21.4 us
    pallas_call x6, Pallas kernels, products(): pl.pallas_call(kernel, out_shape=shapes, in_specs=[spec(SMEM)] * 4 + [spe...  17.2 us
    pallas_call x4, Pallas kernels, build_tiles(): pl.pallas_call(kernel, out_shape=shapes, in_specs=[spec(SMEM)] * len(scal...  16.2 us
    pallas_call x1, Pallas kernels, listing(): pl.pallas_call(functools.partial(listing_kernel, group, cap, blocks_dev),...  14.3 us
    ppermute x5, starting transfers between devices, all_sum(): lax.ppermute(value, ('blk', 'grp'), [(source, source ^ move) for source i...  12.1 us
    ppermute x6, starting transfers between devices, from_behind(): lax.ppermute(value, axis, [(source, source + steps) for source in range(i...  10.2 us
    ppermute x16, starting transfers between devices, swap(): lax.ppermute(value, axis, [(source, source ^ bit) for source in range(cou...  9.91 us
    ppermute x16, waiting for transfers between devices, swap(): lax.ppermute(value, axis, [(source, source ^ bit) for source in range(cou...  9.47 us
  transfers between devices with their start and end apart: 27, of which 7 were waited for; matrix products, arithmetic and copies ran while one was open for 1% of the time, Pallas kernels for 35%

profile of v14, /device:TPU:0, one launch (start us, length us, event | category | flops | bytes accessed | tf_op | source)
XLA Modules:
  0.0 135.7 jit_solution(5892043583000760494)
XLA Ops:
  0.0 0.5 collective-permute-start
  0.5 1.5 %fusion = (bf16[512,768]{1,0:T(8,128)(2,1)S(1)}, bf16[512,768]{1,0:T(8,128)(2,1)S(1)}) fusion(bf16[1024,768]{1,0:T(8,128)(2,1)} %refs_3_.1), kind=kLoop, calls=%fused_computation.5 | loop fusion | bytes 3145728 | tf_op jit(solution)/shard_map/slice | solution.py:667
  2.1 1.3 collective-permute-start.1
  3.4 2.7 %collective-permute-start.2 = (bf16[512,768]{1,0:T(8,128)(2,1)S(1)}, bf16[512,768]{1,0:T(8,128)(2,1)S(1)}, u32[]{:S(2)}, u32[]{:S(2)}) collective-permute-start(bf16[512,768]{1,0:T(8,128)(2,1)S(1)} %get-tuple-element.156), channel_id=1, source_target_pairs={{0,2},{1,3},{2,0},{3,1},{4,6},{5,7},{6,4},{7,5},{8,10},{9,11},{10,... | collective-permute-start | bytes 2359304 | tf_op jit(solution)/shard_map/ppermute | solution.py:30
  6.0 1.3 collective-permute-start.3
  7.3 0.1 collective-permute-start.7
  8.1 14.3 %listing.1 = (s32[16]{0:T(128)S(1)}, s32[16]{0:T(128)S(1)}, s32[4]{0:T(128)S(1)}, s32[32]{0:T(128)S(1)}, s32[32]{0:T(128)S(1)}, /*index=5*/s32[32]{0:T(128)S(1)}, s32[7]{0:T(128)S(1)}) custom-call(s32[64]{0:T(128)S(1)} %copy-done.3, s32[64]{0:T(128)S(1)} %copy-done.4, s32[1]{0:T(128)S(6)} %copy.29.live), custom_call_target="tpu_custom_call" | custom-call | flops 1048576 | bytes 1024 | tf_op jit(solution)/shard_map/listing/pallas_call | solution.py:214
  22.4 0.6 opening.1.refs_4_
  23.0 2.0 %collective-permute-done.1.refs_5_ = bf16[512,768]{1,0:T(8,128)(2,1)S(1)} collective-permute-done((bf16[512,768]{1,0:T(8,128)(2,1)S(1)}, bf16[512,768]{1,0:T(8,128)(2,1)S(1)}, u32[]{:S(2)}, u32[]{:S(2)}) %collective-permute-start.1) | collective-permute-done | bytes 786464 | tf_op jit(solution)/shard_map/ppermute | solution.py:36
  25.0 0.1 fusion.1
  25.0 0.1 collective-permute-start.5
  25.1 0.5 collective-permute-start.6
  25.6 0.1 collective-permute-start.4
  25.7 6.8 %first_tiles.1 = (bf16[5120,768]{1,0:T(8,128)(2,1)S(1)}, f32[10,8,512]{2,1,0:T(8,128)S(1)}, f32[8,512,128]{2,1,0:T(8,128)S(1)}, bf16[17,512,512]{2,1,0:T(8,128)(2,1)S(1)}) custom-call(s32[4]{0:T(128)S(1)} %get-tuple-element.88.refs_0_, s32[16]{0:T(128)S(1)} %get-tuple-element.89.refs_1_, s32[16]{0:T(128)S(1)} %get-tuple-element.90.refs_2_, ...), custom_call_target="tpu_custom_call" | custom-call | flops 1048576 | bytes 1048576 | tf_op jit(solution)/shard_map/first_tiles/pallas_call | solution.py:331
  32.5 0.0 collective-permute-done.6
  32.5 0.1 pad_maximum_fusion.refs_3_
  32.6 2.1 %second_tiles.1 = (bf16[5120,768]{1,0:T(8,128)(2,1)S(1)}, f32[10,8,512]{2,1,0:T(8,128)S(1)}, f32[8,512,128]{2,1,0:T(8,128)S(1)}, bf16[17,512,512]{2,1,0:T(8,128)(2,1)S(1)}) custom-call(s32[4]{0:T(128)S(1)} %get-tuple-element.88.refs_0_, s32[16]{0:T(128)S(1)} %get-tuple-element.89.refs_1_, ...), custom_call_target="tpu_custom_call", output_to_operand_aliasing={{0}: (4, {}), {1}: (5, {}), {2}: (6, {}), {3}: (7, {})} | custom-call | flops 1048576 | bytes 1048576 | tf_op jit(solution)/shard_map/second_tiles/pallas_call | solution.py:331
  34.7 6.8 %collective-permute-done.3.refs_0_ = bf16[512,768]{1,0:T(8,128)(2,1)S(1)} collective-permute-done((bf16[512,768]{1,0:T(8,128)(2,1)S(1)}, bf16[512,768]{1,0:T(8,128)(2,1)S(1)}, u32[]{:S(2)}, u32[]{:S(2)}) %collective-permute-start.3) | collective-permute-done | bytes 786464 | tf_op jit(solution)/shard_map/ppermute | solution.py:36
  41.5 0.0 collective-permute-done.7.refs_1_
  41.5 0.0 collective-permute-done.4.refs_5_
  41.5 0.0 collective-permute-start.8
  41.5 1.8 %collective-permute-start.9 = (bf16[80,1024]{1,0:T(8,128)(2,1)S(1)}, bf16[80,1024]{1,0:T(8,128)(2,1)S(1)}, u32[]{:S(2)}, u32[]{:S(2)}) collective-permute-start(bf16[80,1024]{1,0:T(8,128)(2,1)S(1)} %opening.1.refs_4_), channel_id=1, source_target_pairs={{0,2},{1,3},{2,0},{3,1},{4,6},{5,7},{6,4},{7,5},{8,10},{9,11},{10,... | collective-permute-start | bytes 491528 | tf_op jit(solution)/shard_map/ppermute | solution.py:30
  43.3 1.3 collective-permute-start.11
  44.6 0.8 more_blocks.1
  45.3 6.5 %last_tiles.1 = (bf16[5120,768]{1,0:T(8,128)(2,1)S(1)}, f32[10,8,512]{2,1,0:T(8,128)S(1)}, f32[8,512,128]{2,1,0:T(8,128)S(1)}, bf16[17,512,512]{2,1,0:T(8,128)(2,1)S(1)}) custom-call(s32[4]{0:T(128)S(1)} %get-tuple-element.88.refs_0_, s32[16]{0:T(128)S(1)} %get-tuple-element.89.refs_1_, ...), custom_call_target="tpu_custom_call", output_to_operand_aliasing={{0}: (4, {}), {1}: (5, {}), {2}: (6, {}), {3}: (7, {})} | custom-call | flops 4294967296 | bytes 1048576 | tf_op jit(solution)/shard_map/last_tiles/pallas_call | solution.py:331
  51.8 0.0 collective-permute-done.9.refs_4_
  51.8 0.2 collective-permute-start.10
  52.1 3.0 %products.6 = (f32[2,72,512]{2,1,0:T(8,128)S(1)}, f32[4,72,512]{2,1,0:T(8,128)S(1)}, f32[2,72,512]{2,1,0:T(8,128)S(1)}, f32[2,72,512]{2,1,0:T(8,128)S(1)}) custom-call(s32[32]{0:T(128)S(1)} %get-tuple-element.80.refs_0_, s32[32]{0:T(128)S(1)} %get-tuple-element.81.refs_1_, s32[32]{0:T(128)S(1)} %get-tuple-element.82.refs_2_, ...), custom_call_target="tpu_custom_call" | custom-call | flops 1048576 | bytes 1048576 | tf_op jit(solution)/shard_map/products/pallas_call | solution.py:422
  55.1 0.0 collective-permute-done.10.refs_5_
  55.1 3.3 %products.7 = (f32[4,72,512]{2,1,0:T(8,128)S(1)}, f32[2,72,512]{2,1,0:T(8,128)S(1)}, f32[2,72,512]{2,1,0:T(8,128)S(1)}) custom-call(s32[32]{0:T(128)S(1)} %get-tuple-element.80.refs_0_, s32[32]{0:T(128)S(1)} %get-tuple-element.81.refs_1_, s32[32]{0:T(128)S(1)} %get-tuple-element.82.refs_2_, s32[7]{0:T(128)S(1)} %get-tuple-element.83.refs_3_, ...), custom_call_target="tpu_custom_call" | custom-call | flops 2147483648 | bytes 1048576 | tf_op jit(solution)/shard_map/products/pallas_call | solution.py:422
  58.4 1.2 collective-permute-start.12
  59.6 1.6 %collective-permute-done.12.refs_2_ = f32[4,72,512]{2,1,0:T(8,128)S(1)} collective-permute-done((f32[4,72,512]{2,1,0:T(8,128)S(1)}, f32[4,72,512]{2,1,0:T(8,128)S(1)}, u32[]{:S(2)}, u32[]{:S(2)}) %collective-permute-start.12) | collective-permute-done | bytes 589856 | tf_op jit(solution)/shard_map/ppermute | solution.py:30
  61.2 0.4 collective-permute-start.14
  61.6 2.2 %collective-permute-start.13 = (f32[2,72,512]{2,1,0:T(8,128)S(1)}, f32[2,72,512]{2,1,0:T(8,128)S(1)}, u32[]{:S(2)}, u32[]{:S(2)}) collective-permute-start(f32[2,72,512]{2,1,0:T(8,128)S(1)} %get-tuple-element.122), channel_id=1, source_target_pairs={{0,4},{4,8},{8,12},{12,16},{16,20},{20,24},{24,28},{1,5},{5,9},{9,... | collective-permute-start | bytes 884744 | tf_op jit(solution)/shard_map/ppermute | solution.py:36
  63.8 2.2 %products.8.refs_0_ = f32[2,72,512]{2,1,0:T(8,128)S(1)} custom-call(s32[32]{0:T(128)S(1)} %get-tuple-element.80.refs_0_, s32[32]{0:T(128)S(1)} %get-tuple-element.81.refs_1_, s32[32]{0:T(128)S(1)} %get-tuple-element.82.refs_2_, s32[7]{0:T(128)S(1)} %get-tuple-element.83.refs_3_, bf16[80,1024]{1,0:T(8,128)(2,1)S(1)} %collective-permute-done.9.refs_4_, ...), custom_call_target="tpu_custom_call" | custom-call | flops 1048576 | bytes 1048576 | tf_op jit(solution)/shard_map/products/pallas_call | solution.py:422
  66.0 4.6 %collective-permute-done.14.refs_3_ = f32[2,72,512]{2,1,0:T(8,128)S(1)} collective-permute-done((f32[2,72,512]{2,1,0:T(8,128)S(1)}, f32[2,72,512]{2,1,0:T(8,128)S(1)}, u32[]{:S(2)}, u32[]{:S(2)}) %collective-permute-start.14) | collective-permute-done | bytes 294944 | tf_op jit(solution)/shard_map/ppermute | solution.py:30
  70.6 0.0 collective-permute-done.13.refs_1_
  70.6 1.0 scaled_gram.2
  71.5 0.1 collective-permute-start.16
  71.6 0.9 collective-permute-start.17
  72.5 0.2 collective-permute-start.15
  72.7 1.3 collective-permute-start.19
  74.0 0.0 collective-permute-done.16.refs_5_
  74.0 3.1 %products.9 = (f32[2,64,512]{2,1,0:T(8,128)S(1)}, f32[4,64,512]{2,1,0:T(8,128)S(1)}, f32[2,64,512]{2,1,0:T(8,128)S(1)}, f32[2,64,512]{2,1,0:T(8,128)S(1)}) custom-call(s32[32]{0:T(128)S(1)} %get-tuple-element.80.refs_0_, s32[32]{0:T(128)S(1)} %get-tuple-element.81.refs_1_, s32[32]{0:T(128)S(1)} %get-tuple-element.82.refs_2_, ...), custom_call_target="tpu_custom_call" | custom-call | flops 1048576 | bytes 1048576 | tf_op jit(solution)/shard_map/products/pallas_call | solution.py:422
  77.1 3.2 %collective-permute-done.17.refs_4_ = bf16[128,1024]{1,0:T(8,128)(2,1)S(1)} collective-permute-done((bf16[128,1024]{1,0:T(8,128)(2,1)S(1)}, bf16[128,1024]{1,0:T(8,128)(2,1)S(1)}, u32[]{:S(2)}, u32[]{:S(2)}) %collective-permute-start.17) | collective-permute-done | bytes 262176 | tf_op jit(solution)/shard_map/ppermute | solution.py:30
  80.4 0.0 collective-permute-start.20
  80.4 0.8 collective-permute-start.18
  81.2 3.1 %collective-permute-done.18 = f32[64,64]{1,0:T(8,128)S(1)} collective-permute-done((f32[64,64]{1,0:T(8,128)S(1)}, f32[64,64]{1,0:T(8,128)S(1)}, u32[]{:S(2)}, u32[]{:S(2)}) %collective-permute-start.18) | collective-permute-done | bytes 16416 | tf_op jit(solution)/shard_map/ppermute | solution.py:642
  84.3 3.5 %collective-permute-start.21 = (f32[64,64]{1,0:T(8,128)S(1)}, f32[64,64]{1,0:T(8,128)S(1)}, u32[]{:S(2)}, u32[]{:S(2)}) collective-permute-start(f32[64,64]{1,0:T(8,128)S(1)} %add.23), channel_id=1, source_target_pairs={{0,4},{1,5},{2,6},{3,7},{4,0},{5,1},{6,2},{7,3},{8,12},{9,13},{10,... | collective-permute-start | bytes 49160 | tf_op jit(solution)/shard_map/ppermute | solution.py:642
  87.8 3.3 %products.10 = (f32[4,64,512]{2,1,0:T(8,128)S(1)}, f32[2,64,512]{2,1,0:T(8,128)S(1)}, f32[2,64,512]{2,1,0:T(8,128)S(1)}) custom-call(s32[32]{0:T(128)S(1)} %get-tuple-element.80.refs_0_, s32[32]{0:T(128)S(1)} %get-tuple-element.81.refs_1_, s32[32]{0:T(128)S(1)} %get-tuple-element.82.refs_2_, s32[7]{0:T(128)S(1)} %get-tuple-element.83.refs_3_, ...), custom_call_target="tpu_custom_call" | custom-call | flops 2147483648 | bytes 1048576 | tf_op jit(solution)/shard_map/products/pallas_call | solution.py:422
  91.1 0.4 collective-permute-start.22
  91.6 3.3 %collective-permute-start.23 = (f32[64,64]{1,0:T(8,128)S(1)}, f32[64,64]{1,0:T(8,128)S(1)}, u32[]{:S(2)}, u32[]{:S(2)}) collective-permute-start(f32[64,64]{1,0:T(8,128)S(1)} %add.24), channel_id=1, source_target_pairs={{0,8},{1,9},{2,10},{3,11},{4,12},{5,13},{6,14},{7,15},{8,0},{9,1},... | collective-permute-start | bytes 49160 | tf_op jit(solution)/shard_map/ppermute | solution.py:642
  94.9 2.0 %collective-permute-done.23 = f32[64,64]{1,0:T(8,128)S(1)} collective-permute-done((f32[64,64]{1,0:T(8,128)S(1)}, f32[64,64]{1,0:T(8,128)S(1)}, u32[]{:S(2)}, u32[]{:S(2)}) %collective-permute-start.23) | collective-permute-done | bytes 16416 | tf_op jit(solution)/shard_map/ppermute | solution.py:642
  96.9 1.0 collective-permute-start.25
  97.9 2.9 %collective-permute-start.24 = (f32[2,64,512]{2,1,0:T(8,128)S(1)}, f32[2,64,512]{2,1,0:T(8,128)S(1)}, u32[]{:S(2)}, u32[]{:S(2)}) collective-permute-start(f32[2,64,512]{2,1,0:T(8,128)S(1)} %get-tuple-element.148), channel_id=1, source_target_pairs={{0,4},{4,8},{8,12},{12,16},{16,20},{20,24},{24,28},{1,5},{5,9},{9,... | collective-permute-start | bytes 786440 | tf_op jit(solution)/shard_map/ppermute | solution.py:36
  100.8 4.3 %collective-permute-start.26 = (f32[64,64]{1,0:T(8,128)S(1)}, f32[64,64]{1,0:T(8,128)S(1)}, u32[]{:S(2)}, u32[]{:S(2)}) collective-permute-start(f32[64,64]{1,0:T(8,128)S(1)} %add.26), channel_id=1, source_target_pairs={{0,16},{1,17},{2,18},{3,19},{4,20},{5,21},{6,22},{7,23},{8,24},{9,... | collective-permute-start | bytes 49160 | tf_op jit(solution)/shard_map/ppermute | solution.py:642
  105.1 2.3 %products.11.refs_0_ = f32[2,64,512]{2,1,0:T(8,128)S(1)} custom-call(s32[32]{0:T(128)S(1)} %get-tuple-element.80.refs_0_, s32[32]{0:T(128)S(1)} %get-tuple-element.81.refs_1_, s32[32]{0:T(128)S(1)} %get-tuple-element.82.refs_2_, s32[7]{0:T(128)S(1)} %get-tuple-element.83.refs_3_, bf16[128,1024]{1,0:T(8,128)(2,1)S(1)} %collective-permute-done.17.refs_4_, ...), custom_call_target="tpu_custom_call" | custom-call | flops 1048576 | bytes 1048576 | tf_op jit(solution)/shard_map/products/pallas_call | solution.py:422
  107.5 2.0 %factor.1.refs_6_ = f32[64,64]{1,0:T(8,128)S(1)} custom-call(f32[64,64]{1,0:T(8,128)S(1)} %add.27.gram), custom_call_target="tpu_custom_call" | custom-call | flops 65536 | bytes 65536 | tf_op jit(solution)/shard_map/factor/pallas_call | solution.py:592
  109.4 1.5 %scaled_gram.3 = (f32[64,1024]{1,0:T(8,128)S(1)}, f32[64,64]{1,0:T(8,128)S(1)}) custom-call(s32[2]{0:T(128)S(1)} %copy-done.2, f32[2,64,512]{2,1,0:T(8,128)S(1)} %products.11.refs_0_, f32[2,64,512]{2,1,0:T(8,128)S(1)} %collective-permute-done.24.refs_1_, f32[4,64,512]{2,1,0:T(8,128)S(1)} %collective-permute-done.22.refs_2_, ...), custom_call_target="tpu_custom_call" | custom-call | flops 67108864 | bytes 2097152 | tf_op jit(solution)/shard_map/scaled_gram/pallas_call | solution.py:533
  111.0 0.1 pad_maximum_fusion.2
  111.0 6.5 %all_to_all.10 = f32[4,32,128]{2,1,0:T(8,128)S(1)} all-to-all(f32[4,32,128]{2,1,0:T(8,128)S(1)} %broadcast_in_dim.4), channel_id=1, replica_groups=mesh['blk'=8,'grp'=4] {'grp'}, dimensions={0} | all-to-all | bytes 131072 | tf_op jit(solution)/shard_map/all_to_all | solution.py:628
  117.5 15.0 %all_to_all.11 = f32[8,32,128]{2,1,0:T(8,128)S(1)} all-to-all(f32[8,32,128]{2,1,0:T(8,128)S(1)} %broadcast_in_dim.5), channel_id=1, replica_groups=mesh['blk'=8,'grp'=4] {'blk'}, dimensions={0} | all-to-all | bytes 262144 | tf_op jit(solution)/shard_map/all_to_all | solution.py:628
  132.5 0.1 fusion.3
  132.6 3.0 %embedding.1 = f32[64,1024]{1,0:T(8,128)} custom-call(f32[64,64]{1,0:T(8,128)S(1)} %pad_maximum_fusion.1.gram, f32[64,1024]{1,0:T(8,128)S(1)} %get-tuple-element.154.z), custom_call_target="tpu_custom_call" | custom-call | flops 1073741824 | bytes 1048576 | tf_op jit(solution)/shard_map/embedding/pallas_call | solution.py:610
  (36 shorter events, 0.2 us)
Async XLA Ops:
  0.0 25.7 %copy-start = (bf16[1024,768]{1,0:T(8,128)(2,1)S(1)}, bf16[1024,768]{1,0:T(8,128)(2,1)}, u32[]{:S(2)}) copy-start(bf16[1024,768]{1,0:T(8,128)(2,1)} %refs_3_.1) | copy-start | bytes 4718596
  0.0 8.1 %copy-start.3 = (s32[64]{0:T(128)S(1)}, s32[64]{0:T(128)}, u32[]{:S(2)}) copy-start(s32[64]{0:T(128)} %rows.1) | copy-start | bytes 772
  0.0 8.1 %copy-start.4 = (s32[64]{0:T(128)S(1)}, s32[64]{0:T(128)}, u32[]{:S(2)}) copy-start(s32[64]{0:T(128)} %cols.1) | copy-start | bytes 772
  0.0 22.4 %copy-start.1 = (f32[64,1024]{1,0:T(8,128)S(1)}, f32[64,1024]{1,0:T(8,128)}, u32[]{:S(2)}) copy-start(f32[64,1024]{1,0:T(8,128)} %start) | copy-start | bytes 786436
  0.0 22.4 %copy-start.2 = (s32[2]{0:T(128)S(1)}, s32[2]{0:T(128)}, u32[]{:S(2)}) copy-start(s32[2]{0:T(128)} %count_ref.3) | copy-start | bytes 28
  0.0 22.4 %collective-permute-start = (bf16[1024,768]{1,0:T(8,128)(2,1)}, bf16[1024,768]{1,0:T(8,128)(2,1)S(1)}, u32[]{:S(2)}, u32[]{:S(2)}) collective-permute-start(bf16[1024,768]{1,0:T(8,128)(2,1)} %refs_3_.1), channel_id=1, source_target_pairs={{0,1},{1,0},{2,3},{3,2},{4,5},{5,4},{6,7},{7,6},{8,9},{9,8},{10,11... | collective-permute-start | bytes 4718600 | tf_op jit(solution)/shard_map/ppermute | solution.py:30
  2.1 22.9 %collective-permute-start.1 = (bf16[512,768]{1,0:T(8,128)(2,1)S(1)}, bf16[512,768]{1,0:T(8,128)(2,1)S(1)}, u32[]{:S(2)}, u32[]{:S(2)}) collective-permute-start(bf16[512,768]{1,0:T(8,128)(2,1)S(1)} %get-tuple-element.156), channel_id=1, source_target_pairs={{4,0},{8,4},{12,8},{16,12},{20,16},{24,20},{28,24},{5,1},{9,5},{13... | collective-permute-start | bytes 2359304 | tf_op jit(solution)/shard_map/ppermute | solution.py:36
  3.4 21.6 %collective-permute-start.2 = (bf16[512,768]{1,0:T(8,128)(2,1)S(1)}, bf16[512,768]{1,0:T(8,128)(2,1)S(1)}, u32[]{:S(2)}, u32[]{:S(2)}) collective-permute-start(bf16[512,768]{1,0:T(8,128)(2,1)S(1)} %get-tuple-element.156), channel_id=1, source_target_pairs={{0,2},{1,3},{2,0},{3,1},{4,6},{5,7},{6,4},{7,5},{8,10},{9,11},{10,... | collective-permute-start | bytes 2359304 | tf_op jit(solution)/shard_map/ppermute | solution.py:30
  6.0 35.5 %collective-permute-start.3 = (bf16[512,768]{1,0:T(8,128)(2,1)S(1)}, bf16[512,768]{1,0:T(8,128)(2,1)S(1)}, u32[]{:S(2)}, u32[]{:S(2)}) collective-permute-start(bf16[512,768]{1,0:T(8,128)(2,1)S(1)} %get-tuple-element.155), channel_id=1, source_target_pairs={{4,0},{8,4},{12,8},{16,12},{20,16},{24,20},{28,24},{5,1},{9,5},{13... | collective-permute-start | bytes 2359304 | tf_op jit(solution)/shard_map/ppermute | solution.py:36
  7.3 34.2 %collective-permute-start.7 = (bf16[512,768]{1,0:T(8,128)(2,1)S(1)}, bf16[512,768]{1,0:T(8,128)(2,1)S(1)}, u32[]{:S(2)}, u32[]{:S(2)}) collective-permute-start(bf16[512,768]{1,0:T(8,128)(2,1)S(1)} %get-tuple-element.155), channel_id=1, source_target_pairs={{0,2},{1,3},{2,0},{3,1},{4,6},{5,7},{6,4},{7,5},{8,10},{9,11},{10,... | collective-permute-start | bytes 2359304 | tf_op jit(solution)/shard_map/ppermute | solution.py:30
  25.0 7.5 %collective-permute-start.5 = (bf16[256,768]{1,0:T(8,128)(2,1)S(1)}, bf16[256,768]{1,0:T(8,128)(2,1)S(1)}, u32[]{:S(2)}, u32[]{:S(2)}) collective-permute-start(bf16[256,768]{1,0:T(8,128)(2,1)S(1)} %get-tuple-element.157), channel_id=1, source_target_pairs={{0,1},{1,0},{2,3},{3,2},{4,5},{5,4},{6,7},{7,6},{8,9},{9,8},{10,11... | collective-permute-start | bytes 1179656 | tf_op jit(solution)/shard_map/ppermute | solution.py:30
  25.1 7.4 %collective-permute-start.6 = (bf16[256,768]{1,0:T(8,128)(2,1)S(1)}, bf16[256,768]{1,0:T(8,128)(2,1)S(1)}, u32[]{:S(2)}, u32[]{:S(2)}) collective-permute-start(bf16[256,768]{1,0:T(8,128)(2,1)S(1)} %get-tuple-element.158), channel_id=1, source_target_pairs={{0,1},{1,0},{2,3},{3,2},{4,5},{5,4},{6,7},{7,6},{8,9},{9,8},{10,11... | collective-permute-start | bytes 1179656 | tf_op jit(solution)/shard_map/ppermute | solution.py:30
  25.6 15.9 %collective-permute-start.4 = (bf16[80,1024]{1,0:T(8,128)(2,1)S(1)}, bf16[80,1024]{1,0:T(8,128)(2,1)S(1)}, u32[]{:S(2)}, u32[]{:S(2)}) collective-permute-start(bf16[80,1024]{1,0:T(8,128)(2,1)S(1)} %opening.1.refs_4_), channel_id=1, source_target_pairs={{0,1},{1,0},{2,3},{3,2},{4,5},{5,4},{6,7},{7,6},{8,9},{9,8},{10,11... | collective-permute-start | bytes 491528 | tf_op jit(solution)/shard_map/ppermute | solution.py:30
  41.5 3.8 %collective-permute-start.8 = (bf16[512,768]{1,0:T(8,128)(2,1)S(1)}, bf16[512,768]{1,0:T(8,128)(2,1)S(1)}, u32[]{:S(2)}, u32[]{:S(2)}) collective-permute-start(bf16[512,768]{1,0:T(8,128)(2,1)S(1)} %collective-permute-done.7.refs_1_), channel_id=1, source_target_pairs={{0,1},{1,0},{2,3},{3,2},{4,5},{5,4},{6,7},{7,6},{8,9},{9,8},{10,11... | collective-permute-start | bytes 2359304 | tf_op jit(solution)/shard_map/ppermute | solution.py:30
  41.5 10.3 %collective-permute-start.9 = (bf16[80,1024]{1,0:T(8,128)(2,1)S(1)}, bf16[80,1024]{1,0:T(8,128)(2,1)S(1)}, u32[]{:S(2)}, u32[]{:S(2)}) collective-permute-start(bf16[80,1024]{1,0:T(8,128)(2,1)S(1)} %opening.1.refs_4_), channel_id=1, source_target_pairs={{0,2},{1,3},{2,0},{3,1},{4,6},{5,7},{6,4},{7,5},{8,10},{9,11},{10,... | collective-permute-start | bytes 491528 | tf_op jit(solution)/shard_map/ppermute | solution.py:30
  43.3 11.8 %collective-permute-start.11 = (bf16[80,1024]{1,0:T(8,128)(2,1)S(1)}, bf16[80,1024]{1,0:T(8,128)(2,1)S(1)}, u32[]{:S(2)}, u32[]{:S(2)}) collective-permute-start(bf16[80,1024]{1,0:T(8,128)(2,1)S(1)} %opening.1.refs_4_), channel_id=1, source_target_pairs={{4,0},{8,4},{12,8},{16,12},{20,16},{24,20},{28,24},{5,1},{9,5},{13... | collective-permute-start | bytes 491528 | tf_op jit(solution)/shard_map/ppermute | solution.py:36
  51.8 3.3 %collective-permute-start.10 = (bf16[80,1024]{1,0:T(8,128)(2,1)S(1)}, bf16[80,1024]{1,0:T(8,128)(2,1)S(1)}, u32[]{:S(2)}, u32[]{:S(2)}) collective-permute-start(bf16[80,1024]{1,0:T(8,128)(2,1)S(1)} %collective-permute-done.9.refs_4_), channel_id=1, source_target_pairs={{0,1},{1,0},{2,3},{3,2},{4,5},{5,4},{6,7},{7,6},{8,9},{9,8},{10,11... | collective-permute-start | bytes 491528 | tf_op jit(solution)/shard_map/ppermute | solution.py:30
  58.4 2.8 %collective-permute-start.12 = (f32[4,72,512]{2,1,0:T(8,128)S(1)}, f32[4,72,512]{2,1,0:T(8,128)S(1)}, u32[]{:S(2)}, u32[]{:S(2)}) collective-permute-start(f32[4,72,512]{2,1,0:T(8,128)S(1)} %get-tuple-element.117), channel_id=1, source_target_pairs={{0,1},{1,0},{2,3},{3,2},{4,5},{5,4},{6,7},{7,6},{8,9},{9,8},{10,11... | collective-permute-start | bytes 1769480 | tf_op jit(solution)/shard_map/ppermute | solution.py:30
  61.2 9.4 %collective-permute-start.14 = (f32[2,72,512]{2,1,0:T(8,128)S(1)}, f32[2,72,512]{2,1,0:T(8,128)S(1)}, u32[]{:S(2)}, u32[]{:S(2)}) collective-permute-start(f32[2,72,512]{2,1,0:T(8,128)S(1)} %slice_add_fusion), channel_id=1, source_target_pairs={{0,2},{1,3},{2,0},{3,1},{4,6},{5,7},{6,4},{7,5},{8,10},{9,11},{10,... | collective-permute-start | bytes 884744 | tf_op jit(solution)/shard_map/ppermute | solution.py:30
  61.6 8.9 %collective-permute-start.13 = (f32[2,72,512]{2,1,0:T(8,128)S(1)}, f32[2,72,512]{2,1,0:T(8,128)S(1)}, u32[]{:S(2)}, u32[]{:S(2)}) collective-permute-start(f32[2,72,512]{2,1,0:T(8,128)S(1)} %get-tuple-element.122), channel_id=1, source_target_pairs={{0,4},{4,8},{8,12},{12,16},{16,20},{20,24},{24,28},{1,5},{5,9},{9,... | collective-permute-start | bytes 884744 | tf_op jit(solution)/shard_map/ppermute | solution.py:36
  71.5 2.4 %collective-permute-start.16 = (bf16[128,1024]{1,0:T(8,128)(2,1)S(1)}, bf16[128,1024]{1,0:T(8,128)(2,1)S(1)}, u32[]{:S(2)}, u32[]{:S(2)}) collective-permute-start(bf16[128,1024]{1,0:T(8,128)(2,1)S(1)} %get-tuple-element.125.refs_4_), channel_id=1, source_target_pairs={{0,1},{1,0},{2,3},{3,2},{4,5},{5,4},{6,7},{7,6},{8,9},{9,8},{10,11... | collective-permute-start | bytes 786440 | tf_op jit(solution)/shard_map/ppermute | solution.py:30
  71.6 8.7 %collective-permute-start.17 = (bf16[128,1024]{1,0:T(8,128)(2,1)S(1)}, bf16[128,1024]{1,0:T(8,128)(2,1)S(1)}, u32[]{:S(2)}, u32[]{:S(2)}) collective-permute-start(bf16[128,1024]{1,0:T(8,128)(2,1)S(1)} %get-tuple-element.125.refs_4_), channel_id=1, source_target_pairs={{0,2},{1,3},{2,0},{3,1},{4,6},{5,7},{6,4},{7,5},{8,10},{9,11},{10,... | collective-permute-start | bytes 786440 | tf_op jit(solution)/shard_map/ppermute | solution.py:30
  72.5 1.5 %collective-permute-start.15 = (f32[64,64]{1,0:T(8,128)S(1)}, f32[64,64]{1,0:T(8,128)S(1)}, u32[]{:S(2)}, u32[]{:S(2)}) collective-permute-start(f32[64,64]{1,0:T(8,128)S(1)} %get-tuple-element.124), channel_id=1, source_target_pairs={{0,1},{1,0},{2,3},{3,2},{4,5},{5,4},{6,7},{7,6},{8,9},{9,8},{10,11... | collective-permute-start | bytes 49160 | tf_op jit(solution)/shard_map/ppermute | solution.py:642
  72.7 11.6 %collective-permute-start.19 = (bf16[128,1024]{1,0:T(8,128)(2,1)S(1)}, bf16[128,1024]{1,0:T(8,128)(2,1)S(1)}, u32[]{:S(2)}, u32[]{:S(2)}) collective-permute-start(bf16[128,1024]{1,0:T(8,128)(2,1)S(1)} %get-tuple-element.125.refs_4_), channel_id=1, source_target_pairs={{4,0},{8,4},{12,8},{16,12},{20,16},{24,20},{28,24},{5,1},{9,5},{13... | collective-permute-start | bytes 786440 | tf_op jit(solution)/shard_map/ppermute | solution.py:36
  80.4 3.9 %collective-permute-start.20 = (bf16[128,1024]{1,0:T(8,128)(2,1)S(1)}, bf16[128,1024]{1,0:T(8,128)(2,1)S(1)}, u32[]{:S(2)}, u32[]{:S(2)}) collective-permute-start(bf16[128,1024]{1,0:T(8,128)(2,1)S(1)} %collective-permute-done.17.refs_4_), channel_id=1, source_target_pairs={{0,1},{1,0},{2,3},{3,2},{4,5},{5,4},{6,7},{7,6},{8,9},{9,8},{10,11... | collective-permute-start | bytes 786440 | tf_op jit(solution)/shard_map/ppermute | solution.py:30
  80.4 3.9 %collective-permute-start.18 = (f32[64,64]{1,0:T(8,128)S(1)}, f32[64,64]{1,0:T(8,128)S(1)}, u32[]{:S(2)}, u32[]{:S(2)}) collective-permute-start(f32[64,64]{1,0:T(8,128)S(1)} %add.22), channel_id=1, source_target_pairs={{0,2},{1,3},{2,0},{3,1},{4,6},{5,7},{6,4},{7,5},{8,10},{9,11},{10,... | collective-permute-start | bytes 49160 | tf_op jit(solution)/shard_map/ppermute | solution.py:642
  84.3 6.8 %collective-permute-start.21 = (f32[64,64]{1,0:T(8,128)S(1)}, f32[64,64]{1,0:T(8,128)S(1)}, u32[]{:S(2)}, u32[]{:S(2)}) collective-permute-start(f32[64,64]{1,0:T(8,128)S(1)} %add.23), channel_id=1, source_target_pairs={{0,4},{1,5},{2,6},{3,7},{4,0},{5,1},{6,2},{7,3},{8,12},{9,13},{10,... | collective-permute-start | bytes 49160 | tf_op jit(solution)/shard_map/ppermute | solution.py:642
  91.1 5.8 %collective-permute-start.22 = (f32[4,64,512]{2,1,0:T(8,128)S(1)}, f32[4,64,512]{2,1,0:T(8,128)S(1)}, u32[]{:S(2)}, u32[]{:S(2)}) collective-permute-start(f32[4,64,512]{2,1,0:T(8,128)S(1)} %get-tuple-element.140), channel_id=1, source_target_pairs={{0,1},{1,0},{2,3},{3,2},{4,5},{5,4},{6,7},{7,6},{8,9},{9,8},{10,11... | collective-permute-start | bytes 1572872 | tf_op jit(solution)/shard_map/ppermute | solution.py:30
  91.6 5.3 %collective-permute-start.23 = (f32[64,64]{1,0:T(8,128)S(1)}, f32[64,64]{1,0:T(8,128)S(1)}, u32[]{:S(2)}, u32[]{:S(2)}) collective-permute-start(f32[64,64]{1,0:T(8,128)S(1)} %add.24), channel_id=1, source_target_pairs={{0,8},{1,9},{2,10},{3,11},{4,12},{5,13},{6,14},{7,15},{8,0},{9,1},... | collective-permute-start | bytes 49160 | tf_op jit(solution)/shard_map/ppermute | solution.py:642
  96.9 12.5 %collective-permute-start.25 = (f32[2,64,512]{2,1,0:T(8,128)S(1)}, f32[2,64,512]{2,1,0:T(8,128)S(1)}, u32[]{:S(2)}, u32[]{:S(2)}) collective-permute-start(f32[2,64,512]{2,1,0:T(8,128)S(1)} %slice_add_fusion.1), channel_id=1, source_target_pairs={{0,2},{1,3},{2,0},{3,1},{4,6},{5,7},{6,4},{7,5},{8,10},{9,11},{10,... | collective-permute-start | bytes 786440 | tf_op jit(solution)/shard_map/ppermute | solution.py:30
  97.9 11.5 %collective-permute-start.24 = (f32[2,64,512]{2,1,0:T(8,128)S(1)}, f32[2,64,512]{2,1,0:T(8,128)S(1)}, u32[]{:S(2)}, u32[]{:S(2)}) collective-permute-start(f32[2,64,512]{2,1,0:T(8,128)S(1)} %get-tuple-element.148), channel_id=1, source_target_pairs={{0,4},{4,8},{8,12},{12,16},{16,20},{20,24},{24,28},{1,5},{5,9},{9,... | collective-permute-start | bytes 786440 | tf_op jit(solution)/shard_map/ppermute | solution.py:36
  100.8 6.6 %collective-permute-start.26 = (f32[64,64]{1,0:T(8,128)S(1)}, f32[64,64]{1,0:T(8,128)S(1)}, u32[]{:S(2)}, u32[]{:S(2)}) collective-permute-start(f32[64,64]{1,0:T(8,128)S(1)} %add.26), channel_id=1, source_target_pairs={{0,16},{1,17},{2,18},{3,19},{4,20},{5,21},{6,22},{7,23},{8,24},{9,... | collective-permute-start | bytes 49160 | tf_op jit(solution)/shard_map/ppermute | solution.py:642

commit v15 on v12

--- a/solution.py
+++ b/solution.py
@@ -622,8 +622,29 @@
     return bits_of(lax.axis_size("blk") * lax.axis_size("grp"))
 
 
-def pairs_of(bits):
-    return [bits[first : first + 2] for first in range(0, len(bits), 2)]
+def all_sum_split(value):
+    axes = ("blk", "grp")
+    count = lax.axis_size("blk") * lax.axis_size("grp")
+    index = lax.axis_index("blk") * lax.axis_size("grp") + lax.axis_index("grp")
+    odd = lax.rem(index, 2) == 1
+
+    def move(value, even_by, odd_by):
+        steps = [odd_by if source % 2 else even_by for source in range(count)]
+        pairs = [(source, source ^ step) for source, step in enumerate(steps) if step]
+        return lax.ppermute(value, axes, pairs)
+
+    bits = bits_of(count)
+    value = value + move(value, 1, 1)
+    bits = bits[1:]
+    while len(bits) > 1:
+        one, two, bits = bits[0], bits[1], bits[2:]
+        near = move(value, one, two)
+        far = move(value, 0, one ^ two)
+        part = near + jnp.where(odd, far, value)
+        value = part + move(part, 1, 1)
+    for bit in bits:
+        value = value + move(value, bit, bit)
+    return value
 
 
 def all_sum(value, stages, beside=None):
@@ -657,8 +678,10 @@
     rows, cols, n, *entries = listing(
         pair_rows, pair_cols, pair_live, group, cap, blocks_dev
     )
-    mate = swap(points, "grp", 1)
-    chunks = [points[:half], points[half:]]
+    first = points[:half]
+    rest, first = lax.optimization_barrier((points, first))
+    mate = swap(rest, "grp", 1)
+    chunks = [first, rest[half:]]
     far = [from_behind(chunk, "blk", -1) for chunk in chunks]
     crossed = [gather_far_bits(chunk) for chunk in chunks]
     begin, mate = lax.optimization_barrier((start, mate))
@@ -766,8 +789,7 @@
         inverse = factor(gram)
         z, gram, *parts = scaled_gram(sums, z, counts, degree, inverse, turn + 1 < ITERS)
         parts = parts[0] if parts else None
-    stages = sum_stages()
-    return embedding(all_sum(gram, stages[:1] + pairs_of(stages[1:])), z)
+    return embedding(all_sum_split(gram), z)
 
 
 def solution(mesh):

time: 132 us -> 133 us (level)
  waiting for transfers between devices: 32.3 us -> 34.2 us
    ppermute x0 -> x7, starting transfers between devices: none -> 12.5 us  [move(): return lax.ppermute(value, axes, pairs)]
    ppermute x12 -> x5, starting transfers between devices: 21.7 us -> 10.2 us  [all_sum(): lax.ppermute(value, ('blk', 'grp'), [(source, source ^ move) for source i...]
    ppermute x12 -> x5, waiting for transfers between devices: 15 us -> 7.12 us  [all_sum(): lax.ppermute(value, ('blk', 'grp'), [(source, source ^ move) for source i...]
    ppermute x0 -> x7, waiting for transfers between devices: none -> 7.29 us  [move(): return lax.ppermute(value, axes, pairs)]
  transfers between devices with their start and end apart: 34 -> 34, of which waited for: 14 -> 13; matrix products, arithmetic and copies ran while one was open for 1% -> 0% of each run, Pallas kernels for 35% -> 35%
where the time goes in v15:
time: 133 us
  Pallas kernels  55.7 us (42%)
  starting transfers between devices  40.8 us (31%)
  waiting for transfers between devices  34.2 us (26%)
  local copies, waits for them, and re-layouts  1.44 us (1%)
    pallas_call x6, Pallas kernels, products(): pl.pallas_call(kernel, out_shape=shapes, in_specs=[spec(SMEM)] * 4 + [spe...  17.2 us
    pallas_call x4, Pallas kernels, build_tiles(): pl.pallas_call(kernel, out_shape=shapes, in_specs=[spec(SMEM)] * len(scal...  16.2 us
    pallas_call x1, Pallas kernels, listing(): pl.pallas_call(functools.partial(listing_kernel, group, cap, blocks_dev),...  14.3 us
    ppermute x7, starting transfers between devices, move(): return lax.ppermute(value, axes, pairs)  12.5 us
    ppermute x16, waiting for transfers between devices, swap(): lax.ppermute(value, axis, [(source, source ^ bit) for source in range(cou...  10.9 us
    ppermute x5, starting transfers between devices, all_sum(): lax.ppermute(value, ('blk', 'grp'), [(source, source ^ move) for source i...  10.2 us
    ppermute x6, starting transfers between devices, from_behind(): lax.ppermute(value, axis, [(source, source + steps) for source in range(i...  9.33 us
    ppermute x6, waiting for transfers between devices, from_behind(): lax.ppermute(value, axis, [(source, source + steps) for source in range(i...  8.84 us
  transfers between devices with their start and end apart: 34, of which 13 were waited for; matrix products, arithmetic and copies ran while one was open for 0% of the time, Pallas kernels for 35%

profile of v15, /device:TPU:0, one launch (start us, length us, event | category | flops | bytes accessed | tf_op | source)
XLA Modules:
  0.0 133.4 jit_solution(8235635298037919477)
XLA Ops:
  0.0 1.3 slice.18
  1.3 0.5 collective-permute-start
  1.9 1.3 collective-permute-start.1
  3.2 2.6 %collective-permute-start.2 = (bf16[512,768]{1,0:T(8,128)(2,1)S(1)}, bf16[512,768]{1,0:T(8,128)(2,1)S(1)}, u32[]{:S(2)}, u32[]{:S(2)}) collective-permute-start(bf16[512,768]{1,0:T(8,128)(2,1)S(1)} %slice.18), channel_id=1, source_target_pairs={{0,2},{1,3},{2,0},{3,1},{4,6},{5,7},{6,4},{7,5},{8,10},{9,11},{10,... | collective-permute-start | bytes 2359304 | tf_op jit(solution)/shard_map/ppermute | solution.py:30
  5.7 0.1 slice.19
  5.8 1.3 collective-permute-start.3
  7.1 0.1 collective-permute-start.7
  7.9 14.3 %listing.1 = (s32[16]{0:T(128)S(1)}, s32[16]{0:T(128)S(1)}, s32[4]{0:T(128)S(1)}, s32[32]{0:T(128)S(1)}, s32[32]{0:T(128)S(1)}, /*index=5*/s32[32]{0:T(128)S(1)}, s32[7]{0:T(128)S(1)}) custom-call(s32[64]{0:T(128)S(1)} %copy-done.3, s32[64]{0:T(128)S(1)} %copy-done.4, s32[1]{0:T(128)S(6)} %copy.29.live), custom_call_target="tpu_custom_call" | custom-call | flops 1048576 | bytes 1024 | tf_op jit(solution)/shard_map/listing/pallas_call | solution.py:214
  22.2 0.6 opening.1.refs_4_
  22.8 1.9 %collective-permute-done.1.refs_5_ = bf16[512,768]{1,0:T(8,128)(2,1)S(1)} collective-permute-done((bf16[512,768]{1,0:T(8,128)(2,1)S(1)}, bf16[512,768]{1,0:T(8,128)(2,1)S(1)}, u32[]{:S(2)}, u32[]{:S(2)}) %collective-permute-start.1) | collective-permute-done | bytes 786464 | tf_op jit(solution)/shard_map/ppermute | solution.py:36
  24.7 0.1 collective-permute-start.5
  24.8 0.5 collective-permute-start.6
  25.3 0.1 collective-permute-start.4
  25.4 6.8 %first_tiles.1 = (bf16[5120,768]{1,0:T(8,128)(2,1)S(1)}, f32[10,8,512]{2,1,0:T(8,128)S(1)}, f32[8,512,128]{2,1,0:T(8,128)S(1)}, bf16[17,512,512]{2,1,0:T(8,128)(2,1)S(1)}) custom-call(s32[4]{0:T(128)S(1)} %get-tuple-element.92.refs_0_, s32[16]{0:T(128)S(1)} %get-tuple-element.93.refs_1_, s32[16]{0:T(128)S(1)} %get-tuple-element.94.refs_2_, ...), custom_call_target="tpu_custom_call" | custom-call | flops 1048576 | bytes 1048576 | tf_op jit(solution)/shard_map/first_tiles/pallas_call | solution.py:331
  32.3 0.1 pad_maximum_fusion.refs_3_
  32.3 2.1 %second_tiles.1 = (bf16[5120,768]{1,0:T(8,128)(2,1)S(1)}, f32[10,8,512]{2,1,0:T(8,128)S(1)}, f32[8,512,128]{2,1,0:T(8,128)S(1)}, bf16[17,512,512]{2,1,0:T(8,128)(2,1)S(1)}) custom-call(s32[4]{0:T(128)S(1)} %get-tuple-element.92.refs_0_, s32[16]{0:T(128)S(1)} %get-tuple-element.93.refs_1_, ...), custom_call_target="tpu_custom_call", output_to_operand_aliasing={{0}: (4, {}), {1}: (5, {}), {2}: (6, {}), {3}: (7, {})} | custom-call | flops 1048576 | bytes 1048576 | tf_op jit(solution)/shard_map/second_tiles/pallas_call | solution.py:331
  34.4 6.9 %collective-permute-done.3.refs_0_ = bf16[512,768]{1,0:T(8,128)(2,1)S(1)} collective-permute-done((bf16[512,768]{1,0:T(8,128)(2,1)S(1)}, bf16[512,768]{1,0:T(8,128)(2,1)S(1)}, u32[]{:S(2)}, u32[]{:S(2)}) %collective-permute-start.3) | collective-permute-done | bytes 786464 | tf_op jit(solution)/shard_map/ppermute | solution.py:36
  41.4 1.8 %collective-permute-start.9 = (bf16[80,1024]{1,0:T(8,128)(2,1)S(1)}, bf16[80,1024]{1,0:T(8,128)(2,1)S(1)}, u32[]{:S(2)}, u32[]{:S(2)}) collective-permute-start(bf16[80,1024]{1,0:T(8,128)(2,1)S(1)} %opening.1.refs_4_), channel_id=1, source_target_pairs={{0,2},{1,3},{2,0},{3,1},{4,6},{5,7},{6,4},{7,5},{8,10},{9,11},{10,... | collective-permute-start | bytes 491528 | tf_op jit(solution)/shard_map/ppermute | solution.py:30
  43.1 1.3 collective-permute-start.11
  44.4 0.8 more_blocks.1
  45.2 6.5 %last_tiles.1 = (bf16[5120,768]{1,0:T(8,128)(2,1)S(1)}, f32[10,8,512]{2,1,0:T(8,128)S(1)}, f32[8,512,128]{2,1,0:T(8,128)S(1)}, bf16[17,512,512]{2,1,0:T(8,128)(2,1)S(1)}) custom-call(s32[4]{0:T(128)S(1)} %get-tuple-element.92.refs_0_, s32[16]{0:T(128)S(1)} %get-tuple-element.93.refs_1_, ...), custom_call_target="tpu_custom_call", output_to_operand_aliasing={{0}: (4, {}), {1}: (5, {}), {2}: (6, {}), {3}: (7, {})} | custom-call | flops 4294967296 | bytes 1048576 | tf_op jit(solution)/shard_map/last_tiles/pallas_call | solution.py:331
  51.7 0.2 collective-permute-start.10
  51.9 3.0 %products.6 = (f32[2,72,512]{2,1,0:T(8,128)S(1)}, f32[4,72,512]{2,1,0:T(8,128)S(1)}, f32[2,72,512]{2,1,0:T(8,128)S(1)}, f32[2,72,512]{2,1,0:T(8,128)S(1)}) custom-call(s32[32]{0:T(128)S(1)} %get-tuple-element.82.refs_0_, s32[32]{0:T(128)S(1)} %get-tuple-element.83.refs_1_, s32[32]{0:T(128)S(1)} %get-tuple-element.84.refs_2_, ...), custom_call_target="tpu_custom_call" | custom-call | flops 1048576 | bytes 1048576 | tf_op jit(solution)/shard_map/products/pallas_call | solution.py:422
  55.0 4.0 %products.7 = (f32[4,72,512]{2,1,0:T(8,128)S(1)}, f32[2,72,512]{2,1,0:T(8,128)S(1)}, f32[2,72,512]{2,1,0:T(8,128)S(1)}) custom-call(s32[32]{0:T(128)S(1)} %get-tuple-element.82.refs_0_, s32[32]{0:T(128)S(1)} %get-tuple-element.83.refs_1_, s32[32]{0:T(128)S(1)} %get-tuple-element.84.refs_2_, s32[7]{0:T(128)S(1)} %get-tuple-element.85.refs_3_, ...), custom_call_target="tpu_custom_call" | custom-call | flops 2147483648 | bytes 1048576 | tf_op jit(solution)/shard_map/products/pallas_call | solution.py:422
  59.0 0.1 collective-permute-start.12
  59.1 2.0 %collective-permute-done.12.refs_2_ = f32[4,72,512]{2,1,0:T(8,128)S(1)} collective-permute-done((f32[4,72,512]{2,1,0:T(8,128)S(1)}, f32[4,72,512]{2,1,0:T(8,128)S(1)}, u32[]{:S(2)}, u32[]{:S(2)}) %collective-permute-start.12) | collective-permute-done | bytes 589856 | tf_op jit(solution)/shard_map/ppermute | solution.py:30
  61.1 0.7 collective-permute-start.14
  61.8 1.3 collective-permute-start.13
  63.1 1.4 %products.8.refs_0_ = f32[2,72,512]{2,1,0:T(8,128)S(1)} custom-call(s32[32]{0:T(128)S(1)} %get-tuple-element.82.refs_0_, s32[32]{0:T(128)S(1)} %get-tuple-element.83.refs_1_, s32[32]{0:T(128)S(1)} %get-tuple-element.84.refs_2_, s32[7]{0:T(128)S(1)} %get-tuple-element.85.refs_3_, bf16[80,1024]{1,0:T(8,128)(2,1)S(1)} %collective-permute-done.9.refs_4_, ...), custom_call_target="tpu_custom_call" | custom-call | flops 1048576 | bytes 1048576 | tf_op jit(solution)/shard_map/products/pallas_call | solution.py:422
  64.5 5.7 %collective-permute-done.14.refs_3_ = f32[2,72,512]{2,1,0:T(8,128)S(1)} collective-permute-done((f32[2,72,512]{2,1,0:T(8,128)S(1)}, f32[2,72,512]{2,1,0:T(8,128)S(1)}, u32[]{:S(2)}, u32[]{:S(2)}) %collective-permute-start.14) | collective-permute-done | bytes 294944 | tf_op jit(solution)/shard_map/ppermute | solution.py:30
  70.2 0.9 scaled_gram.2
  71.2 0.1 collective-permute-start.16
  71.3 0.9 collective-permute-start.17
  72.1 0.2 collective-permute-start.15
  72.3 1.3 collective-permute-start.19
  73.6 3.2 %products.9 = (f32[2,64,512]{2,1,0:T(8,128)S(1)}, f32[4,64,512]{2,1,0:T(8,128)S(1)}, f32[2,64,512]{2,1,0:T(8,128)S(1)}, f32[2,64,512]{2,1,0:T(8,128)S(1)}) custom-call(s32[32]{0:T(128)S(1)} %get-tuple-element.82.refs_0_, s32[32]{0:T(128)S(1)} %get-tuple-element.83.refs_1_, s32[32]{0:T(128)S(1)} %get-tuple-element.84.refs_2_, ...), custom_call_target="tpu_custom_call" | custom-call | flops 1048576 | bytes 1048576 | tf_op jit(solution)/shard_map/products/pallas_call | solution.py:422
  76.8 3.2 %collective-permute-done.17.refs_4_ = bf16[128,1024]{1,0:T(8,128)(2,1)S(1)} collective-permute-done((bf16[128,1024]{1,0:T(8,128)(2,1)S(1)}, bf16[128,1024]{1,0:T(8,128)(2,1)S(1)}, u32[]{:S(2)}, u32[]{:S(2)}) %collective-permute-start.17) | collective-permute-done | bytes 262176 | tf_op jit(solution)/shard_map/ppermute | solution.py:30
  80.0 0.8 collective-permute-start.18
  80.8 3.1 %collective-permute-done.18 = f32[64,64]{1,0:T(8,128)S(1)} collective-permute-done((f32[64,64]{1,0:T(8,128)S(1)}, f32[64,64]{1,0:T(8,128)S(1)}, u32[]{:S(2)}, u32[]{:S(2)}) %collective-permute-start.18) | collective-permute-done | bytes 16416 | tf_op jit(solution)/shard_map/ppermute | solution.py:657
  83.9 2.2 %collective-permute-start.21 = (f32[64,64]{1,0:T(8,128)S(1)}, f32[64,64]{1,0:T(8,128)S(1)}, u32[]{:S(2)}, u32[]{:S(2)}) collective-permute-start(f32[64,64]{1,0:T(8,128)S(1)} %add.41), channel_id=1, source_target_pairs={{0,4},{1,5},{2,6},{3,7},{4,0},{5,1},{6,2},{7,3},{8,12},{9,13},{10,... | collective-permute-start | bytes 49160 | tf_op jit(solution)/shard_map/ppermute | solution.py:657
  86.1 4.1 %products.10 = (f32[4,64,512]{2,1,0:T(8,128)S(1)}, f32[2,64,512]{2,1,0:T(8,128)S(1)}, f32[2,64,512]{2,1,0:T(8,128)S(1)}) custom-call(s32[32]{0:T(128)S(1)} %get-tuple-element.82.refs_0_, s32[32]{0:T(128)S(1)} %get-tuple-element.83.refs_1_, s32[32]{0:T(128)S(1)} %get-tuple-element.84.refs_2_, s32[7]{0:T(128)S(1)} %get-tuple-element.85.refs_3_, ...), custom_call_target="tpu_custom_call" | custom-call | flops 2147483648 | bytes 1048576 | tf_op jit(solution)/shard_map/products/pallas_call | solution.py:422
  90.3 0.1 collective-permute-start.22
  90.3 0.7 collective-permute-start.23
  91.1 3.3 %collective-permute-done.23 = f32[64,64]{1,0:T(8,128)S(1)} collective-permute-done((f32[64,64]{1,0:T(8,128)S(1)}, f32[64,64]{1,0:T(8,128)S(1)}, u32[]{:S(2)}, u32[]{:S(2)}) %collective-permute-start.23) | collective-permute-done | bytes 16416 | tf_op jit(solution)/shard_map/ppermute | solution.py:657
  94.4 1.2 collective-permute-start.25
  95.6 2.9 %collective-permute-start.24 = (f32[2,64,512]{2,1,0:T(8,128)S(1)}, f32[2,64,512]{2,1,0:T(8,128)S(1)}, u32[]{:S(2)}, u32[]{:S(2)}) collective-permute-start(f32[2,64,512]{2,1,0:T(8,128)S(1)} %get-tuple-element.152), channel_id=1, source_target_pairs={{0,4},{4,8},{8,12},{12,16},{16,20},{20,24},{24,28},{1,5},{5,9},{9,... | collective-permute-start | bytes 786440 | tf_op jit(solution)/shard_map/ppermute | solution.py:36
  98.5 6.3 %collective-permute-start.26 = (f32[64,64]{1,0:T(8,128)S(1)}, f32[64,64]{1,0:T(8,128)S(1)}, u32[]{:S(2)}, u32[]{:S(2)}) collective-permute-start(f32[64,64]{1,0:T(8,128)S(1)} %add.44), channel_id=1, source_target_pairs={{0,16},{1,17},{2,18},{3,19},{4,20},{5,21},{6,22},{7,23},{8,24},{9,... | collective-permute-start | bytes 49160 | tf_op jit(solution)/shard_map/ppermute | solution.py:657
  104.8 1.5 %products.11.refs_0_ = f32[2,64,512]{2,1,0:T(8,128)S(1)} custom-call(s32[32]{0:T(128)S(1)} %get-tuple-element.82.refs_0_, s32[32]{0:T(128)S(1)} %get-tuple-element.83.refs_1_, s32[32]{0:T(128)S(1)} %get-tuple-element.84.refs_2_, s32[7]{0:T(128)S(1)} %get-tuple-element.85.refs_3_, bf16[128,1024]{1,0:T(8,128)(2,1)S(1)} %collective-permute-done.17.refs_4_, ...), custom_call_target="tpu_custom_call" | custom-call | flops 1048576 | bytes 1048576 | tf_op jit(solution)/shard_map/products/pallas_call | solution.py:422
  106.3 0.8 collective-permute-done.26
  107.0 2.0 %factor.1.refs_6_ = f32[64,64]{1,0:T(8,128)S(1)} custom-call(f32[64,64]{1,0:T(8,128)S(1)} %add.45.gram), custom_call_target="tpu_custom_call" | custom-call | flops 65536 | bytes 65536 | tf_op jit(solution)/shard_map/factor/pallas_call | solution.py:592
  109.0 1.5 %scaled_gram.3 = (f32[64,1024]{1,0:T(8,128)S(1)}, f32[64,64]{1,0:T(8,128)S(1)}) custom-call(s32[2]{0:T(128)S(1)} %copy-done.2, f32[2,64,512]{2,1,0:T(8,128)S(1)} %products.11.refs_0_, f32[2,64,512]{2,1,0:T(8,128)S(1)} %collective-permute-done.24.refs_1_, f32[4,64,512]{2,1,0:T(8,128)S(1)} %collective-permute-done.22.refs_2_, ...), custom_call_target="tpu_custom_call" | custom-call | flops 67108864 | bytes 2097152 | tf_op jit(solution)/shard_map/scaled_gram/pallas_call | solution.py:533
  110.5 0.1 collective-permute-start.27
  110.6 1.2 collective-permute-done.27
  111.8 0.1 collective-permute-start.28
  111.9 0.7 collective-permute-start.29
  112.6 3.1 %collective-permute-done.28 = f32[64,64]{1,0:T(8,128)S(1)} collective-permute-done((f32[64,64]{1,0:T(8,128)S(1)}, f32[64,64]{1,0:T(8,128)S(1)}, u32[]{:S(2)}, u32[]{:S(2)}) %collective-permute-start.28) | collective-permute-done | bytes 16416 | tf_op jit(solution)/shard_map/ppermute | solution.py:634
  115.7 3.4 %collective-permute-start.30 = (f32[64,64]{1,0:T(8,128)S(1)}, f32[64,64]{1,0:T(8,128)S(1)}, u32[]{:S(2)}, u32[]{:S(2)}) collective-permute-start(f32[64,64]{1,0:T(8,128)S(1)} %select_add_fusion.1), channel_id=1, source_target_pairs={{0,1},{1,0},{2,3},{3,2},{4,5},{5,4},{6,7},{7,6},{8,9},{9,8},{10,11... | collective-permute-start | bytes 49160 | tf_op jit(solution)/shard_map/ppermute | solution.py:634
  119.1 0.9 collective-permute-done.30
  120.0 3.2 %collective-permute-start.31 = (f32[64,64]{1,0:T(8,128)S(1)}, f32[64,64]{1,0:T(8,128)S(1)}, u32[]{:S(2)}, u32[]{:S(2)}) collective-permute-start(f32[64,64]{1,0:T(8,128)S(1)} %add.49), channel_id=1, source_target_pairs={{0,8},{1,17},{2,10},{3,19},{4,12},{5,21},{6,14},{7,23},{8,0},{9,25... | collective-permute-start | bytes 49160 | tf_op jit(solution)/shard_map/ppermute | solution.py:634
  123.2 0.7 collective-permute-start.32
  123.9 1.2 collective-permute-done.31
  125.1 4.4 %collective-permute-start.33 = (f32[64,64]{1,0:T(8,128)S(1)}, f32[64,64]{1,0:T(8,128)S(1)}, u32[]{:S(2)}, u32[]{:S(2)}) collective-permute-start(f32[64,64]{1,0:T(8,128)S(1)} %select_add_fusion), channel_id=1, source_target_pairs={{0,1},{1,0},{2,3},{3,2},{4,5},{5,4},{6,7},{7,6},{8,9},{9,8},{10,11... | collective-permute-start | bytes 49160 | tf_op jit(solution)/shard_map/ppermute | solution.py:634
  129.5 0.9 collective-permute-done.33
  130.4 3.0 %embedding.1 = f32[64,1024]{1,0:T(8,128)} custom-call(f32[64,64]{1,0:T(8,128)S(1)} %add.51.gram, f32[64,1024]{1,0:T(8,128)S(1)} %get-tuple-element.158.z), custom_call_target="tpu_custom_call" | custom-call | flops 1073741824 | bytes 1048576 | tf_op jit(solution)/shard_map/embedding/pallas_call | solution.py:610
  (46 shorter events, 0.3 us)
Async XLA Ops:
  0.0 5.7 %copy-start = (bf16[1024,768]{1,0:T(8,128)(2,1)S(1)}, bf16[1024,768]{1,0:T(8,128)(2,1)}, u32[]{:S(2)}) copy-start(bf16[1024,768]{1,0:T(8,128)(2,1)} %refs_3_.1) | copy-start | bytes 4718596
  0.0 7.8 %copy-start.3 = (s32[64]{0:T(128)S(1)}, s32[64]{0:T(128)}, u32[]{:S(2)}) copy-start(s32[64]{0:T(128)} %rows.1) | copy-start | bytes 772
  0.0 7.8 %copy-start.4 = (s32[64]{0:T(128)S(1)}, s32[64]{0:T(128)}, u32[]{:S(2)}) copy-start(s32[64]{0:T(128)} %cols.1) | copy-start | bytes 772
  0.0 22.2 %copy-start.1 = (f32[64,1024]{1,0:T(8,128)S(1)}, f32[64,1024]{1,0:T(8,128)}, u32[]{:S(2)}) copy-start(f32[64,1024]{1,0:T(8,128)} %start) | copy-start | bytes 786436
  0.0 22.2 %copy-start.2 = (s32[2]{0:T(128)S(1)}, s32[2]{0:T(128)}, u32[]{:S(2)}) copy-start(s32[2]{0:T(128)} %count_ref.3) | copy-start | bytes 28
  1.3 20.8 %collective-permute-start = (bf16[1024,768]{1,0:T(8,128)(2,1)}, bf16[1024,768]{1,0:T(8,128)(2,1)S(1)}, u32[]{:S(2)}, u32[]{:S(2)}) collective-permute-start(bf16[1024,768]{1,0:T(8,128)(2,1)} %refs_3_.1), channel_id=1, source_target_pairs={{0,1},{1,0},{2,3},{3,2},{4,5},{5,4},{6,7},{7,6},{8,9},{9,8},{10,11... | collective-permute-start | bytes 4718600 | tf_op jit(solution)/shard_map/ppermute | solution.py:30
  1.9 22.8 %collective-permute-start.1 = (bf16[512,768]{1,0:T(8,128)(2,1)S(1)}, bf16[512,768]{1,0:T(8,128)(2,1)S(1)}, u32[]{:S(2)}, u32[]{:S(2)}) collective-permute-start(bf16[512,768]{1,0:T(8,128)(2,1)S(1)} %slice.18), channel_id=1, source_target_pairs={{4,0},{8,4},{12,8},{16,12},{20,16},{24,20},{28,24},{5,1},{9,5},{13... | collective-permute-start | bytes 2359304 | tf_op jit(solution)/shard_map/ppermute | solution.py:36
  3.2 21.5 %collective-permute-start.2 = (bf16[512,768]{1,0:T(8,128)(2,1)S(1)}, bf16[512,768]{1,0:T(8,128)(2,1)S(1)}, u32[]{:S(2)}, u32[]{:S(2)}) collective-permute-start(bf16[512,768]{1,0:T(8,128)(2,1)S(1)} %slice.18), channel_id=1, source_target_pairs={{0,2},{1,3},{2,0},{3,1},{4,6},{5,7},{6,4},{7,5},{8,10},{9,11},{10,... | collective-permute-start | bytes 2359304 | tf_op jit(solution)/shard_map/ppermute | solution.py:30
  5.8 35.5 %collective-permute-start.3 = (bf16[512,768]{1,0:T(8,128)(2,1)S(1)}, bf16[512,768]{1,0:T(8,128)(2,1)S(1)}, u32[]{:S(2)}, u32[]{:S(2)}) collective-permute-start(bf16[512,768]{1,0:T(8,128)(2,1)S(1)} %slice.19), channel_id=1, source_target_pairs={{4,0},{8,4},{12,8},{16,12},{20,16},{24,20},{28,24},{5,1},{9,5},{13... | collective-permute-start | bytes 2359304 | tf_op jit(solution)/shard_map/ppermute | solution.py:36
  7.1 34.2 %collective-permute-start.7 = (bf16[512,768]{1,0:T(8,128)(2,1)S(1)}, bf16[512,768]{1,0:T(8,128)(2,1)S(1)}, u32[]{:S(2)}, u32[]{:S(2)}) collective-permute-start(bf16[512,768]{1,0:T(8,128)(2,1)S(1)} %slice.19), channel_id=1, source_target_pairs={{0,2},{1,3},{2,0},{3,1},{4,6},{5,7},{6,4},{7,5},{8,10},{9,11},{10,... | collective-permute-start | bytes 2359304 | tf_op jit(solution)/shard_map/ppermute | solution.py:30
  24.7 7.5 %collective-permute-start.5 = (bf16[256,768]{1,0:T(8,128)(2,1)S(1)}, bf16[256,768]{1,0:T(8,128)(2,1)S(1)}, u32[]{:S(2)}, u32[]{:S(2)}) collective-permute-start(bf16[256,768]{1,0:T(8,128)(2,1)S(1)} %get-tuple-element.159), channel_id=1, source_target_pairs={{0,1},{1,0},{2,3},{3,2},{4,5},{5,4},{6,7},{7,6},{8,9},{9,8},{10,11... | collective-permute-start | bytes 1179656 | tf_op jit(solution)/shard_map/ppermute | solution.py:30
  24.8 7.4 %collective-permute-start.6 = (bf16[256,768]{1,0:T(8,128)(2,1)S(1)}, bf16[256,768]{1,0:T(8,128)(2,1)S(1)}, u32[]{:S(2)}, u32[]{:S(2)}) collective-permute-start(bf16[256,768]{1,0:T(8,128)(2,1)S(1)} %get-tuple-element.160), channel_id=1, source_target_pairs={{0,1},{1,0},{2,3},{3,2},{4,5},{5,4},{6,7},{7,6},{8,9},{9,8},{10,11... | collective-permute-start | bytes 1179656 | tf_op jit(solution)/shard_map/ppermute | solution.py:30
  25.3 16.0 %collective-permute-start.4 = (bf16[80,1024]{1,0:T(8,128)(2,1)S(1)}, bf16[80,1024]{1,0:T(8,128)(2,1)S(1)}, u32[]{:S(2)}, u32[]{:S(2)}) collective-permute-start(bf16[80,1024]{1,0:T(8,128)(2,1)S(1)} %opening.1.refs_4_), channel_id=1, source_target_pairs={{0,1},{1,0},{2,3},{3,2},{4,5},{5,4},{6,7},{7,6},{8,9},{9,8},{10,11... | collective-permute-start | bytes 491528 | tf_op jit(solution)/shard_map/ppermute | solution.py:30
  41.3 3.8 %collective-permute-start.8 = (bf16[512,768]{1,0:T(8,128)(2,1)S(1)}, bf16[512,768]{1,0:T(8,128)(2,1)S(1)}, u32[]{:S(2)}, u32[]{:S(2)}) collective-permute-start(bf16[512,768]{1,0:T(8,128)(2,1)S(1)} %collective-permute-done.7.refs_1_), channel_id=1, source_target_pairs={{0,1},{1,0},{2,3},{3,2},{4,5},{5,4},{6,7},{7,6},{8,9},{9,8},{10,11... | collective-permute-start | bytes 2359304 | tf_op jit(solution)/shard_map/ppermute | solution.py:30
  41.4 10.3 %collective-permute-start.9 = (bf16[80,1024]{1,0:T(8,128)(2,1)S(1)}, bf16[80,1024]{1,0:T(8,128)(2,1)S(1)}, u32[]{:S(2)}, u32[]{:S(2)}) collective-permute-start(bf16[80,1024]{1,0:T(8,128)(2,1)S(1)} %opening.1.refs_4_), channel_id=1, source_target_pairs={{0,2},{1,3},{2,0},{3,1},{4,6},{5,7},{6,4},{7,5},{8,10},{9,11},{10,... | collective-permute-start | bytes 491528 | tf_op jit(solution)/shard_map/ppermute | solution.py:30
  43.1 11.8 %collective-permute-start.11 = (bf16[80,1024]{1,0:T(8,128)(2,1)S(1)}, bf16[80,1024]{1,0:T(8,128)(2,1)S(1)}, u32[]{:S(2)}, u32[]{:S(2)}) collective-permute-start(bf16[80,1024]{1,0:T(8,128)(2,1)S(1)} %opening.1.refs_4_), channel_id=1, source_target_pairs={{4,0},{8,4},{12,8},{16,12},{20,16},{24,20},{28,24},{5,1},{9,5},{13... | collective-permute-start | bytes 491528 | tf_op jit(solution)/shard_map/ppermute | solution.py:36
  51.7 3.3 %collective-permute-start.10 = (bf16[80,1024]{1,0:T(8,128)(2,1)S(1)}, bf16[80,1024]{1,0:T(8,128)(2,1)S(1)}, u32[]{:S(2)}, u32[]{:S(2)}) collective-permute-start(bf16[80,1024]{1,0:T(8,128)(2,1)S(1)} %collective-permute-done.9.refs_4_), channel_id=1, source_target_pairs={{0,1},{1,0},{2,3},{3,2},{4,5},{5,4},{6,7},{7,6},{8,9},{9,8},{10,11... | collective-permute-start | bytes 491528 | tf_op jit(solution)/shard_map/ppermute | solution.py:30
  59.0 2.1 %collective-permute-start.12 = (f32[4,72,512]{2,1,0:T(8,128)S(1)}, f32[4,72,512]{2,1,0:T(8,128)S(1)}, u32[]{:S(2)}, u32[]{:S(2)}) collective-permute-start(f32[4,72,512]{2,1,0:T(8,128)S(1)} %get-tuple-element.121), channel_id=1, source_target_pairs={{0,1},{1,0},{2,3},{3,2},{4,5},{5,4},{6,7},{7,6},{8,9},{9,8},{10,11... | collective-permute-start | bytes 1769480 | tf_op jit(solution)/shard_map/ppermute | solution.py:30
  61.1 9.1 %collective-permute-start.14 = (f32[2,72,512]{2,1,0:T(8,128)S(1)}, f32[2,72,512]{2,1,0:T(8,128)S(1)}, u32[]{:S(2)}, u32[]{:S(2)}) collective-permute-start(f32[2,72,512]{2,1,0:T(8,128)S(1)} %slice_add_fusion), channel_id=1, source_target_pairs={{0,2},{1,3},{2,0},{3,1},{4,6},{5,7},{6,4},{7,5},{8,10},{9,11},{10,... | collective-permute-start | bytes 884744 | tf_op jit(solution)/shard_map/ppermute | solution.py:30
  61.8 8.5 %collective-permute-start.13 = (f32[2,72,512]{2,1,0:T(8,128)S(1)}, f32[2,72,512]{2,1,0:T(8,128)S(1)}, u32[]{:S(2)}, u32[]{:S(2)}) collective-permute-start(f32[2,72,512]{2,1,0:T(8,128)S(1)} %get-tuple-element.126), channel_id=1, source_target_pairs={{0,4},{4,8},{8,12},{12,16},{16,20},{20,24},{24,28},{1,5},{5,9},{9,... | collective-permute-start | bytes 884744 | tf_op jit(solution)/shard_map/ppermute | solution.py:36
  71.2 2.4 %collective-permute-start.16 = (bf16[128,1024]{1,0:T(8,128)(2,1)S(1)}, bf16[128,1024]{1,0:T(8,128)(2,1)S(1)}, u32[]{:S(2)}, u32[]{:S(2)}) collective-permute-start(bf16[128,1024]{1,0:T(8,128)(2,1)S(1)} %get-tuple-element.129.refs_4_), channel_id=1, source_target_pairs={{0,1},{1,0},{2,3},{3,2},{4,5},{5,4},{6,7},{7,6},{8,9},{9,8},{10,11... | collective-permute-start | bytes 786440 | tf_op jit(solution)/shard_map/ppermute | solution.py:30
  71.3 8.7 %collective-permute-start.17 = (bf16[128,1024]{1,0:T(8,128)(2,1)S(1)}, bf16[128,1024]{1,0:T(8,128)(2,1)S(1)}, u32[]{:S(2)}, u32[]{:S(2)}) collective-permute-start(bf16[128,1024]{1,0:T(8,128)(2,1)S(1)} %get-tuple-element.129.refs_4_), channel_id=1, source_target_pairs={{0,2},{1,3},{2,0},{3,1},{4,6},{5,7},{6,4},{7,5},{8,10},{9,11},{10,... | collective-permute-start | bytes 786440 | tf_op jit(solution)/shard_map/ppermute | solution.py:30
  72.1 1.5 %collective-permute-start.15 = (f32[64,64]{1,0:T(8,128)S(1)}, f32[64,64]{1,0:T(8,128)S(1)}, u32[]{:S(2)}, u32[]{:S(2)}) collective-permute-start(f32[64,64]{1,0:T(8,128)S(1)} %get-tuple-element.128), channel_id=1, source_target_pairs={{0,1},{1,0},{2,3},{3,2},{4,5},{5,4},{6,7},{7,6},{8,9},{9,8},{10,11... | collective-permute-start | bytes 49160 | tf_op jit(solution)/shard_map/ppermute | solution.py:657
  72.3 11.6 %collective-permute-start.19 = (bf16[128,1024]{1,0:T(8,128)(2,1)S(1)}, bf16[128,1024]{1,0:T(8,128)(2,1)S(1)}, u32[]{:S(2)}, u32[]{:S(2)}) collective-permute-start(bf16[128,1024]{1,0:T(8,128)(2,1)S(1)} %get-tuple-element.129.refs_4_), channel_id=1, source_target_pairs={{4,0},{8,4},{12,8},{16,12},{20,16},{24,20},{28,24},{5,1},{9,5},{13... | collective-permute-start | bytes 786440 | tf_op jit(solution)/shard_map/ppermute | solution.py:36
  80.0 3.9 %collective-permute-start.20 = (bf16[128,1024]{1,0:T(8,128)(2,1)S(1)}, bf16[128,1024]{1,0:T(8,128)(2,1)S(1)}, u32[]{:S(2)}, u32[]{:S(2)}) collective-permute-start(bf16[128,1024]{1,0:T(8,128)(2,1)S(1)} %collective-permute-done.17.refs_4_), channel_id=1, source_target_pairs={{0,1},{1,0},{2,3},{3,2},{4,5},{5,4},{6,7},{7,6},{8,9},{9,8},{10,11... | collective-permute-start | bytes 786440 | tf_op jit(solution)/shard_map/ppermute | solution.py:30
  80.0 3.9 %collective-permute-start.18 = (f32[64,64]{1,0:T(8,128)S(1)}, f32[64,64]{1,0:T(8,128)S(1)}, u32[]{:S(2)}, u32[]{:S(2)}) collective-permute-start(f32[64,64]{1,0:T(8,128)S(1)} %add.40), channel_id=1, source_target_pairs={{0,2},{1,3},{2,0},{3,1},{4,6},{5,7},{6,4},{7,5},{8,10},{9,11},{10,... | collective-permute-start | bytes 49160 | tf_op jit(solution)/shard_map/ppermute | solution.py:657
  83.9 6.3 %collective-permute-start.21 = (f32[64,64]{1,0:T(8,128)S(1)}, f32[64,64]{1,0:T(8,128)S(1)}, u32[]{:S(2)}, u32[]{:S(2)}) collective-permute-start(f32[64,64]{1,0:T(8,128)S(1)} %add.41), channel_id=1, source_target_pairs={{0,4},{1,5},{2,6},{3,7},{4,0},{5,1},{6,2},{7,3},{8,12},{9,13},{10,... | collective-permute-start | bytes 49160 | tf_op jit(solution)/shard_map/ppermute | solution.py:657
  90.3 4.1 %collective-permute-start.22 = (f32[4,64,512]{2,1,0:T(8,128)S(1)}, f32[4,64,512]{2,1,0:T(8,128)S(1)}, u32[]{:S(2)}, u32[]{:S(2)}) collective-permute-start(f32[4,64,512]{2,1,0:T(8,128)S(1)} %get-tuple-element.144), channel_id=1, source_target_pairs={{0,1},{1,0},{2,3},{3,2},{4,5},{5,4},{6,7},{7,6},{8,9},{9,8},{10,11... | collective-permute-start | bytes 1572872 | tf_op jit(solution)/shard_map/ppermute | solution.py:30
  90.3 4.0 %collective-permute-start.23 = (f32[64,64]{1,0:T(8,128)S(1)}, f32[64,64]{1,0:T(8,128)S(1)}, u32[]{:S(2)}, u32[]{:S(2)}) collective-permute-start(f32[64,64]{1,0:T(8,128)S(1)} %add.42), channel_id=1, source_target_pairs={{0,8},{1,9},{2,10},{3,11},{4,12},{5,13},{6,14},{7,15},{8,0},{9,1},... | collective-permute-start | bytes 49160 | tf_op jit(solution)/shard_map/ppermute | solution.py:657
  94.4 14.6 %collective-permute-start.25 = (f32[2,64,512]{2,1,0:T(8,128)S(1)}, f32[2,64,512]{2,1,0:T(8,128)S(1)}, u32[]{:S(2)}, u32[]{:S(2)}) collective-permute-start(f32[2,64,512]{2,1,0:T(8,128)S(1)} %slice_add_fusion.1), channel_id=1, source_target_pairs={{0,2},{1,3},{2,0},{3,1},{4,6},{5,7},{6,4},{7,5},{8,10},{9,11},{10,... | collective-permute-start | bytes 786440 | tf_op jit(solution)/shard_map/ppermute | solution.py:30
  95.6 13.4 %collective-permute-start.24 = (f32[2,64,512]{2,1,0:T(8,128)S(1)}, f32[2,64,512]{2,1,0:T(8,128)S(1)}, u32[]{:S(2)}, u32[]{:S(2)}) collective-permute-start(f32[2,64,512]{2,1,0:T(8,128)S(1)} %get-tuple-element.152), channel_id=1, source_target_pairs={{0,4},{4,8},{8,12},{12,16},{16,20},{20,24},{24,28},{1,5},{5,9},{9,... | collective-permute-start | bytes 786440 | tf_op jit(solution)/shard_map/ppermute | solution.py:36
  98.5 8.5 %collective-permute-start.26 = (f32[64,64]{1,0:T(8,128)S(1)}, f32[64,64]{1,0:T(8,128)S(1)}, u32[]{:S(2)}, u32[]{:S(2)}) collective-permute-start(f32[64,64]{1,0:T(8,128)S(1)} %add.44), channel_id=1, source_target_pairs={{0,16},{1,17},{2,18},{3,19},{4,20},{5,21},{6,22},{7,23},{8,24},{9,... | collective-permute-start | bytes 49160 | tf_op jit(solution)/shard_map/ppermute | solution.py:657
  110.5 1.3 collective-permute-start.27
  111.8 3.9 %collective-permute-start.28 = (f32[64,64]{1,0:T(8,128)S(1)}, f32[64,64]{1,0:T(8,128)S(1)}, u32[]{:S(2)}, u32[]{:S(2)}) collective-permute-start(f32[64,64]{1,0:T(8,128)S(1)} %add.46), channel_id=1, source_target_pairs={{0,2},{1,5},{2,0},{3,7},{4,6},{5,1},{6,4},{7,3},{8,10},{9,13},{10,... | collective-permute-start | bytes 49160 | tf_op jit(solution)/shard_map/ppermute | solution.py:634
  111.9 3.8 %collective-permute-start.29 = (f32[64,64]{1,0:T(8,128)S(1)}, f32[64,64]{1,0:T(8,128)S(1)}, u32[]{:S(2)}, u32[]{:S(2)}) collective-permute-start(f32[64,64]{1,0:T(8,128)S(1)} %add.46), channel_id=1, source_target_pairs={{1,7},{3,5},{5,3},{7,1},{9,15},{11,13},{13,11},{15,9},{17,23},{19,... | collective-permute-start | bytes 49160 | tf_op jit(solution)/shard_map/ppermute | solution.py:634
  115.7 4.2 %collective-permute-start.30 = (f32[64,64]{1,0:T(8,128)S(1)}, f32[64,64]{1,0:T(8,128)S(1)}, u32[]{:S(2)}, u32[]{:S(2)}) collective-permute-start(f32[64,64]{1,0:T(8,128)S(1)} %select_add_fusion.1), channel_id=1, source_target_pairs={{0,1},{1,0},{2,3},{3,2},{4,5},{5,4},{6,7},{7,6},{8,9},{9,8},{10,11... | collective-permute-start | bytes 49160 | tf_op jit(solution)/shard_map/ppermute | solution.py:634
  120.0 5.1 %collective-permute-start.31 = (f32[64,64]{1,0:T(8,128)S(1)}, f32[64,64]{1,0:T(8,128)S(1)}, u32[]{:S(2)}, u32[]{:S(2)}) collective-permute-start(f32[64,64]{1,0:T(8,128)S(1)} %add.49), channel_id=1, source_target_pairs={{0,8},{1,17},{2,10},{3,19},{4,12},{5,21},{6,14},{7,23},{8,0},{9,25... | collective-permute-start | bytes 49160 | tf_op jit(solution)/shard_map/ppermute | solution.py:634
  123.2 1.9 %collective-permute-start.32 = (f32[64,64]{1,0:T(8,128)S(1)}, f32[64,64]{1,0:T(8,128)S(1)}, u32[]{:S(2)}, u32[]{:S(2)}) collective-permute-start(f32[64,64]{1,0:T(8,128)S(1)} %add.49), channel_id=1, source_target_pairs={{1,25},{3,27},{5,29},{7,31},{9,17},{11,19},{13,21},{15,23},{17,9},... | collective-permute-start | bytes 49160 | tf_op jit(solution)/shard_map/ppermute | solution.py:634
  125.1 5.3 %collective-permute-start.33 = (f32[64,64]{1,0:T(8,128)S(1)}, f32[64,64]{1,0:T(8,128)S(1)}, u32[]{:S(2)}, u32[]{:S(2)}) collective-permute-start(f32[64,64]{1,0:T(8,128)S(1)} %select_add_fusion), channel_id=1, source_target_pairs={{0,1},{1,0},{2,3},{3,2},{4,5},{5,4},{6,7},{7,6},{8,9},{9,8},{10,11... | collective-permute-start | bytes 49160 | tf_op jit(solution)/shard_map/ppermute | solution.py:634

commit v16 on v12

--- a/solution.py
+++ b/solution.py
@@ -8,7 +8,6 @@
 from jax.sharding import PartitionSpec as P
 
 PTS = 512
-ITERS = 2
 LOG2E = 1.4426950408889634
 DEAD = 65536.0
 EXTRA = 16
@@ -479,21 +478,19 @@
     )
 
 
-def scaled_gram(parts, own, counts, degree, inverse, split):
+def scaled_gram(parts, own, counts, degree, earlier):
     columns = own.shape[0] if degree is not None else own.shape[0] - EXTRA
     total = own.shape[1]
     first = degree is None
     shapes = [
         jax.ShapeDtypeStruct((columns, total), jnp.float32),
-        jax.ShapeDtypeStruct((columns, columns), jnp.float32),
+        jax.ShapeDtypeStruct((columns, columns * (1 if first else 2)), jnp.float32),
     ]
-    if split:
+    if first:
         shapes.append(jax.ShapeDtypeStruct((2 * columns, total), jnp.bfloat16))
-    if first:
         shapes.append(jax.ShapeDtypeStruct((8, total), jnp.float32))
     operands = list(parts) + [own]
-    operands += [] if first else [degree]
-    operands += [] if inverse is None else [inverse]
+    operands += [] if first else [degree, earlier]
 
     def kernel(count_ref, *refs):
         ins = list(refs[: len(operands)])
@@ -515,12 +512,8 @@
             used = lax.broadcasted_iota(jnp.int32, (columns, PTS), 1) < count_ref[block]
             held = own_ref[0:columns, lanes].astype(jnp.float32)
             z = (held + jnp.where(used, sums[0:columns], 0.0)) / level
-            if inverse is not None:
-                z = jnp.dot(
-                    ins[-1][...], z, precision=HIGHEST, preferred_element_type=jnp.float32
-                )
             z_out[:, lanes] = z
-            if split:
+            if first:
                 high = z.astype(jnp.bfloat16)
                 outs[2][0:columns, lanes] = high
                 rest = z - high.astype(jnp.float32)
@@ -528,6 +521,8 @@
             gram = gram + lax.dot_general(
                 z, z, (((1,), (1,)), ((), ())), precision=HIGHEST, preferred_element_type=jnp.float32
             )
+        if not first:
+            gram = jnp.concatenate([ins[-1][...], gram], axis=1)
         gram_out[...] = gram
 
     return pl.pallas_call(
@@ -584,26 +579,70 @@
     return jnp.concatenate(results, axis=0)[:, size:wide]
 
 
-def factor_kernel(gram, out):
-    out[...] = inverse_factor(gram[...])
-
-
-def factor(gram):
+def exact_dot(left, right, contract):
+    return lax.dot_general(
+        left,
+        right,
+        (contract, ((), ())),
+        precision=HIGHEST,
+        preferred_element_type=jnp.float32,
+    )
+
+
+def factors_kernel(grams, both_out, first_out, sound_out):
+    columns = grams.shape[0]
+    plain = ((1,), (0,))
+    turned = ((1,), (1,))
+    second = grams[:, columns : 2 * columns]
+    first_inverse = inverse_factor(grams[:, 0:columns])
+    middle = exact_dot(exact_dot(first_inverse, second, plain), first_inverse, turned)
+    both = exact_dot(inverse_factor(middle), first_inverse, plain)
+    both_out[...] = both
+    first_out[...] = first_inverse
+    row_id = lax.broadcasted_iota(jnp.int32, (columns, columns), 0)
+    col_id = lax.broadcasted_iota(jnp.int32, (columns, columns), 1)
+    trace = jnp.sum(jnp.where(row_id == col_id, second, 0.0))
+    spread = jnp.sum(both * both) * trace / (columns * columns)
+    sound_out[0] = jnp.where(spread < 64.0, 1, 0)
+
+
+def factors(grams):
+    columns = grams.shape[0]
+    square = jax.ShapeDtypeStruct((columns, columns), jnp.float32)
     return pl.pallas_call(
-        factor_kernel,
-        out_shape=jax.ShapeDtypeStruct(gram.shape, jnp.float32),
+        factors_kernel,
+        out_shape=(square, square, jax.ShapeDtypeStruct((1,), jnp.int32)),
         in_specs=[spec(VMEM)],
-        out_specs=spec(VMEM),
-        cost_estimate=cost(2**16, 2**16),
+        out_specs=(spec(VMEM), spec(VMEM), spec(SMEM)),
+        cost_estimate=cost(2**30, 2**16),
         compiler_params=pltpu.CompilerParams(vmem_limit_bytes=2 * 2**20),
-        name="factor",
-    )(gram)
+        name="factors",
+    )(grams)
+
+
+def apply_kernel(factor, z, out, *gram):
+    value = exact_dot(factor[...], z[...], ((1,), (0,)))
+    out[...] = value
+    if gram:
+        gram[0][...] = exact_dot(value, value, ((1,), (1,)))
+
+
+def applied(factor, z, with_gram):
+    shapes = [jax.ShapeDtypeStruct(z.shape, jnp.float32)]
+    if with_gram:
+        shapes.append(jax.ShapeDtypeStruct(factor.shape, jnp.float32))
+    return pl.pallas_call(
+        apply_kernel,
+        out_shape=shapes,
+        in_specs=[spec(VMEM)] * 2,
+        out_specs=[spec(VMEM)] * len(shapes),
+        compiler_params=pltpu.CompilerParams(vmem_limit_bytes=4 * 2**20),
+        name="applied",
+    )(factor, z)
 
 
 def embed_kernel(gram, z, out):
-    out[...] = jnp.dot(
-        inverse_factor(gram[...]), z[...], precision=HIGHEST, preferred_element_type=jnp.float32
-    )
+    out[...] = exact_dot(inverse_factor(gram[...]), z[...], ((1,), (0,)))
 
 
 def embedding(gram, z):
@@ -612,7 +651,6 @@
         out_shape=jax.ShapeDtypeStruct(z.shape, jnp.float32),
         in_specs=[spec(VMEM)] * 2,
         out_specs=spec(VMEM),
-        cost_estimate=cost(2**30, 2**20),
         compiler_params=pltpu.CompilerParams(vmem_limit_bytes=4 * 2**20),
         name="embedding",
     )(gram, z)
@@ -731,43 +769,41 @@
     results = products(entries, (1,), beyond(vecs), kept, results, urgent, height, 1)
     sums, (at_home,) = send_urgent(results, (at_home,), group, blocks_dev)
     sums = finish_home(entries, beyond(vecs), kept, at_home, blocks_dev, height, 1) + sums
-    z, gram, parts, degree = scaled_gram(sums, vec, counts, None, None, True)
-    for turn in range(1, ITERS):
-        stages = sum_stages()
-        far_part = from_behind(parts, "blk", -1)
-        crossed = gather_far_bits(parts)
-        mate_part = swap(parts, "grp", 1)
-        gram = all_sum(gram, stages[:1])
-        at_home, *results = products(
-            entries,
-            (0,),
-            {0: parts, blocks_dev: mate_part},
-            kept,
-            (),
-            [[(0, blocks_dev)]] + urgent,
-            columns,
-            2,
-        )
-        gram, at_home, *tied = lax.optimization_barrier((gram, at_home, *crossed.values()))
-        crossed = dict(zip(crossed, tied))
-        vecs = beyond(window_of(parts, mate_part, crossed, far_part))
-        gram = all_sum(gram, stages[1:2])
-        gram, *tied = lax.optimization_barrier((gram, *vecs.values()))
-        vecs = dict(zip(vecs, tied))
-        results = products(entries, (1,), vecs, kept, results, urgent, columns, 2)
-        gram = all_sum(gram, stages[2:3])
-        gram, *results = lax.optimization_barrier((gram, *results))
-        gram = all_sum(gram, stages[3:4])
-        sums, (at_home, gram) = send_urgent(results, (at_home, gram), group, blocks_dev)
-        gram = all_sum(gram, stages[4:-1])
-        own = finish_home(entries, vecs, kept, at_home, blocks_dev, columns, 2)
-        gram, own[0] = all_sum(gram, stages[4:][-1:], own[0])
-        sums = own + sums
-        inverse = factor(gram)
-        z, gram, *parts = scaled_gram(sums, z, counts, degree, inverse, turn + 1 < ITERS)
-        parts = parts[0] if parts else None
+    z, gram, parts, degree = scaled_gram(sums, vec, counts, None, None)
+
+    far_part = from_behind(parts, "blk", -1)
+    crossed = gather_far_bits(parts)
+    mate_part = swap(parts, "grp", 1)
+    at_home, *results = products(
+        entries,
+        (0,),
+        {0: parts, blocks_dev: mate_part},
+        kept,
+        (),
+        [[(0, blocks_dev)]] + urgent,
+        columns,
+        2,
+    )
+    at_home, *tied = lax.optimization_barrier((at_home, *crossed.values()))
+    crossed = dict(zip(crossed, tied))
+    vecs = beyond(window_of(parts, mate_part, crossed, far_part))
+    results = products(entries, (1,), vecs, kept, results, urgent, columns, 2)
+    sums, (at_home,) = send_urgent(results, (at_home,), group, blocks_dev)
+    sums = finish_home(entries, vecs, kept, at_home, blocks_dev, columns, 2) + sums
+    z, grams = scaled_gram(sums, z, counts, degree, gram)
+
     stages = sum_stages()
-    return embedding(all_sum(gram, stages[:1] + pairs_of(stages[1:])), z)
+    stages = stages[:1] + pairs_of(stages[1:])
+    both, first, sound = factors(all_sum(grams, stages))
+
+    def at_once(both, first, z):
+        return applied(both, z, False)[0]
+
+    def in_two(both, first, z):
+        value, gram = applied(first, z, True)
+        return embedding(all_sum(gram, stages), value)
+
+    return lax.cond(sound[0] == 1, at_once, in_two, both, first, z)
 
 
 def solution(mesh):

time: 132 us -> 130 us (0.985)
  starting transfers between devices: 41.9 us -> 28.5 us
  waiting for transfers between devices: 32.3 us -> 42.2 us
    ppermute x12 -> x7, starting transfers between devices: 21.7 us -> 9.79 us  [all_sum(): lax.ppermute(value, ('blk', 'grp'), [(source, source ^ move) for source i...]
    ppermute x6, waiting for transfers between devices: 7.69 us -> 16.1 us  [from_behind(): lax.ppermute(value, axis, [(source, source + steps) for source in range(i...]
    ppermute x16, waiting for transfers between devices: 9.64 us -> 14.9 us  [swap(): lax.ppermute(value, axis, [(source, source ^ bit) for source in range(cou...]
    ppermute x12 -> x7, waiting for transfers between devices: 15 us -> 11.2 us  [all_sum(): lax.ppermute(value, ('blk', 'grp'), [(source, source ^ move) for source i...]
    pallas_call x6, Pallas kernels: 17.2 us -> 18.7 us  [products(): pl.pallas_call(kernel, out_shape=shapes, in_specs=[spec(SMEM)] * 4 + [spe...]
  transfers between devices with their start and end apart: 34 -> 29, of which waited for: 14 -> 14; matrix products, arithmetic and copies ran while one was open for 1% -> 1% of each run, Pallas kernels for 35% -> 32%
where the time goes in v16:
time: 130 us; the launch traced here: 132 us
  Pallas kernels  57 us (44%)
  waiting for transfers between devices  42.2 us (32%)
  starting transfers between devices  28.5 us (22%)
  local copies, waits for them, and re-layouts  2.27 us (2%)
  between operations  1.64 us (1%)
    pallas_call x6, Pallas kernels, products(): pl.pallas_call(kernel, out_shape=shapes, in_specs=[spec(SMEM)] * 4 + [spe...  18.7 us
    pallas_call x4, Pallas kernels, build_tiles(): pl.pallas_call(kernel, out_shape=shapes, in_specs=[spec(SMEM)] * len(scal...  16.2 us
    ppermute x6, waiting for transfers between devices, from_behind(): lax.ppermute(value, axis, [(source, source + steps) for source in range(i...  16.1 us
    ppermute x16, waiting for transfers between devices, swap(): lax.ppermute(value, axis, [(source, source ^ bit) for source in range(cou...  14.9 us
    pallas_call x1, Pallas kernels, listing(): pl.pallas_call(functools.partial(listing_kernel, group, cap, blocks_dev),...  14.3 us
    ppermute x7, waiting for transfers between devices, all_sum(): lax.ppermute(value, ('blk', 'grp'), [(source, source ^ move) for source i...  11.2 us
    ppermute x7, starting transfers between devices, all_sum(): lax.ppermute(value, ('blk', 'grp'), [(source, source ^ move) for source i...  9.79 us
    ppermute x6, starting transfers between devices, from_behind(): lax.ppermute(value, axis, [(source, source + steps) for source in range(i...  9.66 us
  transfers between devices with their start and end apart: 29, of which 14 were waited for; matrix products, arithmetic and copies ran while one was open for 1% of the time, Pallas kernels for 32%

profile of v16, /device:TPU:0, one launch (start us, length us, event | category | flops | bytes accessed | tf_op | source)
XLA Modules:
  0.0 131.8 jit_solution(10652854956595737249)
XLA Ops:
  0.0 0.5 collective-permute-start.7
  0.5 1.5 %fusion = (bf16[512,768]{1,0:T(8,128)(2,1)S(1)}, bf16[512,768]{1,0:T(8,128)(2,1)S(1)}) fusion(bf16[1024,768]{1,0:T(8,128)(2,1)} %refs_3_.1), kind=kLoop, calls=%fused_computation.7 | loop fusion | bytes 3145728 | tf_op jit(solution)/shard_map/slice | solution.py:699
  2.1 1.3 collective-permute-start.8
  3.4 2.7 %collective-permute-start.9 = (bf16[512,768]{1,0:T(8,128)(2,1)S(1)}, bf16[512,768]{1,0:T(8,128)(2,1)S(1)}, u32[]{:S(2)}, u32[]{:S(2)}) collective-permute-start(bf16[512,768]{1,0:T(8,128)(2,1)S(1)} %get-tuple-element.156), channel_id=1, source_target_pairs={{0,2},{1,3},{2,0},{3,1},{4,6},{5,7},{6,4},{7,5},{8,10},{9,11},{10,... | collective-permute-start | bytes 2359304 | tf_op jit(solution)/shard_map/ppermute | solution.py:29
  6.0 1.3 collective-permute-start.10
  7.3 0.1 collective-permute-start.14
  8.1 14.3 %listing.1 = (s32[16]{0:T(128)S(1)}, s32[16]{0:T(128)S(1)}, s32[4]{0:T(128)S(1)}, s32[32]{0:T(128)S(1)}, s32[32]{0:T(128)S(1)}, /*index=5*/s32[32]{0:T(128)S(1)}, s32[7]{0:T(128)S(1)}) custom-call(s32[64]{0:T(128)S(1)} %copy-done.3, s32[64]{0:T(128)S(1)} %copy-done.4, s32[1]{0:T(128)S(6)} %copy.33.live), custom_call_target="tpu_custom_call" | custom-call | flops 1048576 | bytes 1024 | tf_op jit(solution)/shard_map/listing/pallas_call | solution.py:213
  22.4 0.0 collective-permute-done.7.refs_4_
  22.4 0.6 opening.1.refs_4_
  23.0 2.0 %collective-permute-done.8.refs_5_ = bf16[512,768]{1,0:T(8,128)(2,1)S(1)} collective-permute-done((bf16[512,768]{1,0:T(8,128)(2,1)S(1)}, bf16[512,768]{1,0:T(8,128)(2,1)S(1)}, u32[]{:S(2)}, u32[]{:S(2)}) %collective-permute-start.8) | collective-permute-done | bytes 786464 | tf_op jit(solution)/shard_map/ppermute | solution.py:35
  25.0 0.1 fusion.1
  25.0 0.1 collective-permute-start.12
  25.1 0.5 collective-permute-start.13
  25.6 0.1 collective-permute-start.11
  25.7 7.9 %first_tiles.1 = (bf16[5120,768]{1,0:T(8,128)(2,1)S(1)}, f32[10,8,512]{2,1,0:T(8,128)S(1)}, f32[8,512,128]{2,1,0:T(8,128)S(1)}, bf16[17,512,512]{2,1,0:T(8,128)(2,1)S(1)}) custom-call(s32[4]{0:T(128)S(1)} %get-tuple-element.96.refs_0_, s32[16]{0:T(128)S(1)} %get-tuple-element.97.refs_1_, s32[16]{0:T(128)S(1)} %get-tuple-element.98.refs_2_, ...), custom_call_target="tpu_custom_call" | custom-call | flops 1048576 | bytes 1048576 | tf_op jit(solution)/shard_map/first_tiles/pallas_call | solution.py:330
  33.6 0.1 pad_maximum_fusion.refs_3_
  33.7 2.1 %second_tiles.1 = (bf16[5120,768]{1,0:T(8,128)(2,1)S(1)}, f32[10,8,512]{2,1,0:T(8,128)S(1)}, f32[8,512,128]{2,1,0:T(8,128)S(1)}, bf16[17,512,512]{2,1,0:T(8,128)(2,1)S(1)}) custom-call(s32[4]{0:T(128)S(1)} %get-tuple-element.96.refs_0_, s32[16]{0:T(128)S(1)} %get-tuple-element.97.refs_1_, ...), custom_call_target="tpu_custom_call", output_to_operand_aliasing={{0}: (4, {}), {1}: (5, {}), {2}: (6, {}), {3}: (7, {})} | custom-call | flops 1048576 | bytes 1048576 | tf_op jit(solution)/shard_map/second_tiles/pallas_call | solution.py:330
  35.8 5.7 %collective-permute-done.10.refs_0_ = bf16[512,768]{1,0:T(8,128)(2,1)S(1)} collective-permute-done((bf16[512,768]{1,0:T(8,128)(2,1)S(1)}, bf16[512,768]{1,0:T(8,128)(2,1)S(1)}, u32[]{:S(2)}, u32[]{:S(2)}) %collective-permute-start.10) | collective-permute-done | bytes 786464 | tf_op jit(solution)/shard_map/ppermute | solution.py:35
  41.5 1.8 %collective-permute-start.16 = (bf16[80,1024]{1,0:T(8,128)(2,1)S(1)}, bf16[80,1024]{1,0:T(8,128)(2,1)S(1)}, u32[]{:S(2)}, u32[]{:S(2)}) collective-permute-start(bf16[80,1024]{1,0:T(8,128)(2,1)S(1)} %opening.1.refs_4_), channel_id=1, source_target_pairs={{0,2},{1,3},{2,0},{3,1},{4,6},{5,7},{6,4},{7,5},{8,10},{9,11},{10,... | collective-permute-start | bytes 491528 | tf_op jit(solution)/shard_map/ppermute | solution.py:29
  43.3 1.3 collective-permute-start.18
  44.6 0.8 more_blocks.1
  45.3 5.4 %last_tiles.1 = (bf16[5120,768]{1,0:T(8,128)(2,1)S(1)}, f32[10,8,512]{2,1,0:T(8,128)S(1)}, f32[8,512,128]{2,1,0:T(8,128)S(1)}, bf16[17,512,512]{2,1,0:T(8,128)(2,1)S(1)}) custom-call(s32[4]{0:T(128)S(1)} %get-tuple-element.96.refs_0_, s32[16]{0:T(128)S(1)} %get-tuple-element.97.refs_1_, ...), custom_call_target="tpu_custom_call", output_to_operand_aliasing={{0}: (4, {}), {1}: (5, {}), {2}: (6, {}), {3}: (7, {})} | custom-call | flops 4294967296 | bytes 1048576 | tf_op jit(solution)/shard_map/last_tiles/pallas_call | solution.py:330
  50.7 1.3 collective-permute-start.17
  52.1 3.0 %products.6 = (f32[2,72,512]{2,1,0:T(8,128)S(1)}, f32[4,72,512]{2,1,0:T(8,128)S(1)}, f32[2,72,512]{2,1,0:T(8,128)S(1)}, f32[2,72,512]{2,1,0:T(8,128)S(1)}) custom-call(s32[32]{0:T(128)S(1)} %get-tuple-element.88.refs_0_, s32[32]{0:T(128)S(1)} %get-tuple-element.89.refs_1_, s32[32]{0:T(128)S(1)} %get-tuple-element.90.refs_2_, ...), custom_call_target="tpu_custom_call" | custom-call | flops 1048576 | bytes 1048576 | tf_op jit(solution)/shard_map/products/pallas_call | solution.py:421
  55.1 4.0 %products.7 = (f32[4,72,512]{2,1,0:T(8,128)S(1)}, f32[2,72,512]{2,1,0:T(8,128)S(1)}, f32[2,72,512]{2,1,0:T(8,128)S(1)}) custom-call(s32[32]{0:T(128)S(1)} %get-tuple-element.88.refs_0_, s32[32]{0:T(128)S(1)} %get-tuple-element.89.refs_1_, s32[32]{0:T(128)S(1)} %get-tuple-element.90.refs_2_, s32[7]{0:T(128)S(1)} %get-tuple-element.91.refs_3_, ...), custom_call_target="tpu_custom_call" | custom-call | flops 2147483648 | bytes 1048576 | tf_op jit(solution)/shard_map/products/pallas_call | solution.py:421
  59.1 0.1 collective-permute-start.19
  59.2 2.0 %collective-permute-done.19.refs_2_ = f32[4,72,512]{2,1,0:T(8,128)S(1)} collective-permute-done((f32[4,72,512]{2,1,0:T(8,128)S(1)}, f32[4,72,512]{2,1,0:T(8,128)S(1)}, u32[]{:S(2)}, u32[]{:S(2)}) %collective-permute-start.19) | collective-permute-done | bytes 589856 | tf_op jit(solution)/shard_map/ppermute | solution.py:29
  61.3 0.1 collective-permute-start.21
  61.3 1.3 collective-permute-start.20
  62.7 2.2 %products.8.refs_0_ = f32[2,72,512]{2,1,0:T(8,128)S(1)} custom-call(s32[32]{0:T(128)S(1)} %get-tuple-element.88.refs_0_, s32[32]{0:T(128)S(1)} %get-tuple-element.89.refs_1_, s32[32]{0:T(128)S(1)} %get-tuple-element.90.refs_2_, s32[7]{0:T(128)S(1)} %get-tuple-element.91.refs_3_, bf16[80,1024]{1,0:T(8,128)(2,1)S(1)} %collective-permute-done.16.refs_4_, ...), custom_call_target="tpu_custom_call" | custom-call | flops 1048576 | bytes 1048576 | tf_op jit(solution)/shard_map/products/pallas_call | solution.py:421
  64.8 5.5 %collective-permute-done.21.refs_3_ = f32[2,72,512]{2,1,0:T(8,128)S(1)} collective-permute-done((f32[2,72,512]{2,1,0:T(8,128)S(1)}, f32[2,72,512]{2,1,0:T(8,128)S(1)}, u32[]{:S(2)}, u32[]{:S(2)}) %collective-permute-start.21) | collective-permute-done | bytes 294944 | tf_op jit(solution)/shard_map/ppermute | solution.py:29
  70.4 0.9 scaled_gram.2
  71.3 0.1 collective-permute-start.22
  71.4 0.9 collective-permute-start.23
  72.3 1.3 collective-permute-start.25
  73.6 3.1 %products.9 = (f32[2,64,512]{2,1,0:T(8,128)S(1)}, f32[4,64,512]{2,1,0:T(8,128)S(1)}, f32[2,64,512]{2,1,0:T(8,128)S(1)}, f32[2,64,512]{2,1,0:T(8,128)S(1)}) custom-call(s32[32]{0:T(128)S(1)} %get-tuple-element.88.refs_0_, s32[32]{0:T(128)S(1)} %get-tuple-element.89.refs_1_, s32[32]{0:T(128)S(1)} %get-tuple-element.90.refs_2_, ...), custom_call_target="tpu_custom_call" | custom-call | flops 1048576 | bytes 1048576 | tf_op jit(solution)/shard_map/products/pallas_call | solution.py:421
  76.7 3.4 %collective-permute-done.23.refs_4_ = bf16[128,1024]{1,0:T(8,128)(2,1)S(1)} collective-permute-done((bf16[128,1024]{1,0:T(8,128)(2,1)S(1)}, bf16[128,1024]{1,0:T(8,128)(2,1)S(1)}, u32[]{:S(2)}, u32[]{:S(2)}) %collective-permute-start.23) | collective-permute-done | bytes 262176 | tf_op jit(solution)/shard_map/ppermute | solution.py:29
  80.1 7.2 %collective-permute-done.25.refs_6_ = bf16[128,1024]{1,0:T(8,128)(2,1)S(1)} collective-permute-done((bf16[128,1024]{1,0:T(8,128)(2,1)S(1)}, bf16[128,1024]{1,0:T(8,128)(2,1)S(1)}, u32[]{:S(2)}, u32[]{:S(2)}) %collective-permute-start.25) | collective-permute-done | bytes 262176 | tf_op jit(solution)/shard_map/ppermute | solution.py:35
  87.3 4.1 %products.10 = (f32[4,64,512]{2,1,0:T(8,128)S(1)}, f32[2,64,512]{2,1,0:T(8,128)S(1)}, f32[2,64,512]{2,1,0:T(8,128)S(1)}) custom-call(s32[32]{0:T(128)S(1)} %get-tuple-element.88.refs_0_, s32[32]{0:T(128)S(1)} %get-tuple-element.89.refs_1_, s32[32]{0:T(128)S(1)} %get-tuple-element.90.refs_2_, s32[7]{0:T(128)S(1)} %get-tuple-element.91.refs_3_, ...), custom_call_target="tpu_custom_call" | custom-call | flops 2147483648 | bytes 1048576 | tf_op jit(solution)/shard_map/products/pallas_call | solution.py:421
  91.4 0.1 collective-permute-start.26
  91.5 1.9 %collective-permute-done.26.refs_2_ = f32[4,64,512]{2,1,0:T(8,128)S(1)} collective-permute-done((f32[4,64,512]{2,1,0:T(8,128)S(1)}, f32[4,64,512]{2,1,0:T(8,128)S(1)}, u32[]{:S(2)}, u32[]{:S(2)}) %collective-permute-start.26) | collective-permute-done | bytes 524320 | tf_op jit(solution)/shard_map/ppermute | solution.py:29
  93.4 0.9 collective-permute-start.28
  94.3 3.2 %collective-permute-start.27 = (f32[2,64,512]{2,1,0:T(8,128)S(1)}, f32[2,64,512]{2,1,0:T(8,128)S(1)}, u32[]{:S(2)}, u32[]{:S(2)}) collective-permute-start(f32[2,64,512]{2,1,0:T(8,128)S(1)} %get-tuple-element.144), channel_id=1, source_target_pairs={{0,4},{4,8},{8,12},{12,16},{16,20},{20,24},{24,28},{1,5},{5,9},{9,... | collective-permute-start | bytes 786440 | tf_op jit(solution)/shard_map/ppermute | solution.py:35
  97.5 2.3 %products.11.refs_0_ = f32[2,64,512]{2,1,0:T(8,128)S(1)} custom-call(s32[32]{0:T(128)S(1)} %get-tuple-element.88.refs_0_, s32[32]{0:T(128)S(1)} %get-tuple-element.89.refs_1_, s32[32]{0:T(128)S(1)} %get-tuple-element.90.refs_2_, s32[7]{0:T(128)S(1)} %get-tuple-element.91.refs_3_, bf16[128,1024]{1,0:T(8,128)(2,1)S(1)} %collective-permute-done.23.refs_4_, ...), custom_call_target="tpu_custom_call" | custom-call | flops 1048576 | bytes 1048576 | tf_op jit(solution)/shard_map/products/pallas_call | solution.py:421
  99.8 2.0 %collective-permute-done.28.refs_3_ = f32[2,64,512]{2,1,0:T(8,128)S(1)} collective-permute-done((f32[2,64,512]{2,1,0:T(8,128)S(1)}, f32[2,64,512]{2,1,0:T(8,128)S(1)}, u32[]{:S(2)}, u32[]{:S(2)}) %collective-permute-start.28) | collective-permute-done | bytes 262176 | tf_op jit(solution)/shard_map/ppermute | solution.py:29
  101.9 1.2 collective-permute-done.27.refs_1_
  103.1 1.0 scaled_gram.3
  104.1 0.1 collective-permute-start.29
  104.2 1.2 collective-permute-done.29
  105.4 1.2 collective-permute-start.30
  106.6 3.8 %collective-permute-start.31 = (f32[64,128]{1,0:T(8,128)S(1)}, f32[64,128]{1,0:T(8,128)S(1)}, u32[]{:S(2)}, u32[]{:S(2)}) collective-permute-start(f32[64,128]{1,0:T(8,128)S(1)} %add.50), channel_id=1, source_target_pairs={{0,4},{1,5},{2,6},{3,7},{4,0},{5,1},{6,2},{7,3},{8,12},{9,13},{10,... | collective-permute-start | bytes 98312 | tf_op jit(solution)/shard_map/ppermute | solution.py:674
  110.4 0.2 collective-permute-start.32
  110.7 1.6 %collective-permute-done.31 = f32[64,128]{1,0:T(8,128)S(1)} collective-permute-done((f32[64,128]{1,0:T(8,128)S(1)}, f32[64,128]{1,0:T(8,128)S(1)}, u32[]{:S(2)}, u32[]{:S(2)}) %collective-permute-start.31) | collective-permute-done | bytes 32800 | tf_op jit(solution)/shard_map/ppermute | solution.py:674
  112.3 2.9 %collective-permute-done.32 = f32[64,128]{1,0:T(8,128)S(1)} collective-permute-done((f32[64,128]{1,0:T(8,128)S(1)}, f32[64,128]{1,0:T(8,128)S(1)}, u32[]{:S(2)}, u32[]{:S(2)}) %collective-permute-start.32) | collective-permute-done | bytes 32800 | tf_op jit(solution)/shard_map/ppermute | solution.py:674
  115.2 2.0 %collective-permute-start.33 = (f32[64,128]{1,0:T(8,128)S(1)}, f32[64,128]{1,0:T(8,128)S(1)}, u32[]{:S(2)}, u32[]{:S(2)}) collective-permute-start(f32[64,128]{1,0:T(8,128)S(1)} %add_add_fusion.3), channel_id=1, source_target_pairs={{0,8},{1,9},{2,10},{3,11},{4,12},{5,13},{6,14},{7,15},{8,0},{9,1},... | collective-permute-start | bytes 98312 | tf_op jit(solution)/shard_map/ppermute | solution.py:674
  117.2 2.2 %collective-permute-start.34 = (f32[64,128]{1,0:T(8,128)S(1)}, f32[64,128]{1,0:T(8,128)S(1)}, u32[]{:S(2)}, u32[]{:S(2)}) collective-permute-start(f32[64,128]{1,0:T(8,128)S(1)} %add_add_fusion.3), channel_id=1, source_target_pairs={{0,16},{1,17},{2,18},{3,19},{4,20},{5,21},{6,22},{7,23},{8,24},{9,... | collective-permute-start | bytes 98312 | tf_op jit(solution)/shard_map/ppermute | solution.py:674
  119.5 0.2 collective-permute-start.35
  119.7 2.4 %collective-permute-done.34 = f32[64,128]{1,0:T(8,128)S(1)} collective-permute-done((f32[64,128]{1,0:T(8,128)S(1)}, f32[64,128]{1,0:T(8,128)S(1)}, u32[]{:S(2)}, u32[]{:S(2)}) %collective-permute-start.34) | collective-permute-done | bytes 32800 | tf_op jit(solution)/shard_map/ppermute | solution.py:674
  122.1 3.1 %collective-permute-done.35 = f32[64,128]{1,0:T(8,128)S(1)} collective-permute-done((f32[64,128]{1,0:T(8,128)S(1)}, f32[64,128]{1,0:T(8,128)S(1)}, u32[]{:S(2)}, u32[]{:S(2)}) %collective-permute-start.35) | collective-permute-done | bytes 32800 | tf_op jit(solution)/shard_map/ppermute | solution.py:674
  125.2 4.9 %factors.1 = (f32[64,64]{1,0:T(8,128)S(1)}, f32[64,64]{1,0:T(8,128)S(1)}, s32[1]{0:T(128)}) custom-call(f32[64,128]{1,0:T(8,128)S(1)} %add_add_fusion.2.grams), custom_call_target="tpu_custom_call" | custom-call | flops 1073741824 | bytes 65536 | tf_op jit(solution)/shard_map/factors/pallas_call | solution.py:612
  130.7 0.4 conditional.1
  130.8 0.4 applied.3
  131.1 0.0 copy-start.5
  131.1 0.7 copy-done.5
  (31 shorter events, 0.2 us)
Async XLA Ops:
  0.0 25.7 %copy-start = (bf16[1024,768]{1,0:T(8,128)(2,1)S(1)}, bf16[1024,768]{1,0:T(8,128)(2,1)}, u32[]{:S(2)}) copy-start(bf16[1024,768]{1,0:T(8,128)(2,1)} %refs_3_.1) | copy-start | bytes 4718596
  0.0 8.1 %copy-start.3 = (s32[64]{0:T(128)S(1)}, s32[64]{0:T(128)}, u32[]{:S(2)}) copy-start(s32[64]{0:T(128)} %rows.1) | copy-start | bytes 772
  0.0 8.1 %copy-start.4 = (s32[64]{0:T(128)S(1)}, s32[64]{0:T(128)}, u32[]{:S(2)}) copy-start(s32[64]{0:T(128)} %cols.1) | copy-start | bytes 772
  0.0 22.4 %copy-start.1 = (f32[64,1024]{1,0:T(8,128)S(1)}, f32[64,1024]{1,0:T(8,128)}, u32[]{:S(2)}) copy-start(f32[64,1024]{1,0:T(8,128)} %start) | copy-start | bytes 786436
  0.0 22.4 %copy-start.2 = (s32[2]{0:T(128)S(1)}, s32[2]{0:T(128)}, u32[]{:S(2)}) copy-start(s32[2]{0:T(128)} %count_ref.3) | copy-start | bytes 28
  0.0 22.4 %collective-permute-start.7 = (bf16[1024,768]{1,0:T(8,128)(2,1)}, bf16[1024,768]{1,0:T(8,128)(2,1)S(1)}, u32[]{:S(2)}, u32[]{:S(2)}) collective-permute-start(bf16[1024,768]{1,0:T(8,128)(2,1)} %refs_3_.1), channel_id=1, source_target_pairs={{0,1},{1,0},{2,3},{3,2},{4,5},{5,4},{6,7},{7,6},{8,9},{9,8},{10,11... | collective-permute-start | bytes 4718600 | tf_op jit(solution)/shard_map/ppermute | solution.py:29
  2.1 22.9 %collective-permute-start.8 = (bf16[512,768]{1,0:T(8,128)(2,1)S(1)}, bf16[512,768]{1,0:T(8,128)(2,1)S(1)}, u32[]{:S(2)}, u32[]{:S(2)}) collective-permute-start(bf16[512,768]{1,0:T(8,128)(2,1)S(1)} %get-tuple-element.156), channel_id=1, source_target_pairs={{4,0},{8,4},{12,8},{16,12},{20,16},{24,20},{28,24},{5,1},{9,5},{13... | collective-permute-start | bytes 2359304 | tf_op jit(solution)/shard_map/ppermute | solution.py:35
  3.4 21.6 %collective-permute-start.9 = (bf16[512,768]{1,0:T(8,128)(2,1)S(1)}, bf16[512,768]{1,0:T(8,128)(2,1)S(1)}, u32[]{:S(2)}, u32[]{:S(2)}) collective-permute-start(bf16[512,768]{1,0:T(8,128)(2,1)S(1)} %get-tuple-element.156), channel_id=1, source_target_pairs={{0,2},{1,3},{2,0},{3,1},{4,6},{5,7},{6,4},{7,5},{8,10},{9,11},{10,... | collective-permute-start | bytes 2359304 | tf_op jit(solution)/shard_map/ppermute | solution.py:29
  6.0 35.5 %collective-permute-start.10 = (bf16[512,768]{1,0:T(8,128)(2,1)S(1)}, bf16[512,768]{1,0:T(8,128)(2,1)S(1)}, u32[]{:S(2)}, u32[]{:S(2)}) collective-permute-start(bf16[512,768]{1,0:T(8,128)(2,1)S(1)} %get-tuple-element.155), channel_id=1, source_target_pairs={{4,0},{8,4},{12,8},{16,12},{20,16},{24,20},{28,24},{5,1},{9,5},{13... | collective-permute-start | bytes 2359304 | tf_op jit(solution)/shard_map/ppermute | solution.py:35
  7.3 34.2 %collective-permute-start.14 = (bf16[512,768]{1,0:T(8,128)(2,1)S(1)}, bf16[512,768]{1,0:T(8,128)(2,1)S(1)}, u32[]{:S(2)}, u32[]{:S(2)}) collective-permute-start(bf16[512,768]{1,0:T(8,128)(2,1)S(1)} %get-tuple-element.155), channel_id=1, source_target_pairs={{0,2},{1,3},{2,0},{3,1},{4,6},{5,7},{6,4},{7,5},{8,10},{9,11},{10,... | collective-permute-start | bytes 2359304 | tf_op jit(solution)/shard_map/ppermute | solution.py:29
  25.0 8.6 %collective-permute-start.12 = (bf16[256,768]{1,0:T(8,128)(2,1)S(1)}, bf16[256,768]{1,0:T(8,128)(2,1)S(1)}, u32[]{:S(2)}, u32[]{:S(2)}) collective-permute-start(bf16[256,768]{1,0:T(8,128)(2,1)S(1)} %get-tuple-element.157), channel_id=1, source_target_pairs={{0,1},{1,0},{2,3},{3,2},{4,5},{5,4},{6,7},{7,6},{8,9},{9,8},{10,11... | collective-permute-start | bytes 1179656 | tf_op jit(solution)/shard_map/ppermute | solution.py:29
  25.1 8.5 %collective-permute-start.13 = (bf16[256,768]{1,0:T(8,128)(2,1)S(1)}, bf16[256,768]{1,0:T(8,128)(2,1)S(1)}, u32[]{:S(2)}, u32[]{:S(2)}) collective-permute-start(bf16[256,768]{1,0:T(8,128)(2,1)S(1)} %get-tuple-element.158), channel_id=1, source_target_pairs={{0,1},{1,0},{2,3},{3,2},{4,5},{5,4},{6,7},{7,6},{8,9},{9,8},{10,11... | collective-permute-start | bytes 1179656 | tf_op jit(solution)/shard_map/ppermute | solution.py:29
  25.6 15.9 %collective-permute-start.11 = (bf16[80,1024]{1,0:T(8,128)(2,1)S(1)}, bf16[80,1024]{1,0:T(8,128)(2,1)S(1)}, u32[]{:S(2)}, u32[]{:S(2)}) collective-permute-start(bf16[80,1024]{1,0:T(8,128)(2,1)S(1)} %opening.1.refs_4_), channel_id=1, source_target_pairs={{0,1},{1,0},{2,3},{3,2},{4,5},{5,4},{6,7},{7,6},{8,9},{9,8},{10,11... | collective-permute-start | bytes 491528 | tf_op jit(solution)/shard_map/ppermute | solution.py:29
  41.5 3.8 %collective-permute-start.15 = (bf16[512,768]{1,0:T(8,128)(2,1)S(1)}, bf16[512,768]{1,0:T(8,128)(2,1)S(1)}, u32[]{:S(2)}, u32[]{:S(2)}) collective-permute-start(bf16[512,768]{1,0:T(8,128)(2,1)S(1)} %collective-permute-done.14.refs_1_), channel_id=1, source_target_pairs={{0,1},{1,0},{2,3},{3,2},{4,5},{5,4},{6,7},{7,6},{8,9},{9,8},{10,11... | collective-permute-start | bytes 2359304 | tf_op jit(solution)/shard_map/ppermute | solution.py:29
  41.5 9.2 %collective-permute-start.16 = (bf16[80,1024]{1,0:T(8,128)(2,1)S(1)}, bf16[80,1024]{1,0:T(8,128)(2,1)S(1)}, u32[]{:S(2)}, u32[]{:S(2)}) collective-permute-start(bf16[80,1024]{1,0:T(8,128)(2,1)S(1)} %opening.1.refs_4_), channel_id=1, source_target_pairs={{0,2},{1,3},{2,0},{3,1},{4,6},{5,7},{6,4},{7,5},{8,10},{9,11},{10,... | collective-permute-start | bytes 491528 | tf_op jit(solution)/shard_map/ppermute | solution.py:29
  43.3 11.8 %collective-permute-start.18 = (bf16[80,1024]{1,0:T(8,128)(2,1)S(1)}, bf16[80,1024]{1,0:T(8,128)(2,1)S(1)}, u32[]{:S(2)}, u32[]{:S(2)}) collective-permute-start(bf16[80,1024]{1,0:T(8,128)(2,1)S(1)} %opening.1.refs_4_), channel_id=1, source_target_pairs={{4,0},{8,4},{12,8},{16,12},{20,16},{24,20},{28,24},{5,1},{9,5},{13... | collective-permute-start | bytes 491528 | tf_op jit(solution)/shard_map/ppermute | solution.py:35
  50.7 4.4 %collective-permute-start.17 = (bf16[80,1024]{1,0:T(8,128)(2,1)S(1)}, bf16[80,1024]{1,0:T(8,128)(2,1)S(1)}, u32[]{:S(2)}, u32[]{:S(2)}) collective-permute-start(bf16[80,1024]{1,0:T(8,128)(2,1)S(1)} %collective-permute-done.16.refs_4_), channel_id=1, source_target_pairs={{0,1},{1,0},{2,3},{3,2},{4,5},{5,4},{6,7},{7,6},{8,9},{9,8},{10,11... | collective-permute-start | bytes 491528 | tf_op jit(solution)/shard_map/ppermute | solution.py:29
  59.1 2.1 %collective-permute-start.19 = (f32[4,72,512]{2,1,0:T(8,128)S(1)}, f32[4,72,512]{2,1,0:T(8,128)S(1)}, u32[]{:S(2)}, u32[]{:S(2)}) collective-permute-start(f32[4,72,512]{2,1,0:T(8,128)S(1)} %get-tuple-element.125), channel_id=1, source_target_pairs={{0,1},{1,0},{2,3},{3,2},{4,5},{5,4},{6,7},{7,6},{8,9},{9,8},{10,11... | collective-permute-start | bytes 1769480 | tf_op jit(solution)/shard_map/ppermute | solution.py:29
  61.3 9.1 %collective-permute-start.21 = (f32[2,72,512]{2,1,0:T(8,128)S(1)}, f32[2,72,512]{2,1,0:T(8,128)S(1)}, u32[]{:S(2)}, u32[]{:S(2)}) collective-permute-start(f32[2,72,512]{2,1,0:T(8,128)S(1)} %slice_add_fusion), channel_id=1, source_target_pairs={{0,2},{1,3},{2,0},{3,1},{4,6},{5,7},{6,4},{7,5},{8,10},{9,11},{10,... | collective-permute-start | bytes 884744 | tf_op jit(solution)/shard_map/ppermute | solution.py:29
  61.3 9.0 %collective-permute-start.20 = (f32[2,72,512]{2,1,0:T(8,128)S(1)}, f32[2,72,512]{2,1,0:T(8,128)S(1)}, u32[]{:S(2)}, u32[]{:S(2)}) collective-permute-start(f32[2,72,512]{2,1,0:T(8,128)S(1)} %get-tuple-element.130), channel_id=1, source_target_pairs={{0,4},{4,8},{8,12},{12,16},{16,20},{20,24},{24,28},{1,5},{5,9},{9,... | collective-permute-start | bytes 884744 | tf_op jit(solution)/shard_map/ppermute | solution.py:35
  71.3 2.2 %collective-permute-start.22 = (bf16[128,1024]{1,0:T(8,128)(2,1)S(1)}, bf16[128,1024]{1,0:T(8,128)(2,1)S(1)}, u32[]{:S(2)}, u32[]{:S(2)}) collective-permute-start(bf16[128,1024]{1,0:T(8,128)(2,1)S(1)} %get-tuple-element.132.refs_4_), channel_id=1, source_target_pairs={{0,1},{1,0},{2,3},{3,2},{4,5},{5,4},{6,7},{7,6},{8,9},{9,8},{10,11... | collective-permute-start | bytes 786440 | tf_op jit(solution)/shard_map/ppermute | solution.py:29
  71.4 8.7 %collective-permute-start.23 = (bf16[128,1024]{1,0:T(8,128)(2,1)S(1)}, bf16[128,1024]{1,0:T(8,128)(2,1)S(1)}, u32[]{:S(2)}, u32[]{:S(2)}) collective-permute-start(bf16[128,1024]{1,0:T(8,128)(2,1)S(1)} %get-tuple-element.132.refs_4_), channel_id=1, source_target_pairs={{0,2},{1,3},{2,0},{3,1},{4,6},{5,7},{6,4},{7,5},{8,10},{9,11},{10,... | collective-permute-start | bytes 786440 | tf_op jit(solution)/shard_map/ppermute | solution.py:29
  72.3 15.0 %collective-permute-start.25 = (bf16[128,1024]{1,0:T(8,128)(2,1)S(1)}, bf16[128,1024]{1,0:T(8,128)(2,1)S(1)}, u32[]{:S(2)}, u32[]{:S(2)}) collective-permute-start(bf16[128,1024]{1,0:T(8,128)(2,1)S(1)} %get-tuple-element.132.refs_4_), channel_id=1, source_target_pairs={{4,0},{8,4},{12,8},{16,12},{20,16},{24,20},{28,24},{5,1},{9,5},{13... | collective-permute-start | bytes 786440 | tf_op jit(solution)/shard_map/ppermute | solution.py:35
  80.1 7.2 %collective-permute-start.24 = (bf16[128,1024]{1,0:T(8,128)(2,1)S(1)}, bf16[128,1024]{1,0:T(8,128)(2,1)S(1)}, u32[]{:S(2)}, u32[]{:S(2)}) collective-permute-start(bf16[128,1024]{1,0:T(8,128)(2,1)S(1)} %collective-permute-done.23.refs_4_), channel_id=1, source_target_pairs={{0,1},{1,0},{2,3},{3,2},{4,5},{5,4},{6,7},{7,6},{8,9},{9,8},{10,11... | collective-permute-start | bytes 786440 | tf_op jit(solution)/shard_map/ppermute | solution.py:29
  91.4 2.0 %collective-permute-start.26 = (f32[4,64,512]{2,1,0:T(8,128)S(1)}, f32[4,64,512]{2,1,0:T(8,128)S(1)}, u32[]{:S(2)}, u32[]{:S(2)}) collective-permute-start(f32[4,64,512]{2,1,0:T(8,128)S(1)} %get-tuple-element.139), channel_id=1, source_target_pairs={{0,1},{1,0},{2,3},{3,2},{4,5},{5,4},{6,7},{7,6},{8,9},{9,8},{10,11... | collective-permute-start | bytes 1572872 | tf_op jit(solution)/shard_map/ppermute | solution.py:29
  93.4 8.4 %collective-permute-start.28 = (f32[2,64,512]{2,1,0:T(8,128)S(1)}, f32[2,64,512]{2,1,0:T(8,128)S(1)}, u32[]{:S(2)}, u32[]{:S(2)}) collective-permute-start(f32[2,64,512]{2,1,0:T(8,128)S(1)} %slice_add_fusion.1), channel_id=1, source_target_pairs={{0,2},{1,3},{2,0},{3,1},{4,6},{5,7},{6,4},{7,5},{8,10},{9,11},{10,... | collective-permute-start | bytes 786440 | tf_op jit(solution)/shard_map/ppermute | solution.py:29
  94.3 8.8 %collective-permute-start.27 = (f32[2,64,512]{2,1,0:T(8,128)S(1)}, f32[2,64,512]{2,1,0:T(8,128)S(1)}, u32[]{:S(2)}, u32[]{:S(2)}) collective-permute-start(f32[2,64,512]{2,1,0:T(8,128)S(1)} %get-tuple-element.144), channel_id=1, source_target_pairs={{0,4},{4,8},{8,12},{12,16},{16,20},{20,24},{24,28},{1,5},{5,9},{9,... | collective-permute-start | bytes 786440 | tf_op jit(solution)/shard_map/ppermute | solution.py:35
  104.1 1.3 collective-permute-start.29
  105.4 5.3 %collective-permute-start.30 = (f32[64,128]{1,0:T(8,128)S(1)}, f32[64,128]{1,0:T(8,128)S(1)}, u32[]{:S(2)}, u32[]{:S(2)}) collective-permute-start(f32[64,128]{1,0:T(8,128)S(1)} %add.50), channel_id=1, source_target_pairs={{0,2},{1,3},{2,0},{3,1},{4,6},{5,7},{6,4},{7,5},{8,10},{9,11},{10,... | collective-permute-start | bytes 98312 | tf_op jit(solution)/shard_map/ppermute | solution.py:674
  106.6 5.7 %collective-permute-start.31 = (f32[64,128]{1,0:T(8,128)S(1)}, f32[64,128]{1,0:T(8,128)S(1)}, u32[]{:S(2)}, u32[]{:S(2)}) collective-permute-start(f32[64,128]{1,0:T(8,128)S(1)} %add.50), channel_id=1, source_target_pairs={{0,4},{1,5},{2,6},{3,7},{4,0},{5,1},{6,2},{7,3},{8,12},{9,13},{10,... | collective-permute-start | bytes 98312 | tf_op jit(solution)/shard_map/ppermute | solution.py:674
  110.4 4.8 %collective-permute-start.32 = (f32[64,128]{1,0:T(8,128)S(1)}, f32[64,128]{1,0:T(8,128)S(1)}, u32[]{:S(2)}, u32[]{:S(2)}) collective-permute-start(f32[64,128]{1,0:T(8,128)S(1)} %add.50), channel_id=1, source_target_pairs={{0,6},{1,7},{2,4},{3,5},{4,2},{5,3},{6,0},{7,1},{8,14},{9,15},{10,... | collective-permute-start | bytes 98312 | tf_op jit(solution)/shard_map/ppermute | solution.py:674
  115.2 4.5 %collective-permute-start.33 = (f32[64,128]{1,0:T(8,128)S(1)}, f32[64,128]{1,0:T(8,128)S(1)}, u32[]{:S(2)}, u32[]{:S(2)}) collective-permute-start(f32[64,128]{1,0:T(8,128)S(1)} %add_add_fusion.3), channel_id=1, source_target_pairs={{0,8},{1,9},{2,10},{3,11},{4,12},{5,13},{6,14},{7,15},{8,0},{9,1},... | collective-permute-start | bytes 98312 | tf_op jit(solution)/shard_map/ppermute | solution.py:674
  117.2 4.8 %collective-permute-start.34 = (f32[64,128]{1,0:T(8,128)S(1)}, f32[64,128]{1,0:T(8,128)S(1)}, u32[]{:S(2)}, u32[]{:S(2)}) collective-permute-start(f32[64,128]{1,0:T(8,128)S(1)} %add_add_fusion.3), channel_id=1, source_target_pairs={{0,16},{1,17},{2,18},{3,19},{4,20},{5,21},{6,22},{7,23},{8,24},{9,... | collective-permute-start | bytes 98312 | tf_op jit(solution)/shard_map/ppermute | solution.py:674
  119.5 5.7 %collective-permute-start.35 = (f32[64,128]{1,0:T(8,128)S(1)}, f32[64,128]{1,0:T(8,128)S(1)}, u32[]{:S(2)}, u32[]{:S(2)}) collective-permute-start(f32[64,128]{1,0:T(8,128)S(1)} %add_add_fusion.3), channel_id=1, source_target_pairs={{0,24},{1,25},{2,26},{3,27},{4,28},{5,29},{6,30},{7,31},{8,16},{9,... | collective-permute-start | bytes 98312 | tf_op jit(solution)/shard_map/ppermute | solution.py:674
  131.1 0.7 copy-start.5
